TPU v7x, 32 devices: a whole 2x2x4 slice. The times are simulated.
32 devices in a mesh: parts: 2 (over y), dp: 16 (over z, x, core).
Axes of the slice: x: 2, y: 2, z: 4, core: 2. Of those that a mesh axis runs over, the one named last changes fastest.
Arguments:
- acts: bfloat16 [4096, 8192], P(('parts', 'dp')), parts along dimension 0, may hold values from -6 to 6
- cotan: bfloat16 [4096, 8192], P(('parts', 'dp')), parts along dimension 0, may hold values from -6 to 6
- token_task_index: int32 [4096, 1], P(('parts', 'dp')), parts along dimension 0, may hold values from 0 to 15; in each aligned block of 128 rows (0 to 127, 128 to 255, ...) at most 16 rows name the same one
- task_slot_lookup: int32 [32], P('parts'), parts along dimension 0, may hold values from 0 to 15, each once
- pool_down_factors: bfloat16 [32, 64, 8192], P(('parts', 'dp')), parts along dimension 0, may hold values from -0.0625 to 0.0625
- pool_up_factors: bfloat16 [32, 64, 8192], P(('parts', 'dp')), parts along dimension 0, may hold values from -0.75 to 0.75
Outputs:
- grad_acts: bfloat16 [4096, 8192], P(('parts', 'dp')), parts along dimension 0
- grad_down: float32 [32, 64, 8192], P(('parts', 'dp')), parts along dimension 0
- grad_up: float32 [32, 64, 8192], P(('parts', 'dp')), parts along dimension 0
There are 2 independent parts, one for each index of `parts`. A program takes and returns all parts, laid end to end along the dimension named above; each array names one. Nothing has to cross between parts.
Inputs may be any that keep to these rules, and one draw needn't show every extreme that they name: `token_task_index`: among the 128 tokens of one device (aligned blocks) no task is named by more than 16 tokens; some task is named by exactly 16. `task_slot_lookup`: each slot appears once.
All inputs are finite; a program needn't handle non-finite values.
Results may differ from a plain program's by a relative error of at most 0.0049.
Values may be sent and summed in bfloat16 or wider, within the bound.
No kernel may reach another device: no remote copies, remote signals or barrier semaphores. Data moves between devices by JAX's collectives and lax.ppermute only.
A program may use at most 128 MiB of HBM per device.

v0:
```python
import jax
import jax.numpy as jnp
from jax import lax
from jax.sharding import PartitionSpec as P


def per_device(acts, cotan, token_task_index, task_slot_lookup, pool_down_factors, pool_up_factors):
    ndevices = lax.axis_size("dp")
    tokens = acts.shape[0]
    width = acts.shape[1]
    rank_width = pool_down_factors.shape[1]
    capacity = 2 * ((tokens + ndevices - 1) // ndevices)
    slots = ndevices * capacity
    pool = task_slot_lookup.shape[0]
    task_hot = (token_task_index == jnp.arange(pool, dtype=jnp.int32)[None, :]).astype(jnp.int32)
    owner = jnp.sum(task_hot * task_slot_lookup[None, :], axis=1)
    owner_hot = (owner[:, None] == jnp.arange(ndevices, dtype=jnp.int32)[None, :]).astype(jnp.int32)
    before = jnp.cumsum(owner_hot, axis=0) - owner_hot
    position = jnp.sum(before * owner_hot, axis=1)
    dest = owner * capacity + position
    placed = jnp.arange(slots, dtype=jnp.int32)[:, None] == dest[None, :]
    place_mat = placed.astype(jnp.bfloat16)
    send_x = jnp.dot(place_mat, acts, preferred_element_type=jnp.float32).astype(jnp.bfloat16)
    send_g = jnp.dot(place_mat, cotan, preferred_element_type=jnp.float32).astype(jnp.bfloat16)
    send_x = send_x.reshape(ndevices, capacity, width)
    send_g = send_g.reshape(ndevices, capacity, width)
    down_matrix = pool_down_factors[0]
    up_matrix = pool_up_factors[0]
    dims = (((1,), (1,)), ((), ()))
    rows_x, rows_g = (
        lax.all_to_all(send_x, "dp", split_axis=0, concat_axis=0, tiled=True),
        lax.all_to_all(send_g, "dp", split_axis=0, concat_axis=0, tiled=True),
    )
    rows_x = rows_x.reshape(slots, width)
    rows_g = rows_g.reshape(slots, width)
    hidden = lax.dot_general(rows_x, down_matrix, dims, preferred_element_type=jnp.float32).astype(
        jnp.bfloat16
    )
    inner = lax.dot_general(rows_g, up_matrix, dims, preferred_element_type=jnp.float32).astype(
        jnp.bfloat16
    )
    rows_dx = jnp.dot(inner, down_matrix, preferred_element_type=jnp.float32).astype(jnp.bfloat16)
    returned = lax.all_to_all(
        rows_dx.reshape(ndevices, capacity, width), "dp", split_axis=0, concat_axis=0, tiled=True
    ).reshape(slots, width)
    grad_acts = lax.dot_general(
        placed.astype(jnp.bfloat16),
        returned,
        (((0,), (0,)), ((), ())),
        preferred_element_type=jnp.float32,
    ).astype(jnp.bfloat16)
    tdims = (((0,), (0,)), ((), ()))
    raw_up = lax.dot_general(hidden, rows_g, tdims, preferred_element_type=jnp.float32)
    raw_down = lax.dot_general(inner, rows_x, tdims, preferred_element_type=jnp.float32)
    local_sq = jnp.sum(raw_down * raw_down) + jnp.sum(raw_up * raw_up)
    total = lax.psum(local_sq, "dp")
    norm = jnp.sqrt(total + 1e-06)
    limit = jnp.sqrt(jnp.float32(2 * rank_width * width * ndevices))
    factor = jnp.minimum(jnp.float32(1.0), limit / norm)
    return (grad_acts, (raw_down * factor)[None], (raw_up * factor)[None])


def solution(mesh):
    return jax.shard_map(
        per_device,
        mesh=mesh,
        in_specs=(
            P(("parts", "dp"), None),
            P(("parts", "dp"), None),
            P(("parts", "dp"), None),
            P("parts"),
            P(("parts", "dp"), None, None),
            P(("parts", "dp"), None, None),
        ),
        out_specs=(
            P(("parts", "dp"), None),
            P(("parts", "dp"), None, None),
            P(("parts", "dp"), None, None),
        ),
        check_vma=False,
    )
```

profile of v0, /device:TPU:16, one launch (start us, length us, event | category | flops | bytes accessed | tf_op | source)
XLA Modules:
  0.0 327.2 jit_solution(10040072506904688930)
XLA Ops:
  0.6 0.0 copy-start
  0.6 1.0 select_reduce_fusion.1
  1.6 0.1 fusion.8
  1.7 0.2 reduce_window_sum.11
  1.9 0.2 select_reduce_fusion
  2.1 0.2 copy-done
  2.3 3.2 convolution_convert_fusion.2
  5.5 6.2 %all-to-all-start = ((bf16[16,16,8192]{2,1,0:T(8,128)(2,1)}), bf16[16,16,8192]{2,1,0:T(8,128)(2,1)}, u32[]{:S(2)}, u32[]{:S(2)}) async-start(bf16[16,16,8192]{2,1,0:T(8,128)(2,1)} %bitcast.33), calls=%async_computation | async-start | bytes 8388608 | tf_op jit(solution)/shard_map/all_to_all | solution.py:32
  11.6 4.8 %convolution_convert_fusion = bf16[256,8192]{1,0:T(8,128)(2,1)} fusion(bf16[128,8192]{1,0:T(8,128)(2,1)} %param.6, s32[128]{0:T(128)S(1)} %multiply_add_fusion), kind=kOutput, calls=%fused_computation | convolution fusion | flops 539000832 | bytes 6291968 | tf_op jit(solution)/shard_map/dot_general | solution.py:23
  16.4 87.9 %all-to-all-done = bf16[16,16,8192]{2,1,0:T(8,128)(2,1)} async-done(((bf16[16,16,8192]{2,1,0:T(8,128)(2,1)}), bf16[16,16,8192]{2,1,0:T(8,128)(2,1)}, u32[]{:S(2)}, u32[]{:S(2)}) %all-to-all-start) | async-done | bytes 4194336 | tf_op jit(solution)/shard_map/all_to_all | solution.py:32
  104.3 4.7 %all-to-all-start.2 = ((bf16[16,16,8192]{2,1,0:T(8,128)(2,1)}), bf16[16,16,8192]{2,1,0:T(8,128)(2,1)}, u32[]{:S(2)}, u32[]{:S(2)}) async-start(bf16[16,16,8192]{2,1,0:T(8,128)(2,1)} %bitcast.32), calls=%async_computation.2 | async-start | bytes 8388608 | tf_op jit(solution)/shard_map/all_to_all | solution.py:31
  109.0 0.0 copy-start.1
  109.0 4.0 %convolution_convert_fusion.5 = bf16[256,64]{0,1:T(8,128)(2,1)S(1)} fusion(bf16[256,8192]{1,0:T(8,128)(2,1)} %bitcast.2, bf16[1,64,8192]{2,1,0:T(8,128)(2,1)} %param.11), kind=kOutput, calls=%fused_computation.10 | convolution fusion | flops 268451840 | bytes 5275648 | tf_op jit(solution)/shard_map/dot_general | solution.py:39
  113.0 0.0 copy-done.1
  113.0 3.2 convolution_convert_fusion.1
  116.2 85.5 %all-to-all-done.2 = bf16[16,16,8192]{2,1,0:T(8,128)(2,1)} async-done(((bf16[16,16,8192]{2,1,0:T(8,128)(2,1)}), bf16[16,16,8192]{2,1,0:T(8,128)(2,1)}, u32[]{:S(2)}, u32[]{:S(2)}) %all-to-all-start.2) | async-done | bytes 4194336 | tf_op jit(solution)/shard_map/all_to_all | solution.py:31
  201.7 4.7 %all-to-all-start.1 = ((bf16[16,16,8192]{2,1,0:T(8,128)(2,1)}), bf16[16,16,8192]{2,1,0:T(8,128)(2,1)}, u32[]{:S(2)}, u32[]{:S(2)}) async-start(bf16[16,16,8192]{2,1,0:T(8,128)(2,1)} %bitcast.31), calls=%async_computation.1 | async-start | bytes 8388608 | tf_op jit(solution)/shard_map/all_to_all | solution.py:43
  206.4 5.0 %multiply_reduce_fusion.1 = (f32[]{:T(128)}, f32[64,8192]{1,0:T(8,128)}) fusion(bf16[256,64]{0,1:T(8,128)(2,1)S(1)} %convolution_convert_fusion.5, bf16[256,8192]{1,0:T(8,128)(2,1)} %bitcast.8), kind=kOutput, calls=%fused_computation.7 | convolution fusion | flops 269484032 | bytes 6324228 | tf_op jit(solution)/shard_map/dot_general | solution.py:54
  211.3 8.5 %multiply_reduce_fusion = (f32[]{:T(128)}, f32[64,8192]{1,0:T(8,128)}) fusion(bf16[256,8192]{1,0:T(8,128)(2,1)} %bitcast.2, bf16[256,8192]{1,0:T(8,128)(2,1)} %bitcast.8, bf16[1,64,8192]{2,1,0:T(8,128)(2,1)S(1)} %copy-done.1), kind=kOutput, calls=%fused_computation.6 | convolution fusion | flops 537935872 | bytes 11534340 | tf_op jit(solution)/shard_map/dot_general | solution.py:53
  221.0 96.6 %psum.7 = f32[]{:T(128)} all-reduce(f32[]{:T(128)S(6)} %add.16), channel_id=1, replica_groups=mesh['parts'=2,'dp'=16] {'dp'}, use_global_device_ids=true, to_apply=%region_5.6 | all-reduce | flops 1 | bytes 8 | tf_op jit(solution)/shard_map/psum | solution.py:56
  318.4 4.6 %multiply_bitcast_fusion = (f32[1,64,8192]{2,1,0:T(8,128)}, f32[1,64,8192]{2,1,0:T(8,128)}) fusion(f32[64,8192]{1,0:T(8,128)} %get-tuple-element.6, f32[]{:T(128)S(6)} %min_shard_map.3, f32[64,8192]{1,0:T(8,128)} %get-tuple-element.4), kind=kLoop, calls=%fused_computation.4 | loop fusion | flops 1048576 | bytes 8388612 | tf_op jit(solution)/shard_map/broadcast_in_dim | solution.py:60
  323.0 0.0 all-to-all-done.1
  323.0 4.3 %convolution_convert_fusion.3 = bf16[128,8192]{1,0:T(8,128)(2,1)} fusion(bf16[256,8192]{1,0:T(8,128)(2,1)} %bitcast.6, s32[128]{0:T(128)S(1)} %multiply_add_fusion), kind=kOutput, calls=%fused_computation.3 | convolution fusion | flops 537952256 | bytes 6291968 | tf_op jit(solution)/shard_map/dot_general | solution.py:46
  (1 shorter events, 0.0 us)
Async XLA Ops:
  0.6 1.6 copy-start
  5.5 98.9 %all-to-all-start = ((bf16[16,16,8192]{2,1,0:T(8,128)(2,1)}), bf16[16,16,8192]{2,1,0:T(8,128)(2,1)}, u32[]{:S(2)}, u32[]{:S(2)}) async-start(bf16[16,16,8192]{2,1,0:T(8,128)(2,1)} %bitcast.33), calls=%async_computation | async-start | bytes 8388608 | tf_op jit(solution)/shard_map/all_to_all | solution.py:32
  104.3 97.4 %all-to-all-start.2 = ((bf16[16,16,8192]{2,1,0:T(8,128)(2,1)}), bf16[16,16,8192]{2,1,0:T(8,128)(2,1)}, u32[]{:S(2)}, u32[]{:S(2)}) async-start(bf16[16,16,8192]{2,1,0:T(8,128)(2,1)} %bitcast.32), calls=%async_computation.2 | async-start | bytes 8388608 | tf_op jit(solution)/shard_map/all_to_all | solution.py:31
  109.0 4.0 %copy-start.1 = (bf16[1,64,8192]{2,1,0:T(8,128)(2,1)S(1)}, bf16[1,64,8192]{2,1,0:T(8,128)(2,1)}, u32[]{:S(2)}) copy-start(bf16[1,64,8192]{2,1,0:T(8,128)(2,1)} %param.10) | copy-start | bytes 3145732
  201.7 121.3 %all-to-all-start.1 = ((bf16[16,16,8192]{2,1,0:T(8,128)(2,1)}), bf16[16,16,8192]{2,1,0:T(8,128)(2,1)}, u32[]{:S(2)}, u32[]{:S(2)}) async-start(bf16[16,16,8192]{2,1,0:T(8,128)(2,1)} %bitcast.31), calls=%async_computation.1 | async-start | bytes 8388608 | tf_op jit(solution)/shard_map/all_to_all | solution.py:43
where the time goes:
time: 328 us; the launch traced here: 327 us
  waiting for transfers between devices  173 us (53%)
  blocking collectives  96.6 us (29%)
  matrix products  32.9 us (10%)
  starting transfers between devices  15.5 us (5%)
  other arithmetic  6.05 us (2%)
    psum x1, blocking collectives, per_device(): total = lax.psum(local_sq, 'dp')  96.6 us
    all_to_all x1, waiting for transfers between devices, per_device(): lax.all_to_all(send_g, 'dp', split_axis=0, concat_axis=0, tiled=True)  87.9 us
    all_to_all x1, waiting for transfers between devices, per_device(): lax.all_to_all(send_x, 'dp', split_axis=0, concat_axis=0, tiled=True)  85.5 us
    dot_general x1, matrix products, per_device(): lax.dot_general(hidden, rows_g, tdims, preferred_element_type=jnp.float32)  8.47 us
  transfers between devices with their start and end apart: 3, of which 2 were waited for; matrix products, arithmetic and copies ran while one was open for 9% of the time, Pallas kernels for 0%

commit v1 on v0

v1 whole, which is shorter than its diff:
```python
import jax
import jax.numpy as jnp
from jax import lax
from jax.sharding import PartitionSpec as P

ROWS_OF = (((1,), (1,)), ((), ()))
OUTER = (((0,), (0,)), ((), ()))


def dot32(a, b, dims=(((1,), (0,)), ((), ()))):
    return lax.dot_general(a, b, dims, preferred_element_type=jnp.float32)


def route(token_task_index, task_slot_lookup, ndevices):
    pool = task_slot_lookup.shape[0]
    task_hot = (token_task_index == jnp.arange(pool, dtype=jnp.int32)[None, :]).astype(jnp.int32)
    owner = jnp.sum(task_hot * task_slot_lookup[None, :], axis=1)
    owner_hot = (owner[:, None] == jnp.arange(ndevices, dtype=jnp.int32)[None, :]).astype(jnp.int32)
    before = jnp.cumsum(owner_hot, axis=0) - owner_hot
    position = jnp.sum(before * owner_hot, axis=1)
    return owner, position


def clipped(raw_down, raw_up, ndevices):
    local_sq = jnp.sum(raw_down * raw_down) + jnp.sum(raw_up * raw_up)
    total = lax.psum(local_sq, "dp")
    norm = jnp.sqrt(total + 1e-06)
    limit = jnp.sqrt(jnp.float32(2 * raw_down.shape[0] * raw_down.shape[1] * ndevices))
    factor = jnp.minimum(jnp.float32(1.0), limit / norm)
    return (raw_down * factor)[None], (raw_up * factor)[None]


def move_tokens(acts, cotan, token_task_index, task_slot_lookup, pool_down_factors, pool_up_factors):
    ndevices = lax.axis_size("dp")
    tokens, width = acts.shape
    capacity = 2 * ((tokens + ndevices - 1) // ndevices)
    slots = ndevices * capacity
    owner, position = route(token_task_index, task_slot_lookup, ndevices)
    dest = owner * capacity + position
    placed = (jnp.arange(slots, dtype=jnp.int32)[:, None] == dest[None, :]).astype(jnp.bfloat16)

    def exchange(rows):
        rows = rows.reshape(ndevices, capacity, width)
        return lax.all_to_all(rows, "dp", split_axis=0, concat_axis=0, tiled=True).reshape(slots, width)

    down, up = pool_down_factors[0], pool_up_factors[0]
    rows_x = exchange(dot32(placed, acts).astype(jnp.bfloat16))
    rows_g = exchange(dot32(placed, cotan).astype(jnp.bfloat16))
    hidden = dot32(rows_x, down, ROWS_OF).astype(jnp.bfloat16)
    inner = dot32(rows_g, up, ROWS_OF).astype(jnp.bfloat16)
    returned = exchange(dot32(inner, down).astype(jnp.bfloat16))
    grad_acts = dot32(placed, returned, OUTER).astype(jnp.bfloat16)
    raw_up = dot32(hidden, rows_g, OUTER)
    raw_down = dot32(inner, rows_x, OUTER)
    return (grad_acts,) + clipped(raw_down, raw_up, ndevices)


def move_adapters(plane, acts, cotan, token_task_index, task_slot_lookup, pool_down_factors, pool_up_factors):
    ndevices = lax.axis_size("dp")
    tokens, width = acts.shape
    capacity = 2 * ((tokens + ndevices - 1) // ndevices)
    me = lax.axis_index("dp")
    z, column = me // plane, me % plane
    is_end = (z == 0) | (z == 3)
    bf16 = jnp.bfloat16

    def planes(pairs):
        return [(a * plane + c, b * plane + c) for a, b in pairs for c in range(plane)]

    swap = planes([(0, 1), (1, 0), (2, 3), (3, 2)])
    cross = planes([(1, 2), (2, 1)])
    outward = planes([(1, 0), (2, 3)])
    inward = planes([(0, 1), (3, 2)])

    def beside(m):
        return [(i, (i // plane) * plane + ((i % plane) ^ m)) for i in range(ndevices)]

    def send(array, pairs):
        return lax.ppermute(array, "dp", pairs)

    owner, position = route(token_task_index, task_slot_lookup, ndevices)
    owner_z, turn = owner // plane, (owner % plane) ^ column
    other_mid = jnp.where(z < 2, 2, 1)
    kind = jnp.where(owner_z == z, 0, jnp.where(owner_z == (z ^ 1), 1, jnp.where(owner_z == other_mid, 2, 3)))

    def places(wanted, row, rows):
        hot = jnp.arange(rows, dtype=jnp.int32)[:, None] == row[None, :]
        return (hot & wanted[None, :]).astype(bf16)

    block = plane * capacity
    place3 = places(kind == 3, turn * capacity + position, block)
    place2 = places(kind == 2, turn * capacity + position, block)
    place10 = places(kind < 2, turn * (2 * capacity) + kind * capacity + position, 2 * block)

    def in_plane(blocks):
        return [blocks[0]] + [send(blocks[m], beside(m)) for m in range(1, plane)]

    def packed(place, rows):
        out = dot32(place, rows).astype(bf16)
        return list(out.reshape(plane, -1, width))

    down, up = pool_down_factors[0], pool_up_factors[0]
    down_e, up_e = send(down, swap), send(up, swap)
    down_x, up_x = send(down, cross), send(up, cross)

    x3, g3 = in_plane(packed(place3, acts)), in_plane(packed(place3, cotan))
    x2, g2 = in_plane(packed(place2, acts)), in_plane(packed(place2, cotan))
    x3, g3 = jnp.concatenate(x3), jnp.concatenate(g3)
    x3t, g3t = send(x3, inward), send(g3, inward)
    x10, g10 = in_plane(packed(place10, acts)), in_plane(packed(place10, cotan))

    down_o, up_o = send(down_x, outward), send(up_x, outward)
    down_f, up_f = send(down_e, cross), send(up_e, cross)
    down_2, up_2 = jnp.where(is_end, down_o, down_x), jnp.where(is_end, up_o, up_x)

    x2, g2 = jnp.concatenate(x2), jnp.concatenate(g2)
    x3, g3 = jnp.concatenate([x3, x3t]), jnp.concatenate([g3, g3t])
    x0 = jnp.concatenate([b[:capacity] for b in x10])
    g0 = jnp.concatenate([b[:capacity] for b in g10])
    x1 = jnp.concatenate([b[capacity:] for b in x10])
    g1 = jnp.concatenate([b[capacity:] for b in g10])

    def group(x, g, d, u):
        hidden = dot32(x, d, ROWS_OF).astype(bf16)
        inner = dot32(g, u, ROWS_OF).astype(bf16)
        return dot32(inner, d).astype(bf16), dot32(hidden, g, OUTER), dot32(inner, x, OUTER)

    dx3, ru3, rd3 = group(x3, g3, down_f, up_f)
    dx2, ru2, rd2 = group(x2, g2, down_2, up_2)
    dx1, ru1, rd1 = group(x1, g1, down_e, up_e)
    dx0, ru0, rd0 = group(x0, g0, down, up)

    ru3, rd3 = send(ru3.astype(bf16), cross), send(rd3.astype(bf16), cross)
    ru2i, rd2i = send(ru2.astype(bf16), inward), send(rd2.astype(bf16), inward)
    ru2, rd2 = send((ru2 + ru2i).astype(bf16), cross), send((rd2 + rd2i).astype(bf16), cross)
    ru1, rd1 = send((ru1 + ru3).astype(bf16), swap), send((rd1 + rd3).astype(bf16), swap)
    raw_up = ru0 + ru2 + ru1
    raw_down = rd0 + rd2 + rd1

    dx3 = jnp.where(is_end, send(dx3[block:], outward), dx3[:block])
    back3 = in_plane(list(dx3.reshape(plane, capacity, width)))
    back2 = in_plane(list(dx2.reshape(plane, capacity, width)))
    dx10 = jnp.concatenate([dx0.reshape(plane, capacity, width), dx1.reshape(plane, capacity, width)], axis=1)
    back10 = in_plane(list(dx10))
    place = jnp.concatenate([place3, place2, place10])
    grad_acts = dot32(place, jnp.concatenate(back3 + back2 + back10), OUTER).astype(bf16)
    return (grad_acts,) + clipped(raw_down, raw_up, ndevices)


def solution(mesh):
    ndevices = mesh.shape["dp"]
    plane = 1
    while (2 * plane) ** 2 <= ndevices:
        plane *= 2

    def per_device(*arrays):
        if ndevices == 4 * plane:
            return move_adapters(plane, *arrays)
        return move_tokens(*arrays)

    rows, pools = P(("parts", "dp"), None), P(("parts", "dp"), None, None)
    return jax.shard_map(
        per_device,
        mesh=mesh,
        in_specs=(rows, rows, rows, P("parts"), pools, pools),
        out_specs=(rows, pools, pools),
        check_vma=False,
    )
```

time: 328 us -> 441 us (1.34)
  the two profiles are of different devices: /device:TPU:16 before, /device:TPU:0 now
where the time goes in v1:
time: 441 us; the launch traced here: 439 us
  waiting for transfers between devices  253 us (57%)
  starting transfers between devices  52.1 us (12%)
  matrix products  45.6 us (10%)
  blocking collectives  43.7 us (10%)
  local copies, waits for them, and re-layouts  28.6 us (6%)
  other arithmetic  12.8 us (3%)
    ppermute x46, waiting for transfers between devices, send(): return lax.ppermute(array, 'dp', pairs)  253 us
    ppermute x46, starting transfers between devices, send(): return lax.ppermute(array, 'dp', pairs)  52.1 us
    dot_general x23, matrix products, dot32(): return lax.dot_general(a, b, dims, preferred_element_type=jnp.float32)  45.6 us
    psum x1, blocking collectives, clipped(): total = lax.psum(local_sq, 'dp')  43.7 us
    unnamed x142, local copies, waits for them, and re-layouts  13.2 us
  transfers between devices with their start and end apart: 46, of which 25 were waited for; matrix products, arithmetic and copies ran while one was open for 16% of the time, Pallas kernels for 0%

profile of v1, /device:TPU:0, one launch (start us, length us, event | category | flops | bytes accessed | tf_op | source)
XLA Modules:
  0.0 439.5 jit_solution(2685980098971562148)
XLA Ops:
  26.9 6.7 %collective-permute-done.37 = bf16[16,8192]{1,0:T(8,128)(2,1)S(1)} collective-permute-done((bf16[16,8192]{1,0:T(8,128)(2,1)}, bf16[16,8192]{1,0:T(8,128)(2,1)S(1)}, u32[]{:S(2)}, u32[]{:S(2)}) %collective-permute-start.37) | collective-permute-done | bytes 262176 | tf_op jit(solution)/shard_map/ppermute | solution.py:79
  35.3 7.0 %collective-permute-done.38 = bf16[16,8192]{1,0:T(8,128)(2,1)S(1)} collective-permute-done((bf16[16,8192]{1,0:T(8,128)(2,1)S(1)}, bf16[16,8192]{1,0:T(8,128)(2,1)S(1)}, u32[]{:S(2)}, u32[]{:S(2)}) %collective-permute-start.38) | collective-permute-done | bytes 262176 | tf_op jit(solution)/shard_map/ppermute | solution.py:79
  45.5 6.9 %collective-permute-done.1 = bf16[16,8192]{1,0:T(8,128)(2,1)S(1)} collective-permute-done((bf16[16,8192]{1,0:T(8,128)(2,1)S(1)}, bf16[16,8192]{1,0:T(8,128)(2,1)S(1)}, u32[]{:S(2)}, u32[]{:S(2)}) %collective-permute-start.1) | collective-permute-done | bytes 262176 | tf_op jit(solution)/shard_map/ppermute | solution.py:79
  52.9 8.1 %collective-permute-done.2 = bf16[16,8192]{1,0:T(8,128)(2,1)S(1)} collective-permute-done((bf16[16,8192]{1,0:T(8,128)(2,1)S(1)}, bf16[16,8192]{1,0:T(8,128)(2,1)S(1)}, u32[]{:S(2)}, u32[]{:S(2)}) %collective-permute-start.2) | collective-permute-done | bytes 262176 | tf_op jit(solution)/shard_map/ppermute | solution.py:79
  64.0 12.9 %collective-permute-done.23 = bf16[32,8192]{1,0:T(8,128)(2,1)S(1)} collective-permute-done((bf16[32,8192]{1,0:T(8,128)(2,1)S(1)}, bf16[32,8192]{1,0:T(8,128)(2,1)S(1)}, u32[]{:S(2)}, u32[]{:S(2)}) %collective-permute-start.23) | collective-permute-done | bytes 524320 | tf_op jit(solution)/shard_map/ppermute | solution.py:79
  77.0 13.7 %collective-permute-done.24 = bf16[32,8192]{1,0:T(8,128)(2,1)S(1)} collective-permute-done((bf16[32,8192]{1,0:T(8,128)(2,1)S(1)}, bf16[32,8192]{1,0:T(8,128)(2,1)S(1)}, u32[]{:S(2)}, u32[]{:S(2)}) %collective-permute-start.24) | collective-permute-done | bytes 524320 | tf_op jit(solution)/shard_map/ppermute | solution.py:79
  94.5 12.1 %collective-permute-done.29 = bf16[32,8192]{1,0:T(8,128)(2,1)S(1)} collective-permute-done((bf16[32,8192]{1,0:T(8,128)(2,1)S(1)}, bf16[32,8192]{1,0:T(8,128)(2,1)S(1)}, u32[]{:S(2)}, u32[]{:S(2)}) %collective-permute-start.29) | collective-permute-done | bytes 524320 | tf_op jit(solution)/shard_map/ppermute | solution.py:79
  107.5 12.9 %collective-permute-done.30 = bf16[32,8192]{1,0:T(8,128)(2,1)S(1)} collective-permute-done((bf16[32,8192]{1,0:T(8,128)(2,1)S(1)}, bf16[32,8192]{1,0:T(8,128)(2,1)S(1)}, u32[]{:S(2)}, u32[]{:S(2)}) %collective-permute-start.30) | collective-permute-done | bytes 524320 | tf_op jit(solution)/shard_map/ppermute | solution.py:79
  131.6 17.4 %collective-permute-done.39 = bf16[64,8192]{1,0:T(8,128)(2,1)S(1)} collective-permute-done((bf16[64,8192]{1,0:T(8,128)(2,1)S(1)}, bf16[64,8192]{1,0:T(8,128)(2,1)S(1)}, u32[]{:S(2)}, u32[]{:S(2)}) %collective-permute-start.39) | collective-permute-done | bytes 1048608 | tf_op jit(solution)/shard_map/ppermute | solution.py:79
  150.6 20.5 %collective-permute-done.3 = bf16[64,8192]{1,0:T(8,128)(2,1)S(1)} collective-permute-done((bf16[64,8192]{1,0:T(8,128)(2,1)S(1)}, bf16[64,8192]{1,0:T(8,128)(2,1)S(1)}, u32[]{:S(2)}, u32[]{:S(2)}) %collective-permute-start.3) | collective-permute-done | bytes 1048608 | tf_op jit(solution)/shard_map/ppermute | solution.py:79
  188.2 9.9 %collective-permute-done.16 = bf16[64,8192]{1,0:T(8,128)(2,1)S(1)} collective-permute-done((bf16[64,8192]{1,0:T(8,128)(2,1)}, bf16[64,8192]{1,0:T(8,128)(2,1)S(1)}, u32[]{:S(2)}, u32[]{:S(2)}) %collective-permute-start.16) | collective-permute-done | bytes 1048608 | tf_op jit(solution)/shard_map/ppermute | solution.py:79
  205.7 18.0 %collective-permute-done.18 = bf16[64,8192]{1,0:T(8,128)(2,1)S(1)} collective-permute-done((bf16[64,8192]{1,0:T(8,128)(2,1)}, bf16[64,8192]{1,0:T(8,128)(2,1)S(1)}, u32[]{:S(2)}, u32[]{:S(2)}) %collective-permute-start.18) | collective-permute-done | bytes 1048608 | tf_op jit(solution)/shard_map/ppermute | solution.py:79
  232.5 4.8 %fusion.67 = (bf16[64,8192]{1,0:T(8,128)(2,1)}, f32[64,8192]{1,0:T(8,128)}) fusion(bf16[16,8192]{1,0:T(8,128)(2,1)} %copy-done.63, bf16[16,8192]{1,0:T(8,128)(2,1)} %copy-done.62, bf16[16,8192]{1,0:T(8,128)(2,1)} %copy-done.61, bf16[16,8192]{1,0:T(8,128)(2,1)} %get-tuple-element.33, bf16[64,8192]{1,0:T(8,128)(2,1)} %copy-done.14, ...), kind=kOutput, calls=%fused_computation.144 | convolution fusion | flops 143659008 | bytes 7340033 | tf_op jit(solution)/shard_map/dot_general | solution.py:11
  237.3 11.6 %collective-permute-done.34 = bf16[64,8192]{1,0:T(8,128)(2,1)} collective-permute-done((bf16[64,8192]{1,0:T(8,128)(2,1)}, bf16[64,8192]{1,0:T(8,128)(2,1)}, u32[]{:S(2)}, u32[]{:S(2)}) %collective-permute-start.34) | collective-permute-done | bytes 1048608 | tf_op jit(solution)/shard_map/ppermute | solution.py:79
  253.5 22.4 %collective-permute-done.8 = bf16[64,8192]{1,0:T(8,128)(2,1)S(1)} collective-permute-done((bf16[64,8192]{1,0:T(8,128)(2,1)}, bf16[64,8192]{1,0:T(8,128)(2,1)S(1)}, u32[]{:S(2)}, u32[]{:S(2)}) %collective-permute-start.8) | collective-permute-done | bytes 1048608 | tf_op jit(solution)/shard_map/ppermute | solution.py:79
  277.7 21.2 %collective-permute-done.42 = bf16[64,8192]{1,0:T(8,128)(2,1)S(1)} collective-permute-done((bf16[64,8192]{1,0:T(8,128)(2,1)S(1)}, bf16[64,8192]{1,0:T(8,128)(2,1)S(1)}, u32[]{:S(2)}, u32[]{:S(2)}) %collective-permute-start.42) | collective-permute-done | bytes 1048608 | tf_op jit(solution)/shard_map/ppermute | solution.py:79
  306.6 6.4 %collective-permute-done.10 = bf16[16,8192]{1,0:T(8,128)(2,1)S(1)} collective-permute-done((bf16[16,8192]{1,0:T(8,128)(2,1)S(1)}, bf16[16,8192]{1,0:T(8,128)(2,1)S(1)}, u32[]{:S(2)}, u32[]{:S(2)}) %collective-permute-start.10) | collective-permute-done | bytes 262176 | tf_op jit(solution)/shard_map/ppermute | solution.py:79
  313.8 7.5 %collective-permute-done.11 = bf16[16,8192]{1,0:T(8,128)(2,1)S(1)} collective-permute-done((bf16[16,8192]{1,0:T(8,128)(2,1)S(1)}, bf16[16,8192]{1,0:T(8,128)(2,1)S(1)}, u32[]{:S(2)}, u32[]{:S(2)}) %collective-permute-start.11) | collective-permute-done | bytes 262176 | tf_op jit(solution)/shard_map/ppermute | solution.py:79
  334.1 7.2 %collective-permute-done.20 = bf16[16,8192]{1,0:T(8,128)(2,1)S(1)} collective-permute-done((bf16[16,8192]{1,0:T(8,128)(2,1)}, bf16[16,8192]{1,0:T(8,128)(2,1)S(1)}, u32[]{:S(2)}, u32[]{:S(2)}) %collective-permute-start.20) | collective-permute-done | bytes 262176 | tf_op jit(solution)/shard_map/ppermute | solution.py:79
  342.3 7.7 %collective-permute-done.21 = bf16[16,8192]{1,0:T(8,128)(2,1)S(1)} collective-permute-done((bf16[16,8192]{1,0:T(8,128)(2,1)}, bf16[16,8192]{1,0:T(8,128)(2,1)S(1)}, u32[]{:S(2)}, u32[]{:S(2)}) %collective-permute-start.21) | collective-permute-done | bytes 262176 | tf_op jit(solution)/shard_map/ppermute | solution.py:79
  367.1 11.8 %collective-permute-done.45 = bf16[64,8192]{1,0:T(8,128)(2,1)S(1)} collective-permute-done((bf16[64,8192]{1,0:T(8,128)(2,1)S(1)}, bf16[64,8192]{1,0:T(8,128)(2,1)S(1)}, u32[]{:S(2)}, u32[]{:S(2)}) %collective-permute-start.45) | collective-permute-done | bytes 1048608 | tf_op jit(solution)/shard_map/ppermute | solution.py:79
  379.8 4.9 %multiply_reduce_fusion = (f32[]{:T(128)}, f32[64,8192]{1,0:T(8,128)}) fusion(bf16[64,8192]{1,0:T(8,128)(2,1)} %copy-done.59, bf16[64,8192]{1,0:T(8,128)(2,1)} %collective-permute-done.43, bf16[16,8192]{1,0:T(8,128)(2,1)S(1)} %copy-done.39, bf16[16,8192]{1,0:T(8,128)(2,1)S(1)} %copy-done.37, bf16[16,8192]{1,0:T(8,128)(2,1)S(1)} %copy-done.35, ...), kind=kOutput, calls=%fused_computation.29 | convolution fusion | flops 145756160 | bytes 7340036 | tf_op jit(solution)/shard_map/dot_general | solution.py:11
  390.3 43.7 %psum.7 = f32[]{:T(128)} all-reduce(f32[]{:T(128)S(6)} %add.99), channel_id=1, replica_groups=mesh['parts'=2,'dp'=16] {'dp'}, use_global_device_ids=true, to_apply=%region_5.6 | all-reduce | flops 1 | bytes 8 | tf_op jit(solution)/shard_map/psum | solution.py:26
  434.7 4.8 %multiply_bitcast_fusion = (f32[1,64,8192]{2,1,0:T(8,128)}, f32[1,64,8192]{2,1,0:T(8,128)}) fusion(f32[64,8192]{1,0:T(8,128)} %get-tuple-element.69, f32[]{:T(128)S(6)} %min_shard_map.3, f32[64,8192]{1,0:T(8,128)} %get-tuple-element.65), kind=kLoop, calls=%fused_computation.27 | loop fusion | flops 1048576 | bytes 8388612 | tf_op jit(solution)/shard_map/broadcast_in_dim | solution.py:30
  (272 shorter events, 135.6 us)
Async XLA Ops:
  0.6 122.3 %collective-permute-start.4 = (bf16[64,8192]{1,0:T(8,128)(2,1)}, bf16[64,8192]{1,0:T(8,128)(2,1)}, u32[]{:S(2)}, u32[]{:S(2)}) collective-permute-start(bf16[64,8192]{1,0:T(8,128)(2,1)} %bitcast.59), channel_id=1, source_target_pairs={{0,4},{1,5},{2,6},{3,7},{4,0},{5,1},{6,2},{7,3},{8,12},{9,13},{10,... | collective-permute-start | bytes 3145736 | tf_op jit(solution)/shard_map/ppermute | solution.py:79
  3.7 146.1 %collective-permute-start.15 = (bf16[64,8192]{1,0:T(8,128)(2,1)}, bf16[64,8192]{1,0:T(8,128)(2,1)}, u32[]{:S(2)}, u32[]{:S(2)}) collective-permute-start(bf16[64,8192]{1,0:T(8,128)(2,1)} %bitcast.60), channel_id=1, source_target_pairs={{4,8},{5,9},{6,10},{7,11},{8,4},{9,5},{10,6},{11,7},{20,24},{21,25... | collective-permute-start | bytes 3145736 | tf_op jit(solution)/shard_map/ppermute | solution.py:79
  5.4 121.9 %collective-permute-start.6 = (bf16[64,8192]{1,0:T(8,128)(2,1)}, bf16[64,8192]{1,0:T(8,128)(2,1)}, u32[]{:S(2)}, u32[]{:S(2)}) collective-permute-start(bf16[64,8192]{1,0:T(8,128)(2,1)} %bitcast.57), channel_id=1, source_target_pairs={{0,4},{1,5},{2,6},{3,7},{4,0},{5,1},{6,2},{7,3},{8,12},{9,13},{10,... | collective-permute-start | bytes 3145736 | tf_op jit(solution)/shard_map/ppermute | solution.py:79
  8.9 165.7 %collective-permute-start.17 = (bf16[64,8192]{1,0:T(8,128)(2,1)}, bf16[64,8192]{1,0:T(8,128)(2,1)}, u32[]{:S(2)}, u32[]{:S(2)}) collective-permute-start(bf16[64,8192]{1,0:T(8,128)(2,1)} %bitcast.58), channel_id=1, source_target_pairs={{4,8},{5,9},{6,10},{7,11},{8,4},{9,5},{10,6},{11,7},{20,24},{21,25... | collective-permute-start | bytes 3145736 | tf_op jit(solution)/shard_map/ppermute | solution.py:79
  120.4 57.6 %collective-permute-start.12 = (bf16[16,8192]{1,0:T(8,128)(2,1)S(1)}, bf16[16,8192]{1,0:T(8,128)(2,1)S(1)}, u32[]{:S(2)}, u32[]{:S(2)}) collective-permute-start(bf16[16,8192]{1,0:T(8,128)(2,1)S(1)} %copy-done.55), channel_id=1, source_target_pairs={{0,1},{1,0},{2,3},{3,2},{4,5},{5,4},{6,7},{7,6},{8,9},{9,8},{10,11... | collective-permute-start | bytes 786440 | tf_op jit(solution)/shard_map/ppermute | solution.py:79
  122.9 26.1 %collective-permute-start.39 = (bf16[64,8192]{1,0:T(8,128)(2,1)S(1)}, bf16[64,8192]{1,0:T(8,128)(2,1)S(1)}, u32[]{:S(2)}, u32[]{:S(2)}) collective-permute-start(bf16[64,8192]{1,0:T(8,128)(2,1)S(1)} %pad_maximum_fusion.7), channel_id=1, source_target_pairs={{0,4},{1,5},{2,6},{3,7},{12,8},{13,9},{14,10},{15,11},{16,20},{17,... | collective-permute-start | bytes 3145736 | tf_op jit(solution)/shard_map/ppermute | solution.py:79
  127.4 43.8 %collective-permute-start.3 = (bf16[64,8192]{1,0:T(8,128)(2,1)S(1)}, bf16[64,8192]{1,0:T(8,128)(2,1)S(1)}, u32[]{:S(2)}, u32[]{:S(2)}) collective-permute-start(bf16[64,8192]{1,0:T(8,128)(2,1)S(1)} %pad_maximum_fusion), channel_id=1, source_target_pairs={{0,4},{1,5},{2,6},{3,7},{12,8},{13,9},{14,10},{15,11},{16,20},{17,... | collective-permute-start | bytes 3145736 | tf_op jit(solution)/shard_map/ppermute | solution.py:79
  149.0 23.5 %collective-permute-start.5 = (bf16[64,8192]{1,0:T(8,128)(2,1)}, bf16[64,8192]{1,0:T(8,128)(2,1)S(1)}, u32[]{:S(2)}, u32[]{:S(2)}) collective-permute-start(bf16[64,8192]{1,0:T(8,128)(2,1)} %collective-permute-done.4), channel_id=1, source_target_pairs={{4,8},{5,9},{6,10},{7,11},{8,4},{9,5},{10,6},{11,7},{20,24},{21,25... | collective-permute-start | bytes 3145736 | tf_op jit(solution)/shard_map/ppermute | solution.py:79
  149.9 24.8 %collective-permute-start.7 = (bf16[64,8192]{1,0:T(8,128)(2,1)}, bf16[64,8192]{1,0:T(8,128)(2,1)S(1)}, u32[]{:S(2)}, u32[]{:S(2)}) collective-permute-start(bf16[64,8192]{1,0:T(8,128)(2,1)} %collective-permute-done.6), channel_id=1, source_target_pairs={{4,8},{5,9},{6,10},{7,11},{8,4},{9,5},{10,6},{11,7},{20,24},{21,25... | collective-permute-start | bytes 3145736 | tf_op jit(solution)/shard_map/ppermute | solution.py:79
  171.1 27.0 %collective-permute-start.16 = (bf16[64,8192]{1,0:T(8,128)(2,1)}, bf16[64,8192]{1,0:T(8,128)(2,1)S(1)}, u32[]{:S(2)}, u32[]{:S(2)}) collective-permute-start(bf16[64,8192]{1,0:T(8,128)(2,1)} %collective-permute-done.15), channel_id=1, source_target_pairs={{4,0},{5,1},{6,2},{7,3},{8,12},{9,13},{10,14},{11,15},{20,16},{21,... | collective-permute-start | bytes 3145736 | tf_op jit(solution)/shard_map/ppermute | solution.py:79
  174.7 49.0 %collective-permute-start.18 = (bf16[64,8192]{1,0:T(8,128)(2,1)}, bf16[64,8192]{1,0:T(8,128)(2,1)S(1)}, u32[]{:S(2)}, u32[]{:S(2)}) collective-permute-start(bf16[64,8192]{1,0:T(8,128)(2,1)} %collective-permute-done.17), channel_id=1, source_target_pairs={{4,0},{5,1},{6,2},{7,3},{8,12},{9,13},{10,14},{11,15},{20,16},{21,... | collective-permute-start | bytes 3145736 | tf_op jit(solution)/shard_map/ppermute | solution.py:79
  178.0 22.1 %collective-permute-start.31 = (bf16[16,8192]{1,0:T(8,128)(2,1)S(1)}, bf16[16,8192]{1,0:T(8,128)(2,1)S(1)}, u32[]{:S(2)}, u32[]{:S(2)}) collective-permute-start(bf16[16,8192]{1,0:T(8,128)(2,1)S(1)} %copy-done.52), channel_id=1, source_target_pairs={{0,1},{1,0},{2,3},{3,2},{4,5},{5,4},{6,7},{7,6},{8,9},{9,8},{10,11... | collective-permute-start | bytes 786440 | tf_op jit(solution)/shard_map/ppermute | solution.py:79
  181.8 19.4 %collective-permute-start.32 = (bf16[16,8192]{1,0:T(8,128)(2,1)S(1)}, bf16[16,8192]{1,0:T(8,128)(2,1)S(1)}, u32[]{:S(2)}, u32[]{:S(2)}) collective-permute-start(bf16[16,8192]{1,0:T(8,128)(2,1)S(1)} %copy-done.51), channel_id=1, source_target_pairs={{0,2},{1,3},{2,0},{3,1},{4,6},{5,7},{6,4},{7,5},{8,10},{9,11},{10,... | collective-permute-start | bytes 786440 | tf_op jit(solution)/shard_map/ppermute | solution.py:79
  198.1 154.2 %collective-permute-start.25 = (bf16[32,8192]{1,0:T(8,128)(2,1)}, bf16[32,8192]{1,0:T(8,128)(2,1)}, u32[]{:S(2)}, u32[]{:S(2)}) collective-permute-start(bf16[32,8192]{1,0:T(8,128)(2,1)} %get-tuple-element.13), channel_id=1, source_target_pairs={{0,1},{1,0},{2,3},{3,2},{4,5},{5,4},{6,7},{7,6},{8,9},{9,8},{10,11... | collective-permute-start | bytes 1572872 | tf_op jit(solution)/shard_map/ppermute | solution.py:79
  200.1 157.4 %collective-permute-start.26 = (bf16[32,8192]{1,0:T(8,128)(2,1)}, bf16[32,8192]{1,0:T(8,128)(2,1)}, u32[]{:S(2)}, u32[]{:S(2)}) collective-permute-start(bf16[32,8192]{1,0:T(8,128)(2,1)} %get-tuple-element.14), channel_id=1, source_target_pairs={{0,2},{1,3},{2,0},{3,1},{4,6},{5,7},{6,4},{7,5},{8,10},{9,11},{10,... | collective-permute-start | bytes 1572872 | tf_op jit(solution)/shard_map/ppermute | solution.py:79
  201.2 159.9 %collective-permute-start.27 = (bf16[32,8192]{1,0:T(8,128)(2,1)}, bf16[32,8192]{1,0:T(8,128)(2,1)}, u32[]{:S(2)}, u32[]{:S(2)}) collective-permute-start(bf16[32,8192]{1,0:T(8,128)(2,1)} %get-tuple-element.12), channel_id=1, source_target_pairs={{0,3},{1,2},{2,1},{3,0},{4,7},{5,6},{6,5},{7,4},{8,11},{9,10},{10,... | collective-permute-start | bytes 1572872 | tf_op jit(solution)/shard_map/ppermute | solution.py:79
  201.9 99.6 %collective-permute-start.40 = (bf16[64,8192]{1,0:T(8,128)(2,1)}, bf16[64,8192]{1,0:T(8,128)(2,1)}, u32[]{:S(2)}, u32[]{:S(2)}) collective-permute-start(bf16[64,8192]{1,0:T(8,128)(2,1)} %convolution_convert_fusion.5), channel_id=1, source_target_pairs={{4,8},{5,9},{6,10},{7,11},{8,4},{9,5},{10,6},{11,7},{20,24},{21,25... | collective-permute-start | bytes 3145736 | tf_op jit(solution)/shard_map/ppermute | solution.py:79
  223.7 25.3 %collective-permute-start.34 = (bf16[64,8192]{1,0:T(8,128)(2,1)}, bf16[64,8192]{1,0:T(8,128)(2,1)}, u32[]{:S(2)}, u32[]{:S(2)}) collective-permute-start(bf16[64,8192]{1,0:T(8,128)(2,1)} %get-tuple-element.62), channel_id=1, source_target_pairs={{0,4},{1,5},{2,6},{3,7},{12,8},{13,9},{14,10},{15,11},{16,20},{17,... | collective-permute-start | bytes 3145736 | tf_op jit(solution)/shard_map/ppermute | solution.py:79
  249.0 26.9 %collective-permute-start.8 = (bf16[64,8192]{1,0:T(8,128)(2,1)}, bf16[64,8192]{1,0:T(8,128)(2,1)S(1)}, u32[]{:S(2)}, u32[]{:S(2)}) collective-permute-start(bf16[64,8192]{1,0:T(8,128)(2,1)} %slice.110), channel_id=1, source_target_pairs={{4,0},{5,1},{6,2},{7,3},{8,12},{9,13},{10,14},{11,15},{20,16},{21,... | collective-permute-start | bytes 3145736 | tf_op jit(solution)/shard_map/ppermute | solution.py:79
  275.9 23.0 %collective-permute-start.42 = (bf16[64,8192]{1,0:T(8,128)(2,1)S(1)}, bf16[64,8192]{1,0:T(8,128)(2,1)S(1)}, u32[]{:S(2)}, u32[]{:S(2)}) collective-permute-start(bf16[64,8192]{1,0:T(8,128)(2,1)S(1)} %copy-done.60), channel_id=1, source_target_pairs={{0,4},{1,5},{2,6},{3,7},{12,8},{13,9},{14,10},{15,11},{16,20},{17,... | collective-permute-start | bytes 3145736 | tf_op jit(solution)/shard_map/ppermute | solution.py:79
  298.9 27.8 %collective-permute-start.44 = (bf16[64,8192]{1,0:T(8,128)(2,1)S(1)}, bf16[64,8192]{1,0:T(8,128)(2,1)S(1)}, u32[]{:S(2)}, u32[]{:S(2)}) collective-permute-start(bf16[64,8192]{1,0:T(8,128)(2,1)S(1)} %copy-done.17), channel_id=1, source_target_pairs={{4,8},{5,9},{6,10},{7,11},{8,4},{9,5},{10,6},{11,7},{20,24},{21,25... | collective-permute-start | bytes 3145736 | tf_op jit(solution)/shard_map/ppermute | solution.py:79
  321.3 41.6 %collective-permute-start.41 = (bf16[64,8192]{1,0:T(8,128)(2,1)}, bf16[64,8192]{1,0:T(8,128)(2,1)}, u32[]{:S(2)}, u32[]{:S(2)}) collective-permute-start(bf16[64,8192]{1,0:T(8,128)(2,1)} %fusion.2), channel_id=1, source_target_pairs={{0,4},{1,5},{2,6},{3,7},{4,0},{5,1},{6,2},{7,3},{8,12},{9,13},{10,... | collective-permute-start | bytes 3145736 | tf_op jit(solution)/shard_map/ppermute | solution.py:79
  352.3 26.5 %collective-permute-start.45 = (bf16[64,8192]{1,0:T(8,128)(2,1)S(1)}, bf16[64,8192]{1,0:T(8,128)(2,1)S(1)}, u32[]{:S(2)}, u32[]{:S(2)}) collective-permute-start(bf16[64,8192]{1,0:T(8,128)(2,1)S(1)} %copy-done.57), channel_id=1, source_target_pairs={{0,4},{1,5},{2,6},{3,7},{4,0},{5,1},{6,2},{7,3},{8,12},{9,13},{10,... | collective-permute-start | bytes 3145736 | tf_op jit(solution)/shard_map/ppermute | solution.py:79
  357.5 22.3 %collective-permute-start.43 = (bf16[64,8192]{1,0:T(8,128)(2,1)S(1)}, bf16[64,8192]{1,0:T(8,128)(2,1)}, u32[]{:S(2)}, u32[]{:S(2)}) collective-permute-start(bf16[64,8192]{1,0:T(8,128)(2,1)S(1)} %copy-done.16), channel_id=1, source_target_pairs={{4,8},{5,9},{6,10},{7,11},{8,4},{9,5},{10,6},{11,7},{20,24},{21,25... | collective-permute-start | bytes 3145736 | tf_op jit(solution)/shard_map/ppermute | solution.py:79
  (86 other events, 1460.4 us)

commit v2 on v1

v2 whole, which is shorter than its diff:
```python
import functools

import jax
import jax.numpy as jnp
from jax import lax
from jax.experimental import pallas as pl
from jax.experimental.pallas import tpu as pltpu
from jax.sharding import PartitionSpec as P

BF16, F32 = jnp.bfloat16, jnp.float32
ROWS_OF = (((1,), (1,)), ((), ()))
OUTER = (((0,), (0,)), ((), ()))
INNER = (((1,), (0,)), ((), ()))
ANY = pl.BlockSpec(memory_space=pl.ANY)
VMEM_BYTES = 50 * 2**20


def dot32(a, b, dims=INNER):
    return lax.dot_general(a, b, dims, preferred_element_type=F32)


def route(token_task_index, task_slot_lookup, ndevices):
    pool = task_slot_lookup.shape[0]
    task_hot = (token_task_index == jnp.arange(pool, dtype=jnp.int32)[None, :]).astype(jnp.int32)
    owner = jnp.sum(task_hot * task_slot_lookup[None, :], axis=1)
    owner_hot = (owner[:, None] == jnp.arange(ndevices, dtype=jnp.int32)[None, :]).astype(jnp.int32)
    before = jnp.cumsum(owner_hot, axis=0) - owner_hot
    position = jnp.sum(before * owner_hot, axis=1)
    return owner, position


def clipped(raw_down, raw_up, ndevices):
    local_sq = jnp.sum(raw_down * raw_down) + jnp.sum(raw_up * raw_up)
    total = lax.psum(local_sq, "dp")
    norm = jnp.sqrt(total + 1e-06)
    limit = jnp.sqrt(jnp.float32(2 * raw_down.shape[0] * raw_down.shape[1] * ndevices))
    factor = jnp.minimum(jnp.float32(1.0), limit / norm)
    return (raw_down * factor)[None], (raw_up * factor)[None]


def move_tokens(acts, cotan, token_task_index, task_slot_lookup, pool_down_factors, pool_up_factors):
    ndevices = lax.axis_size("dp")
    tokens, width = acts.shape
    capacity = 2 * ((tokens + ndevices - 1) // ndevices)
    slots = ndevices * capacity
    owner, position = route(token_task_index, task_slot_lookup, ndevices)
    dest = owner * capacity + position
    placed = (jnp.arange(slots, dtype=jnp.int32)[:, None] == dest[None, :]).astype(BF16)

    def exchange(rows):
        rows = rows.reshape(ndevices, capacity, width)
        return lax.all_to_all(rows, "dp", split_axis=0, concat_axis=0, tiled=True).reshape(slots, width)

    down, up = pool_down_factors[0], pool_up_factors[0]
    rows_x = exchange(dot32(placed, acts).astype(BF16))
    rows_g = exchange(dot32(placed, cotan).astype(BF16))
    hidden = dot32(rows_x, down, ROWS_OF).astype(BF16)
    inner = dot32(rows_g, up, ROWS_OF).astype(BF16)
    returned = exchange(dot32(inner, down).astype(BF16))
    grad_acts = dot32(placed, returned, OUTER).astype(BF16)
    raw_up = dot32(hidden, rows_g, OUTER)
    raw_down = dot32(inner, rows_x, OUTER)
    return (grad_acts,) + clipped(raw_down, raw_up, ndevices)


def kernel_params(semantics=("arbitrary",)):
    return pltpu.CompilerParams(dimension_semantics=semantics, vmem_limit_bytes=VMEM_BYTES)


def cost(flops, nbytes):
    return pl.CostEstimate(flops=flops, bytes_accessed=nbytes, transcendentals=0)


def pack(place, acts, cotan, plane):
    rows, (tokens, width) = place.shape[0] // plane, acts.shape
    tile = min(width, 1024)

    def body(place_ref, x_ref, g_ref, *out_refs):
        for k, ref in enumerate((x_ref, g_ref)):
            moved = dot32(place_ref[...], ref[...]).astype(BF16)
            for m in range(plane):
                out_refs[m][k] = moved[m * rows:(m + 1) * rows]

    rows_spec = pl.BlockSpec((tokens, tile), lambda i: (0, i))
    return pl.pallas_call(
        body,
        grid=(width // tile,),
        in_specs=[pl.BlockSpec(place.shape, lambda i: (0, 0)), rows_spec, rows_spec],
        out_specs=[pl.BlockSpec((2, rows, tile), lambda i: (0, 0, i))] * plane,
        out_shape=[jax.ShapeDtypeStruct((2, rows, width), BF16)] * plane,
        compiler_params=kernel_params(),
        cost_estimate=cost(4 * place.shape[0] * tokens * width, 4 * (tokens + place.shape[0]) * width),
    )(place, acts, cotan)


def unpack(place, blocks, tokens):
    width = blocks[0].shape[1]
    tile = min(width, 1024)
    total = place.shape[0]

    def body(place_ref, *refs):
        rows = jnp.concatenate([ref[...] for ref in refs[:-1]], axis=0)
        refs[-1][...] = dot32(place_ref[...], rows, OUTER).astype(BF16)

    return pl.pallas_call(
        body,
        grid=(width // tile,),
        in_specs=[pl.BlockSpec(place.shape, lambda i: (0, 0))]
        + [pl.BlockSpec((b.shape[0], tile), lambda i: (0, i)) for b in blocks],
        out_specs=pl.BlockSpec((tokens, tile), lambda i: (0, i)),
        out_shape=jax.ShapeDtypeStruct((tokens, width), BF16),
        compiler_params=kernel_params(),
        cost_estimate=cost(2 * total * tokens * width, 2 * (tokens + total) * width),
    )(place, *blocks)


def far_groups(is_end, stage, mids, far, outer, crossed, capacity):
    plane = len(stage)
    _, rank, width = far.shape
    block = plane * capacity
    tile = min(width, 1024)
    tiles = width // tile

    def body(end_ref, *refs):
        stage_in, (mids_in, far_in, outer_in, crossed_in) = refs[:plane], refs[plane:plane + 4]
        sum3_ref, sum2_ref, dx_ref, inner3_ref, inner2_ref = refs[plane + 4:plane + 9]
        tokens, ends, far_w, near_w, hidden3, hidden2, sems = refs[plane + 9:]
        step = pl.program_id(0)

        def copies(i):
            cut = pl.ds(i * tile, tile)
            pairs = [(stage_in[m], tokens.at[m]) for m in range(plane)] + [(mids_in, ends), (far_in, far_w)]
            return [
                pltpu.make_async_copy(src.at[:, :, cut], dst.at[:, :, cut], sems.at[i, n])
                for n, (src, dst) in enumerate(pairs)
            ]

        def near_copy(src, i):
            cut = pl.ds(i * tile, tile)
            return pltpu.make_async_copy(src.at[:, :, cut], near_w.at[:, :, cut], sems.at[i, plane + 2])

        def rows3(k, cut):
            return jnp.concatenate([tokens[m, k, :capacity, cut] for m in range(plane)] + [ends[k, :, cut]], axis=0)

        def rows2(k, cut):
            return jnp.concatenate([tokens[m, k, capacity:, cut] for m in range(plane)], axis=0)

        @pl.when(step == 0)
        def _():
            for i in range(tiles):
                for c in copies(i):
                    c.start()

                @pl.when(end_ref[0] == 1)
                def _():
                    near_copy(outer_in, i).start()

                @pl.when(end_ref[0] != 1)
                def _():
                    near_copy(crossed_in, i).start()

            sums = [jnp.zeros((2 * block, rank), F32)] * 2 + [jnp.zeros((block, rank), F32)] * 2
            for i in range(tiles):
                for c in copies(i):
                    c.wait()
                near_copy(outer_in, i).wait()
                cut = pl.ds(i * tile, tile)
                for k in range(2):
                    sums[k] += dot32(rows3(k, cut), far_w[k, :, cut], ROWS_OF)
                    sums[2 + k] += dot32(rows2(k, cut), near_w[k, :, cut], ROWS_OF)
            hidden3[...] = sums[0].astype(BF16)
            inner3_ref[...] = sums[1].astype(BF16)
            hidden2[...] = sums[2].astype(BF16)
            inner2_ref[...] = sums[3].astype(BF16)

        cut = pl.ds(pl.multiple_of(step * tile, tile), tile)
        sum3_ref[0] = dot32(hidden3[...], rows3(1, cut), OUTER).astype(BF16)
        sum3_ref[1] = dot32(inner3_ref[...], rows3(0, cut), OUTER).astype(BF16)
        sum2_ref[0] = dot32(hidden2[...], rows2(1, cut), OUTER).astype(BF16)
        sum2_ref[1] = dot32(inner2_ref[...], rows2(0, cut), OUTER).astype(BF16)
        dx_ref[...] = dot32(inner3_ref[block:], far_w[0, :, cut]).astype(BF16)

    pair = jax.ShapeDtypeStruct((2, rank, width), BF16)
    pair_spec = pl.BlockSpec((2, rank, tile), lambda i: (0, 0, i))
    return pl.pallas_call(
        body,
        grid=(tiles,),
        in_specs=[pl.BlockSpec(memory_space=pltpu.SMEM)] + [ANY] * (plane + 4),
        out_specs=[
            pair_spec,
            pair_spec,
            pl.BlockSpec((block, tile), lambda i: (0, i)),
            pl.BlockSpec((2 * block, rank), lambda i: (0, 0)),
            pl.BlockSpec((block, rank), lambda i: (0, 0)),
        ],
        out_shape=[
            pair,
            pair,
            jax.ShapeDtypeStruct((block, width), BF16),
            jax.ShapeDtypeStruct((2 * block, rank), BF16),
            jax.ShapeDtypeStruct((block, rank), BF16),
        ],
        scratch_shapes=[
            pltpu.VMEM((plane, 2, 2 * capacity, width), BF16),
            pltpu.VMEM((2, block, width), BF16),
            pltpu.VMEM((2, rank, width), BF16),
            pltpu.VMEM((2, rank, width), BF16),
            pltpu.VMEM((2 * block, rank), BF16),
            pltpu.VMEM((block, rank), BF16),
            pltpu.SemaphoreType.DMA((tiles, plane + 3)),
        ],
        compiler_params=kernel_params(),
        cost_estimate=cost(26 * block * rank * width, 38 * block * width),
    )(is_end, *stage, mids, far, outer, crossed)


def near_groups(is_end, stage, pair, down, up, far, outer, crossed, inner3, inner2, capacity):
    plane = len(stage)
    _, rank, width = far.shape
    block = plane * capacity
    tile = min(width, 1024)
    tiles = width // tile

    def body(end_ref, *refs):
        stage_in, refs = refs[:plane], refs[plane:]
        pair_in, down_in, up_in, far_in, outer_in, crossed_in, inner3, inner2 = refs[:8]
        dx_refs, (sum1_ref, sum0_ref) = refs[8:8 + plane], refs[8 + plane:10 + plane]
        tokens, pair_w, own_w, dx_w, hidden1, inner1, hidden0, inner0, sems = refs[10 + plane:]
        step = pl.program_id(0)

        def copies(i):
            cut = pl.ds(i * tile, tile)
            pairs = [(stage_in[m].at[:, :, cut], tokens.at[m, :, :, cut]) for m in range(plane)] + [
                (pair_in.at[:, :, cut], pair_w.at[:, :, cut]),
                (down_in.at[:, cut], own_w.at[0, :, cut]),
                (up_in.at[:, cut], own_w.at[1, :, cut]),
                (far_in.at[0, :, cut], dx_w.at[0, :, cut]),
            ]
            return [pltpu.make_async_copy(src, dst, sems.at[i, n]) for n, (src, dst) in enumerate(pairs)]

        def near_copy(src, i):
            cut = pl.ds(i * tile, tile)
            return pltpu.make_async_copy(src.at[0, :, cut], dx_w.at[1, :, cut], sems.at[i, plane + 4])

        def rows1(k, cut):
            return jnp.concatenate([tokens[m, k, :capacity, cut] for m in range(plane)], axis=0)

        def rows0(k, cut):
            return jnp.concatenate([tokens[m, k, capacity:, cut] for m in range(plane)], axis=0)

        @pl.when(step == 0)
        def _():
            for i in range(tiles):
                for c in copies(i):
                    c.start()

                @pl.when(end_ref[0] == 1)
                def _():
                    near_copy(outer_in, i).start()

                @pl.when(end_ref[0] != 1)
                def _():
                    near_copy(crossed_in, i).start()

            sums = [jnp.zeros((block, rank), F32)] * 4
            for i in range(tiles):
                for c in copies(i):
                    c.wait()
                near_copy(outer_in, i).wait()
                cut = pl.ds(i * tile, tile)
                for k in range(2):
                    sums[k] += dot32(rows1(k, cut), pair_w[k, :, cut], ROWS_OF)
                    sums[2 + k] += dot32(rows0(k, cut), own_w[k, :, cut], ROWS_OF)
            for ref, value in zip((hidden1, inner1, hidden0, inner0), sums):
                ref[...] = value.astype(BF16)

        cut = pl.ds(pl.multiple_of(step * tile, tile), tile)
        sum1_ref[0] = dot32(hidden1[...], rows1(1, cut), OUTER)
        sum1_ref[1] = dot32(inner1[...], rows1(0, cut), OUTER)
        sum0_ref[0] = dot32(hidden0[...], rows0(1, cut), OUTER)
        sum0_ref[1] = dot32(inner0[...], rows0(0, cut), OUTER)
        moved = [
            dot32(inner3[:block], dx_w[0, :, cut]),
            dot32(inner2[...], dx_w[1, :, cut]),
            dot32(inner1[...], pair_w[0, :, cut]),
            dot32(inner0[...], own_w[0, :, cut]),
        ]
        for n, dx in enumerate(moved):
            dx = dx.astype(BF16)
            for m in range(plane):
                dx_refs[m][n * capacity:(n + 1) * capacity] = dx[m * capacity:(m + 1) * capacity]

    total = jax.ShapeDtypeStruct((2, rank, width), F32)
    total_spec = pl.BlockSpec((2, rank, tile), lambda i: (0, 0, i))
    whole = [pl.BlockSpec(a.shape, lambda i: (0, 0)) for a in (inner3, inner2)]
    return pl.pallas_call(
        body,
        grid=(tiles,),
        in_specs=[pl.BlockSpec(memory_space=pltpu.SMEM)] + [ANY] * (plane + 6) + whole,
        out_specs=[pl.BlockSpec((4 * capacity, tile), lambda i: (0, i))] * plane + [total_spec] * 2,
        out_shape=[jax.ShapeDtypeStruct((4 * capacity, width), BF16)] * plane + [total] * 2,
        scratch_shapes=[
            pltpu.VMEM((plane, 2, 2 * capacity, width), BF16),
            pltpu.VMEM((2, rank, width), BF16),
            pltpu.VMEM((2, rank, width), BF16),
            pltpu.VMEM((2, rank, width), BF16),
        ]
        + [pltpu.VMEM((block, rank), BF16)] * 4
        + [pltpu.SemaphoreType.DMA((tiles, plane + 5))],
        compiler_params=kernel_params(),
        cost_estimate=cost(24 * block * rank * width, 48 * block * width),
    )(is_end, *stage, pair, down, up, far, outer, crossed, inner3, inner2)


def move_adapters(plane, acts, cotan, token_task_index, task_slot_lookup, pool_down_factors, pool_up_factors):
    ndevices = lax.axis_size("dp")
    tokens, width = acts.shape
    capacity = 2 * ((tokens + ndevices - 1) // ndevices)
    me = lax.axis_index("dp")
    z, column = me // plane, me % plane
    is_end = (z == 0) | (z == 3)
    end_flag = is_end.astype(jnp.int32).reshape(1)

    def planes(pairs):
        return [(a * plane + c, b * plane + c) for a, b in pairs for c in range(plane)]

    swap = planes([(0, 1), (1, 0), (2, 3), (3, 2)])
    cross = planes([(1, 2), (2, 1)])
    outward = planes([(1, 0), (2, 3)])
    inward = planes([(0, 1), (3, 2)])

    def send(array, pairs):
        return lax.ppermute(array, "dp", pairs)

    def in_plane(blocks, among=(0, 1, 2, 3)):
        moved = [blocks[0]]
        for m in range(1, plane):
            pairs = [(i, (i // plane) * plane + ((i % plane) ^ m)) for i in range(ndevices) if i // plane in among]
            moved.append(send(blocks[m], pairs))
        return moved

    down, up = pool_down_factors[0], pool_up_factors[0]
    own = jnp.concatenate([pool_down_factors, pool_up_factors])
    pair = send(own, swap)
    crossed = send(own, cross)

    owner, position = route(token_task_index, task_slot_lookup, ndevices)
    owner_z, turn = owner // plane, (owner % plane) ^ column
    other_mid = jnp.where(z < 2, 2, 1)
    kind = jnp.where(owner_z == z, 0, jnp.where(owner_z == (z ^ 1), 1, jnp.where(owner_z == other_mid, 2, 3)))

    def places(wanted, row, rows):
        hot = jnp.arange(rows, dtype=jnp.int32)[:, None] == row[None, :]
        return (hot & wanted[None, :]).astype(BF16)

    half = 2 * capacity
    place_a = places(kind >= 2, turn * half + (3 - kind) * capacity + position, plane * half)
    place_b = places(kind < 2, turn * half + (1 - kind) * capacity + position, plane * half)
    place_back = places(kind >= 0, turn * 2 * half + (3 - kind) * capacity + position, 2 * plane * half)
    place_ends = places(kind == 3, turn * capacity + position, plane * capacity)

    stage_a = in_plane(pack(place_a, acts, cotan, plane))
    ends = send(jnp.concatenate([b[:, :capacity] for b in stage_a], axis=1), inward)
    packed_b, _ = lax.optimization_barrier((pack(place_b, acts, cotan, plane), stage_a))
    stage_b = in_plane(packed_b)
    outer = send(crossed, outward)
    far = send(pair, cross)

    sum3, sum2, dx_ends, inner3, inner2 = far_groups(end_flag, stage_a, ends, far, outer, crossed, capacity)
    sum3 = send(sum3, cross)
    sum2_in = send(sum2, inward)
    dx_ends = send(dx_ends, outward)

    *dx, sum1, sum0 = near_groups(
        end_flag, stage_b, pair, down, up, far, outer, crossed, inner3, inner2, capacity
    )
    sum2 = send((sum2.astype(F32) + sum2_in.astype(F32)).astype(BF16), cross)
    sum1 = send((sum1 + sum3.astype(F32)).astype(BF16), swap)

    back = in_plane(dx)
    back_ends = in_plane([dx_ends[m * capacity:(m + 1) * capacity] for m in range(plane)], (0, 3))
    grad_acts = unpack(jnp.concatenate([place_back, place_ends]), back + back_ends, tokens)
    raw_up, raw_down = (sum0[k] + sum2[k].astype(F32) + sum1[k].astype(F32) for k in range(2))
    return (grad_acts,) + clipped(raw_down, raw_up, ndevices)


def solution(mesh):
    ndevices = mesh.shape["dp"]
    plane = 1
    while (2 * plane) ** 2 <= ndevices:
        plane *= 2

    def per_device(*arrays):
        if ndevices == 4 * plane:
            return move_adapters(plane, *arrays)
        return move_tokens(*arrays)

    rows, pools = P(("parts", "dp"), None), P(("parts", "dp"), None, None)
    return jax.shard_map(
        per_device,
        mesh=mesh,
        in_specs=(rows, rows, rows, P("parts"), pools, pools),
        out_specs=(rows, pools, pools),
        check_vma=False,
    )
```

time: 441 us -> 315 us (0.71)
  waiting for transfers between devices: 253 us -> 180 us
  matrix products: 45.6 us -> 0 us
  Pallas kernels: 0 us -> 41.6 us
  local copies, waits for them, and re-layouts: 28.6 us -> 8.27 us
  starting transfers between devices: 52.1 us -> 38.2 us
  blocking collectives: 43.7 us -> 32.2 us
    ppermute x46 -> x22, waiting for transfers between devices: 253 us -> 180 us  [send(): return lax.ppermute(array, 'dp', pairs)]
    dot_general x23 -> x0, matrix products: 45.6 us -> none  [dot32(): return lax.dot_general(a, b, dims, preferred_element_type=jnp.float32)]
    pallas_call x0 -> x5, Pallas kernels: none -> 41.6 us  [the longest x2 13.8 us: pack(): pl.pallas_call(body, grid=(width // tile,), in_specs=[pl.BlockSpec(place....]
    ppermute x46 -> x22, starting transfers between devices: 52.1 us -> 38.2 us  [send(): return lax.ppermute(array, 'dp', pairs)]
    psum x1, blocking collectives: 43.7 us -> 32.2 us  [clipped(): total = lax.psum(local_sq, 'dp')]
    unnamed x142 -> x29, local copies, waits for them, and re-layouts: 13.2 us -> 5.05 us
    another operation x8 -> x0, local copies, waits for them, and re-layouts: 7.91 us -> none  [the longest x6 6.14 us: packed(): return list(out.reshape(plane, -1, width))]
    mul x0 -> x1, other arithmetic: none -> 6.25 us  [clipped(): return ((raw_down * factor)[None], (raw_up * factor)[None])]
  transfers between devices with their start and end apart: 46 -> 22, of which waited for: 25 -> 10; matrix products, arithmetic and copies ran while one was open for 16% -> 2% of each run, Pallas kernels for 0% -> 8%
where the time goes in v2:
time: 315 us; the launch traced here: 314 us
  waiting for transfers between devices  180 us (57%)
  Pallas kernels  41.6 us (13%)
  starting transfers between devices  38.2 us (12%)
  blocking collectives  32.2 us (10%)
  other arithmetic  11.2 us (4%)
  local copies, waits for them, and re-layouts  8.27 us (3%)
    ppermute x22, waiting for transfers between devices, send(): return lax.ppermute(array, 'dp', pairs)  180 us
    ppermute x22, starting transfers between devices, send(): return lax.ppermute(array, 'dp', pairs)  38.2 us
    psum x1, blocking collectives, clipped(): total = lax.psum(local_sq, 'dp')  32.2 us
    pallas_call x2, Pallas kernels, pack(): pl.pallas_call(body, grid=(width // tile,), in_specs=[pl.BlockSpec(place....  13.8 us
    pallas_call x1, Pallas kernels, near_groups(): pl.pallas_call(body, grid=(tiles,), in_specs=[pl.BlockSpec(memory_space=p...  11.8 us
    pallas_call x1, Pallas kernels, far_groups(): pl.pallas_call(body, grid=(tiles,), in_specs=[pl.BlockSpec(memory_space=p...  8.99 us
    pallas_call x1, Pallas kernels, unpack(): pl.pallas_call(body, grid=(width // tile,), in_specs=[pl.BlockSpec(place....  6.92 us
  transfers between devices with their start and end apart: 22, of which 10 were waited for; matrix products, arithmetic and copies ran while one was open for 2% of the time, Pallas kernels for 8%

profile of v2, /device:TPU:0, one launch (start us, length us, event | category | flops | bytes accessed | tf_op | source)
XLA Modules:
  0.0 314.1 jit_solution(10875841672482979386)
XLA Ops:
  0.7 2.3 constant_dynamic-update-slice_fusion.1
  6.1 4.6 %collective-permute-start.6 = (bf16[2,64,8192]{2,1,0:T(8,128)(2,1)}, bf16[2,64,8192]{2,1,0:T(8,128)(2,1)}, u32[]{:S(2)}, u32[]{:S(2)}) collective-permute-start(bf16[2,64,8192]{2,1,0:T(8,128)(2,1)} %constant_dynamic-update-slice_fusion), channel_id=1, source_target_pairs={{0,4},{1,5},{2,6},{3,7},{4,0},{5,1},{6,2},{7,3},{8,12},{9,13},{10,... | collective-permute-start | bytes 6291464 | tf_op jit(solution)/shard_map/ppermute | solution.py:333
  11.3 6.9 %shard_map.86 = (bf16[2,32,8192]{2,1,0:T(8,128)(2,1)S(1)}, bf16[2,32,8192]{2,1,0:T(8,128)(2,1)S(1)}, bf16[2,32,8192]{2,1,0:T(8,128)(2,1)S(1)}, bf16[2,32,8192]{2,1,0:T(8,128)(2,1)}) custom-call(bf16[128,128]{1,0:T(8,128)(2,1)S(1)} %fusion.4.place_ref, bf16[128,8192]{1,0:T(8,128)(2,1)} %x_ref.3, bf16[128,8192]{1,0:T(8,128)(2,1)} %g_ref.3), custom_call_target="tpu_custom_call" | custom-call | flops 536870912 | bytes 8388608 | tf_op jit(solution)/shard_map/pallas_call | solution.py:85
  20.9 23.3 %collective-permute-done.1.refs_2_ = bf16[2,32,8192]{2,1,0:T(8,128)(2,1)S(1)} collective-permute-done((bf16[2,32,8192]{2,1,0:T(8,128)(2,1)S(1)}, bf16[2,32,8192]{2,1,0:T(8,128)(2,1)S(1)}, u32[]{:S(2)}, u32[]{:S(2)}) %collective-permute-start.1) | collective-permute-done | bytes 1048608 | tf_op jit(solution)/shard_map/ppermute | solution.py:333
  44.2 21.7 %collective-permute-done.2.refs_3_ = bf16[2,32,8192]{2,1,0:T(8,128)(2,1)S(1)} collective-permute-done((bf16[2,32,8192]{2,1,0:T(8,128)(2,1)}, bf16[2,32,8192]{2,1,0:T(8,128)(2,1)S(1)}, u32[]{:S(2)}, u32[]{:S(2)}) %collective-permute-start.2) | collective-permute-done | bytes 1048608 | tf_op jit(solution)/shard_map/ppermute | solution.py:333
  67.6 3.3 %collective-permute-start.10 = (bf16[2,64,8192]{2,1,0:T(8,128)(2,1)}, bf16[2,64,8192]{2,1,0:T(8,128)(2,1)}, u32[]{:S(2)}, u32[]{:S(2)}) collective-permute-start(bf16[2,64,8192]{2,1,0:T(8,128)(2,1)} %pad_maximum_fusion), channel_id=1, source_target_pairs={{0,4},{1,5},{2,6},{3,7},{12,8},{13,9},{14,10},{15,11},{16,20},{17,... | collective-permute-start | bytes 6291464 | tf_op jit(solution)/shard_map/ppermute | solution.py:333
  74.1 41.0 %collective-permute-done.10.refs_4_ = bf16[2,64,8192]{2,1,0:T(8,128)(2,1)} collective-permute-done((bf16[2,64,8192]{2,1,0:T(8,128)(2,1)}, bf16[2,64,8192]{2,1,0:T(8,128)(2,1)}, u32[]{:S(2)}, u32[]{:S(2)}) %collective-permute-start.10) | collective-permute-done | bytes 2097184 | tf_op jit(solution)/shard_map/ppermute | solution.py:333
  115.1 5.4 %collective-permute-done.9.refs_6_.refs_8_ = bf16[2,64,8192]{2,1,0:T(8,128)(2,1)} collective-permute-done((bf16[2,64,8192]{2,1,0:T(8,128)(2,1)}, bf16[2,64,8192]{2,1,0:T(8,128)(2,1)}, u32[]{:S(2)}, u32[]{:S(2)}) %collective-permute-start.9) | collective-permute-done | bytes 2097184 | tf_op jit(solution)/shard_map/ppermute | solution.py:333
  120.5 9.0 %shard_map.87 = (bf16[2,64,8192]{2,1,0:T(8,128)(2,1)}, bf16[2,64,8192]{2,1,0:T(8,128)(2,1)}, bf16[64,8192]{1,0:T(8,128)(2,1)S(1)}, bf16[128,64]{1,0:T(8,128)(2,1)S(1)}, bf16[64,64]{1,0:T(8,128)(2,1)S(1)}) custom-call(s32[1]{0:T(128)} %bitcast.1.end_ref, bf16[2,32,8192]{2,1,0:T(8,128)(2,1)S(1)} %get-tuple-element.30.refs_0_, ...), custom_call_target="tpu_custom_call" | custom-call | flops 872415232 | bytes 19922944 | tf_op jit(solution)/shard_map/pallas_call | solution.py:185
  129.5 7.0 %collective-permute-start.18 = (bf16[2,64,8192]{2,1,0:T(8,128)(2,1)}, bf16[2,64,8192]{2,1,0:T(8,128)(2,1)S(1)}, u32[]{:S(2)}, u32[]{:S(2)}) collective-permute-start(bf16[2,64,8192]{2,1,0:T(8,128)(2,1)} %get-tuple-element.46), channel_id=1, source_target_pairs={{0,4},{1,5},{2,6},{3,7},{12,8},{13,9},{14,10},{15,11},{16,20},{17,... | collective-permute-start | bytes 6291464 | tf_op jit(solution)/shard_map/ppermute | solution.py:333
  136.6 6.9 %shard_map.85 = (bf16[2,32,8192]{2,1,0:T(8,128)(2,1)S(1)}, bf16[2,32,8192]{2,1,0:T(8,128)(2,1)S(1)}, bf16[2,32,8192]{2,1,0:T(8,128)(2,1)S(1)}, bf16[2,32,8192]{2,1,0:T(8,128)(2,1)}) custom-call(bf16[128,128]{1,0:T(8,128)(2,1)S(1)} %fusion.2.place_ref, bf16[128,8192]{1,0:T(8,128)(2,1)} %x_ref.3, bf16[128,8192]{1,0:T(8,128)(2,1)} %g_ref.3), custom_call_target="tpu_custom_call" | custom-call | flops 536870912 | bytes 8388608 | tf_op jit(solution)/shard_map/pallas_call | solution.py:85
  148.5 22.0 %collective-permute-done.4.refs_2_ = bf16[2,32,8192]{2,1,0:T(8,128)(2,1)S(1)} collective-permute-done((bf16[2,32,8192]{2,1,0:T(8,128)(2,1)S(1)}, bf16[2,32,8192]{2,1,0:T(8,128)(2,1)S(1)}, u32[]{:S(2)}, u32[]{:S(2)}) %collective-permute-start.4) | collective-permute-done | bytes 1048608 | tf_op jit(solution)/shard_map/ppermute | solution.py:333
  170.4 21.7 %collective-permute-done.5.refs_3_ = bf16[2,32,8192]{2,1,0:T(8,128)(2,1)S(1)} collective-permute-done((bf16[2,32,8192]{2,1,0:T(8,128)(2,1)}, bf16[2,32,8192]{2,1,0:T(8,128)(2,1)S(1)}, u32[]{:S(2)}, u32[]{:S(2)}) %collective-permute-start.5) | collective-permute-done | bytes 1048608 | tf_op jit(solution)/shard_map/ppermute | solution.py:333
  193.1 11.8 %shard_map.88 = (bf16[64,8192]{1,0:T(8,128)(2,1)S(1)}, bf16[64,8192]{1,0:T(8,128)(2,1)S(1)}, bf16[64,8192]{1,0:T(8,128)(2,1)}, bf16[64,8192]{1,0:T(8,128)(2,1)},...) custom-call(s32[1]{0:T(128)} %bitcast.1.end_ref, bf16[2,32,8192]{2,1,0:T(8,128)(2,1)} %copy-done, ...), custom_call_target="tpu_custom_call" | custom-call | flops 805306368 | bytes 25165824 | tf_op jit(solution)/shard_map/pallas_call | solution.py:296
  210.9 2.0 fusion.8
  213.0 2.2 collective-permute-start.15
  215.3 3.4 %collective-permute-start.16 = (bf16[16,8192]{1,0:T(8,128)(2,1)}, bf16[16,8192]{1,0:T(8,128)(2,1)S(1)}, u32[]{:S(2)}, u32[]{:S(2)}) collective-permute-start(bf16[16,8192]{1,0:T(8,128)(2,1)} %get-tuple-element.58), channel_id=1, source_target_pairs={{0,2},{1,3},{2,0},{3,1},{12,14},{13,15},{14,12},{15,13},{16,18},{1... | collective-permute-start | bytes 786440 | tf_op jit(solution)/shard_map/ppermute | solution.py:333
  218.7 36.8 %collective-permute-done.21 = bf16[2,64,8192]{2,1,0:T(8,128)(2,1)S(1)} collective-permute-done((bf16[2,64,8192]{2,1,0:T(8,128)(2,1)S(1)}, bf16[2,64,8192]{2,1,0:T(8,128)(2,1)S(1)}, u32[]{:S(2)}, u32[]{:S(2)}) %collective-permute-start.21) | collective-permute-done | bytes 2097184 | tf_op jit(solution)/shard_map/ppermute | solution.py:333
  255.5 2.5 collective-permute-start.17
  260.9 2.5 collective-permute-done.16.refs_6_
  263.4 4.7 %collective-permute-done.17.refs_7_ = bf16[16,8192]{1,0:T(8,128)(2,1)S(1)} collective-permute-done((bf16[16,8192]{1,0:T(8,128)(2,1)S(1)}, bf16[16,8192]{1,0:T(8,128)(2,1)S(1)}, u32[]{:S(2)}, u32[]{:S(2)}) %collective-permute-start.17) | collective-permute-done | bytes 262176 | tf_op jit(solution)/shard_map/ppermute | solution.py:333
  268.1 6.9 %shard_map.89 = bf16[128,8192]{1,0:T(8,128)(2,1)} custom-call(bf16[320,128]{1,0:T(8,128)(2,1)S(1)} %add_convert_fusion.2.place_ref, bf16[64,8192]{1,0:T(8,128)(2,1)S(1)} %get-tuple-element.40.refs_0_, bf16[64,8192]{1,0:T(8,128)(2,1)S(1)} %collective-permute-done.11.refs_1_, bf16[64,8192]{1,0:T(8,128)(2,1)} %collective-permute-done.12.refs_2_, ...), custom_call_target="tpu_custom_call" | custom-call | flops 671088640 | bytes 7340032 | tf_op jit(solution)/shard_map/pallas_call | solution.py:105
  275.0 32.2 %psum.7 = f32[]{:T(128)} all-reduce(f32[]{:T(128)S(6)} %add.142), channel_id=1, replica_groups=mesh['parts'=2,'dp'=16] {'dp'}, use_global_device_ids=true, to_apply=%region_5.6 | all-reduce | flops 1 | bytes 8 | tf_op jit(solution)/shard_map/psum | solution.py:34
  307.9 6.2 %broadcast_multiply_fusion = (f32[1,64,8192]{2,1,0:T(8,128)}, f32[1,64,8192]{2,1,0:T(8,128)}) fusion(f32[]{:T(128)S(6)} %min_shard_map.3, bf16[2,64,8192]{2,1,0:T(8,128)(2,1)} %copy-done.3, bf16[2,64,8192]{2,1,0:T(8,128)(2,1)} %copy-done.2, f32[2,64,8192]{2,1,0:T(8,128)} %get-tuple-element.45), kind=kLoop, calls=%fused_computation.7 | loop fusion | flops 5242880 | bytes 12582916 | tf_op jit(solution)/shard_map/mul | solution.py:38
  (79 shorter events, 24.8 us)
Async XLA Ops:
  4.1 66.8 %collective-permute-start.8 = (bf16[2,64,8192]{2,1,0:T(8,128)(2,1)}, bf16[2,64,8192]{2,1,0:T(8,128)(2,1)}, u32[]{:S(2)}, u32[]{:S(2)}) collective-permute-start(bf16[2,64,8192]{2,1,0:T(8,128)(2,1)} %constant_dynamic-update-slice_fusion), channel_id=1, source_target_pairs={{4,8},{5,9},{6,10},{7,11},{8,4},{9,5},{10,6},{11,7},{20,24},{21,25... | collective-permute-start | bytes 6291464 | tf_op jit(solution)/shard_map/ppermute | solution.py:333
  6.1 66.1 %collective-permute-start.6 = (bf16[2,64,8192]{2,1,0:T(8,128)(2,1)}, bf16[2,64,8192]{2,1,0:T(8,128)(2,1)}, u32[]{:S(2)}, u32[]{:S(2)}) collective-permute-start(bf16[2,64,8192]{2,1,0:T(8,128)(2,1)} %constant_dynamic-update-slice_fusion), channel_id=1, source_target_pairs={{0,4},{1,5},{2,6},{3,7},{4,0},{5,1},{6,2},{7,3},{8,12},{9,13},{10,... | collective-permute-start | bytes 6291464 | tf_op jit(solution)/shard_map/ppermute | solution.py:333
  18.2 2.7 collective-permute-start
  18.2 26.0 %collective-permute-start.1 = (bf16[2,32,8192]{2,1,0:T(8,128)(2,1)S(1)}, bf16[2,32,8192]{2,1,0:T(8,128)(2,1)S(1)}, u32[]{:S(2)}, u32[]{:S(2)}) collective-permute-start(bf16[2,32,8192]{2,1,0:T(8,128)(2,1)S(1)} %get-tuple-element.32), channel_id=1, source_target_pairs={{0,2},{1,3},{2,0},{3,1},{4,6},{5,7},{6,4},{7,5},{8,10},{9,11},{10,... | collective-permute-start | bytes 3145736 | tf_op jit(solution)/shard_map/ppermute | solution.py:333
  19.7 46.2 %collective-permute-start.2 = (bf16[2,32,8192]{2,1,0:T(8,128)(2,1)}, bf16[2,32,8192]{2,1,0:T(8,128)(2,1)S(1)}, u32[]{:S(2)}, u32[]{:S(2)}) collective-permute-start(bf16[2,32,8192]{2,1,0:T(8,128)(2,1)} %get-tuple-element.33), channel_id=1, source_target_pairs={{0,3},{1,2},{2,1},{3,0},{4,7},{5,6},{6,5},{7,4},{8,11},{9,10},{10,... | collective-permute-start | bytes 3145736 | tf_op jit(solution)/shard_map/ppermute | solution.py:333
  67.6 47.5 %collective-permute-start.10 = (bf16[2,64,8192]{2,1,0:T(8,128)(2,1)}, bf16[2,64,8192]{2,1,0:T(8,128)(2,1)}, u32[]{:S(2)}, u32[]{:S(2)}) collective-permute-start(bf16[2,64,8192]{2,1,0:T(8,128)(2,1)} %pad_maximum_fusion), channel_id=1, source_target_pairs={{0,4},{1,5},{2,6},{3,7},{12,8},{13,9},{14,10},{15,11},{16,20},{17,... | collective-permute-start | bytes 6291464 | tf_op jit(solution)/shard_map/ppermute | solution.py:333
  70.9 49.7 %collective-permute-start.9 = (bf16[2,64,8192]{2,1,0:T(8,128)(2,1)}, bf16[2,64,8192]{2,1,0:T(8,128)(2,1)}, u32[]{:S(2)}, u32[]{:S(2)}) collective-permute-start(bf16[2,64,8192]{2,1,0:T(8,128)(2,1)} %collective-permute-done.8.refs_7_.refs_9_), channel_id=1, source_target_pairs={{4,0},{5,1},{6,2},{7,3},{8,12},{9,13},{10,14},{11,15},{20,16},{21,... | collective-permute-start | bytes 6291464 | tf_op jit(solution)/shard_map/ppermute | solution.py:333
  72.2 48.4 %collective-permute-start.7 = (bf16[2,64,8192]{2,1,0:T(8,128)(2,1)}, bf16[2,64,8192]{2,1,0:T(8,128)(2,1)}, u32[]{:S(2)}, u32[]{:S(2)}) collective-permute-start(bf16[2,64,8192]{2,1,0:T(8,128)(2,1)} %collective-permute-done.6.refs_4_), channel_id=1, source_target_pairs={{4,8},{5,9},{6,10},{7,11},{8,4},{9,5},{10,6},{11,7},{20,24},{21,25... | collective-permute-start | bytes 6291464 | tf_op jit(solution)/shard_map/ppermute | solution.py:333
  129.5 75.4 %collective-permute-start.18 = (bf16[2,64,8192]{2,1,0:T(8,128)(2,1)}, bf16[2,64,8192]{2,1,0:T(8,128)(2,1)S(1)}, u32[]{:S(2)}, u32[]{:S(2)}) collective-permute-start(bf16[2,64,8192]{2,1,0:T(8,128)(2,1)} %get-tuple-element.46), channel_id=1, source_target_pairs={{0,4},{1,5},{2,6},{3,7},{12,8},{13,9},{14,10},{15,11},{16,20},{17,... | collective-permute-start | bytes 6291464 | tf_op jit(solution)/shard_map/ppermute | solution.py:333
  144.5 2.7 collective-permute-start.3
  144.5 26.0 %collective-permute-start.4 = (bf16[2,32,8192]{2,1,0:T(8,128)(2,1)S(1)}, bf16[2,32,8192]{2,1,0:T(8,128)(2,1)S(1)}, u32[]{:S(2)}, u32[]{:S(2)}) collective-permute-start(bf16[2,32,8192]{2,1,0:T(8,128)(2,1)S(1)} %get-tuple-element.36), channel_id=1, source_target_pairs={{0,2},{1,3},{2,0},{3,1},{4,6},{5,7},{6,4},{7,5},{8,10},{9,11},{10,... | collective-permute-start | bytes 3145736 | tf_op jit(solution)/shard_map/ppermute | solution.py:333
  146.0 46.1 %collective-permute-start.5 = (bf16[2,32,8192]{2,1,0:T(8,128)(2,1)}, bf16[2,32,8192]{2,1,0:T(8,128)(2,1)S(1)}, u32[]{:S(2)}, u32[]{:S(2)}) collective-permute-start(bf16[2,32,8192]{2,1,0:T(8,128)(2,1)} %get-tuple-element.37), channel_id=1, source_target_pairs={{0,3},{1,2},{2,1},{3,0},{4,7},{5,6},{6,5},{7,4},{8,11},{9,10},{10,... | collective-permute-start | bytes 3145736 | tf_op jit(solution)/shard_map/ppermute | solution.py:333
  146.3 60.1 %collective-permute-start.20 = (bf16[2,64,8192]{2,1,0:T(8,128)(2,1)}, bf16[2,64,8192]{2,1,0:T(8,128)(2,1)S(1)}, u32[]{:S(2)}, u32[]{:S(2)}) collective-permute-start(bf16[2,64,8192]{2,1,0:T(8,128)(2,1)} %get-tuple-element.48), channel_id=1, source_target_pairs={{4,8},{5,9},{6,10},{7,11},{8,4},{9,5},{10,6},{11,7},{20,24},{21,25... | collective-permute-start | bytes 6291464 | tf_op jit(solution)/shard_map/ppermute | solution.py:333
  147.2 45.9 %copy-start.9 = (bf16[2,32,8192]{2,1,0:T(8,128)(2,1)}, bf16[2,32,8192]{2,1,0:T(8,128)(2,1)S(1)}, u32[]{:S(2)}) copy-start(bf16[2,32,8192]{2,1,0:T(8,128)(2,1)S(1)} %collective-permute-done.3.refs_1_) | copy-start | bytes 3145732
  147.2 63.5 %collective-permute-start.14 = (bf16[64,8192]{1,0:T(8,128)(2,1)S(1)}, bf16[64,8192]{1,0:T(8,128)(2,1)}, u32[]{:S(2)}, u32[]{:S(2)}) collective-permute-start(bf16[64,8192]{1,0:T(8,128)(2,1)S(1)} %get-tuple-element.44), channel_id=1, source_target_pairs={{4,0},{5,1},{6,2},{7,3},{8,12},{9,13},{10,14},{11,15},{20,16},{21,... | collective-permute-start | bytes 3145736 | tf_op jit(solution)/shard_map/ppermute | solution.py:333
  205.5 9.8 %collective-permute-start.19 = (bf16[2,64,8192]{2,1,0:T(8,128)(2,1)S(1)}, bf16[2,64,8192]{2,1,0:T(8,128)(2,1)S(1)}, u32[]{:S(2)}, u32[]{:S(2)}) collective-permute-start(bf16[2,64,8192]{2,1,0:T(8,128)(2,1)S(1)} %add_convert_fusion.1), channel_id=1, source_target_pairs={{4,8},{5,9},{6,10},{7,11},{8,4},{9,5},{10,6},{11,7},{20,24},{21,25... | collective-permute-start | bytes 6291464 | tf_op jit(solution)/shard_map/ppermute | solution.py:333
  207.1 50.8 %copy-start.1 = (f32[2,64,8192]{2,1,0:T(8,128)S(1)}, f32[2,64,8192]{2,1,0:T(8,128)}, u32[]{:S(2)}) copy-start(f32[2,64,8192]{2,1,0:T(8,128)} %get-tuple-element.45) | copy-start | bytes 12582916
  207.7 47.8 %collective-permute-start.21 = (bf16[2,64,8192]{2,1,0:T(8,128)(2,1)S(1)}, bf16[2,64,8192]{2,1,0:T(8,128)(2,1)S(1)}, u32[]{:S(2)}, u32[]{:S(2)}) collective-permute-start(bf16[2,64,8192]{2,1,0:T(8,128)(2,1)S(1)} %add_convert_fusion), channel_id=1, source_target_pairs={{0,4},{1,5},{2,6},{3,7},{4,0},{5,1},{6,2},{7,3},{8,12},{9,13},{10,... | collective-permute-start | bytes 6291464 | tf_op jit(solution)/shard_map/ppermute | solution.py:333
  209.0 4.0 %collective-permute-start.11 = (bf16[64,8192]{1,0:T(8,128)(2,1)S(1)}, bf16[64,8192]{1,0:T(8,128)(2,1)S(1)}, u32[]{:S(2)}, u32[]{:S(2)}) collective-permute-start(bf16[64,8192]{1,0:T(8,128)(2,1)S(1)} %get-tuple-element.41), channel_id=1, source_target_pairs={{0,1},{1,0},{2,3},{3,2},{4,5},{5,4},{6,7},{7,6},{8,9},{9,8},{10,11... | collective-permute-start | bytes 3145736 | tf_op jit(solution)/shard_map/ppermute | solution.py:333
  209.1 51.8 %collective-permute-start.12 = (bf16[64,8192]{1,0:T(8,128)(2,1)}, bf16[64,8192]{1,0:T(8,128)(2,1)}, u32[]{:S(2)}, u32[]{:S(2)}) collective-permute-start(bf16[64,8192]{1,0:T(8,128)(2,1)} %get-tuple-element.42), channel_id=1, source_target_pairs={{0,2},{1,3},{2,0},{3,1},{4,6},{5,7},{6,4},{7,5},{8,10},{9,11},{10,... | collective-permute-start | bytes 3145736 | tf_op jit(solution)/shard_map/ppermute | solution.py:333
  210.6 50.2 %collective-permute-start.13 = (bf16[64,8192]{1,0:T(8,128)(2,1)}, bf16[64,8192]{1,0:T(8,128)(2,1)}, u32[]{:S(2)}, u32[]{:S(2)}) collective-permute-start(bf16[64,8192]{1,0:T(8,128)(2,1)} %get-tuple-element.43), channel_id=1, source_target_pairs={{0,3},{1,2},{2,1},{3,0},{4,7},{5,6},{6,5},{7,4},{8,11},{9,10},{10,... | collective-permute-start | bytes 3145736 | tf_op jit(solution)/shard_map/ppermute | solution.py:333
  213.0 47.9 %collective-permute-start.15 = (bf16[16,8192]{1,0:T(8,128)(2,1)}, bf16[16,8192]{1,0:T(8,128)(2,1)S(1)}, u32[]{:S(2)}, u32[]{:S(2)}) collective-permute-start(bf16[16,8192]{1,0:T(8,128)(2,1)} %get-tuple-element.59), channel_id=1, source_target_pairs={{0,1},{1,0},{2,3},{3,2},{12,13},{13,12},{14,15},{15,14},{16,17},{1... | collective-permute-start | bytes 786440 | tf_op jit(solution)/shard_map/ppermute | solution.py:333
  215.3 48.1 %collective-permute-start.16 = (bf16[16,8192]{1,0:T(8,128)(2,1)}, bf16[16,8192]{1,0:T(8,128)(2,1)S(1)}, u32[]{:S(2)}, u32[]{:S(2)}) collective-permute-start(bf16[16,8192]{1,0:T(8,128)(2,1)} %get-tuple-element.58), channel_id=1, source_target_pairs={{0,2},{1,3},{2,0},{3,1},{12,14},{13,15},{14,12},{15,13},{16,18},{1... | collective-permute-start | bytes 786440 | tf_op jit(solution)/shard_map/ppermute | solution.py:333
  255.5 12.6 %collective-permute-start.17 = (bf16[16,8192]{1,0:T(8,128)(2,1)S(1)}, bf16[16,8192]{1,0:T(8,128)(2,1)S(1)}, u32[]{:S(2)}, u32[]{:S(2)}) collective-permute-start(bf16[16,8192]{1,0:T(8,128)(2,1)S(1)} %get-tuple-element.57), channel_id=1, source_target_pairs={{0,3},{1,2},{2,1},{3,0},{12,15},{13,14},{14,13},{15,12},{16,19},{1... | collective-permute-start | bytes 786440 | tf_op jit(solution)/shard_map/ppermute | solution.py:333
  (12 other events, 134.4 us)

commit v3 on v2

--- a/solution.py
+++ b/solution.py
@@ -31,7 +31,8 @@
 
 def clipped(raw_down, raw_up, ndevices):
     local_sq = jnp.sum(raw_down * raw_down) + jnp.sum(raw_up * raw_up)
-    total = lax.psum(local_sq, "dp")
+    shares = jnp.broadcast_to(local_sq, (ndevices, 8, 128))
+    total = jnp.sum(lax.all_to_all(shares, "dp", split_axis=0, concat_axis=0, tiled=True)[:, 0, 0])
     norm = jnp.sqrt(total + 1e-06)
     limit = jnp.sqrt(jnp.float32(2 * raw_down.shape[0] * raw_down.shape[1] * ndevices))
     factor = jnp.minimum(jnp.float32(1.0), limit / norm)
@@ -71,26 +72,32 @@
     return pl.CostEstimate(flops=flops, bytes_accessed=nbytes, transcendentals=0)
 
 
-def pack(place, acts, cotan, plane):
-    rows, (tokens, width) = place.shape[0] // plane, acts.shape
+def pack(place, acts, cotan, plane, parts):
+    tokens, width = acts.shape
     tile = min(width, 1024)
+    cuts, start = [], 0
+    for rows in parts:
+        for _ in range(plane):
+            cuts.append((start, rows))
+            start += rows
 
     def body(place_ref, x_ref, g_ref, *out_refs):
         for k, ref in enumerate((x_ref, g_ref)):
             moved = dot32(place_ref[...], ref[...]).astype(BF16)
-            for m in range(plane):
-                out_refs[m][k] = moved[m * rows:(m + 1) * rows]
+            for out_ref, (first, rows) in zip(out_refs, cuts):
+                out_ref[k] = moved[first:first + rows]
 
     rows_spec = pl.BlockSpec((tokens, tile), lambda i: (0, i))
-    return pl.pallas_call(
+    packed = pl.pallas_call(
         body,
         grid=(width // tile,),
         in_specs=[pl.BlockSpec(place.shape, lambda i: (0, 0)), rows_spec, rows_spec],
-        out_specs=[pl.BlockSpec((2, rows, tile), lambda i: (0, 0, i))] * plane,
-        out_shape=[jax.ShapeDtypeStruct((2, rows, width), BF16)] * plane,
+        out_specs=[pl.BlockSpec((2, rows, tile), lambda i: (0, 0, i)) for _, rows in cuts],
+        out_shape=[jax.ShapeDtypeStruct((2, rows, width), BF16) for _, rows in cuts],
         compiler_params=kernel_params(),
         cost_estimate=cost(4 * place.shape[0] * tokens * width, 4 * (tokens + place.shape[0]) * width),
     )(place, acts, cotan)
+    return [packed[n * plane:(n + 1) * plane] for n in range(len(parts))]
 
 
 def unpack(place, blocks, tokens):
@@ -114,22 +121,23 @@
     )(place, *blocks)
 
 
-def far_groups(is_end, stage, mids, far, outer, crossed, capacity):
-    plane = len(stage)
+def far_groups(is_end, stage3, stage2, ends, far, outer, crossed, capacity):
+    plane = len(stage3)
     _, rank, width = far.shape
     block = plane * capacity
     tile = min(width, 1024)
     tiles = width // tile
 
     def body(end_ref, *refs):
-        stage_in, (mids_in, far_in, outer_in, crossed_in) = refs[:plane], refs[plane:plane + 4]
-        sum3_ref, sum2_ref, dx_ref, inner3_ref, inner2_ref = refs[plane + 4:plane + 9]
-        tokens, ends, far_w, near_w, hidden3, hidden2, sems = refs[plane + 9:]
+        stage_in, refs = refs[:2 * plane], refs[2 * plane:]
+        ends_in, far_in, outer_in, crossed_in = refs[:4]
+        sum3_ref, sum2_ref, dx_ref, inner3_ref, inner2_ref = refs[4:9]
+        tokens, ends_t, far_w, near_w, hidden3, hidden2, sems = refs[9:]
         step = pl.program_id(0)
 
         def copies(i):
             cut = pl.ds(i * tile, tile)
-            pairs = [(stage_in[m], tokens.at[m]) for m in range(plane)] + [(mids_in, ends), (far_in, far_w)]
+            pairs = [(stage_in[m], tokens.at[m]) for m in range(2 * plane)] + [(ends_in, ends_t), (far_in, far_w)]
             return [
                 pltpu.make_async_copy(src.at[:, :, cut], dst.at[:, :, cut], sems.at[i, n])
                 for n, (src, dst) in enumerate(pairs)
@@ -137,13 +145,13 @@
 
         def near_copy(src, i):
             cut = pl.ds(i * tile, tile)
-            return pltpu.make_async_copy(src.at[:, :, cut], near_w.at[:, :, cut], sems.at[i, plane + 2])
+            return pltpu.make_async_copy(src.at[:, :, cut], near_w.at[:, :, cut], sems.at[i, 2 * plane + 2])
 
         def rows3(k, cut):
-            return jnp.concatenate([tokens[m, k, :capacity, cut] for m in range(plane)] + [ends[k, :, cut]], axis=0)
+            return jnp.concatenate([tokens[m, k, :, cut] for m in range(plane)] + [ends_t[k, :, cut]], axis=0)
 
         def rows2(k, cut):
-            return jnp.concatenate([tokens[m, k, capacity:, cut] for m in range(plane)], axis=0)
+            return jnp.concatenate([tokens[m, k, :, cut] for m in range(plane, 2 * plane)], axis=0)
 
         @pl.when(step == 0)
         def _():
@@ -185,7 +193,7 @@
     return pl.pallas_call(
         body,
         grid=(tiles,),
-        in_specs=[pl.BlockSpec(memory_space=pltpu.SMEM)] + [ANY] * (plane + 4),
+        in_specs=[pl.BlockSpec(memory_space=pltpu.SMEM)] + [ANY] * (2 * plane + 4),
         out_specs=[
             pair_spec,
             pair_spec,
@@ -201,31 +209,31 @@
             jax.ShapeDtypeStruct((block, rank), BF16),
         ],
         scratch_shapes=[
-            pltpu.VMEM((plane, 2, 2 * capacity, width), BF16),
+            pltpu.VMEM((2 * plane, 2, capacity, width), BF16),
             pltpu.VMEM((2, block, width), BF16),
             pltpu.VMEM((2, rank, width), BF16),
             pltpu.VMEM((2, rank, width), BF16),
             pltpu.VMEM((2 * block, rank), BF16),
             pltpu.VMEM((block, rank), BF16),
-            pltpu.SemaphoreType.DMA((tiles, plane + 3)),
+            pltpu.SemaphoreType.DMA((tiles, 2 * plane + 3)),
         ],
         compiler_params=kernel_params(),
         cost_estimate=cost(26 * block * rank * width, 38 * block * width),
-    )(is_end, *stage, mids, far, outer, crossed)
-
-
-def near_groups(is_end, stage, pair, down, up, far, outer, crossed, inner3, inner2, capacity):
+    )(is_end, *stage3, *stage2, ends, far, outer, crossed)
+
+
+def near_groups(stage, pair, down, up, capacity):
     plane = len(stage)
-    _, rank, width = far.shape
+    _, rank, width = pair.shape
     block = plane * capacity
     tile = min(width, 1024)
     tiles = width // tile
 
-    def body(end_ref, *refs):
+    def body(*refs):
         stage_in, refs = refs[:plane], refs[plane:]
-        pair_in, down_in, up_in, far_in, outer_in, crossed_in, inner3, inner2 = refs[:8]
-        dx_refs, (sum1_ref, sum0_ref) = refs[8:8 + plane], refs[8 + plane:10 + plane]
-        tokens, pair_w, own_w, dx_w, hidden1, inner1, hidden0, inner0, sems = refs[10 + plane:]
+        pair_in, down_in, up_in = refs[:3]
+        dx_refs, (sum1_ref, sum0_ref) = refs[3:3 + plane], refs[3 + plane:5 + plane]
+        tokens, pair_w, own_w, hidden1, inner1, hidden0, inner0, sems = refs[5 + plane:]
         step = pl.program_id(0)
 
         def copies(i):
@@ -234,13 +242,8 @@
                 (pair_in.at[:, :, cut], pair_w.at[:, :, cut]),
                 (down_in.at[:, cut], own_w.at[0, :, cut]),
                 (up_in.at[:, cut], own_w.at[1, :, cut]),
-                (far_in.at[0, :, cut], dx_w.at[0, :, cut]),
             ]
             return [pltpu.make_async_copy(src, dst, sems.at[i, n]) for n, (src, dst) in enumerate(pairs)]
-
-        def near_copy(src, i):
-            cut = pl.ds(i * tile, tile)
-            return pltpu.make_async_copy(src.at[0, :, cut], dx_w.at[1, :, cut], sems.at[i, plane + 4])
 
         def rows1(k, cut):
             return jnp.concatenate([tokens[m, k, :capacity, cut] for m in range(plane)], axis=0)
@@ -253,20 +256,10 @@
             for i in range(tiles):
                 for c in copies(i):
                     c.start()
-
-                @pl.when(end_ref[0] == 1)
-                def _():
-                    near_copy(outer_in, i).start()
-
-                @pl.when(end_ref[0] != 1)
-                def _():
-                    near_copy(crossed_in, i).start()
-
             sums = [jnp.zeros((block, rank), F32)] * 4
             for i in range(tiles):
                 for c in copies(i):
                     c.wait()
-                near_copy(outer_in, i).wait()
                 cut = pl.ds(i * tile, tile)
                 for k in range(2):
                     sums[k] += dot32(rows1(k, cut), pair_w[k, :, cut], ROWS_OF)
@@ -279,37 +272,59 @@
         sum1_ref[1] = dot32(inner1[...], rows1(0, cut), OUTER)
         sum0_ref[0] = dot32(hidden0[...], rows0(1, cut), OUTER)
         sum0_ref[1] = dot32(inner0[...], rows0(0, cut), OUTER)
-        moved = [
-            dot32(inner3[:block], dx_w[0, :, cut]),
-            dot32(inner2[...], dx_w[1, :, cut]),
-            dot32(inner1[...], pair_w[0, :, cut]),
-            dot32(inner0[...], own_w[0, :, cut]),
-        ]
-        for n, dx in enumerate(moved):
-            dx = dx.astype(BF16)
+        for n, (inner, w) in enumerate(((inner1, pair_w), (inner0, own_w))):
+            dx = dot32(inner[...], w[0, :, cut]).astype(BF16)
             for m in range(plane):
                 dx_refs[m][n * capacity:(n + 1) * capacity] = dx[m * capacity:(m + 1) * capacity]
 
     total = jax.ShapeDtypeStruct((2, rank, width), F32)
     total_spec = pl.BlockSpec((2, rank, tile), lambda i: (0, 0, i))
-    whole = [pl.BlockSpec(a.shape, lambda i: (0, 0)) for a in (inner3, inner2)]
     return pl.pallas_call(
         body,
         grid=(tiles,),
-        in_specs=[pl.BlockSpec(memory_space=pltpu.SMEM)] + [ANY] * (plane + 6) + whole,
-        out_specs=[pl.BlockSpec((4 * capacity, tile), lambda i: (0, i))] * plane + [total_spec] * 2,
-        out_shape=[jax.ShapeDtypeStruct((4 * capacity, width), BF16)] * plane + [total] * 2,
+        in_specs=[ANY] * (plane + 3),
+        out_specs=[pl.BlockSpec((2 * capacity, tile), lambda i: (0, i))] * plane + [total_spec] * 2,
+        out_shape=[jax.ShapeDtypeStruct((2 * capacity, width), BF16)] * plane + [total] * 2,
         scratch_shapes=[
             pltpu.VMEM((plane, 2, 2 * capacity, width), BF16),
             pltpu.VMEM((2, rank, width), BF16),
             pltpu.VMEM((2, rank, width), BF16),
-            pltpu.VMEM((2, rank, width), BF16),
         ]
         + [pltpu.VMEM((block, rank), BF16)] * 4
-        + [pltpu.SemaphoreType.DMA((tiles, plane + 5))],
+        + [pltpu.SemaphoreType.DMA((tiles, plane + 3))],
         compiler_params=kernel_params(),
-        cost_estimate=cost(24 * block * rank * width, 48 * block * width),
-    )(is_end, *stage, pair, down, up, far, outer, crossed, inner3, inner2)
+        cost_estimate=cost(20 * block * rank * width, 36 * block * width),
+    )(*stage, pair, down, up)
+
+
+def far_inputs(is_end, dx_ends, far, outer, crossed, inner3, inner2, capacity):
+    block = inner2.shape[0]
+    plane = block // capacity
+    _, rank, width = far.shape
+    tile = min(width, 1024)
+
+    def body(end_ref, ends_ref, far_ref, outer_ref, crossed_ref, inner3_ref, inner2_ref, *dx_refs):
+        end = end_ref[0] == 1
+        near = jnp.where(end, outer_ref[0], crossed_ref[0])
+        dx3 = dot32(inner3_ref[:block], far_ref[0]).astype(BF16)
+        dx3 = jnp.where(end, ends_ref[...], dx3)
+        dx2 = dot32(inner2_ref[...], near).astype(BF16)
+        for m in range(plane):
+            dx_refs[m][:capacity] = dx3[m * capacity:(m + 1) * capacity]
+            dx_refs[m][capacity:] = dx2[m * capacity:(m + 1) * capacity]
+
+    down_spec = pl.BlockSpec((1, rank, tile), lambda i: (0, 0, i))
+    return pl.pallas_call(
+        body,
+        grid=(width // tile,),
+        in_specs=[pl.BlockSpec(memory_space=pltpu.SMEM), pl.BlockSpec((block, tile), lambda i: (0, i))]
+        + [down_spec] * 3
+        + [pl.BlockSpec(a.shape, lambda i: (0, 0)) for a in (inner3, inner2)],
+        out_specs=[pl.BlockSpec((2 * capacity, tile), lambda i: (0, i))] * plane,
+        out_shape=[jax.ShapeDtypeStruct((2 * capacity, width), BF16)] * plane,
+        compiler_params=kernel_params(),
+        cost_estimate=cost(4 * block * rank * width, 12 * block * width),
+    )(is_end, dx_ends, far, outer, crossed, inner3, inner2)
 
 
 def move_adapters(plane, acts, cotan, token_task_index, task_slot_lookup, pool_down_factors, pool_up_factors):
@@ -332,11 +347,10 @@
     def send(array, pairs):
         return lax.ppermute(array, "dp", pairs)
 
-    def in_plane(blocks, among=(0, 1, 2, 3)):
+    def in_plane(blocks):
         moved = [blocks[0]]
         for m in range(1, plane):
-            pairs = [(i, (i // plane) * plane + ((i % plane) ^ m)) for i in range(ndevices) if i // plane in among]
-            moved.append(send(blocks[m], pairs))
+            moved.append(send(blocks[m], [(i, (i // plane) * plane + ((i % plane) ^ m)) for i in range(ndevices)]))
         return moved
 
     down, up = pool_down_factors[0], pool_up_factors[0]
@@ -353,33 +367,46 @@
         hot = jnp.arange(rows, dtype=jnp.int32)[:, None] == row[None, :]
         return (hot & wanted[None, :]).astype(BF16)
 
-    half = 2 * capacity
-    place_a = places(kind >= 2, turn * half + (3 - kind) * capacity + position, plane * half)
-    place_b = places(kind < 2, turn * half + (1 - kind) * capacity + position, plane * half)
-    place_back = places(kind >= 0, turn * 2 * half + (3 - kind) * capacity + position, 2 * plane * half)
-    place_ends = places(kind == 3, turn * capacity + position, plane * capacity)
-
-    stage_a = in_plane(pack(place_a, acts, cotan, plane))
-    ends = send(jnp.concatenate([b[:, :capacity] for b in stage_a], axis=1), inward)
-    packed_b, _ = lax.optimization_barrier((pack(place_b, acts, cotan, plane), stage_a))
-    stage_b = in_plane(packed_b)
+    def after(arrays, *others):
+        return lax.optimization_barrier((arrays, others))[0]
+
+    half, block = 2 * capacity, plane * capacity
+    place3 = places(kind == 3, turn * capacity + position, block)
+    place2 = places(kind == 2, turn * capacity + position, block)
+    place10 = places(kind < 2, turn * half + (1 - kind) * capacity + position, 2 * block)
+    place_back = places(
+        kind >= 0,
+        jnp.where(kind >= 2, turn * half + (3 - kind) * capacity, 2 * block + turn * half + (1 - kind) * capacity)
+        + position,
+        4 * block,
+    )
+
+    (packed3,) = pack(place3, acts, cotan, plane, (capacity,))
+    packed2, packed10 = pack(
+        jnp.concatenate([place2, place10]), after(acts, packed3), cotan, plane, (capacity, half)
+    )
+    stage3 = in_plane(packed3)
+    ends = send(after(jnp.concatenate(stage3, axis=1), packed2, packed10), inward)
+    stage2 = in_plane(after(packed2, stage3))
     outer = send(crossed, outward)
     far = send(pair, cross)
-
-    sum3, sum2, dx_ends, inner3, inner2 = far_groups(end_flag, stage_a, ends, far, outer, crossed, capacity)
+    stage10 = in_plane(after(packed10, stage2))
+
+    ends = after(ends, stage10[1])
+    sum3, sum2, dx_ends, inner3, inner2 = far_groups(
+        end_flag, stage3, stage2, ends, far, outer, crossed, capacity
+    )
     sum3 = send(sum3, cross)
     sum2_in = send(sum2, inward)
     dx_ends = send(dx_ends, outward)
 
-    *dx, sum1, sum0 = near_groups(
-        end_flag, stage_b, pair, down, up, far, outer, crossed, inner3, inner2, capacity
-    )
+    *dx10, sum1, sum0 = near_groups(stage10, pair, down, up, capacity)
+    back10 = in_plane(dx10)
     sum2 = send((sum2.astype(F32) + sum2_in.astype(F32)).astype(BF16), cross)
     sum1 = send((sum1 + sum3.astype(F32)).astype(BF16), swap)
 
-    back = in_plane(dx)
-    back_ends = in_plane([dx_ends[m * capacity:(m + 1) * capacity] for m in range(plane)], (0, 3))
-    grad_acts = unpack(jnp.concatenate([place_back, place_ends]), back + back_ends, tokens)
+    back32 = in_plane(far_inputs(end_flag, dx_ends, far, outer, crossed, inner3, inner2, capacity))
+    grad_acts = unpack(place_back, back32 + back10, tokens)
     raw_up, raw_down = (sum0[k] + sum2[k].astype(F32) + sum1[k].astype(F32) for k in range(2))
     return (grad_acts,) + clipped(raw_down, raw_up, ndevices)
 

time: 315 us -> 308 us (0.978)
  blocking collectives: 32.2 us -> 0 us
  waiting for transfers between devices: 180 us -> 187 us
  other arithmetic: 11.2 us -> 17.3 us
  starting transfers between devices: 38.2 us -> 43.1 us
  Pallas kernels: 41.6 us -> 45.9 us
    psum x1 -> x0, blocking collectives: 32.2 us -> none  [clipped(): total = lax.psum(local_sq, 'dp')]
    ppermute x22 -> x25, waiting for transfers between devices: 180 us -> 187 us  [send(): return lax.ppermute(array, 'dp', pairs)]
    pallas_call x1 -> x2, Pallas kernels: 11.8 us -> 17.4 us  [the longest x1 10.5 us: near_groups(): pl.pallas_call(body, grid=(tiles,), in_specs=[ANY] * (plane + 3), out_spe...]
    all_to_all x0 -> x1, starting transfers between devices: none -> 5.08 us  [clipped(): lax.all_to_all(shares, 'dp', split_axis=0, concat_axis=0, tiled=True)]
    unnamed x29 -> x39, local copies, waits for them, and re-layouts: 5.05 us -> 9.09 us
    ppermute x22 -> x25, starting transfers between devices: 38.2 us -> 38 us  [send(): return lax.ppermute(array, 'dp', pairs)]
  transfers between devices with their start and end apart: 22 -> 26, of which waited for: 10 -> 13; matrix products, arithmetic and copies ran while one was open for 2% -> 4% of each run, Pallas kernels for 8% -> 12%
where the time goes in v3:
time: 308 us; the launch traced here: 307 us
  waiting for transfers between devices  187 us (61%)
  Pallas kernels  45.9 us (15%)
  starting transfers between devices  43.1 us (14%)
  other arithmetic  17.3 us (6%)
  local copies, waits for them, and re-layouts  10.8 us (4%)
    ppermute x25, waiting for transfers between devices, send(): return lax.ppermute(array, 'dp', pairs)  187 us
    ppermute x25, starting transfers between devices, send(): return lax.ppermute(array, 'dp', pairs)  38 us
    pallas_call x2, Pallas kernels, pack(): pl.pallas_call(body, grid=(width // tile,), in_specs=[pl.BlockSpec(place....  13 us
    pallas_call x1, Pallas kernels, near_groups(): pl.pallas_call(body, grid=(tiles,), in_specs=[ANY] * (plane + 3), out_spe...  10.5 us
    pallas_call x1, Pallas kernels, far_groups(): pl.pallas_call(body, grid=(tiles,), in_specs=[pl.BlockSpec(memory_space=p...  9.25 us
    unnamed x39, local copies, waits for them, and re-layouts  9.09 us
    pallas_call x1, Pallas kernels, far_inputs(): pl.pallas_call(body, grid=(width // tile,), in_specs=[pl.BlockSpec(memory...  6.9 us
    mul x1, other arithmetic, clipped(): return ((raw_down * factor)[None], (raw_up * factor)[None])  6.25 us
  transfers between devices with their start and end apart: 26, of which 13 were waited for; matrix products, arithmetic and copies ran while one was open for 4% of the time, Pallas kernels for 12%

profile of v3, /device:TPU:0, one launch (start us, length us, event | category | flops | bytes accessed | tf_op | source)
XLA Modules:
  0.0 306.6 jit_solution(1438721791053351970)
XLA Ops:
  6.1 4.5 %collective-permute-start.8 = (bf16[2,64,8192]{2,1,0:T(8,128)(2,1)}, bf16[2,64,8192]{2,1,0:T(8,128)(2,1)}, u32[]{:S(2)}, u32[]{:S(2)}) collective-permute-start(bf16[2,64,8192]{2,1,0:T(8,128)(2,1)} %constant_dynamic-update-slice_fusion), channel_id=1, source_target_pairs={{0,4},{1,5},{2,6},{3,7},{4,0},{5,1},{6,2},{7,3},{8,12},{9,13},{10,... | collective-permute-start | bytes 6291464 | tf_op jit(solution)/shard_map/ppermute | solution.py:348
  11.4 5.5 %shard_map.85 = (bf16[2,16,8192]{2,1,0:T(8,128)(2,1)S(1)}, bf16[2,16,8192]{2,1,0:T(8,128)(2,1)S(1)}, bf16[2,16,8192]{2,1,0:T(8,128)(2,1)S(1)}, bf16[2,16,8192]{2,1,0:T(8,128)(2,1)S(1)}) custom-call(bf16[64,128]{1,0:T(8,128)(2,1)S(1)} %get-tuple-element.90.place_ref, bf16[128,8192]{1,0:T(8,128)(2,1)} %x_ref.2, bf16[128,8192]{1,0:T(8,128)(2,1)} %g_ref.3), custom_call_target="tpu_custom_call" | custom-call | flops 268435456 | bytes 6291456 | tf_op jit(solution)/shard_map/pallas_call | solution.py:91
  18.8 7.6 %shard_map.86 = (bf16[2,16,8192]{2,1,0:T(8,128)(2,1)S(1)}, bf16[2,16,8192]{2,1,0:T(8,128)(2,1)S(1)}, bf16[2,16,8192]{2,1,0:T(8,128)(2,1)S(1)}, bf16[2,16,8192]{2...) custom-call(bf16[192,128]{1,0:T(8,128)(2,1)S(1)} %add_convert_fusion, ...), custom_call_target="tpu_custom_call" | custom-call | flops 805306368 | bytes 10485760 | tf_op jit(solution)/shard_map/pallas_call | solution.py:91
  26.4 5.3 %collective-permute-done.1.refs_2_ = bf16[2,16,8192]{2,1,0:T(8,128)(2,1)S(1)} collective-permute-done((bf16[2,16,8192]{2,1,0:T(8,128)(2,1)S(1)}, bf16[2,16,8192]{2,1,0:T(8,128)(2,1)S(1)}, u32[]{:S(2)}, u32[]{:S(2)}) %collective-permute-start.1) | collective-permute-done | bytes 524320 | tf_op jit(solution)/shard_map/ppermute | solution.py:348
  31.7 10.3 %collective-permute-done.2.refs_3_ = bf16[2,16,8192]{2,1,0:T(8,128)(2,1)S(1)} collective-permute-done((bf16[2,16,8192]{2,1,0:T(8,128)(2,1)S(1)}, bf16[2,16,8192]{2,1,0:T(8,128)(2,1)S(1)}, u32[]{:S(2)}, u32[]{:S(2)}) %collective-permute-start.2) | collective-permute-done | bytes 524320 | tf_op jit(solution)/shard_map/ppermute | solution.py:348
  44.2 3.3 %collective-permute-start.6 = (bf16[2,64,8192]{2,1,0:T(8,128)(2,1)}, bf16[2,64,8192]{2,1,0:T(8,128)(2,1)}, u32[]{:S(2)}, u32[]{:S(2)}) collective-permute-start(bf16[2,64,8192]{2,1,0:T(8,128)(2,1)} %pad_maximum_fusion), channel_id=1, source_target_pairs={{0,4},{1,5},{2,6},{3,7},{12,8},{13,9},{14,10},{15,11},{16,20},{17,... | collective-permute-start | bytes 6291464 | tf_op jit(solution)/shard_map/ppermute | solution.py:348
  48.8 8.2 %collective-permute-done.8.refs_4_ = bf16[2,64,8192]{2,1,0:T(8,128)(2,1)} collective-permute-done((bf16[2,64,8192]{2,1,0:T(8,128)(2,1)}, bf16[2,64,8192]{2,1,0:T(8,128)(2,1)}, u32[]{:S(2)}, u32[]{:S(2)}) %collective-permute-start.8) | collective-permute-done | bytes 2097184 | tf_op jit(solution)/shard_map/ppermute | solution.py:348
  61.3 12.6 %collective-permute-done.4.refs_6_ = bf16[2,16,8192]{2,1,0:T(8,128)(2,1)S(1)} collective-permute-done((bf16[2,16,8192]{2,1,0:T(8,128)(2,1)S(1)}, bf16[2,16,8192]{2,1,0:T(8,128)(2,1)S(1)}, u32[]{:S(2)}, u32[]{:S(2)}) %collective-permute-start.4) | collective-permute-done | bytes 524320 | tf_op jit(solution)/shard_map/ppermute | solution.py:348
  74.7 6.7 %collective-permute-done.5.refs_7_ = bf16[2,16,8192]{2,1,0:T(8,128)(2,1)S(1)} collective-permute-done((bf16[2,16,8192]{2,1,0:T(8,128)(2,1)S(1)}, bf16[2,16,8192]{2,1,0:T(8,128)(2,1)S(1)}, u32[]{:S(2)}, u32[]{:S(2)}) %collective-permute-start.5) | collective-permute-done | bytes 524320 | tf_op jit(solution)/shard_map/ppermute | solution.py:348
  86.0 14.5 %collective-permute-done.6.refs_8_ = bf16[2,64,8192]{2,1,0:T(8,128)(2,1)} collective-permute-done((bf16[2,64,8192]{2,1,0:T(8,128)(2,1)}, bf16[2,64,8192]{2,1,0:T(8,128)(2,1)}, u32[]{:S(2)}, u32[]{:S(2)}) %collective-permute-start.6) | collective-permute-done | bytes 2097184 | tf_op jit(solution)/shard_map/ppermute | solution.py:348
  106.1 9.3 %shard_map.87 = (bf16[2,64,8192]{2,1,0:T(8,128)(2,1)}, bf16[2,64,8192]{2,1,0:T(8,128)(2,1)}, bf16[64,8192]{1,0:T(8,128)(2,1)}, bf16[128,64]{1,0:T(8,128)(2,1)S(1)}, bf16[64,64]{1,0:T(8,128)(2,1)S(1)}) custom-call(s32[1]{0:T(128)} %bitcast.1.end_ref, bf16[2,16,8192]{2,1,0:T(8,128)(2,1)S(1)} %get-tuple-element.41.refs_0_, ...), custom_call_target="tpu_custom_call" | custom-call | flops 872415232 | bytes 19922944 | tf_op jit(solution)/shard_map/pallas_call | solution.py:193
  115.4 7.0 %collective-permute-start.21 = (bf16[2,64,8192]{2,1,0:T(8,128)(2,1)}, bf16[2,64,8192]{2,1,0:T(8,128)(2,1)S(1)}, u32[]{:S(2)}, u32[]{:S(2)}) collective-permute-start(bf16[2,64,8192]{2,1,0:T(8,128)(2,1)} %get-tuple-element.76), channel_id=1, source_target_pairs={{0,4},{1,5},{2,6},{3,7},{12,8},{13,9},{14,10},{15,11},{16,20},{17,... | collective-permute-start | bytes 6291464 | tf_op jit(solution)/shard_map/ppermute | solution.py:348
  126.0 22.6 %collective-permute-done.16.refs_2_ = bf16[2,32,8192]{2,1,0:T(8,128)(2,1)S(1)} collective-permute-done((bf16[2,32,8192]{2,1,0:T(8,128)(2,1)S(1)}, bf16[2,32,8192]{2,1,0:T(8,128)(2,1)S(1)}, u32[]{:S(2)}, u32[]{:S(2)}) %collective-permute-start.16) | collective-permute-done | bytes 1048608 | tf_op jit(solution)/shard_map/ppermute | solution.py:348
  148.6 18.0 %collective-permute-done.17.refs_3_ = bf16[2,32,8192]{2,1,0:T(8,128)(2,1)S(1)} collective-permute-done((bf16[2,32,8192]{2,1,0:T(8,128)(2,1)S(1)}, bf16[2,32,8192]{2,1,0:T(8,128)(2,1)S(1)}, u32[]{:S(2)}, u32[]{:S(2)}) %collective-permute-start.17) | collective-permute-done | bytes 1048608 | tf_op jit(solution)/shard_map/ppermute | solution.py:348
  167.6 10.5 %shard_map.89 = (bf16[32,8192]{1,0:T(8,128)(2,1)S(1)}, bf16[32,8192]{1,0:T(8,128)(2,1)S(1)}, bf16[32,8192]{1,0:T(8,128)(2,1)}, bf16[32,8192]{1,0:T(8,128)(2,1)},...) custom-call(bf16[2,32,8192]{2,1,0:T(8,128)(2,1)S(1)} %get-tuple-element.68.refs_0_, ...), custom_call_target="tpu_custom_call" | custom-call | flops 671088640 | bytes 18874368 | tf_op jit(solution)/shard_map/pallas_call | solution.py:282
  181.0 3.4 %add_convert_fusion = bf16[2,64,8192]{2,1,0:T(8,128)(2,1)} fusion(f32[2,64,8192]{2,1,0:T(8,128)S(1)} %copy-done.8, bf16[2,64,8192]{2,1,0:T(8,128)(2,1)} %collective-permute-done.23), kind=kLoop, calls=%fused_computation | loop fusion | flops 3145728 | bytes 8388608 | tf_op jit(solution)/shard_map/convert_element_type | solution.py:406
  190.2 65.4 %collective-permute-done.12.ends_ref = bf16[64,8192]{1,0:T(8,128)(2,1)S(1)} collective-permute-done((bf16[64,8192]{1,0:T(8,128)(2,1)S(1)}, bf16[64,8192]{1,0:T(8,128)(2,1)S(1)}, u32[]{:S(2)}, u32[]{:S(2)}) %collective-permute-start.12) | collective-permute-done | bytes 1048608 | tf_op jit(solution)/shard_map/ppermute | solution.py:348
  255.8 6.9 %shard_map.88 = (bf16[32,8192]{1,0:T(8,128)(2,1)S(1)}, bf16[32,8192]{1,0:T(8,128)(2,1)}, bf16[32,8192]{1,0:T(8,128)(2,1)}, bf16[32,8192]{1,0:T(8,128)(2,1)}) custom-call(s32[1]{0:T(128)} %bitcast.1.end_ref, bf16[64,8192]{1,0:T(8,128)(2,1)S(1)} %collective-permute-done.12.ends_ref, bf16[2,64,8192]{2,1,0:T(8,128)(2,1)} %collective-permute-done.9.refs_9_.far_ref, ...), custom_call_target="tpu_custom_call" | custom-call | flops 134217728 | bytes 6291456 | tf_op jit(solution)/shard_map/pallas_call | solution.py:317
  264.7 3.0 multiply_reduce_fusion
  269.7 5.1 %all-to-all-start = ((f32[16,8,128]{2,1,0:T(8,128)}), f32[16,8,128]{2,1,0:T(8,128)S(1)}, u32[]{:S(2)}, u32[]{:S(2)}) async-start(f32[16,8,128]{2,1,0:T(8,128)} %broadcast_in_dim.8), calls=%async_computation | async-start | bytes 131072 | tf_op jit(solution)/shard_map/all_to_all | solution.py:35
  274.8 7.3 %collective-permute-done.14.refs_2_ = bf16[32,8192]{1,0:T(8,128)(2,1)S(1)} collective-permute-done((bf16[32,8192]{1,0:T(8,128)(2,1)}, bf16[32,8192]{1,0:T(8,128)(2,1)S(1)}, u32[]{:S(2)}, u32[]{:S(2)}) %collective-permute-start.14) | collective-permute-done | bytes 524320 | tf_op jit(solution)/shard_map/ppermute | solution.py:348
  282.1 10.8 %collective-permute-done.15.refs_3_ = bf16[32,8192]{1,0:T(8,128)(2,1)} collective-permute-done((bf16[32,8192]{1,0:T(8,128)(2,1)}, bf16[32,8192]{1,0:T(8,128)(2,1)}, u32[]{:S(2)}, u32[]{:S(2)}) %collective-permute-start.15) | collective-permute-done | bytes 524320 | tf_op jit(solution)/shard_map/ppermute | solution.py:348
  292.8 6.2 %shard_map.90 = bf16[128,8192]{1,0:T(8,128)(2,1)} custom-call(bf16[256,128]{1,0:T(8,128)(2,1)S(1)} %fusion.place_ref, bf16[32,8192]{1,0:T(8,128)(2,1)S(1)} %get-tuple-element.64.refs_0_, bf16[32,8192]{1,0:T(8,128)(2,1)S(1)} %collective-permute-done.13.refs_1_, bf16[32,8192]{1,0:T(8,128)(2,1)S(1)} %collective-permute-done.14.refs_2_, ...), custom_call_target="tpu_custom_call" | custom-call | flops 536870912 | bytes 6291456 | tf_op jit(solution)/shard_map/pallas_call | solution.py:112
  300.4 6.2 %broadcast_multiply_fusion = (f32[1,64,8192]{2,1,0:T(8,128)}, f32[1,64,8192]{2,1,0:T(8,128)}) fusion(f32[]{:T(128)S(6)} %min_shard_map.3, bf16[2,64,8192]{2,1,0:T(8,128)(2,1)} %collective-permute-done.24, bf16[2,64,8192]{2,1,0:T(8,128)(2,1)} %copy-done.7, f32[2,64,8192]{2,1,0:T(8,128)} %get-tuple-element.75), kind=kLoop, calls=%fused_computation.7 | loop fusion | flops 5242880 | bytes 12582916 | tf_op jit(solution)/shard_map/mul | solution.py:39
  (93 shorter events, 43.7 us)
Async XLA Ops:
  4.1 43.5 %collective-permute-start.10 = (bf16[2,64,8192]{2,1,0:T(8,128)(2,1)}, bf16[2,64,8192]{2,1,0:T(8,128)(2,1)}, u32[]{:S(2)}, u32[]{:S(2)}) collective-permute-start(bf16[2,64,8192]{2,1,0:T(8,128)(2,1)} %constant_dynamic-update-slice_fusion), channel_id=1, source_target_pairs={{4,8},{5,9},{6,10},{7,11},{8,4},{9,5},{10,6},{11,7},{20,24},{21,25... | collective-permute-start | bytes 6291464 | tf_op jit(solution)/shard_map/ppermute | solution.py:348
  6.1 50.9 %collective-permute-start.8 = (bf16[2,64,8192]{2,1,0:T(8,128)(2,1)}, bf16[2,64,8192]{2,1,0:T(8,128)(2,1)}, u32[]{:S(2)}, u32[]{:S(2)}) collective-permute-start(bf16[2,64,8192]{2,1,0:T(8,128)(2,1)} %constant_dynamic-update-slice_fusion), channel_id=1, source_target_pairs={{0,4},{1,5},{2,6},{3,7},{4,0},{5,1},{6,2},{7,3},{8,12},{9,13},{10,... | collective-permute-start | bytes 6291464 | tf_op jit(solution)/shard_map/ppermute | solution.py:348
  16.9 14.8 %collective-permute-start.1 = (bf16[2,16,8192]{2,1,0:T(8,128)(2,1)S(1)}, bf16[2,16,8192]{2,1,0:T(8,128)(2,1)S(1)}, u32[]{:S(2)}, u32[]{:S(2)}) collective-permute-start(bf16[2,16,8192]{2,1,0:T(8,128)(2,1)S(1)} %get-tuple-element.43), channel_id=1, source_target_pairs={{0,2},{1,3},{2,0},{3,1},{4,6},{5,7},{6,4},{7,5},{8,10},{9,11},{10,... | collective-permute-start | bytes 1572872 | tf_op jit(solution)/shard_map/ppermute | solution.py:348
  18.5 23.6 %collective-permute-start.2 = (bf16[2,16,8192]{2,1,0:T(8,128)(2,1)S(1)}, bf16[2,16,8192]{2,1,0:T(8,128)(2,1)S(1)}, u32[]{:S(2)}, u32[]{:S(2)}) collective-permute-start(bf16[2,16,8192]{2,1,0:T(8,128)(2,1)S(1)} %get-tuple-element.44), channel_id=1, source_target_pairs={{0,3},{1,2},{2,1},{3,0},{4,7},{5,6},{6,5},{7,4},{8,11},{9,10},{10,... | collective-permute-start | bytes 1572872 | tf_op jit(solution)/shard_map/ppermute | solution.py:348
  42.1 18.5 %collective-permute-start.3 = (bf16[2,16,8192]{2,1,0:T(8,128)(2,1)S(1)}, bf16[2,16,8192]{2,1,0:T(8,128)(2,1)S(1)}, u32[]{:S(2)}, u32[]{:S(2)}) collective-permute-start(bf16[2,16,8192]{2,1,0:T(8,128)(2,1)S(1)} %get-tuple-element.51), channel_id=1, source_target_pairs={{0,1},{1,0},{2,3},{3,2},{4,5},{5,4},{6,7},{7,6},{8,9},{9,8},{10,11... | collective-permute-start | bytes 1572872 | tf_op jit(solution)/shard_map/ppermute | solution.py:348
  44.2 56.3 %collective-permute-start.6 = (bf16[2,64,8192]{2,1,0:T(8,128)(2,1)}, bf16[2,64,8192]{2,1,0:T(8,128)(2,1)}, u32[]{:S(2)}, u32[]{:S(2)}) collective-permute-start(bf16[2,64,8192]{2,1,0:T(8,128)(2,1)} %pad_maximum_fusion), channel_id=1, source_target_pairs={{0,4},{1,5},{2,6},{3,7},{12,8},{13,9},{14,10},{15,11},{16,20},{17,... | collective-permute-start | bytes 6291464 | tf_op jit(solution)/shard_map/ppermute | solution.py:348
  47.5 55.5 %collective-permute-start.11 = (bf16[2,64,8192]{2,1,0:T(8,128)(2,1)}, bf16[2,64,8192]{2,1,0:T(8,128)(2,1)}, u32[]{:S(2)}, u32[]{:S(2)}) collective-permute-start(bf16[2,64,8192]{2,1,0:T(8,128)(2,1)} %collective-permute-done.10.refs_11_.crossed_ref), channel_id=1, source_target_pairs={{4,0},{5,1},{6,2},{7,3},{8,12},{9,13},{10,14},{11,15},{20,16},{21,... | collective-permute-start | bytes 6291464 | tf_op jit(solution)/shard_map/ppermute | solution.py:348
  57.0 46.0 %collective-permute-start.9 = (bf16[2,64,8192]{2,1,0:T(8,128)(2,1)}, bf16[2,64,8192]{2,1,0:T(8,128)(2,1)}, u32[]{:S(2)}, u32[]{:S(2)}) collective-permute-start(bf16[2,64,8192]{2,1,0:T(8,128)(2,1)} %collective-permute-done.8.refs_4_), channel_id=1, source_target_pairs={{4,8},{5,9},{6,10},{7,11},{8,4},{9,5},{10,6},{11,7},{20,24},{21,25... | collective-permute-start | bytes 6291464 | tf_op jit(solution)/shard_map/ppermute | solution.py:348
  59.1 14.9 %collective-permute-start.4 = (bf16[2,16,8192]{2,1,0:T(8,128)(2,1)S(1)}, bf16[2,16,8192]{2,1,0:T(8,128)(2,1)S(1)}, u32[]{:S(2)}, u32[]{:S(2)}) collective-permute-start(bf16[2,16,8192]{2,1,0:T(8,128)(2,1)S(1)} %get-tuple-element.52), channel_id=1, source_target_pairs={{0,2},{1,3},{2,0},{3,1},{4,6},{5,7},{6,4},{7,5},{8,10},{9,11},{10,... | collective-permute-start | bytes 1572872 | tf_op jit(solution)/shard_map/ppermute | solution.py:348
  61.3 20.0 %collective-permute-start.5 = (bf16[2,16,8192]{2,1,0:T(8,128)(2,1)S(1)}, bf16[2,16,8192]{2,1,0:T(8,128)(2,1)S(1)}, u32[]{:S(2)}, u32[]{:S(2)}) collective-permute-start(bf16[2,16,8192]{2,1,0:T(8,128)(2,1)S(1)} %get-tuple-element.53), channel_id=1, source_target_pairs={{0,3},{1,2},{2,1},{3,0},{4,7},{5,6},{6,5},{7,4},{8,11},{9,10},{10,... | collective-permute-start | bytes 1572872 | tf_op jit(solution)/shard_map/ppermute | solution.py:348
  115.4 62.7 %collective-permute-start.21 = (bf16[2,64,8192]{2,1,0:T(8,128)(2,1)}, bf16[2,64,8192]{2,1,0:T(8,128)(2,1)S(1)}, u32[]{:S(2)}, u32[]{:S(2)}) collective-permute-start(bf16[2,64,8192]{2,1,0:T(8,128)(2,1)} %get-tuple-element.76), channel_id=1, source_target_pairs={{0,4},{1,5},{2,6},{3,7},{12,8},{13,9},{14,10},{15,11},{16,20},{17,... | collective-permute-start | bytes 6291464 | tf_op jit(solution)/shard_map/ppermute | solution.py:348
  122.4 26.2 %collective-permute-start.16 = (bf16[2,32,8192]{2,1,0:T(8,128)(2,1)S(1)}, bf16[2,32,8192]{2,1,0:T(8,128)(2,1)S(1)}, u32[]{:S(2)}, u32[]{:S(2)}) collective-permute-start(bf16[2,32,8192]{2,1,0:T(8,128)(2,1)S(1)} %copy-done.15), channel_id=1, source_target_pairs={{0,2},{1,3},{2,0},{3,1},{4,6},{5,7},{6,4},{7,5},{8,10},{9,11},{10,... | collective-permute-start | bytes 3145736 | tf_op jit(solution)/shard_map/ppermute | solution.py:348
  124.0 42.6 %collective-permute-start.17 = (bf16[2,32,8192]{2,1,0:T(8,128)(2,1)S(1)}, bf16[2,32,8192]{2,1,0:T(8,128)(2,1)S(1)}, u32[]{:S(2)}, u32[]{:S(2)}) collective-permute-start(bf16[2,32,8192]{2,1,0:T(8,128)(2,1)S(1)} %copy-done.14), channel_id=1, source_target_pairs={{0,3},{1,2},{2,1},{3,0},{4,7},{5,6},{6,5},{7,4},{8,11},{9,10},{10,... | collective-permute-start | bytes 3145736 | tf_op jit(solution)/shard_map/ppermute | solution.py:348
  124.0 56.8 %collective-permute-start.23 = (bf16[2,64,8192]{2,1,0:T(8,128)(2,1)}, bf16[2,64,8192]{2,1,0:T(8,128)(2,1)}, u32[]{:S(2)}, u32[]{:S(2)}) collective-permute-start(bf16[2,64,8192]{2,1,0:T(8,128)(2,1)} %get-tuple-element.78), channel_id=1, source_target_pairs={{4,8},{5,9},{6,10},{7,11},{8,4},{9,5},{10,6},{11,7},{20,24},{21,25... | collective-permute-start | bytes 6291464 | tf_op jit(solution)/shard_map/ppermute | solution.py:348
  179.9 82.9 %collective-permute-start.22 = (bf16[2,64,8192]{2,1,0:T(8,128)(2,1)}, bf16[2,64,8192]{2,1,0:T(8,128)(2,1)S(1)}, u32[]{:S(2)}, u32[]{:S(2)}) collective-permute-start(bf16[2,64,8192]{2,1,0:T(8,128)(2,1)} %add_convert_fusion.1), channel_id=1, source_target_pairs={{4,8},{5,9},{6,10},{7,11},{8,4},{9,5},{10,6},{11,7},{20,24},{21,25... | collective-permute-start | bytes 6291464 | tf_op jit(solution)/shard_map/ppermute | solution.py:348
  184.4 80.3 %collective-permute-start.24 = (bf16[2,64,8192]{2,1,0:T(8,128)(2,1)}, bf16[2,64,8192]{2,1,0:T(8,128)(2,1)}, u32[]{:S(2)}, u32[]{:S(2)}) collective-permute-start(bf16[2,64,8192]{2,1,0:T(8,128)(2,1)} %add_convert_fusion), channel_id=1, source_target_pairs={{0,4},{1,5},{2,6},{3,7},{4,0},{5,1},{6,2},{7,3},{8,12},{9,13},{10,... | collective-permute-start | bytes 6291464 | tf_op jit(solution)/shard_map/ppermute | solution.py:348
  186.7 68.9 %collective-permute-start.12 = (bf16[64,8192]{1,0:T(8,128)(2,1)S(1)}, bf16[64,8192]{1,0:T(8,128)(2,1)S(1)}, u32[]{:S(2)}, u32[]{:S(2)}) collective-permute-start(bf16[64,8192]{1,0:T(8,128)(2,1)S(1)} %copy-done.16), channel_id=1, source_target_pairs={{4,0},{5,1},{6,2},{7,3},{8,12},{9,13},{10,14},{11,15},{20,16},{21,... | collective-permute-start | bytes 3145736 | tf_op jit(solution)/shard_map/ppermute | solution.py:348
  188.0 74.7 %collective-permute-start.18 = (bf16[32,8192]{1,0:T(8,128)(2,1)S(1)}, bf16[32,8192]{1,0:T(8,128)(2,1)S(1)}, u32[]{:S(2)}, u32[]{:S(2)}) collective-permute-start(bf16[32,8192]{1,0:T(8,128)(2,1)S(1)} %get-tuple-element.72), channel_id=1, source_target_pairs={{0,1},{1,0},{2,3},{3,2},{4,5},{5,4},{6,7},{7,6},{8,9},{9,8},{10,11... | collective-permute-start | bytes 1572872 | tf_op jit(solution)/shard_map/ppermute | solution.py:348
  188.7 86.1 %collective-permute-start.19 = (bf16[32,8192]{1,0:T(8,128)(2,1)}, bf16[32,8192]{1,0:T(8,128)(2,1)S(1)}, u32[]{:S(2)}, u32[]{:S(2)}) collective-permute-start(bf16[32,8192]{1,0:T(8,128)(2,1)} %get-tuple-element.73), channel_id=1, source_target_pairs={{0,2},{1,3},{2,0},{3,1},{4,6},{5,7},{6,4},{7,5},{8,10},{9,11},{10,... | collective-permute-start | bytes 1572872 | tf_op jit(solution)/shard_map/ppermute | solution.py:348
  255.6 19.2 %collective-permute-start.20 = (bf16[32,8192]{1,0:T(8,128)(2,1)}, bf16[32,8192]{1,0:T(8,128)(2,1)}, u32[]{:S(2)}, u32[]{:S(2)}) collective-permute-start(bf16[32,8192]{1,0:T(8,128)(2,1)} %get-tuple-element.74), channel_id=1, source_target_pairs={{0,3},{1,2},{2,1},{3,0},{4,7},{5,6},{6,5},{7,4},{8,11},{9,10},{10,... | collective-permute-start | bytes 1572872 | tf_op jit(solution)/shard_map/ppermute | solution.py:348
  262.7 12.1 %collective-permute-start.13 = (bf16[32,8192]{1,0:T(8,128)(2,1)}, bf16[32,8192]{1,0:T(8,128)(2,1)S(1)}, u32[]{:S(2)}, u32[]{:S(2)}) collective-permute-start(bf16[32,8192]{1,0:T(8,128)(2,1)} %get-tuple-element.65), channel_id=1, source_target_pairs={{0,1},{1,0},{2,3},{3,2},{4,5},{5,4},{6,7},{7,6},{8,9},{9,8},{10,11... | collective-permute-start | bytes 1572872 | tf_op jit(solution)/shard_map/ppermute | solution.py:348
  262.8 19.3 %collective-permute-start.14 = (bf16[32,8192]{1,0:T(8,128)(2,1)}, bf16[32,8192]{1,0:T(8,128)(2,1)S(1)}, u32[]{:S(2)}, u32[]{:S(2)}) collective-permute-start(bf16[32,8192]{1,0:T(8,128)(2,1)} %get-tuple-element.66), channel_id=1, source_target_pairs={{0,2},{1,3},{2,0},{3,1},{4,6},{5,7},{6,4},{7,5},{8,10},{9,11},{10,... | collective-permute-start | bytes 1572872 | tf_op jit(solution)/shard_map/ppermute | solution.py:348
  264.7 28.1 %collective-permute-start.15 = (bf16[32,8192]{1,0:T(8,128)(2,1)}, bf16[32,8192]{1,0:T(8,128)(2,1)}, u32[]{:S(2)}, u32[]{:S(2)}) collective-permute-start(bf16[32,8192]{1,0:T(8,128)(2,1)} %get-tuple-element.67), channel_id=1, source_target_pairs={{0,3},{1,2},{2,1},{3,0},{4,7},{5,6},{6,5},{7,4},{8,11},{9,10},{10,... | collective-permute-start | bytes 1572872 | tf_op jit(solution)/shard_map/ppermute | solution.py:348
  269.7 29.4 %all-to-all-start = ((f32[16,8,128]{2,1,0:T(8,128)}), f32[16,8,128]{2,1,0:T(8,128)S(1)}, u32[]{:S(2)}, u32[]{:S(2)}) async-start(f32[16,8,128]{2,1,0:T(8,128)} %broadcast_in_dim.8), calls=%async_computation | async-start | bytes 131072 | tf_op jit(solution)/shard_map/all_to_all | solution.py:35
  (21 other events, 145.1 us)

commit v4 on v2

v4 whole, which is shorter than its diff:
```python
import functools

import jax
import jax.numpy as jnp
from jax import lax
from jax.experimental import pallas as pl
from jax.experimental.pallas import tpu as pltpu
from jax.sharding import PartitionSpec as P

BF16, F32 = jnp.bfloat16, jnp.float32
ROWS_OF = (((1,), (1,)), ((), ()))
OUTER = (((0,), (0,)), ((), ()))
INNER = (((1,), (0,)), ((), ()))
ANY = pl.BlockSpec(memory_space=pl.ANY)
VMEM_BYTES = 28 * 2**20
NO_COST = pl.CostEstimate(flops=1, bytes_accessed=1, transcendentals=0)


def dot32(a, b, dims=INNER):
    return lax.dot_general(a, b, dims, preferred_element_type=F32)


def route(token_task_index, task_slot_lookup, ndevices):
    pool = task_slot_lookup.shape[0]
    task_hot = (token_task_index == jnp.arange(pool, dtype=jnp.int32)[None, :]).astype(jnp.int32)
    owner = jnp.sum(task_hot * task_slot_lookup[None, :], axis=1)
    owner_hot = (owner[:, None] == jnp.arange(ndevices, dtype=jnp.int32)[None, :]).astype(jnp.int32)
    before = jnp.cumsum(owner_hot, axis=0) - owner_hot
    position = jnp.sum(before * owner_hot, axis=1)
    return owner, position


def clipped(raw_down, raw_up, ndevices):
    local_sq = jnp.sum(raw_down * raw_down) + jnp.sum(raw_up * raw_up)
    shares = jnp.broadcast_to(local_sq, (ndevices, 8, 128))
    total = jnp.sum(lax.all_to_all(shares, "dp", split_axis=0, concat_axis=0, tiled=True)[:, 0, 0])
    norm = jnp.sqrt(total + 1e-06)
    limit = jnp.sqrt(jnp.float32(2 * raw_down.shape[0] * raw_down.shape[1] * ndevices))
    factor = jnp.minimum(jnp.float32(1.0), limit / norm)
    return (raw_down * factor)[None], (raw_up * factor)[None]


def move_tokens(acts, cotan, token_task_index, task_slot_lookup, pool_down_factors, pool_up_factors):
    ndevices = lax.axis_size("dp")
    tokens, width = acts.shape
    capacity = 2 * ((tokens + ndevices - 1) // ndevices)
    slots = ndevices * capacity
    owner, position = route(token_task_index, task_slot_lookup, ndevices)
    dest = owner * capacity + position
    placed = (jnp.arange(slots, dtype=jnp.int32)[:, None] == dest[None, :]).astype(BF16)

    def exchange(rows):
        rows = rows.reshape(ndevices, capacity, width)
        return lax.all_to_all(rows, "dp", split_axis=0, concat_axis=0, tiled=True).reshape(slots, width)

    down, up = pool_down_factors[0], pool_up_factors[0]
    rows_x = exchange(dot32(placed, acts).astype(BF16))
    rows_g = exchange(dot32(placed, cotan).astype(BF16))
    hidden = dot32(rows_x, down, ROWS_OF).astype(BF16)
    inner = dot32(rows_g, up, ROWS_OF).astype(BF16)
    returned = exchange(dot32(inner, down).astype(BF16))
    grad_acts = dot32(placed, returned, OUTER).astype(BF16)
    raw_up = dot32(hidden, rows_g, OUTER)
    raw_down = dot32(inner, rows_x, OUTER)
    return (grad_acts,) + clipped(raw_down, raw_up, ndevices)


def kernel_params(semantics=("arbitrary",)):
    return pltpu.CompilerParams(dimension_semantics=semantics, vmem_limit_bytes=VMEM_BYTES)


def pack(place, acts, cotan, plane, parts):
    tokens, width = acts.shape
    tile = min(width, 1024)
    cuts, start = [], 0
    for rows in parts:
        for _ in range(plane):
            cuts.append((start, rows))
            start += rows

    def body(place_ref, x_ref, g_ref, *out_refs):
        for k, ref in enumerate((x_ref, g_ref)):
            moved = dot32(place_ref[...], ref[...]).astype(BF16)
            for out_ref, (first, rows) in zip(out_refs, cuts):
                out_ref[k] = moved[first:first + rows]

    rows_spec = pl.BlockSpec((tokens, tile), lambda i: (0, i))
    packed = pl.pallas_call(
        body,
        grid=(width // tile,),
        in_specs=[pl.BlockSpec(place.shape, lambda i: (0, 0)), rows_spec, rows_spec],
        out_specs=[pl.BlockSpec((2, rows, tile), lambda i: (0, 0, i)) for _, rows in cuts],
        out_shape=[jax.ShapeDtypeStruct((2, rows, width), BF16) for _, rows in cuts],
        compiler_params=kernel_params(),
        cost_estimate=NO_COST,
    )(place, acts, cotan)
    return [packed[n * plane:(n + 1) * plane] for n in range(len(parts))]


def unpack(place, blocks, tokens):
    width = blocks[0].shape[1]
    tile = min(width, 1024)

    def body(place_ref, *refs):
        rows = jnp.concatenate([ref[...].reshape(-1, tile) for ref in refs[:-1]], axis=0)
        refs[-1][...] = dot32(place_ref[...], rows, OUTER).astype(BF16)

    return pl.pallas_call(
        body,
        grid=(width // tile,),
        in_specs=[pl.BlockSpec(place.shape, lambda i: (0, 0))]
        + [
            pl.BlockSpec((b.shape[0], tile), lambda i: (0, i))
            if b.ndim == 2
            else pl.BlockSpec((1, b.shape[1], tile), lambda i: (0, 0, i))
            for b in blocks
        ],
        out_specs=pl.BlockSpec((tokens, tile), lambda i: (0, i)),
        out_shape=jax.ShapeDtypeStruct((tokens, width), BF16),
        compiler_params=kernel_params(),
        cost_estimate=NO_COST,
    )(place, *blocks)


def far_sums(k, is_end, stage3, stage2, ends, far, outer, crossed, capacity):
    plane = len(stage3)
    _, rank, width = far.shape
    block = plane * capacity
    tile = min(width, 2048)
    tiles = width // tile
    last = k + 1

    def body(end_ref, *refs):
        stage3_in, stage2_in, refs = refs[:plane], refs[plane:2 * plane], refs[2 * plane:]
        ends_in, far_in, outer_in, crossed_in, sum3_ref, sum2_ref = refs[:6]
        outs, (rows3, rows2, far_w, near_w, left3, left2, sems) = refs[6:-7], refs[-7:]
        step = pl.program_id(0)

        def copies(i):
            cut = pl.ds(i * tile, tile)
            pairs = [(ends_in.at[:, :, cut], rows3.at[:, block:, cut]), (far_in.at[:last, :, cut], far_w.at[:, :, cut])]
            for m in range(plane):
                place = pl.ds(m * capacity, capacity)
                pairs.append((stage3_in[m].at[:, :, cut], rows3.at[:, place, cut]))
                pairs.append((stage2_in[m].at[:, :capacity, cut], rows2.at[:, place, cut]))
            return [pltpu.make_async_copy(src, dst, sems.at[i, n]) for n, (src, dst) in enumerate(pairs)]

        def near_copy(src, i):
            cut = pl.ds(i * tile, tile)
            return pltpu.make_async_copy(src.at[k, :, cut], near_w.at[:, cut], sems.at[i, 2 * plane + 2])

        @pl.when(step == 0)
        def _():
            for i in range(tiles):
                for c in copies(i):
                    c.start()

                @pl.when(end_ref[0] == 1)
                def _():
                    near_copy(outer_in, i).start()

                @pl.when(end_ref[0] != 1)
                def _():
                    near_copy(crossed_in, i).start()

            sum3, sum2 = jnp.zeros((2 * block, rank), F32), jnp.zeros((block, rank), F32)
            for i in range(tiles):
                for c in copies(i):
                    c.wait()
                near_copy(outer_in, i).wait()
                cut = pl.ds(i * tile, tile)
                sum3 += dot32(rows3[k, :, cut], far_w[k, :, cut], ROWS_OF)
                sum2 += dot32(rows2[k, :, cut], near_w[:, cut], ROWS_OF)
            left3[...] = sum3.astype(BF16)
            left2[...] = sum2.astype(BF16)
            if k == 1:
                outs[1][...] = left3[...]
                outs[2][...] = left2[...]

        cut = pl.ds(pl.multiple_of(step * tile, tile), tile)
        sum3_ref[...] = dot32(left3[...], rows3[1 - k, :, cut], OUTER).astype(BF16)
        sum2_ref[...] = dot32(left2[...], rows2[1 - k, :, cut], OUTER).astype(BF16)
        if k == 1:
            outs[0][...] = dot32(left3[block:], far_w[0, :, cut]).astype(BF16)

    def small(rows):
        return pl.BlockSpec((rows, rank), lambda i: (0, 0)), jax.ShapeDtypeStruct((rows, rank), BF16)

    def wide(rows):
        return pl.BlockSpec((rows, tile), lambda i: (0, i)), jax.ShapeDtypeStruct((rows, width), BF16)

    outs = [wide(rank), wide(rank)] + ([wide(block), small(2 * block), small(block)] if k == 1 else [])
    return pl.pallas_call(
        body,
        grid=(tiles,),
        in_specs=[pl.BlockSpec(memory_space=pltpu.SMEM)] + [ANY] * (2 * plane + 4),
        out_specs=[o[0] for o in outs],
        out_shape=[o[1] for o in outs],
        scratch_shapes=[
            pltpu.VMEM((2, 2 * block, width), BF16),
            pltpu.VMEM((2, block, width), BF16),
            pltpu.VMEM((last, rank, width), BF16),
            pltpu.VMEM((rank, width), BF16),
            pltpu.VMEM((2 * block, rank), BF16),
            pltpu.VMEM((block, rank), BF16),
            pltpu.SemaphoreType.DMA((tiles, 2 * plane + 3)),
        ],
        compiler_params=kernel_params(),
        cost_estimate=NO_COST,
    )(is_end, *stage3, *stage2, ends, far, outer, crossed)


def near_groups(is_end, stage, pair, down, up, dx_ends, far, outer, crossed, inner3, inner2, capacity):
    plane = len(stage)
    _, rank, width = pair.shape
    block = plane * capacity
    tile = min(width, 2048)
    tiles = width // tile

    def body(end_ref, *refs):
        stage_in, refs = refs[:plane], refs[plane:]
        pair_in, down_in, up_in, ends_in, far_in, outer_in, crossed_in, inner3, inner2 = refs[:9]
        dx_refs, sum_refs = [refs[9], refs[10], refs[11].at[0], refs[11].at[1]], refs[12:16]
        rows1, rows0, pair_w, own_w, far_w, near_w, ends, hidden1, inner1, hidden0, inner0, sems = refs[16:]
        step = pl.program_id(0)

        def copies(i):
            cut = pl.ds(i * tile, tile)
            pairs = [
                (pair_in.at[:, :, cut], pair_w.at[:, :, cut]),
                (down_in.at[:, cut], own_w.at[0, :, cut]),
                (up_in.at[:, cut], own_w.at[1, :, cut]),
                (far_in.at[0, :, cut], far_w.at[:, cut]),
                (ends_in.at[:, cut], ends.at[:, cut]),
            ]
            for m in range(plane):
                place = pl.ds(m * capacity, capacity)
                pairs.append((stage_in[m].at[:, capacity:2 * capacity, cut], rows1.at[:, place, cut]))
                pairs.append((stage_in[m].at[:, 2 * capacity:, cut], rows0.at[:, place, cut]))
            return [pltpu.make_async_copy(src, dst, sems.at[i, n]) for n, (src, dst) in enumerate(pairs)]

        def near_copy(src, i):
            cut = pl.ds(i * tile, tile)
            return pltpu.make_async_copy(src.at[0, :, cut], near_w.at[:, cut], sems.at[i, 2 * plane + 5])

        @pl.when(step == 0)
        def _():
            for i in range(tiles):
                for c in copies(i):
                    c.start()

                @pl.when(end_ref[0] == 1)
                def _():
                    near_copy(outer_in, i).start()

                @pl.when(end_ref[0] != 1)
                def _():
                    near_copy(crossed_in, i).start()

            sums = [jnp.zeros((block, rank), F32)] * 4
            for i in range(tiles):
                for c in copies(i):
                    c.wait()
                near_copy(outer_in, i).wait()
                cut = pl.ds(i * tile, tile)
                for k in range(2):
                    sums[k] += dot32(rows1[k, :, cut], pair_w[k, :, cut], ROWS_OF)
                    sums[2 + k] += dot32(rows0[k, :, cut], own_w[k, :, cut], ROWS_OF)
            for ref, value in zip((hidden1, inner1, hidden0, inner0), sums):
                ref[...] = value.astype(BF16)

        cut = pl.ds(pl.multiple_of(step * tile, tile), tile)
        sum_refs[0][...] = dot32(hidden1[...], rows1[1, :, cut], OUTER)
        sum_refs[1][...] = dot32(inner1[...], rows1[0, :, cut], OUTER)
        sum_refs[2][...] = dot32(hidden0[...], rows0[1, :, cut], OUTER)
        sum_refs[3][...] = dot32(inner0[...], rows0[0, :, cut], OUTER)
        moved = [
            jnp.where(end_ref[0] == 1, ends[:, cut], dot32(inner3[:block], far_w[:, cut]).astype(BF16)),
            dot32(inner2[...], near_w[:, cut]).astype(BF16),
            dot32(inner1[...], pair_w[0, :, cut]).astype(BF16),
            dot32(inner0[...], own_w[0, :, cut]).astype(BF16),
        ]
        for n, dx in enumerate(moved):
            for m in range(plane):
                dx_refs[m][n * capacity:(n + 1) * capacity] = dx[m * capacity:(m + 1) * capacity]

    return pl.pallas_call(
        body,
        grid=(tiles,),
        in_specs=[pl.BlockSpec(memory_space=pltpu.SMEM)]
        + [ANY] * (plane + 7)
        + [pl.BlockSpec(a.shape, lambda i: (0, 0)) for a in (inner3, inner2)],
        out_specs=[pl.BlockSpec((4 * capacity, tile), lambda i: (0, i))] * 2
        + [pl.BlockSpec((2, 4 * capacity, tile), lambda i: (0, 0, i))]
        + [pl.BlockSpec((rank, tile), lambda i: (0, i))] * 4,
        out_shape=[jax.ShapeDtypeStruct((4 * capacity, width), BF16)] * 2
        + [jax.ShapeDtypeStruct((2, 4 * capacity, width), BF16)]
        + [jax.ShapeDtypeStruct((rank, width), F32)] * 4,
        scratch_shapes=[
            pltpu.VMEM((2, block, width), BF16),
            pltpu.VMEM((2, block, width), BF16),
            pltpu.VMEM((2, rank, width), BF16),
            pltpu.VMEM((2, rank, width), BF16),
            pltpu.VMEM((rank, width), BF16),
            pltpu.VMEM((rank, width), BF16),
            pltpu.VMEM((block, width), BF16),
        ]
        + [pltpu.VMEM((block, rank), BF16)] * 4
        + [pltpu.SemaphoreType.DMA((tiles, 2 * plane + 6))],
        compiler_params=kernel_params(),
        cost_estimate=NO_COST,
    )(is_end, *stage, pair, down, up, dx_ends, far, outer, crossed, inner3, inner2)


def move_adapters(plane, acts, cotan, token_task_index, task_slot_lookup, pool_down_factors, pool_up_factors):
    ndevices = lax.axis_size("dp")
    tokens, width = acts.shape
    capacity = 2 * ((tokens + ndevices - 1) // ndevices)
    me = lax.axis_index("dp")
    z, column = me // plane, me % plane
    is_end = (z == 0) | (z == 3)
    end_flag = is_end.astype(jnp.int32).reshape(1)

    def planes(pairs):
        return [(a * plane + c, b * plane + c) for a, b in pairs for c in range(plane)]

    swap = planes([(0, 1), (1, 0), (2, 3), (3, 2)])
    cross = planes([(1, 2), (2, 1)])
    outward = planes([(1, 0), (2, 3)])
    inward = planes([(0, 1), (3, 2)])

    def send(array, pairs):
        return lax.ppermute(array, "dp", pairs)

    def after(arrays, *others):
        return lax.optimization_barrier((arrays, others))[0]

    def beside(m):
        return [(i, (i // plane) * plane + ((i % plane) ^ m)) for i in range(ndevices)]

    def in_plane(blocks):
        return [blocks[0]] + [send(blocks[m], beside(m)) for m in range(1, plane)]

    down, up = pool_down_factors[0], pool_up_factors[0]
    own = jnp.concatenate([pool_down_factors, pool_up_factors])
    pair = send(own, swap)
    crossed = send(own, cross)

    owner, position = route(token_task_index, task_slot_lookup, ndevices)
    owner_z, turn = owner // plane, (owner % plane) ^ column
    other_mid = jnp.where(z < 2, 2, 1)
    kind = jnp.where(owner_z == z, 0, jnp.where(owner_z == (z ^ 1), 1, jnp.where(owner_z == other_mid, 2, 3)))

    def places(wanted, row, rows):
        hot = jnp.arange(rows, dtype=jnp.int32)[:, None] == row[None, :]
        return (hot & wanted[None, :]).astype(BF16)

    def after(arrays, *others):
        return lax.optimization_barrier((arrays, others))[0]

    block = plane * capacity
    place3 = places(kind == 3, turn * capacity + position, block)
    place_rest = places(kind < 3, (turn * 3 + 2 - kind) * capacity + position, 3 * block)
    place_back = places(kind >= 0, (turn * 4 + 3 - kind) * capacity + position, 4 * block)

    packed3, packed = pack(jnp.concatenate([place3, place_rest]), acts, cotan, plane, (capacity, 3 * capacity))
    stage3 = in_plane(packed3)
    ends = send(jnp.concatenate(stage3, axis=1), inward)
    stage = in_plane(after(packed, stage3))
    outer = send(crossed, outward)
    far = send(pair, cross)

    far_args = (end_flag, stage3, after(stage, ends), ends, far, outer, crossed, capacity)
    up3, up2 = far_sums(0, *far_args)
    up3, up2_in = send(up3, cross), send(up2, inward)
    down3, down2, dx_ends, inner3, inner2 = far_sums(1, after(end_flag, up2), *far_args[1:])
    down3, down2_in = send(down3, cross), send(down2, inward)
    dx_ends = send(dx_ends, outward)

    dx_own, dx_beside, dx_across, up1, down1, up0, down0 = near_groups(
        end_flag, stage, pair, down, up, dx_ends, far, outer, crossed, inner3, inner2, capacity
    )

    def add(a, b):
        return (a.astype(F32) + b.astype(F32)).astype(BF16)

    up2, up1 = send(add(up2, up2_in), cross), send(add(up1, up3), swap)
    down2, down1 = send(add(down2, down2_in), cross), send(add(down1, down3), swap)

    dx_across = send(dx_across, beside(2))
    back = [dx_own, send(dx_beside, beside(1)), dx_across, send(dx_across[1], beside(1))]
    grad_acts = unpack(place_back, back, tokens)
    raw_up = up0 + up2.astype(F32) + up1.astype(F32)
    raw_down = down0 + down2.astype(F32) + down1.astype(F32)
    return (grad_acts,) + clipped(raw_down, raw_up, ndevices)


def solution(mesh):
    plane = 4
    by_planes = mesh.shape["dp"] == 4 * plane

    def per_device(*arrays):
        if by_planes:
            return move_adapters(plane, *arrays)
        return move_tokens(*arrays)

    rows, pools = P(("parts", "dp"), None), P(("parts", "dp"), None, None)
    return jax.shard_map(
        per_device,
        mesh=mesh,
        in_specs=(rows, rows, rows, P("parts"), pools, pools),
        out_specs=(rows, pools, pools),
        check_vma=False,
    )
```

time: 315 us -> 277 us (0.88)
  blocking collectives: 32.2 us -> 0 us
  waiting for transfers between devices: 180 us -> 149 us
  starting transfers between devices: 38.2 us -> 64.2 us
  Pallas kernels: 41.6 us -> 31.5 us
  local copies, waits for them, and re-layouts: 8.27 us -> 16.1 us
    ppermute x22 -> x23, waiting for transfers between devices: 180 us -> 143 us  [send(): return lax.ppermute(array, 'dp', pairs)]
    psum x1 -> x0, blocking collectives: 32.2 us -> none  [clipped(): total = lax.psum(local_sq, 'dp')]
    all_to_all x0 -> x1, starting transfers between devices: none -> 16 us  [clipped(): lax.all_to_all(shares, 'dp', split_axis=0, concat_axis=0, tiled=True)]
    ppermute x22 -> x23, starting transfers between devices: 38.2 us -> 48.2 us  [send(): return lax.ppermute(array, 'dp', pairs)]
    pallas_call x2 -> x1, Pallas kernels: 13.8 us -> 5.73 us  [pack(): pl.pallas_call(body, grid=(width // tile,), in_specs=[pl.BlockSpec(place....]
    unnamed x29 -> x49, local copies, waits for them, and re-layouts: 5.05 us -> 13 us
    all_to_all x0 -> x1, waiting for transfers between devices: none -> 6.4 us  [clipped(): lax.all_to_all(shares, 'dp', split_axis=0, concat_axis=0, tiled=True)]
    mul x1 -> x0, other arithmetic: 6.25 us -> none  [clipped(): return ((raw_down * factor)[None], (raw_up * factor)[None])]
  transfers between devices with their start and end apart: 22 -> 24, of which waited for: 10 -> 11; matrix products, arithmetic and copies ran while one was open for 2% -> 5% of each run, Pallas kernels for 8% -> 7%
where the time goes in v4:
time: 277 us; the launch traced here: 276 us
  waiting for transfers between devices  149 us (54%)
  starting transfers between devices  64.2 us (23%)
  Pallas kernels  31.5 us (11%)
  local copies, waits for them, and re-layouts  16.1 us (6%)
  other arithmetic  12.3 us (4%)
  between operations  2.85 us (1%)
    ppermute x23, waiting for transfers between devices, send(): return lax.ppermute(array, 'dp', pairs)  143 us
    ppermute x23, starting transfers between devices, send(): return lax.ppermute(array, 'dp', pairs)  48.2 us
    all_to_all x1, starting transfers between devices, clipped(): lax.all_to_all(shares, 'dp', split_axis=0, concat_axis=0, tiled=True)  16 us
    unnamed x49, local copies, waits for them, and re-layouts  13 us
    pallas_call x2, Pallas kernels, far_sums(): pl.pallas_call(body, grid=(tiles,), in_specs=[pl.BlockSpec(memory_space=p...  10.8 us
    pallas_call x1, Pallas kernels, near_groups(): pl.pallas_call(body, grid=(tiles,), in_specs=[pl.BlockSpec(memory_space=p...  8.35 us
    pallas_call x1, Pallas kernels, unpack(): pl.pallas_call(body, grid=(width // tile,), in_specs=[pl.BlockSpec(place....  6.64 us
    all_to_all x1, waiting for transfers between devices, clipped(): lax.all_to_all(shares, 'dp', split_axis=0, concat_axis=0, tiled=True)  6.4 us
  transfers between devices with their start and end apart: 24, of which 11 were waited for; matrix products, arithmetic and copies ran while one was open for 5% of the time, Pallas kernels for 7%

profile of v4, /device:TPU:0, one launch (start us, length us, event | category | flops | bytes accessed | tf_op | source)
XLA Modules:
  0.0 276.1 jit_solution(5363436767510016222)
XLA Ops:
  4.8 5.8 %collective-permute-start.6 = (bf16[2,64,8192]{2,1,0:T(8,128)(2,1)}, bf16[2,64,8192]{2,1,0:T(8,128)(2,1)}, u32[]{:S(2)}, u32[]{:S(2)}) collective-permute-start(bf16[2,64,8192]{2,1,0:T(8,128)(2,1)} %constant_dynamic-update-slice_fusion), channel_id=1, source_target_pairs={{0,4},{1,5},{2,6},{3,7},{4,0},{5,1},{6,2},{7,3},{8,12},{9,13},{10,... | collective-permute-start | bytes 6291464 | tf_op jit(solution)/shard_map/ppermute | solution.py:333
  14.6 5.7 %shard_map.85 = (bf16[2,16,8192]{2,1,0:T(8,128)(2,1)S(1)}, bf16[2,16,8192]{2,1,0:T(8,128)(2,1)S(1)}, bf16[2,16,8192]{2,1,0:T(8,128)(2,1)S(1)}, bf16[2,16,8192]{2...) custom-call(bf16[256,128]{1,0:T(8,128)(2,1)S(1)} %add_convert_fusion, ...), custom_call_target="tpu_custom_call" | custom-call | flops 1 | bytes 1 | tf_op jit(solution)/shard_map/pallas_call | solution.py:88
  22.2 12.8 %collective-permute-done.1.refs_2_ = bf16[2,16,8192]{2,1,0:T(8,128)(2,1)S(1)} collective-permute-done((bf16[2,16,8192]{2,1,0:T(8,128)(2,1)S(1)}, bf16[2,16,8192]{2,1,0:T(8,128)(2,1)S(1)}, u32[]{:S(2)}, u32[]{:S(2)}) %collective-permute-start.1) | collective-permute-done | bytes 524320 | tf_op jit(solution)/shard_map/ppermute | solution.py:333
  35.1 10.4 %collective-permute-done.2.refs_3_ = bf16[2,16,8192]{2,1,0:T(8,128)(2,1)S(1)} collective-permute-done((bf16[2,16,8192]{2,1,0:T(8,128)(2,1)S(1)}, bf16[2,16,8192]{2,1,0:T(8,128)(2,1)S(1)}, u32[]{:S(2)}, u32[]{:S(2)}) %collective-permute-start.2) | collective-permute-done | bytes 524320 | tf_op jit(solution)/shard_map/ppermute | solution.py:333
  47.6 3.4 %collective-permute-start.7 = (bf16[2,64,8192]{2,1,0:T(8,128)(2,1)}, bf16[2,64,8192]{2,1,0:T(8,128)(2,1)}, u32[]{:S(2)}, u32[]{:S(2)}) collective-permute-start(bf16[2,64,8192]{2,1,0:T(8,128)(2,1)} %pad_maximum_fusion), channel_id=1, source_target_pairs={{0,4},{1,5},{2,6},{3,7},{12,8},{13,9},{14,10},{15,11},{16,20},{17,... | collective-permute-start | bytes 6291464 | tf_op jit(solution)/shard_map/ppermute | solution.py:333
  52.3 4.7 %collective-permute-done.6.refs_4_ = bf16[2,64,8192]{2,1,0:T(8,128)(2,1)} collective-permute-done((bf16[2,64,8192]{2,1,0:T(8,128)(2,1)}, bf16[2,64,8192]{2,1,0:T(8,128)(2,1)}, u32[]{:S(2)}, u32[]{:S(2)}) %collective-permute-start.6) | collective-permute-done | bytes 2097184 | tf_op jit(solution)/shard_map/ppermute | solution.py:333
  61.6 35.0 %collective-permute-done.4.refs_6_.refs_2_ = bf16[2,48,8192]{2,1,0:T(8,128)(2,1)} collective-permute-done((bf16[2,48,8192]{2,1,0:T(8,128)(2,1)}, bf16[2,48,8192]{2,1,0:T(8,128)(2,1)}, u32[]{:S(2)}, u32[]{:S(2)}) %collective-permute-start.4) | collective-permute-done | bytes 1572896 | tf_op jit(solution)/shard_map/ppermute | solution.py:333
  96.6 29.9 %collective-permute-done.5.refs_7_.refs_3_ = bf16[2,48,8192]{2,1,0:T(8,128)(2,1)} collective-permute-done((bf16[2,48,8192]{2,1,0:T(8,128)(2,1)}, bf16[2,48,8192]{2,1,0:T(8,128)(2,1)}, u32[]{:S(2)}, u32[]{:S(2)}) %collective-permute-start.5) | collective-permute-done | bytes 1572896 | tf_op jit(solution)/shard_map/ppermute | solution.py:333
  131.5 4.9 %shard_map.86 = (bf16[64,8192]{1,0:T(8,128)(2,1)S(1)}, bf16[64,8192]{1,0:T(8,128)(2,1)S(1)}) custom-call(s32[1]{0:T(128)} %bitcast.1.end_ref, bf16[2,16,8192]{2,1,0:T(8,128)(2,1)S(1)} %get-tuple-element.38.refs_0_, bf16[2,16,8192]{2,1,0:T(8,128)(2,1)S(1)} %collective-permute-done.refs_1_, bf16[2,16,8192]{2,1,0:T(8,128)(2,1)S(1)} %copy-done.10, ...), custom_call_target="tpu_custom_call" | custom-call | flops 1 | bytes 1 | tf_op jit(solution)/shard_map/pallas_call | solution.py:193
  136.4 6.0 %collective-permute-start.19 = (bf16[64,8192]{1,0:T(8,128)(2,1)S(1)}, bf16[64,8192]{1,0:T(8,128)(2,1)S(1)}, u32[]{:S(2)}, u32[]{:S(2)}) collective-permute-start(bf16[64,8192]{1,0:T(8,128)(2,1)S(1)} %get-tuple-element.50), channel_id=1, source_target_pairs={{0,4},{1,5},{2,6},{3,7},{12,8},{13,9},{14,10},{15,11},{16,20},{17,... | collective-permute-start | bytes 3145736 | tf_op jit(solution)/shard_map/ppermute | solution.py:333
  142.5 5.8 %shard_map.87 = (bf16[64,8192]{1,0:T(8,128)(2,1)S(1)}, bf16[64,8192]{1,0:T(8,128)(2,1)S(1)}, bf16[64,8192]{1,0:T(8,128)(2,1)S(1)}, bf16[128,64]{1,0:T(8,128)(2,1)S(1)}, bf16[64,64]{1,0:T(8,128)(2,1)S(1)}) custom-call(s32[1]{0:T(128)} %bitcast.1.end_ref, bf16[2,16,8192]{2,1,0:T(8,128)(2,1)S(1)} %get-tuple-element.38.refs_0_, ...), custom_call_target="tpu_custom_call" | custom-call | flops 1 | bytes 1 | tf_op jit(solution)/shard_map/pallas_call | solution.py:193
  150.6 6.3 %collective-permute-start.15 = (bf16[64,8192]{1,0:T(8,128)(2,1)S(1)}, bf16[64,8192]{1,0:T(8,128)(2,1)S(1)}, u32[]{:S(2)}, u32[]{:S(2)}) collective-permute-start(bf16[64,8192]{1,0:T(8,128)(2,1)S(1)} %get-tuple-element.59), channel_id=1, source_target_pairs={{0,4},{1,5},{2,6},{3,7},{12,8},{13,9},{14,10},{15,11},{16,20},{17,... | collective-permute-start | bytes 3145736 | tf_op jit(solution)/shard_map/ppermute | solution.py:333
  157.7 8.2 %collective-permute-done.19 = bf16[64,8192]{1,0:T(8,128)(2,1)S(1)} collective-permute-done((bf16[64,8192]{1,0:T(8,128)(2,1)S(1)}, bf16[64,8192]{1,0:T(8,128)(2,1)S(1)}, u32[]{:S(2)}, u32[]{:S(2)}) %collective-permute-start.19) | collective-permute-done | bytes 1048608 | tf_op jit(solution)/shard_map/ppermute | solution.py:333
  166.9 9.2 %collective-permute-done.11.refs_7_ = bf16[64,8192]{1,0:T(8,128)(2,1)S(1)} collective-permute-done((bf16[64,8192]{1,0:T(8,128)(2,1)S(1)}, bf16[64,8192]{1,0:T(8,128)(2,1)S(1)}, u32[]{:S(2)}, u32[]{:S(2)}) %collective-permute-start.11) | collective-permute-done | bytes 1048608 | tf_op jit(solution)/shard_map/ppermute | solution.py:333
  176.1 8.4 %shard_map.88 = (bf16[64,8192]{1,0:T(8,128)(2,1)S(1)}, bf16[64,8192]{1,0:T(8,128)(2,1)S(1)}, bf16[2,64,8192]{2,1,0:T(8,128)(2,1)}, f32[64,8192]{1,0:T(8,128)S(1)...) custom-call(s32[1]{0:T(128)} %bitcast.1.end_ref, bf16[2,48,8192]{2,1,0:T(8,128)(2,1)S(1)} %copy-done.3, ...), custom_call_target="tpu_custom_call" | custom-call | flops 1 | bytes 1 | tf_op jit(solution)/shard_map/pallas_call | solution.py:287
  184.8 3.6 %collective-permute-done.15 = bf16[64,8192]{1,0:T(8,128)(2,1)S(1)} collective-permute-done((bf16[64,8192]{1,0:T(8,128)(2,1)S(1)}, bf16[64,8192]{1,0:T(8,128)(2,1)S(1)}, u32[]{:S(2)}, u32[]{:S(2)}) %collective-permute-start.15) | collective-permute-done | bytes 1048608 | tf_op jit(solution)/shard_map/ppermute | solution.py:333
  190.5 12.7 %collective-permute-start.18 = (bf16[64,8192]{1,0:T(8,128)(2,1)S(1)}, bf16[64,8192]{1,0:T(8,128)(2,1)S(1)}, u32[]{:S(2)}, u32[]{:S(2)}) collective-permute-start(bf16[64,8192]{1,0:T(8,128)(2,1)S(1)} %add_convert_fusion.2), channel_id=1, source_target_pairs={{0,4},{1,5},{2,6},{3,7},{4,0},{5,1},{6,2},{7,3},{8,12},{9,13},{10,... | collective-permute-start | bytes 3145736 | tf_op jit(solution)/shard_map/ppermute | solution.py:333
  203.2 7.7 %collective-permute-done.22 = bf16[64,8192]{1,0:T(8,128)(2,1)S(1)} collective-permute-done((bf16[64,8192]{1,0:T(8,128)(2,1)S(1)}, bf16[64,8192]{1,0:T(8,128)(2,1)S(1)}, u32[]{:S(2)}, u32[]{:S(2)}) %collective-permute-start.22) | collective-permute-done | bytes 1048608 | tf_op jit(solution)/shard_map/ppermute | solution.py:333
  212.1 21.1 %collective-permute-done.18 = bf16[64,8192]{1,0:T(8,128)(2,1)S(1)} collective-permute-done((bf16[64,8192]{1,0:T(8,128)(2,1)S(1)}, bf16[64,8192]{1,0:T(8,128)(2,1)S(1)}, u32[]{:S(2)}, u32[]{:S(2)}) %collective-permute-start.18) | collective-permute-done | bytes 1048608 | tf_op jit(solution)/shard_map/ppermute | solution.py:333
  234.2 2.5 multiply_reduce_fusion.1
  238.5 16.0 %all-to-all-start = ((f32[16,8,128]{2,1,0:T(8,128)}), f32[16,8,128]{2,1,0:T(8,128)S(1)}, u32[]{:S(2)}, u32[]{:S(2)}) async-start(f32[16,8,128]{2,1,0:T(8,128)} %broadcast_in_dim.13), calls=%async_computation | async-start | bytes 131072 | tf_op jit(solution)/shard_map/all_to_all | solution.py:36
  255.0 6.4 %all-to-all-done = f32[16,8,128]{2,1,0:T(8,128)S(1)} async-done(((f32[16,8,128]{2,1,0:T(8,128)}), f32[16,8,128]{2,1,0:T(8,128)S(1)}, u32[]{:S(2)}, u32[]{:S(2)}) %all-to-all-start) | async-done | bytes 65568 | tf_op jit(solution)/shard_map/all_to_all | solution.py:36
  264.5 5.0 %multiply_bitcast_fusion = (f32[1,64,8192]{2,1,0:T(8,128)}, f32[1,64,8192]{2,1,0:T(8,128)}) fusion(f32[]{:T(128)S(6)} %min_shard_map.3, bf16[64,8192]{1,0:T(8,128)(2,1)} %copy-done.20, f32[64,8192]{1,0:T(8,128)S(1)} %get-tuple-element.62, bf16[64,8192]{1,0:T(8,128)(2,1)} %copy-done.19, bf16[64,8192]{1,0:T(8,128)(2,1)} %copy-done.21, ...), kind=kLoop, calls=%fused_computation.1 | loop fusion | flops 5242880 | bytes 12582916 | tf_op jit(solution)/shard_map/broadcast_in_dim | solution.py:40
  269.5 6.6 %shard_map.89 = bf16[128,8192]{1,0:T(8,128)(2,1)} custom-call(bf16[256,128]{1,0:T(8,128)(2,1)S(1)} %fusion.place_ref, bf16[64,8192]{1,0:T(8,128)(2,1)S(1)} %get-tuple-element.55.refs_0_, bf16[64,8192]{1,0:T(8,128)(2,1)} %collective-permute-done.12.refs_1_, bf16[2,64,8192]{2,1,0:T(8,128)(2,1)} %collective-permute-done.13.refs_2_, ...), custom_call_target="tpu_custom_call" | custom-call | flops 1 | bytes 1 | tf_op jit(solution)/shard_map/pallas_call | solution.py:108
  (102 shorter events, 35.1 us)
Async XLA Ops:
  4.1 47.0 %collective-permute-start.9 = (bf16[2,64,8192]{2,1,0:T(8,128)(2,1)}, bf16[2,64,8192]{2,1,0:T(8,128)(2,1)S(1)}, u32[]{:S(2)}, u32[]{:S(2)}) collective-permute-start(bf16[2,64,8192]{2,1,0:T(8,128)(2,1)} %constant_dynamic-update-slice_fusion), channel_id=1, source_target_pairs={{4,8},{5,9},{6,10},{7,11},{8,4},{9,5},{10,6},{11,7},{20,24},{21,25... | collective-permute-start | bytes 6291464 | tf_op jit(solution)/shard_map/ppermute | solution.py:333
  4.8 52.2 %collective-permute-start.6 = (bf16[2,64,8192]{2,1,0:T(8,128)(2,1)}, bf16[2,64,8192]{2,1,0:T(8,128)(2,1)}, u32[]{:S(2)}, u32[]{:S(2)}) collective-permute-start(bf16[2,64,8192]{2,1,0:T(8,128)(2,1)} %constant_dynamic-update-slice_fusion), channel_id=1, source_target_pairs={{0,4},{1,5},{2,6},{3,7},{4,0},{5,1},{6,2},{7,3},{8,12},{9,13},{10,... | collective-permute-start | bytes 6291464 | tf_op jit(solution)/shard_map/ppermute | solution.py:333
  20.3 1.9 collective-permute-start
  20.3 14.7 %collective-permute-start.1 = (bf16[2,16,8192]{2,1,0:T(8,128)(2,1)S(1)}, bf16[2,16,8192]{2,1,0:T(8,128)(2,1)S(1)}, u32[]{:S(2)}, u32[]{:S(2)}) collective-permute-start(bf16[2,16,8192]{2,1,0:T(8,128)(2,1)S(1)} %get-tuple-element.40), channel_id=1, source_target_pairs={{0,2},{1,3},{2,0},{3,1},{4,6},{5,7},{6,4},{7,5},{8,10},{9,11},{10,... | collective-permute-start | bytes 1572872 | tf_op jit(solution)/shard_map/ppermute | solution.py:333
  21.8 23.6 %collective-permute-start.2 = (bf16[2,16,8192]{2,1,0:T(8,128)(2,1)S(1)}, bf16[2,16,8192]{2,1,0:T(8,128)(2,1)S(1)}, u32[]{:S(2)}, u32[]{:S(2)}) collective-permute-start(bf16[2,16,8192]{2,1,0:T(8,128)(2,1)S(1)} %get-tuple-element.41), channel_id=1, source_target_pairs={{0,3},{1,2},{2,1},{3,0},{4,7},{5,6},{6,5},{7,4},{8,11},{9,10},{10,... | collective-permute-start | bytes 1572872 | tf_op jit(solution)/shard_map/ppermute | solution.py:333
  45.5 15.0 %collective-permute-start.3 = (bf16[2,48,8192]{2,1,0:T(8,128)(2,1)S(1)}, bf16[2,48,8192]{2,1,0:T(8,128)(2,1)S(1)}, u32[]{:S(2)}, u32[]{:S(2)}) collective-permute-start(bf16[2,48,8192]{2,1,0:T(8,128)(2,1)S(1)} %get-tuple-element.43), channel_id=1, source_target_pairs={{0,1},{1,0},{2,3},{3,2},{4,5},{5,4},{6,7},{7,6},{8,9},{9,8},{10,11... | collective-permute-start | bytes 4718600 | tf_op jit(solution)/shard_map/ppermute | solution.py:333
  47.6 78.9 %collective-permute-start.7 = (bf16[2,64,8192]{2,1,0:T(8,128)(2,1)}, bf16[2,64,8192]{2,1,0:T(8,128)(2,1)}, u32[]{:S(2)}, u32[]{:S(2)}) collective-permute-start(bf16[2,64,8192]{2,1,0:T(8,128)(2,1)} %pad_maximum_fusion), channel_id=1, source_target_pairs={{0,4},{1,5},{2,6},{3,7},{12,8},{13,9},{14,10},{15,11},{16,20},{17,... | collective-permute-start | bytes 6291464 | tf_op jit(solution)/shard_map/ppermute | solution.py:333
  51.0 75.6 %collective-permute-start.10 = (bf16[2,64,8192]{2,1,0:T(8,128)(2,1)S(1)}, bf16[2,64,8192]{2,1,0:T(8,128)(2,1)}, u32[]{:S(2)}, u32[]{:S(2)}) collective-permute-start(bf16[2,64,8192]{2,1,0:T(8,128)(2,1)S(1)} %collective-permute-done.9.refs_11_.refs_10_), channel_id=1, source_target_pairs={{4,0},{5,1},{6,2},{7,3},{8,12},{9,13},{10,14},{11,15},{20,16},{21,... | collective-permute-start | bytes 6291464 | tf_op jit(solution)/shard_map/ppermute | solution.py:333
  57.0 69.6 %collective-permute-start.8 = (bf16[2,64,8192]{2,1,0:T(8,128)(2,1)}, bf16[2,64,8192]{2,1,0:T(8,128)(2,1)}, u32[]{:S(2)}, u32[]{:S(2)}) collective-permute-start(bf16[2,64,8192]{2,1,0:T(8,128)(2,1)} %collective-permute-done.6.refs_4_), channel_id=1, source_target_pairs={{4,8},{5,9},{6,10},{7,11},{8,4},{9,5},{10,6},{11,7},{20,24},{21,25... | collective-permute-start | bytes 6291464 | tf_op jit(solution)/shard_map/ppermute | solution.py:333
  59.0 37.6 %collective-permute-start.4 = (bf16[2,48,8192]{2,1,0:T(8,128)(2,1)}, bf16[2,48,8192]{2,1,0:T(8,128)(2,1)}, u32[]{:S(2)}, u32[]{:S(2)}) collective-permute-start(bf16[2,48,8192]{2,1,0:T(8,128)(2,1)} %get-tuple-element.44), channel_id=1, source_target_pairs={{0,2},{1,3},{2,0},{3,1},{4,6},{5,7},{6,4},{7,5},{8,10},{9,11},{10,... | collective-permute-start | bytes 4718600 | tf_op jit(solution)/shard_map/ppermute | solution.py:333
  61.6 64.9 %collective-permute-start.5 = (bf16[2,48,8192]{2,1,0:T(8,128)(2,1)}, bf16[2,48,8192]{2,1,0:T(8,128)(2,1)}, u32[]{:S(2)}, u32[]{:S(2)}) collective-permute-start(bf16[2,48,8192]{2,1,0:T(8,128)(2,1)} %get-tuple-element.45), channel_id=1, source_target_pairs={{0,3},{1,2},{2,1},{3,0},{4,7},{5,6},{6,5},{7,4},{8,11},{9,10},{10,... | collective-permute-start | bytes 4718600 | tf_op jit(solution)/shard_map/ppermute | solution.py:333
  136.4 29.5 %collective-permute-start.19 = (bf16[64,8192]{1,0:T(8,128)(2,1)S(1)}, bf16[64,8192]{1,0:T(8,128)(2,1)S(1)}, u32[]{:S(2)}, u32[]{:S(2)}) collective-permute-start(bf16[64,8192]{1,0:T(8,128)(2,1)S(1)} %get-tuple-element.50), channel_id=1, source_target_pairs={{0,4},{1,5},{2,6},{3,7},{12,8},{13,9},{14,10},{15,11},{16,20},{17,... | collective-permute-start | bytes 3145736 | tf_op jit(solution)/shard_map/ppermute | solution.py:333
  148.4 27.8 %collective-permute-start.11 = (bf16[64,8192]{1,0:T(8,128)(2,1)S(1)}, bf16[64,8192]{1,0:T(8,128)(2,1)S(1)}, u32[]{:S(2)}, u32[]{:S(2)}) collective-permute-start(bf16[64,8192]{1,0:T(8,128)(2,1)S(1)} %get-tuple-element.52), channel_id=1, source_target_pairs={{4,0},{5,1},{6,2},{7,3},{8,12},{9,13},{10,14},{11,15},{20,16},{21,... | collective-permute-start | bytes 3145736 | tf_op jit(solution)/shard_map/ppermute | solution.py:333
  149.9 34.6 %collective-permute-start.21 = (bf16[64,8192]{1,0:T(8,128)(2,1)S(1)}, bf16[64,8192]{1,0:T(8,128)(2,1)S(1)}, u32[]{:S(2)}, u32[]{:S(2)}) collective-permute-start(bf16[64,8192]{1,0:T(8,128)(2,1)S(1)} %get-tuple-element.64), channel_id=1, source_target_pairs={{4,8},{5,9},{6,10},{7,11},{8,4},{9,5},{10,6},{11,7},{20,24},{21,25... | collective-permute-start | bytes 3145736 | tf_op jit(solution)/shard_map/ppermute | solution.py:333
  150.6 37.8 %collective-permute-start.15 = (bf16[64,8192]{1,0:T(8,128)(2,1)S(1)}, bf16[64,8192]{1,0:T(8,128)(2,1)S(1)}, u32[]{:S(2)}, u32[]{:S(2)}) collective-permute-start(bf16[64,8192]{1,0:T(8,128)(2,1)S(1)} %get-tuple-element.59), channel_id=1, source_target_pairs={{0,4},{1,5},{2,6},{3,7},{12,8},{13,9},{14,10},{15,11},{16,20},{17,... | collective-permute-start | bytes 3145736 | tf_op jit(solution)/shard_map/ppermute | solution.py:333
  157.0 33.4 %collective-permute-start.17 = (bf16[64,8192]{1,0:T(8,128)(2,1)S(1)}, bf16[64,8192]{1,0:T(8,128)(2,1)S(1)}, u32[]{:S(2)}, u32[]{:S(2)}) collective-permute-start(bf16[64,8192]{1,0:T(8,128)(2,1)S(1)} %get-tuple-element.61), channel_id=1, source_target_pairs={{4,8},{5,9},{6,10},{7,11},{8,4},{9,5},{10,6},{11,7},{20,24},{21,25... | collective-permute-start | bytes 3145736 | tf_op jit(solution)/shard_map/ppermute | solution.py:333
  166.2 37.0 %collective-permute-start.20 = (bf16[64,8192]{1,0:T(8,128)(2,1)S(1)}, bf16[64,8192]{1,0:T(8,128)(2,1)S(1)}, u32[]{:S(2)}, u32[]{:S(2)}) collective-permute-start(bf16[64,8192]{1,0:T(8,128)(2,1)S(1)} %add_convert_fusion.1), channel_id=1, source_target_pairs={{4,8},{5,9},{6,10},{7,11},{8,4},{9,5},{10,6},{11,7},{20,24},{21,25... | collective-permute-start | bytes 3145736 | tf_op jit(solution)/shard_map/ppermute | solution.py:333
  184.7 26.2 %collective-permute-start.22 = (bf16[64,8192]{1,0:T(8,128)(2,1)S(1)}, bf16[64,8192]{1,0:T(8,128)(2,1)S(1)}, u32[]{:S(2)}, u32[]{:S(2)}) collective-permute-start(bf16[64,8192]{1,0:T(8,128)(2,1)S(1)} %add_convert_fusion), channel_id=1, source_target_pairs={{0,4},{1,5},{2,6},{3,7},{4,0},{5,1},{6,2},{7,3},{8,12},{9,13},{10,... | collective-permute-start | bytes 3145736 | tf_op jit(solution)/shard_map/ppermute | solution.py:333
  188.7 23.4 %collective-permute-start.16 = (bf16[64,8192]{1,0:T(8,128)(2,1)S(1)}, bf16[64,8192]{1,0:T(8,128)(2,1)}, u32[]{:S(2)}, u32[]{:S(2)}) collective-permute-start(bf16[64,8192]{1,0:T(8,128)(2,1)S(1)} %add_convert_fusion.3), channel_id=1, source_target_pairs={{4,8},{5,9},{6,10},{7,11},{8,4},{9,5},{10,6},{11,7},{20,24},{21,25... | collective-permute-start | bytes 3145736 | tf_op jit(solution)/shard_map/ppermute | solution.py:333
  190.3 72.3 %collective-permute-start.13 = (bf16[2,64,8192]{2,1,0:T(8,128)(2,1)}, bf16[2,64,8192]{2,1,0:T(8,128)(2,1)}, u32[]{:S(2)}, u32[]{:S(2)}) collective-permute-start(bf16[2,64,8192]{2,1,0:T(8,128)(2,1)} %get-tuple-element.57), channel_id=1, source_target_pairs={{0,2},{1,3},{2,0},{3,1},{4,6},{5,7},{6,4},{7,5},{8,10},{9,11},{10,... | collective-permute-start | bytes 6291464 | tf_op jit(solution)/shard_map/ppermute | solution.py:333
  190.5 42.7 %collective-permute-start.18 = (bf16[64,8192]{1,0:T(8,128)(2,1)S(1)}, bf16[64,8192]{1,0:T(8,128)(2,1)S(1)}, u32[]{:S(2)}, u32[]{:S(2)}) collective-permute-start(bf16[64,8192]{1,0:T(8,128)(2,1)S(1)} %add_convert_fusion.2), channel_id=1, source_target_pairs={{0,4},{1,5},{2,6},{3,7},{4,0},{5,1},{6,2},{7,3},{8,12},{9,13},{10,... | collective-permute-start | bytes 3145736 | tf_op jit(solution)/shard_map/ppermute | solution.py:333
  238.5 22.9 %all-to-all-start = ((f32[16,8,128]{2,1,0:T(8,128)}), f32[16,8,128]{2,1,0:T(8,128)S(1)}, u32[]{:S(2)}, u32[]{:S(2)}) async-start(f32[16,8,128]{2,1,0:T(8,128)} %broadcast_in_dim.13), calls=%async_computation | async-start | bytes 131072 | tf_op jit(solution)/shard_map/all_to_all | solution.py:36
  254.6 14.9 %collective-permute-start.12 = (bf16[64,8192]{1,0:T(8,128)(2,1)}, bf16[64,8192]{1,0:T(8,128)(2,1)}, u32[]{:S(2)}, u32[]{:S(2)}) collective-permute-start(bf16[64,8192]{1,0:T(8,128)(2,1)} %copy-done.18), channel_id=1, source_target_pairs={{0,1},{1,0},{2,3},{3,2},{4,5},{5,4},{6,7},{7,6},{8,9},{9,8},{10,11... | collective-permute-start | bytes 3145736 | tf_op jit(solution)/shard_map/ppermute | solution.py:333
  264.1 5.4 %collective-permute-start.14 = (bf16[64,8192]{1,0:T(8,128)(2,1)S(1)}, bf16[64,8192]{1,0:T(8,128)(2,1)S(1)}, u32[]{:S(2)}, u32[]{:S(2)}) collective-permute-start(bf16[64,8192]{1,0:T(8,128)(2,1)S(1)} %slice_bitcast_fusion), channel_id=1, source_target_pairs={{0,1},{1,0},{2,3},{3,2},{4,5},{5,4},{6,7},{7,6},{8,9},{9,8},{10,11... | collective-permute-start | bytes 3145736 | tf_op jit(solution)/shard_map/ppermute | solution.py:333
  (24 other events, 398.3 us)

commit v5 on v4

v5 whole, which is shorter than its diff:
```python
import jax
import jax.numpy as jnp
from jax import lax
from jax.experimental import pallas as pl
from jax.experimental.pallas import tpu as pltpu
from jax.sharding import PartitionSpec as P

BF16, F32 = jnp.bfloat16, jnp.float32
ROWS_OF = (((1,), (1,)), ((), ()))
OUTER = (((0,), (0,)), ((), ()))
INNER = (((1,), (0,)), ((), ()))
HBM = pl.BlockSpec(memory_space=pltpu.HBM)
WHOLE = pl.BlockSpec(memory_space=pltpu.VMEM)
VMEM_BYTES = 20 * 2**20


def dot32(a, b, dims=INNER):
    return lax.dot_general(a, b, dims, preferred_element_type=F32)


def route(token_task_index, task_slot_lookup, ndevices):
    pool = task_slot_lookup.shape[0]
    task_hot = (token_task_index == jnp.arange(pool, dtype=jnp.int32)[None, :]).astype(jnp.int32)
    owner = jnp.sum(task_hot * task_slot_lookup[None, :], axis=1)
    owner_hot = (owner[:, None] == jnp.arange(ndevices, dtype=jnp.int32)[None, :]).astype(jnp.int32)
    before = jnp.cumsum(owner_hot, axis=0) - owner_hot
    position = jnp.sum(before * owner_hot, axis=1)
    return owner, position


def clipped(raw_down, raw_up, ndevices, add_up):
    local_sq = jnp.sum(raw_down * raw_down) + jnp.sum(raw_up * raw_up)
    total = add_up(local_sq)
    norm = jnp.sqrt(total + 1e-06)
    limit = jnp.sqrt(jnp.float32(2 * raw_down.shape[0] * raw_down.shape[1] * ndevices))
    factor = jnp.minimum(jnp.float32(1.0), limit / norm)
    return (raw_down * factor)[None], (raw_up * factor)[None]


def move_tokens(acts, cotan, token_task_index, task_slot_lookup, pool_down_factors, pool_up_factors):
    ndevices = lax.axis_size("dp")
    tokens, width = acts.shape
    capacity = 2 * ((tokens + ndevices - 1) // ndevices)
    slots = ndevices * capacity
    owner, position = route(token_task_index, task_slot_lookup, ndevices)
    dest = owner * capacity + position
    placed = (jnp.arange(slots, dtype=jnp.int32)[:, None] == dest[None, :]).astype(BF16)

    def exchange(rows):
        rows = rows.reshape(ndevices, capacity, width)
        return lax.all_to_all(rows, "dp", split_axis=0, concat_axis=0, tiled=True).reshape(slots, width)

    down, up = pool_down_factors[0], pool_up_factors[0]
    rows_x = exchange(dot32(placed, acts).astype(BF16))
    rows_g = exchange(dot32(placed, cotan).astype(BF16))
    hidden = dot32(rows_x, down, ROWS_OF).astype(BF16)
    inner = dot32(rows_g, up, ROWS_OF).astype(BF16)
    returned = exchange(dot32(inner, down).astype(BF16))
    grad_acts = dot32(placed, returned, OUTER).astype(BF16)
    raw_up = dot32(hidden, rows_g, OUTER)
    raw_down = dot32(inner, rows_x, OUTER)
    return (grad_acts,) + clipped(raw_down, raw_up, ndevices, lambda term: lax.psum(term, "dp"))


def in_hbm(*arrays):
    return [pltpu.with_memory_space_constraint(a, pltpu.HBM) for a in arrays]


def in_vmem(*arrays):
    return [pltpu.with_memory_space_constraint(a, pltpu.VMEM) for a in arrays]


def kernel_params(semantics=("arbitrary",)):
    return pltpu.CompilerParams(dimension_semantics=semantics, vmem_limit_bytes=VMEM_BYTES)


def pack(place, acts, cotan, shapes):
    tokens, width = acts.shape
    tile = min(width, 1024)
    tiles = width // tile

    def body(place_ref, x_in, g_in, *refs):
        out_refs, (rows, sems) = refs[:-2], refs[-2:]
        step = pl.program_id(0)

        def copies(i):
            cut = pl.ds(pl.multiple_of(i * tile, tile), tile)
            return [pltpu.make_async_copy(r.at[:, cut], rows.at[k, :, cut], sems.at[k, i]) for k, r in enumerate((x_in, g_in))]

        @pl.when(step == 0)
        def _():
            for i in range(tiles):
                for c in copies(i):
                    c.start()

        for c in copies(step):
            c.wait()
        cut = pl.ds(pl.multiple_of(step * tile, tile), tile)
        for k in range(2):
            moved = dot32(place_ref[...], rows[k, :, cut]).astype(BF16)
            first = 0
            for out_ref, (columns, size) in zip(out_refs, shapes):
                for c in range(columns):
                    out_ref[c, k] = moved[first:first + size]
                    first += size

    return pl.pallas_call(
        body,
        grid=(tiles,),
        in_specs=[pl.BlockSpec(place.shape, lambda i: (0, 0)), HBM, HBM],
        out_specs=[pl.BlockSpec((c, 2, size, tile), lambda i: (0, 0, 0, i)) for c, size in shapes],
        out_shape=[jax.ShapeDtypeStruct((c, 2, size, width), BF16) for c, size in shapes],
        scratch_shapes=[pltpu.VMEM((2, tokens, width), BF16), pltpu.SemaphoreType.DMA((2, tiles))],
        compiler_params=kernel_params(),
    )(place, *in_hbm(acts, cotan))


def unpack(place, blocks, tokens):
    width = blocks[0].shape[1]
    tile = min(width, 2048)

    def body(place_ref, *refs):
        rows = jnp.concatenate([ref[...].reshape(-1, tile) for ref in refs[:-1]], axis=0)
        refs[-1][...] = dot32(place_ref[...], rows).astype(BF16)

    return pl.pallas_call(
        body,
        grid=(width // tile,),
        in_specs=[pl.BlockSpec(place.shape, lambda i: (0, 0))]
        + [
            pl.BlockSpec((b.shape[0], tile), lambda i: (0, i))
            if b.ndim == 2
            else pl.BlockSpec((1, b.shape[1], tile), lambda i: (0, 0, i))
            for b in blocks
        ],
        out_specs=pl.BlockSpec((tokens, tile), lambda i: (0, i)),
        out_shape=jax.ShapeDtypeStruct((tokens, width), BF16),
        compiler_params=kernel_params(),
    )(place, *blocks)


def far_groups(is_end, stage3, stage2, ends, far, outer, crossed, capacity, first2):
    plane = len(stage3)
    _, rank, width = far.shape
    block = plane * capacity
    tile = min(width, 2048)
    tiles = width // tile

    def body(end_ref, *refs):
        stage3_in, stage2_in, refs = refs[:plane], refs[plane:2 * plane], refs[2 * plane:]
        ends_in, far_in, outer_in, crossed_in = refs[:4]
        sum3_refs, sum2_refs, swap_ref, inner2_ref, dx_ref = refs[4:6], refs[6:8], *refs[8:11]
        left3, left2 = refs[11:]
        step = pl.program_id(0)

        def rows3(k, cut):
            return jnp.concatenate([r[0, k, :capacity, cut] for r in stage3_in] + [ends_in[k, :, cut]], axis=0)

        def rows2(k, cut):
            return jnp.concatenate([r[0, k, first:first + capacity, cut] for r, first in zip(stage2_in, first2)], axis=0)

        @pl.when(step == 0)
        def _():
            sums3, sums2 = [jnp.zeros((2 * block, rank), F32)] * 2, [jnp.zeros((block, rank), F32)] * 2
            for i in range(tiles):
                cut = pl.ds(i * tile, tile)
                for k in range(2):
                    near = jnp.where(end_ref[0] == 1, outer_in[k, :, cut], crossed_in[k, :, cut])
                    sums3[k] += dot32(rows3(k, cut), far_in[k, :, cut], ROWS_OF)
                    sums2[k] += dot32(rows2(k, cut), near, ROWS_OF)
            for k in range(2):
                left3[k] = sums3[k].astype(BF16)
                left2[k] = sums2[k].astype(BF16)
            inner2_ref[...] = left2[1]

        cut = pl.ds(pl.multiple_of(step * tile, tile), tile)
        for k in range(2):
            sum3_refs[k][...] = dot32(left3[k], rows3(1 - k, cut), OUTER).astype(BF16)
            sum2_refs[k][...] = dot32(left2[k], rows2(1 - k, cut), OUTER).astype(BF16)
        dx = dot32(left3[1], far_in[0, :, cut]).astype(BF16)
        dx_ref[...] = dx[:block]
        swap_ref[...] = jnp.where(end_ref[0] == 1, sum2_refs[1][...], dx[block:])

    def wide(rows):
        return pl.BlockSpec((rows, tile), lambda i: (0, i)), jax.ShapeDtypeStruct((rows, width), BF16)

    outs = [wide(rank)] * 4 + [wide(block)]
    outs += [(pl.BlockSpec((block, rank), lambda i: (0, 0)), jax.ShapeDtypeStruct((block, rank), BF16)), wide(block)]
    return pl.pallas_call(
        body,
        grid=(tiles,),
        in_specs=[pl.BlockSpec(memory_space=pltpu.SMEM)] + [WHOLE] * (2 * plane + 4),
        out_specs=[o[0] for o in outs],
        out_shape=[o[1] for o in outs],
        scratch_shapes=[pltpu.VMEM((2, 2 * block, rank), BF16), pltpu.VMEM((2, block, rank), BF16)],
        compiler_params=kernel_params(),
    )(is_end, *in_vmem(*stage3, *stage2, ends, far, outer, crossed))


def near_groups(is_end, stage, pair, down, up, outer, crossed, inner2, dx3, swapped, capacity, first1):
    plane = len(stage)
    _, rank, width = pair.shape
    block = plane * capacity
    tile = min(width, 2048)
    tiles = width // tile

    def body(end_ref, *refs):
        stage_in, refs = refs[:plane], refs[plane:]
        pair_in, down_in, up_in, outer_in, crossed_in, inner2, dx3, swapped = refs[:8]
        dx_refs, sum_refs = [refs[8], refs[9], refs[10].at[0], refs[10].at[1]], refs[11:15]
        hidden1, inner1, hidden0, inner0 = refs[15:]
        step = pl.program_id(0)
        own_in = (down_in, up_in)

        def rows(kind, k, cut):
            return jnp.concatenate(
                [r[0, k, pl.ds(first + (1 - kind) * capacity, capacity), cut] for r, first in zip(stage_in, first1)],
                axis=0,
            )

        @pl.when(step == 0)
        def _():
            sums = [jnp.zeros((block, rank), F32)] * 4
            for i in range(tiles):
                cut = pl.ds(i * tile, tile)
                for k in range(2):
                    sums[k] += dot32(rows(1, k, cut), pair_in[k, :, cut], ROWS_OF)
                    sums[2 + k] += dot32(rows(0, k, cut), own_in[k][:, cut], ROWS_OF)
            for ref, value in zip((hidden1, inner1, hidden0, inner0), sums):
                ref[...] = value.astype(BF16)

        cut = pl.ds(pl.multiple_of(step * tile, tile), tile)
        sum_refs[0][...] = dot32(hidden1[...], rows(1, 1, cut), OUTER)
        sum_refs[1][...] = dot32(inner1[...], rows(1, 0, cut), OUTER)
        sum_refs[2][...] = dot32(hidden0[...], rows(0, 1, cut), OUTER)
        sum_refs[3][...] = dot32(inner0[...], rows(0, 0, cut), OUTER)
        near = jnp.where(end_ref[0] == 1, outer_in[0, :, cut], crossed_in[0, :, cut])
        moved = [
            jnp.where(end_ref[0] == 1, swapped[...], dx3[...]),
            dot32(inner2[...], near).astype(BF16),
            dot32(inner1[...], pair_in[0, :, cut]).astype(BF16),
            dot32(inner0[...], down_in[:, cut]).astype(BF16),
        ]
        for n, dx in enumerate(moved):
            for m in range(plane):
                dx_refs[m][n * capacity:(n + 1) * capacity] = dx[m * capacity:(m + 1) * capacity]

    return pl.pallas_call(
        body,
        grid=(tiles,),
        in_specs=[pl.BlockSpec(memory_space=pltpu.SMEM)]
        + [WHOLE] * (plane + 5)
        + [pl.BlockSpec(inner2.shape, lambda i: (0, 0))]
        + [pl.BlockSpec((block, tile), lambda i: (0, i))] * 2,
        out_specs=[pl.BlockSpec((4 * capacity, tile), lambda i: (0, i))] * 2
        + [pl.BlockSpec((2, 4 * capacity, tile), lambda i: (0, 0, i))]
        + [pl.BlockSpec((rank, tile), lambda i: (0, i))] * 4,
        out_shape=[jax.ShapeDtypeStruct((4 * capacity, width), BF16)] * 2
        + [jax.ShapeDtypeStruct((2, 4 * capacity, width), BF16)]
        + [jax.ShapeDtypeStruct((rank, width), F32)] * 4,
        scratch_shapes=[pltpu.VMEM((block, rank), BF16)] * 4,
        compiler_params=kernel_params(),
    )(is_end, *in_vmem(*stage, pair, down, up, outer, crossed), inner2, dx3, swapped)


def move_adapters(plane, acts, cotan, token_task_index, task_slot_lookup, pool_down_factors, pool_up_factors):
    ndevices = lax.axis_size("dp")
    tokens, width = acts.shape
    capacity = 2 * ((tokens + ndevices - 1) // ndevices)
    me = lax.axis_index("dp")
    z, column = me // plane, me % plane
    is_end = (z == 0) | (z == 3)
    end_flag = is_end.astype(jnp.int32).reshape(1)

    def planes(pairs):
        return [(a * plane + c, b * plane + c) for a, b in pairs for c in range(plane)]

    swap = planes([(0, 1), (1, 0), (2, 3), (3, 2)])
    cross = planes([(1, 2), (2, 1)])
    outward = planes([(1, 0), (2, 3)])
    inward = planes([(0, 1), (3, 2)])

    def send(array, pairs):
        return lax.ppermute(array, "dp", pairs)

    def after(arrays, *others):
        return lax.optimization_barrier((arrays, others))[0]

    def beside(m):
        return [(i, (i // plane) * plane + ((i % plane) ^ m)) for i in range(ndevices)]

    def add_up(term):
        around = [beside(m) for m in range(1, plane)]
        along = [[(i, (i // plane ^ m) * plane + i % plane) for i in range(ndevices)] for m in range(1, 4)]
        term = jnp.broadcast_to(term, (8, 128))
        term = term + sum(send(term, pairs) for pairs in around)
        term = after(term, dx_across)
        return (term + sum(after([send(term, pairs) for pairs in along], grad_acts)))[0, 0]

    down, up = pool_down_factors[0], pool_up_factors[0]
    own = jnp.concatenate([pool_down_factors, pool_up_factors])
    pair = send(own, swap)
    crossed = send(own, cross)

    owner, position = route(token_task_index, task_slot_lookup, ndevices)
    owner_z, turn = owner // plane, (owner % plane) ^ column
    other_mid = jnp.where(z < 2, 2, 1)
    kind = jnp.where(owner_z == z, 0, jnp.where(owner_z == (z ^ 1), 1, jnp.where(owner_z == other_mid, 2, 3)))

    def places(wanted, row, rows):
        hot = jnp.arange(rows, dtype=jnp.int32)[:, None] == row[None, :]
        return (hot & wanted[None, :]).astype(BF16)

    def after(arrays, *others):
        return lax.optimization_barrier((arrays, others))[0]

    block = plane * capacity
    mine = (3 - kind) * capacity + position
    row = jnp.where(kind == 2, 10 * capacity, 12 * capacity) + (turn - 2) * jnp.where(kind == 2, capacity, 2 * capacity)
    row += jnp.where(kind == 2, 0, (1 - kind) * capacity) + position
    row = jnp.where(kind == 3, (6 + turn) * capacity + position, row)
    row = jnp.where(turn < 2, turn * block + mine, row)
    place = places(kind >= 0, row, 4 * block)
    place_back = places(kind >= 0, turn * block + mine, 4 * block)
    own_rows, beside_rows, across3, across2, across10 = pack(
        place, acts, cotan, [(1, 4 * capacity)] * 2 + [(2, capacity)] * 2 + [(2, 2 * capacity)]
    )

    def over_x(blocks):
        moved = send(blocks, beside(2))
        return moved, send(moved[1:], beside(1))

    beside_rows = send(beside_rows, beside(1))
    across3 = over_x(across3)
    stage3 = (own_rows, beside_rows) + across3
    ends = jnp.concatenate([r[0, :, :capacity] for r in stage3], axis=1)
    ends = send(ends, inward)
    across2 = over_x(after(across2, across3[0]))
    across10 = over_x(after(across10, across2[0]))
    stage2 = (own_rows, beside_rows) + across2
    stage10 = (own_rows, beside_rows) + across10
    outer = send(crossed, outward)
    far = send(pair, cross)

    up3, down3, up2, down2, swapped, inner2, dx3 = far_groups(
        end_flag, stage3, stage2, ends, far, outer, crossed, capacity, (capacity, capacity, 0, 0)
    )
    down3, swapped = send(down3, cross), send(swapped, swap)
    up3, up2_in = send(up3, cross), send(up2, inward)

    swapped, down3 = lax.optimization_barrier((swapped, down3))
    dx_own, dx_beside, dx_across, up1, down1, up0, down0 = near_groups(
        end_flag, stage10, pair, down, up, outer, crossed, inner2, dx3, swapped, capacity,
        (2 * capacity, 2 * capacity, 0, 0),
    )

    def add(a, b):
        return (a.astype(F32) + b.astype(F32)).astype(BF16)

    up2_in, up3 = after((up2_in, up3), dx_own)
    down2, down1 = send(add(down2, swapped), cross), send(add(down1, down3), swap)
    up2, up1 = send(add(up2, up2_in), cross), send(add(up1, up3), swap)

    dx_across = send(dx_across, beside(2))
    back = [dx_own, send(dx_beside, beside(1)), dx_across, send(dx_across[1], beside(1))]
    grad_acts = unpack(place_back.T, back, tokens)
    raw_up = up0 + up2.astype(F32) + up1.astype(F32)
    raw_down = down0 + down2.astype(F32) + down1.astype(F32)
    return (grad_acts,) + clipped(raw_down, raw_up, ndevices, add_up)


def solution(mesh):
    plane = 4
    by_planes = mesh.shape["dp"] == 4 * plane

    def per_device(*arrays):
        if by_planes:
            return move_adapters(plane, *arrays)
        return move_tokens(*arrays)

    rows, pools = P(("parts", "dp"), None), P(("parts", "dp"), None, None)
    return jax.shard_map(
        per_device,
        mesh=mesh,
        in_specs=(rows, rows, rows, P("parts"), pools, pools),
        out_specs=(rows, pools, pools),
        check_vma=False,
    )
```

time: 277 us -> 244 us (0.88)
  starting transfers between devices: 64.2 us -> 48.6 us
  waiting for transfers between devices: 149 us -> 138 us
  other arithmetic: 12.3 us -> 9.49 us
  Pallas kernels: 31.5 us -> 28.7 us
    all_to_all x1 -> x0, starting transfers between devices: 16 us -> none  [clipped(): lax.all_to_all(shares, 'dp', split_axis=0, concat_axis=0, tiled=True)]
    all_to_all x1 -> x0, waiting for transfers between devices: 6.4 us -> none  [clipped(): lax.all_to_all(shares, 'dp', split_axis=0, concat_axis=0, tiled=True)]
    ppermute x23 -> x29, waiting for transfers between devices: 143 us -> 138 us  [send(): return lax.ppermute(array, 'dp', pairs)]
    unnamed x49 -> x51, local copies, waits for them, and re-layouts: 13 us -> 11.1 us
    pallas_call x3 -> x2, Pallas kernels: 16.5 us -> 14.6 us  [the longest x1 8.27 us: far_groups(): pl.pallas_call(body, grid=(tiles,), in_specs=[pl.BlockSpec(memory_space=p...]
    ppermute x23 -> x29, starting transfers between devices: 48.2 us -> 48.6 us  [send(): return lax.ppermute(array, 'dp', pairs)]
  transfers between devices with their start and end apart: 24 -> 29, of which waited for: 11 -> 11; matrix products, arithmetic and copies ran while one was open for 5% -> 4% of each run, Pallas kernels for 7% -> 12%
where the time goes in v5:
time: 244 us
  waiting for transfers between devices  138 us (57%)
  starting transfers between devices  48.6 us (20%)
  Pallas kernels  28.7 us (12%)
  local copies, waits for them, and re-layouts  16 us (7%)
  other arithmetic  9.49 us (4%)
  between operations  2.9 us (1%)
    ppermute x29, waiting for transfers between devices, send(): return lax.ppermute(array, 'dp', pairs)  138 us
    ppermute x29, starting transfers between devices, send(): return lax.ppermute(array, 'dp', pairs)  48.6 us
    unnamed x51, local copies, waits for them, and re-layouts  11.1 us
    pallas_call x1, Pallas kernels, near_groups(): pl.pallas_call(body, grid=(tiles,), in_specs=[pl.BlockSpec(memory_space=p...  8.91 us
    pallas_call x1, Pallas kernels, far_groups(): pl.pallas_call(body, grid=(tiles,), in_specs=[pl.BlockSpec(memory_space=p...  8.27 us
    pallas_call x1, Pallas kernels, pack(): pl.pallas_call(body, grid=(tiles,), in_specs=[pl.BlockSpec(place.shape, l...  6.36 us
    pallas_call x1, Pallas kernels, unpack(): pl.pallas_call(body, grid=(width // tile,), in_specs=[pl.BlockSpec(place....  5.16 us
  transfers between devices with their start and end apart: 29, of which 11 were waited for; matrix products, arithmetic and copies ran while one was open for 4% of the time, Pallas kernels for 12%

profile of v5, /device:TPU:0, one launch (start us, length us, event | category | flops | bytes accessed | tf_op | source)
XLA Modules:
  0.0 243.5 jit_solution(8189300891670490466)
XLA Ops:
  0.7 2.3 constant_dynamic-update-slice_fusion.1
  4.0 2.0 collective-permute-start.6
  6.0 4.6 %collective-permute-start.5 = (bf16[2,64,8192]{2,1,0:T(8,128)(2,1)}, bf16[2,64,8192]{2,1,0:T(8,128)(2,1)}, u32[]{:S(2)}, u32[]{:S(2)}) collective-permute-start(bf16[2,64,8192]{2,1,0:T(8,128)(2,1)} %constant_dynamic-update-slice_fusion), channel_id=1, source_target_pairs={{0,4},{1,5},{2,6},{3,7},{4,0},{5,1},{6,2},{7,3},{8,12},{9,13},{10,... | collective-permute-start | bytes 6291464 | tf_op jit(solution)/shard_map/ppermute | solution.py:284
  11.3 6.4 %shard_map.85 = (bf16[1,2,64,8192]{3,2,1,0:T(8,128)(2,1)S(1)}, bf16[1,2,64,8192]{3,2,1,0:T(8,128)(2,1)S(1)}, bf16[2,2,16,8192]{3,2,1,0:T(8,128)(2,1)S(1)}, bf16[...) custom-call(bf16[256,128]{1,0:T(8,128)(2,1)S(1)} %fusion.1.place_ref, bf16[128,8192]{1,0:T(8,128)(2,1)} %x_in.1, ...), custom_call_target="tpu_custom_call" | custom-call | tf_op jit(solution)/shard_map/pallas_call | solution.py:107
  19.3 22.8 %collective-permute-done.1.refs_2_ = bf16[2,2,16,8192]{3,2,1,0:T(8,128)(2,1)S(1)} collective-permute-done((bf16[2,2,16,8192]{3,2,1,0:T(8,128)(2,1)S(1)}, bf16[2,2,16,8192]{3,2,1,0:T(8,128)(2,1)S(1)}, u32[]{:S(2)}, u32[]{:S(2)}) %collective-permute-start.1) | collective-permute-done | bytes 1048608 | tf_op jit(solution)/shard_map/ppermute | solution.py:284
  46.7 3.6 %collective-permute-start.10 = (bf16[2,64,8192]{2,1,0:T(8,128)(2,1)}, bf16[2,64,8192]{2,1,0:T(8,128)(2,1)}, u32[]{:S(2)}, u32[]{:S(2)}) collective-permute-start(bf16[2,64,8192]{2,1,0:T(8,128)(2,1)} %pad_maximum_fusion), channel_id=1, source_target_pairs={{0,4},{1,5},{2,6},{3,7},{12,8},{13,9},{14,10},{15,11},{16,20},{17,... | collective-permute-start | bytes 6291464 | tf_op jit(solution)/shard_map/ppermute | solution.py:284
  51.5 5.5 %collective-permute-done.5.refs_4_ = bf16[2,64,8192]{2,1,0:T(8,128)(2,1)} collective-permute-done((bf16[2,64,8192]{2,1,0:T(8,128)(2,1)}, bf16[2,64,8192]{2,1,0:T(8,128)(2,1)}, u32[]{:S(2)}, u32[]{:S(2)}) %collective-permute-start.5) | collective-permute-done | bytes 2097184 | tf_op jit(solution)/shard_map/ppermute | solution.py:284
  57.0 2.0 collective-permute-start.11
  59.1 8.8 %collective-permute-done.2.refs_6_ = bf16[2,2,16,8192]{3,2,1,0:T(8,128)(2,1)S(1)} collective-permute-done((bf16[2,2,16,8192]{3,2,1,0:T(8,128)(2,1)S(1)}, bf16[2,2,16,8192]{3,2,1,0:T(8,128)(2,1)S(1)}, u32[]{:S(2)}, u32[]{:S(2)}) %collective-permute-start.2) | collective-permute-done | bytes 1048608 | tf_op jit(solution)/shard_map/ppermute | solution.py:284
  71.1 2.2 collective-permute-done.9.refs_7_
  73.4 27.1 %collective-permute-done.10.refs_8_ = bf16[2,64,8192]{2,1,0:T(8,128)(2,1)} collective-permute-done((bf16[2,64,8192]{2,1,0:T(8,128)(2,1)}, bf16[2,64,8192]{2,1,0:T(8,128)(2,1)}, u32[]{:S(2)}, u32[]{:S(2)}) %collective-permute-start.10) | collective-permute-done | bytes 2097184 | tf_op jit(solution)/shard_map/ppermute | solution.py:284
  100.5 2.5 %collective-permute-done.7.refs_10_.refs_7_ = bf16[2,64,8192]{2,1,0:T(8,128)(2,1)} collective-permute-done((bf16[2,64,8192]{2,1,0:T(8,128)(2,1)}, bf16[2,64,8192]{2,1,0:T(8,128)(2,1)}, u32[]{:S(2)}, u32[]{:S(2)}) %collective-permute-start.7) | collective-permute-done | bytes 2097184 | tf_op jit(solution)/shard_map/ppermute | solution.py:284
  108.1 8.3 %shard_map.86 = (bf16[64,8192]{1,0:T(8,128)(2,1)S(1)}, bf16[64,8192]{1,0:T(8,128)(2,1)S(1)}, bf16[64,8192]{1,0:T(8,128)(2,1)S(1)}, bf16[64,8192]{1,0:T(8,128)(2,...) custom-call(s32[1]{0:T(128)} %bitcast.1.end_ref, ...), custom_call_target="tpu_custom_call" | custom-call | tf_op jit(solution)/shard_map/pallas_call | solution.py:189
  116.4 5.1 %collective-permute-start.12 = (bf16[64,8192]{1,0:T(8,128)(2,1)S(1)}, bf16[64,8192]{1,0:T(8,128)(2,1)S(1)}, u32[]{:S(2)}, u32[]{:S(2)}) collective-permute-start(bf16[64,8192]{1,0:T(8,128)(2,1)S(1)} %get-tuple-element.41), channel_id=1, source_target_pairs={{0,4},{1,5},{2,6},{3,7},{4,0},{5,1},{6,2},{7,3},{8,12},{9,13},{10,... | collective-permute-start | bytes 3145736 | tf_op jit(solution)/shard_map/ppermute | solution.py:284
  123.6 4.9 %collective-permute-start.19 = (bf16[64,8192]{1,0:T(8,128)(2,1)S(1)}, bf16[64,8192]{1,0:T(8,128)(2,1)S(1)}, u32[]{:S(2)}, u32[]{:S(2)}) collective-permute-start(bf16[64,8192]{1,0:T(8,128)(2,1)S(1)} %get-tuple-element.52), channel_id=1, source_target_pairs={{0,4},{1,5},{2,6},{3,7},{12,8},{13,9},{14,10},{15,11},{16,20},{17,... | collective-permute-start | bytes 3145736 | tf_op jit(solution)/shard_map/ppermute | solution.py:284
  129.2 15.9 %collective-permute-done.12.refs_11_ = bf16[64,8192]{1,0:T(8,128)(2,1)S(1)} collective-permute-done((bf16[64,8192]{1,0:T(8,128)(2,1)S(1)}, bf16[64,8192]{1,0:T(8,128)(2,1)S(1)}, u32[]{:S(2)}, u32[]{:S(2)}) %collective-permute-start.12) | collective-permute-done | bytes 1048608 | tf_op jit(solution)/shard_map/ppermute | solution.py:284
  145.1 8.9 %shard_map.87 = (bf16[64,8192]{1,0:T(8,128)(2,1)S(1)}, bf16[64,8192]{1,0:T(8,128)(2,1)}, bf16[2,64,8192]{2,1,0:T(8,128)(2,1)S(1)}, f32[64,8192]{1,0:T(8,128)S(1)...) custom-call(s32[1]{0:T(128)} %bitcast.1.end_ref, ...), custom_call_target="tpu_custom_call" | custom-call | tf_op jit(solution)/shard_map/pallas_call | solution.py:248
  154.0 10.4 %collective-permute-done.19 = bf16[64,8192]{1,0:T(8,128)(2,1)S(1)} collective-permute-done((bf16[64,8192]{1,0:T(8,128)(2,1)S(1)}, bf16[64,8192]{1,0:T(8,128)(2,1)S(1)}, u32[]{:S(2)}, u32[]{:S(2)}) %collective-permute-start.19) | collective-permute-done | bytes 1048608 | tf_op jit(solution)/shard_map/ppermute | solution.py:284
  165.6 7.5 %collective-permute-start.22 = (bf16[64,8192]{1,0:T(8,128)(2,1)S(1)}, bf16[64,8192]{1,0:T(8,128)(2,1)S(1)}, u32[]{:S(2)}, u32[]{:S(2)}) collective-permute-start(bf16[64,8192]{1,0:T(8,128)(2,1)S(1)} %add_convert_fusion), channel_id=1, source_target_pairs={{0,4},{1,5},{2,6},{3,7},{4,0},{5,1},{6,2},{7,3},{8,12},{9,13},{10,... | collective-permute-start | bytes 3145736 | tf_op jit(solution)/shard_map/ppermute | solution.py:284
  177.5 39.8 %collective-permute-done.15.refs_2_ = bf16[2,64,8192]{2,1,0:T(8,128)(2,1)S(1)} collective-permute-done((bf16[2,64,8192]{2,1,0:T(8,128)(2,1)S(1)}, bf16[2,64,8192]{2,1,0:T(8,128)(2,1)S(1)}, u32[]{:S(2)}, u32[]{:S(2)}) %collective-permute-start.15) | collective-permute-done | bytes 2097184 | tf_op jit(solution)/shard_map/ppermute | solution.py:284
  225.6 2.0 collective-permute-done.24
  230.2 2.6 %collective-permute-start.28 = (f32[8,128]{1,0:T(8,128)S(1)}, f32[8,128]{1,0:T(8,128)S(1)}, u32[]{:S(2)}, u32[]{:S(2)}) collective-permute-start(f32[8,128]{1,0:T(8,128)S(1)} %add_add_fusion.1), channel_id=1, source_target_pairs={{0,12},{1,13},{2,14},{3,15},{4,8},{5,9},{6,10},{7,11},{8,4},{9,5},... | collective-permute-start | bytes 12296 | tf_op jit(solution)/shard_map/ppermute | solution.py:284
  233.1 5.2 %shard_map.88 = bf16[128,8192]{1,0:T(8,128)(2,1)} custom-call(bf16[128,256]{1,0:T(8,128)(2,1)S(1)} %fusion.place_ref, bf16[64,8192]{1,0:T(8,128)(2,1)S(1)} %copy-done.15, bf16[64,8192]{1,0:T(8,128)(2,1)} %collective-permute-done.14.refs_1_, bf16[2,64,8192]{2,1,0:T(8,128)(2,1)S(1)} %collective-permute-done.15.refs_2_, ...), custom_call_target="tpu_custom_call" | custom-call | tf_op jit(solution)/shard_map/pallas_call | solution.py:126
  239.5 4.0 %multiply_bitcast_fusion = (f32[1,64,8192]{2,1,0:T(8,128)}, f32[1,64,8192]{2,1,0:T(8,128)}) fusion(f32[]{:T(128)} %bitcast.9, bf16[64,8192]{1,0:T(8,128)(2,1)S(1)} %copy-done.19, f32[64,8192]{1,0:T(8,128)S(1)} %copy-done.3, bf16[64,8192]{1,0:T(8,128)(2,1)S(1)} %copy-done.17, bf16[64,8192]{1,0:T(8,128)(2,1)} %copy-done.22, f32[64,8192]{1,0:T(8,128)S(1)} %copy-done.5, ...), kind=kLoop, calls=%fused_computation.1 | loop fusion | flops 5242880 | bytes 12582916 | tf_op jit(solution)/shard_map/broadcast_in_dim | solution.py:37
  (116 shorter events, 36.4 us)
Async XLA Ops:
  4.0 46.2 %collective-permute-start.6 = (bf16[2,64,8192]{2,1,0:T(8,128)(2,1)}, bf16[2,64,8192]{2,1,0:T(8,128)(2,1)}, u32[]{:S(2)}, u32[]{:S(2)}) collective-permute-start(bf16[2,64,8192]{2,1,0:T(8,128)(2,1)} %constant_dynamic-update-slice_fusion), channel_id=1, source_target_pairs={{4,8},{5,9},{6,10},{7,11},{8,4},{9,5},{10,6},{11,7},{20,24},{21,25... | collective-permute-start | bytes 6291464 | tf_op jit(solution)/shard_map/ppermute | solution.py:284
  6.0 51.0 %collective-permute-start.5 = (bf16[2,64,8192]{2,1,0:T(8,128)(2,1)}, bf16[2,64,8192]{2,1,0:T(8,128)(2,1)}, u32[]{:S(2)}, u32[]{:S(2)}) collective-permute-start(bf16[2,64,8192]{2,1,0:T(8,128)(2,1)} %constant_dynamic-update-slice_fusion), channel_id=1, source_target_pairs={{0,4},{1,5},{2,6},{3,7},{4,0},{5,1},{6,2},{7,3},{8,12},{9,13},{10,... | collective-permute-start | bytes 6291464 | tf_op jit(solution)/shard_map/ppermute | solution.py:284
  17.7 24.4 %collective-permute-start.1 = (bf16[2,2,16,8192]{3,2,1,0:T(8,128)(2,1)S(1)}, bf16[2,2,16,8192]{3,2,1,0:T(8,128)(2,1)S(1)}, u32[]{:S(2)}, u32[]{:S(2)}) collective-permute-start(bf16[2,2,16,8192]{3,2,1,0:T(8,128)(2,1)S(1)} %get-tuple-element.36), channel_id=1, source_target_pairs={{0,2},{1,3},{2,0},{3,1},{4,6},{5,7},{6,4},{7,5},{8,10},{9,11},{10,... | collective-permute-start | bytes 3145736 | tf_op jit(solution)/shard_map/ppermute | solution.py:284
  19.2 24.6 %collective-permute-start = (bf16[1,2,64,8192]{3,2,1,0:T(8,128)(2,1)S(1)}, bf16[1,2,64,8192]{3,2,1,0:T(8,128)(2,1)S(1)}, u32[]{:S(2)}, u32[]{:S(2)}) collective-permute-start(bf16[1,2,64,8192]{3,2,1,0:T(8,128)(2,1)S(1)} %get-tuple-element.33), channel_id=1, source_target_pairs={{0,1},{1,0},{2,3},{3,2},{4,5},{5,4},{6,7},{7,6},{8,9},{9,8},{10,11... | collective-permute-start | bytes 6291464 | tf_op jit(solution)/shard_map/ppermute | solution.py:284
  42.2 25.6 %collective-permute-start.2 = (bf16[2,2,16,8192]{3,2,1,0:T(8,128)(2,1)S(1)}, bf16[2,2,16,8192]{3,2,1,0:T(8,128)(2,1)S(1)}, u32[]{:S(2)}, u32[]{:S(2)}) collective-permute-start(bf16[2,2,16,8192]{3,2,1,0:T(8,128)(2,1)S(1)} %get-tuple-element.37), channel_id=1, source_target_pairs={{0,2},{1,3},{2,0},{3,1},{4,6},{5,7},{6,4},{7,5},{8,10},{9,11},{10,... | collective-permute-start | bytes 3145736 | tf_op jit(solution)/shard_map/ppermute | solution.py:284
  46.7 53.8 %collective-permute-start.10 = (bf16[2,64,8192]{2,1,0:T(8,128)(2,1)}, bf16[2,64,8192]{2,1,0:T(8,128)(2,1)}, u32[]{:S(2)}, u32[]{:S(2)}) collective-permute-start(bf16[2,64,8192]{2,1,0:T(8,128)(2,1)} %pad_maximum_fusion), channel_id=1, source_target_pairs={{0,4},{1,5},{2,6},{3,7},{12,8},{13,9},{14,10},{15,11},{16,20},{17,... | collective-permute-start | bytes 6291464 | tf_op jit(solution)/shard_map/ppermute | solution.py:284
  50.2 52.7 %collective-permute-start.7 = (bf16[2,64,8192]{2,1,0:T(8,128)(2,1)}, bf16[2,64,8192]{2,1,0:T(8,128)(2,1)}, u32[]{:S(2)}, u32[]{:S(2)}) collective-permute-start(bf16[2,64,8192]{2,1,0:T(8,128)(2,1)} %collective-permute-done.6.refs_11_.refs_8_), channel_id=1, source_target_pairs={{4,0},{5,1},{6,2},{7,3},{8,12},{9,13},{10,14},{11,15},{20,16},{21,... | collective-permute-start | bytes 6291464 | tf_op jit(solution)/shard_map/ppermute | solution.py:284
  57.0 46.0 %collective-permute-start.11 = (bf16[2,64,8192]{2,1,0:T(8,128)(2,1)}, bf16[2,64,8192]{2,1,0:T(8,128)(2,1)}, u32[]{:S(2)}, u32[]{:S(2)}) collective-permute-start(bf16[2,64,8192]{2,1,0:T(8,128)(2,1)} %collective-permute-done.5.refs_4_), channel_id=1, source_target_pairs={{4,8},{5,9},{6,10},{7,11},{8,4},{9,5},{10,6},{11,7},{20,24},{21,25... | collective-permute-start | bytes 6291464 | tf_op jit(solution)/shard_map/ppermute | solution.py:284
  67.8 54.4 %collective-permute-start.3 = (bf16[2,2,32,8192]{3,2,1,0:T(8,128)(2,1)}, bf16[2,2,32,8192]{3,2,1,0:T(8,128)(2,1)}, u32[]{:S(2)}, u32[]{:S(2)}) collective-permute-start(bf16[2,2,32,8192]{3,2,1,0:T(8,128)(2,1)} %get-tuple-element.38), channel_id=1, source_target_pairs={{0,2},{1,3},{2,0},{3,1},{4,6},{5,7},{6,4},{7,5},{8,10},{9,11},{10,... | collective-permute-start | bytes 6291464 | tf_op jit(solution)/shard_map/ppermute | solution.py:284
  116.4 28.7 %collective-permute-start.12 = (bf16[64,8192]{1,0:T(8,128)(2,1)S(1)}, bf16[64,8192]{1,0:T(8,128)(2,1)S(1)}, u32[]{:S(2)}, u32[]{:S(2)}) collective-permute-start(bf16[64,8192]{1,0:T(8,128)(2,1)S(1)} %get-tuple-element.41), channel_id=1, source_target_pairs={{0,4},{1,5},{2,6},{3,7},{4,0},{5,1},{6,2},{7,3},{8,12},{9,13},{10,... | collective-permute-start | bytes 3145736 | tf_op jit(solution)/shard_map/ppermute | solution.py:284
  121.4 23.6 %collective-permute-start.13 = (bf16[64,8192]{1,0:T(8,128)(2,1)S(1)}, bf16[64,8192]{1,0:T(8,128)(2,1)S(1)}, u32[]{:S(2)}, u32[]{:S(2)}) collective-permute-start(bf16[64,8192]{1,0:T(8,128)(2,1)S(1)} %get-tuple-element.42), channel_id=1, source_target_pairs={{4,8},{5,9},{6,10},{7,11},{8,4},{9,5},{10,6},{11,7},{20,24},{21,25... | collective-permute-start | bytes 3145736 | tf_op jit(solution)/shard_map/ppermute | solution.py:284
  123.5 21.6 %collective-permute-start.4 = (bf16[1,2,32,8192]{3,2,1,0:T(8,128)(2,1)S(1)}, bf16[1,2,32,8192]{3,2,1,0:T(8,128)(2,1)S(1)}, u32[]{:S(2)}, u32[]{:S(2)}) collective-permute-start(bf16[1,2,32,8192]{3,2,1,0:T(8,128)(2,1)S(1)} %slice.32), channel_id=1, source_target_pairs={{0,1},{1,0},{2,3},{3,2},{4,5},{5,4},{6,7},{7,6},{8,9},{9,8},{10,11... | collective-permute-start | bytes 3145736 | tf_op jit(solution)/shard_map/ppermute | solution.py:284
  123.6 40.8 %collective-permute-start.19 = (bf16[64,8192]{1,0:T(8,128)(2,1)S(1)}, bf16[64,8192]{1,0:T(8,128)(2,1)S(1)}, u32[]{:S(2)}, u32[]{:S(2)}) collective-permute-start(bf16[64,8192]{1,0:T(8,128)(2,1)S(1)} %get-tuple-element.52), channel_id=1, source_target_pairs={{0,4},{1,5},{2,6},{3,7},{12,8},{13,9},{14,10},{15,11},{16,20},{17,... | collective-permute-start | bytes 3145736 | tf_op jit(solution)/shard_map/ppermute | solution.py:284
  128.5 35.9 %collective-permute-start.20 = (bf16[64,8192]{1,0:T(8,128)(2,1)S(1)}, bf16[64,8192]{1,0:T(8,128)(2,1)S(1)}, u32[]{:S(2)}, u32[]{:S(2)}) collective-permute-start(bf16[64,8192]{1,0:T(8,128)(2,1)S(1)} %get-tuple-element.53), channel_id=1, source_target_pairs={{4,8},{5,9},{6,10},{7,11},{8,4},{9,5},{10,6},{11,7},{20,24},{21,25... | collective-permute-start | bytes 3145736 | tf_op jit(solution)/shard_map/ppermute | solution.py:284
  164.6 53.7 %collective-permute-start.21 = (bf16[64,8192]{1,0:T(8,128)(2,1)S(1)}, bf16[64,8192]{1,0:T(8,128)(2,1)S(1)}, u32[]{:S(2)}, u32[]{:S(2)}) collective-permute-start(bf16[64,8192]{1,0:T(8,128)(2,1)S(1)} %add_convert_fusion.1), channel_id=1, source_target_pairs={{4,8},{5,9},{6,10},{7,11},{8,4},{9,5},{10,6},{11,7},{20,24},{21,25... | collective-permute-start | bytes 3145736 | tf_op jit(solution)/shard_map/ppermute | solution.py:284
  165.6 53.3 %collective-permute-start.22 = (bf16[64,8192]{1,0:T(8,128)(2,1)S(1)}, bf16[64,8192]{1,0:T(8,128)(2,1)S(1)}, u32[]{:S(2)}, u32[]{:S(2)}) collective-permute-start(bf16[64,8192]{1,0:T(8,128)(2,1)S(1)} %add_convert_fusion), channel_id=1, source_target_pairs={{0,4},{1,5},{2,6},{3,7},{4,0},{5,1},{6,2},{7,3},{8,12},{9,13},{10,... | collective-permute-start | bytes 3145736 | tf_op jit(solution)/shard_map/ppermute | solution.py:284
  173.1 44.1 %collective-permute-start.15 = (bf16[2,64,8192]{2,1,0:T(8,128)(2,1)S(1)}, bf16[2,64,8192]{2,1,0:T(8,128)(2,1)S(1)}, u32[]{:S(2)}, u32[]{:S(2)}) collective-permute-start(bf16[2,64,8192]{2,1,0:T(8,128)(2,1)S(1)} %get-tuple-element.46), channel_id=1, source_target_pairs={{0,2},{1,3},{2,0},{3,1},{4,6},{5,7},{6,4},{7,5},{8,10},{9,11},{10,... | collective-permute-start | bytes 6291464 | tf_op jit(solution)/shard_map/ppermute | solution.py:284
  174.9 45.1 %collective-permute-start.17 = (bf16[64,8192]{1,0:T(8,128)(2,1)S(1)}, bf16[64,8192]{1,0:T(8,128)(2,1)S(1)}, u32[]{:S(2)}, u32[]{:S(2)}) collective-permute-start(bf16[64,8192]{1,0:T(8,128)(2,1)S(1)} %add_convert_fusion.3), channel_id=1, source_target_pairs={{4,8},{5,9},{6,10},{7,11},{8,4},{9,5},{10,6},{11,7},{20,24},{21,25... | collective-permute-start | bytes 3145736 | tf_op jit(solution)/shard_map/ppermute | solution.py:284
  175.8 44.2 %collective-permute-start.18 = (bf16[64,8192]{1,0:T(8,128)(2,1)S(1)}, bf16[64,8192]{1,0:T(8,128)(2,1)S(1)}, u32[]{:S(2)}, u32[]{:S(2)}) collective-permute-start(bf16[64,8192]{1,0:T(8,128)(2,1)S(1)} %add_convert_fusion.2), channel_id=1, source_target_pairs={{0,4},{1,5},{2,6},{3,7},{4,0},{5,1},{6,2},{7,3},{8,12},{9,13},{10,... | collective-permute-start | bytes 3145736 | tf_op jit(solution)/shard_map/ppermute | solution.py:284
  217.2 15.8 %collective-permute-start.14 = (bf16[64,8192]{1,0:T(8,128)(2,1)}, bf16[64,8192]{1,0:T(8,128)(2,1)}, u32[]{:S(2)}, u32[]{:S(2)}) collective-permute-start(bf16[64,8192]{1,0:T(8,128)(2,1)} %get-tuple-element.45), channel_id=1, source_target_pairs={{0,1},{1,0},{2,3},{3,2},{4,5},{5,4},{6,7},{7,6},{8,9},{9,8},{10,11... | collective-permute-start | bytes 3145736 | tf_op jit(solution)/shard_map/ppermute | solution.py:284
  218.4 14.7 %collective-permute-start.16 = (bf16[64,8192]{1,0:T(8,128)(2,1)}, bf16[64,8192]{1,0:T(8,128)(2,1)}, u32[]{:S(2)}, u32[]{:S(2)}) collective-permute-start(bf16[64,8192]{1,0:T(8,128)(2,1)} %slice_bitcast_fusion), channel_id=1, source_target_pairs={{0,1},{1,0},{2,3},{3,2},{4,5},{5,4},{6,7},{7,6},{8,9},{9,8},{10,11... | collective-permute-start | bytes 3145736 | tf_op jit(solution)/shard_map/ppermute | solution.py:284
  228.5 9.7 %collective-permute-start.26 = (f32[8,128]{1,0:T(8,128)S(1)}, f32[8,128]{1,0:T(8,128)S(1)}, u32[]{:S(2)}, u32[]{:S(2)}) collective-permute-start(f32[8,128]{1,0:T(8,128)S(1)} %add_add_fusion.1), channel_id=1, source_target_pairs={{0,4},{1,5},{2,6},{3,7},{4,0},{5,1},{6,2},{7,3},{8,12},{9,13},{10,... | collective-permute-start | bytes 12296 | tf_op jit(solution)/shard_map/ppermute | solution.py:284
  228.9 9.4 %collective-permute-start.27 = (f32[8,128]{1,0:T(8,128)S(1)}, f32[8,128]{1,0:T(8,128)S(1)}, u32[]{:S(2)}, u32[]{:S(2)}) collective-permute-start(f32[8,128]{1,0:T(8,128)S(1)} %add_add_fusion.1), channel_id=1, source_target_pairs={{0,8},{1,9},{2,10},{3,11},{4,12},{5,13},{6,14},{7,15},{8,0},{9,1},... | collective-permute-start | bytes 12296 | tf_op jit(solution)/shard_map/ppermute | solution.py:284
  230.2 8.0 %collective-permute-start.28 = (f32[8,128]{1,0:T(8,128)S(1)}, f32[8,128]{1,0:T(8,128)S(1)}, u32[]{:S(2)}, u32[]{:S(2)}) collective-permute-start(f32[8,128]{1,0:T(8,128)S(1)} %add_add_fusion.1), channel_id=1, source_target_pairs={{0,12},{1,13},{2,14},{3,15},{4,8},{5,9},{6,10},{7,11},{8,4},{9,5},... | collective-permute-start | bytes 12296 | tf_op jit(solution)/shard_map/ppermute | solution.py:284
  (30 other events, 267.3 us)

commit v6 on v5

--- a/solution.py
+++ b/solution.py
@@ -139,6 +139,37 @@
     )(place, *blocks)
 
 
+def corner(rows, first_rows, columns, first_columns):
+    upper = lax.broadcasted_iota(jnp.int32, (rows, columns), 0) < first_rows
+    return upper == (lax.broadcasted_iota(jnp.int32, (rows, columns), 1) < first_columns)
+
+
+def stack(down, up):
+    _, rank, width = down.shape
+    pieces = 4
+    part = rank // pieces
+
+    def body(*refs):
+        out, sems = refs[2:]
+        copies = [
+            pltpu.make_async_copy(refs[k].at[0, pl.ds(n * part, part)], out.at[k, pl.ds(n * part, part)], sems.at[k, n])
+            for k in range(2)
+            for n in range(pieces)
+        ]
+        for c in copies:
+            c.start()
+        for c in copies:
+            c.wait()
+
+    return pl.pallas_call(
+        body,
+        in_specs=[HBM, HBM],
+        out_specs=pl.BlockSpec(memory_space=pl.ANY),
+        out_shape=jax.ShapeDtypeStruct((2, rank, width), BF16),
+        scratch_shapes=[pltpu.SemaphoreType.DMA((2, pieces))],
+    )(*in_hbm(down, up))
+
+
 def far_groups(is_end, stage3, stage2, ends, far, outer, crossed, capacity, first2):
     plane = len(stage3)
     _, rank, width = far.shape
@@ -146,40 +177,55 @@
     tile = min(width, 2048)
     tiles = width // tile
 
+    tall = 3 * block
+
     def body(end_ref, *refs):
-        stage3_in, stage2_in, refs = refs[:plane], refs[plane:2 * plane], refs[2 * plane:]
+        stage_in, refs = refs[:2 * plane], refs[2 * plane:]
         ends_in, far_in, outer_in, crossed_in = refs[:4]
         sum3_refs, sum2_refs, swap_ref, inner2_ref, dx_ref = refs[4:6], refs[6:8], *refs[8:11]
-        left3, left2 = refs[11:]
+        held, left, sems = refs[11:]
         step = pl.program_id(0)
-
-        def rows3(k, cut):
-            return jnp.concatenate([r[0, k, :capacity, cut] for r in stage3_in] + [ends_in[k, :, cut]], axis=0)
-
-        def rows2(k, cut):
-            return jnp.concatenate([r[0, k, first:first + capacity, cut] for r, first in zip(stage2_in, first2)], axis=0)
+        is_mine = corner(tall, 2 * block, 2 * rank, rank)
+
+        def copies(i):
+            cut = pl.ds(i * tile, tile)
+            firsts = (0,) * plane + first2
+            return [
+                pltpu.make_async_copy(
+                    r.at[0, :, pl.ds(first, capacity), cut], held.at[:, pl.ds(n * capacity, capacity), cut], sems.at[i, n]
+                )
+                for n, (r, first) in enumerate(zip(stage_in, firsts))
+            ]
+
+        def rows(k, cut):
+            return jnp.concatenate([held[k, :block, cut], ends_in[k, :, cut], held[k, block:, cut]], axis=0)
 
         @pl.when(step == 0)
         def _():
-            sums3, sums2 = [jnp.zeros((2 * block, rank), F32)] * 2, [jnp.zeros((block, rank), F32)] * 2
             for i in range(tiles):
+                for c in copies(i):
+                    c.start()
+            sums = [jnp.zeros((tall, 2 * rank), F32)] * 2
+            for i in range(tiles):
+                for c in copies(i):
+                    c.wait()
                 cut = pl.ds(i * tile, tile)
                 for k in range(2):
                     near = jnp.where(end_ref[0] == 1, outer_in[k, :, cut], crossed_in[k, :, cut])
-                    sums3[k] += dot32(rows3(k, cut), far_in[k, :, cut], ROWS_OF)
-                    sums2[k] += dot32(rows2(k, cut), near, ROWS_OF)
+                    both = jnp.concatenate([far_in[k, :, cut], near], axis=0)
+                    sums[k] += dot32(rows(k, cut), both, ROWS_OF)
             for k in range(2):
-                left3[k] = sums3[k].astype(BF16)
-                left2[k] = sums2[k].astype(BF16)
-            inner2_ref[...] = left2[1]
+                left[k] = jnp.where(is_mine, sums[k], 0.0).astype(BF16)
+            inner2_ref[...] = left[1, 2 * block:, rank:]
 
         cut = pl.ds(pl.multiple_of(step * tile, tile), tile)
         for k in range(2):
-            sum3_refs[k][...] = dot32(left3[k], rows3(1 - k, cut), OUTER).astype(BF16)
-            sum2_refs[k][...] = dot32(left2[k], rows2(1 - k, cut), OUTER).astype(BF16)
-        dx = dot32(left3[1], far_in[0, :, cut]).astype(BF16)
+            both = dot32(left[k], rows(1 - k, cut), OUTER).astype(BF16)
+            sum3_refs[k][...] = both[:rank]
+            sum2_refs[k][...] = both[rank:]
+        dx = dot32(left[1, :2 * block, :rank], far_in[0, :, cut]).astype(BF16)
         dx_ref[...] = dx[:block]
-        swap_ref[...] = jnp.where(end_ref[0] == 1, sum2_refs[1][...], dx[block:])
+        swap_ref[...] = jnp.where(end_ref[0] == 1, both[rank:], dx[block:])
 
     def wide(rows):
         return pl.BlockSpec((rows, tile), lambda i: (0, i)), jax.ShapeDtypeStruct((rows, width), BF16)
@@ -189,12 +235,16 @@
     return pl.pallas_call(
         body,
         grid=(tiles,),
-        in_specs=[pl.BlockSpec(memory_space=pltpu.SMEM)] + [WHOLE] * (2 * plane + 4),
+        in_specs=[pl.BlockSpec(memory_space=pltpu.SMEM)] + [HBM] * (2 * plane) + [WHOLE] * 4,
         out_specs=[o[0] for o in outs],
         out_shape=[o[1] for o in outs],
-        scratch_shapes=[pltpu.VMEM((2, 2 * block, rank), BF16), pltpu.VMEM((2, block, rank), BF16)],
+        scratch_shapes=[
+            pltpu.VMEM((2, 2 * block, width), BF16),
+            pltpu.VMEM((2, tall, 2 * rank), BF16),
+            pltpu.SemaphoreType.DMA((tiles, 2 * plane)),
+        ],
         compiler_params=kernel_params(),
-    )(is_end, *in_vmem(*stage3, *stage2, ends, far, outer, crossed))
+    )(is_end, *in_hbm(*stage3, *stage2), *in_vmem(ends, far, outer, crossed))
 
 
 def near_groups(is_end, stage, pair, down, up, outer, crossed, inner2, dx3, swapped, capacity, first1):
@@ -208,39 +258,43 @@
         stage_in, refs = refs[:plane], refs[plane:]
         pair_in, down_in, up_in, outer_in, crossed_in, inner2, dx3, swapped = refs[:8]
         dx_refs, sum_refs = [refs[8], refs[9], refs[10].at[0], refs[10].at[1]], refs[11:15]
-        hidden1, inner1, hidden0, inner0 = refs[15:]
+        left, inners = refs[15:]
         step = pl.program_id(0)
         own_in = (down_in, up_in)
-
-        def rows(kind, k, cut):
+        is_mine = corner(2 * block, block, 2 * rank, rank)
+
+        def rows(k, cut):
             return jnp.concatenate(
-                [r[0, k, pl.ds(first + (1 - kind) * capacity, capacity), cut] for r, first in zip(stage_in, first1)],
+                [
+                    r[0, k, pl.ds(first + n * capacity, capacity), cut]
+                    for n in range(2)
+                    for r, first in zip(stage_in, first1)
+                ],
                 axis=0,
             )
 
         @pl.when(step == 0)
         def _():
-            sums = [jnp.zeros((block, rank), F32)] * 4
+            sums = [jnp.zeros((2 * block, 2 * rank), F32)] * 2
             for i in range(tiles):
                 cut = pl.ds(i * tile, tile)
                 for k in range(2):
-                    sums[k] += dot32(rows(1, k, cut), pair_in[k, :, cut], ROWS_OF)
-                    sums[2 + k] += dot32(rows(0, k, cut), own_in[k][:, cut], ROWS_OF)
-            for ref, value in zip((hidden1, inner1, hidden0, inner0), sums):
-                ref[...] = value.astype(BF16)
+                    both = jnp.concatenate([pair_in[k, :, cut], own_in[k][:, cut]], axis=0)
+                    sums[k] += dot32(rows(k, cut), both, ROWS_OF)
+            for k in range(2):
+                left[k] = jnp.where(is_mine, sums[k], 0.0).astype(BF16)
+            first = jnp.concatenate([inner2[...], jnp.zeros((block, 2 * rank), BF16)], axis=1)
+            inners[...] = jnp.concatenate([first, jnp.concatenate([jnp.zeros((2 * block, rank), BF16), left[1]], axis=1)])
 
         cut = pl.ds(pl.multiple_of(step * tile, tile), tile)
-        sum_refs[0][...] = dot32(hidden1[...], rows(1, 1, cut), OUTER)
-        sum_refs[1][...] = dot32(inner1[...], rows(1, 0, cut), OUTER)
-        sum_refs[2][...] = dot32(hidden0[...], rows(0, 1, cut), OUTER)
-        sum_refs[3][...] = dot32(inner0[...], rows(0, 0, cut), OUTER)
+        for k in range(2):
+            both = dot32(left[k], rows(1 - k, cut), OUTER)
+            sum_refs[k][...] = both[:rank]
+            sum_refs[2 + k][...] = both[rank:]
         near = jnp.where(end_ref[0] == 1, outer_in[0, :, cut], crossed_in[0, :, cut])
-        moved = [
-            jnp.where(end_ref[0] == 1, swapped[...], dx3[...]),
-            dot32(inner2[...], near).astype(BF16),
-            dot32(inner1[...], pair_in[0, :, cut]).astype(BF16),
-            dot32(inner0[...], down_in[:, cut]).astype(BF16),
-        ]
+        downs = jnp.concatenate([near, pair_in[0, :, cut], down_in[:, cut]], axis=0)
+        dx = dot32(inners[...], downs).astype(BF16)
+        moved = [jnp.where(end_ref[0] == 1, swapped[...], dx3[...])] + [dx[n * block:(n + 1) * block] for n in range(3)]
         for n, dx in enumerate(moved):
             for m in range(plane):
                 dx_refs[m][n * capacity:(n + 1) * capacity] = dx[m * capacity:(m + 1) * capacity]
@@ -258,7 +312,7 @@
         out_shape=[jax.ShapeDtypeStruct((4 * capacity, width), BF16)] * 2
         + [jax.ShapeDtypeStruct((2, 4 * capacity, width), BF16)]
         + [jax.ShapeDtypeStruct((rank, width), F32)] * 4,
-        scratch_shapes=[pltpu.VMEM((block, rank), BF16)] * 4,
+        scratch_shapes=[pltpu.VMEM((2, 2 * block, 2 * rank), BF16), pltpu.VMEM((3 * block, 3 * rank), BF16)],
         compiler_params=kernel_params(),
     )(is_end, *in_vmem(*stage, pair, down, up, outer, crossed), inner2, dx3, swapped)
 
@@ -298,11 +352,10 @@
         return (term + sum(after([send(term, pairs) for pairs in along], grad_acts)))[0, 0]
 
     down, up = pool_down_factors[0], pool_up_factors[0]
-    own = jnp.concatenate([pool_down_factors, pool_up_factors])
+    own = stack(pool_down_factors, pool_up_factors)
     pair = send(own, swap)
-    crossed = send(own, cross)
-
-    owner, position = route(token_task_index, task_slot_lookup, ndevices)
+
+    owner, position = route(after(token_task_index, own), task_slot_lookup, ndevices)
     owner_z, turn = owner // plane, (owner % plane) ^ column
     other_mid = jnp.where(z < 2, 2, 1)
     kind = jnp.where(owner_z == z, 0, jnp.where(owner_z == (z ^ 1), 1, jnp.where(owner_z == other_mid, 2, 3)))
@@ -322,6 +375,7 @@
     row = jnp.where(turn < 2, turn * block + mine, row)
     place = places(kind >= 0, row, 4 * block)
     place_back = places(kind >= 0, turn * block + mine, 4 * block)
+    crossed = send(own, cross)
     own_rows, beside_rows, across3, across2, across10 = pack(
         place, acts, cotan, [(1, 4 * capacity)] * 2 + [(2, capacity)] * 2 + [(2, 2 * capacity)]
     )
@@ -357,8 +411,9 @@
     def add(a, b):
         return (a.astype(F32) + b.astype(F32)).astype(BF16)
 
-    up2_in, up3 = after((up2_in, up3), dx_own)
-    down2, down1 = send(add(down2, swapped), cross), send(add(down1, down3), swap)
+    down2, down1 = add(down2, swapped), add(down1, down3)
+    up2_in, up3 = after((up2_in, up3), down2, down1)
+    down2, down1 = send(down2, cross), send(down1, swap)
     up2, up1 = send(add(up2, up2_in), cross), send(add(up1, up3), swap)
 
     dx_across = send(dx_across, beside(2))

time: 244 us -> 295 us (1.21)
  Pallas kernels: 28.7 us -> 95 us
  waiting for transfers between devices: 138 us -> 122 us
  starting transfers between devices: 48.6 us -> 56.5 us
  local copies, waits for them, and re-layouts: 16 us -> 8.8 us
    pallas_call x0 -> x1, Pallas kernels: none -> 64.7 us  [stack(): pl.pallas_call(body, in_specs=[HBM, HBM], out_specs=pl.BlockSpec(memory_s...]
    ppermute x29, waiting for transfers between devices: 138 us -> 122 us  [send(): return lax.ppermute(array, 'dp', pairs)]
    ppermute x29, starting transfers between devices: 48.6 us -> 56.5 us  [send(): return lax.ppermute(array, 'dp', pairs)]
    unnamed x51 -> x52, local copies, waits for them, and re-layouts: 11.1 us -> 5.51 us
  transfers between devices with their start and end apart: 29 -> 29, of which waited for: 11 -> 12; matrix products, arithmetic and copies ran while one was open for 4% -> 3% of each run, Pallas kernels for 12% -> 10%
where the time goes in v6:
time: 295 us; the launch traced here: 294 us
  waiting for transfers between devices  122 us (41%)
  Pallas kernels  95 us (32%)
  starting transfers between devices  56.5 us (19%)
  local copies, waits for them, and re-layouts  8.8 us (3%)
  other arithmetic  8.46 us (3%)
  between operations  3.12 us (1%)
    ppermute x29, waiting for transfers between devices, send(): return lax.ppermute(array, 'dp', pairs)  122 us
    pallas_call x1, Pallas kernels, stack(): pl.pallas_call(body, in_specs=[HBM, HBM], out_specs=pl.BlockSpec(memory_s...  64.7 us
    ppermute x29, starting transfers between devices, send(): return lax.ppermute(array, 'dp', pairs)  56.5 us
    pallas_call x1, Pallas kernels, far_groups(): pl.pallas_call(body, grid=(tiles,), in_specs=[pl.BlockSpec(memory_space=p...  10.5 us
    pallas_call x1, Pallas kernels, near_groups(): pl.pallas_call(body, grid=(tiles,), in_specs=[pl.BlockSpec(memory_space=p...  8.4 us
    pallas_call x1, Pallas kernels, pack(): pl.pallas_call(body, grid=(tiles,), in_specs=[pl.BlockSpec(place.shape, l...  6.36 us
  transfers between devices with their start and end apart: 29, of which 12 were waited for; matrix products, arithmetic and copies ran while one was open for 3% of the time, Pallas kernels for 10%

profile of v6, /device:TPU:0, one launch (start us, length us, event | category | flops | bytes accessed | tf_op | source)
XLA Modules:
  0.0 294.2 jit_solution(747933501462384661)
XLA Ops:
  0.7 64.7 %shard_map.85 = bf16[2,64,8192]{2,1,0:T(8,128)(2,1)} custom-call(bf16[1,64,8192]{2,1,0:T(8,128)(2,1)} %refs_0_.1, bf16[1,64,8192]{2,1,0:T(8,128)(2,1)} %refs_1_.1), custom_call_target="tpu_custom_call" | custom-call | tf_op jit(solution)/shard_map/pallas_call | solution.py:164
  65.4 2.0 collective-permute-start.6
  67.4 4.6 %collective-permute-start.5 = (bf16[2,64,8192]{2,1,0:T(8,128)(2,1)}, bf16[2,64,8192]{2,1,0:T(8,128)(2,1)}, u32[]{:S(2)}, u32[]{:S(2)}) collective-permute-start(bf16[2,64,8192]{2,1,0:T(8,128)(2,1)} %shard_map.85), channel_id=1, source_target_pairs={{0,4},{1,5},{2,6},{3,7},{4,0},{5,1},{6,2},{7,3},{8,12},{9,13},{10,... | collective-permute-start | bytes 6291464 | tf_op jit(solution)/shard_map/ppermute | solution.py:338
  72.6 6.4 %shard_map.86 = (bf16[1,2,64,8192]{3,2,1,0:T(8,128)(2,1)S(1)}, bf16[1,2,64,8192]{3,2,1,0:T(8,128)(2,1)S(1)}, bf16[2,2,16,8192]{3,2,1,0:T(8,128)(2,1)S(1)}, bf16[...) custom-call(bf16[256,128]{1,0:T(8,128)(2,1)S(1)} %fusion.1.place_ref, bf16[128,8192]{1,0:T(8,128)(2,1)} %x_in.1, ...), custom_call_target="tpu_custom_call" | custom-call | tf_op jit(solution)/shard_map/pallas_call | solution.py:107
  80.6 22.8 %collective-permute-done.1.refs_2_ = bf16[2,2,16,8192]{3,2,1,0:T(8,128)(2,1)S(1)} collective-permute-done((bf16[2,2,16,8192]{3,2,1,0:T(8,128)(2,1)S(1)}, bf16[2,2,16,8192]{3,2,1,0:T(8,128)(2,1)S(1)}, u32[]{:S(2)}, u32[]{:S(2)}) %collective-permute-start.1) | collective-permute-done | bytes 1048608 | tf_op jit(solution)/shard_map/ppermute | solution.py:338
  108.0 3.6 %collective-permute-start.10 = (bf16[2,64,8192]{2,1,0:T(8,128)(2,1)}, bf16[2,64,8192]{2,1,0:T(8,128)(2,1)}, u32[]{:S(2)}, u32[]{:S(2)}) collective-permute-start(bf16[2,64,8192]{2,1,0:T(8,128)(2,1)} %pad_maximum_fusion), channel_id=1, source_target_pairs={{0,4},{1,5},{2,6},{3,7},{12,8},{13,9},{14,10},{15,11},{16,20},{17,... | collective-permute-start | bytes 6291464 | tf_op jit(solution)/shard_map/ppermute | solution.py:338
  112.9 5.4 %collective-permute-done.5.refs_4_ = bf16[2,64,8192]{2,1,0:T(8,128)(2,1)} collective-permute-done((bf16[2,64,8192]{2,1,0:T(8,128)(2,1)}, bf16[2,64,8192]{2,1,0:T(8,128)(2,1)}, u32[]{:S(2)}, u32[]{:S(2)}) %collective-permute-start.5) | collective-permute-done | bytes 2097184 | tf_op jit(solution)/shard_map/ppermute | solution.py:338
  118.3 2.0 collective-permute-start.11
  120.3 8.8 %collective-permute-done.2.refs_6_ = bf16[2,2,16,8192]{3,2,1,0:T(8,128)(2,1)S(1)} collective-permute-done((bf16[2,2,16,8192]{3,2,1,0:T(8,128)(2,1)S(1)}, bf16[2,2,16,8192]{3,2,1,0:T(8,128)(2,1)S(1)}, u32[]{:S(2)}, u32[]{:S(2)}) %collective-permute-start.2) | collective-permute-done | bytes 1048608 | tf_op jit(solution)/shard_map/ppermute | solution.py:338
  132.7 29.1 %collective-permute-done.10.refs_8_ = bf16[2,64,8192]{2,1,0:T(8,128)(2,1)} collective-permute-done((bf16[2,64,8192]{2,1,0:T(8,128)(2,1)}, bf16[2,64,8192]{2,1,0:T(8,128)(2,1)}, u32[]{:S(2)}, u32[]{:S(2)}) %collective-permute-start.10) | collective-permute-done | bytes 2097184 | tf_op jit(solution)/shard_map/ppermute | solution.py:338
  161.8 2.4 collective-permute-done.7.refs_10_.refs_7_
  164.2 10.5 %shard_map.87 = (bf16[64,8192]{1,0:T(8,128)(2,1)S(1)}, bf16[64,8192]{1,0:T(8,128)(2,1)S(1)}, bf16[64,8192]{1,0:T(8,128)(2,1)S(1)}, bf16[64,8192]{1,0:T(8,128)(2,...) custom-call(s32[1]{0:T(128)} %bitcast.1.end_ref, ...), custom_call_target="tpu_custom_call" | custom-call | tf_op jit(solution)/shard_map/pallas_call | solution.py:235
  174.8 3.2 %collective-permute-start.12 = (bf16[64,8192]{1,0:T(8,128)(2,1)S(1)}, bf16[64,8192]{1,0:T(8,128)(2,1)S(1)}, u32[]{:S(2)}, u32[]{:S(2)}) collective-permute-start(bf16[64,8192]{1,0:T(8,128)(2,1)S(1)} %get-tuple-element.43), channel_id=1, source_target_pairs={{0,4},{1,5},{2,6},{3,7},{4,0},{5,1},{6,2},{7,3},{8,12},{9,13},{10,... | collective-permute-start | bytes 3145736 | tf_op jit(solution)/shard_map/ppermute | solution.py:338
  180.3 5.0 %collective-permute-start.19 = (bf16[64,8192]{1,0:T(8,128)(2,1)S(1)}, bf16[64,8192]{1,0:T(8,128)(2,1)S(1)}, u32[]{:S(2)}, u32[]{:S(2)}) collective-permute-start(bf16[64,8192]{1,0:T(8,128)(2,1)S(1)} %get-tuple-element.54), channel_id=1, source_target_pairs={{0,4},{1,5},{2,6},{3,7},{12,8},{13,9},{14,10},{15,11},{16,20},{17,... | collective-permute-start | bytes 3145736 | tf_op jit(solution)/shard_map/ppermute | solution.py:338
  186.0 15.6 %collective-permute-done.12.refs_11_ = bf16[64,8192]{1,0:T(8,128)(2,1)S(1)} collective-permute-done((bf16[64,8192]{1,0:T(8,128)(2,1)S(1)}, bf16[64,8192]{1,0:T(8,128)(2,1)S(1)}, u32[]{:S(2)}, u32[]{:S(2)}) %collective-permute-start.12) | collective-permute-done | bytes 1048608 | tf_op jit(solution)/shard_map/ppermute | solution.py:338
  204.2 8.4 %shard_map.88 = (bf16[64,8192]{1,0:T(8,128)(2,1)S(1)}, bf16[64,8192]{1,0:T(8,128)(2,1)}, bf16[2,64,8192]{2,1,0:T(8,128)(2,1)S(1)}, f32[64,8192]{1,0:T(8,128)S(1)...) custom-call(s32[1]{0:T(128)} %bitcast.1.end_ref, ...), custom_call_target="tpu_custom_call" | custom-call | tf_op jit(solution)/shard_map/pallas_call | solution.py:302
  212.8 7.2 %collective-permute-start.18 = (bf16[64,8192]{1,0:T(8,128)(2,1)S(1)}, bf16[64,8192]{1,0:T(8,128)(2,1)S(1)}, u32[]{:S(2)}, u32[]{:S(2)}) collective-permute-start(bf16[64,8192]{1,0:T(8,128)(2,1)S(1)} %add_convert_fusion.2), channel_id=1, source_target_pairs={{0,4},{1,5},{2,6},{3,7},{4,0},{5,1},{6,2},{7,3},{8,12},{9,13},{10,... | collective-permute-start | bytes 3145736 | tf_op jit(solution)/shard_map/ppermute | solution.py:338
  220.1 4.0 %collective-permute-done.19 = bf16[64,8192]{1,0:T(8,128)(2,1)S(1)} collective-permute-done((bf16[64,8192]{1,0:T(8,128)(2,1)S(1)}, bf16[64,8192]{1,0:T(8,128)(2,1)S(1)}, u32[]{:S(2)}, u32[]{:S(2)}) %collective-permute-start.19) | collective-permute-done | bytes 1048608 | tf_op jit(solution)/shard_map/ppermute | solution.py:338
  227.0 7.2 %collective-permute-start.22 = (bf16[64,8192]{1,0:T(8,128)(2,1)S(1)}, bf16[64,8192]{1,0:T(8,128)(2,1)S(1)}, u32[]{:S(2)}, u32[]{:S(2)}) collective-permute-start(bf16[64,8192]{1,0:T(8,128)(2,1)S(1)} %add_convert_fusion), channel_id=1, source_target_pairs={{0,4},{1,5},{2,6},{3,7},{4,0},{5,1},{6,2},{7,3},{8,12},{9,13},{10,... | collective-permute-start | bytes 3145736 | tf_op jit(solution)/shard_map/ppermute | solution.py:338
  234.2 29.2 %collective-permute-done.15.refs_2_ = bf16[2,64,8192]{2,1,0:T(8,128)(2,1)S(1)} collective-permute-done((bf16[2,64,8192]{2,1,0:T(8,128)(2,1)S(1)}, bf16[2,64,8192]{2,1,0:T(8,128)(2,1)S(1)}, u32[]{:S(2)}, u32[]{:S(2)}) %collective-permute-start.15) | collective-permute-done | bytes 2097184 | tf_op jit(solution)/shard_map/ppermute | solution.py:338
  271.9 1.9 collective-permute-done.24
  274.7 5.9 %collective-permute-start.26 = (f32[8,128]{1,0:T(8,128)S(1)}, f32[8,128]{1,0:T(8,128)S(1)}, u32[]{:S(2)}, u32[]{:S(2)}) collective-permute-start(f32[8,128]{1,0:T(8,128)S(1)} %add_add_fusion.1), channel_id=1, source_target_pairs={{0,4},{1,5},{2,6},{3,7},{4,0},{5,1},{6,2},{7,3},{8,12},{9,13},{10,... | collective-permute-start | bytes 12296 | tf_op jit(solution)/shard_map/ppermute | solution.py:338
  285.1 5.0 %shard_map.89 = bf16[128,8192]{1,0:T(8,128)(2,1)} custom-call(bf16[128,256]{1,0:T(8,128)(2,1)S(1)} %fusion.place_ref, bf16[64,8192]{1,0:T(8,128)(2,1)S(1)} %get-tuple-element.46.refs_0_, bf16[64,8192]{1,0:T(8,128)(2,1)} %collective-permute-done.14.refs_1_, bf16[2,64,8192]{2,1,0:T(8,128)(2,1)S(1)} %copy-done.9, bf16[64,8192]{1,0:T(8,128)(2,1)} %collective-permute-done.16.refs_3_), custom_call_target="tpu_custom_call" | custom-call | tf_op jit(solution)/shard_map/pallas_call | solution.py:126
  291.4 2.8 multiply_bitcast_fusion
  (117 shorter events, 33.4 us)
Async XLA Ops:
  65.4 46.3 %collective-permute-start.6 = (bf16[2,64,8192]{2,1,0:T(8,128)(2,1)}, bf16[2,64,8192]{2,1,0:T(8,128)(2,1)}, u32[]{:S(2)}, u32[]{:S(2)}) collective-permute-start(bf16[2,64,8192]{2,1,0:T(8,128)(2,1)} %shard_map.85), channel_id=1, source_target_pairs={{4,8},{5,9},{6,10},{7,11},{8,4},{9,5},{10,6},{11,7},{20,24},{21,25... | collective-permute-start | bytes 6291464 | tf_op jit(solution)/shard_map/ppermute | solution.py:338
  67.4 51.0 %collective-permute-start.5 = (bf16[2,64,8192]{2,1,0:T(8,128)(2,1)}, bf16[2,64,8192]{2,1,0:T(8,128)(2,1)}, u32[]{:S(2)}, u32[]{:S(2)}) collective-permute-start(bf16[2,64,8192]{2,1,0:T(8,128)(2,1)} %shard_map.85), channel_id=1, source_target_pairs={{0,4},{1,5},{2,6},{3,7},{4,0},{5,1},{6,2},{7,3},{8,12},{9,13},{10,... | collective-permute-start | bytes 6291464 | tf_op jit(solution)/shard_map/ppermute | solution.py:338
  79.0 24.4 %collective-permute-start.1 = (bf16[2,2,16,8192]{3,2,1,0:T(8,128)(2,1)S(1)}, bf16[2,2,16,8192]{3,2,1,0:T(8,128)(2,1)S(1)}, u32[]{:S(2)}, u32[]{:S(2)}) collective-permute-start(bf16[2,2,16,8192]{3,2,1,0:T(8,128)(2,1)S(1)} %get-tuple-element.38), channel_id=1, source_target_pairs={{0,2},{1,3},{2,0},{3,1},{4,6},{5,7},{6,4},{7,5},{8,10},{9,11},{10,... | collective-permute-start | bytes 3145736 | tf_op jit(solution)/shard_map/ppermute | solution.py:338
  80.6 24.6 %collective-permute-start = (bf16[1,2,64,8192]{3,2,1,0:T(8,128)(2,1)S(1)}, bf16[1,2,64,8192]{3,2,1,0:T(8,128)(2,1)S(1)}, u32[]{:S(2)}, u32[]{:S(2)}) collective-permute-start(bf16[1,2,64,8192]{3,2,1,0:T(8,128)(2,1)S(1)} %get-tuple-element.35), channel_id=1, source_target_pairs={{0,1},{1,0},{2,3},{3,2},{4,5},{5,4},{6,7},{7,6},{8,9},{9,8},{10,11... | collective-permute-start | bytes 6291464 | tf_op jit(solution)/shard_map/ppermute | solution.py:338
  103.6 25.6 %collective-permute-start.2 = (bf16[2,2,16,8192]{3,2,1,0:T(8,128)(2,1)S(1)}, bf16[2,2,16,8192]{3,2,1,0:T(8,128)(2,1)S(1)}, u32[]{:S(2)}, u32[]{:S(2)}) collective-permute-start(bf16[2,2,16,8192]{3,2,1,0:T(8,128)(2,1)S(1)} %get-tuple-element.39), channel_id=1, source_target_pairs={{0,2},{1,3},{2,0},{3,1},{4,6},{5,7},{6,4},{7,5},{8,10},{9,11},{10,... | collective-permute-start | bytes 3145736 | tf_op jit(solution)/shard_map/ppermute | solution.py:338
  108.0 53.8 %collective-permute-start.10 = (bf16[2,64,8192]{2,1,0:T(8,128)(2,1)}, bf16[2,64,8192]{2,1,0:T(8,128)(2,1)}, u32[]{:S(2)}, u32[]{:S(2)}) collective-permute-start(bf16[2,64,8192]{2,1,0:T(8,128)(2,1)} %pad_maximum_fusion), channel_id=1, source_target_pairs={{0,4},{1,5},{2,6},{3,7},{12,8},{13,9},{14,10},{15,11},{16,20},{17,... | collective-permute-start | bytes 6291464 | tf_op jit(solution)/shard_map/ppermute | solution.py:338
  111.7 52.5 %collective-permute-start.7 = (bf16[2,64,8192]{2,1,0:T(8,128)(2,1)}, bf16[2,64,8192]{2,1,0:T(8,128)(2,1)S(1)}, u32[]{:S(2)}, u32[]{:S(2)}) collective-permute-start(bf16[2,64,8192]{2,1,0:T(8,128)(2,1)} %collective-permute-done.6.refs_11_.refs_8_), channel_id=1, source_target_pairs={{4,0},{5,1},{6,2},{7,3},{8,12},{9,13},{10,14},{11,15},{20,16},{21,... | collective-permute-start | bytes 6291464 | tf_op jit(solution)/shard_map/ppermute | solution.py:338
  118.3 45.9 %collective-permute-start.11 = (bf16[2,64,8192]{2,1,0:T(8,128)(2,1)}, bf16[2,64,8192]{2,1,0:T(8,128)(2,1)}, u32[]{:S(2)}, u32[]{:S(2)}) collective-permute-start(bf16[2,64,8192]{2,1,0:T(8,128)(2,1)} %collective-permute-done.5.refs_4_), channel_id=1, source_target_pairs={{4,8},{5,9},{6,10},{7,11},{8,4},{9,5},{10,6},{11,7},{20,24},{21,25... | collective-permute-start | bytes 6291464 | tf_op jit(solution)/shard_map/ppermute | solution.py:338
  129.2 49.5 %collective-permute-start.3 = (bf16[2,2,32,8192]{3,2,1,0:T(8,128)(2,1)}, bf16[2,2,32,8192]{3,2,1,0:T(8,128)(2,1)}, u32[]{:S(2)}, u32[]{:S(2)}) collective-permute-start(bf16[2,2,32,8192]{3,2,1,0:T(8,128)(2,1)} %get-tuple-element.40), channel_id=1, source_target_pairs={{0,2},{1,3},{2,0},{3,1},{4,6},{5,7},{6,4},{7,5},{8,10},{9,11},{10,... | collective-permute-start | bytes 6291464 | tf_op jit(solution)/shard_map/ppermute | solution.py:338
  174.8 26.8 %collective-permute-start.12 = (bf16[64,8192]{1,0:T(8,128)(2,1)S(1)}, bf16[64,8192]{1,0:T(8,128)(2,1)S(1)}, u32[]{:S(2)}, u32[]{:S(2)}) collective-permute-start(bf16[64,8192]{1,0:T(8,128)(2,1)S(1)} %get-tuple-element.43), channel_id=1, source_target_pairs={{0,4},{1,5},{2,6},{3,7},{4,0},{5,1},{6,2},{7,3},{8,12},{9,13},{10,... | collective-permute-start | bytes 3145736 | tf_op jit(solution)/shard_map/ppermute | solution.py:338
  178.0 23.6 %collective-permute-start.13 = (bf16[64,8192]{1,0:T(8,128)(2,1)S(1)}, bf16[64,8192]{1,0:T(8,128)(2,1)S(1)}, u32[]{:S(2)}, u32[]{:S(2)}) collective-permute-start(bf16[64,8192]{1,0:T(8,128)(2,1)S(1)} %get-tuple-element.44), channel_id=1, source_target_pairs={{4,8},{5,9},{6,10},{7,11},{8,4},{9,5},{10,6},{11,7},{20,24},{21,25... | collective-permute-start | bytes 3145736 | tf_op jit(solution)/shard_map/ppermute | solution.py:338
  180.2 22.4 %collective-permute-start.4 = (bf16[1,2,32,8192]{3,2,1,0:T(8,128)(2,1)S(1)}, bf16[1,2,32,8192]{3,2,1,0:T(8,128)(2,1)S(1)}, u32[]{:S(2)}, u32[]{:S(2)}) collective-permute-start(bf16[1,2,32,8192]{3,2,1,0:T(8,128)(2,1)S(1)} %slice.32), channel_id=1, source_target_pairs={{0,1},{1,0},{2,3},{3,2},{4,5},{5,4},{6,7},{7,6},{8,9},{9,8},{10,11... | collective-permute-start | bytes 3145736 | tf_op jit(solution)/shard_map/ppermute | solution.py:338
  180.3 43.8 %collective-permute-start.19 = (bf16[64,8192]{1,0:T(8,128)(2,1)S(1)}, bf16[64,8192]{1,0:T(8,128)(2,1)S(1)}, u32[]{:S(2)}, u32[]{:S(2)}) collective-permute-start(bf16[64,8192]{1,0:T(8,128)(2,1)S(1)} %get-tuple-element.54), channel_id=1, source_target_pairs={{0,4},{1,5},{2,6},{3,7},{12,8},{13,9},{14,10},{15,11},{16,20},{17,... | collective-permute-start | bytes 3145736 | tf_op jit(solution)/shard_map/ppermute | solution.py:338
  185.3 38.8 %collective-permute-start.20 = (bf16[64,8192]{1,0:T(8,128)(2,1)S(1)}, bf16[64,8192]{1,0:T(8,128)(2,1)S(1)}, u32[]{:S(2)}, u32[]{:S(2)}) collective-permute-start(bf16[64,8192]{1,0:T(8,128)(2,1)S(1)} %get-tuple-element.55), channel_id=1, source_target_pairs={{4,8},{5,9},{6,10},{7,11},{8,4},{9,5},{10,6},{11,7},{20,24},{21,25... | collective-permute-start | bytes 3145736 | tf_op jit(solution)/shard_map/ppermute | solution.py:338
  201.8 64.3 %collective-permute-start.17 = (bf16[64,8192]{1,0:T(8,128)(2,1)S(1)}, bf16[64,8192]{1,0:T(8,128)(2,1)S(1)}, u32[]{:S(2)}, u32[]{:S(2)}) collective-permute-start(bf16[64,8192]{1,0:T(8,128)(2,1)S(1)} %add_convert_fusion.3), channel_id=1, source_target_pairs={{4,8},{5,9},{6,10},{7,11},{8,4},{9,5},{10,6},{11,7},{20,24},{21,25... | collective-permute-start | bytes 3145736 | tf_op jit(solution)/shard_map/ppermute | solution.py:338
  212.8 53.3 %collective-permute-start.18 = (bf16[64,8192]{1,0:T(8,128)(2,1)S(1)}, bf16[64,8192]{1,0:T(8,128)(2,1)S(1)}, u32[]{:S(2)}, u32[]{:S(2)}) collective-permute-start(bf16[64,8192]{1,0:T(8,128)(2,1)S(1)} %add_convert_fusion.2), channel_id=1, source_target_pairs={{0,4},{1,5},{2,6},{3,7},{4,0},{5,1},{6,2},{7,3},{8,12},{9,13},{10,... | collective-permute-start | bytes 3145736 | tf_op jit(solution)/shard_map/ppermute | solution.py:338
  224.1 39.3 %collective-permute-start.15 = (bf16[2,64,8192]{2,1,0:T(8,128)(2,1)S(1)}, bf16[2,64,8192]{2,1,0:T(8,128)(2,1)S(1)}, u32[]{:S(2)}, u32[]{:S(2)}) collective-permute-start(bf16[2,64,8192]{2,1,0:T(8,128)(2,1)S(1)} %get-tuple-element.48), channel_id=1, source_target_pairs={{0,2},{1,3},{2,0},{3,1},{4,6},{5,7},{6,4},{7,5},{8,10},{9,11},{10,... | collective-permute-start | bytes 6291464 | tf_op jit(solution)/shard_map/ppermute | solution.py:338
  225.8 38.7 %collective-permute-start.21 = (bf16[64,8192]{1,0:T(8,128)(2,1)S(1)}, bf16[64,8192]{1,0:T(8,128)(2,1)S(1)}, u32[]{:S(2)}, u32[]{:S(2)}) collective-permute-start(bf16[64,8192]{1,0:T(8,128)(2,1)S(1)} %add_convert_fusion.1), channel_id=1, source_target_pairs={{4,8},{5,9},{6,10},{7,11},{8,4},{9,5},{10,6},{11,7},{20,24},{21,25... | collective-permute-start | bytes 3145736 | tf_op jit(solution)/shard_map/ppermute | solution.py:338
  227.0 38.0 %collective-permute-start.22 = (bf16[64,8192]{1,0:T(8,128)(2,1)S(1)}, bf16[64,8192]{1,0:T(8,128)(2,1)S(1)}, u32[]{:S(2)}, u32[]{:S(2)}) collective-permute-start(bf16[64,8192]{1,0:T(8,128)(2,1)S(1)} %add_convert_fusion), channel_id=1, source_target_pairs={{0,4},{1,5},{2,6},{3,7},{4,0},{5,1},{6,2},{7,3},{8,12},{9,13},{10,... | collective-permute-start | bytes 3145736 | tf_op jit(solution)/shard_map/ppermute | solution.py:338
  263.4 20.1 %collective-permute-start.14 = (bf16[64,8192]{1,0:T(8,128)(2,1)}, bf16[64,8192]{1,0:T(8,128)(2,1)}, u32[]{:S(2)}, u32[]{:S(2)}) collective-permute-start(bf16[64,8192]{1,0:T(8,128)(2,1)} %get-tuple-element.47), channel_id=1, source_target_pairs={{0,1},{1,0},{2,3},{3,2},{4,5},{5,4},{6,7},{7,6},{8,9},{9,8},{10,11... | collective-permute-start | bytes 3145736 | tf_op jit(solution)/shard_map/ppermute | solution.py:338
  264.5 18.9 %collective-permute-start.16 = (bf16[64,8192]{1,0:T(8,128)(2,1)}, bf16[64,8192]{1,0:T(8,128)(2,1)}, u32[]{:S(2)}, u32[]{:S(2)}) collective-permute-start(bf16[64,8192]{1,0:T(8,128)(2,1)} %slice_bitcast_fusion), channel_id=1, source_target_pairs={{0,1},{1,0},{2,3},{3,2},{4,5},{5,4},{6,7},{7,6},{8,9},{9,8},{10,11... | collective-permute-start | bytes 3145736 | tf_op jit(solution)/shard_map/ppermute | solution.py:338
  274.7 15.4 %collective-permute-start.26 = (f32[8,128]{1,0:T(8,128)S(1)}, f32[8,128]{1,0:T(8,128)S(1)}, u32[]{:S(2)}, u32[]{:S(2)}) collective-permute-start(f32[8,128]{1,0:T(8,128)S(1)} %add_add_fusion.1), channel_id=1, source_target_pairs={{0,4},{1,5},{2,6},{3,7},{4,0},{5,1},{6,2},{7,3},{8,12},{9,13},{10,... | collective-permute-start | bytes 12296 | tf_op jit(solution)/shard_map/ppermute | solution.py:338
  280.6 9.5 %collective-permute-start.27 = (f32[8,128]{1,0:T(8,128)S(1)}, f32[8,128]{1,0:T(8,128)S(1)}, u32[]{:S(2)}, u32[]{:S(2)}) collective-permute-start(f32[8,128]{1,0:T(8,128)S(1)} %add_add_fusion.1), channel_id=1, source_target_pairs={{0,8},{1,9},{2,10},{3,11},{4,12},{5,13},{6,14},{7,15},{8,0},{9,1},... | collective-permute-start | bytes 12296 | tf_op jit(solution)/shard_map/ppermute | solution.py:338
  282.0 8.2 %collective-permute-start.28 = (f32[8,128]{1,0:T(8,128)S(1)}, f32[8,128]{1,0:T(8,128)S(1)}, u32[]{:S(2)}, u32[]{:S(2)}) collective-permute-start(f32[8,128]{1,0:T(8,128)S(1)} %add_add_fusion.1), channel_id=1, source_target_pairs={{0,12},{1,13},{2,14},{3,15},{4,8},{5,9},{6,10},{7,11},{8,4},{9,5},... | collective-permute-start | bytes 12296 | tf_op jit(solution)/shard_map/ppermute | solution.py:338
  (31 other events, 435.5 us)

commit v7 on v6

--- a/solution.py
+++ b/solution.py
@@ -144,112 +144,115 @@
     return upper == (lax.broadcasted_iota(jnp.int32, (rows, columns), 1) < first_columns)
 
 
-def stack(down, up):
-    _, rank, width = down.shape
-    pieces = 4
-    part = rank // pieces
-
-    def body(*refs):
-        out, sems = refs[2:]
-        copies = [
-            pltpu.make_async_copy(refs[k].at[0, pl.ds(n * part, part)], out.at[k, pl.ds(n * part, part)], sems.at[k, n])
-            for k in range(2)
-            for n in range(pieces)
-        ]
-        for c in copies:
-            c.start()
-        for c in copies:
-            c.wait()
-
-    return pl.pallas_call(
-        body,
-        in_specs=[HBM, HBM],
-        out_specs=pl.BlockSpec(memory_space=pl.ANY),
-        out_shape=jax.ShapeDtypeStruct((2, rank, width), BF16),
-        scratch_shapes=[pltpu.SemaphoreType.DMA((2, pieces))],
-    )(*in_hbm(down, up))
-
-
-def far_groups(is_end, stage3, stage2, ends, far, outer, crossed, capacity, first2):
-    plane = len(stage3)
-    _, rank, width = far.shape
-    block = plane * capacity
+def held_copies(source, held, sems, tile):
+    return [
+        pltpu.make_async_copy(source.at[:, :, pl.ds(i * tile, tile)], held.at[:, :, pl.ds(i * tile, tile)], sems.at[i])
+        for i in range(held.shape[2] // tile)
+    ]
+
+
+def far_end(mine, handed, far):
+    _, block, width = mine.shape
+    rank = far.shape[1]
     tile = min(width, 2048)
     tiles = width // tile
 
-    tall = 3 * block
-
-    def body(end_ref, *refs):
-        stage_in, refs = refs[:2 * plane], refs[2 * plane:]
-        ends_in, far_in, outer_in, crossed_in = refs[:4]
-        sum3_refs, sum2_refs, swap_ref, inner2_ref, dx_ref = refs[4:6], refs[6:8], *refs[8:11]
-        held, left, sems = refs[11:]
+    def body(mine_in, handed_in, far_in, up_ref, down_ref, dx_ref, handed_dx_ref, held, left, sems):
         step = pl.program_id(0)
-        is_mine = corner(tall, 2 * block, 2 * rank, rank)
-
-        def copies(i):
-            cut = pl.ds(i * tile, tile)
-            firsts = (0,) * plane + first2
-            return [
-                pltpu.make_async_copy(
-                    r.at[0, :, pl.ds(first, capacity), cut], held.at[:, pl.ds(n * capacity, capacity), cut], sems.at[i, n]
-                )
-                for n, (r, first) in enumerate(zip(stage_in, firsts))
-            ]
 
         def rows(k, cut):
-            return jnp.concatenate([held[k, :block, cut], ends_in[k, :, cut], held[k, block:, cut]], axis=0)
+            return jnp.concatenate([held[k, :, cut], handed_in[k, :, cut]], axis=0)
 
         @pl.when(step == 0)
         def _():
-            for i in range(tiles):
-                for c in copies(i):
-                    c.start()
-            sums = [jnp.zeros((tall, 2 * rank), F32)] * 2
-            for i in range(tiles):
-                for c in copies(i):
-                    c.wait()
+            copies = held_copies(mine_in, held, sems, tile)
+            for c in copies:
+                c.start()
+            sums = [jnp.zeros((rank, 2 * block), F32)] * 2
+            for i, c in enumerate(copies):
+                c.wait()
                 cut = pl.ds(i * tile, tile)
                 for k in range(2):
-                    near = jnp.where(end_ref[0] == 1, outer_in[k, :, cut], crossed_in[k, :, cut])
-                    both = jnp.concatenate([far_in[k, :, cut], near], axis=0)
-                    sums[k] += dot32(rows(k, cut), both, ROWS_OF)
+                    sums[k] += dot32(far_in[k, :, cut], rows(k, cut), ROWS_OF)
             for k in range(2):
-                left[k] = jnp.where(is_mine, sums[k], 0.0).astype(BF16)
-            inner2_ref[...] = left[1, 2 * block:, rank:]
+                left[k] = sums[k].astype(BF16)
 
         cut = pl.ds(pl.multiple_of(step * tile, tile), tile)
-        for k in range(2):
-            both = dot32(left[k], rows(1 - k, cut), OUTER).astype(BF16)
-            sum3_refs[k][...] = both[:rank]
-            sum2_refs[k][...] = both[rank:]
-        dx = dot32(left[1, :2 * block, :rank], far_in[0, :, cut]).astype(BF16)
+        up_ref[...] = dot32(left[0], rows(1, cut)).astype(BF16)
+        down_ref[...] = dot32(left[1], rows(0, cut)).astype(BF16)
+        dx = dot32(left[1], far_in[0, :, cut], OUTER).astype(BF16)
         dx_ref[...] = dx[:block]
-        swap_ref[...] = jnp.where(end_ref[0] == 1, both[rank:], dx[block:])
+        handed_dx_ref[...] = dx[block:]
 
     def wide(rows):
-        return pl.BlockSpec((rows, tile), lambda i: (0, i)), jax.ShapeDtypeStruct((rows, width), BF16)
-
-    outs = [wide(rank)] * 4 + [wide(block)]
-    outs += [(pl.BlockSpec((block, rank), lambda i: (0, 0)), jax.ShapeDtypeStruct((block, rank), BF16)), wide(block)]
+        return pl.BlockSpec((rows, tile), lambda i: (0, i))
+
+    sizes = (rank, rank, block, block)
     return pl.pallas_call(
         body,
         grid=(tiles,),
-        in_specs=[pl.BlockSpec(memory_space=pltpu.SMEM)] + [HBM] * (2 * plane) + [WHOLE] * 4,
-        out_specs=[o[0] for o in outs],
-        out_shape=[o[1] for o in outs],
+        in_specs=[HBM] + [WHOLE] * 2,
+        out_specs=[wide(n) for n in sizes],
+        out_shape=[jax.ShapeDtypeStruct((n, width), BF16) for n in sizes],
         scratch_shapes=[
-            pltpu.VMEM((2, 2 * block, width), BF16),
-            pltpu.VMEM((2, tall, 2 * rank), BF16),
-            pltpu.SemaphoreType.DMA((tiles, 2 * plane)),
+            pltpu.VMEM((2, block, width), BF16),
+            pltpu.VMEM((2, rank, 2 * block), BF16),
+            pltpu.SemaphoreType.DMA((tiles,)),
         ],
         compiler_params=kernel_params(),
-    )(is_end, *in_hbm(*stage3, *stage2), *in_vmem(ends, far, outer, crossed))
+    )(*in_hbm(mine), *in_vmem(handed, far))
+
+
+def far_mid(is_end, mine, outer, crossed, handed_dx):
+    _, block, width = mine.shape
+    rank = outer.shape[1]
+    tile = min(width, 2048)
+    tiles = width // tile
+
+    def body(end_ref, mine_in, outer_in, crossed_in, handed_ref, up_ref, down_ref, swap_ref, inner_ref, held, left, sems):
+        step = pl.program_id(0)
+
+        @pl.when(step == 0)
+        def _():
+            copies = held_copies(mine_in, held, sems, tile)
+            for c in copies:
+                c.start()
+            sums = [jnp.zeros((rank, block), F32)] * 2
+            for i, c in enumerate(copies):
+                c.wait()
+                cut = pl.ds(i * tile, tile)
+                for k in range(2):
+                    factors = jnp.where(end_ref[0] == 1, outer_in[k, :, cut], crossed_in[k, :, cut])
+                    sums[k] += dot32(factors, held[k, :, cut], ROWS_OF)
+            for k in range(2):
+                left[k] = sums[k].astype(BF16)
+            inner_ref[...] = sums[1].T.astype(BF16)
+
+        cut = pl.ds(pl.multiple_of(step * tile, tile), tile)
+        up_ref[...] = dot32(left[0], held[1, :, cut]).astype(BF16)
+        down = dot32(left[1], held[0, :, cut]).astype(BF16)
+        down_ref[...] = down
+        swap_ref[...] = jnp.where(end_ref[0] == 1, down, handed_ref[...])
+
+    wide = pl.BlockSpec((rank, tile), lambda i: (0, i))
+    return pl.pallas_call(
+        body,
+        grid=(tiles,),
+        in_specs=[pl.BlockSpec(memory_space=pltpu.SMEM), HBM, WHOLE, WHOLE, pl.BlockSpec((block, tile), lambda i: (0, i))],
+        out_specs=[wide] * 3 + [pl.BlockSpec((block, rank), lambda i: (0, 0))],
+        out_shape=[jax.ShapeDtypeStruct((rank, width), BF16)] * 3 + [jax.ShapeDtypeStruct((block, rank), BF16)],
+        scratch_shapes=[
+            pltpu.VMEM((2, block, width), BF16),
+            pltpu.VMEM((2, rank, block), BF16),
+            pltpu.SemaphoreType.DMA((tiles,)),
+        ],
+        compiler_params=kernel_params(),
+    )(is_end, *in_hbm(mine), *in_vmem(outer, crossed), handed_dx)
 
 
 def near_groups(is_end, stage, pair, down, up, outer, crossed, inner2, dx3, swapped, capacity, first1):
     plane = len(stage)
-    _, rank, width = pair.shape
+    rank, width = down.shape
     block = plane * capacity
     tile = min(width, 2048)
     tiles = width // tile
@@ -352,10 +355,11 @@
         return (term + sum(after([send(term, pairs) for pairs in along], grad_acts)))[0, 0]
 
     down, up = pool_down_factors[0], pool_up_factors[0]
-    own = stack(pool_down_factors, pool_up_factors)
+    own = jnp.concatenate([pool_down_factors, pool_up_factors])
     pair = send(own, swap)
-
-    owner, position = route(after(token_task_index, own), task_slot_lookup, ndevices)
+    crossed = send(own, cross)
+
+    owner, position = route(token_task_index, task_slot_lookup, ndevices)
     owner_z, turn = owner // plane, (owner % plane) ^ column
     other_mid = jnp.where(z < 2, 2, 1)
     kind = jnp.where(owner_z == z, 0, jnp.where(owner_z == (z ^ 1), 1, jnp.where(owner_z == other_mid, 2, 3)))
@@ -375,7 +379,6 @@
     row = jnp.where(turn < 2, turn * block + mine, row)
     place = places(kind >= 0, row, 4 * block)
     place_back = places(kind >= 0, turn * block + mine, 4 * block)
-    crossed = send(own, cross)
     own_rows, beside_rows, across3, across2, across10 = pack(
         place, acts, cotan, [(1, 4 * capacity)] * 2 + [(2, capacity)] * 2 + [(2, 2 * capacity)]
     )
@@ -387,20 +390,20 @@
     beside_rows = send(beside_rows, beside(1))
     across3 = over_x(across3)
     stage3 = (own_rows, beside_rows) + across3
-    ends = jnp.concatenate([r[0, :, :capacity] for r in stage3], axis=1)
-    ends = send(ends, inward)
+    rows3 = jnp.concatenate([r[0, :, :capacity] for r in stage3], axis=1)
+    handed = send(rows3, inward)
     across2 = over_x(after(across2, across3[0]))
     across10 = over_x(after(across10, across2[0]))
-    stage2 = (own_rows, beside_rows) + across2
+    rows2 = [r[0, :, capacity:2 * capacity] for r in (own_rows, beside_rows)] + [r[0] for r in across2]
+    rows2 = jnp.concatenate(rows2, axis=1)
     stage10 = (own_rows, beside_rows) + across10
     outer = send(crossed, outward)
     far = send(pair, cross)
 
-    up3, down3, up2, down2, swapped, inner2, dx3 = far_groups(
-        end_flag, stage3, stage2, ends, far, outer, crossed, capacity, (capacity, capacity, 0, 0)
-    )
-    down3, swapped = send(down3, cross), send(swapped, swap)
-    up3, up2_in = send(up3, cross), send(up2, inward)
+    up3, down3, dx3, handed_dx = far_end(rows3, handed, far)
+    down3, up3 = send(down3, cross), send(up3, cross)
+    up2, down2, swapped, inner2 = far_mid(end_flag, rows2, outer, crossed, handed_dx)
+    swapped, up2_in = send(swapped, swap), send(up2, inward)
 
     swapped, down3 = lax.optimization_barrier((swapped, down3))
     dx_own, dx_beside, dx_across, up1, down1, up0, down0 = near_groups(

time: 295 us -> 232 us (0.79)
  Pallas kernels: 95 us -> 32.2 us
  waiting for transfers between devices: 122 us -> 111 us
  local copies, waits for them, and re-layouts: 8.8 us -> 14.4 us
  other arithmetic: 8.46 us -> 11.5 us
    pallas_call x2, Pallas kernels: 75.2 us -> 12.4 us  [the longest x1 7.09 us: far_end(): pl.pallas_call(body, grid=(tiles,), in_specs=[HBM] + [WHOLE] * 2, out_spe...]
    ppermute x29, waiting for transfers between devices: 122 us -> 111 us  [send(): return lax.ppermute(array, 'dp', pairs)]
    concatenate x1 -> x2, other arithmetic: 1.56 us -> 4.59 us  [the longest x1 2.99 us: move_adapters(): rows2 = jnp.concatenate(rows2, axis=1)]
    unnamed x52 -> x49, local copies, waits for them, and re-layouts: 5.51 us -> 7.37 us
  transfers between devices with their start and end apart: 29 -> 29, of which waited for: 12 -> 10; matrix products, arithmetic and copies ran while one was open for 3% -> 6% of each run, Pallas kernels for 10% -> 14%
where the time goes in v7:
time: 232 us; the launch traced here: 231 us
  waiting for transfers between devices  111 us (48%)
  starting transfers between devices  58.7 us (25%)
  Pallas kernels  32.2 us (14%)
  local copies, waits for them, and re-layouts  14.4 us (6%)
  other arithmetic  11.5 us (5%)
  between operations  3.13 us (1%)
    ppermute x29, waiting for transfers between devices, send(): return lax.ppermute(array, 'dp', pairs)  111 us
    ppermute x29, starting transfers between devices, send(): return lax.ppermute(array, 'dp', pairs)  58.7 us
    pallas_call x1, Pallas kernels, near_groups(): pl.pallas_call(body, grid=(tiles,), in_specs=[pl.BlockSpec(memory_space=p...  8.43 us
    unnamed x49, local copies, waits for them, and re-layouts  7.37 us
    pallas_call x1, Pallas kernels, far_end(): pl.pallas_call(body, grid=(tiles,), in_specs=[HBM] + [WHOLE] * 2, out_spe...  7.09 us
    pallas_call x1, Pallas kernels, pack(): pl.pallas_call(body, grid=(tiles,), in_specs=[pl.BlockSpec(place.shape, l...  6.36 us
    pallas_call x1, Pallas kernels, far_mid(): pl.pallas_call(body, grid=(tiles,), in_specs=[pl.BlockSpec(memory_space=p...  5.31 us
    pallas_call x1, Pallas kernels, unpack(): pl.pallas_call(body, grid=(width // tile,), in_specs=[pl.BlockSpec(place....  5.01 us
  transfers between devices with their start and end apart: 29, of which 10 were waited for; matrix products, arithmetic and copies ran while one was open for 6% of the time, Pallas kernels for 14%

profile of v7, /device:TPU:0, one launch (start us, length us, event | category | flops | bytes accessed | tf_op | source)
XLA Modules:
  0.0 231.4 jit_solution(3411678170088458533)
XLA Ops:
  0.7 2.4 %constant_dynamic-update-slice_fusion.1 = bf16[2,64,8192]{2,1,0:T(8,128)(2,1)} fusion(bf16[1,64,8192]{2,1,0:T(8,128)(2,1)} %param.10), kind=kLoop, calls=%fused_computation.29 | loop fusion | bytes 2097152
  4.1 3.0 %collective-permute-start.5 = (bf16[2,64,8192]{2,1,0:T(8,128)(2,1)}, bf16[2,64,8192]{2,1,0:T(8,128)(2,1)}, u32[]{:S(2)}, u32[]{:S(2)}) collective-permute-start(bf16[2,64,8192]{2,1,0:T(8,128)(2,1)} %constant_dynamic-update-slice_fusion), channel_id=1, source_target_pairs={{0,4},{1,5},{2,6},{3,7},{4,0},{5,1},{6,2},{7,3},{8,12},{9,13},{10,... | collective-permute-start | bytes 6291464 | tf_op jit(solution)/shard_map/ppermute | solution.py:341
  8.6 6.4 %shard_map.85 = (bf16[1,2,64,8192]{3,2,1,0:T(8,128)(2,1)S(1)}, bf16[1,2,64,8192]{3,2,1,0:T(8,128)(2,1)S(1)}, bf16[2,2,16,8192]{3,2,1,0:T(8,128)(2,1)S(1)}, bf16[...) custom-call(bf16[256,128]{1,0:T(8,128)(2,1)S(1)} %fusion.1.place_ref, bf16[128,8192]{1,0:T(8,128)(2,1)} %x_in.1, ...), custom_call_target="tpu_custom_call" | custom-call | tf_op jit(solution)/shard_map/pallas_call | solution.py:107
  17.5 23.1 %collective-permute-done.1 = bf16[2,2,16,8192]{3,2,1,0:T(8,128)(2,1)S(1)} collective-permute-done((bf16[2,2,16,8192]{3,2,1,0:T(8,128)(2,1)S(1)}, bf16[2,2,16,8192]{3,2,1,0:T(8,128)(2,1)S(1)}, u32[]{:S(2)}, u32[]{:S(2)}) %collective-permute-start.1) | collective-permute-done | bytes 1048608 | tf_op jit(solution)/shard_map/ppermute | solution.py:341
  46.2 7.5 %collective-permute-start.10 = (bf16[2,64,8192]{2,1,0:T(8,128)(2,1)}, bf16[2,64,8192]{2,1,0:T(8,128)(2,1)}, u32[]{:S(2)}, u32[]{:S(2)}) collective-permute-start(bf16[2,64,8192]{2,1,0:T(8,128)(2,1)} %pad_maximum_fusion.1.mine_in), channel_id=1, source_target_pairs={{0,4},{1,5},{2,6},{3,7},{12,8},{13,9},{14,10},{15,11},{16,20},{17,... | collective-permute-start | bytes 6291464 | tf_op jit(solution)/shard_map/ppermute | solution.py:341
  53.6 2.1 collective-permute-start.11
  57.0 9.4 %collective-permute-done.2 = bf16[2,2,16,8192]{3,2,1,0:T(8,128)(2,1)S(1)} collective-permute-done((bf16[2,2,16,8192]{3,2,1,0:T(8,128)(2,1)S(1)}, bf16[2,2,16,8192]{3,2,1,0:T(8,128)(2,1)S(1)}, u32[]{:S(2)}, u32[]{:S(2)}) %collective-permute-start.2) | collective-permute-done | bytes 1048608 | tf_op jit(solution)/shard_map/ppermute | solution.py:341
  69.7 3.0 %pad_maximum_fusion.mine_in = bf16[2,64,8192]{2,1,0:T(8,128)(2,1)} fusion(bf16[2,16,8192]{2,1,0:T(8,128)(2,1)} %bitcast.7, bf16[2,16,8192]{2,1,0:T(8,128)(2,1)} %get-tuple-element.72, bf16[2,16,8192]{2,1,0:T(8,128)(2,1)} %get-tuple-element.69, bf16[2,16,8192]{2,1,0:T(8,128)(2,1)} %get-tuple-element.67), kind=kLoop, calls=%fused_computation | loop fusion | flops 8388608 | bytes 4194304 | tf_op jit(solution)/shard_map/concatenate | solution.py:398
  72.7 25.2 %collective-permute-done.10.handed_in = bf16[2,64,8192]{2,1,0:T(8,128)(2,1)} collective-permute-done((bf16[2,64,8192]{2,1,0:T(8,128)(2,1)}, bf16[2,64,8192]{2,1,0:T(8,128)(2,1)}, u32[]{:S(2)}, u32[]{:S(2)}) %collective-permute-start.10) | collective-permute-done | bytes 2097184 | tf_op jit(solution)/shard_map/ppermute | solution.py:341
  97.8 7.1 %shard_map.86 = (bf16[64,8192]{1,0:T(8,128)(2,1)S(1)}, bf16[64,8192]{1,0:T(8,128)(2,1)S(1)}, bf16[64,8192]{1,0:T(8,128)(2,1)S(1)}, bf16[64,8192]{1,0:T(8,128)(2,1)S(1)}) custom-call(bf16[2,64,8192]{2,1,0:T(8,128)(2,1)} %pad_maximum_fusion.1.mine_in, bf16[2,64,8192]{2,1,0:T(8,128)(2,1)} %collective-permute-done.10.handed_in, ...), custom_call_target="tpu_custom_call" | custom-call | tf_op jit(solution)/shard_map/pallas_call | solution.py:191
  105.1 5.3 %shard_map.87 = (bf16[64,8192]{1,0:T(8,128)(2,1)S(1)}, bf16[64,8192]{1,0:T(8,128)(2,1)S(1)}, bf16[64,8192]{1,0:T(8,128)(2,1)S(1)}, bf16[64,64]{1,0:T(8,128)(2,1)S(1)}) custom-call(s32[1]{0:T(128)} %bitcast.1.end_ref, bf16[2,64,8192]{2,1,0:T(8,128)(2,1)} %pad_maximum_fusion.mine_in, bf16[2,64,8192]{2,1,0:T(8,128)(2,1)} %collective-permute-done.7.outer_in.refs_7_, ...), custom_call_target="tpu_custom_call" | custom-call | tf_op jit(solution)/shard_map/pallas_call | solution.py:238
  110.4 5.6 %collective-permute-start.12 = (bf16[64,8192]{1,0:T(8,128)(2,1)S(1)}, bf16[64,8192]{1,0:T(8,128)(2,1)S(1)}, u32[]{:S(2)}, u32[]{:S(2)}) collective-permute-start(bf16[64,8192]{1,0:T(8,128)(2,1)S(1)} %get-tuple-element.43), channel_id=1, source_target_pairs={{0,4},{1,5},{2,6},{3,7},{4,0},{5,1},{6,2},{7,3},{8,12},{9,13},{10,... | collective-permute-start | bytes 3145736 | tf_op jit(solution)/shard_map/ppermute | solution.py:341
  118.3 5.6 %collective-permute-start.19 = (bf16[64,8192]{1,0:T(8,128)(2,1)S(1)}, bf16[64,8192]{1,0:T(8,128)(2,1)S(1)}, u32[]{:S(2)}, u32[]{:S(2)}) collective-permute-start(bf16[64,8192]{1,0:T(8,128)(2,1)S(1)} %get-tuple-element.54), channel_id=1, source_target_pairs={{0,4},{1,5},{2,6},{3,7},{12,8},{13,9},{14,10},{15,11},{16,20},{17,... | collective-permute-start | bytes 3145736 | tf_op jit(solution)/shard_map/ppermute | solution.py:341
  124.6 15.0 %collective-permute-done.12.refs_11_ = bf16[64,8192]{1,0:T(8,128)(2,1)S(1)} collective-permute-done((bf16[64,8192]{1,0:T(8,128)(2,1)S(1)}, bf16[64,8192]{1,0:T(8,128)(2,1)S(1)}, u32[]{:S(2)}, u32[]{:S(2)}) %collective-permute-start.12) | collective-permute-done | bytes 1048608 | tf_op jit(solution)/shard_map/ppermute | solution.py:341
  140.6 8.4 %shard_map.88 = (bf16[64,8192]{1,0:T(8,128)(2,1)S(1)}, bf16[64,8192]{1,0:T(8,128)(2,1)}, bf16[2,64,8192]{2,1,0:T(8,128)(2,1)S(1)}, f32[64,8192]{1,0:T(8,128)S(1)...) custom-call(s32[1]{0:T(128)} %bitcast.1.end_ref, ...), custom_call_target="tpu_custom_call" | custom-call | tf_op jit(solution)/shard_map/pallas_call | solution.py:305
  150.1 7.1 %collective-permute-start.18 = (bf16[64,8192]{1,0:T(8,128)(2,1)S(1)}, bf16[64,8192]{1,0:T(8,128)(2,1)S(1)}, u32[]{:S(2)}, u32[]{:S(2)}) collective-permute-start(bf16[64,8192]{1,0:T(8,128)(2,1)S(1)} %add_convert_fusion.2), channel_id=1, source_target_pairs={{0,4},{1,5},{2,6},{3,7},{4,0},{5,1},{6,2},{7,3},{8,12},{9,13},{10,... | collective-permute-start | bytes 3145736 | tf_op jit(solution)/shard_map/ppermute | solution.py:341
  157.2 4.9 %collective-permute-done.19 = bf16[64,8192]{1,0:T(8,128)(2,1)S(1)} collective-permute-done((bf16[64,8192]{1,0:T(8,128)(2,1)S(1)}, bf16[64,8192]{1,0:T(8,128)(2,1)S(1)}, u32[]{:S(2)}, u32[]{:S(2)}) %collective-permute-start.19) | collective-permute-done | bytes 1048608 | tf_op jit(solution)/shard_map/ppermute | solution.py:341
  165.0 7.2 %collective-permute-start.22 = (bf16[64,8192]{1,0:T(8,128)(2,1)S(1)}, bf16[64,8192]{1,0:T(8,128)(2,1)S(1)}, u32[]{:S(2)}, u32[]{:S(2)}) collective-permute-start(bf16[64,8192]{1,0:T(8,128)(2,1)S(1)} %add_convert_fusion), channel_id=1, source_target_pairs={{0,4},{1,5},{2,6},{3,7},{4,0},{5,1},{6,2},{7,3},{8,12},{9,13},{10,... | collective-permute-start | bytes 3145736 | tf_op jit(solution)/shard_map/ppermute | solution.py:341
  172.2 30.7 %collective-permute-done.15.refs_2_ = bf16[2,64,8192]{2,1,0:T(8,128)(2,1)S(1)} collective-permute-done((bf16[2,64,8192]{2,1,0:T(8,128)(2,1)S(1)}, bf16[2,64,8192]{2,1,0:T(8,128)(2,1)S(1)}, u32[]{:S(2)}, u32[]{:S(2)}) %collective-permute-start.15) | collective-permute-done | bytes 2097184 | tf_op jit(solution)/shard_map/ppermute | solution.py:341
  211.4 1.9 collective-permute-done.24
  213.7 4.4 %collective-permute-start.26 = (f32[8,128]{1,0:T(8,128)S(1)}, f32[8,128]{1,0:T(8,128)S(1)}, u32[]{:S(2)}, u32[]{:S(2)}) collective-permute-start(f32[8,128]{1,0:T(8,128)S(1)} %add_add_fusion.1), channel_id=1, source_target_pairs={{0,4},{1,5},{2,6},{3,7},{4,0},{5,1},{6,2},{7,3},{8,12},{9,13},{10,... | collective-permute-start | bytes 12296 | tf_op jit(solution)/shard_map/ppermute | solution.py:341
  218.6 2.0 collective-permute-start.28
  222.3 5.0 %shard_map.89 = bf16[128,8192]{1,0:T(8,128)(2,1)} custom-call(bf16[128,256]{1,0:T(8,128)(2,1)S(1)} %fusion.place_ref, bf16[64,8192]{1,0:T(8,128)(2,1)S(1)} %copy-done.13, bf16[64,8192]{1,0:T(8,128)(2,1)} %collective-permute-done.14.refs_1_, bf16[2,64,8192]{2,1,0:T(8,128)(2,1)S(1)} %copy-done.9, bf16[64,8192]{1,0:T(8,128)(2,1)} %collective-permute-done.16.refs_3_), custom_call_target="tpu_custom_call" | custom-call | tf_op jit(solution)/shard_map/pallas_call | solution.py:126
  228.6 2.8 %multiply_bitcast_fusion = (f32[1,64,8192]{2,1,0:T(8,128)}, f32[1,64,8192]{2,1,0:T(8,128)}) fusion(f32[]{:T(128)} %bitcast.13, bf16[64,8192]{1,0:T(8,128)(2,1)S(1)} %copy-done.21, f32[64,8192]{1,0:T(8,128)S(1)} %get-tuple-element.53, bf16[64,8192]{1,0:T(8,128)(2,1)S(1)} %copy-done.19, bf16[64,8192]{1,0:T(8,128)(2,1)S(1)} %copy-done.17, ...), kind=kLoop, calls=%fused_computation.2 | loop fusion | flops 5242880 | bytes 12582916 | tf_op jit(solution)/shard_map/broadcast_in_dim | solution.py:37
  (116 shorter events, 33.4 us)
Async XLA Ops:
  4.1 49.6 %collective-permute-start.5 = (bf16[2,64,8192]{2,1,0:T(8,128)(2,1)}, bf16[2,64,8192]{2,1,0:T(8,128)(2,1)}, u32[]{:S(2)}, u32[]{:S(2)}) collective-permute-start(bf16[2,64,8192]{2,1,0:T(8,128)(2,1)} %constant_dynamic-update-slice_fusion), channel_id=1, source_target_pairs={{0,4},{1,5},{2,6},{3,7},{4,0},{5,1},{6,2},{7,3},{8,12},{9,13},{10,... | collective-permute-start | bytes 6291464 | tf_op jit(solution)/shard_map/ppermute | solution.py:341
  7.1 48.6 %collective-permute-start.6 = (bf16[2,64,8192]{2,1,0:T(8,128)(2,1)}, bf16[2,64,8192]{2,1,0:T(8,128)(2,1)S(1)}, u32[]{:S(2)}, u32[]{:S(2)}) collective-permute-start(bf16[2,64,8192]{2,1,0:T(8,128)(2,1)} %constant_dynamic-update-slice_fusion), channel_id=1, source_target_pairs={{4,8},{5,9},{6,10},{7,11},{8,4},{9,5},{10,6},{11,7},{20,24},{21,25... | collective-permute-start | bytes 6291464 | tf_op jit(solution)/shard_map/ppermute | solution.py:341
  15.0 27.4 %collective-permute-start = (bf16[1,2,64,8192]{3,2,1,0:T(8,128)(2,1)S(1)}, bf16[1,2,64,8192]{3,2,1,0:T(8,128)(2,1)S(1)}, u32[]{:S(2)}, u32[]{:S(2)}) collective-permute-start(bf16[1,2,64,8192]{3,2,1,0:T(8,128)(2,1)S(1)} %get-tuple-element.34), channel_id=1, source_target_pairs={{0,1},{1,0},{2,3},{3,2},{4,5},{5,4},{6,7},{7,6},{8,9},{9,8},{10,11... | collective-permute-start | bytes 6291464 | tf_op jit(solution)/shard_map/ppermute | solution.py:341
  15.1 25.6 %collective-permute-start.1 = (bf16[2,2,16,8192]{3,2,1,0:T(8,128)(2,1)S(1)}, bf16[2,2,16,8192]{3,2,1,0:T(8,128)(2,1)S(1)}, u32[]{:S(2)}, u32[]{:S(2)}) collective-permute-start(bf16[2,2,16,8192]{3,2,1,0:T(8,128)(2,1)S(1)} %get-tuple-element.37), channel_id=1, source_target_pairs={{0,2},{1,3},{2,0},{3,1},{4,6},{5,7},{6,4},{7,5},{8,10},{9,11},{10,... | collective-permute-start | bytes 3145736 | tf_op jit(solution)/shard_map/ppermute | solution.py:341
  40.8 25.6 %collective-permute-start.2 = (bf16[2,2,16,8192]{3,2,1,0:T(8,128)(2,1)S(1)}, bf16[2,2,16,8192]{3,2,1,0:T(8,128)(2,1)S(1)}, u32[]{:S(2)}, u32[]{:S(2)}) collective-permute-start(bf16[2,2,16,8192]{3,2,1,0:T(8,128)(2,1)S(1)} %get-tuple-element.38), channel_id=1, source_target_pairs={{0,2},{1,3},{2,0},{3,1},{4,6},{5,7},{6,4},{7,5},{8,10},{9,11},{10,... | collective-permute-start | bytes 3145736 | tf_op jit(solution)/shard_map/ppermute | solution.py:341
  46.2 51.7 %collective-permute-start.10 = (bf16[2,64,8192]{2,1,0:T(8,128)(2,1)}, bf16[2,64,8192]{2,1,0:T(8,128)(2,1)}, u32[]{:S(2)}, u32[]{:S(2)}) collective-permute-start(bf16[2,64,8192]{2,1,0:T(8,128)(2,1)} %pad_maximum_fusion.1.mine_in), channel_id=1, source_target_pairs={{0,4},{1,5},{2,6},{3,7},{12,8},{13,9},{14,10},{15,11},{16,20},{17,... | collective-permute-start | bytes 6291464 | tf_op jit(solution)/shard_map/ppermute | solution.py:341
  53.6 44.2 %collective-permute-start.11 = (bf16[2,64,8192]{2,1,0:T(8,128)(2,1)}, bf16[2,64,8192]{2,1,0:T(8,128)(2,1)}, u32[]{:S(2)}, u32[]{:S(2)}) collective-permute-start(bf16[2,64,8192]{2,1,0:T(8,128)(2,1)} %collective-permute-done.5.refs_4_), channel_id=1, source_target_pairs={{4,8},{5,9},{6,10},{7,11},{8,4},{9,5},{10,6},{11,7},{20,24},{21,25... | collective-permute-start | bytes 6291464 | tf_op jit(solution)/shard_map/ppermute | solution.py:341
  55.7 49.4 %collective-permute-start.7 = (bf16[2,64,8192]{2,1,0:T(8,128)(2,1)S(1)}, bf16[2,64,8192]{2,1,0:T(8,128)(2,1)}, u32[]{:S(2)}, u32[]{:S(2)}) collective-permute-start(bf16[2,64,8192]{2,1,0:T(8,128)(2,1)S(1)} %collective-permute-done.6.crossed_in.refs_8_), channel_id=1, source_target_pairs={{4,0},{5,1},{6,2},{7,3},{8,12},{9,13},{10,14},{11,15},{20,16},{21,... | collective-permute-start | bytes 6291464 | tf_op jit(solution)/shard_map/ppermute | solution.py:341
  67.4 49.3 %collective-permute-start.3 = (bf16[2,2,32,8192]{3,2,1,0:T(8,128)(2,1)}, bf16[2,2,32,8192]{3,2,1,0:T(8,128)(2,1)}, u32[]{:S(2)}, u32[]{:S(2)}) collective-permute-start(bf16[2,2,32,8192]{3,2,1,0:T(8,128)(2,1)} %get-tuple-element.39), channel_id=1, source_target_pairs={{0,2},{1,3},{2,0},{3,1},{4,6},{5,7},{6,4},{7,5},{8,10},{9,11},{10,... | collective-permute-start | bytes 6291464 | tf_op jit(solution)/shard_map/ppermute | solution.py:341
  110.4 29.2 %collective-permute-start.12 = (bf16[64,8192]{1,0:T(8,128)(2,1)S(1)}, bf16[64,8192]{1,0:T(8,128)(2,1)S(1)}, u32[]{:S(2)}, u32[]{:S(2)}) collective-permute-start(bf16[64,8192]{1,0:T(8,128)(2,1)S(1)} %get-tuple-element.43), channel_id=1, source_target_pairs={{0,4},{1,5},{2,6},{3,7},{4,0},{5,1},{6,2},{7,3},{8,12},{9,13},{10,... | collective-permute-start | bytes 3145736 | tf_op jit(solution)/shard_map/ppermute | solution.py:341
  116.0 23.6 %collective-permute-start.13 = (bf16[64,8192]{1,0:T(8,128)(2,1)S(1)}, bf16[64,8192]{1,0:T(8,128)(2,1)S(1)}, u32[]{:S(2)}, u32[]{:S(2)}) collective-permute-start(bf16[64,8192]{1,0:T(8,128)(2,1)S(1)} %get-tuple-element.44), channel_id=1, source_target_pairs={{4,8},{5,9},{6,10},{7,11},{8,4},{9,5},{10,6},{11,7},{20,24},{21,25... | collective-permute-start | bytes 3145736 | tf_op jit(solution)/shard_map/ppermute | solution.py:341
  118.2 22.4 %collective-permute-start.4 = (bf16[1,2,32,8192]{3,2,1,0:T(8,128)(2,1)S(1)}, bf16[1,2,32,8192]{3,2,1,0:T(8,128)(2,1)S(1)}, u32[]{:S(2)}, u32[]{:S(2)}) collective-permute-start(bf16[1,2,32,8192]{3,2,1,0:T(8,128)(2,1)S(1)} %slice.44), channel_id=1, source_target_pairs={{0,1},{1,0},{2,3},{3,2},{4,5},{5,4},{6,7},{7,6},{8,9},{9,8},{10,11... | collective-permute-start | bytes 3145736 | tf_op jit(solution)/shard_map/ppermute | solution.py:341
  118.3 43.8 %collective-permute-start.19 = (bf16[64,8192]{1,0:T(8,128)(2,1)S(1)}, bf16[64,8192]{1,0:T(8,128)(2,1)S(1)}, u32[]{:S(2)}, u32[]{:S(2)}) collective-permute-start(bf16[64,8192]{1,0:T(8,128)(2,1)S(1)} %get-tuple-element.54), channel_id=1, source_target_pairs={{0,4},{1,5},{2,6},{3,7},{12,8},{13,9},{14,10},{15,11},{16,20},{17,... | collective-permute-start | bytes 3145736 | tf_op jit(solution)/shard_map/ppermute | solution.py:341
  123.9 38.2 %collective-permute-start.20 = (bf16[64,8192]{1,0:T(8,128)(2,1)S(1)}, bf16[64,8192]{1,0:T(8,128)(2,1)S(1)}, u32[]{:S(2)}, u32[]{:S(2)}) collective-permute-start(bf16[64,8192]{1,0:T(8,128)(2,1)S(1)} %get-tuple-element.55), channel_id=1, source_target_pairs={{4,8},{5,9},{6,10},{7,11},{8,4},{9,5},{10,6},{11,7},{20,24},{21,25... | collective-permute-start | bytes 3145736 | tf_op jit(solution)/shard_map/ppermute | solution.py:341
  139.9 65.7 %collective-permute-start.17 = (bf16[64,8192]{1,0:T(8,128)(2,1)S(1)}, bf16[64,8192]{1,0:T(8,128)(2,1)S(1)}, u32[]{:S(2)}, u32[]{:S(2)}) collective-permute-start(bf16[64,8192]{1,0:T(8,128)(2,1)S(1)} %add_convert_fusion.3), channel_id=1, source_target_pairs={{4,8},{5,9},{6,10},{7,11},{8,4},{9,5},{10,6},{11,7},{20,24},{21,25... | collective-permute-start | bytes 3145736 | tf_op jit(solution)/shard_map/ppermute | solution.py:341
  150.1 55.6 %collective-permute-start.18 = (bf16[64,8192]{1,0:T(8,128)(2,1)S(1)}, bf16[64,8192]{1,0:T(8,128)(2,1)S(1)}, u32[]{:S(2)}, u32[]{:S(2)}) collective-permute-start(bf16[64,8192]{1,0:T(8,128)(2,1)S(1)} %add_convert_fusion.2), channel_id=1, source_target_pairs={{0,4},{1,5},{2,6},{3,7},{4,0},{5,1},{6,2},{7,3},{8,12},{9,13},{10,... | collective-permute-start | bytes 3145736 | tf_op jit(solution)/shard_map/ppermute | solution.py:341
  162.1 40.8 %collective-permute-start.15 = (bf16[2,64,8192]{2,1,0:T(8,128)(2,1)S(1)}, bf16[2,64,8192]{2,1,0:T(8,128)(2,1)S(1)}, u32[]{:S(2)}, u32[]{:S(2)}) collective-permute-start(bf16[2,64,8192]{2,1,0:T(8,128)(2,1)S(1)} %get-tuple-element.48), channel_id=1, source_target_pairs={{0,2},{1,3},{2,0},{3,1},{4,6},{5,7},{6,4},{7,5},{8,10},{9,11},{10,... | collective-permute-start | bytes 6291464 | tf_op jit(solution)/shard_map/ppermute | solution.py:341
  163.8 40.1 %collective-permute-start.21 = (bf16[64,8192]{1,0:T(8,128)(2,1)S(1)}, bf16[64,8192]{1,0:T(8,128)(2,1)S(1)}, u32[]{:S(2)}, u32[]{:S(2)}) collective-permute-start(bf16[64,8192]{1,0:T(8,128)(2,1)S(1)} %add_convert_fusion.1), channel_id=1, source_target_pairs={{4,8},{5,9},{6,10},{7,11},{8,4},{9,5},{10,6},{11,7},{20,24},{21,25... | collective-permute-start | bytes 3145736 | tf_op jit(solution)/shard_map/ppermute | solution.py:341
  165.0 39.4 %collective-permute-start.22 = (bf16[64,8192]{1,0:T(8,128)(2,1)S(1)}, bf16[64,8192]{1,0:T(8,128)(2,1)S(1)}, u32[]{:S(2)}, u32[]{:S(2)}) collective-permute-start(bf16[64,8192]{1,0:T(8,128)(2,1)S(1)} %add_convert_fusion), channel_id=1, source_target_pairs={{0,4},{1,5},{2,6},{3,7},{4,0},{5,1},{6,2},{7,3},{8,12},{9,13},{10,... | collective-permute-start | bytes 3145736 | tf_op jit(solution)/shard_map/ppermute | solution.py:341
  202.8 17.8 %collective-permute-start.14 = (bf16[64,8192]{1,0:T(8,128)(2,1)}, bf16[64,8192]{1,0:T(8,128)(2,1)}, u32[]{:S(2)}, u32[]{:S(2)}) collective-permute-start(bf16[64,8192]{1,0:T(8,128)(2,1)} %get-tuple-element.47), channel_id=1, source_target_pairs={{0,1},{1,0},{2,3},{3,2},{4,5},{5,4},{6,7},{7,6},{8,9},{9,8},{10,11... | collective-permute-start | bytes 3145736 | tf_op jit(solution)/shard_map/ppermute | solution.py:341
  204.0 16.7 %collective-permute-start.16 = (bf16[64,8192]{1,0:T(8,128)(2,1)}, bf16[64,8192]{1,0:T(8,128)(2,1)}, u32[]{:S(2)}, u32[]{:S(2)}) collective-permute-start(bf16[64,8192]{1,0:T(8,128)(2,1)} %slice_bitcast_fusion), channel_id=1, source_target_pairs={{0,1},{1,0},{2,3},{3,2},{4,5},{5,4},{6,7},{7,6},{8,9},{9,8},{10,11... | collective-permute-start | bytes 3145736 | tf_op jit(solution)/shard_map/ppermute | solution.py:341
  213.7 13.6 %collective-permute-start.26 = (f32[8,128]{1,0:T(8,128)S(1)}, f32[8,128]{1,0:T(8,128)S(1)}, u32[]{:S(2)}, u32[]{:S(2)}) collective-permute-start(f32[8,128]{1,0:T(8,128)S(1)} %add_add_fusion.1), channel_id=1, source_target_pairs={{0,4},{1,5},{2,6},{3,7},{4,0},{5,1},{6,2},{7,3},{8,12},{9,13},{10,... | collective-permute-start | bytes 12296 | tf_op jit(solution)/shard_map/ppermute | solution.py:341
  218.1 9.2 %collective-permute-start.27 = (f32[8,128]{1,0:T(8,128)S(1)}, f32[8,128]{1,0:T(8,128)S(1)}, u32[]{:S(2)}, u32[]{:S(2)}) collective-permute-start(f32[8,128]{1,0:T(8,128)S(1)} %add_add_fusion.1), channel_id=1, source_target_pairs={{0,8},{1,9},{2,10},{3,11},{4,12},{5,13},{6,14},{7,15},{8,0},{9,1},... | collective-permute-start | bytes 12296 | tf_op jit(solution)/shard_map/ppermute | solution.py:341
  218.6 8.7 %collective-permute-start.28 = (f32[8,128]{1,0:T(8,128)S(1)}, f32[8,128]{1,0:T(8,128)S(1)}, u32[]{:S(2)}, u32[]{:S(2)}) collective-permute-start(f32[8,128]{1,0:T(8,128)S(1)} %add_add_fusion.1), channel_id=1, source_target_pairs={{0,12},{1,13},{2,14},{3,15},{4,8},{5,9},{6,10},{7,11},{8,4},{9,5},... | collective-permute-start | bytes 12296 | tf_op jit(solution)/shard_map/ppermute | solution.py:341
  (29 other events, 324.6 us)

commit v8 on v7

--- a/solution.py
+++ b/solution.py
@@ -120,23 +120,18 @@
     tile = min(width, 2048)
 
     def body(place_ref, *refs):
-        rows = jnp.concatenate([ref[...].reshape(-1, tile) for ref in refs[:-1]], axis=0)
+        rows = jnp.concatenate([ref[...] for ref in refs[:-1]], axis=0)
         refs[-1][...] = dot32(place_ref[...], rows).astype(BF16)
 
     return pl.pallas_call(
         body,
         grid=(width // tile,),
         in_specs=[pl.BlockSpec(place.shape, lambda i: (0, 0))]
-        + [
-            pl.BlockSpec((b.shape[0], tile), lambda i: (0, i))
-            if b.ndim == 2
-            else pl.BlockSpec((1, b.shape[1], tile), lambda i: (0, 0, i))
-            for b in blocks
-        ],
+        + [pl.BlockSpec((b.shape[0], tile), lambda i: (0, i)) for b in blocks],
         out_specs=pl.BlockSpec((tokens, tile), lambda i: (0, i)),
         out_shape=jax.ShapeDtypeStruct((tokens, width), BF16),
         compiler_params=kernel_params(),
-    )(place, *blocks)
+    )(place, *in_hbm(blocks[0]), *blocks[1:])
 
 
 def corner(rows, first_rows, columns, first_columns):
@@ -144,113 +139,79 @@
     return upper == (lax.broadcasted_iota(jnp.int32, (rows, columns), 1) < first_columns)
 
 
-def held_copies(source, held, sems, tile):
-    return [
-        pltpu.make_async_copy(source.at[:, :, pl.ds(i * tile, tile)], held.at[:, :, pl.ds(i * tile, tile)], sems.at[i])
-        for i in range(held.shape[2] // tile)
-    ]
-
-
-def far_end(mine, handed, far):
-    _, block, width = mine.shape
-    rank = far.shape[1]
+def far_group(is_end, rows, factors, handed=None):
+    _, block, width = rows[0].shape
+    rank = factors[0].shape[1]
     tile = min(width, 2048)
     tiles = width // tile
-
-    def body(mine_in, handed_in, far_in, up_ref, down_ref, dx_ref, handed_dx_ref, held, left, sems):
+    total = block if handed is None else 2 * block
+
+    def body(end_ref, *refs):
+        rows_in, refs = refs[:len(rows)], refs[len(rows):]
+        factors_in, refs = refs[:len(factors)], refs[len(factors):]
+        handed_in, refs = (None, refs) if handed is None else (refs[0], refs[1:])
+        (up_ref, down_ref, dx_ref), (held, left, sems) = refs[:3], refs[-3:]
         step = pl.program_id(0)
-
-        def rows(k, cut):
-            return jnp.concatenate([held[k, :, cut], handed_in[k, :, cut]], axis=0)
+        at_end = end_ref[0] == 1
+
+        def copy(source, i):
+            cut = pl.ds(i * tile, tile)
+            return pltpu.make_async_copy(source.at[:, :, cut], held.at[:, :, cut], sems.at[i])
+
+        def tokens(k, cut):
+            own = held[k, :, cut]
+            return own if handed is None else jnp.concatenate([own, handed_in[k, :, cut]], axis=0)
+
+        def factor(k, cut):
+            first = factors_in[0][k, :, cut]
+            return first if len(factors) == 1 else jnp.where(at_end, factors_in[1][k, :, cut], first)
 
         @pl.when(step == 0)
         def _():
-            copies = held_copies(mine_in, held, sems, tile)
-            for c in copies:
-                c.start()
-            sums = [jnp.zeros((rank, 2 * block), F32)] * 2
-            for i, c in enumerate(copies):
-                c.wait()
+            for n, source in enumerate(rows_in):
+                chosen = at_end == (n == 1) if len(rows) == 2 else step == 0
+
+                @pl.when(chosen)
+                def _(source=source):
+                    for i in range(tiles):
+                        copy(source, i).start()
+
+            sums = [jnp.zeros((rank, total), F32)] * 2
+            for i in range(tiles):
+                copy(rows_in[0], i).wait()
                 cut = pl.ds(i * tile, tile)
                 for k in range(2):
-                    sums[k] += dot32(far_in[k, :, cut], rows(k, cut), ROWS_OF)
+                    sums[k] += dot32(factor(k, cut), tokens(k, cut), ROWS_OF)
             for k in range(2):
                 left[k] = sums[k].astype(BF16)
 
         cut = pl.ds(pl.multiple_of(step * tile, tile), tile)
-        up_ref[...] = dot32(left[0], rows(1, cut)).astype(BF16)
-        down_ref[...] = dot32(left[1], rows(0, cut)).astype(BF16)
-        dx = dot32(left[1], far_in[0, :, cut], OUTER).astype(BF16)
+        up_ref[...] = dot32(left[0], tokens(1, cut)).astype(BF16)
+        down = dot32(left[1], tokens(0, cut)).astype(BF16)
+        down_ref[...] = down
+        dx = dot32(left[1], factor(0, cut), OUTER).astype(BF16)
         dx_ref[...] = dx[:block]
-        handed_dx_ref[...] = dx[block:]
-
-    def wide(rows):
-        return pl.BlockSpec((rows, tile), lambda i: (0, i))
-
-    sizes = (rank, rank, block, block)
+        if handed is not None:
+            refs[3][...] = jnp.where(at_end, down, dx[block:])
+
+    outs = 3 if handed is None else 4
+    more = () if handed is None else (handed,)
     return pl.pallas_call(
         body,
         grid=(tiles,),
-        in_specs=[HBM] + [WHOLE] * 2,
-        out_specs=[wide(n) for n in sizes],
-        out_shape=[jax.ShapeDtypeStruct((n, width), BF16) for n in sizes],
+        in_specs=[pl.BlockSpec(memory_space=pltpu.SMEM)] + [HBM] * len(rows) + [WHOLE] * (len(factors) + len(more)),
+        out_specs=[pl.BlockSpec((rank, tile), lambda i: (0, i))] * outs,
+        out_shape=[jax.ShapeDtypeStruct((rank, width), BF16)] * outs,
         scratch_shapes=[
             pltpu.VMEM((2, block, width), BF16),
-            pltpu.VMEM((2, rank, 2 * block), BF16),
+            pltpu.VMEM((2, rank, total), BF16),
             pltpu.SemaphoreType.DMA((tiles,)),
         ],
         compiler_params=kernel_params(),
-    )(*in_hbm(mine), *in_vmem(handed, far))
-
-
-def far_mid(is_end, mine, outer, crossed, handed_dx):
-    _, block, width = mine.shape
-    rank = outer.shape[1]
-    tile = min(width, 2048)
-    tiles = width // tile
-
-    def body(end_ref, mine_in, outer_in, crossed_in, handed_ref, up_ref, down_ref, swap_ref, inner_ref, held, left, sems):
-        step = pl.program_id(0)
-
-        @pl.when(step == 0)
-        def _():
-            copies = held_copies(mine_in, held, sems, tile)
-            for c in copies:
-                c.start()
-            sums = [jnp.zeros((rank, block), F32)] * 2
-            for i, c in enumerate(copies):
-                c.wait()
-                cut = pl.ds(i * tile, tile)
-                for k in range(2):
-                    factors = jnp.where(end_ref[0] == 1, outer_in[k, :, cut], crossed_in[k, :, cut])
-                    sums[k] += dot32(factors, held[k, :, cut], ROWS_OF)
-            for k in range(2):
-                left[k] = sums[k].astype(BF16)
-            inner_ref[...] = sums[1].T.astype(BF16)
-
-        cut = pl.ds(pl.multiple_of(step * tile, tile), tile)
-        up_ref[...] = dot32(left[0], held[1, :, cut]).astype(BF16)
-        down = dot32(left[1], held[0, :, cut]).astype(BF16)
-        down_ref[...] = down
-        swap_ref[...] = jnp.where(end_ref[0] == 1, down, handed_ref[...])
-
-    wide = pl.BlockSpec((rank, tile), lambda i: (0, i))
-    return pl.pallas_call(
-        body,
-        grid=(tiles,),
-        in_specs=[pl.BlockSpec(memory_space=pltpu.SMEM), HBM, WHOLE, WHOLE, pl.BlockSpec((block, tile), lambda i: (0, i))],
-        out_specs=[wide] * 3 + [pl.BlockSpec((block, rank), lambda i: (0, 0))],
-        out_shape=[jax.ShapeDtypeStruct((rank, width), BF16)] * 3 + [jax.ShapeDtypeStruct((block, rank), BF16)],
-        scratch_shapes=[
-            pltpu.VMEM((2, block, width), BF16),
-            pltpu.VMEM((2, rank, block), BF16),
-            pltpu.SemaphoreType.DMA((tiles,)),
-        ],
-        compiler_params=kernel_params(),
-    )(is_end, *in_hbm(mine), *in_vmem(outer, crossed), handed_dx)
-
-
-def near_groups(is_end, stage, pair, down, up, outer, crossed, inner2, dx3, swapped, capacity, first1):
+    )(is_end, *in_hbm(*rows), *in_vmem(*factors, *more))
+
+
+def near_groups(is_end, stage, pair, down, up, dx_late, dx_early, swapped, capacity, first1):
     plane = len(stage)
     rank, width = down.shape
     block = plane * capacity
@@ -259,9 +220,9 @@
 
     def body(end_ref, *refs):
         stage_in, refs = refs[:plane], refs[plane:]
-        pair_in, down_in, up_in, outer_in, crossed_in, inner2, dx3, swapped = refs[:8]
-        dx_refs, sum_refs = [refs[8], refs[9], refs[10].at[0], refs[10].at[1]], refs[11:15]
-        left, inners = refs[15:]
+        pair_in, down_in, up_in, late_ref, early_ref, swapped_ref = refs[:6]
+        dx_refs, sum_refs = refs[6:10], refs[10:14]
+        (left,) = refs[14:]
         step = pl.program_id(0)
         own_in = (down_in, up_in)
         is_mine = corner(2 * block, block, 2 * rank, rank)
@@ -286,18 +247,16 @@
                     sums[k] += dot32(rows(k, cut), both, ROWS_OF)
             for k in range(2):
                 left[k] = jnp.where(is_mine, sums[k], 0.0).astype(BF16)
-            first = jnp.concatenate([inner2[...], jnp.zeros((block, 2 * rank), BF16)], axis=1)
-            inners[...] = jnp.concatenate([first, jnp.concatenate([jnp.zeros((2 * block, rank), BF16), left[1]], axis=1)])
 
         cut = pl.ds(pl.multiple_of(step * tile, tile), tile)
         for k in range(2):
             both = dot32(left[k], rows(1 - k, cut), OUTER)
             sum_refs[k][...] = both[:rank]
             sum_refs[2 + k][...] = both[rank:]
-        near = jnp.where(end_ref[0] == 1, outer_in[0, :, cut], crossed_in[0, :, cut])
-        downs = jnp.concatenate([near, pair_in[0, :, cut], down_in[:, cut]], axis=0)
-        dx = dot32(inners[...], downs).astype(BF16)
-        moved = [jnp.where(end_ref[0] == 1, swapped[...], dx3[...])] + [dx[n * block:(n + 1) * block] for n in range(3)]
+        downs = jnp.concatenate([pair_in[0, :, cut], down_in[:, cut]], axis=0)
+        dx = dot32(left[1], downs).astype(BF16)
+        at_end, late = end_ref[0] == 1, late_ref[...]
+        moved = [jnp.where(at_end, swapped_ref[...], late), jnp.where(at_end, late, early_ref[...]), dx[:block], dx[block:]]
         for n, dx in enumerate(moved):
             for m in range(plane):
                 dx_refs[m][n * capacity:(n + 1) * capacity] = dx[m * capacity:(m + 1) * capacity]
@@ -306,18 +265,15 @@
         body,
         grid=(tiles,),
         in_specs=[pl.BlockSpec(memory_space=pltpu.SMEM)]
-        + [WHOLE] * (plane + 5)
-        + [pl.BlockSpec(inner2.shape, lambda i: (0, 0))]
-        + [pl.BlockSpec((block, tile), lambda i: (0, i))] * 2,
-        out_specs=[pl.BlockSpec((4 * capacity, tile), lambda i: (0, i))] * 2
-        + [pl.BlockSpec((2, 4 * capacity, tile), lambda i: (0, 0, i))]
+        + [WHOLE] * (plane + 3)
+        + [pl.BlockSpec((block, tile), lambda i: (0, i))] * 3,
+        out_specs=[pl.BlockSpec((4 * capacity, tile), lambda i: (0, i))] * plane
         + [pl.BlockSpec((rank, tile), lambda i: (0, i))] * 4,
-        out_shape=[jax.ShapeDtypeStruct((4 * capacity, width), BF16)] * 2
-        + [jax.ShapeDtypeStruct((2, 4 * capacity, width), BF16)]
+        out_shape=[jax.ShapeDtypeStruct((4 * capacity, width), BF16)] * plane
         + [jax.ShapeDtypeStruct((rank, width), F32)] * 4,
-        scratch_shapes=[pltpu.VMEM((2, 2 * block, 2 * rank), BF16), pltpu.VMEM((3 * block, 3 * rank), BF16)],
+        scratch_shapes=[pltpu.VMEM((2, 2 * block, 2 * rank), BF16)],
         compiler_params=kernel_params(),
-    )(is_end, *in_vmem(*stage, pair, down, up, outer, crossed), inner2, dx3, swapped)
+    )(is_end, *in_vmem(*stage, pair, down, up), dx_late, dx_early, swapped)
 
 
 def move_adapters(plane, acts, cotan, token_task_index, task_slot_lookup, pool_down_factors, pool_up_factors):
@@ -351,7 +307,7 @@
         along = [[(i, (i // plane ^ m) * plane + i % plane) for i in range(ndevices)] for m in range(1, 4)]
         term = jnp.broadcast_to(term, (8, 128))
         term = term + sum(send(term, pairs) for pairs in around)
-        term = after(term, dx_across)
+        term = after(term, dx_across[1])
         return (term + sum(after([send(term, pairs) for pairs in along], grad_acts)))[0, 0]
 
     down, up = pool_down_factors[0], pool_up_factors[0]
@@ -400,14 +356,15 @@
     outer = send(crossed, outward)
     far = send(pair, cross)
 
-    up3, down3, dx3, handed_dx = far_end(rows3, handed, far)
-    down3, up3 = send(down3, cross), send(up3, cross)
-    up2, down2, swapped, inner2 = far_mid(end_flag, rows2, outer, crossed, handed_dx)
-    swapped, up2_in = send(swapped, swap), send(up2, inward)
+    up2, down2, dx_early = far_group(end_flag, (rows2,), (crossed,))
+    rows3, rows2 = after((rows3, rows2), dx_early)
+    up3, down3, dx_late, swapped = far_group(end_flag, (rows3, rows2), (far, outer), handed)
+    up2_in = send(up3, inward)
+    down3, swapped, up3 = send(down3, cross), send(swapped, swap), send(up3, cross)
 
     swapped, down3 = lax.optimization_barrier((swapped, down3))
-    dx_own, dx_beside, dx_across, up1, down1, up0, down0 = near_groups(
-        end_flag, stage10, pair, down, up, outer, crossed, inner2, dx3, swapped, capacity,
+    dx_own, dx_beside, *dx_across, up1, down1, up0, down0 = near_groups(
+        end_flag, stage10, pair, down, up, dx_late, dx_early, swapped, capacity,
         (2 * capacity, 2 * capacity, 0, 0),
     )
 
@@ -415,12 +372,12 @@
         return (a.astype(F32) + b.astype(F32)).astype(BF16)
 
     down2, down1 = add(down2, swapped), add(down1, down3)
-    up2_in, up3 = after((up2_in, up3), down2, down1)
+    dx_across = [send(block, beside(2)) for block in dx_across]
+    up2_in, up3 = after((up2_in, up3), down2, down1, dx_across[0])
     down2, down1 = send(down2, cross), send(down1, swap)
     up2, up1 = send(add(up2, up2_in), cross), send(add(up1, up3), swap)
 
-    dx_across = send(dx_across, beside(2))
-    back = [dx_own, send(dx_beside, beside(1)), dx_across, send(dx_across[1], beside(1))]
+    back = [dx_own, send(dx_beside, beside(1)), dx_across[0], send(dx_across[1], beside(1))]
     grad_acts = unpack(place_back.T, back, tokens)
     raw_up = up0 + up2.astype(F32) + up1.astype(F32)
     raw_down = down0 + down2.astype(F32) + down1.astype(F32)

time: 232 us -> 227 us (0.978)
  local copies, waits for them, and re-layouts: 14.4 us -> 9.04 us
  waiting for transfers between devices: 111 us -> 114 us
    ppermute x29 -> x30, waiting for transfers between devices: 111 us -> 114 us  [send(): return lax.ppermute(array, 'dp', pairs)]
    unnamed x49 -> x43, local copies, waits for them, and re-layouts: 7.37 us -> 5.46 us
    ppermute x29 -> x30, starting transfers between devices: 58.7 us -> 57.9 us  [send(): return lax.ppermute(array, 'dp', pairs)]
  transfers between devices with their start and end apart: 29 -> 30, of which waited for: 10 -> 13; matrix products, arithmetic and copies ran while one was open for 6% -> 5% of each run, Pallas kernels for 14% -> 14%
where the time goes in v8:
time: 227 us
  waiting for transfers between devices  114 us (50%)
  starting transfers between devices  57.9 us (26%)
  Pallas kernels  31.4 us (14%)
  other arithmetic  11.4 us (5%)
  local copies, waits for them, and re-layouts  9.04 us (4%)
  between operations  3.09 us (1%)
    ppermute x30, waiting for transfers between devices, send(): return lax.ppermute(array, 'dp', pairs)  114 us
    ppermute x30, starting transfers between devices, send(): return lax.ppermute(array, 'dp', pairs)  57.9 us
    pallas_call x2, Pallas kernels, far_group(): pl.pallas_call(body, grid=(tiles,), in_specs=[pl.BlockSpec(memory_space=p...  13 us
    pallas_call x1, Pallas kernels, near_groups(): pl.pallas_call(body, grid=(tiles,), in_specs=[pl.BlockSpec(memory_space=p...  6.88 us
    pallas_call x1, Pallas kernels, pack(): pl.pallas_call(body, grid=(tiles,), in_specs=[pl.BlockSpec(place.shape, l...  6.36 us
    unnamed x43, local copies, waits for them, and re-layouts  5.46 us
    pallas_call x1, Pallas kernels, unpack(): pl.pallas_call(body, grid=(width // tile,), in_specs=[pl.BlockSpec(place....  5.23 us
  transfers between devices with their start and end apart: 30, of which 13 were waited for; matrix products, arithmetic and copies ran while one was open for 5% of the time, Pallas kernels for 14%

profile of v8, /device:TPU:0, one launch (start us, length us, event | category | flops | bytes accessed | tf_op | source)
XLA Modules:
  0.0 226.7 jit_solution(7398332082023504493)
XLA Ops:
  4.2 4.6 %collective-permute-start.5 = (bf16[2,64,8192]{2,1,0:T(8,128)(2,1)S(1)}, bf16[2,64,8192]{2,1,0:T(8,128)(2,1)}, u32[]{:S(2)}, u32[]{:S(2)}) collective-permute-start(bf16[2,64,8192]{2,1,0:T(8,128)(2,1)S(1)} %constant_dynamic-update-slice_fusion), channel_id=1, source_target_pairs={{0,4},{1,5},{2,6},{3,7},{4,0},{5,1},{6,2},{7,3},{8,12},{9,13},{10,... | collective-permute-start | bytes 6291464 | tf_op jit(solution)/shard_map/ppermute | solution.py:297
  9.5 6.4 %shard_map.85 = (bf16[1,2,64,8192]{3,2,1,0:T(8,128)(2,1)S(1)}, bf16[1,2,64,8192]{3,2,1,0:T(8,128)(2,1)S(1)}, bf16[2,2,16,8192]{3,2,1,0:T(8,128)(2,1)S(1)}, bf16[...) custom-call(bf16[256,128]{1,0:T(8,128)(2,1)S(1)} %fusion.1.place_ref, bf16[128,8192]{1,0:T(8,128)(2,1)} %x_in.1, ...), custom_call_target="tpu_custom_call" | custom-call | tf_op jit(solution)/shard_map/pallas_call | solution.py:107
  18.4 21.9 %collective-permute-done.1 = bf16[2,2,16,8192]{3,2,1,0:T(8,128)(2,1)S(1)} collective-permute-done((bf16[2,2,16,8192]{3,2,1,0:T(8,128)(2,1)S(1)}, bf16[2,2,16,8192]{3,2,1,0:T(8,128)(2,1)S(1)}, u32[]{:S(2)}, u32[]{:S(2)}) %collective-permute-start.1) | collective-permute-done | bytes 1048608 | tf_op jit(solution)/shard_map/ppermute | solution.py:297
  45.7 3.6 %collective-permute-start.11 = (bf16[2,64,8192]{2,1,0:T(8,128)(2,1)}, bf16[2,64,8192]{2,1,0:T(8,128)(2,1)}, u32[]{:S(2)}, u32[]{:S(2)}) collective-permute-start(bf16[2,64,8192]{2,1,0:T(8,128)(2,1)} %pad_maximum_fusion.refs_0_), channel_id=1, source_target_pairs={{0,4},{1,5},{2,6},{3,7},{12,8},{13,9},{14,10},{15,11},{16,20},{17,... | collective-permute-start | bytes 6291464 | tf_op jit(solution)/shard_map/ppermute | solution.py:297
  50.7 4.2 %collective-permute-done.5.refs_4_ = bf16[2,64,8192]{2,1,0:T(8,128)(2,1)} collective-permute-done((bf16[2,64,8192]{2,1,0:T(8,128)(2,1)S(1)}, bf16[2,64,8192]{2,1,0:T(8,128)(2,1)}, u32[]{:S(2)}, u32[]{:S(2)}) %collective-permute-start.5) | collective-permute-done | bytes 2097184 | tf_op jit(solution)/shard_map/ppermute | solution.py:297
  56.9 6.9 %collective-permute-done.2 = bf16[2,2,16,8192]{3,2,1,0:T(8,128)(2,1)S(1)} collective-permute-done((bf16[2,2,16,8192]{3,2,1,0:T(8,128)(2,1)S(1)}, bf16[2,2,16,8192]{3,2,1,0:T(8,128)(2,1)S(1)}, u32[]{:S(2)}, u32[]{:S(2)}) %collective-permute-start.2) | collective-permute-done | bytes 1048608 | tf_op jit(solution)/shard_map/ppermute | solution.py:297
  67.2 3.0 %pad_maximum_fusion.1.refs_0_.refs_1_ = bf16[2,64,8192]{2,1,0:T(8,128)(2,1)} fusion(bf16[2,16,8192]{2,1,0:T(8,128)(2,1)} %bitcast.11, bf16[2,16,8192]{2,1,0:T(8,128)(2,1)} %get-tuple-element.74, bf16[2,16,8192]{2,1,0:T(8,128)(2,1)} %get-tuple-element.72, bf16[2,16,8192]{2,1,0:T(8,128)(2,1)} %get-tuple-element.70), kind=kLoop, calls=%fused_computation.1 | loop fusion | flops 8388608 | bytes 4194304 | tf_op jit(solution)/shard_map/concatenate | solution.py:354
  70.1 5.2 %shard_map.86 = (bf16[64,8192]{1,0:T(8,128)(2,1)S(1)}, bf16[64,8192]{1,0:T(8,128)(2,1)S(1)}, bf16[64,8192]{1,0:T(8,128)(2,1)S(1)}) custom-call(s32[1]{0:T(128)} %bitcast.1.end_ref, bf16[2,64,8192]{2,1,0:T(8,128)(2,1)} %pad_maximum_fusion.1.refs_0_.refs_1_, bf16[2,64,8192]{2,1,0:T(8,128)(2,1)} %collective-permute-done.8.refs_1_), custom_call_target="tpu_custom_call" | custom-call | tf_op jit(solution)/shard_map/pallas_call | solution.py:199
  75.3 23.2 %collective-permute-done.11.refs_4_ = bf16[2,64,8192]{2,1,0:T(8,128)(2,1)} collective-permute-done((bf16[2,64,8192]{2,1,0:T(8,128)(2,1)}, bf16[2,64,8192]{2,1,0:T(8,128)(2,1)}, u32[]{:S(2)}, u32[]{:S(2)}) %collective-permute-start.11) | collective-permute-done | bytes 2097184 | tf_op jit(solution)/shard_map/ppermute | solution.py:297
  98.5 2.5 %collective-permute-done.10.refs_3_ = bf16[2,64,8192]{2,1,0:T(8,128)(2,1)} collective-permute-done((bf16[2,64,8192]{2,1,0:T(8,128)(2,1)}, bf16[2,64,8192]{2,1,0:T(8,128)(2,1)}, u32[]{:S(2)}, u32[]{:S(2)}) %collective-permute-start.10) | collective-permute-done | bytes 2097184 | tf_op jit(solution)/shard_map/ppermute | solution.py:297
  101.0 7.8 %shard_map.87 = (bf16[64,8192]{1,0:T(8,128)(2,1)S(1)}, bf16[64,8192]{1,0:T(8,128)(2,1)S(1)}, bf16[64,8192]{1,0:T(8,128)(2,1)S(1)}, bf16[64,8192]{1,0:T(8,128)(2,1)S(1)}) custom-call(s32[1]{0:T(128)} %bitcast.1.end_ref, bf16[2,64,8192]{2,1,0:T(8,128)(2,1)} %pad_maximum_fusion.refs_0_, bf16[2,64,8192]{2,1,0:T(8,128)(2,1)} %pad_maximum_fusion.1.refs_0_.refs_1_, ...), custom_call_target="tpu_custom_call" | custom-call | tf_op jit(solution)/shard_map/pallas_call | solution.py:199
  108.8 5.0 %collective-permute-start.12 = (bf16[64,8192]{1,0:T(8,128)(2,1)S(1)}, bf16[64,8192]{1,0:T(8,128)(2,1)S(1)}, u32[]{:S(2)}, u32[]{:S(2)}) collective-permute-start(bf16[64,8192]{1,0:T(8,128)(2,1)S(1)} %get-tuple-element.46), channel_id=1, source_target_pairs={{0,4},{1,5},{2,6},{3,7},{4,0},{5,1},{6,2},{7,3},{8,12},{9,13},{10,... | collective-permute-start | bytes 3145736 | tf_op jit(solution)/shard_map/ppermute | solution.py:297
  114.5 4.8 %collective-permute-start.20 = (bf16[64,8192]{1,0:T(8,128)(2,1)S(1)}, bf16[64,8192]{1,0:T(8,128)(2,1)S(1)}, u32[]{:S(2)}, u32[]{:S(2)}) collective-permute-start(bf16[64,8192]{1,0:T(8,128)(2,1)S(1)} %get-tuple-element.59), channel_id=1, source_target_pairs={{0,4},{1,5},{2,6},{3,7},{12,8},{13,9},{14,10},{15,11},{16,20},{17,... | collective-permute-start | bytes 3145736 | tf_op jit(solution)/shard_map/ppermute | solution.py:297
  120.3 17.2 %collective-permute-done.12.refs_9_ = bf16[64,8192]{1,0:T(8,128)(2,1)S(1)} collective-permute-done((bf16[64,8192]{1,0:T(8,128)(2,1)S(1)}, bf16[64,8192]{1,0:T(8,128)(2,1)S(1)}, u32[]{:S(2)}, u32[]{:S(2)}) %collective-permute-start.12) | collective-permute-done | bytes 1048608 | tf_op jit(solution)/shard_map/ppermute | solution.py:297
  139.3 6.9 %shard_map.88 = (bf16[64,8192]{1,0:T(8,128)(2,1)S(1)}, bf16[64,8192]{1,0:T(8,128)(2,1)}, bf16[64,8192]{1,0:T(8,128)(2,1)S(1)}, bf16[64,8192]{1,0:T(8,128)(2,1)S(...) custom-call(s32[1]{0:T(128)} %bitcast.1.end_ref, ...), custom_call_target="tpu_custom_call" | custom-call | tf_op jit(solution)/shard_map/pallas_call | solution.py:264
  148.7 7.2 %collective-permute-start.19 = (bf16[64,8192]{1,0:T(8,128)(2,1)S(1)}, bf16[64,8192]{1,0:T(8,128)(2,1)S(1)}, u32[]{:S(2)}, u32[]{:S(2)}) collective-permute-start(bf16[64,8192]{1,0:T(8,128)(2,1)S(1)} %add_convert_fusion.2), channel_id=1, source_target_pairs={{0,4},{1,5},{2,6},{3,7},{4,0},{5,1},{6,2},{7,3},{8,12},{9,13},{10,... | collective-permute-start | bytes 3145736 | tf_op jit(solution)/shard_map/ppermute | solution.py:297
  155.9 4.0 %collective-permute-done.20 = bf16[64,8192]{1,0:T(8,128)(2,1)S(1)} collective-permute-done((bf16[64,8192]{1,0:T(8,128)(2,1)S(1)}, bf16[64,8192]{1,0:T(8,128)(2,1)S(1)}, u32[]{:S(2)}, u32[]{:S(2)}) %collective-permute-start.20) | collective-permute-done | bytes 1048608 | tf_op jit(solution)/shard_map/ppermute | solution.py:297
  161.4 10.9 %collective-permute-done.15.refs_2_ = bf16[64,8192]{1,0:T(8,128)(2,1)S(1)} collective-permute-done((bf16[64,8192]{1,0:T(8,128)(2,1)S(1)}, bf16[64,8192]{1,0:T(8,128)(2,1)S(1)}, u32[]{:S(2)}, u32[]{:S(2)}) %collective-permute-start.15) | collective-permute-done | bytes 1048608 | tf_op jit(solution)/shard_map/ppermute | solution.py:297
  173.7 7.2 %collective-permute-start.23 = (bf16[64,8192]{1,0:T(8,128)(2,1)S(1)}, bf16[64,8192]{1,0:T(8,128)(2,1)S(1)}, u32[]{:S(2)}, u32[]{:S(2)}) collective-permute-start(bf16[64,8192]{1,0:T(8,128)(2,1)S(1)} %add_convert_fusion), channel_id=1, source_target_pairs={{0,4},{1,5},{2,6},{3,7},{4,0},{5,1},{6,2},{7,3},{8,12},{9,13},{10,... | collective-permute-start | bytes 3145736 | tf_op jit(solution)/shard_map/ppermute | solution.py:297
  181.0 7.6 %collective-permute-done.16 = bf16[64,8192]{1,0:T(8,128)(2,1)} collective-permute-done((bf16[64,8192]{1,0:T(8,128)(2,1)S(1)}, bf16[64,8192]{1,0:T(8,128)(2,1)}, u32[]{:S(2)}, u32[]{:S(2)}) %collective-permute-start.16) | collective-permute-done | bytes 1048608 | tf_op jit(solution)/shard_map/ppermute | solution.py:297
  189.7 11.9 %collective-permute-done.23 = bf16[64,8192]{1,0:T(8,128)(2,1)S(1)} collective-permute-done((bf16[64,8192]{1,0:T(8,128)(2,1)S(1)}, bf16[64,8192]{1,0:T(8,128)(2,1)S(1)}, u32[]{:S(2)}, u32[]{:S(2)}) %collective-permute-start.23) | collective-permute-done | bytes 1048608 | tf_op jit(solution)/shard_map/ppermute | solution.py:297
  209.7 4.8 %collective-permute-start.27 = (f32[8,128]{1,0:T(8,128)S(1)}, f32[8,128]{1,0:T(8,128)S(1)}, u32[]{:S(2)}, u32[]{:S(2)}) collective-permute-start(f32[8,128]{1,0:T(8,128)S(1)} %add_add_fusion.1), channel_id=1, source_target_pairs={{0,4},{1,5},{2,6},{3,7},{4,0},{5,1},{6,2},{7,3},{8,12},{9,13},{10,... | collective-permute-start | bytes 12296 | tf_op jit(solution)/shard_map/ppermute | solution.py:297
  217.3 5.2 %shard_map.89 = bf16[128,8192]{1,0:T(8,128)(2,1)} custom-call(bf16[128,256]{1,0:T(8,128)(2,1)S(1)} %fusion.place_ref, bf16[64,8192]{1,0:T(8,128)(2,1)} %copy-done.10, bf16[64,8192]{1,0:T(8,128)(2,1)} %collective-permute-done.14.refs_1_, bf16[64,8192]{1,0:T(8,128)(2,1)S(1)} %collective-permute-done.15.refs_2_, bf16[64,8192]{1,0:T(8,128)(2,1)} %collective-permute-done.17.refs_3_), custom_call_target="tpu_custom_call" | custom-call | tf_op jit(solution)/shard_map/pallas_call | solution.py:126
  223.9 2.8 %multiply_bitcast_fusion = (f32[1,64,8192]{2,1,0:T(8,128)}, f32[1,64,8192]{2,1,0:T(8,128)}) fusion(f32[]{:T(128)} %bitcast.12, bf16[64,8192]{1,0:T(8,128)(2,1)S(1)} %copy-done.18, f32[64,8192]{1,0:T(8,128)S(1)} %get-tuple-element.57, bf16[64,8192]{1,0:T(8,128)(2,1)S(1)} %copy-done.16, bf16[64,8192]{1,0:T(8,128)(2,1)S(1)} %copy-done.14, ...), kind=kLoop, calls=%fused_computation.2 | loop fusion | flops 5242880 | bytes 12582916 | tf_op jit(solution)/shard_map/broadcast_in_dim | solution.py:37
  (111 shorter events, 38.8 us)
Async XLA Ops:
  2.2 47.1 %collective-permute-start.8 = (bf16[2,64,8192]{2,1,0:T(8,128)(2,1)S(1)}, bf16[2,64,8192]{2,1,0:T(8,128)(2,1)}, u32[]{:S(2)}, u32[]{:S(2)}) collective-permute-start(bf16[2,64,8192]{2,1,0:T(8,128)(2,1)S(1)} %constant_dynamic-update-slice_fusion), channel_id=1, source_target_pairs={{4,8},{5,9},{6,10},{7,11},{8,4},{9,5},{10,6},{11,7},{20,24},{21,25... | collective-permute-start | bytes 6291464 | tf_op jit(solution)/shard_map/ppermute | solution.py:297
  4.2 50.7 %collective-permute-start.5 = (bf16[2,64,8192]{2,1,0:T(8,128)(2,1)S(1)}, bf16[2,64,8192]{2,1,0:T(8,128)(2,1)}, u32[]{:S(2)}, u32[]{:S(2)}) collective-permute-start(bf16[2,64,8192]{2,1,0:T(8,128)(2,1)S(1)} %constant_dynamic-update-slice_fusion), channel_id=1, source_target_pairs={{0,4},{1,5},{2,6},{3,7},{4,0},{5,1},{6,2},{7,3},{8,12},{9,13},{10,... | collective-permute-start | bytes 6291464 | tf_op jit(solution)/shard_map/ppermute | solution.py:297
  15.9 24.4 %collective-permute-start.1 = (bf16[2,2,16,8192]{3,2,1,0:T(8,128)(2,1)S(1)}, bf16[2,2,16,8192]{3,2,1,0:T(8,128)(2,1)S(1)}, u32[]{:S(2)}, u32[]{:S(2)}) collective-permute-start(bf16[2,2,16,8192]{3,2,1,0:T(8,128)(2,1)S(1)} %get-tuple-element.39), channel_id=1, source_target_pairs={{0,2},{1,3},{2,0},{3,1},{4,6},{5,7},{6,4},{7,5},{8,10},{9,11},{10,... | collective-permute-start | bytes 3145736 | tf_op jit(solution)/shard_map/ppermute | solution.py:297
  17.5 24.5 %collective-permute-start = (bf16[1,2,64,8192]{3,2,1,0:T(8,128)(2,1)S(1)}, bf16[1,2,64,8192]{3,2,1,0:T(8,128)(2,1)S(1)}, u32[]{:S(2)}, u32[]{:S(2)}) collective-permute-start(bf16[1,2,64,8192]{3,2,1,0:T(8,128)(2,1)S(1)} %get-tuple-element.36), channel_id=1, source_target_pairs={{0,1},{1,0},{2,3},{3,2},{4,5},{5,4},{6,7},{7,6},{8,9},{9,8},{10,11... | collective-permute-start | bytes 6291464 | tf_op jit(solution)/shard_map/ppermute | solution.py:297
  40.3 23.5 %collective-permute-start.2 = (bf16[2,2,16,8192]{3,2,1,0:T(8,128)(2,1)S(1)}, bf16[2,2,16,8192]{3,2,1,0:T(8,128)(2,1)S(1)}, u32[]{:S(2)}, u32[]{:S(2)}) collective-permute-start(bf16[2,2,16,8192]{3,2,1,0:T(8,128)(2,1)S(1)} %get-tuple-element.40), channel_id=1, source_target_pairs={{0,2},{1,3},{2,0},{3,1},{4,6},{5,7},{6,4},{7,5},{8,10},{9,11},{10,... | collective-permute-start | bytes 3145736 | tf_op jit(solution)/shard_map/ppermute | solution.py:297
  45.7 52.7 %collective-permute-start.11 = (bf16[2,64,8192]{2,1,0:T(8,128)(2,1)}, bf16[2,64,8192]{2,1,0:T(8,128)(2,1)}, u32[]{:S(2)}, u32[]{:S(2)}) collective-permute-start(bf16[2,64,8192]{2,1,0:T(8,128)(2,1)} %pad_maximum_fusion.refs_0_), channel_id=1, source_target_pairs={{0,4},{1,5},{2,6},{3,7},{12,8},{13,9},{14,10},{15,11},{16,20},{17,... | collective-permute-start | bytes 6291464 | tf_op jit(solution)/shard_map/ppermute | solution.py:297
  49.4 51.6 %collective-permute-start.10 = (bf16[2,64,8192]{2,1,0:T(8,128)(2,1)}, bf16[2,64,8192]{2,1,0:T(8,128)(2,1)}, u32[]{:S(2)}, u32[]{:S(2)}) collective-permute-start(bf16[2,64,8192]{2,1,0:T(8,128)(2,1)} %collective-permute-done.8.refs_1_), channel_id=1, source_target_pairs={{4,0},{5,1},{6,2},{7,3},{8,12},{9,13},{10,14},{11,15},{20,16},{21,... | collective-permute-start | bytes 6291464 | tf_op jit(solution)/shard_map/ppermute | solution.py:297
  54.9 46.1 %collective-permute-start.9 = (bf16[2,64,8192]{2,1,0:T(8,128)(2,1)}, bf16[2,64,8192]{2,1,0:T(8,128)(2,1)}, u32[]{:S(2)}, u32[]{:S(2)}) collective-permute-start(bf16[2,64,8192]{2,1,0:T(8,128)(2,1)} %collective-permute-done.5.refs_4_), channel_id=1, source_target_pairs={{4,8},{5,9},{6,10},{7,11},{8,4},{9,5},{10,6},{11,7},{20,24},{21,25... | collective-permute-start | bytes 6291464 | tf_op jit(solution)/shard_map/ppermute | solution.py:297
  64.9 55.1 %collective-permute-start.3 = (bf16[2,2,32,8192]{3,2,1,0:T(8,128)(2,1)}, bf16[2,2,32,8192]{3,2,1,0:T(8,128)(2,1)S(1)}, u32[]{:S(2)}, u32[]{:S(2)}) collective-permute-start(bf16[2,2,32,8192]{3,2,1,0:T(8,128)(2,1)} %get-tuple-element.41), channel_id=1, source_target_pairs={{0,2},{1,3},{2,0},{3,1},{4,6},{5,7},{6,4},{7,5},{8,10},{9,11},{10,... | collective-permute-start | bytes 6291464 | tf_op jit(solution)/shard_map/ppermute | solution.py:297
  108.8 28.6 %collective-permute-start.12 = (bf16[64,8192]{1,0:T(8,128)(2,1)S(1)}, bf16[64,8192]{1,0:T(8,128)(2,1)S(1)}, u32[]{:S(2)}, u32[]{:S(2)}) collective-permute-start(bf16[64,8192]{1,0:T(8,128)(2,1)S(1)} %get-tuple-element.46), channel_id=1, source_target_pairs={{0,4},{1,5},{2,6},{3,7},{4,0},{5,1},{6,2},{7,3},{8,12},{9,13},{10,... | collective-permute-start | bytes 3145736 | tf_op jit(solution)/shard_map/ppermute | solution.py:297
  113.8 23.6 %collective-permute-start.13 = (bf16[64,8192]{1,0:T(8,128)(2,1)S(1)}, bf16[64,8192]{1,0:T(8,128)(2,1)S(1)}, u32[]{:S(2)}, u32[]{:S(2)}) collective-permute-start(bf16[64,8192]{1,0:T(8,128)(2,1)S(1)} %get-tuple-element.47), channel_id=1, source_target_pairs={{4,8},{5,9},{6,10},{7,11},{8,4},{9,5},{10,6},{11,7},{20,24},{21,25... | collective-permute-start | bytes 3145736 | tf_op jit(solution)/shard_map/ppermute | solution.py:297
  114.5 45.4 %collective-permute-start.20 = (bf16[64,8192]{1,0:T(8,128)(2,1)S(1)}, bf16[64,8192]{1,0:T(8,128)(2,1)S(1)}, u32[]{:S(2)}, u32[]{:S(2)}) collective-permute-start(bf16[64,8192]{1,0:T(8,128)(2,1)S(1)} %get-tuple-element.59), channel_id=1, source_target_pairs={{0,4},{1,5},{2,6},{3,7},{12,8},{13,9},{14,10},{15,11},{16,20},{17,... | collective-permute-start | bytes 3145736 | tf_op jit(solution)/shard_map/ppermute | solution.py:297
  119.3 42.1 %collective-permute-start.21 = (bf16[64,8192]{1,0:T(8,128)(2,1)S(1)}, bf16[64,8192]{1,0:T(8,128)(2,1)S(1)}, u32[]{:S(2)}, u32[]{:S(2)}) collective-permute-start(bf16[64,8192]{1,0:T(8,128)(2,1)S(1)} %get-tuple-element.59), channel_id=1, source_target_pairs={{4,8},{5,9},{6,10},{7,11},{8,4},{9,5},{10,6},{11,7},{20,24},{21,25... | collective-permute-start | bytes 3145736 | tf_op jit(solution)/shard_map/ppermute | solution.py:297
  120.2 17.5 %collective-permute-start.4 = (bf16[1,2,32,8192]{3,2,1,0:T(8,128)(2,1)S(1)}, bf16[1,2,32,8192]{3,2,1,0:T(8,128)(2,1)S(1)}, u32[]{:S(2)}, u32[]{:S(2)}) collective-permute-start(bf16[1,2,32,8192]{3,2,1,0:T(8,128)(2,1)S(1)} %slice.40), channel_id=1, source_target_pairs={{0,1},{1,0},{2,3},{3,2},{4,5},{5,4},{6,7},{7,6},{8,9},{9,8},{10,11... | collective-permute-start | bytes 3145736 | tf_op jit(solution)/shard_map/ppermute | solution.py:297
  146.2 26.1 %collective-permute-start.15 = (bf16[64,8192]{1,0:T(8,128)(2,1)S(1)}, bf16[64,8192]{1,0:T(8,128)(2,1)S(1)}, u32[]{:S(2)}, u32[]{:S(2)}) collective-permute-start(bf16[64,8192]{1,0:T(8,128)(2,1)S(1)} %get-tuple-element.51), channel_id=1, source_target_pairs={{0,2},{1,3},{2,0},{3,1},{4,6},{5,7},{6,4},{7,5},{8,10},{9,11},{10,... | collective-permute-start | bytes 3145736 | tf_op jit(solution)/shard_map/ppermute | solution.py:297
  147.7 33.2 %collective-permute-start.18 = (bf16[64,8192]{1,0:T(8,128)(2,1)S(1)}, bf16[64,8192]{1,0:T(8,128)(2,1)S(1)}, u32[]{:S(2)}, u32[]{:S(2)}) collective-permute-start(bf16[64,8192]{1,0:T(8,128)(2,1)S(1)} %add_convert_fusion.3), channel_id=1, source_target_pairs={{4,8},{5,9},{6,10},{7,11},{8,4},{9,5},{10,6},{11,7},{20,24},{21,25... | collective-permute-start | bytes 3145736 | tf_op jit(solution)/shard_map/ppermute | solution.py:297
  148.7 39.9 %collective-permute-start.19 = (bf16[64,8192]{1,0:T(8,128)(2,1)S(1)}, bf16[64,8192]{1,0:T(8,128)(2,1)S(1)}, u32[]{:S(2)}, u32[]{:S(2)}) collective-permute-start(bf16[64,8192]{1,0:T(8,128)(2,1)S(1)} %add_convert_fusion.2), channel_id=1, source_target_pairs={{0,4},{1,5},{2,6},{3,7},{4,0},{5,1},{6,2},{7,3},{8,12},{9,13},{10,... | collective-permute-start | bytes 3145736 | tf_op jit(solution)/shard_map/ppermute | solution.py:297
  159.9 28.6 %collective-permute-start.16 = (bf16[64,8192]{1,0:T(8,128)(2,1)S(1)}, bf16[64,8192]{1,0:T(8,128)(2,1)}, u32[]{:S(2)}, u32[]{:S(2)}) collective-permute-start(bf16[64,8192]{1,0:T(8,128)(2,1)S(1)} %get-tuple-element.52), channel_id=1, source_target_pairs={{0,2},{1,3},{2,0},{3,1},{4,6},{5,7},{6,4},{7,5},{8,10},{9,11},{10,... | collective-permute-start | bytes 3145736 | tf_op jit(solution)/shard_map/ppermute | solution.py:297
  172.6 17.1 %collective-permute-start.22 = (bf16[64,8192]{1,0:T(8,128)(2,1)S(1)}, bf16[64,8192]{1,0:T(8,128)(2,1)S(1)}, u32[]{:S(2)}, u32[]{:S(2)}) collective-permute-start(bf16[64,8192]{1,0:T(8,128)(2,1)S(1)} %add_convert_fusion.1), channel_id=1, source_target_pairs={{4,8},{5,9},{6,10},{7,11},{8,4},{9,5},{10,6},{11,7},{20,24},{21,25... | collective-permute-start | bytes 3145736 | tf_op jit(solution)/shard_map/ppermute | solution.py:297
  173.7 27.9 %collective-permute-start.23 = (bf16[64,8192]{1,0:T(8,128)(2,1)S(1)}, bf16[64,8192]{1,0:T(8,128)(2,1)S(1)}, u32[]{:S(2)}, u32[]{:S(2)}) collective-permute-start(bf16[64,8192]{1,0:T(8,128)(2,1)S(1)} %add_convert_fusion), channel_id=1, source_target_pairs={{0,4},{1,5},{2,6},{3,7},{4,0},{5,1},{6,2},{7,3},{8,12},{9,13},{10,... | collective-permute-start | bytes 3145736 | tf_op jit(solution)/shard_map/ppermute | solution.py:297
  180.9 36.3 %collective-permute-start.14 = (bf16[64,8192]{1,0:T(8,128)(2,1)}, bf16[64,8192]{1,0:T(8,128)(2,1)}, u32[]{:S(2)}, u32[]{:S(2)}) collective-permute-start(bf16[64,8192]{1,0:T(8,128)(2,1)} %get-tuple-element.50), channel_id=1, source_target_pairs={{0,1},{1,0},{2,3},{3,2},{4,5},{5,4},{6,7},{7,6},{8,9},{9,8},{10,11... | collective-permute-start | bytes 3145736 | tf_op jit(solution)/shard_map/ppermute | solution.py:297
  188.5 28.7 %collective-permute-start.17 = (bf16[64,8192]{1,0:T(8,128)(2,1)}, bf16[64,8192]{1,0:T(8,128)(2,1)}, u32[]{:S(2)}, u32[]{:S(2)}) collective-permute-start(bf16[64,8192]{1,0:T(8,128)(2,1)} %collective-permute-done.16), channel_id=1, source_target_pairs={{0,1},{1,0},{2,3},{3,2},{4,5},{5,4},{6,7},{7,6},{8,9},{9,8},{10,11... | collective-permute-start | bytes 3145736 | tf_op jit(solution)/shard_map/ppermute | solution.py:297
  209.7 12.8 %collective-permute-start.27 = (f32[8,128]{1,0:T(8,128)S(1)}, f32[8,128]{1,0:T(8,128)S(1)}, u32[]{:S(2)}, u32[]{:S(2)}) collective-permute-start(f32[8,128]{1,0:T(8,128)S(1)} %add_add_fusion.1), channel_id=1, source_target_pairs={{0,4},{1,5},{2,6},{3,7},{4,0},{5,1},{6,2},{7,3},{8,12},{9,13},{10,... | collective-permute-start | bytes 12296 | tf_op jit(solution)/shard_map/ppermute | solution.py:297
  214.5 8.0 %collective-permute-start.28 = (f32[8,128]{1,0:T(8,128)S(1)}, f32[8,128]{1,0:T(8,128)S(1)}, u32[]{:S(2)}, u32[]{:S(2)}) collective-permute-start(f32[8,128]{1,0:T(8,128)S(1)} %add_add_fusion.1), channel_id=1, source_target_pairs={{0,8},{1,9},{2,10},{3,11},{4,12},{5,13},{6,14},{7,15},{8,0},{9,1},... | collective-permute-start | bytes 12296 | tf_op jit(solution)/shard_map/ppermute | solution.py:297
  (27 other events, 237.4 us)

commit v9 on v8

--- a/solution.py
+++ b/solution.py
@@ -139,7 +139,7 @@
     return upper == (lax.broadcasted_iota(jnp.int32, (rows, columns), 1) < first_columns)
 
 
-def far_group(is_end, rows, factors, handed=None):
+def far_group(is_end, rows, factors, handed=None, terms=(0, 1)):
     _, block, width = rows[0].shape
     rank = factors[0].shape[1]
     tile = min(width, 2048)
@@ -150,7 +150,7 @@
         rows_in, refs = refs[:len(rows)], refs[len(rows):]
         factors_in, refs = refs[:len(factors)], refs[len(factors):]
         handed_in, refs = (None, refs) if handed is None else (refs[0], refs[1:])
-        (up_ref, down_ref, dx_ref), (held, left, sems) = refs[:3], refs[-3:]
+        outs, (held, left, sems) = list(refs[:-3]), refs[-3:]
         step = pl.program_id(0)
         at_end = end_ref[0] == 1
 
@@ -176,25 +176,25 @@
                     for i in range(tiles):
                         copy(source, i).start()
 
-            sums = [jnp.zeros((rank, total), F32)] * 2
+            sums = {k: jnp.zeros((rank, total), F32) for k in terms}
             for i in range(tiles):
                 copy(rows_in[0], i).wait()
                 cut = pl.ds(i * tile, tile)
-                for k in range(2):
+                for k in terms:
                     sums[k] += dot32(factor(k, cut), tokens(k, cut), ROWS_OF)
-            for k in range(2):
+            for k in terms:
                 left[k] = sums[k].astype(BF16)
 
         cut = pl.ds(pl.multiple_of(step * tile, tile), tile)
-        up_ref[...] = dot32(left[0], tokens(1, cut)).astype(BF16)
-        down = dot32(left[1], tokens(0, cut)).astype(BF16)
-        down_ref[...] = down
-        dx = dot32(left[1], factor(0, cut), OUTER).astype(BF16)
-        dx_ref[...] = dx[:block]
-        if handed is not None:
-            refs[3][...] = jnp.where(at_end, down, dx[block:])
-
-    outs = 3 if handed is None else 4
+        for out, k in zip(outs, terms):
+            out[...] = dot32(left[k], tokens(1 - k, cut)).astype(BF16)
+        if 1 in terms:
+            dx = dot32(left[1], factor(0, cut), OUTER).astype(BF16)
+            outs[len(terms)][...] = dx[:block]
+            if handed is not None:
+                outs[-1][...] = jnp.where(at_end, outs[len(terms) - 1][...], dx[block:])
+
+    outs = len(terms) + (0 if 1 not in terms else 1 if handed is None else 2)
     more = () if handed is None else (handed,)
     return pl.pallas_call(
         body,
@@ -358,9 +358,10 @@
 
     up2, down2, dx_early = far_group(end_flag, (rows2,), (crossed,))
     rows3, rows2 = after((rows3, rows2), dx_early)
-    up3, down3, dx_late, swapped = far_group(end_flag, (rows3, rows2), (far, outer), handed)
-    up2_in = send(up3, inward)
-    down3, swapped, up3 = send(down3, cross), send(swapped, swap), send(up3, cross)
+    down3, dx_late, swapped = far_group(end_flag, (rows3, rows2), (far, outer), handed, (1,))
+    (up3,) = far_group(after(end_flag, dx_late), (rows3, rows2), (far, outer), handed, (0,))
+    down3, swapped = send(down3, cross), send(swapped, swap)
+    up3, up2_in = send(up3, cross), send(up3, inward)
 
     swapped, down3 = lax.optimization_barrier((swapped, down3))
     dx_own, dx_beside, *dx_across, up1, down1, up0, down0 = near_groups(

time: 227 us -> 228 us (level)
  Pallas kernels: 31.4 us -> 36.7 us
  waiting for transfers between devices: 114 us -> 109 us
    ppermute x30, waiting for transfers between devices: 114 us -> 109 us  [send(): return lax.ppermute(array, 'dp', pairs)]
    pallas_call x2 -> x3, Pallas kernels: 13 us -> 17.5 us  [far_group(): pl.pallas_call(body, grid=(tiles,), in_specs=[pl.BlockSpec(memory_space=p...]
    unnamed x43 -> x39, local copies, waits for them, and re-layouts: 5.46 us -> 4.73 us
  transfers between devices with their start and end apart: 30 -> 30, of which waited for: 13 -> 13; matrix products, arithmetic and copies ran while one was open for 5% -> 6% of each run, Pallas kernels for 14% -> 16%
where the time goes in v9:
time: 228 us
  waiting for transfers between devices  109 us (48%)
  starting transfers between devices  56.5 us (25%)
  Pallas kernels  36.7 us (16%)
  other arithmetic  11.4 us (5%)
  local copies, waits for them, and re-layouts  10.7 us (5%)
  between operations  3.07 us (1%)
    ppermute x30, waiting for transfers between devices, send(): return lax.ppermute(array, 'dp', pairs)  109 us
    ppermute x30, starting transfers between devices, send(): return lax.ppermute(array, 'dp', pairs)  56.5 us
    pallas_call x3, Pallas kernels, far_group(): pl.pallas_call(body, grid=(tiles,), in_specs=[pl.BlockSpec(memory_space=p...  17.5 us
    pallas_call x1, Pallas kernels, near_groups(): pl.pallas_call(body, grid=(tiles,), in_specs=[pl.BlockSpec(memory_space=p...  7.55 us
    pallas_call x1, Pallas kernels, pack(): pl.pallas_call(body, grid=(tiles,), in_specs=[pl.BlockSpec(place.shape, l...  6.36 us
    pallas_call x1, Pallas kernels, unpack(): pl.pallas_call(body, grid=(width // tile,), in_specs=[pl.BlockSpec(place....  5.23 us
    unnamed x39, local copies, waits for them, and re-layouts  4.73 us
  transfers between devices with their start and end apart: 30, of which 13 were waited for; matrix products, arithmetic and copies ran while one was open for 6% of the time, Pallas kernels for 16%

profile of v9, /device:TPU:0, one launch (start us, length us, event | category | flops | bytes accessed | tf_op | source)
XLA Modules:
  0.0 227.5 jit_solution(12633730118844864938)
XLA Ops:
  6.0 4.6 %collective-permute-start.5 = (bf16[2,64,8192]{2,1,0:T(8,128)(2,1)}, bf16[2,64,8192]{2,1,0:T(8,128)(2,1)}, u32[]{:S(2)}, u32[]{:S(2)}) collective-permute-start(bf16[2,64,8192]{2,1,0:T(8,128)(2,1)} %constant_dynamic-update-slice_fusion), channel_id=1, source_target_pairs={{0,4},{1,5},{2,6},{3,7},{4,0},{5,1},{6,2},{7,3},{8,12},{9,13},{10,... | collective-permute-start | bytes 6291464 | tf_op jit(solution)/shard_map/ppermute | solution.py:297
  11.3 6.4 %shard_map.85 = (bf16[1,2,64,8192]{3,2,1,0:T(8,128)(2,1)S(1)}, bf16[1,2,64,8192]{3,2,1,0:T(8,128)(2,1)S(1)}, bf16[2,2,16,8192]{3,2,1,0:T(8,128)(2,1)S(1)}, bf16[...) custom-call(bf16[256,128]{1,0:T(8,128)(2,1)S(1)} %fusion.1.place_ref, bf16[128,8192]{1,0:T(8,128)(2,1)} %x_in.1, ...), custom_call_target="tpu_custom_call" | custom-call | tf_op jit(solution)/shard_map/pallas_call | solution.py:107
  20.2 21.9 %collective-permute-done.1 = bf16[2,2,16,8192]{3,2,1,0:T(8,128)(2,1)S(1)} collective-permute-done((bf16[2,2,16,8192]{3,2,1,0:T(8,128)(2,1)S(1)}, bf16[2,2,16,8192]{3,2,1,0:T(8,128)(2,1)S(1)}, u32[]{:S(2)}, u32[]{:S(2)}) %collective-permute-start.1) | collective-permute-done | bytes 1048608 | tf_op jit(solution)/shard_map/ppermute | solution.py:297
  51.2 5.8 %collective-permute-done.5.refs_4_ = bf16[2,64,8192]{2,1,0:T(8,128)(2,1)} collective-permute-done((bf16[2,64,8192]{2,1,0:T(8,128)(2,1)}, bf16[2,64,8192]{2,1,0:T(8,128)(2,1)}, u32[]{:S(2)}, u32[]{:S(2)}) %collective-permute-start.5) | collective-permute-done | bytes 2097184 | tf_op jit(solution)/shard_map/ppermute | solution.py:297
  59.0 6.6 %collective-permute-done.2 = bf16[2,2,16,8192]{3,2,1,0:T(8,128)(2,1)S(1)} collective-permute-done((bf16[2,2,16,8192]{3,2,1,0:T(8,128)(2,1)S(1)}, bf16[2,2,16,8192]{3,2,1,0:T(8,128)(2,1)S(1)}, u32[]{:S(2)}, u32[]{:S(2)}) %collective-permute-start.2) | collective-permute-done | bytes 1048608 | tf_op jit(solution)/shard_map/ppermute | solution.py:297
  69.0 3.0 %pad_maximum_fusion.1.refs_0_.refs_1_ = bf16[2,64,8192]{2,1,0:T(8,128)(2,1)} fusion(bf16[2,16,8192]{2,1,0:T(8,128)(2,1)} %bitcast.11, bf16[2,16,8192]{2,1,0:T(8,128)(2,1)} %get-tuple-element.74, bf16[2,16,8192]{2,1,0:T(8,128)(2,1)} %get-tuple-element.72, bf16[2,16,8192]{2,1,0:T(8,128)(2,1)} %get-tuple-element.70), kind=kLoop, calls=%fused_computation.1 | loop fusion | flops 8388608 | bytes 4194304 | tf_op jit(solution)/shard_map/concatenate | solution.py:354
  72.0 5.2 %shard_map.86 = (bf16[64,8192]{1,0:T(8,128)(2,1)S(1)}, bf16[64,8192]{1,0:T(8,128)(2,1)S(1)}, bf16[64,8192]{1,0:T(8,128)(2,1)S(1)}) custom-call(s32[1]{0:T(128)} %bitcast.1.end_ref, bf16[2,64,8192]{2,1,0:T(8,128)(2,1)} %pad_maximum_fusion.1.refs_0_.refs_1_, bf16[2,64,8192]{2,1,0:T(8,128)(2,1)} %collective-permute-done.8.refs_1_), custom_call_target="tpu_custom_call" | custom-call | tf_op jit(solution)/shard_map/pallas_call | solution.py:199
  77.2 23.3 %collective-permute-done.11.refs_4_ = bf16[2,64,8192]{2,1,0:T(8,128)(2,1)S(1)} collective-permute-done((bf16[2,64,8192]{2,1,0:T(8,128)(2,1)}, bf16[2,64,8192]{2,1,0:T(8,128)(2,1)S(1)}, u32[]{:S(2)}, u32[]{:S(2)}) %collective-permute-start.11) | collective-permute-done | bytes 2097184 | tf_op jit(solution)/shard_map/ppermute | solution.py:297
  100.5 2.5 %collective-permute-done.10.refs_3_ = bf16[2,64,8192]{2,1,0:T(8,128)(2,1)} collective-permute-done((bf16[2,64,8192]{2,1,0:T(8,128)(2,1)}, bf16[2,64,8192]{2,1,0:T(8,128)(2,1)}, u32[]{:S(2)}, u32[]{:S(2)}) %collective-permute-start.10) | collective-permute-done | bytes 2097184 | tf_op jit(solution)/shard_map/ppermute | solution.py:297
  103.0 6.6 %shard_map.87 = (bf16[64,8192]{1,0:T(8,128)(2,1)S(1)}, bf16[64,8192]{1,0:T(8,128)(2,1)S(1)}, bf16[64,8192]{1,0:T(8,128)(2,1)S(1)}) custom-call(s32[1]{0:T(128)} %bitcast.1.end_ref, bf16[2,64,8192]{2,1,0:T(8,128)(2,1)} %pad_maximum_fusion.refs_0_, bf16[2,64,8192]{2,1,0:T(8,128)(2,1)} %pad_maximum_fusion.1.refs_0_.refs_1_, ...), custom_call_target="tpu_custom_call" | custom-call | tf_op jit(solution)/shard_map/pallas_call | solution.py:199
  109.6 5.1 %collective-permute-start.12 = (bf16[64,8192]{1,0:T(8,128)(2,1)S(1)}, bf16[64,8192]{1,0:T(8,128)(2,1)S(1)}, u32[]{:S(2)}, u32[]{:S(2)}) collective-permute-start(bf16[64,8192]{1,0:T(8,128)(2,1)S(1)} %get-tuple-element.46), channel_id=1, source_target_pairs={{0,4},{1,5},{2,6},{3,7},{4,0},{5,1},{6,2},{7,3},{8,12},{9,13},{10,... | collective-permute-start | bytes 3145736 | tf_op jit(solution)/shard_map/ppermute | solution.py:297
  115.4 5.8 %shard_map.90 = bf16[64,8192]{1,0:T(8,128)(2,1)S(1)} custom-call(s32[1]{0:T(128)} %bitcast.1.end_ref, bf16[2,64,8192]{2,1,0:T(8,128)(2,1)} %pad_maximum_fusion.refs_0_, bf16[2,64,8192]{2,1,0:T(8,128)(2,1)} %pad_maximum_fusion.1.refs_0_.refs_1_, bf16[2,64,8192]{2,1,0:T(8,128)(2,1)} %collective-permute-done.9.refs_2_, ...), custom_call_target="tpu_custom_call" | custom-call | tf_op jit(solution)/shard_map/pallas_call | solution.py:199
  121.2 4.8 %collective-permute-start.20 = (bf16[64,8192]{1,0:T(8,128)(2,1)S(1)}, bf16[64,8192]{1,0:T(8,128)(2,1)S(1)}, u32[]{:S(2)}, u32[]{:S(2)}) collective-permute-start(bf16[64,8192]{1,0:T(8,128)(2,1)S(1)} %shard_map.90), channel_id=1, source_target_pairs={{0,4},{1,5},{2,6},{3,7},{12,8},{13,9},{14,10},{15,11},{16,20},{17,... | collective-permute-start | bytes 3145736 | tf_op jit(solution)/shard_map/ppermute | solution.py:297
  128.3 10.0 %collective-permute-done.12.refs_9_ = bf16[64,8192]{1,0:T(8,128)(2,1)S(1)} collective-permute-done((bf16[64,8192]{1,0:T(8,128)(2,1)S(1)}, bf16[64,8192]{1,0:T(8,128)(2,1)S(1)}, u32[]{:S(2)}, u32[]{:S(2)}) %collective-permute-start.12) | collective-permute-done | bytes 1048608 | tf_op jit(solution)/shard_map/ppermute | solution.py:297
  138.6 7.5 %shard_map.88 = (bf16[64,8192]{1,0:T(8,128)(2,1)S(1)}, bf16[64,8192]{1,0:T(8,128)(2,1)}, bf16[64,8192]{1,0:T(8,128)(2,1)S(1)}, bf16[64,8192]{1,0:T(8,128)(2,1)S(...) custom-call(s32[1]{0:T(128)} %bitcast.1.end_ref, ...), custom_call_target="tpu_custom_call" | custom-call | tf_op jit(solution)/shard_map/pallas_call | solution.py:264
  148.6 7.2 %collective-permute-start.19 = (bf16[64,8192]{1,0:T(8,128)(2,1)S(1)}, bf16[64,8192]{1,0:T(8,128)(2,1)S(1)}, u32[]{:S(2)}, u32[]{:S(2)}) collective-permute-start(bf16[64,8192]{1,0:T(8,128)(2,1)S(1)} %add_convert_fusion.2), channel_id=1, source_target_pairs={{0,4},{1,5},{2,6},{3,7},{4,0},{5,1},{6,2},{7,3},{8,12},{9,13},{10,... | collective-permute-start | bytes 3145736 | tf_op jit(solution)/shard_map/ppermute | solution.py:297
  155.8 4.9 %collective-permute-done.20 = bf16[64,8192]{1,0:T(8,128)(2,1)S(1)} collective-permute-done((bf16[64,8192]{1,0:T(8,128)(2,1)S(1)}, bf16[64,8192]{1,0:T(8,128)(2,1)S(1)}, u32[]{:S(2)}, u32[]{:S(2)}) %collective-permute-start.20) | collective-permute-done | bytes 1048608 | tf_op jit(solution)/shard_map/ppermute | solution.py:297
  162.3 10.0 %collective-permute-done.15.refs_2_ = bf16[64,8192]{1,0:T(8,128)(2,1)S(1)} collective-permute-done((bf16[64,8192]{1,0:T(8,128)(2,1)S(1)}, bf16[64,8192]{1,0:T(8,128)(2,1)S(1)}, u32[]{:S(2)}, u32[]{:S(2)}) %collective-permute-start.15) | collective-permute-done | bytes 1048608 | tf_op jit(solution)/shard_map/ppermute | solution.py:297
  173.6 7.2 %collective-permute-start.23 = (bf16[64,8192]{1,0:T(8,128)(2,1)S(1)}, bf16[64,8192]{1,0:T(8,128)(2,1)S(1)}, u32[]{:S(2)}, u32[]{:S(2)}) collective-permute-start(bf16[64,8192]{1,0:T(8,128)(2,1)S(1)} %add_convert_fusion), channel_id=1, source_target_pairs={{0,4},{1,5},{2,6},{3,7},{4,0},{5,1},{6,2},{7,3},{8,12},{9,13},{10,... | collective-permute-start | bytes 3145736 | tf_op jit(solution)/shard_map/ppermute | solution.py:297
  180.9 7.8 %collective-permute-done.16 = bf16[64,8192]{1,0:T(8,128)(2,1)} collective-permute-done((bf16[64,8192]{1,0:T(8,128)(2,1)S(1)}, bf16[64,8192]{1,0:T(8,128)(2,1)}, u32[]{:S(2)}, u32[]{:S(2)}) %collective-permute-start.16) | collective-permute-done | bytes 1048608 | tf_op jit(solution)/shard_map/ppermute | solution.py:297
  189.8 12.7 %collective-permute-done.23 = bf16[64,8192]{1,0:T(8,128)(2,1)S(1)} collective-permute-done((bf16[64,8192]{1,0:T(8,128)(2,1)S(1)}, bf16[64,8192]{1,0:T(8,128)(2,1)S(1)}, u32[]{:S(2)}, u32[]{:S(2)}) %collective-permute-start.23) | collective-permute-done | bytes 1048608 | tf_op jit(solution)/shard_map/ppermute | solution.py:297
  210.7 4.7 %collective-permute-start.27 = (f32[8,128]{1,0:T(8,128)S(1)}, f32[8,128]{1,0:T(8,128)S(1)}, u32[]{:S(2)}, u32[]{:S(2)}) collective-permute-start(f32[8,128]{1,0:T(8,128)S(1)} %add_add_fusion.1), channel_id=1, source_target_pairs={{0,4},{1,5},{2,6},{3,7},{4,0},{5,1},{6,2},{7,3},{8,12},{9,13},{10,... | collective-permute-start | bytes 12296 | tf_op jit(solution)/shard_map/ppermute | solution.py:297
  218.2 5.2 %shard_map.89 = bf16[128,8192]{1,0:T(8,128)(2,1)} custom-call(bf16[128,256]{1,0:T(8,128)(2,1)S(1)} %fusion.place_ref, bf16[64,8192]{1,0:T(8,128)(2,1)} %copy-done.8, bf16[64,8192]{1,0:T(8,128)(2,1)} %collective-permute-done.14.refs_1_, bf16[64,8192]{1,0:T(8,128)(2,1)S(1)} %collective-permute-done.15.refs_2_, bf16[64,8192]{1,0:T(8,128)(2,1)} %collective-permute-done.17.refs_3_), custom_call_target="tpu_custom_call" | custom-call | tf_op jit(solution)/shard_map/pallas_call | solution.py:126
  224.7 2.8 %multiply_bitcast_fusion = (f32[1,64,8192]{2,1,0:T(8,128)}, f32[1,64,8192]{2,1,0:T(8,128)}) fusion(f32[]{:T(128)} %bitcast.12, bf16[64,8192]{1,0:T(8,128)(2,1)S(1)} %copy-done.16, f32[64,8192]{1,0:T(8,128)S(1)} %get-tuple-element.57, bf16[64,8192]{1,0:T(8,128)(2,1)S(1)} %copy-done.14, bf16[64,8192]{1,0:T(8,128)(2,1)S(1)} %copy-done.12, ...), kind=kLoop, calls=%fused_computation.2 | loop fusion | flops 5242880 | bytes 12582916 | tf_op jit(solution)/shard_map/broadcast_in_dim | solution.py:37
  (108 shorter events, 42.8 us)
Async XLA Ops:
  4.1 45.9 %collective-permute-start.8 = (bf16[2,64,8192]{2,1,0:T(8,128)(2,1)}, bf16[2,64,8192]{2,1,0:T(8,128)(2,1)}, u32[]{:S(2)}, u32[]{:S(2)}) collective-permute-start(bf16[2,64,8192]{2,1,0:T(8,128)(2,1)} %constant_dynamic-update-slice_fusion), channel_id=1, source_target_pairs={{4,8},{5,9},{6,10},{7,11},{8,4},{9,5},{10,6},{11,7},{20,24},{21,25... | collective-permute-start | bytes 6291464 | tf_op jit(solution)/shard_map/ppermute | solution.py:297
  6.0 51.0 %collective-permute-start.5 = (bf16[2,64,8192]{2,1,0:T(8,128)(2,1)}, bf16[2,64,8192]{2,1,0:T(8,128)(2,1)}, u32[]{:S(2)}, u32[]{:S(2)}) collective-permute-start(bf16[2,64,8192]{2,1,0:T(8,128)(2,1)} %constant_dynamic-update-slice_fusion), channel_id=1, source_target_pairs={{0,4},{1,5},{2,6},{3,7},{4,0},{5,1},{6,2},{7,3},{8,12},{9,13},{10,... | collective-permute-start | bytes 6291464 | tf_op jit(solution)/shard_map/ppermute | solution.py:297
  17.7 24.4 %collective-permute-start.1 = (bf16[2,2,16,8192]{3,2,1,0:T(8,128)(2,1)S(1)}, bf16[2,2,16,8192]{3,2,1,0:T(8,128)(2,1)S(1)}, u32[]{:S(2)}, u32[]{:S(2)}) collective-permute-start(bf16[2,2,16,8192]{3,2,1,0:T(8,128)(2,1)S(1)} %get-tuple-element.39), channel_id=1, source_target_pairs={{0,2},{1,3},{2,0},{3,1},{4,6},{5,7},{6,4},{7,5},{8,10},{9,11},{10,... | collective-permute-start | bytes 3145736 | tf_op jit(solution)/shard_map/ppermute | solution.py:297
  19.3 24.5 %collective-permute-start = (bf16[1,2,64,8192]{3,2,1,0:T(8,128)(2,1)S(1)}, bf16[1,2,64,8192]{3,2,1,0:T(8,128)(2,1)S(1)}, u32[]{:S(2)}, u32[]{:S(2)}) collective-permute-start(bf16[1,2,64,8192]{3,2,1,0:T(8,128)(2,1)S(1)} %get-tuple-element.36), channel_id=1, source_target_pairs={{0,1},{1,0},{2,3},{3,2},{4,5},{5,4},{6,7},{7,6},{8,9},{9,8},{10,11... | collective-permute-start | bytes 6291464 | tf_op jit(solution)/shard_map/ppermute | solution.py:297
  42.1 23.5 %collective-permute-start.2 = (bf16[2,2,16,8192]{3,2,1,0:T(8,128)(2,1)S(1)}, bf16[2,2,16,8192]{3,2,1,0:T(8,128)(2,1)S(1)}, u32[]{:S(2)}, u32[]{:S(2)}) collective-permute-start(bf16[2,2,16,8192]{3,2,1,0:T(8,128)(2,1)S(1)} %get-tuple-element.40), channel_id=1, source_target_pairs={{0,2},{1,3},{2,0},{3,1},{4,6},{5,7},{6,4},{7,5},{8,10},{9,11},{10,... | collective-permute-start | bytes 3145736 | tf_op jit(solution)/shard_map/ppermute | solution.py:297
  47.6 52.9 %collective-permute-start.11 = (bf16[2,64,8192]{2,1,0:T(8,128)(2,1)}, bf16[2,64,8192]{2,1,0:T(8,128)(2,1)S(1)}, u32[]{:S(2)}, u32[]{:S(2)}) collective-permute-start(bf16[2,64,8192]{2,1,0:T(8,128)(2,1)} %pad_maximum_fusion.refs_0_), channel_id=1, source_target_pairs={{0,4},{1,5},{2,6},{3,7},{12,8},{13,9},{14,10},{15,11},{16,20},{17,... | collective-permute-start | bytes 6291464 | tf_op jit(solution)/shard_map/ppermute | solution.py:297
  49.9 53.1 %collective-permute-start.10 = (bf16[2,64,8192]{2,1,0:T(8,128)(2,1)}, bf16[2,64,8192]{2,1,0:T(8,128)(2,1)}, u32[]{:S(2)}, u32[]{:S(2)}) collective-permute-start(bf16[2,64,8192]{2,1,0:T(8,128)(2,1)} %collective-permute-done.8.refs_1_), channel_id=1, source_target_pairs={{4,0},{5,1},{6,2},{7,3},{8,12},{9,13},{10,14},{11,15},{20,16},{21,... | collective-permute-start | bytes 6291464 | tf_op jit(solution)/shard_map/ppermute | solution.py:297
  57.0 46.0 %collective-permute-start.9 = (bf16[2,64,8192]{2,1,0:T(8,128)(2,1)}, bf16[2,64,8192]{2,1,0:T(8,128)(2,1)}, u32[]{:S(2)}, u32[]{:S(2)}) collective-permute-start(bf16[2,64,8192]{2,1,0:T(8,128)(2,1)} %collective-permute-done.5.refs_4_), channel_id=1, source_target_pairs={{4,8},{5,9},{6,10},{7,11},{8,4},{9,5},{10,6},{11,7},{20,24},{21,25... | collective-permute-start | bytes 6291464 | tf_op jit(solution)/shard_map/ppermute | solution.py:297
  66.8 60.0 %collective-permute-start.3 = (bf16[2,2,32,8192]{3,2,1,0:T(8,128)(2,1)}, bf16[2,2,32,8192]{3,2,1,0:T(8,128)(2,1)}, u32[]{:S(2)}, u32[]{:S(2)}) collective-permute-start(bf16[2,2,32,8192]{3,2,1,0:T(8,128)(2,1)} %get-tuple-element.41), channel_id=1, source_target_pairs={{0,2},{1,3},{2,0},{3,1},{4,6},{5,7},{6,4},{7,5},{8,10},{9,11},{10,... | collective-permute-start | bytes 6291464 | tf_op jit(solution)/shard_map/ppermute | solution.py:297
  109.6 28.7 %collective-permute-start.12 = (bf16[64,8192]{1,0:T(8,128)(2,1)S(1)}, bf16[64,8192]{1,0:T(8,128)(2,1)S(1)}, u32[]{:S(2)}, u32[]{:S(2)}) collective-permute-start(bf16[64,8192]{1,0:T(8,128)(2,1)S(1)} %get-tuple-element.46), channel_id=1, source_target_pairs={{0,4},{1,5},{2,6},{3,7},{4,0},{5,1},{6,2},{7,3},{8,12},{9,13},{10,... | collective-permute-start | bytes 3145736 | tf_op jit(solution)/shard_map/ppermute | solution.py:297
  114.7 23.6 %collective-permute-start.13 = (bf16[64,8192]{1,0:T(8,128)(2,1)S(1)}, bf16[64,8192]{1,0:T(8,128)(2,1)S(1)}, u32[]{:S(2)}, u32[]{:S(2)}) collective-permute-start(bf16[64,8192]{1,0:T(8,128)(2,1)S(1)} %get-tuple-element.47), channel_id=1, source_target_pairs={{4,8},{5,9},{6,10},{7,11},{8,4},{9,5},{10,6},{11,7},{20,24},{21,25... | collective-permute-start | bytes 3145736 | tf_op jit(solution)/shard_map/ppermute | solution.py:297
  121.2 39.5 %collective-permute-start.20 = (bf16[64,8192]{1,0:T(8,128)(2,1)S(1)}, bf16[64,8192]{1,0:T(8,128)(2,1)S(1)}, u32[]{:S(2)}, u32[]{:S(2)}) collective-permute-start(bf16[64,8192]{1,0:T(8,128)(2,1)S(1)} %shard_map.90), channel_id=1, source_target_pairs={{0,4},{1,5},{2,6},{3,7},{12,8},{13,9},{14,10},{15,11},{16,20},{17,... | collective-permute-start | bytes 3145736 | tf_op jit(solution)/shard_map/ppermute | solution.py:297
  126.0 36.3 %collective-permute-start.21 = (bf16[64,8192]{1,0:T(8,128)(2,1)S(1)}, bf16[64,8192]{1,0:T(8,128)(2,1)S(1)}, u32[]{:S(2)}, u32[]{:S(2)}) collective-permute-start(bf16[64,8192]{1,0:T(8,128)(2,1)S(1)} %shard_map.90), channel_id=1, source_target_pairs={{4,8},{5,9},{6,10},{7,11},{8,4},{9,5},{10,6},{11,7},{20,24},{21,25... | collective-permute-start | bytes 3145736 | tf_op jit(solution)/shard_map/ppermute | solution.py:297
  128.2 10.3 %collective-permute-start.4 = (bf16[1,2,32,8192]{3,2,1,0:T(8,128)(2,1)S(1)}, bf16[1,2,32,8192]{3,2,1,0:T(8,128)(2,1)S(1)}, u32[]{:S(2)}, u32[]{:S(2)}) collective-permute-start(bf16[1,2,32,8192]{3,2,1,0:T(8,128)(2,1)S(1)} %slice.40), channel_id=1, source_target_pairs={{0,1},{1,0},{2,3},{3,2},{4,5},{5,4},{6,7},{7,6},{8,9},{9,8},{10,11... | collective-permute-start | bytes 3145736 | tf_op jit(solution)/shard_map/ppermute | solution.py:297
  146.1 26.1 %collective-permute-start.15 = (bf16[64,8192]{1,0:T(8,128)(2,1)S(1)}, bf16[64,8192]{1,0:T(8,128)(2,1)S(1)}, u32[]{:S(2)}, u32[]{:S(2)}) collective-permute-start(bf16[64,8192]{1,0:T(8,128)(2,1)S(1)} %get-tuple-element.51), channel_id=1, source_target_pairs={{0,2},{1,3},{2,0},{3,1},{4,6},{5,7},{6,4},{7,5},{8,10},{9,11},{10,... | collective-permute-start | bytes 3145736 | tf_op jit(solution)/shard_map/ppermute | solution.py:297
  147.6 33.2 %collective-permute-start.18 = (bf16[64,8192]{1,0:T(8,128)(2,1)S(1)}, bf16[64,8192]{1,0:T(8,128)(2,1)S(1)}, u32[]{:S(2)}, u32[]{:S(2)}) collective-permute-start(bf16[64,8192]{1,0:T(8,128)(2,1)S(1)} %add_convert_fusion.3), channel_id=1, source_target_pairs={{4,8},{5,9},{6,10},{7,11},{8,4},{9,5},{10,6},{11,7},{20,24},{21,25... | collective-permute-start | bytes 3145736 | tf_op jit(solution)/shard_map/ppermute | solution.py:297
  148.6 40.0 %collective-permute-start.19 = (bf16[64,8192]{1,0:T(8,128)(2,1)S(1)}, bf16[64,8192]{1,0:T(8,128)(2,1)S(1)}, u32[]{:S(2)}, u32[]{:S(2)}) collective-permute-start(bf16[64,8192]{1,0:T(8,128)(2,1)S(1)} %add_convert_fusion.2), channel_id=1, source_target_pairs={{0,4},{1,5},{2,6},{3,7},{4,0},{5,1},{6,2},{7,3},{8,12},{9,13},{10,... | collective-permute-start | bytes 3145736 | tf_op jit(solution)/shard_map/ppermute | solution.py:297
  160.8 27.9 %collective-permute-start.16 = (bf16[64,8192]{1,0:T(8,128)(2,1)S(1)}, bf16[64,8192]{1,0:T(8,128)(2,1)}, u32[]{:S(2)}, u32[]{:S(2)}) collective-permute-start(bf16[64,8192]{1,0:T(8,128)(2,1)S(1)} %get-tuple-element.52), channel_id=1, source_target_pairs={{0,2},{1,3},{2,0},{3,1},{4,6},{5,7},{6,4},{7,5},{8,10},{9,11},{10,... | collective-permute-start | bytes 3145736 | tf_op jit(solution)/shard_map/ppermute | solution.py:297
  172.5 17.3 %collective-permute-start.22 = (bf16[64,8192]{1,0:T(8,128)(2,1)S(1)}, bf16[64,8192]{1,0:T(8,128)(2,1)S(1)}, u32[]{:S(2)}, u32[]{:S(2)}) collective-permute-start(bf16[64,8192]{1,0:T(8,128)(2,1)S(1)} %add_convert_fusion.1), channel_id=1, source_target_pairs={{4,8},{5,9},{6,10},{7,11},{8,4},{9,5},{10,6},{11,7},{20,24},{21,25... | collective-permute-start | bytes 3145736 | tf_op jit(solution)/shard_map/ppermute | solution.py:297
  173.6 28.9 %collective-permute-start.23 = (bf16[64,8192]{1,0:T(8,128)(2,1)S(1)}, bf16[64,8192]{1,0:T(8,128)(2,1)S(1)}, u32[]{:S(2)}, u32[]{:S(2)}) collective-permute-start(bf16[64,8192]{1,0:T(8,128)(2,1)S(1)} %add_convert_fusion), channel_id=1, source_target_pairs={{0,4},{1,5},{2,6},{3,7},{4,0},{5,1},{6,2},{7,3},{8,12},{9,13},{10,... | collective-permute-start | bytes 3145736 | tf_op jit(solution)/shard_map/ppermute | solution.py:297
  180.9 37.3 %collective-permute-start.14 = (bf16[64,8192]{1,0:T(8,128)(2,1)}, bf16[64,8192]{1,0:T(8,128)(2,1)}, u32[]{:S(2)}, u32[]{:S(2)}) collective-permute-start(bf16[64,8192]{1,0:T(8,128)(2,1)} %get-tuple-element.50), channel_id=1, source_target_pairs={{0,1},{1,0},{2,3},{3,2},{4,5},{5,4},{6,7},{7,6},{8,9},{9,8},{10,11... | collective-permute-start | bytes 3145736 | tf_op jit(solution)/shard_map/ppermute | solution.py:297
  188.6 29.5 %collective-permute-start.17 = (bf16[64,8192]{1,0:T(8,128)(2,1)}, bf16[64,8192]{1,0:T(8,128)(2,1)}, u32[]{:S(2)}, u32[]{:S(2)}) collective-permute-start(bf16[64,8192]{1,0:T(8,128)(2,1)} %collective-permute-done.16), channel_id=1, source_target_pairs={{0,1},{1,0},{2,3},{3,2},{4,5},{5,4},{6,7},{7,6},{8,9},{9,8},{10,11... | collective-permute-start | bytes 3145736 | tf_op jit(solution)/shard_map/ppermute | solution.py:297
  210.7 12.7 %collective-permute-start.27 = (f32[8,128]{1,0:T(8,128)S(1)}, f32[8,128]{1,0:T(8,128)S(1)}, u32[]{:S(2)}, u32[]{:S(2)}) collective-permute-start(f32[8,128]{1,0:T(8,128)S(1)} %add_add_fusion.1), channel_id=1, source_target_pairs={{0,4},{1,5},{2,6},{3,7},{4,0},{5,1},{6,2},{7,3},{8,12},{9,13},{10,... | collective-permute-start | bytes 12296 | tf_op jit(solution)/shard_map/ppermute | solution.py:297
  215.4 8.0 %collective-permute-start.28 = (f32[8,128]{1,0:T(8,128)S(1)}, f32[8,128]{1,0:T(8,128)S(1)}, u32[]{:S(2)}, u32[]{:S(2)}) collective-permute-start(f32[8,128]{1,0:T(8,128)S(1)} %add_add_fusion.1), channel_id=1, source_target_pairs={{0,8},{1,9},{2,10},{3,11},{4,12},{5,13},{6,14},{7,15},{8,0},{9,1},... | collective-permute-start | bytes 12296 | tf_op jit(solution)/shard_map/ppermute | solution.py:297
  (25 other events, 203.6 us)

commit v10 on v8

--- a/solution.py
+++ b/solution.py
@@ -150,7 +150,7 @@
         rows_in, refs = refs[:len(rows)], refs[len(rows):]
         factors_in, refs = refs[:len(factors)], refs[len(factors):]
         handed_in, refs = (None, refs) if handed is None else (refs[0], refs[1:])
-        (up_ref, down_ref, dx_ref), (held, left, sems) = refs[:3], refs[-3:]
+        (up_ref, down_ref, dx_ref), (held, left, inner, sems) = refs[:3], refs[-4:]
         step = pl.program_id(0)
         at_end = end_ref[0] == 1
 
@@ -176,35 +176,37 @@
                     for i in range(tiles):
                         copy(source, i).start()
 
-            sums = [jnp.zeros((rank, total), F32)] * 2
+            sums = [jnp.zeros((total, rank), F32)] * 2
             for i in range(tiles):
                 copy(rows_in[0], i).wait()
                 cut = pl.ds(i * tile, tile)
                 for k in range(2):
-                    sums[k] += dot32(factor(k, cut), tokens(k, cut), ROWS_OF)
+                    sums[k] += dot32(tokens(k, cut), factor(k, cut), ROWS_OF)
             for k in range(2):
-                left[k] = sums[k].astype(BF16)
+                left[k] = sums[k].T.astype(BF16)
+            inner[...] = sums[1].astype(BF16)
 
         cut = pl.ds(pl.multiple_of(step * tile, tile), tile)
         up_ref[...] = dot32(left[0], tokens(1, cut)).astype(BF16)
         down = dot32(left[1], tokens(0, cut)).astype(BF16)
         down_ref[...] = down
-        dx = dot32(left[1], factor(0, cut), OUTER).astype(BF16)
+        dx = dot32(inner[...], factor(0, cut)).astype(BF16)
         dx_ref[...] = dx[:block]
         if handed is not None:
             refs[3][...] = jnp.where(at_end, down, dx[block:])
 
-    outs = 3 if handed is None else 4
+    sizes = (rank, rank, block) + (() if handed is None else (block,))
     more = () if handed is None else (handed,)
     return pl.pallas_call(
         body,
         grid=(tiles,),
         in_specs=[pl.BlockSpec(memory_space=pltpu.SMEM)] + [HBM] * len(rows) + [WHOLE] * (len(factors) + len(more)),
-        out_specs=[pl.BlockSpec((rank, tile), lambda i: (0, i))] * outs,
-        out_shape=[jax.ShapeDtypeStruct((rank, width), BF16)] * outs,
+        out_specs=[pl.BlockSpec((n, tile), lambda i: (0, i)) for n in sizes],
+        out_shape=[jax.ShapeDtypeStruct((n, width), BF16) for n in sizes],
         scratch_shapes=[
             pltpu.VMEM((2, block, width), BF16),
             pltpu.VMEM((2, rank, total), BF16),
+            pltpu.VMEM((total, rank), BF16),
             pltpu.SemaphoreType.DMA((tiles,)),
         ],
         compiler_params=kernel_params(),
@@ -222,7 +224,7 @@
         stage_in, refs = refs[:plane], refs[plane:]
         pair_in, down_in, up_in, late_ref, early_ref, swapped_ref = refs[:6]
         dx_refs, sum_refs = refs[6:10], refs[10:14]
-        (left,) = refs[14:]
+        left, inner = refs[14:]
         step = pl.program_id(0)
         own_in = (down_in, up_in)
         is_mine = corner(2 * block, block, 2 * rank, rank)
@@ -246,15 +248,17 @@
                     both = jnp.concatenate([pair_in[k, :, cut], own_in[k][:, cut]], axis=0)
                     sums[k] += dot32(rows(k, cut), both, ROWS_OF)
             for k in range(2):
-                left[k] = jnp.where(is_mine, sums[k], 0.0).astype(BF16)
+                masked = jnp.where(is_mine, sums[k], 0.0)
+                left[k] = masked.T.astype(BF16)
+            inner[...] = masked.astype(BF16)
 
         cut = pl.ds(pl.multiple_of(step * tile, tile), tile)
         for k in range(2):
-            both = dot32(left[k], rows(1 - k, cut), OUTER)
+            both = dot32(left[k], rows(1 - k, cut))
             sum_refs[k][...] = both[:rank]
             sum_refs[2 + k][...] = both[rank:]
         downs = jnp.concatenate([pair_in[0, :, cut], down_in[:, cut]], axis=0)
-        dx = dot32(left[1], downs).astype(BF16)
+        dx = dot32(inner[...], downs).astype(BF16)
         at_end, late = end_ref[0] == 1, late_ref[...]
         moved = [jnp.where(at_end, swapped_ref[...], late), jnp.where(at_end, late, early_ref[...]), dx[:block], dx[block:]]
         for n, dx in enumerate(moved):
@@ -271,7 +275,7 @@
         + [pl.BlockSpec((rank, tile), lambda i: (0, i))] * 4,
         out_shape=[jax.ShapeDtypeStruct((4 * capacity, width), BF16)] * plane
         + [jax.ShapeDtypeStruct((rank, width), F32)] * 4,
-        scratch_shapes=[pltpu.VMEM((2, 2 * block, 2 * rank), BF16)],
+        scratch_shapes=[pltpu.VMEM((2, 2 * rank, 2 * block), BF16), pltpu.VMEM((2 * block, 2 * rank), BF16)],
         compiler_params=kernel_params(),
     )(is_end, *in_vmem(*stage, pair, down, up), dx_late, dx_early, swapped)
 

time: 227 us -> 227 us (level)
  no operation moved by 1% of the time
where the time goes in v10:
time: 227 us; the launch traced here: 226 us
  waiting for transfers between devices  114 us (50%)
  starting transfers between devices  57.9 us (26%)
  Pallas kernels  31.3 us (14%)
  other arithmetic  11.4 us (5%)
  local copies, waits for them, and re-layouts  9.04 us (4%)
  between operations  3.09 us (1%)
    ppermute x30, waiting for transfers between devices, send(): return lax.ppermute(array, 'dp', pairs)  114 us
    ppermute x30, starting transfers between devices, send(): return lax.ppermute(array, 'dp', pairs)  57.9 us
    pallas_call x2, Pallas kernels, far_group(): pl.pallas_call(body, grid=(tiles,), in_specs=[pl.BlockSpec(memory_space=p...  12.9 us
    pallas_call x1, Pallas kernels, near_groups(): pl.pallas_call(body, grid=(tiles,), in_specs=[pl.BlockSpec(memory_space=p...  6.82 us
    pallas_call x1, Pallas kernels, pack(): pl.pallas_call(body, grid=(tiles,), in_specs=[pl.BlockSpec(place.shape, l...  6.36 us
    unnamed x43, local copies, waits for them, and re-layouts  5.46 us
    pallas_call x1, Pallas kernels, unpack(): pl.pallas_call(body, grid=(width // tile,), in_specs=[pl.BlockSpec(place....  5.23 us
  transfers between devices with their start and end apart: 30, of which 13 were waited for; matrix products, arithmetic and copies ran while one was open for 5% of the time, Pallas kernels for 14%

profile of v10, /device:TPU:0, one launch (start us, length us, event | category | flops | bytes accessed | tf_op | source)
XLA Modules:
  0.0 226.5 jit_solution(8931175752932274291)
XLA Ops:
  4.2 4.6 %collective-permute-start.5 = (bf16[2,64,8192]{2,1,0:T(8,128)(2,1)S(1)}, bf16[2,64,8192]{2,1,0:T(8,128)(2,1)}, u32[]{:S(2)}, u32[]{:S(2)}) collective-permute-start(bf16[2,64,8192]{2,1,0:T(8,128)(2,1)S(1)} %constant_dynamic-update-slice_fusion), channel_id=1, source_target_pairs={{0,4},{1,5},{2,6},{3,7},{4,0},{5,1},{6,2},{7,3},{8,12},{9,13},{10,... | collective-permute-start | bytes 6291464 | tf_op jit(solution)/shard_map/ppermute | solution.py:301
  9.5 6.4 %shard_map.85 = (bf16[1,2,64,8192]{3,2,1,0:T(8,128)(2,1)S(1)}, bf16[1,2,64,8192]{3,2,1,0:T(8,128)(2,1)S(1)}, bf16[2,2,16,8192]{3,2,1,0:T(8,128)(2,1)S(1)}, bf16[...) custom-call(bf16[256,128]{1,0:T(8,128)(2,1)S(1)} %fusion.1.place_ref, bf16[128,8192]{1,0:T(8,128)(2,1)} %x_in.1, ...), custom_call_target="tpu_custom_call" | custom-call | tf_op jit(solution)/shard_map/pallas_call | solution.py:107
  18.4 21.9 %collective-permute-done.1 = bf16[2,2,16,8192]{3,2,1,0:T(8,128)(2,1)S(1)} collective-permute-done((bf16[2,2,16,8192]{3,2,1,0:T(8,128)(2,1)S(1)}, bf16[2,2,16,8192]{3,2,1,0:T(8,128)(2,1)S(1)}, u32[]{:S(2)}, u32[]{:S(2)}) %collective-permute-start.1) | collective-permute-done | bytes 1048608 | tf_op jit(solution)/shard_map/ppermute | solution.py:301
  45.7 3.6 %collective-permute-start.11 = (bf16[2,64,8192]{2,1,0:T(8,128)(2,1)}, bf16[2,64,8192]{2,1,0:T(8,128)(2,1)}, u32[]{:S(2)}, u32[]{:S(2)}) collective-permute-start(bf16[2,64,8192]{2,1,0:T(8,128)(2,1)} %pad_maximum_fusion.refs_0_), channel_id=1, source_target_pairs={{0,4},{1,5},{2,6},{3,7},{12,8},{13,9},{14,10},{15,11},{16,20},{17,... | collective-permute-start | bytes 6291464 | tf_op jit(solution)/shard_map/ppermute | solution.py:301
  50.7 4.2 %collective-permute-done.5.refs_4_ = bf16[2,64,8192]{2,1,0:T(8,128)(2,1)} collective-permute-done((bf16[2,64,8192]{2,1,0:T(8,128)(2,1)S(1)}, bf16[2,64,8192]{2,1,0:T(8,128)(2,1)}, u32[]{:S(2)}, u32[]{:S(2)}) %collective-permute-start.5) | collective-permute-done | bytes 2097184 | tf_op jit(solution)/shard_map/ppermute | solution.py:301
  56.9 6.9 %collective-permute-done.2 = bf16[2,2,16,8192]{3,2,1,0:T(8,128)(2,1)S(1)} collective-permute-done((bf16[2,2,16,8192]{3,2,1,0:T(8,128)(2,1)S(1)}, bf16[2,2,16,8192]{3,2,1,0:T(8,128)(2,1)S(1)}, u32[]{:S(2)}, u32[]{:S(2)}) %collective-permute-start.2) | collective-permute-done | bytes 1048608 | tf_op jit(solution)/shard_map/ppermute | solution.py:301
  67.2 3.0 %pad_maximum_fusion.1.refs_0_.refs_1_ = bf16[2,64,8192]{2,1,0:T(8,128)(2,1)} fusion(bf16[2,16,8192]{2,1,0:T(8,128)(2,1)} %bitcast.11, bf16[2,16,8192]{2,1,0:T(8,128)(2,1)} %get-tuple-element.74, bf16[2,16,8192]{2,1,0:T(8,128)(2,1)} %get-tuple-element.72, bf16[2,16,8192]{2,1,0:T(8,128)(2,1)} %get-tuple-element.70), kind=kLoop, calls=%fused_computation.1 | loop fusion | flops 8388608 | bytes 4194304 | tf_op jit(solution)/shard_map/concatenate | solution.py:358
  70.1 5.3 %shard_map.86 = (bf16[64,8192]{1,0:T(8,128)(2,1)S(1)}, bf16[64,8192]{1,0:T(8,128)(2,1)S(1)}, bf16[64,8192]{1,0:T(8,128)(2,1)S(1)}) custom-call(s32[1]{0:T(128)} %bitcast.1.end_ref, bf16[2,64,8192]{2,1,0:T(8,128)(2,1)} %pad_maximum_fusion.1.refs_0_.refs_1_, bf16[2,64,8192]{2,1,0:T(8,128)(2,1)} %collective-permute-done.8.refs_1_), custom_call_target="tpu_custom_call" | custom-call | tf_op jit(solution)/shard_map/pallas_call | solution.py:200
  75.4 23.1 %collective-permute-done.11.refs_4_ = bf16[2,64,8192]{2,1,0:T(8,128)(2,1)} collective-permute-done((bf16[2,64,8192]{2,1,0:T(8,128)(2,1)}, bf16[2,64,8192]{2,1,0:T(8,128)(2,1)}, u32[]{:S(2)}, u32[]{:S(2)}) %collective-permute-start.11) | collective-permute-done | bytes 2097184 | tf_op jit(solution)/shard_map/ppermute | solution.py:301
  98.5 2.5 %collective-permute-done.10.refs_3_ = bf16[2,64,8192]{2,1,0:T(8,128)(2,1)} collective-permute-done((bf16[2,64,8192]{2,1,0:T(8,128)(2,1)}, bf16[2,64,8192]{2,1,0:T(8,128)(2,1)}, u32[]{:S(2)}, u32[]{:S(2)}) %collective-permute-start.10) | collective-permute-done | bytes 2097184 | tf_op jit(solution)/shard_map/ppermute | solution.py:301
  101.0 7.6 %shard_map.87 = (bf16[64,8192]{1,0:T(8,128)(2,1)S(1)}, bf16[64,8192]{1,0:T(8,128)(2,1)S(1)}, bf16[64,8192]{1,0:T(8,128)(2,1)S(1)}, bf16[64,8192]{1,0:T(8,128)(2,1)S(1)}) custom-call(s32[1]{0:T(128)} %bitcast.1.end_ref, bf16[2,64,8192]{2,1,0:T(8,128)(2,1)} %pad_maximum_fusion.refs_0_, bf16[2,64,8192]{2,1,0:T(8,128)(2,1)} %pad_maximum_fusion.1.refs_0_.refs_1_, ...), custom_call_target="tpu_custom_call" | custom-call | tf_op jit(solution)/shard_map/pallas_call | solution.py:200
  108.6 5.0 %collective-permute-start.12 = (bf16[64,8192]{1,0:T(8,128)(2,1)S(1)}, bf16[64,8192]{1,0:T(8,128)(2,1)S(1)}, u32[]{:S(2)}, u32[]{:S(2)}) collective-permute-start(bf16[64,8192]{1,0:T(8,128)(2,1)S(1)} %get-tuple-element.46), channel_id=1, source_target_pairs={{0,4},{1,5},{2,6},{3,7},{4,0},{5,1},{6,2},{7,3},{8,12},{9,13},{10,... | collective-permute-start | bytes 3145736 | tf_op jit(solution)/shard_map/ppermute | solution.py:301
  114.4 4.7 %collective-permute-start.20 = (bf16[64,8192]{1,0:T(8,128)(2,1)S(1)}, bf16[64,8192]{1,0:T(8,128)(2,1)S(1)}, u32[]{:S(2)}, u32[]{:S(2)}) collective-permute-start(bf16[64,8192]{1,0:T(8,128)(2,1)S(1)} %get-tuple-element.59), channel_id=1, source_target_pairs={{0,4},{1,5},{2,6},{3,7},{12,8},{13,9},{14,10},{15,11},{16,20},{17,... | collective-permute-start | bytes 3145736 | tf_op jit(solution)/shard_map/ppermute | solution.py:301
  120.1 17.2 %collective-permute-done.12.refs_9_ = bf16[64,8192]{1,0:T(8,128)(2,1)S(1)} collective-permute-done((bf16[64,8192]{1,0:T(8,128)(2,1)S(1)}, bf16[64,8192]{1,0:T(8,128)(2,1)S(1)}, u32[]{:S(2)}, u32[]{:S(2)}) %collective-permute-start.12) | collective-permute-done | bytes 1048608 | tf_op jit(solution)/shard_map/ppermute | solution.py:301
  139.1 6.8 %shard_map.88 = (bf16[64,8192]{1,0:T(8,128)(2,1)S(1)}, bf16[64,8192]{1,0:T(8,128)(2,1)}, bf16[64,8192]{1,0:T(8,128)(2,1)S(1)}, bf16[64,8192]{1,0:T(8,128)(2,1)S(...) custom-call(s32[1]{0:T(128)} %bitcast.1.end_ref, ...), custom_call_target="tpu_custom_call" | custom-call | tf_op jit(solution)/shard_map/pallas_call | solution.py:268
  148.4 7.2 %collective-permute-start.19 = (bf16[64,8192]{1,0:T(8,128)(2,1)S(1)}, bf16[64,8192]{1,0:T(8,128)(2,1)S(1)}, u32[]{:S(2)}, u32[]{:S(2)}) collective-permute-start(bf16[64,8192]{1,0:T(8,128)(2,1)S(1)} %add_convert_fusion.2), channel_id=1, source_target_pairs={{0,4},{1,5},{2,6},{3,7},{4,0},{5,1},{6,2},{7,3},{8,12},{9,13},{10,... | collective-permute-start | bytes 3145736 | tf_op jit(solution)/shard_map/ppermute | solution.py:301
  155.6 4.1 %collective-permute-done.20 = bf16[64,8192]{1,0:T(8,128)(2,1)S(1)} collective-permute-done((bf16[64,8192]{1,0:T(8,128)(2,1)S(1)}, bf16[64,8192]{1,0:T(8,128)(2,1)S(1)}, u32[]{:S(2)}, u32[]{:S(2)}) %collective-permute-start.20) | collective-permute-done | bytes 1048608 | tf_op jit(solution)/shard_map/ppermute | solution.py:301
  161.2 10.9 %collective-permute-done.15.refs_2_ = bf16[64,8192]{1,0:T(8,128)(2,1)S(1)} collective-permute-done((bf16[64,8192]{1,0:T(8,128)(2,1)S(1)}, bf16[64,8192]{1,0:T(8,128)(2,1)S(1)}, u32[]{:S(2)}, u32[]{:S(2)}) %collective-permute-start.15) | collective-permute-done | bytes 1048608 | tf_op jit(solution)/shard_map/ppermute | solution.py:301
  173.5 7.2 %collective-permute-start.23 = (bf16[64,8192]{1,0:T(8,128)(2,1)S(1)}, bf16[64,8192]{1,0:T(8,128)(2,1)S(1)}, u32[]{:S(2)}, u32[]{:S(2)}) collective-permute-start(bf16[64,8192]{1,0:T(8,128)(2,1)S(1)} %add_convert_fusion), channel_id=1, source_target_pairs={{0,4},{1,5},{2,6},{3,7},{4,0},{5,1},{6,2},{7,3},{8,12},{9,13},{10,... | collective-permute-start | bytes 3145736 | tf_op jit(solution)/shard_map/ppermute | solution.py:301
  180.7 7.6 %collective-permute-done.16 = bf16[64,8192]{1,0:T(8,128)(2,1)} collective-permute-done((bf16[64,8192]{1,0:T(8,128)(2,1)S(1)}, bf16[64,8192]{1,0:T(8,128)(2,1)}, u32[]{:S(2)}, u32[]{:S(2)}) %collective-permute-start.16) | collective-permute-done | bytes 1048608 | tf_op jit(solution)/shard_map/ppermute | solution.py:301
  189.5 12.0 %collective-permute-done.23 = bf16[64,8192]{1,0:T(8,128)(2,1)S(1)} collective-permute-done((bf16[64,8192]{1,0:T(8,128)(2,1)S(1)}, bf16[64,8192]{1,0:T(8,128)(2,1)S(1)}, u32[]{:S(2)}, u32[]{:S(2)}) %collective-permute-start.23) | collective-permute-done | bytes 1048608 | tf_op jit(solution)/shard_map/ppermute | solution.py:301
  209.5 4.8 %collective-permute-start.27 = (f32[8,128]{1,0:T(8,128)S(1)}, f32[8,128]{1,0:T(8,128)S(1)}, u32[]{:S(2)}, u32[]{:S(2)}) collective-permute-start(f32[8,128]{1,0:T(8,128)S(1)} %add_add_fusion.1), channel_id=1, source_target_pairs={{0,4},{1,5},{2,6},{3,7},{4,0},{5,1},{6,2},{7,3},{8,12},{9,13},{10,... | collective-permute-start | bytes 12296 | tf_op jit(solution)/shard_map/ppermute | solution.py:301
  217.1 5.2 %shard_map.89 = bf16[128,8192]{1,0:T(8,128)(2,1)} custom-call(bf16[128,256]{1,0:T(8,128)(2,1)S(1)} %fusion.place_ref, bf16[64,8192]{1,0:T(8,128)(2,1)} %copy-done.10, bf16[64,8192]{1,0:T(8,128)(2,1)} %collective-permute-done.14.refs_1_, bf16[64,8192]{1,0:T(8,128)(2,1)S(1)} %collective-permute-done.15.refs_2_, bf16[64,8192]{1,0:T(8,128)(2,1)} %collective-permute-done.17.refs_3_), custom_call_target="tpu_custom_call" | custom-call | tf_op jit(solution)/shard_map/pallas_call | solution.py:126
  223.7 2.8 %multiply_bitcast_fusion = (f32[1,64,8192]{2,1,0:T(8,128)}, f32[1,64,8192]{2,1,0:T(8,128)}) fusion(f32[]{:T(128)} %bitcast.12, bf16[64,8192]{1,0:T(8,128)(2,1)S(1)} %copy-done.18, f32[64,8192]{1,0:T(8,128)S(1)} %get-tuple-element.57, bf16[64,8192]{1,0:T(8,128)(2,1)S(1)} %copy-done.16, bf16[64,8192]{1,0:T(8,128)(2,1)S(1)} %copy-done.14, ...), kind=kLoop, calls=%fused_computation.2 | loop fusion | flops 5242880 | bytes 12582916 | tf_op jit(solution)/shard_map/broadcast_in_dim | solution.py:37
  (111 shorter events, 38.8 us)
Async XLA Ops:
  2.2 47.1 %collective-permute-start.8 = (bf16[2,64,8192]{2,1,0:T(8,128)(2,1)S(1)}, bf16[2,64,8192]{2,1,0:T(8,128)(2,1)}, u32[]{:S(2)}, u32[]{:S(2)}) collective-permute-start(bf16[2,64,8192]{2,1,0:T(8,128)(2,1)S(1)} %constant_dynamic-update-slice_fusion), channel_id=1, source_target_pairs={{4,8},{5,9},{6,10},{7,11},{8,4},{9,5},{10,6},{11,7},{20,24},{21,25... | collective-permute-start | bytes 6291464 | tf_op jit(solution)/shard_map/ppermute | solution.py:301
  4.2 50.7 %collective-permute-start.5 = (bf16[2,64,8192]{2,1,0:T(8,128)(2,1)S(1)}, bf16[2,64,8192]{2,1,0:T(8,128)(2,1)}, u32[]{:S(2)}, u32[]{:S(2)}) collective-permute-start(bf16[2,64,8192]{2,1,0:T(8,128)(2,1)S(1)} %constant_dynamic-update-slice_fusion), channel_id=1, source_target_pairs={{0,4},{1,5},{2,6},{3,7},{4,0},{5,1},{6,2},{7,3},{8,12},{9,13},{10,... | collective-permute-start | bytes 6291464 | tf_op jit(solution)/shard_map/ppermute | solution.py:301
  15.9 24.4 %collective-permute-start.1 = (bf16[2,2,16,8192]{3,2,1,0:T(8,128)(2,1)S(1)}, bf16[2,2,16,8192]{3,2,1,0:T(8,128)(2,1)S(1)}, u32[]{:S(2)}, u32[]{:S(2)}) collective-permute-start(bf16[2,2,16,8192]{3,2,1,0:T(8,128)(2,1)S(1)} %get-tuple-element.39), channel_id=1, source_target_pairs={{0,2},{1,3},{2,0},{3,1},{4,6},{5,7},{6,4},{7,5},{8,10},{9,11},{10,... | collective-permute-start | bytes 3145736 | tf_op jit(solution)/shard_map/ppermute | solution.py:301
  17.5 24.5 %collective-permute-start = (bf16[1,2,64,8192]{3,2,1,0:T(8,128)(2,1)S(1)}, bf16[1,2,64,8192]{3,2,1,0:T(8,128)(2,1)S(1)}, u32[]{:S(2)}, u32[]{:S(2)}) collective-permute-start(bf16[1,2,64,8192]{3,2,1,0:T(8,128)(2,1)S(1)} %get-tuple-element.36), channel_id=1, source_target_pairs={{0,1},{1,0},{2,3},{3,2},{4,5},{5,4},{6,7},{7,6},{8,9},{9,8},{10,11... | collective-permute-start | bytes 6291464 | tf_op jit(solution)/shard_map/ppermute | solution.py:301
  40.3 23.5 %collective-permute-start.2 = (bf16[2,2,16,8192]{3,2,1,0:T(8,128)(2,1)S(1)}, bf16[2,2,16,8192]{3,2,1,0:T(8,128)(2,1)S(1)}, u32[]{:S(2)}, u32[]{:S(2)}) collective-permute-start(bf16[2,2,16,8192]{3,2,1,0:T(8,128)(2,1)S(1)} %get-tuple-element.40), channel_id=1, source_target_pairs={{0,2},{1,3},{2,0},{3,1},{4,6},{5,7},{6,4},{7,5},{8,10},{9,11},{10,... | collective-permute-start | bytes 3145736 | tf_op jit(solution)/shard_map/ppermute | solution.py:301
  45.7 52.7 %collective-permute-start.11 = (bf16[2,64,8192]{2,1,0:T(8,128)(2,1)}, bf16[2,64,8192]{2,1,0:T(8,128)(2,1)}, u32[]{:S(2)}, u32[]{:S(2)}) collective-permute-start(bf16[2,64,8192]{2,1,0:T(8,128)(2,1)} %pad_maximum_fusion.refs_0_), channel_id=1, source_target_pairs={{0,4},{1,5},{2,6},{3,7},{12,8},{13,9},{14,10},{15,11},{16,20},{17,... | collective-permute-start | bytes 6291464 | tf_op jit(solution)/shard_map/ppermute | solution.py:301
  49.4 51.6 %collective-permute-start.10 = (bf16[2,64,8192]{2,1,0:T(8,128)(2,1)}, bf16[2,64,8192]{2,1,0:T(8,128)(2,1)}, u32[]{:S(2)}, u32[]{:S(2)}) collective-permute-start(bf16[2,64,8192]{2,1,0:T(8,128)(2,1)} %collective-permute-done.8.refs_1_), channel_id=1, source_target_pairs={{4,0},{5,1},{6,2},{7,3},{8,12},{9,13},{10,14},{11,15},{20,16},{21,... | collective-permute-start | bytes 6291464 | tf_op jit(solution)/shard_map/ppermute | solution.py:301
  54.9 46.1 %collective-permute-start.9 = (bf16[2,64,8192]{2,1,0:T(8,128)(2,1)}, bf16[2,64,8192]{2,1,0:T(8,128)(2,1)}, u32[]{:S(2)}, u32[]{:S(2)}) collective-permute-start(bf16[2,64,8192]{2,1,0:T(8,128)(2,1)} %collective-permute-done.5.refs_4_), channel_id=1, source_target_pairs={{4,8},{5,9},{6,10},{7,11},{8,4},{9,5},{10,6},{11,7},{20,24},{21,25... | collective-permute-start | bytes 6291464 | tf_op jit(solution)/shard_map/ppermute | solution.py:301
  64.9 54.9 %collective-permute-start.3 = (bf16[2,2,32,8192]{3,2,1,0:T(8,128)(2,1)}, bf16[2,2,32,8192]{3,2,1,0:T(8,128)(2,1)S(1)}, u32[]{:S(2)}, u32[]{:S(2)}) collective-permute-start(bf16[2,2,32,8192]{3,2,1,0:T(8,128)(2,1)} %get-tuple-element.41), channel_id=1, source_target_pairs={{0,2},{1,3},{2,0},{3,1},{4,6},{5,7},{6,4},{7,5},{8,10},{9,11},{10,... | collective-permute-start | bytes 6291464 | tf_op jit(solution)/shard_map/ppermute | solution.py:301
  108.6 28.7 %collective-permute-start.12 = (bf16[64,8192]{1,0:T(8,128)(2,1)S(1)}, bf16[64,8192]{1,0:T(8,128)(2,1)S(1)}, u32[]{:S(2)}, u32[]{:S(2)}) collective-permute-start(bf16[64,8192]{1,0:T(8,128)(2,1)S(1)} %get-tuple-element.46), channel_id=1, source_target_pairs={{0,4},{1,5},{2,6},{3,7},{4,0},{5,1},{6,2},{7,3},{8,12},{9,13},{10,... | collective-permute-start | bytes 3145736 | tf_op jit(solution)/shard_map/ppermute | solution.py:301
  113.6 23.6 %collective-permute-start.13 = (bf16[64,8192]{1,0:T(8,128)(2,1)S(1)}, bf16[64,8192]{1,0:T(8,128)(2,1)S(1)}, u32[]{:S(2)}, u32[]{:S(2)}) collective-permute-start(bf16[64,8192]{1,0:T(8,128)(2,1)S(1)} %get-tuple-element.47), channel_id=1, source_target_pairs={{4,8},{5,9},{6,10},{7,11},{8,4},{9,5},{10,6},{11,7},{20,24},{21,25... | collective-permute-start | bytes 3145736 | tf_op jit(solution)/shard_map/ppermute | solution.py:301
  114.4 45.4 %collective-permute-start.20 = (bf16[64,8192]{1,0:T(8,128)(2,1)S(1)}, bf16[64,8192]{1,0:T(8,128)(2,1)S(1)}, u32[]{:S(2)}, u32[]{:S(2)}) collective-permute-start(bf16[64,8192]{1,0:T(8,128)(2,1)S(1)} %get-tuple-element.59), channel_id=1, source_target_pairs={{0,4},{1,5},{2,6},{3,7},{12,8},{13,9},{14,10},{15,11},{16,20},{17,... | collective-permute-start | bytes 3145736 | tf_op jit(solution)/shard_map/ppermute | solution.py:301
  119.1 42.1 %collective-permute-start.21 = (bf16[64,8192]{1,0:T(8,128)(2,1)S(1)}, bf16[64,8192]{1,0:T(8,128)(2,1)S(1)}, u32[]{:S(2)}, u32[]{:S(2)}) collective-permute-start(bf16[64,8192]{1,0:T(8,128)(2,1)S(1)} %get-tuple-element.59), channel_id=1, source_target_pairs={{4,8},{5,9},{6,10},{7,11},{8,4},{9,5},{10,6},{11,7},{20,24},{21,25... | collective-permute-start | bytes 3145736 | tf_op jit(solution)/shard_map/ppermute | solution.py:301
  120.0 17.5 %collective-permute-start.4 = (bf16[1,2,32,8192]{3,2,1,0:T(8,128)(2,1)S(1)}, bf16[1,2,32,8192]{3,2,1,0:T(8,128)(2,1)S(1)}, u32[]{:S(2)}, u32[]{:S(2)}) collective-permute-start(bf16[1,2,32,8192]{3,2,1,0:T(8,128)(2,1)S(1)} %slice.40), channel_id=1, source_target_pairs={{0,1},{1,0},{2,3},{3,2},{4,5},{5,4},{6,7},{7,6},{8,9},{9,8},{10,11... | collective-permute-start | bytes 3145736 | tf_op jit(solution)/shard_map/ppermute | solution.py:301
  146.0 26.1 %collective-permute-start.15 = (bf16[64,8192]{1,0:T(8,128)(2,1)S(1)}, bf16[64,8192]{1,0:T(8,128)(2,1)S(1)}, u32[]{:S(2)}, u32[]{:S(2)}) collective-permute-start(bf16[64,8192]{1,0:T(8,128)(2,1)S(1)} %get-tuple-element.51), channel_id=1, source_target_pairs={{0,2},{1,3},{2,0},{3,1},{4,6},{5,7},{6,4},{7,5},{8,10},{9,11},{10,... | collective-permute-start | bytes 3145736 | tf_op jit(solution)/shard_map/ppermute | solution.py:301
  147.5 33.2 %collective-permute-start.18 = (bf16[64,8192]{1,0:T(8,128)(2,1)S(1)}, bf16[64,8192]{1,0:T(8,128)(2,1)S(1)}, u32[]{:S(2)}, u32[]{:S(2)}) collective-permute-start(bf16[64,8192]{1,0:T(8,128)(2,1)S(1)} %add_convert_fusion.3), channel_id=1, source_target_pairs={{4,8},{5,9},{6,10},{7,11},{8,4},{9,5},{10,6},{11,7},{20,24},{21,25... | collective-permute-start | bytes 3145736 | tf_op jit(solution)/shard_map/ppermute | solution.py:301
  148.4 39.9 %collective-permute-start.19 = (bf16[64,8192]{1,0:T(8,128)(2,1)S(1)}, bf16[64,8192]{1,0:T(8,128)(2,1)S(1)}, u32[]{:S(2)}, u32[]{:S(2)}) collective-permute-start(bf16[64,8192]{1,0:T(8,128)(2,1)S(1)} %add_convert_fusion.2), channel_id=1, source_target_pairs={{0,4},{1,5},{2,6},{3,7},{4,0},{5,1},{6,2},{7,3},{8,12},{9,13},{10,... | collective-permute-start | bytes 3145736 | tf_op jit(solution)/shard_map/ppermute | solution.py:301
  159.7 28.5 %collective-permute-start.16 = (bf16[64,8192]{1,0:T(8,128)(2,1)S(1)}, bf16[64,8192]{1,0:T(8,128)(2,1)}, u32[]{:S(2)}, u32[]{:S(2)}) collective-permute-start(bf16[64,8192]{1,0:T(8,128)(2,1)S(1)} %get-tuple-element.52), channel_id=1, source_target_pairs={{0,2},{1,3},{2,0},{3,1},{4,6},{5,7},{6,4},{7,5},{8,10},{9,11},{10,... | collective-permute-start | bytes 3145736 | tf_op jit(solution)/shard_map/ppermute | solution.py:301
  172.3 17.1 %collective-permute-start.22 = (bf16[64,8192]{1,0:T(8,128)(2,1)S(1)}, bf16[64,8192]{1,0:T(8,128)(2,1)S(1)}, u32[]{:S(2)}, u32[]{:S(2)}) collective-permute-start(bf16[64,8192]{1,0:T(8,128)(2,1)S(1)} %add_convert_fusion.1), channel_id=1, source_target_pairs={{4,8},{5,9},{6,10},{7,11},{8,4},{9,5},{10,6},{11,7},{20,24},{21,25... | collective-permute-start | bytes 3145736 | tf_op jit(solution)/shard_map/ppermute | solution.py:301
  173.5 27.9 %collective-permute-start.23 = (bf16[64,8192]{1,0:T(8,128)(2,1)S(1)}, bf16[64,8192]{1,0:T(8,128)(2,1)S(1)}, u32[]{:S(2)}, u32[]{:S(2)}) collective-permute-start(bf16[64,8192]{1,0:T(8,128)(2,1)S(1)} %add_convert_fusion), channel_id=1, source_target_pairs={{0,4},{1,5},{2,6},{3,7},{4,0},{5,1},{6,2},{7,3},{8,12},{9,13},{10,... | collective-permute-start | bytes 3145736 | tf_op jit(solution)/shard_map/ppermute | solution.py:301
  180.7 36.4 %collective-permute-start.14 = (bf16[64,8192]{1,0:T(8,128)(2,1)}, bf16[64,8192]{1,0:T(8,128)(2,1)}, u32[]{:S(2)}, u32[]{:S(2)}) collective-permute-start(bf16[64,8192]{1,0:T(8,128)(2,1)} %get-tuple-element.50), channel_id=1, source_target_pairs={{0,1},{1,0},{2,3},{3,2},{4,5},{5,4},{6,7},{7,6},{8,9},{9,8},{10,11... | collective-permute-start | bytes 3145736 | tf_op jit(solution)/shard_map/ppermute | solution.py:301
  188.3 28.8 %collective-permute-start.17 = (bf16[64,8192]{1,0:T(8,128)(2,1)}, bf16[64,8192]{1,0:T(8,128)(2,1)}, u32[]{:S(2)}, u32[]{:S(2)}) collective-permute-start(bf16[64,8192]{1,0:T(8,128)(2,1)} %collective-permute-done.16), channel_id=1, source_target_pairs={{0,1},{1,0},{2,3},{3,2},{4,5},{5,4},{6,7},{7,6},{8,9},{9,8},{10,11... | collective-permute-start | bytes 3145736 | tf_op jit(solution)/shard_map/ppermute | solution.py:301
  209.5 12.8 %collective-permute-start.27 = (f32[8,128]{1,0:T(8,128)S(1)}, f32[8,128]{1,0:T(8,128)S(1)}, u32[]{:S(2)}, u32[]{:S(2)}) collective-permute-start(f32[8,128]{1,0:T(8,128)S(1)} %add_add_fusion.1), channel_id=1, source_target_pairs={{0,4},{1,5},{2,6},{3,7},{4,0},{5,1},{6,2},{7,3},{8,12},{9,13},{10,... | collective-permute-start | bytes 12296 | tf_op jit(solution)/shard_map/ppermute | solution.py:301
  214.3 8.0 %collective-permute-start.28 = (f32[8,128]{1,0:T(8,128)S(1)}, f32[8,128]{1,0:T(8,128)S(1)}, u32[]{:S(2)}, u32[]{:S(2)}) collective-permute-start(f32[8,128]{1,0:T(8,128)S(1)} %add_add_fusion.1), channel_id=1, source_target_pairs={{0,8},{1,9},{2,10},{3,11},{4,12},{5,13},{6,14},{7,15},{8,0},{9,1},... | collective-permute-start | bytes 12296 | tf_op jit(solution)/shard_map/ppermute | solution.py:301
  (27 other events, 237.5 us)

commit v11 on v10

--- a/solution.py
+++ b/solution.py
@@ -115,23 +115,27 @@
     )(place, *in_hbm(acts, cotan))
 
 
-def unpack(place, blocks, tokens):
+def unpack(place, blocks, tokens, half, into=None):
     width = blocks[0].shape[1]
-    tile = min(width, 2048)
+    tile = min(width // 2, 2048)
+    first = half * (width // 2 // tile)
+    rest = () if into is None else (into,)
 
     def body(place_ref, *refs):
-        rows = jnp.concatenate([ref[...] for ref in refs[:-1]], axis=0)
+        rows = jnp.concatenate([ref[...] for ref in refs[:len(blocks)]], axis=0)
         refs[-1][...] = dot32(place_ref[...], rows).astype(BF16)
 
     return pl.pallas_call(
         body,
-        grid=(width // tile,),
+        grid=(width // 2 // tile,),
         in_specs=[pl.BlockSpec(place.shape, lambda i: (0, 0))]
-        + [pl.BlockSpec((b.shape[0], tile), lambda i: (0, i)) for b in blocks],
-        out_specs=pl.BlockSpec((tokens, tile), lambda i: (0, i)),
+        + [pl.BlockSpec((b.shape[0], tile), lambda i: (0, i + first)) for b in blocks]
+        + [pl.BlockSpec(memory_space=pl.ANY)] * len(rest),
+        out_specs=pl.BlockSpec((tokens, tile), lambda i: (0, i + first)),
         out_shape=jax.ShapeDtypeStruct((tokens, width), BF16),
+        input_output_aliases={1 + len(blocks): 0} if rest else {},
         compiler_params=kernel_params(),
-    )(place, *in_hbm(blocks[0]), *blocks[1:])
+    )(place, *in_hbm(blocks[0]), *blocks[1:], *rest)
 
 
 def corner(rows, first_rows, columns, first_columns):
@@ -176,15 +180,15 @@
                     for i in range(tiles):
                         copy(source, i).start()
 
-            sums = [jnp.zeros((total, rank), F32)] * 2
+            sums = jnp.zeros((2 * total, 2 * rank), F32)
             for i in range(tiles):
                 copy(rows_in[0], i).wait()
                 cut = pl.ds(i * tile, tile)
-                for k in range(2):
-                    sums[k] += dot32(tokens(k, cut), factor(k, cut), ROWS_OF)
-            for k in range(2):
-                left[k] = sums[k].T.astype(BF16)
-            inner[...] = sums[1].astype(BF16)
+                both = [jnp.concatenate([piece(k, cut) for k in range(2)], axis=0) for piece in (tokens, factor)]
+                sums += dot32(*both, ROWS_OF)
+            left[0] = sums[:total, :rank].T.astype(BF16)
+            inner[...] = sums[total:, rank:].astype(BF16)
+            left[1] = sums[total:, rank:].T.astype(BF16)
 
         cut = pl.ds(pl.multiple_of(step * tile, tile), tile)
         up_ref[...] = dot32(left[0], tokens(1, cut)).astype(BF16)
@@ -310,8 +314,7 @@
         around = [beside(m) for m in range(1, plane)]
         along = [[(i, (i // plane ^ m) * plane + i % plane) for i in range(ndevices)] for m in range(1, 4)]
         term = jnp.broadcast_to(term, (8, 128))
-        term = term + sum(send(term, pairs) for pairs in around)
-        term = after(term, dx_across[1])
+        term = term + sum(after([send(term, pairs) for pairs in around], half_acts))
         return (term + sum(after([send(term, pairs) for pairs in along], grad_acts)))[0, 0]
 
     down, up = pool_down_factors[0], pool_up_factors[0]
@@ -353,7 +356,7 @@
     rows3 = jnp.concatenate([r[0, :, :capacity] for r in stage3], axis=1)
     handed = send(rows3, inward)
     across2 = over_x(after(across2, across3[0]))
-    across10 = over_x(after(across10, across2[0]))
+    across10 = over_x(after(across10, across3[0]))
     rows2 = [r[0, :, capacity:2 * capacity] for r in (own_rows, beside_rows)] + [r[0] for r in across2]
     rows2 = jnp.concatenate(rows2, axis=1)
     stage10 = (own_rows, beside_rows) + across10
@@ -363,10 +366,10 @@
     up2, down2, dx_early = far_group(end_flag, (rows2,), (crossed,))
     rows3, rows2 = after((rows3, rows2), dx_early)
     up3, down3, dx_late, swapped = far_group(end_flag, (rows3, rows2), (far, outer), handed)
-    up2_in = send(up3, inward)
-    down3, swapped, up3 = send(down3, cross), send(swapped, swap), send(up3, cross)
-
-    swapped, down3 = lax.optimization_barrier((swapped, down3))
+    down3, swapped = send(down3, cross), send(swapped, swap)
+    up3, up2_in = send(up3, cross), send(up3, inward)
+
+    down3, swapped = lax.optimization_barrier((down3, swapped))
     dx_own, dx_beside, *dx_across, up1, down1, up0, down0 = near_groups(
         end_flag, stage10, pair, down, up, dx_late, dx_early, swapped, capacity,
         (2 * capacity, 2 * capacity, 0, 0),
@@ -377,12 +380,13 @@
 
     down2, down1 = add(down2, swapped), add(down1, down3)
     dx_across = [send(block, beside(2)) for block in dx_across]
-    up2_in, up3 = after((up2_in, up3), down2, down1, dx_across[0])
+    up3, up2_in = after((up3, up2_in), down2, down1, dx_across[0])
     down2, down1 = send(down2, cross), send(down1, swap)
     up2, up1 = send(add(up2, up2_in), cross), send(add(up1, up3), swap)
 
     back = [dx_own, send(dx_beside, beside(1)), dx_across[0], send(dx_across[1], beside(1))]
-    grad_acts = unpack(place_back.T, back, tokens)
+    half_acts = unpack(place_back.T, back, tokens, 0)
+    grad_acts = unpack(place_back.T, back, tokens, 1, half_acts)
     raw_up = up0 + up2.astype(F32) + up1.astype(F32)
     raw_down = down0 + down2.astype(F32) + down1.astype(F32)
     return (grad_acts,) + clipped(raw_down, raw_up, ndevices, add_up)

time: 227 us -> 236 us (1.040)
  waiting for transfers between devices: 114 us -> 122 us
    ppermute x30, waiting for transfers between devices: 114 us -> 122 us  [send(): return lax.ppermute(array, 'dp', pairs)]
    pallas_call x1 -> x2, Pallas kernels: 5.23 us -> 5.13 us  [unpack(): pl.pallas_call(body, grid=(width // 2 // tile,), in_specs=[pl.BlockSpec(p...]
  transfers between devices with their start and end apart: 30 -> 30, of which waited for: 13 -> 10; matrix products, arithmetic and copies ran while one was open for 5% -> 5% of each run, Pallas kernels for 14% -> 14%
where the time goes in v11:
time: 236 us
  waiting for transfers between devices  122 us (52%)
  starting transfers between devices  55.7 us (24%)
  Pallas kernels  33.3 us (14%)
  other arithmetic  11.4 us (5%)
  local copies, waits for them, and re-layouts  10.9 us (5%)
  between operations  3.05 us (1%)
    ppermute x30, waiting for transfers between devices, send(): return lax.ppermute(array, 'dp', pairs)  122 us
    ppermute x30, starting transfers between devices, send(): return lax.ppermute(array, 'dp', pairs)  55.7 us
    pallas_call x2, Pallas kernels, far_group(): pl.pallas_call(body, grid=(tiles,), in_specs=[pl.BlockSpec(memory_space=p...  15 us
    pallas_call x1, Pallas kernels, near_groups(): pl.pallas_call(body, grid=(tiles,), in_specs=[pl.BlockSpec(memory_space=p...  6.81 us
    pallas_call x1, Pallas kernels, pack(): pl.pallas_call(body, grid=(tiles,), in_specs=[pl.BlockSpec(place.shape, l...  6.36 us
    unnamed x43, local copies, waits for them, and re-layouts  6.3 us
    pallas_call x2, Pallas kernels, unpack(): pl.pallas_call(body, grid=(width // 2 // tile,), in_specs=[pl.BlockSpec(p...  5.13 us
  transfers between devices with their start and end apart: 30, of which 10 were waited for; matrix products, arithmetic and copies ran while one was open for 5% of the time, Pallas kernels for 14%

profile of v11, /device:TPU:0, one launch (start us, length us, event | category | flops | bytes accessed | tf_op | source)
XLA Modules:
  0.0 235.9 jit_solution(8281846839595711576)
XLA Ops:
  0.7 2.3 constant_dynamic-update-slice_fusion.1
  6.1 4.6 %collective-permute-start.4 = (bf16[2,64,8192]{2,1,0:T(8,128)(2,1)}, bf16[2,64,8192]{2,1,0:T(8,128)(2,1)}, u32[]{:S(2)}, u32[]{:S(2)}) collective-permute-start(bf16[2,64,8192]{2,1,0:T(8,128)(2,1)} %constant_dynamic-update-slice_fusion), channel_id=1, source_target_pairs={{0,4},{1,5},{2,6},{3,7},{4,0},{5,1},{6,2},{7,3},{8,12},{9,13},{10,... | collective-permute-start | bytes 6291464 | tf_op jit(solution)/shard_map/ppermute | solution.py:305
  11.4 6.4 %shard_map.85 = (bf16[1,2,64,8192]{3,2,1,0:T(8,128)(2,1)S(1)}, bf16[1,2,64,8192]{3,2,1,0:T(8,128)(2,1)S(1)}, bf16[2,2,16,8192]{3,2,1,0:T(8,128)(2,1)S(1)}, bf16[...) custom-call(bf16[256,128]{1,0:T(8,128)(2,1)S(1)} %fusion.1.place_ref, bf16[128,8192]{1,0:T(8,128)(2,1)} %x_in.1, ...), custom_call_target="tpu_custom_call" | custom-call | tf_op jit(solution)/shard_map/pallas_call | solution.py:107
  20.2 21.9 %collective-permute-done.1 = bf16[2,2,16,8192]{3,2,1,0:T(8,128)(2,1)S(1)} collective-permute-done((bf16[2,2,16,8192]{3,2,1,0:T(8,128)(2,1)S(1)}, bf16[2,2,16,8192]{3,2,1,0:T(8,128)(2,1)S(1)}, u32[]{:S(2)}, u32[]{:S(2)}) %collective-permute-start.1) | collective-permute-done | bytes 1048608 | tf_op jit(solution)/shard_map/ppermute | solution.py:305
  48.2 3.6 %collective-permute-start.11 = (bf16[2,64,8192]{2,1,0:T(8,128)(2,1)}, bf16[2,64,8192]{2,1,0:T(8,128)(2,1)}, u32[]{:S(2)}, u32[]{:S(2)}) collective-permute-start(bf16[2,64,8192]{2,1,0:T(8,128)(2,1)} %pad_maximum_fusion.refs_0_), channel_id=1, source_target_pairs={{0,4},{1,5},{2,6},{3,7},{12,8},{13,9},{14,10},{15,11},{16,20},{17,... | collective-permute-start | bytes 6291464 | tf_op jit(solution)/shard_map/ppermute | solution.py:305
  53.0 4.0 %collective-permute-done.4.refs_4_ = bf16[2,64,8192]{2,1,0:T(8,128)(2,1)} collective-permute-done((bf16[2,64,8192]{2,1,0:T(8,128)(2,1)}, bf16[2,64,8192]{2,1,0:T(8,128)(2,1)}, u32[]{:S(2)}, u32[]{:S(2)}) %collective-permute-start.4) | collective-permute-done | bytes 2097184 | tf_op jit(solution)/shard_map/ppermute | solution.py:305
  59.1 9.1 %collective-permute-done.6 = bf16[2,2,16,8192]{3,2,1,0:T(8,128)(2,1)S(1)} collective-permute-done((bf16[2,2,16,8192]{3,2,1,0:T(8,128)(2,1)S(1)}, bf16[2,2,16,8192]{3,2,1,0:T(8,128)(2,1)S(1)}, u32[]{:S(2)}, u32[]{:S(2)}) %collective-permute-start.6) | collective-permute-done | bytes 1048608 | tf_op jit(solution)/shard_map/ppermute | solution.py:305
  69.3 2.2 collective-permute-done.7
  71.6 3.0 %pad_maximum_fusion.1.refs_0_.refs_1_ = bf16[2,64,8192]{2,1,0:T(8,128)(2,1)} fusion(bf16[2,16,8192]{2,1,0:T(8,128)(2,1)} %bitcast.11, bf16[2,16,8192]{2,1,0:T(8,128)(2,1)} %get-tuple-element.78, bf16[2,16,8192]{2,1,0:T(8,128)(2,1)} %get-tuple-element.76, bf16[2,16,8192]{2,1,0:T(8,128)(2,1)} %get-tuple-element.74), kind=kLoop, calls=%fused_computation.1 | loop fusion | flops 8388608 | bytes 4194304 | tf_op jit(solution)/shard_map/concatenate | solution.py:361
  74.6 6.0 %shard_map.86 = (bf16[64,8192]{1,0:T(8,128)(2,1)S(1)}, bf16[64,8192]{1,0:T(8,128)(2,1)S(1)}, bf16[64,8192]{1,0:T(8,128)(2,1)S(1)}) custom-call(s32[1]{0:T(128)} %bitcast.1.end_ref, bf16[2,64,8192]{2,1,0:T(8,128)(2,1)} %pad_maximum_fusion.1.refs_0_.refs_1_, bf16[2,64,8192]{2,1,0:T(8,128)(2,1)} %collective-permute-done.8.refs_1_), custom_call_target="tpu_custom_call" | custom-call | tf_op jit(solution)/shard_map/pallas_call | solution.py:204
  80.5 20.0 %collective-permute-done.11.refs_4_ = bf16[2,64,8192]{2,1,0:T(8,128)(2,1)} collective-permute-done((bf16[2,64,8192]{2,1,0:T(8,128)(2,1)}, bf16[2,64,8192]{2,1,0:T(8,128)(2,1)}, u32[]{:S(2)}, u32[]{:S(2)}) %collective-permute-start.11) | collective-permute-done | bytes 2097184 | tf_op jit(solution)/shard_map/ppermute | solution.py:305
  100.5 2.5 %collective-permute-done.10.refs_3_ = bf16[2,64,8192]{2,1,0:T(8,128)(2,1)} collective-permute-done((bf16[2,64,8192]{2,1,0:T(8,128)(2,1)}, bf16[2,64,8192]{2,1,0:T(8,128)(2,1)}, u32[]{:S(2)}, u32[]{:S(2)}) %collective-permute-start.10) | collective-permute-done | bytes 2097184 | tf_op jit(solution)/shard_map/ppermute | solution.py:305
  103.0 9.0 %shard_map.87 = (bf16[64,8192]{1,0:T(8,128)(2,1)S(1)}, bf16[64,8192]{1,0:T(8,128)(2,1)S(1)}, bf16[64,8192]{1,0:T(8,128)(2,1)S(1)}, bf16[64,8192]{1,0:T(8,128)(2,1)S(1)}) custom-call(s32[1]{0:T(128)} %bitcast.1.end_ref, bf16[2,64,8192]{2,1,0:T(8,128)(2,1)} %pad_maximum_fusion.refs_0_, bf16[2,64,8192]{2,1,0:T(8,128)(2,1)} %pad_maximum_fusion.1.refs_0_.refs_1_, ...), custom_call_target="tpu_custom_call" | custom-call | tf_op jit(solution)/shard_map/pallas_call | solution.py:204
  113.0 7.8 %collective-permute-start.13 = (bf16[64,8192]{1,0:T(8,128)(2,1)S(1)}, bf16[64,8192]{1,0:T(8,128)(2,1)S(1)}, u32[]{:S(2)}, u32[]{:S(2)}) collective-permute-start(bf16[64,8192]{1,0:T(8,128)(2,1)S(1)} %get-tuple-element.49), channel_id=1, source_target_pairs={{0,4},{1,5},{2,6},{3,7},{4,0},{5,1},{6,2},{7,3},{8,12},{9,13},{10,... | collective-permute-start | bytes 3145736 | tf_op jit(solution)/shard_map/ppermute | solution.py:305
  121.7 3.6 %collective-permute-start.21 = (bf16[64,8192]{1,0:T(8,128)(2,1)S(1)}, bf16[64,8192]{1,0:T(8,128)(2,1)S(1)}, u32[]{:S(2)}, u32[]{:S(2)}) collective-permute-start(bf16[64,8192]{1,0:T(8,128)(2,1)S(1)} %get-tuple-element.61), channel_id=1, source_target_pairs={{0,4},{1,5},{2,6},{3,7},{12,8},{13,9},{14,10},{15,11},{16,20},{17,... | collective-permute-start | bytes 3145736 | tf_op jit(solution)/shard_map/ppermute | solution.py:305
  125.3 19.1 %collective-permute-done.13.refs_9_ = bf16[64,8192]{1,0:T(8,128)(2,1)S(1)} collective-permute-done((bf16[64,8192]{1,0:T(8,128)(2,1)S(1)}, bf16[64,8192]{1,0:T(8,128)(2,1)S(1)}, u32[]{:S(2)}, u32[]{:S(2)}) %collective-permute-start.13) | collective-permute-done | bytes 1048608 | tf_op jit(solution)/shard_map/ppermute | solution.py:305
  146.0 6.8 %shard_map.88 = (bf16[64,8192]{1,0:T(8,128)(2,1)S(1)}, bf16[64,8192]{1,0:T(8,128)(2,1)}, bf16[64,8192]{1,0:T(8,128)(2,1)S(1)}, bf16[64,8192]{1,0:T(8,128)(2,1)S(...) custom-call(s32[1]{0:T(128)} %bitcast.1.end_ref, ...), custom_call_target="tpu_custom_call" | custom-call | tf_op jit(solution)/shard_map/pallas_call | solution.py:272
  156.1 11.6 %collective-permute-start.19 = (bf16[64,8192]{1,0:T(8,128)(2,1)S(1)}, bf16[64,8192]{1,0:T(8,128)(2,1)S(1)}, u32[]{:S(2)}, u32[]{:S(2)}) collective-permute-start(bf16[64,8192]{1,0:T(8,128)(2,1)S(1)} %add_convert_fusion.2), channel_id=1, source_target_pairs={{0,4},{1,5},{2,6},{3,7},{4,0},{5,1},{6,2},{7,3},{8,12},{9,13},{10,... | collective-permute-start | bytes 3145736 | tf_op jit(solution)/shard_map/ppermute | solution.py:305
  167.7 27.3 %collective-permute-done.15.refs_2_ = bf16[64,8192]{1,0:T(8,128)(2,1)S(1)} collective-permute-done((bf16[64,8192]{1,0:T(8,128)(2,1)S(1)}, bf16[64,8192]{1,0:T(8,128)(2,1)S(1)}, u32[]{:S(2)}, u32[]{:S(2)}) %collective-permute-start.15) | collective-permute-done | bytes 1048608 | tf_op jit(solution)/shard_map/ppermute | solution.py:305
  196.4 3.2 %collective-permute-start.23 = (bf16[64,8192]{1,0:T(8,128)(2,1)S(1)}, bf16[64,8192]{1,0:T(8,128)(2,1)S(1)}, u32[]{:S(2)}, u32[]{:S(2)}) collective-permute-start(bf16[64,8192]{1,0:T(8,128)(2,1)S(1)} %add_convert_fusion), channel_id=1, source_target_pairs={{0,4},{1,5},{2,6},{3,7},{4,0},{5,1},{6,2},{7,3},{8,12},{9,13},{10,... | collective-permute-start | bytes 3145736 | tf_op jit(solution)/shard_map/ppermute | solution.py:305
  201.3 14.0 %collective-permute-done.23 = bf16[64,8192]{1,0:T(8,128)(2,1)S(1)} collective-permute-done((bf16[64,8192]{1,0:T(8,128)(2,1)S(1)}, bf16[64,8192]{1,0:T(8,128)(2,1)S(1)}, u32[]{:S(2)}, u32[]{:S(2)}) %collective-permute-start.23) | collective-permute-done | bytes 1048608 | tf_op jit(solution)/shard_map/ppermute | solution.py:305
  220.8 2.6 %shard_map.89.refs_4_ = bf16[128,8192]{1,0:T(8,128)(2,1)} custom-call(bf16[128,256]{1,0:T(8,128)(2,1)S(1)} %fusion.place_ref, bf16[64,8192]{1,0:T(8,128)(2,1)} %copy-done.10, bf16[64,8192]{1,0:T(8,128)(2,1)} %collective-permute-done.14.refs_1_, bf16[64,8192]{1,0:T(8,128)(2,1)S(1)} %collective-permute-done.15.refs_2_, ...), custom_call_target="tpu_custom_call" | custom-call | tf_op jit(solution)/shard_map/pallas_call | solution.py:128
  227.9 2.6 %shard_map.90 = bf16[128,8192]{1,0:T(8,128)(2,1)} custom-call(bf16[128,256]{1,0:T(8,128)(2,1)S(1)} %fusion.place_ref, bf16[64,8192]{1,0:T(8,128)(2,1)} %copy-done.10, bf16[64,8192]{1,0:T(8,128)(2,1)} %collective-permute-done.14.refs_1_, bf16[64,8192]{1,0:T(8,128)(2,1)S(1)} %collective-permute-done.15.refs_2_, ...), custom_call_target="tpu_custom_call", output_to_operand_aliasing={{}: (5, {})} | custom-call | tf_op jit(solution)/shard_map/pallas_call | solution.py:128
  233.1 2.8 %multiply_bitcast_fusion = (f32[1,64,8192]{2,1,0:T(8,128)}, f32[1,64,8192]{2,1,0:T(8,128)}) fusion(f32[]{:T(128)} %bitcast.12, bf16[64,8192]{1,0:T(8,128)(2,1)S(1)} %copy-done.18, f32[64,8192]{1,0:T(8,128)S(1)} %get-tuple-element.59, bf16[64,8192]{1,0:T(8,128)(2,1)S(1)} %copy-done.16, bf16[64,8192]{1,0:T(8,128)(2,1)S(1)} %copy-done.14, ...), kind=kLoop, calls=%fused_computation.2 | loop fusion | flops 5242880 | bytes 12582916 | tf_op jit(solution)/shard_map/broadcast_in_dim | solution.py:37
  (112 shorter events, 36.9 us)
Async XLA Ops:
  4.1 47.6 %collective-permute-start.8 = (bf16[2,64,8192]{2,1,0:T(8,128)(2,1)}, bf16[2,64,8192]{2,1,0:T(8,128)(2,1)}, u32[]{:S(2)}, u32[]{:S(2)}) collective-permute-start(bf16[2,64,8192]{2,1,0:T(8,128)(2,1)} %constant_dynamic-update-slice_fusion), channel_id=1, source_target_pairs={{4,8},{5,9},{6,10},{7,11},{8,4},{9,5},{10,6},{11,7},{20,24},{21,25... | collective-permute-start | bytes 6291464 | tf_op jit(solution)/shard_map/ppermute | solution.py:305
  6.1 51.0 %collective-permute-start.4 = (bf16[2,64,8192]{2,1,0:T(8,128)(2,1)}, bf16[2,64,8192]{2,1,0:T(8,128)(2,1)}, u32[]{:S(2)}, u32[]{:S(2)}) collective-permute-start(bf16[2,64,8192]{2,1,0:T(8,128)(2,1)} %constant_dynamic-update-slice_fusion), channel_id=1, source_target_pairs={{0,4},{1,5},{2,6},{3,7},{4,0},{5,1},{6,2},{7,3},{8,12},{9,13},{10,... | collective-permute-start | bytes 6291464 | tf_op jit(solution)/shard_map/ppermute | solution.py:305
  17.8 24.4 %collective-permute-start.1 = (bf16[2,2,16,8192]{3,2,1,0:T(8,128)(2,1)S(1)}, bf16[2,2,16,8192]{3,2,1,0:T(8,128)(2,1)S(1)}, u32[]{:S(2)}, u32[]{:S(2)}) collective-permute-start(bf16[2,2,16,8192]{3,2,1,0:T(8,128)(2,1)S(1)} %get-tuple-element.40), channel_id=1, source_target_pairs={{0,2},{1,3},{2,0},{3,1},{4,6},{5,7},{6,4},{7,5},{8,10},{9,11},{10,... | collective-permute-start | bytes 3145736 | tf_op jit(solution)/shard_map/ppermute | solution.py:305
  19.3 24.5 %collective-permute-start = (bf16[1,2,64,8192]{3,2,1,0:T(8,128)(2,1)S(1)}, bf16[1,2,64,8192]{3,2,1,0:T(8,128)(2,1)S(1)}, u32[]{:S(2)}, u32[]{:S(2)}) collective-permute-start(bf16[1,2,64,8192]{3,2,1,0:T(8,128)(2,1)S(1)} %get-tuple-element.38), channel_id=1, source_target_pairs={{0,1},{1,0},{2,3},{3,2},{4,5},{5,4},{6,7},{7,6},{8,9},{9,8},{10,11... | collective-permute-start | bytes 6291464 | tf_op jit(solution)/shard_map/ppermute | solution.py:305
  42.2 26.1 %collective-permute-start.6 = (bf16[2,2,16,8192]{3,2,1,0:T(8,128)(2,1)S(1)}, bf16[2,2,16,8192]{3,2,1,0:T(8,128)(2,1)S(1)}, u32[]{:S(2)}, u32[]{:S(2)}) collective-permute-start(bf16[2,2,16,8192]{3,2,1,0:T(8,128)(2,1)S(1)} %get-tuple-element.43), channel_id=1, source_target_pairs={{0,2},{1,3},{2,0},{3,1},{4,6},{5,7},{6,4},{7,5},{8,10},{9,11},{10,... | collective-permute-start | bytes 3145736 | tf_op jit(solution)/shard_map/ppermute | solution.py:305
  43.8 77.0 %collective-permute-start.2 = (bf16[2,2,32,8192]{3,2,1,0:T(8,128)(2,1)}, bf16[2,2,32,8192]{3,2,1,0:T(8,128)(2,1)S(1)}, u32[]{:S(2)}, u32[]{:S(2)}) collective-permute-start(bf16[2,2,32,8192]{3,2,1,0:T(8,128)(2,1)} %get-tuple-element.41), channel_id=1, source_target_pairs={{0,2},{1,3},{2,0},{3,1},{4,6},{5,7},{6,4},{7,5},{8,10},{9,11},{10,... | collective-permute-start | bytes 6291464 | tf_op jit(solution)/shard_map/ppermute | solution.py:305
  48.2 52.4 %collective-permute-start.11 = (bf16[2,64,8192]{2,1,0:T(8,128)(2,1)}, bf16[2,64,8192]{2,1,0:T(8,128)(2,1)}, u32[]{:S(2)}, u32[]{:S(2)}) collective-permute-start(bf16[2,64,8192]{2,1,0:T(8,128)(2,1)} %pad_maximum_fusion.refs_0_), channel_id=1, source_target_pairs={{0,4},{1,5},{2,6},{3,7},{12,8},{13,9},{14,10},{15,11},{16,20},{17,... | collective-permute-start | bytes 6291464 | tf_op jit(solution)/shard_map/ppermute | solution.py:305
  51.8 51.3 %collective-permute-start.10 = (bf16[2,64,8192]{2,1,0:T(8,128)(2,1)}, bf16[2,64,8192]{2,1,0:T(8,128)(2,1)}, u32[]{:S(2)}, u32[]{:S(2)}) collective-permute-start(bf16[2,64,8192]{2,1,0:T(8,128)(2,1)} %collective-permute-done.8.refs_1_), channel_id=1, source_target_pairs={{4,0},{5,1},{6,2},{7,3},{8,12},{9,13},{10,14},{11,15},{20,16},{21,... | collective-permute-start | bytes 6291464 | tf_op jit(solution)/shard_map/ppermute | solution.py:305
  57.1 46.0 %collective-permute-start.9 = (bf16[2,64,8192]{2,1,0:T(8,128)(2,1)}, bf16[2,64,8192]{2,1,0:T(8,128)(2,1)}, u32[]{:S(2)}, u32[]{:S(2)}) collective-permute-start(bf16[2,64,8192]{2,1,0:T(8,128)(2,1)} %collective-permute-done.4.refs_4_), channel_id=1, source_target_pairs={{4,8},{5,9},{6,10},{7,11},{8,4},{9,5},{10,6},{11,7},{20,24},{21,25... | collective-permute-start | bytes 6291464 | tf_op jit(solution)/shard_map/ppermute | solution.py:305
  112.1 13.2 %collective-permute-start.12 = (bf16[64,8192]{1,0:T(8,128)(2,1)S(1)}, bf16[64,8192]{1,0:T(8,128)(2,1)S(1)}, u32[]{:S(2)}, u32[]{:S(2)}) collective-permute-start(bf16[64,8192]{1,0:T(8,128)(2,1)S(1)} %get-tuple-element.48), channel_id=1, source_target_pairs={{4,8},{5,9},{6,10},{7,11},{8,4},{9,5},{10,6},{11,7},{20,24},{21,25... | collective-permute-start | bytes 3145736 | tf_op jit(solution)/shard_map/ppermute | solution.py:305
  113.0 31.4 %collective-permute-start.13 = (bf16[64,8192]{1,0:T(8,128)(2,1)S(1)}, bf16[64,8192]{1,0:T(8,128)(2,1)S(1)}, u32[]{:S(2)}, u32[]{:S(2)}) collective-permute-start(bf16[64,8192]{1,0:T(8,128)(2,1)S(1)} %get-tuple-element.49), channel_id=1, source_target_pairs={{0,4},{1,5},{2,6},{3,7},{4,0},{5,1},{6,2},{7,3},{8,12},{9,13},{10,... | collective-permute-start | bytes 3145736 | tf_op jit(solution)/shard_map/ppermute | solution.py:305
  120.9 23.5 %collective-permute-start.3 = (bf16[1,2,32,8192]{3,2,1,0:T(8,128)(2,1)S(1)}, bf16[1,2,32,8192]{3,2,1,0:T(8,128)(2,1)S(1)}, u32[]{:S(2)}, u32[]{:S(2)}) collective-permute-start(bf16[1,2,32,8192]{3,2,1,0:T(8,128)(2,1)S(1)} %slice.40), channel_id=1, source_target_pairs={{0,1},{1,0},{2,3},{3,2},{4,5},{5,4},{6,7},{7,6},{8,9},{9,8},{10,11... | collective-permute-start | bytes 3145736 | tf_op jit(solution)/shard_map/ppermute | solution.py:305
  120.9 35.1 %collective-permute-start.20 = (bf16[64,8192]{1,0:T(8,128)(2,1)S(1)}, bf16[64,8192]{1,0:T(8,128)(2,1)S(1)}, u32[]{:S(2)}, u32[]{:S(2)}) collective-permute-start(bf16[64,8192]{1,0:T(8,128)(2,1)S(1)} %get-tuple-element.61), channel_id=1, source_target_pairs={{4,8},{5,9},{6,10},{7,11},{8,4},{9,5},{10,6},{11,7},{20,24},{21,25... | collective-permute-start | bytes 3145736 | tf_op jit(solution)/shard_map/ppermute | solution.py:305
  121.7 46.0 %collective-permute-start.21 = (bf16[64,8192]{1,0:T(8,128)(2,1)S(1)}, bf16[64,8192]{1,0:T(8,128)(2,1)S(1)}, u32[]{:S(2)}, u32[]{:S(2)}) collective-permute-start(bf16[64,8192]{1,0:T(8,128)(2,1)S(1)} %get-tuple-element.61), channel_id=1, source_target_pairs={{0,4},{1,5},{2,6},{3,7},{12,8},{13,9},{14,10},{15,11},{16,20},{17,... | collective-permute-start | bytes 3145736 | tf_op jit(solution)/shard_map/ppermute | solution.py:305
  152.8 46.8 %collective-permute-start.16 = (bf16[64,8192]{1,0:T(8,128)(2,1)S(1)}, bf16[64,8192]{1,0:T(8,128)(2,1)}, u32[]{:S(2)}, u32[]{:S(2)}) collective-permute-start(bf16[64,8192]{1,0:T(8,128)(2,1)S(1)} %get-tuple-element.54), channel_id=1, source_target_pairs={{0,2},{1,3},{2,0},{3,1},{4,6},{5,7},{6,4},{7,5},{8,10},{9,11},{10,... | collective-permute-start | bytes 3145736 | tf_op jit(solution)/shard_map/ppermute | solution.py:305
  154.3 40.6 %collective-permute-start.15 = (bf16[64,8192]{1,0:T(8,128)(2,1)S(1)}, bf16[64,8192]{1,0:T(8,128)(2,1)S(1)}, u32[]{:S(2)}, u32[]{:S(2)}) collective-permute-start(bf16[64,8192]{1,0:T(8,128)(2,1)S(1)} %get-tuple-element.53), channel_id=1, source_target_pairs={{0,2},{1,3},{2,0},{3,1},{4,6},{5,7},{6,4},{7,5},{8,10},{9,11},{10,... | collective-permute-start | bytes 3145736 | tf_op jit(solution)/shard_map/ppermute | solution.py:305
  155.1 44.5 %collective-permute-start.18 = (bf16[64,8192]{1,0:T(8,128)(2,1)S(1)}, bf16[64,8192]{1,0:T(8,128)(2,1)S(1)}, u32[]{:S(2)}, u32[]{:S(2)}) collective-permute-start(bf16[64,8192]{1,0:T(8,128)(2,1)S(1)} %add_convert_fusion.3), channel_id=1, source_target_pairs={{4,8},{5,9},{6,10},{7,11},{8,4},{9,5},{10,6},{11,7},{20,24},{21,25... | collective-permute-start | bytes 3145736 | tf_op jit(solution)/shard_map/ppermute | solution.py:305
  156.1 44.0 %collective-permute-start.19 = (bf16[64,8192]{1,0:T(8,128)(2,1)S(1)}, bf16[64,8192]{1,0:T(8,128)(2,1)S(1)}, u32[]{:S(2)}, u32[]{:S(2)}) collective-permute-start(bf16[64,8192]{1,0:T(8,128)(2,1)S(1)} %add_convert_fusion.2), channel_id=1, source_target_pairs={{0,4},{1,5},{2,6},{3,7},{4,0},{5,1},{6,2},{7,3},{8,12},{9,13},{10,... | collective-permute-start | bytes 3145736 | tf_op jit(solution)/shard_map/ppermute | solution.py:305
  195.2 6.1 %collective-permute-start.22 = (bf16[64,8192]{1,0:T(8,128)(2,1)S(1)}, bf16[64,8192]{1,0:T(8,128)(2,1)S(1)}, u32[]{:S(2)}, u32[]{:S(2)}) collective-permute-start(bf16[64,8192]{1,0:T(8,128)(2,1)S(1)} %add_convert_fusion.1), channel_id=1, source_target_pairs={{4,8},{5,9},{6,10},{7,11},{8,4},{9,5},{10,6},{11,7},{20,24},{21,25... | collective-permute-start | bytes 3145736 | tf_op jit(solution)/shard_map/ppermute | solution.py:305
  196.4 18.9 %collective-permute-start.23 = (bf16[64,8192]{1,0:T(8,128)(2,1)S(1)}, bf16[64,8192]{1,0:T(8,128)(2,1)S(1)}, u32[]{:S(2)}, u32[]{:S(2)}) collective-permute-start(bf16[64,8192]{1,0:T(8,128)(2,1)S(1)} %add_convert_fusion), channel_id=1, source_target_pairs={{0,4},{1,5},{2,6},{3,7},{4,0},{5,1},{6,2},{7,3},{8,12},{9,13},{10,... | collective-permute-start | bytes 3145736 | tf_op jit(solution)/shard_map/ppermute | solution.py:305
  199.6 21.2 %collective-permute-start.14 = (bf16[64,8192]{1,0:T(8,128)(2,1)}, bf16[64,8192]{1,0:T(8,128)(2,1)}, u32[]{:S(2)}, u32[]{:S(2)}) collective-permute-start(bf16[64,8192]{1,0:T(8,128)(2,1)} %get-tuple-element.52), channel_id=1, source_target_pairs={{0,1},{1,0},{2,3},{3,2},{4,5},{5,4},{6,7},{7,6},{8,9},{9,8},{10,11... | collective-permute-start | bytes 3145736 | tf_op jit(solution)/shard_map/ppermute | solution.py:305
  199.6 21.2 %collective-permute-start.17 = (bf16[64,8192]{1,0:T(8,128)(2,1)}, bf16[64,8192]{1,0:T(8,128)(2,1)}, u32[]{:S(2)}, u32[]{:S(2)}) collective-permute-start(bf16[64,8192]{1,0:T(8,128)(2,1)} %collective-permute-done.16), channel_id=1, source_target_pairs={{0,1},{1,0},{2,3},{3,2},{4,5},{5,4},{6,7},{7,6},{8,9},{9,8},{10,11... | collective-permute-start | bytes 3145736 | tf_op jit(solution)/shard_map/ppermute | solution.py:305
  223.4 7.0 %collective-permute-start.27 = (f32[8,128]{1,0:T(8,128)S(1)}, f32[8,128]{1,0:T(8,128)S(1)}, u32[]{:S(2)}, u32[]{:S(2)}) collective-permute-start(f32[8,128]{1,0:T(8,128)S(1)} %add_add_fusion.1), channel_id=1, source_target_pairs={{0,4},{1,5},{2,6},{3,7},{4,0},{5,1},{6,2},{7,3},{8,12},{9,13},{10,... | collective-permute-start | bytes 12296 | tf_op jit(solution)/shard_map/ppermute | solution.py:305
  226.5 5.4 %collective-permute-start.29 = (f32[8,128]{1,0:T(8,128)S(1)}, f32[8,128]{1,0:T(8,128)S(1)}, u32[]{:S(2)}, u32[]{:S(2)}) collective-permute-start(f32[8,128]{1,0:T(8,128)S(1)} %add_add_fusion.1), channel_id=1, source_target_pairs={{0,12},{1,13},{2,14},{3,15},{4,8},{5,9},{6,10},{7,11},{8,4},{9,5},... | collective-permute-start | bytes 12296 | tf_op jit(solution)/shard_map/ppermute | solution.py:305
  (27 other events, 329.5 us)

commit v12 on v11

--- a/solution.py
+++ b/solution.py
@@ -143,6 +143,26 @@
     return upper == (lax.broadcasted_iota(jnp.int32, (rows, columns), 1) < first_columns)
 
 
+def stack(down, up):
+    _, rank, width = down.shape
+
+    def body(down_in, up_in, out, sems):
+        copies = [pltpu.make_async_copy(r.at[0], out.at[k], sems.at[k]) for k, r in enumerate((down_in, up_in))]
+        for c in copies:
+            c.start()
+        for c in copies:
+            c.wait()
+
+    return pl.pallas_call(
+        body,
+        in_specs=[HBM, HBM],
+        out_specs=WHOLE,
+        out_shape=pltpu.VMEM((2, rank, width), BF16),
+        scratch_shapes=[pltpu.SemaphoreType.DMA((2,))],
+        compiler_params=pltpu.CompilerParams(vmem_limit_bytes=VMEM_BYTES),
+    )(*in_hbm(down, up))
+
+
 def far_group(is_end, rows, factors, handed=None):
     _, block, width = rows[0].shape
     rank = factors[0].shape[1]
@@ -180,15 +200,15 @@
                     for i in range(tiles):
                         copy(source, i).start()
 
-            sums = jnp.zeros((2 * total, 2 * rank), F32)
+            sums = [jnp.zeros((total, rank), F32)] * 2
             for i in range(tiles):
                 copy(rows_in[0], i).wait()
                 cut = pl.ds(i * tile, tile)
-                both = [jnp.concatenate([piece(k, cut) for k in range(2)], axis=0) for piece in (tokens, factor)]
-                sums += dot32(*both, ROWS_OF)
-            left[0] = sums[:total, :rank].T.astype(BF16)
-            inner[...] = sums[total:, rank:].astype(BF16)
-            left[1] = sums[total:, rank:].T.astype(BF16)
+                for k in range(2):
+                    sums[k] += dot32(tokens(k, cut), factor(k, cut), ROWS_OF)
+            for k in range(2):
+                left[k] = sums[k].T.astype(BF16)
+            inner[...] = sums[1].astype(BF16)
 
         cut = pl.ds(pl.multiple_of(step * tile, tile), tile)
         up_ref[...] = dot32(left[0], tokens(1, cut)).astype(BF16)
@@ -318,7 +338,7 @@
         return (term + sum(after([send(term, pairs) for pairs in along], grad_acts)))[0, 0]
 
     down, up = pool_down_factors[0], pool_up_factors[0]
-    own = jnp.concatenate([pool_down_factors, pool_up_factors])
+    own = stack(pool_down_factors, pool_up_factors)
     pair = send(own, swap)
     crossed = send(own, cross)
 
@@ -379,7 +399,8 @@
         return (a.astype(F32) + b.astype(F32)).astype(BF16)
 
     down2, down1 = add(down2, swapped), add(down1, down3)
-    dx_across = [send(block, beside(2)) for block in dx_across]
+    dx_across[0] = send(dx_across[0], beside(2))
+    dx_across[1] = send(after(dx_across[1], dx_across[0]), beside(2))
     up3, up2_in = after((up3, up2_in), down2, down1, dx_across[0])
     down2, down1 = send(down2, cross), send(down1, swap)
     up2, up1 = send(add(up2, up2_in), cross), send(add(up1, up3), swap)

time: 236 us -> 228 us (0.966)
  starting transfers between devices: 55.7 us -> 50.3 us
  local copies, waits for them, and re-layouts: 10.9 us -> 5.79 us
    ppermute x30, starting transfers between devices: 55.7 us -> 50.3 us  [send(): return lax.ppermute(array, 'dp', pairs)]
    pallas_call x0 -> x1, Pallas kernels: none -> 2.97 us  [stack(): pl.pallas_call(body, in_specs=[HBM, HBM], out_specs=WHOLE, out_shape=pltp...]
    unnamed x43 -> x42, local copies, waits for them, and re-layouts: 6.3 us -> 3.94 us
  transfers between devices with their start and end apart: 30 -> 30, of which waited for: 10 -> 11; matrix products, arithmetic and copies ran while one was open for 5% -> 4% of each run, Pallas kernels for 14% -> 14%
where the time goes in v12:
time: 228 us; the launch traced here: 227 us
  waiting for transfers between devices  123 us (54%)
  starting transfers between devices  50.3 us (22%)
  Pallas kernels  34.4 us (15%)
  other arithmetic  11.1 us (5%)
  local copies, waits for them, and re-layouts  5.79 us (3%)
  between operations  3.05 us (1%)
    ppermute x30, waiting for transfers between devices, send(): return lax.ppermute(array, 'dp', pairs)  123 us
    ppermute x30, starting transfers between devices, send(): return lax.ppermute(array, 'dp', pairs)  50.3 us
    pallas_call x2, Pallas kernels, far_group(): pl.pallas_call(body, grid=(tiles,), in_specs=[pl.BlockSpec(memory_space=p...  13.1 us
    pallas_call x1, Pallas kernels, near_groups(): pl.pallas_call(body, grid=(tiles,), in_specs=[pl.BlockSpec(memory_space=p...  6.81 us
    pallas_call x1, Pallas kernels, pack(): pl.pallas_call(body, grid=(tiles,), in_specs=[pl.BlockSpec(place.shape, l...  6.36 us
    pallas_call x2, Pallas kernels, unpack(): pl.pallas_call(body, grid=(width // 2 // tile,), in_specs=[pl.BlockSpec(p...  5.13 us
  transfers between devices with their start and end apart: 30, of which 11 were waited for; matrix products, arithmetic and copies ran while one was open for 4% of the time, Pallas kernels for 14%

profile of v12, /device:TPU:0, one launch (start us, length us, event | category | flops | bytes accessed | tf_op | source)
XLA Modules:
  0.0 227.2 jit_solution(10774482870651254387)
XLA Ops:
  0.7 3.0 %shard_map.86 = bf16[2,64,8192]{2,1,0:T(8,128)(2,1)} custom-call(bf16[1,64,8192]{2,1,0:T(8,128)(2,1)} %down_in.1, bf16[1,64,8192]{2,1,0:T(8,128)(2,1)} %up_in.1), custom_call_target="tpu_custom_call" | custom-call | tf_op jit(solution)/shard_map/pallas_call | solution.py:156
  5.6 4.6 %collective-permute-start.4 = (bf16[2,64,8192]{2,1,0:T(8,128)(2,1)}, bf16[2,64,8192]{2,1,0:T(8,128)(2,1)}, u32[]{:S(2)}, u32[]{:S(2)}) collective-permute-start(bf16[2,64,8192]{2,1,0:T(8,128)(2,1)} %shard_map.86), channel_id=1, source_target_pairs={{0,4},{1,5},{2,6},{3,7},{4,0},{5,1},{6,2},{7,3},{8,12},{9,13},{10,... | collective-permute-start | bytes 6291464 | tf_op jit(solution)/shard_map/ppermute | solution.py:325
  10.9 6.4 %shard_map.85 = (bf16[1,2,64,8192]{3,2,1,0:T(8,128)(2,1)S(1)}, bf16[1,2,64,8192]{3,2,1,0:T(8,128)(2,1)S(1)}, bf16[2,2,16,8192]{3,2,1,0:T(8,128)(2,1)S(1)}, bf16[...) custom-call(bf16[256,128]{1,0:T(8,128)(2,1)S(1)} %fusion.1.place_ref, bf16[128,8192]{1,0:T(8,128)(2,1)} %x_in.1, ...), custom_call_target="tpu_custom_call" | custom-call | tf_op jit(solution)/shard_map/pallas_call | solution.py:107
  18.9 22.8 %collective-permute-done.1 = bf16[2,2,16,8192]{3,2,1,0:T(8,128)(2,1)S(1)} collective-permute-done((bf16[2,2,16,8192]{3,2,1,0:T(8,128)(2,1)S(1)}, bf16[2,2,16,8192]{3,2,1,0:T(8,128)(2,1)S(1)}, u32[]{:S(2)}, u32[]{:S(2)}) %collective-permute-start.1) | collective-permute-done | bytes 1048608 | tf_op jit(solution)/shard_map/ppermute | solution.py:325
  46.9 3.6 %collective-permute-start.11 = (bf16[2,64,8192]{2,1,0:T(8,128)(2,1)}, bf16[2,64,8192]{2,1,0:T(8,128)(2,1)}, u32[]{:S(2)}, u32[]{:S(2)}) collective-permute-start(bf16[2,64,8192]{2,1,0:T(8,128)(2,1)} %pad_maximum_fusion.refs_0_), channel_id=1, source_target_pairs={{0,4},{1,5},{2,6},{3,7},{12,8},{13,9},{14,10},{15,11},{16,20},{17,... | collective-permute-start | bytes 6291464 | tf_op jit(solution)/shard_map/ppermute | solution.py:325
  51.8 4.8 %collective-permute-done.4.refs_4_ = bf16[2,64,8192]{2,1,0:T(8,128)(2,1)} collective-permute-done((bf16[2,64,8192]{2,1,0:T(8,128)(2,1)}, bf16[2,64,8192]{2,1,0:T(8,128)(2,1)}, u32[]{:S(2)}, u32[]{:S(2)}) %collective-permute-start.4) | collective-permute-done | bytes 2097184 | tf_op jit(solution)/shard_map/ppermute | solution.py:325
  58.7 9.1 %collective-permute-done.6 = bf16[2,2,16,8192]{3,2,1,0:T(8,128)(2,1)S(1)} collective-permute-done((bf16[2,2,16,8192]{3,2,1,0:T(8,128)(2,1)S(1)}, bf16[2,2,16,8192]{3,2,1,0:T(8,128)(2,1)S(1)}, u32[]{:S(2)}, u32[]{:S(2)}) %collective-permute-start.6) | collective-permute-done | bytes 1048608 | tf_op jit(solution)/shard_map/ppermute | solution.py:325
  71.1 2.7 %pad_maximum_fusion.1.refs_0_.refs_1_ = bf16[2,64,8192]{2,1,0:T(8,128)(2,1)} fusion(bf16[2,16,8192]{2,1,0:T(8,128)(2,1)} %bitcast.11, bf16[2,16,8192]{2,1,0:T(8,128)(2,1)} %get-tuple-element.80, bf16[2,16,8192]{2,1,0:T(8,128)(2,1)S(1)} %get-tuple-element.78, bf16[2,16,8192]{2,1,0:T(8,128)(2,1)S(1)} %get-tuple-element.76), kind=kLoop, calls=%fused_computation.1 | loop fusion | flops 8388608 | bytes 4194304 | tf_op jit(solution)/shard_map/concatenate | solution.py:381
  73.8 5.3 %shard_map.87 = (bf16[64,8192]{1,0:T(8,128)(2,1)S(1)}, bf16[64,8192]{1,0:T(8,128)(2,1)S(1)}, bf16[64,8192]{1,0:T(8,128)(2,1)S(1)}) custom-call(s32[1]{0:T(128)} %bitcast.1.end_ref, bf16[2,64,8192]{2,1,0:T(8,128)(2,1)} %pad_maximum_fusion.1.refs_0_.refs_1_, bf16[2,64,8192]{2,1,0:T(8,128)(2,1)} %collective-permute-done.8.refs_1_), custom_call_target="tpu_custom_call" | custom-call | tf_op jit(solution)/shard_map/pallas_call | solution.py:224
  79.0 21.0 %collective-permute-done.11.refs_4_ = bf16[2,64,8192]{2,1,0:T(8,128)(2,1)} collective-permute-done((bf16[2,64,8192]{2,1,0:T(8,128)(2,1)}, bf16[2,64,8192]{2,1,0:T(8,128)(2,1)}, u32[]{:S(2)}, u32[]{:S(2)}) %collective-permute-start.11) | collective-permute-done | bytes 2097184 | tf_op jit(solution)/shard_map/ppermute | solution.py:325
  102.6 7.9 %shard_map.88 = (bf16[64,8192]{1,0:T(8,128)(2,1)S(1)}, bf16[64,8192]{1,0:T(8,128)(2,1)S(1)}, bf16[64,8192]{1,0:T(8,128)(2,1)S(1)}, bf16[64,8192]{1,0:T(8,128)(2,1)S(1)}) custom-call(s32[1]{0:T(128)} %bitcast.1.end_ref, bf16[2,64,8192]{2,1,0:T(8,128)(2,1)} %pad_maximum_fusion.refs_0_, bf16[2,64,8192]{2,1,0:T(8,128)(2,1)} %pad_maximum_fusion.1.refs_0_.refs_1_, ...), custom_call_target="tpu_custom_call" | custom-call | tf_op jit(solution)/shard_map/pallas_call | solution.py:224
  111.3 7.9 %collective-permute-start.13 = (bf16[64,8192]{1,0:T(8,128)(2,1)S(1)}, bf16[64,8192]{1,0:T(8,128)(2,1)S(1)}, u32[]{:S(2)}, u32[]{:S(2)}) collective-permute-start(bf16[64,8192]{1,0:T(8,128)(2,1)S(1)} %get-tuple-element.50), channel_id=1, source_target_pairs={{0,4},{1,5},{2,6},{3,7},{4,0},{5,1},{6,2},{7,3},{8,12},{9,13},{10,... | collective-permute-start | bytes 3145736 | tf_op jit(solution)/shard_map/ppermute | solution.py:325
  120.1 3.6 %collective-permute-start.21 = (bf16[64,8192]{1,0:T(8,128)(2,1)S(1)}, bf16[64,8192]{1,0:T(8,128)(2,1)S(1)}, u32[]{:S(2)}, u32[]{:S(2)}) collective-permute-start(bf16[64,8192]{1,0:T(8,128)(2,1)S(1)} %get-tuple-element.63), channel_id=1, source_target_pairs={{0,4},{1,5},{2,6},{3,7},{12,8},{13,9},{14,10},{15,11},{16,20},{17,... | collective-permute-start | bytes 3145736 | tf_op jit(solution)/shard_map/ppermute | solution.py:325
  123.7 19.1 %collective-permute-done.13.refs_9_ = bf16[64,8192]{1,0:T(8,128)(2,1)S(1)} collective-permute-done((bf16[64,8192]{1,0:T(8,128)(2,1)S(1)}, bf16[64,8192]{1,0:T(8,128)(2,1)S(1)}, u32[]{:S(2)}, u32[]{:S(2)}) %collective-permute-start.13) | collective-permute-done | bytes 1048608 | tf_op jit(solution)/shard_map/ppermute | solution.py:325
  144.4 6.8 %shard_map.89 = (bf16[64,8192]{1,0:T(8,128)(2,1)S(1)}, bf16[64,8192]{1,0:T(8,128)(2,1)}, bf16[64,8192]{1,0:T(8,128)(2,1)S(1)}, bf16[64,8192]{1,0:T(8,128)(2,1)S(...) custom-call(s32[1]{0:T(128)} %bitcast.1.end_ref, ...), custom_call_target="tpu_custom_call" | custom-call | tf_op jit(solution)/shard_map/pallas_call | solution.py:292
  154.0 4.2 %collective-permute-start.19 = (bf16[64,8192]{1,0:T(8,128)(2,1)S(1)}, bf16[64,8192]{1,0:T(8,128)(2,1)S(1)}, u32[]{:S(2)}, u32[]{:S(2)}) collective-permute-start(bf16[64,8192]{1,0:T(8,128)(2,1)S(1)} %add_convert_fusion.2), channel_id=1, source_target_pairs={{0,4},{1,5},{2,6},{3,7},{4,0},{5,1},{6,2},{7,3},{8,12},{9,13},{10,... | collective-permute-start | bytes 3145736 | tf_op jit(solution)/shard_map/ppermute | solution.py:325
  158.2 16.4 %collective-permute-done.15.refs_2_ = bf16[64,8192]{1,0:T(8,128)(2,1)S(1)} collective-permute-done((bf16[64,8192]{1,0:T(8,128)(2,1)S(1)}, bf16[64,8192]{1,0:T(8,128)(2,1)S(1)}, u32[]{:S(2)}, u32[]{:S(2)}) %collective-permute-start.15) | collective-permute-done | bytes 1048608 | tf_op jit(solution)/shard_map/ppermute | solution.py:325
  177.5 4.2 %collective-permute-start.23 = (bf16[64,8192]{1,0:T(8,128)(2,1)S(1)}, bf16[64,8192]{1,0:T(8,128)(2,1)S(1)}, u32[]{:S(2)}, u32[]{:S(2)}) collective-permute-start(bf16[64,8192]{1,0:T(8,128)(2,1)S(1)} %add_convert_fusion), channel_id=1, source_target_pairs={{0,4},{1,5},{2,6},{3,7},{4,0},{5,1},{6,2},{7,3},{8,12},{9,13},{10,... | collective-permute-start | bytes 3145736 | tf_op jit(solution)/shard_map/ppermute | solution.py:325
  181.7 11.8 %collective-permute-done.16 = bf16[64,8192]{1,0:T(8,128)(2,1)} collective-permute-done((bf16[64,8192]{1,0:T(8,128)(2,1)S(1)}, bf16[64,8192]{1,0:T(8,128)(2,1)}, u32[]{:S(2)}, u32[]{:S(2)}) %collective-permute-start.16) | collective-permute-done | bytes 1048608 | tf_op jit(solution)/shard_map/ppermute | solution.py:325
  194.7 12.2 %collective-permute-done.23 = bf16[64,8192]{1,0:T(8,128)(2,1)S(1)} collective-permute-done((bf16[64,8192]{1,0:T(8,128)(2,1)S(1)}, bf16[64,8192]{1,0:T(8,128)(2,1)S(1)}, u32[]{:S(2)}, u32[]{:S(2)}) %collective-permute-start.23) | collective-permute-done | bytes 1048608 | tf_op jit(solution)/shard_map/ppermute | solution.py:325
  212.4 2.6 %shard_map.90.refs_4_ = bf16[128,8192]{1,0:T(8,128)(2,1)} custom-call(bf16[128,256]{1,0:T(8,128)(2,1)S(1)} %fusion.place_ref, bf16[64,8192]{1,0:T(8,128)(2,1)} %copy-done.10, bf16[64,8192]{1,0:T(8,128)(2,1)} %collective-permute-done.14.refs_1_, bf16[64,8192]{1,0:T(8,128)(2,1)S(1)} %collective-permute-done.15.refs_2_, ...), custom_call_target="tpu_custom_call" | custom-call | tf_op jit(solution)/shard_map/pallas_call | solution.py:128
  215.1 2.5 %collective-permute-start.27 = (f32[8,128]{1,0:T(8,128)S(1)}, f32[8,128]{1,0:T(8,128)S(1)}, u32[]{:S(2)}, u32[]{:S(2)}) collective-permute-start(f32[8,128]{1,0:T(8,128)S(1)} %add_add_fusion.1), channel_id=1, source_target_pairs={{0,4},{1,5},{2,6},{3,7},{4,0},{5,1},{6,2},{7,3},{8,12},{9,13},{10,... | collective-permute-start | bytes 12296 | tf_op jit(solution)/shard_map/ppermute | solution.py:325
  220.1 2.6 %shard_map.91 = bf16[128,8192]{1,0:T(8,128)(2,1)} custom-call(bf16[128,256]{1,0:T(8,128)(2,1)S(1)} %fusion.place_ref, bf16[64,8192]{1,0:T(8,128)(2,1)} %copy-done.10, bf16[64,8192]{1,0:T(8,128)(2,1)} %collective-permute-done.14.refs_1_, bf16[64,8192]{1,0:T(8,128)(2,1)S(1)} %collective-permute-done.15.refs_2_, ...), custom_call_target="tpu_custom_call", output_to_operand_aliasing={{}: (5, {})} | custom-call | tf_op jit(solution)/shard_map/pallas_call | solution.py:128
  224.3 2.8 %multiply_bitcast_fusion = (f32[1,64,8192]{2,1,0:T(8,128)}, f32[1,64,8192]{2,1,0:T(8,128)}) fusion(f32[]{:T(128)} %bitcast.12, bf16[64,8192]{1,0:T(8,128)(2,1)S(1)} %copy-done.18, f32[64,8192]{1,0:T(8,128)S(1)} %get-tuple-element.61, bf16[64,8192]{1,0:T(8,128)(2,1)S(1)} %copy-done.16, bf16[64,8192]{1,0:T(8,128)(2,1)S(1)} %copy-done.14, ...), kind=kLoop, calls=%fused_computation.2 | loop fusion | flops 5242880 | bytes 12582916 | tf_op jit(solution)/shard_map/broadcast_in_dim | solution.py:37
  (111 shorter events, 36.4 us)
Async XLA Ops:
  3.6 46.9 %collective-permute-start.8 = (bf16[2,64,8192]{2,1,0:T(8,128)(2,1)}, bf16[2,64,8192]{2,1,0:T(8,128)(2,1)}, u32[]{:S(2)}, u32[]{:S(2)}) collective-permute-start(bf16[2,64,8192]{2,1,0:T(8,128)(2,1)} %shard_map.86), channel_id=1, source_target_pairs={{4,8},{5,9},{6,10},{7,11},{8,4},{9,5},{10,6},{11,7},{20,24},{21,25... | collective-permute-start | bytes 6291464 | tf_op jit(solution)/shard_map/ppermute | solution.py:325
  5.6 51.0 %collective-permute-start.4 = (bf16[2,64,8192]{2,1,0:T(8,128)(2,1)}, bf16[2,64,8192]{2,1,0:T(8,128)(2,1)}, u32[]{:S(2)}, u32[]{:S(2)}) collective-permute-start(bf16[2,64,8192]{2,1,0:T(8,128)(2,1)} %shard_map.86), channel_id=1, source_target_pairs={{0,4},{1,5},{2,6},{3,7},{4,0},{5,1},{6,2},{7,3},{8,12},{9,13},{10,... | collective-permute-start | bytes 6291464 | tf_op jit(solution)/shard_map/ppermute | solution.py:325
  17.3 24.4 %collective-permute-start.1 = (bf16[2,2,16,8192]{3,2,1,0:T(8,128)(2,1)S(1)}, bf16[2,2,16,8192]{3,2,1,0:T(8,128)(2,1)S(1)}, u32[]{:S(2)}, u32[]{:S(2)}) collective-permute-start(bf16[2,2,16,8192]{3,2,1,0:T(8,128)(2,1)S(1)} %get-tuple-element.41), channel_id=1, source_target_pairs={{0,2},{1,3},{2,0},{3,1},{4,6},{5,7},{6,4},{7,5},{8,10},{9,11},{10,... | collective-permute-start | bytes 3145736 | tf_op jit(solution)/shard_map/ppermute | solution.py:325
  18.8 24.5 %collective-permute-start = (bf16[1,2,64,8192]{3,2,1,0:T(8,128)(2,1)S(1)}, bf16[1,2,64,8192]{3,2,1,0:T(8,128)(2,1)S(1)}, u32[]{:S(2)}, u32[]{:S(2)}) collective-permute-start(bf16[1,2,64,8192]{3,2,1,0:T(8,128)(2,1)S(1)} %get-tuple-element.39), channel_id=1, source_target_pairs={{0,1},{1,0},{2,3},{3,2},{4,5},{5,4},{6,7},{7,6},{8,9},{9,8},{10,11... | collective-permute-start | bytes 6291464 | tf_op jit(solution)/shard_map/ppermute | solution.py:325
  41.7 26.1 %collective-permute-start.6 = (bf16[2,2,16,8192]{3,2,1,0:T(8,128)(2,1)S(1)}, bf16[2,2,16,8192]{3,2,1,0:T(8,128)(2,1)S(1)}, u32[]{:S(2)}, u32[]{:S(2)}) collective-permute-start(bf16[2,2,16,8192]{3,2,1,0:T(8,128)(2,1)S(1)} %get-tuple-element.44), channel_id=1, source_target_pairs={{0,2},{1,3},{2,0},{3,1},{4,6},{5,7},{6,4},{7,5},{8,10},{9,11},{10,... | collective-permute-start | bytes 3145736 | tf_op jit(solution)/shard_map/ppermute | solution.py:325
  43.4 75.8 %collective-permute-start.2 = (bf16[2,2,32,8192]{3,2,1,0:T(8,128)(2,1)}, bf16[2,2,32,8192]{3,2,1,0:T(8,128)(2,1)S(1)}, u32[]{:S(2)}, u32[]{:S(2)}) collective-permute-start(bf16[2,2,32,8192]{3,2,1,0:T(8,128)(2,1)} %get-tuple-element.42), channel_id=1, source_target_pairs={{0,2},{1,3},{2,0},{3,1},{4,6},{5,7},{6,4},{7,5},{8,10},{9,11},{10,... | collective-permute-start | bytes 6291464 | tf_op jit(solution)/shard_map/ppermute | solution.py:325
  46.9 53.2 %collective-permute-start.11 = (bf16[2,64,8192]{2,1,0:T(8,128)(2,1)}, bf16[2,64,8192]{2,1,0:T(8,128)(2,1)}, u32[]{:S(2)}, u32[]{:S(2)}) collective-permute-start(bf16[2,64,8192]{2,1,0:T(8,128)(2,1)} %pad_maximum_fusion.refs_0_), channel_id=1, source_target_pairs={{0,4},{1,5},{2,6},{3,7},{12,8},{13,9},{14,10},{15,11},{16,20},{17,... | collective-permute-start | bytes 6291464 | tf_op jit(solution)/shard_map/ppermute | solution.py:325
  50.5 52.1 %collective-permute-start.10 = (bf16[2,64,8192]{2,1,0:T(8,128)(2,1)}, bf16[2,64,8192]{2,1,0:T(8,128)(2,1)}, u32[]{:S(2)}, u32[]{:S(2)}) collective-permute-start(bf16[2,64,8192]{2,1,0:T(8,128)(2,1)} %collective-permute-done.8.refs_1_), channel_id=1, source_target_pairs={{4,0},{5,1},{6,2},{7,3},{8,12},{9,13},{10,14},{11,15},{20,16},{21,... | collective-permute-start | bytes 6291464 | tf_op jit(solution)/shard_map/ppermute | solution.py:325
  56.6 46.0 %collective-permute-start.9 = (bf16[2,64,8192]{2,1,0:T(8,128)(2,1)}, bf16[2,64,8192]{2,1,0:T(8,128)(2,1)}, u32[]{:S(2)}, u32[]{:S(2)}) collective-permute-start(bf16[2,64,8192]{2,1,0:T(8,128)(2,1)} %collective-permute-done.4.refs_4_), channel_id=1, source_target_pairs={{4,8},{5,9},{6,10},{7,11},{8,4},{9,5},{10,6},{11,7},{20,24},{21,25... | collective-permute-start | bytes 6291464 | tf_op jit(solution)/shard_map/ppermute | solution.py:325
  110.5 13.3 %collective-permute-start.12 = (bf16[64,8192]{1,0:T(8,128)(2,1)S(1)}, bf16[64,8192]{1,0:T(8,128)(2,1)S(1)}, u32[]{:S(2)}, u32[]{:S(2)}) collective-permute-start(bf16[64,8192]{1,0:T(8,128)(2,1)S(1)} %get-tuple-element.49), channel_id=1, source_target_pairs={{4,8},{5,9},{6,10},{7,11},{8,4},{9,5},{10,6},{11,7},{20,24},{21,25... | collective-permute-start | bytes 3145736 | tf_op jit(solution)/shard_map/ppermute | solution.py:325
  111.3 31.5 %collective-permute-start.13 = (bf16[64,8192]{1,0:T(8,128)(2,1)S(1)}, bf16[64,8192]{1,0:T(8,128)(2,1)S(1)}, u32[]{:S(2)}, u32[]{:S(2)}) collective-permute-start(bf16[64,8192]{1,0:T(8,128)(2,1)S(1)} %get-tuple-element.50), channel_id=1, source_target_pairs={{0,4},{1,5},{2,6},{3,7},{4,0},{5,1},{6,2},{7,3},{8,12},{9,13},{10,... | collective-permute-start | bytes 3145736 | tf_op jit(solution)/shard_map/ppermute | solution.py:325
  119.3 23.5 %collective-permute-start.3 = (bf16[1,2,32,8192]{3,2,1,0:T(8,128)(2,1)S(1)}, bf16[1,2,32,8192]{3,2,1,0:T(8,128)(2,1)S(1)}, u32[]{:S(2)}, u32[]{:S(2)}) collective-permute-start(bf16[1,2,32,8192]{3,2,1,0:T(8,128)(2,1)S(1)} %slice.40), channel_id=1, source_target_pairs={{0,1},{1,0},{2,3},{3,2},{4,5},{5,4},{6,7},{7,6},{8,9},{9,8},{10,11... | collective-permute-start | bytes 3145736 | tf_op jit(solution)/shard_map/ppermute | solution.py:325
  119.4 56.7 %collective-permute-start.20 = (bf16[64,8192]{1,0:T(8,128)(2,1)S(1)}, bf16[64,8192]{1,0:T(8,128)(2,1)S(1)}, u32[]{:S(2)}, u32[]{:S(2)}) collective-permute-start(bf16[64,8192]{1,0:T(8,128)(2,1)S(1)} %get-tuple-element.63), channel_id=1, source_target_pairs={{4,8},{5,9},{6,10},{7,11},{8,4},{9,5},{10,6},{11,7},{20,24},{21,25... | collective-permute-start | bytes 3145736 | tf_op jit(solution)/shard_map/ppermute | solution.py:325
  120.1 56.0 %collective-permute-start.21 = (bf16[64,8192]{1,0:T(8,128)(2,1)S(1)}, bf16[64,8192]{1,0:T(8,128)(2,1)S(1)}, u32[]{:S(2)}, u32[]{:S(2)}) collective-permute-start(bf16[64,8192]{1,0:T(8,128)(2,1)S(1)} %get-tuple-element.63), channel_id=1, source_target_pairs={{0,4},{1,5},{2,6},{3,7},{12,8},{13,9},{14,10},{15,11},{16,20},{17,... | collective-permute-start | bytes 3145736 | tf_op jit(solution)/shard_map/ppermute | solution.py:325
  151.3 23.3 %collective-permute-start.15 = (bf16[64,8192]{1,0:T(8,128)(2,1)S(1)}, bf16[64,8192]{1,0:T(8,128)(2,1)S(1)}, u32[]{:S(2)}, u32[]{:S(2)}) collective-permute-start(bf16[64,8192]{1,0:T(8,128)(2,1)S(1)} %get-tuple-element.54), channel_id=1, source_target_pairs={{0,2},{1,3},{2,0},{3,1},{4,6},{5,7},{6,4},{7,5},{8,10},{9,11},{10,... | collective-permute-start | bytes 3145736 | tf_op jit(solution)/shard_map/ppermute | solution.py:325
  153.0 28.7 %collective-permute-start.18 = (bf16[64,8192]{1,0:T(8,128)(2,1)S(1)}, bf16[64,8192]{1,0:T(8,128)(2,1)S(1)}, u32[]{:S(2)}, u32[]{:S(2)}) collective-permute-start(bf16[64,8192]{1,0:T(8,128)(2,1)S(1)} %add_convert_fusion.3), channel_id=1, source_target_pairs={{4,8},{5,9},{6,10},{7,11},{8,4},{9,5},{10,6},{11,7},{20,24},{21,25... | collective-permute-start | bytes 3145736 | tf_op jit(solution)/shard_map/ppermute | solution.py:325
  154.0 39.5 %collective-permute-start.19 = (bf16[64,8192]{1,0:T(8,128)(2,1)S(1)}, bf16[64,8192]{1,0:T(8,128)(2,1)S(1)}, u32[]{:S(2)}, u32[]{:S(2)}) collective-permute-start(bf16[64,8192]{1,0:T(8,128)(2,1)S(1)} %add_convert_fusion.2), channel_id=1, source_target_pairs={{0,4},{1,5},{2,6},{3,7},{4,0},{5,1},{6,2},{7,3},{8,12},{9,13},{10,... | collective-permute-start | bytes 3145736 | tf_op jit(solution)/shard_map/ppermute | solution.py:325
  174.6 18.9 %collective-permute-start.16 = (bf16[64,8192]{1,0:T(8,128)(2,1)S(1)}, bf16[64,8192]{1,0:T(8,128)(2,1)}, u32[]{:S(2)}, u32[]{:S(2)}) collective-permute-start(bf16[64,8192]{1,0:T(8,128)(2,1)S(1)} %get-tuple-element.56), channel_id=1, source_target_pairs={{0,2},{1,3},{2,0},{3,1},{4,6},{5,7},{6,4},{7,5},{8,10},{9,11},{10,... | collective-permute-start | bytes 3145736 | tf_op jit(solution)/shard_map/ppermute | solution.py:325
  176.4 18.3 %collective-permute-start.22 = (bf16[64,8192]{1,0:T(8,128)(2,1)S(1)}, bf16[64,8192]{1,0:T(8,128)(2,1)S(1)}, u32[]{:S(2)}, u32[]{:S(2)}) collective-permute-start(bf16[64,8192]{1,0:T(8,128)(2,1)S(1)} %add_convert_fusion.1), channel_id=1, source_target_pairs={{4,8},{5,9},{6,10},{7,11},{8,4},{9,5},{10,6},{11,7},{20,24},{21,25... | collective-permute-start | bytes 3145736 | tf_op jit(solution)/shard_map/ppermute | solution.py:325
  177.5 29.4 %collective-permute-start.23 = (bf16[64,8192]{1,0:T(8,128)(2,1)S(1)}, bf16[64,8192]{1,0:T(8,128)(2,1)S(1)}, u32[]{:S(2)}, u32[]{:S(2)}) collective-permute-start(bf16[64,8192]{1,0:T(8,128)(2,1)S(1)} %add_convert_fusion), channel_id=1, source_target_pairs={{0,4},{1,5},{2,6},{3,7},{4,0},{5,1},{6,2},{7,3},{8,12},{9,13},{10,... | collective-permute-start | bytes 3145736 | tf_op jit(solution)/shard_map/ppermute | solution.py:325
  181.7 30.7 %collective-permute-start.14 = (bf16[64,8192]{1,0:T(8,128)(2,1)}, bf16[64,8192]{1,0:T(8,128)(2,1)}, u32[]{:S(2)}, u32[]{:S(2)}) collective-permute-start(bf16[64,8192]{1,0:T(8,128)(2,1)} %get-tuple-element.53), channel_id=1, source_target_pairs={{0,1},{1,0},{2,3},{3,2},{4,5},{5,4},{6,7},{7,6},{8,9},{9,8},{10,11... | collective-permute-start | bytes 3145736 | tf_op jit(solution)/shard_map/ppermute | solution.py:325
  193.5 18.9 %collective-permute-start.17 = (bf16[64,8192]{1,0:T(8,128)(2,1)}, bf16[64,8192]{1,0:T(8,128)(2,1)}, u32[]{:S(2)}, u32[]{:S(2)}) collective-permute-start(bf16[64,8192]{1,0:T(8,128)(2,1)} %collective-permute-done.16), channel_id=1, source_target_pairs={{0,1},{1,0},{2,3},{3,2},{4,5},{5,4},{6,7},{7,6},{8,9},{9,8},{10,11... | collective-permute-start | bytes 3145736 | tf_op jit(solution)/shard_map/ppermute | solution.py:325
  215.1 7.6 %collective-permute-start.27 = (f32[8,128]{1,0:T(8,128)S(1)}, f32[8,128]{1,0:T(8,128)S(1)}, u32[]{:S(2)}, u32[]{:S(2)}) collective-permute-start(f32[8,128]{1,0:T(8,128)S(1)} %add_add_fusion.1), channel_id=1, source_target_pairs={{0,4},{1,5},{2,6},{3,7},{4,0},{5,1},{6,2},{7,3},{8,12},{9,13},{10,... | collective-permute-start | bytes 12296 | tf_op jit(solution)/shard_map/ppermute | solution.py:325
  217.7 5.4 %collective-permute-start.29 = (f32[8,128]{1,0:T(8,128)S(1)}, f32[8,128]{1,0:T(8,128)S(1)}, u32[]{:S(2)}, u32[]{:S(2)}) collective-permute-start(f32[8,128]{1,0:T(8,128)S(1)} %add_add_fusion.1), channel_id=1, source_target_pairs={{0,12},{1,13},{2,14},{3,15},{4,8},{5,9},{6,10},{7,11},{8,4},{9,5},... | collective-permute-start | bytes 12296 | tf_op jit(solution)/shard_map/ppermute | solution.py:325
  (27 other events, 365.0 us)

commit v13 on v12

--- a/solution.py
+++ b/solution.py
@@ -145,9 +145,15 @@
 
 def stack(down, up):
     _, rank, width = down.shape
+    pieces = 4
+    part = width // pieces
 
     def body(down_in, up_in, out, sems):
-        copies = [pltpu.make_async_copy(r.at[0], out.at[k], sems.at[k]) for k, r in enumerate((down_in, up_in))]
+        copies = [
+            pltpu.make_async_copy(r.at[0, :, pl.ds(i * part, part)], out.at[k, :, pl.ds(i * part, part)], sems.at[k, i])
+            for k, r in enumerate((down_in, up_in))
+            for i in range(pieces)
+        ]
         for c in copies:
             c.start()
         for c in copies:
@@ -158,25 +164,25 @@
         in_specs=[HBM, HBM],
         out_specs=WHOLE,
         out_shape=pltpu.VMEM((2, rank, width), BF16),
-        scratch_shapes=[pltpu.SemaphoreType.DMA((2,))],
+        scratch_shapes=[pltpu.SemaphoreType.DMA((2, pieces))],
         compiler_params=pltpu.CompilerParams(vmem_limit_bytes=VMEM_BYTES),
     )(*in_hbm(down, up))
 
 
-def far_group(is_end, rows, factors, handed=None):
+def far_group(flags, rows, factors, handed=None):
     _, block, width = rows[0].shape
     rank = factors[0].shape[1]
     tile = min(width, 2048)
     tiles = width // tile
     total = block if handed is None else 2 * block
 
-    def body(end_ref, *refs):
+    def body(flags_ref, *refs):
         rows_in, refs = refs[:len(rows)], refs[len(rows):]
         factors_in, refs = refs[:len(factors)], refs[len(factors):]
         handed_in, refs = (None, refs) if handed is None else (refs[0], refs[1:])
         (up_ref, down_ref, dx_ref), (held, left, inner, sems) = refs[:3], refs[-4:]
         step = pl.program_id(0)
-        at_end = end_ref[0] == 1
+        at_end, below = flags_ref[0] == 1, flags_ref[1] == 1
 
         def copy(source, i):
             cut = pl.ds(i * tile, tile)
@@ -187,8 +193,7 @@
             return own if handed is None else jnp.concatenate([own, handed_in[k, :, cut]], axis=0)
 
         def factor(k, cut):
-            first = factors_in[0][k, :, cut]
-            return first if len(factors) == 1 else jnp.where(at_end, factors_in[1][k, :, cut], first)
+            return jnp.where(below, factors_in[1][k, :, cut], factors_in[0][k, :, cut])
 
         @pl.when(step == 0)
         def _():
@@ -234,23 +239,27 @@
             pltpu.SemaphoreType.DMA((tiles,)),
         ],
         compiler_params=kernel_params(),
-    )(is_end, *in_hbm(*rows), *in_vmem(*factors, *more))
-
-
-def near_groups(is_end, stage, pair, down, up, dx_late, dx_early, swapped, capacity, first1):
+    )(flags, *in_hbm(*rows), *in_vmem(*factors, *more))
+
+
+def near_groups(flags, stage, pairs, down, up, dx_late, dx_early, swapped, capacity, first1):
     plane = len(stage)
     rank, width = down.shape
     block = plane * capacity
     tile = min(width, 2048)
     tiles = width // tile
 
-    def body(end_ref, *refs):
+    def body(flags_ref, *refs):
         stage_in, refs = refs[:plane], refs[plane:]
-        pair_in, down_in, up_in, late_ref, early_ref, swapped_ref = refs[:6]
-        dx_refs, sum_refs = refs[6:10], refs[10:14]
-        left, inner = refs[14:]
+        pairs_in, (down_in, up_in, late_ref, early_ref, swapped_ref) = refs[:2], refs[2:7]
+        dx_refs, sum_refs = refs[7:11], refs[11:15]
+        left, inner = refs[15:]
         step = pl.program_id(0)
         own_in = (down_in, up_in)
+
+        def pair(k, cut):
+            return jnp.where(flags_ref[2] == 1, pairs_in[1][k, :, cut], pairs_in[0][k, :, cut])
+
         is_mine = corner(2 * block, block, 2 * rank, rank)
 
         def rows(k, cut):
@@ -269,7 +278,7 @@
             for i in range(tiles):
                 cut = pl.ds(i * tile, tile)
                 for k in range(2):
-                    both = jnp.concatenate([pair_in[k, :, cut], own_in[k][:, cut]], axis=0)
+                    both = jnp.concatenate([pair(k, cut), own_in[k][:, cut]], axis=0)
                     sums[k] += dot32(rows(k, cut), both, ROWS_OF)
             for k in range(2):
                 masked = jnp.where(is_mine, sums[k], 0.0)
@@ -281,9 +290,9 @@
             both = dot32(left[k], rows(1 - k, cut))
             sum_refs[k][...] = both[:rank]
             sum_refs[2 + k][...] = both[rank:]
-        downs = jnp.concatenate([pair_in[0, :, cut], down_in[:, cut]], axis=0)
+        downs = jnp.concatenate([pair(0, cut), down_in[:, cut]], axis=0)
         dx = dot32(inner[...], downs).astype(BF16)
-        at_end, late = end_ref[0] == 1, late_ref[...]
+        at_end, late = flags_ref[0] == 1, late_ref[...]
         moved = [jnp.where(at_end, swapped_ref[...], late), jnp.where(at_end, late, early_ref[...]), dx[:block], dx[block:]]
         for n, dx in enumerate(moved):
             for m in range(plane):
@@ -293,7 +302,7 @@
         body,
         grid=(tiles,),
         in_specs=[pl.BlockSpec(memory_space=pltpu.SMEM)]
-        + [WHOLE] * (plane + 3)
+        + [WHOLE] * (plane + 4)
         + [pl.BlockSpec((block, tile), lambda i: (0, i))] * 3,
         out_specs=[pl.BlockSpec((4 * capacity, tile), lambda i: (0, i))] * plane
         + [pl.BlockSpec((rank, tile), lambda i: (0, i))] * 4,
@@ -301,7 +310,7 @@
         + [jax.ShapeDtypeStruct((rank, width), F32)] * 4,
         scratch_shapes=[pltpu.VMEM((2, 2 * rank, 2 * block), BF16), pltpu.VMEM((2 * block, 2 * rank), BF16)],
         compiler_params=kernel_params(),
-    )(is_end, *in_vmem(*stage, pair, down, up), dx_late, dx_early, swapped)
+    )(flags, *in_vmem(*stage, *pairs, down, up), dx_late, dx_early, swapped)
 
 
 def move_adapters(plane, acts, cotan, token_task_index, task_slot_lookup, pool_down_factors, pool_up_factors):
@@ -311,14 +320,13 @@
     me = lax.axis_index("dp")
     z, column = me // plane, me % plane
     is_end = (z == 0) | (z == 3)
-    end_flag = is_end.astype(jnp.int32).reshape(1)
+    flags = jnp.stack([is_end, z < 2, z % 2 == 0]).astype(jnp.int32)
 
     def planes(pairs):
         return [(a * plane + c, b * plane + c) for a, b in pairs for c in range(plane)]
 
     swap = planes([(0, 1), (1, 0), (2, 3), (3, 2)])
     cross = planes([(1, 2), (2, 1)])
-    outward = planes([(1, 0), (2, 3)])
     inward = planes([(0, 1), (3, 2)])
 
     def send(array, pairs):
@@ -339,8 +347,8 @@
 
     down, up = pool_down_factors[0], pool_up_factors[0]
     own = stack(pool_down_factors, pool_up_factors)
-    pair = send(own, swap)
-    crossed = send(own, cross)
+    from_left = send(own, planes([(0, 1), (1, 2), (2, 3)]))
+    from_right = send(own, planes([(3, 2), (2, 1), (1, 0)]))
 
     owner, position = route(token_task_index, task_slot_lookup, ndevices)
     owner_z, turn = owner // plane, (owner % plane) ^ column
@@ -380,18 +388,18 @@
     rows2 = [r[0, :, capacity:2 * capacity] for r in (own_rows, beside_rows)] + [r[0] for r in across2]
     rows2 = jnp.concatenate(rows2, axis=1)
     stage10 = (own_rows, beside_rows) + across10
-    outer = send(crossed, outward)
-    far = send(pair, cross)
-
-    up2, down2, dx_early = far_group(end_flag, (rows2,), (crossed,))
+    far_left = send(from_left, planes([(1, 2), (2, 3)]))
+    far_right = send(from_right, planes([(2, 1), (1, 0)]))
+
+    up2, down2, dx_early = far_group(flags, (rows2,), (from_left, from_right))
     rows3, rows2 = after((rows3, rows2), dx_early)
-    up3, down3, dx_late, swapped = far_group(end_flag, (rows3, rows2), (far, outer), handed)
-    down3, swapped = send(down3, cross), send(swapped, swap)
-    up3, up2_in = send(up3, cross), send(up3, inward)
-
-    down3, swapped = lax.optimization_barrier((down3, swapped))
+    up3, down3, dx_late, swapped = far_group(flags, (rows3, rows2), (far_left, far_right), handed)
+    up2_in = send(up3, inward)
+    down3, swapped, up3 = send(down3, cross), send(swapped, swap), send(up3, cross)
+
+    swapped, down3 = lax.optimization_barrier((swapped, down3))
     dx_own, dx_beside, *dx_across, up1, down1, up0, down0 = near_groups(
-        end_flag, stage10, pair, down, up, dx_late, dx_early, swapped, capacity,
+        flags, stage10, (from_left, from_right), down, up, dx_late, dx_early, swapped, capacity,
         (2 * capacity, 2 * capacity, 0, 0),
     )
 
@@ -401,7 +409,7 @@
     down2, down1 = add(down2, swapped), add(down1, down3)
     dx_across[0] = send(dx_across[0], beside(2))
     dx_across[1] = send(after(dx_across[1], dx_across[0]), beside(2))
-    up3, up2_in = after((up3, up2_in), down2, down1, dx_across[0])
+    up2_in, up3 = after((up2_in, up3), down2, down1, dx_across[0])
     down2, down1 = send(down2, cross), send(down1, swap)
     up2, up1 = send(add(up2, up2_in), cross), send(add(up1, up3), swap)
 

time: 228 us -> 231 us (1.013)
  starting transfers between devices: 50.3 us -> 62.9 us
  waiting for transfers between devices: 123 us -> 112 us
    ppermute x30, starting transfers between devices: 50.3 us -> 62.9 us  [send(): return lax.ppermute(array, 'dp', pairs)]
    ppermute x30, waiting for transfers between devices: 123 us -> 112 us  [send(): return lax.ppermute(array, 'dp', pairs)]
  transfers between devices with their start and end apart: 30 -> 30, of which waited for: 11 -> 12; matrix products, arithmetic and copies ran while one was open for 4% -> 5% of each run, Pallas kernels for 14% -> 14%
where the time goes in v13:
time: 231 us; the launch traced here: 230 us
  waiting for transfers between devices  112 us (48%)
  starting transfers between devices  62.9 us (27%)
  Pallas kernels  35.1 us (15%)
  other arithmetic  11.1 us (5%)
  local copies, waits for them, and re-layouts  5.5 us (2%)
  between operations  3.17 us (1%)
    ppermute x30, waiting for transfers between devices, send(): return lax.ppermute(array, 'dp', pairs)  112 us
    ppermute x30, starting transfers between devices, send(): return lax.ppermute(array, 'dp', pairs)  62.9 us
    pallas_call x2, Pallas kernels, far_group(): pl.pallas_call(body, grid=(tiles,), in_specs=[pl.BlockSpec(memory_space=p...  13.2 us
    pallas_call x1, Pallas kernels, near_groups(): pl.pallas_call(body, grid=(tiles,), in_specs=[pl.BlockSpec(memory_space=p...  7.74 us
    pallas_call x1, Pallas kernels, pack(): pl.pallas_call(body, grid=(tiles,), in_specs=[pl.BlockSpec(place.shape, l...  6.36 us
    pallas_call x2, Pallas kernels, unpack(): pl.pallas_call(body, grid=(width // 2 // tile,), in_specs=[pl.BlockSpec(p...  4.79 us
  transfers between devices with their start and end apart: 30, of which 12 were waited for; matrix products, arithmetic and copies ran while one was open for 5% of the time, Pallas kernels for 14%

profile of v13, /device:TPU:0, one launch (start us, length us, event | category | flops | bytes accessed | tf_op | source)
XLA Modules:
  0.0 230.1 jit_solution(13265053122748597619)
XLA Ops:
  0.7 3.0 %shard_map.86 = bf16[2,64,8192]{2,1,0:T(8,128)(2,1)} custom-call(bf16[1,64,8192]{2,1,0:T(8,128)(2,1)} %down_in.1, bf16[1,64,8192]{2,1,0:T(8,128)(2,1)} %up_in.1), custom_call_target="tpu_custom_call" | custom-call | tf_op jit(solution)/shard_map/pallas_call | solution.py:162
  3.6 5.1 %collective-permute-start.4 = (bf16[2,64,8192]{2,1,0:T(8,128)(2,1)}, bf16[2,64,8192]{2,1,0:T(8,128)(2,1)S(1)}, u32[]{:S(2)}, u32[]{:S(2)}) collective-permute-start(bf16[2,64,8192]{2,1,0:T(8,128)(2,1)} %shard_map.86), channel_id=1, source_target_pairs={{0,4},{1,5},{2,6},{3,7},{4,8},{5,9},{6,10},{7,11},{8,12},{9,13},{1... | collective-permute-start | bytes 6291464 | tf_op jit(solution)/shard_map/ppermute | solution.py:333
  10.8 6.4 %shard_map.85 = (bf16[1,2,64,8192]{3,2,1,0:T(8,128)(2,1)S(1)}, bf16[1,2,64,8192]{3,2,1,0:T(8,128)(2,1)S(1)}, bf16[2,2,16,8192]{3,2,1,0:T(8,128)(2,1)S(1)}, bf16[...) custom-call(bf16[256,128]{1,0:T(8,128)(2,1)S(1)} %fusion.1.place_ref, bf16[128,8192]{1,0:T(8,128)(2,1)} %x_in.1, ...), custom_call_target="tpu_custom_call" | custom-call | tf_op jit(solution)/shard_map/pallas_call | solution.py:107
  18.8 23.1 %collective-permute-done.1 = bf16[2,2,16,8192]{3,2,1,0:T(8,128)(2,1)S(1)} collective-permute-done((bf16[2,2,16,8192]{3,2,1,0:T(8,128)(2,1)S(1)}, bf16[2,2,16,8192]{3,2,1,0:T(8,128)(2,1)S(1)}, u32[]{:S(2)}, u32[]{:S(2)}) %collective-permute-start.1) | collective-permute-done | bytes 1048608 | tf_op jit(solution)/shard_map/ppermute | solution.py:333
  47.0 5.6 %collective-permute-start.11 = (bf16[2,64,8192]{2,1,0:T(8,128)(2,1)}, bf16[2,64,8192]{2,1,0:T(8,128)(2,1)}, u32[]{:S(2)}, u32[]{:S(2)}) collective-permute-start(bf16[2,64,8192]{2,1,0:T(8,128)(2,1)} %pad_maximum_fusion.refs_0_), channel_id=1, source_target_pairs={{0,4},{1,5},{2,6},{3,7},{12,8},{13,9},{14,10},{15,11},{16,20},{17,... | collective-permute-start | bytes 6291464 | tf_op jit(solution)/shard_map/ppermute | solution.py:333
  52.6 5.4 %collective-permute-done.5.refs_2_.refs_5_ = bf16[2,64,8192]{2,1,0:T(8,128)(2,1)} collective-permute-done((bf16[2,64,8192]{2,1,0:T(8,128)(2,1)}, bf16[2,64,8192]{2,1,0:T(8,128)(2,1)}, u32[]{:S(2)}, u32[]{:S(2)}) %collective-permute-start.5) | collective-permute-done | bytes 2097184 | tf_op jit(solution)/shard_map/ppermute | solution.py:333
  61.4 6.5 %collective-permute-done.7 = bf16[2,2,16,8192]{3,2,1,0:T(8,128)(2,1)S(1)} collective-permute-done((bf16[2,2,16,8192]{3,2,1,0:T(8,128)(2,1)S(1)}, bf16[2,2,16,8192]{3,2,1,0:T(8,128)(2,1)S(1)}, u32[]{:S(2)}, u32[]{:S(2)}) %collective-permute-start.7) | collective-permute-done | bytes 1048608 | tf_op jit(solution)/shard_map/ppermute | solution.py:333
  71.2 2.7 %pad_maximum_fusion.1.refs_0_.refs_1_ = bf16[2,64,8192]{2,1,0:T(8,128)(2,1)} fusion(bf16[2,16,8192]{2,1,0:T(8,128)(2,1)} %bitcast.13, bf16[2,16,8192]{2,1,0:T(8,128)(2,1)} %get-tuple-element.80, bf16[2,16,8192]{2,1,0:T(8,128)(2,1)S(1)} %get-tuple-element.78, bf16[2,16,8192]{2,1,0:T(8,128)(2,1)S(1)} %get-tuple-element.76), kind=kLoop, calls=%fused_computation.1 | loop fusion | flops 8388608 | bytes 4194304 | tf_op jit(solution)/shard_map/concatenate | solution.py:389
  73.9 5.4 %shard_map.87 = (bf16[64,8192]{1,0:T(8,128)(2,1)S(1)}, bf16[64,8192]{1,0:T(8,128)(2,1)S(1)}, bf16[64,8192]{1,0:T(8,128)(2,1)S(1)}) custom-call(s32[3]{0:T(128)S(1)} %add_convert_fusion.4.flags_ref, bf16[2,64,8192]{2,1,0:T(8,128)(2,1)} %pad_maximum_fusion.1.refs_0_.refs_1_, bf16[2,64,8192]{2,1,0:T(8,128)(2,1)S(1)} %collective-permute-done.4.refs_1_.refs_4_, ...), custom_call_target="tpu_custom_call" | custom-call | tf_op jit(solution)/shard_map/pallas_call | solution.py:229
  79.3 19.4 %collective-permute-done.11.refs_4_ = bf16[2,64,8192]{2,1,0:T(8,128)(2,1)} collective-permute-done((bf16[2,64,8192]{2,1,0:T(8,128)(2,1)}, bf16[2,64,8192]{2,1,0:T(8,128)(2,1)}, u32[]{:S(2)}, u32[]{:S(2)}) %collective-permute-start.11) | collective-permute-done | bytes 2097184 | tf_op jit(solution)/shard_map/ppermute | solution.py:333
  98.7 7.7 %collective-permute-done.10.refs_3_ = bf16[2,64,8192]{2,1,0:T(8,128)(2,1)} collective-permute-done((bf16[2,64,8192]{2,1,0:T(8,128)(2,1)}, bf16[2,64,8192]{2,1,0:T(8,128)(2,1)}, u32[]{:S(2)}, u32[]{:S(2)}) %collective-permute-start.10) | collective-permute-done | bytes 2097184 | tf_op jit(solution)/shard_map/ppermute | solution.py:333
  106.4 7.9 %shard_map.88 = (bf16[64,8192]{1,0:T(8,128)(2,1)S(1)}, bf16[64,8192]{1,0:T(8,128)(2,1)S(1)}, bf16[64,8192]{1,0:T(8,128)(2,1)S(1)}, bf16[64,8192]{1,0:T(8,128)(2,1)S(1)}) custom-call(s32[3]{0:T(128)S(1)} %add_convert_fusion.4.flags_ref, bf16[2,64,8192]{2,1,0:T(8,128)(2,1)} %pad_maximum_fusion.refs_0_, bf16[2,64,8192]{2,1,0:T(8,128)(2,1)} %pad_maximum_fusion.1.refs_0_.refs_1_, ...), custom_call_target="tpu_custom_call" | custom-call | tf_op jit(solution)/shard_map/pallas_call | solution.py:229
  114.3 3.7 %collective-permute-start.12 = (bf16[64,8192]{1,0:T(8,128)(2,1)S(1)}, bf16[64,8192]{1,0:T(8,128)(2,1)S(1)}, u32[]{:S(2)}, u32[]{:S(2)}) collective-permute-start(bf16[64,8192]{1,0:T(8,128)(2,1)S(1)} %get-tuple-element.49), channel_id=1, source_target_pairs={{0,4},{1,5},{2,6},{3,7},{4,0},{5,1},{6,2},{7,3},{8,12},{9,13},{10,... | collective-permute-start | bytes 3145736 | tf_op jit(solution)/shard_map/ppermute | solution.py:333
  120.2 6.2 %collective-permute-start.20 = (bf16[64,8192]{1,0:T(8,128)(2,1)S(1)}, bf16[64,8192]{1,0:T(8,128)(2,1)S(1)}, u32[]{:S(2)}, u32[]{:S(2)}) collective-permute-start(bf16[64,8192]{1,0:T(8,128)(2,1)S(1)} %get-tuple-element.63), channel_id=1, source_target_pairs={{0,4},{1,5},{2,6},{3,7},{12,8},{13,9},{14,10},{15,11},{16,20},{17,... | collective-permute-start | bytes 3145736 | tf_op jit(solution)/shard_map/ppermute | solution.py:333
  127.1 14.6 %collective-permute-done.12.refs_10_ = bf16[64,8192]{1,0:T(8,128)(2,1)S(1)} collective-permute-done((bf16[64,8192]{1,0:T(8,128)(2,1)S(1)}, bf16[64,8192]{1,0:T(8,128)(2,1)S(1)}, u32[]{:S(2)}, u32[]{:S(2)}) %collective-permute-start.12) | collective-permute-done | bytes 1048608 | tf_op jit(solution)/shard_map/ppermute | solution.py:333
  141.7 7.7 %shard_map.89 = (bf16[64,8192]{1,0:T(8,128)(2,1)S(1)}, bf16[64,8192]{1,0:T(8,128)(2,1)}, bf16[64,8192]{1,0:T(8,128)(2,1)S(1)}, bf16[64,8192]{1,0:T(8,128)(2,1)S(...) custom-call(s32[3]{0:T(128)S(1)} %add_convert_fusion.4.flags_ref, ...), custom_call_target="tpu_custom_call" | custom-call | tf_op jit(solution)/shard_map/pallas_call | solution.py:301
  152.2 8.6 %collective-permute-start.19 = (bf16[64,8192]{1,0:T(8,128)(2,1)S(1)}, bf16[64,8192]{1,0:T(8,128)(2,1)S(1)}, u32[]{:S(2)}, u32[]{:S(2)}) collective-permute-start(bf16[64,8192]{1,0:T(8,128)(2,1)S(1)} %add_convert_fusion.2), channel_id=1, source_target_pairs={{0,4},{1,5},{2,6},{3,7},{4,0},{5,1},{6,2},{7,3},{8,12},{9,13},{10,... | collective-permute-start | bytes 3145736 | tf_op jit(solution)/shard_map/ppermute | solution.py:333
  160.8 12.0 %collective-permute-done.15.refs_2_ = bf16[64,8192]{1,0:T(8,128)(2,1)S(1)} collective-permute-done((bf16[64,8192]{1,0:T(8,128)(2,1)S(1)}, bf16[64,8192]{1,0:T(8,128)(2,1)S(1)}, u32[]{:S(2)}, u32[]{:S(2)}) %collective-permute-start.15) | collective-permute-done | bytes 1048608 | tf_op jit(solution)/shard_map/ppermute | solution.py:333
  175.7 8.6 %collective-permute-start.23 = (bf16[64,8192]{1,0:T(8,128)(2,1)S(1)}, bf16[64,8192]{1,0:T(8,128)(2,1)S(1)}, u32[]{:S(2)}, u32[]{:S(2)}) collective-permute-start(bf16[64,8192]{1,0:T(8,128)(2,1)S(1)} %add_convert_fusion), channel_id=1, source_target_pairs={{0,4},{1,5},{2,6},{3,7},{4,0},{5,1},{6,2},{7,3},{8,12},{9,13},{10,... | collective-permute-start | bytes 3145736 | tf_op jit(solution)/shard_map/ppermute | solution.py:333
  184.3 6.0 %collective-permute-done.16 = bf16[64,8192]{1,0:T(8,128)(2,1)} collective-permute-done((bf16[64,8192]{1,0:T(8,128)(2,1)S(1)}, bf16[64,8192]{1,0:T(8,128)(2,1)}, u32[]{:S(2)}, u32[]{:S(2)}) %collective-permute-start.16) | collective-permute-done | bytes 1048608 | tf_op jit(solution)/shard_map/ppermute | solution.py:333
  191.6 13.5 %collective-permute-done.23 = bf16[64,8192]{1,0:T(8,128)(2,1)S(1)} collective-permute-done((bf16[64,8192]{1,0:T(8,128)(2,1)S(1)}, bf16[64,8192]{1,0:T(8,128)(2,1)S(1)}, u32[]{:S(2)}, u32[]{:S(2)}) %collective-permute-start.23) | collective-permute-done | bytes 1048608 | tf_op jit(solution)/shard_map/ppermute | solution.py:333
  210.7 2.4 %shard_map.90.refs_4_ = bf16[128,8192]{1,0:T(8,128)(2,1)} custom-call(bf16[128,256]{1,0:T(8,128)(2,1)S(1)} %fusion.place_ref, bf16[64,8192]{1,0:T(8,128)(2,1)} %copy-done.10, bf16[64,8192]{1,0:T(8,128)(2,1)S(1)} %collective-permute-done.14.refs_1_, bf16[64,8192]{1,0:T(8,128)(2,1)S(1)} %collective-permute-done.15.refs_2_, ...), custom_call_target="tpu_custom_call" | custom-call | tf_op jit(solution)/shard_map/pallas_call | solution.py:128
  213.3 6.0 %collective-permute-start.27 = (f32[8,128]{1,0:T(8,128)S(1)}, f32[8,128]{1,0:T(8,128)S(1)}, u32[]{:S(2)}, u32[]{:S(2)}) collective-permute-start(f32[8,128]{1,0:T(8,128)S(1)} %add_add_fusion.1), channel_id=1, source_target_pairs={{0,4},{1,5},{2,6},{3,7},{4,0},{5,1},{6,2},{7,3},{8,12},{9,13},{10,... | collective-permute-start | bytes 12296 | tf_op jit(solution)/shard_map/ppermute | solution.py:333
  227.4 2.8 %multiply_bitcast_fusion = (f32[1,64,8192]{2,1,0:T(8,128)}, f32[1,64,8192]{2,1,0:T(8,128)}) fusion(f32[]{:T(128)} %bitcast.14, bf16[64,8192]{1,0:T(8,128)(2,1)S(1)} %copy-done.18, f32[64,8192]{1,0:T(8,128)S(1)} %copy-done.1, bf16[64,8192]{1,0:T(8,128)(2,1)S(1)} %copy-done.16, bf16[64,8192]{1,0:T(8,128)(2,1)S(1)} %copy-done.14, f32[64,8192]{1,0:T(8,128)S(1)} %copy-done.3, ...), kind=kLoop, calls=%fused_computation.2 | loop fusion | flops 5242880 | bytes 12582916 | tf_op jit(solution)/shard_map/broadcast_in_dim | solution.py:37
  (112 shorter events, 36.8 us)
Async XLA Ops:
  3.6 55.7 %collective-permute-start.4 = (bf16[2,64,8192]{2,1,0:T(8,128)(2,1)}, bf16[2,64,8192]{2,1,0:T(8,128)(2,1)S(1)}, u32[]{:S(2)}, u32[]{:S(2)}) collective-permute-start(bf16[2,64,8192]{2,1,0:T(8,128)(2,1)} %shard_map.86), channel_id=1, source_target_pairs={{0,4},{1,5},{2,6},{3,7},{4,8},{5,9},{6,10},{7,11},{8,12},{9,13},{1... | collective-permute-start | bytes 6291464 | tf_op jit(solution)/shard_map/ppermute | solution.py:333
  8.7 49.3 %collective-permute-start.5 = (bf16[2,64,8192]{2,1,0:T(8,128)(2,1)}, bf16[2,64,8192]{2,1,0:T(8,128)(2,1)}, u32[]{:S(2)}, u32[]{:S(2)}) collective-permute-start(bf16[2,64,8192]{2,1,0:T(8,128)(2,1)} %shard_map.86), channel_id=1, source_target_pairs={{12,8},{13,9},{14,10},{15,11},{8,4},{9,5},{10,6},{11,7},{4,0},{5,1... | collective-permute-start | bytes 6291464 | tf_op jit(solution)/shard_map/ppermute | solution.py:333
  17.1 24.7 %collective-permute-start.1 = (bf16[2,2,16,8192]{3,2,1,0:T(8,128)(2,1)S(1)}, bf16[2,2,16,8192]{3,2,1,0:T(8,128)(2,1)S(1)}, u32[]{:S(2)}, u32[]{:S(2)}) collective-permute-start(bf16[2,2,16,8192]{3,2,1,0:T(8,128)(2,1)S(1)} %get-tuple-element.41), channel_id=1, source_target_pairs={{0,2},{1,3},{2,0},{3,1},{4,6},{5,7},{6,4},{7,5},{8,10},{9,11},{10,... | collective-permute-start | bytes 3145736 | tf_op jit(solution)/shard_map/ppermute | solution.py:333
  18.7 24.8 %collective-permute-start = (bf16[1,2,64,8192]{3,2,1,0:T(8,128)(2,1)S(1)}, bf16[1,2,64,8192]{3,2,1,0:T(8,128)(2,1)S(1)}, u32[]{:S(2)}, u32[]{:S(2)}) collective-permute-start(bf16[1,2,64,8192]{3,2,1,0:T(8,128)(2,1)S(1)} %get-tuple-element.39), channel_id=1, source_target_pairs={{0,1},{1,0},{2,3},{3,2},{4,5},{5,4},{6,7},{7,6},{8,9},{9,8},{10,11... | collective-permute-start | bytes 6291464 | tf_op jit(solution)/shard_map/ppermute | solution.py:333
  41.8 26.1 %collective-permute-start.7 = (bf16[2,2,16,8192]{3,2,1,0:T(8,128)(2,1)S(1)}, bf16[2,2,16,8192]{3,2,1,0:T(8,128)(2,1)S(1)}, u32[]{:S(2)}, u32[]{:S(2)}) collective-permute-start(bf16[2,2,16,8192]{3,2,1,0:T(8,128)(2,1)S(1)} %get-tuple-element.44), channel_id=1, source_target_pairs={{0,2},{1,3},{2,0},{3,1},{4,6},{5,7},{6,4},{7,5},{8,10},{9,11},{10,... | collective-permute-start | bytes 3145736 | tf_op jit(solution)/shard_map/ppermute | solution.py:333
  43.5 75.3 %collective-permute-start.2 = (bf16[2,2,32,8192]{3,2,1,0:T(8,128)(2,1)}, bf16[2,2,32,8192]{3,2,1,0:T(8,128)(2,1)}, u32[]{:S(2)}, u32[]{:S(2)}) collective-permute-start(bf16[2,2,32,8192]{3,2,1,0:T(8,128)(2,1)} %get-tuple-element.42), channel_id=1, source_target_pairs={{0,2},{1,3},{2,0},{3,1},{4,6},{5,7},{6,4},{7,5},{8,10},{9,11},{10,... | collective-permute-start | bytes 6291464 | tf_op jit(solution)/shard_map/ppermute | solution.py:333
  47.0 51.7 %collective-permute-start.11 = (bf16[2,64,8192]{2,1,0:T(8,128)(2,1)}, bf16[2,64,8192]{2,1,0:T(8,128)(2,1)}, u32[]{:S(2)}, u32[]{:S(2)}) collective-permute-start(bf16[2,64,8192]{2,1,0:T(8,128)(2,1)} %pad_maximum_fusion.refs_0_), channel_id=1, source_target_pairs={{0,4},{1,5},{2,6},{3,7},{12,8},{13,9},{14,10},{15,11},{16,20},{17,... | collective-permute-start | bytes 6291464 | tf_op jit(solution)/shard_map/ppermute | solution.py:333
  58.0 48.4 %collective-permute-start.10 = (bf16[2,64,8192]{2,1,0:T(8,128)(2,1)}, bf16[2,64,8192]{2,1,0:T(8,128)(2,1)}, u32[]{:S(2)}, u32[]{:S(2)}) collective-permute-start(bf16[2,64,8192]{2,1,0:T(8,128)(2,1)} %collective-permute-done.5.refs_2_.refs_5_), channel_id=1, source_target_pairs={{8,4},{9,5},{10,6},{11,7},{4,0},{5,1},{6,2},{7,3},{24,20},{25,21},... | collective-permute-start | bytes 6291464 | tf_op jit(solution)/shard_map/ppermute | solution.py:333
  59.3 47.1 %collective-permute-start.9 = (bf16[2,64,8192]{2,1,0:T(8,128)(2,1)S(1)}, bf16[2,64,8192]{2,1,0:T(8,128)(2,1)}, u32[]{:S(2)}, u32[]{:S(2)}) collective-permute-start(bf16[2,64,8192]{2,1,0:T(8,128)(2,1)S(1)} %collective-permute-done.4.refs_1_.refs_4_), channel_id=1, source_target_pairs={{4,8},{5,9},{6,10},{7,11},{8,12},{9,13},{10,14},{11,15},{20,24},{2... | collective-permute-start | bytes 6291464 | tf_op jit(solution)/shard_map/ppermute | solution.py:333
  114.3 27.4 %collective-permute-start.12 = (bf16[64,8192]{1,0:T(8,128)(2,1)S(1)}, bf16[64,8192]{1,0:T(8,128)(2,1)S(1)}, u32[]{:S(2)}, u32[]{:S(2)}) collective-permute-start(bf16[64,8192]{1,0:T(8,128)(2,1)S(1)} %get-tuple-element.49), channel_id=1, source_target_pairs={{0,4},{1,5},{2,6},{3,7},{4,0},{5,1},{6,2},{7,3},{8,12},{9,13},{10,... | collective-permute-start | bytes 3145736 | tf_op jit(solution)/shard_map/ppermute | solution.py:333
  118.1 23.6 %collective-permute-start.13 = (bf16[64,8192]{1,0:T(8,128)(2,1)S(1)}, bf16[64,8192]{1,0:T(8,128)(2,1)S(1)}, u32[]{:S(2)}, u32[]{:S(2)}) collective-permute-start(bf16[64,8192]{1,0:T(8,128)(2,1)S(1)} %get-tuple-element.50), channel_id=1, source_target_pairs={{4,8},{5,9},{6,10},{7,11},{8,4},{9,5},{10,6},{11,7},{20,24},{21,25... | collective-permute-start | bytes 3145736 | tf_op jit(solution)/shard_map/ppermute | solution.py:333
  120.1 21.6 %collective-permute-start.3 = (bf16[1,2,32,8192]{3,2,1,0:T(8,128)(2,1)S(1)}, bf16[1,2,32,8192]{3,2,1,0:T(8,128)(2,1)S(1)}, u32[]{:S(2)}, u32[]{:S(2)}) collective-permute-start(bf16[1,2,32,8192]{3,2,1,0:T(8,128)(2,1)S(1)} %slice.40), channel_id=1, source_target_pairs={{0,1},{1,0},{2,3},{3,2},{4,5},{5,4},{6,7},{7,6},{8,9},{9,8},{10,11... | collective-permute-start | bytes 3145736 | tf_op jit(solution)/shard_map/ppermute | solution.py:333
  120.2 54.2 %collective-permute-start.20 = (bf16[64,8192]{1,0:T(8,128)(2,1)S(1)}, bf16[64,8192]{1,0:T(8,128)(2,1)S(1)}, u32[]{:S(2)}, u32[]{:S(2)}) collective-permute-start(bf16[64,8192]{1,0:T(8,128)(2,1)S(1)} %get-tuple-element.63), channel_id=1, source_target_pairs={{0,4},{1,5},{2,6},{3,7},{12,8},{13,9},{14,10},{15,11},{16,20},{17,... | collective-permute-start | bytes 3145736 | tf_op jit(solution)/shard_map/ppermute | solution.py:333
  126.4 48.0 %collective-permute-start.21 = (bf16[64,8192]{1,0:T(8,128)(2,1)S(1)}, bf16[64,8192]{1,0:T(8,128)(2,1)S(1)}, u32[]{:S(2)}, u32[]{:S(2)}) collective-permute-start(bf16[64,8192]{1,0:T(8,128)(2,1)S(1)} %get-tuple-element.63), channel_id=1, source_target_pairs={{4,8},{5,9},{6,10},{7,11},{8,4},{9,5},{10,6},{11,7},{20,24},{21,25... | collective-permute-start | bytes 3145736 | tf_op jit(solution)/shard_map/ppermute | solution.py:333
  149.5 23.4 %collective-permute-start.15 = (bf16[64,8192]{1,0:T(8,128)(2,1)S(1)}, bf16[64,8192]{1,0:T(8,128)(2,1)S(1)}, u32[]{:S(2)}, u32[]{:S(2)}) collective-permute-start(bf16[64,8192]{1,0:T(8,128)(2,1)S(1)} %get-tuple-element.54), channel_id=1, source_target_pairs={{0,2},{1,3},{2,0},{3,1},{4,6},{5,7},{6,4},{7,5},{8,10},{9,11},{10,... | collective-permute-start | bytes 3145736 | tf_op jit(solution)/shard_map/ppermute | solution.py:333
  151.3 33.0 %collective-permute-start.18 = (bf16[64,8192]{1,0:T(8,128)(2,1)S(1)}, bf16[64,8192]{1,0:T(8,128)(2,1)S(1)}, u32[]{:S(2)}, u32[]{:S(2)}) collective-permute-start(bf16[64,8192]{1,0:T(8,128)(2,1)S(1)} %add_convert_fusion.3), channel_id=1, source_target_pairs={{4,8},{5,9},{6,10},{7,11},{8,4},{9,5},{10,6},{11,7},{20,24},{21,25... | collective-permute-start | bytes 3145736 | tf_op jit(solution)/shard_map/ppermute | solution.py:333
  152.2 38.1 %collective-permute-start.19 = (bf16[64,8192]{1,0:T(8,128)(2,1)S(1)}, bf16[64,8192]{1,0:T(8,128)(2,1)S(1)}, u32[]{:S(2)}, u32[]{:S(2)}) collective-permute-start(bf16[64,8192]{1,0:T(8,128)(2,1)S(1)} %add_convert_fusion.2), channel_id=1, source_target_pairs={{0,4},{1,5},{2,6},{3,7},{4,0},{5,1},{6,2},{7,3},{8,12},{9,13},{10,... | collective-permute-start | bytes 3145736 | tf_op jit(solution)/shard_map/ppermute | solution.py:333
  172.9 17.5 %collective-permute-start.16 = (bf16[64,8192]{1,0:T(8,128)(2,1)S(1)}, bf16[64,8192]{1,0:T(8,128)(2,1)}, u32[]{:S(2)}, u32[]{:S(2)}) collective-permute-start(bf16[64,8192]{1,0:T(8,128)(2,1)S(1)} %get-tuple-element.56), channel_id=1, source_target_pairs={{0,2},{1,3},{2,0},{3,1},{4,6},{5,7},{6,4},{7,5},{8,10},{9,11},{10,... | collective-permute-start | bytes 3145736 | tf_op jit(solution)/shard_map/ppermute | solution.py:333
  174.6 17.0 %collective-permute-start.22 = (bf16[64,8192]{1,0:T(8,128)(2,1)S(1)}, bf16[64,8192]{1,0:T(8,128)(2,1)S(1)}, u32[]{:S(2)}, u32[]{:S(2)}) collective-permute-start(bf16[64,8192]{1,0:T(8,128)(2,1)S(1)} %add_convert_fusion.1), channel_id=1, source_target_pairs={{4,8},{5,9},{6,10},{7,11},{8,4},{9,5},{10,6},{11,7},{20,24},{21,25... | collective-permute-start | bytes 3145736 | tf_op jit(solution)/shard_map/ppermute | solution.py:333
  175.7 29.4 %collective-permute-start.23 = (bf16[64,8192]{1,0:T(8,128)(2,1)S(1)}, bf16[64,8192]{1,0:T(8,128)(2,1)S(1)}, u32[]{:S(2)}, u32[]{:S(2)}) collective-permute-start(bf16[64,8192]{1,0:T(8,128)(2,1)S(1)} %add_convert_fusion), channel_id=1, source_target_pairs={{0,4},{1,5},{2,6},{3,7},{4,0},{5,1},{6,2},{7,3},{8,12},{9,13},{10,... | collective-permute-start | bytes 3145736 | tf_op jit(solution)/shard_map/ppermute | solution.py:333
  184.3 26.3 %collective-permute-start.14 = (bf16[64,8192]{1,0:T(8,128)(2,1)}, bf16[64,8192]{1,0:T(8,128)(2,1)S(1)}, u32[]{:S(2)}, u32[]{:S(2)}) collective-permute-start(bf16[64,8192]{1,0:T(8,128)(2,1)} %get-tuple-element.53), channel_id=1, source_target_pairs={{0,1},{1,0},{2,3},{3,2},{4,5},{5,4},{6,7},{7,6},{8,9},{9,8},{10,11... | collective-permute-start | bytes 3145736 | tf_op jit(solution)/shard_map/ppermute | solution.py:333
  190.3 20.3 %collective-permute-start.17 = (bf16[64,8192]{1,0:T(8,128)(2,1)}, bf16[64,8192]{1,0:T(8,128)(2,1)S(1)}, u32[]{:S(2)}, u32[]{:S(2)}) collective-permute-start(bf16[64,8192]{1,0:T(8,128)(2,1)} %collective-permute-done.16), channel_id=1, source_target_pairs={{0,1},{1,0},{2,3},{3,2},{4,5},{5,4},{6,7},{7,6},{8,9},{9,8},{10,11... | collective-permute-start | bytes 3145736 | tf_op jit(solution)/shard_map/ppermute | solution.py:333
  213.3 11.1 %collective-permute-start.27 = (f32[8,128]{1,0:T(8,128)S(1)}, f32[8,128]{1,0:T(8,128)S(1)}, u32[]{:S(2)}, u32[]{:S(2)}) collective-permute-start(f32[8,128]{1,0:T(8,128)S(1)} %add_add_fusion.1), channel_id=1, source_target_pairs={{0,4},{1,5},{2,6},{3,7},{4,0},{5,1},{6,2},{7,3},{8,12},{9,13},{10,... | collective-permute-start | bytes 12296 | tf_op jit(solution)/shard_map/ppermute | solution.py:333
  220.6 5.4 %collective-permute-start.29 = (f32[8,128]{1,0:T(8,128)S(1)}, f32[8,128]{1,0:T(8,128)S(1)}, u32[]{:S(2)}, u32[]{:S(2)}) collective-permute-start(f32[8,128]{1,0:T(8,128)S(1)} %add_add_fusion.1), channel_id=1, source_target_pairs={{0,12},{1,13},{2,14},{3,15},{4,8},{5,9},{6,10},{7,11},{8,4},{9,5},... | collective-permute-start | bytes 12296 | tf_op jit(solution)/shard_map/ppermute | solution.py:333
  (27 other events, 407.3 us)

commit v14 on v8

--- a/solution.py
+++ b/solution.py
@@ -28,9 +28,9 @@
     return owner, position
 
 
-def clipped(raw_down, raw_up, ndevices, add_up):
+def clipped(raw_down, raw_up, ndevices):
     local_sq = jnp.sum(raw_down * raw_down) + jnp.sum(raw_up * raw_up)
-    total = add_up(local_sq)
+    total = lax.psum(local_sq, "dp")
     norm = jnp.sqrt(total + 1e-06)
     limit = jnp.sqrt(jnp.float32(2 * raw_down.shape[0] * raw_down.shape[1] * ndevices))
     factor = jnp.minimum(jnp.float32(1.0), limit / norm)
@@ -59,7 +59,7 @@
     grad_acts = dot32(placed, returned, OUTER).astype(BF16)
     raw_up = dot32(hidden, rows_g, OUTER)
     raw_down = dot32(inner, rows_x, OUTER)
-    return (grad_acts,) + clipped(raw_down, raw_up, ndevices, lambda term: lax.psum(term, "dp"))
+    return (grad_acts,) + clipped(raw_down, raw_up, ndevices)
 
 
 def in_hbm(*arrays):
@@ -115,23 +115,78 @@
     )(place, *in_hbm(acts, cotan))
 
 
-def unpack(place, blocks, tokens):
+def unpack(place, blocks, tokens, half, into=None):
     width = blocks[0].shape[1]
-    tile = min(width, 2048)
+    tile = min(width // 2, 2048)
+    first = half * (width // 2 // tile)
+    rest = () if into is None else (into,)
 
     def body(place_ref, *refs):
-        rows = jnp.concatenate([ref[...] for ref in refs[:-1]], axis=0)
+        rows = jnp.concatenate([ref[...] for ref in refs[:len(blocks)]], axis=0)
         refs[-1][...] = dot32(place_ref[...], rows).astype(BF16)
 
     return pl.pallas_call(
         body,
+        grid=(width // 2 // tile,),
+        in_specs=[pl.BlockSpec(place.shape, lambda i: (0, 0))]
+        + [pl.BlockSpec((b.shape[0], tile), lambda i: (0, i + first)) for b in blocks]
+        + [pl.BlockSpec(memory_space=pl.ANY)] * len(rest),
+        out_specs=pl.BlockSpec((tokens, tile), lambda i: (0, i + first)),
+        out_shape=jax.ShapeDtypeStruct((tokens, width), BF16),
+        input_output_aliases={1 + len(blocks): 0} if rest else {},
+        compiler_params=kernel_params(),
+    )(place, *in_hbm(blocks[0]), *blocks[1:], *rest)
+
+
+def final_sum(first, *others):
+    rank, width = first.shape
+    tile = min(width, 1024)
+
+    def body(first_ref, *refs):
+        other_refs, (total_ref, square_ref) = refs[:-2], refs[-2:]
+        squares = jnp.zeros((8, 128), F32)
+        for i in range(width // tile):
+            cut = pl.ds(i * tile, tile)
+            total = first_ref[:, cut]
+            for ref in other_refs:
+                total += ref[:, cut].astype(F32)
+            total_ref[:, cut] = total
+            total = total * total
+            for r in range(0, rank, 8):
+                for c in range(0, tile, 128):
+                    squares += total[r:r + 8, c:c + 128]
+        square_ref[...] = squares
+
+    return pl.pallas_call(
+        body,
+        in_specs=[WHOLE] * (1 + len(others)),
+        out_specs=[WHOLE] * 2,
+        out_shape=[pltpu.VMEM((rank, width), F32), pltpu.VMEM((8, 128), F32)],
+        compiler_params=pltpu.CompilerParams(vmem_limit_bytes=VMEM_BYTES),
+    )(*in_vmem(first, *others))
+
+
+def scaled(raws, parts, ndevices):
+    rank, width = raws[0].shape
+    tile = min(width, 1024)
+    limit = float(2 * rank * width * ndevices) ** 0.5
+
+    def body(*refs):
+        raw_refs, part_refs, out_refs = refs[:len(raws)], refs[len(raws):-len(raws)], refs[-len(raws):]
+        total = jnp.sum(sum(ref[...] for ref in part_refs), axis=(0, 1), keepdims=True)
+        factor = jnp.minimum(jnp.float32(1.0), jnp.float32(limit) / jnp.sqrt(total + 1e-06))
+        cut = pl.ds(pl.multiple_of(pl.program_id(0) * tile, tile), tile)
+        for raw_ref, out_ref in zip(raw_refs, out_refs):
+            out_ref[0] = raw_ref[:, cut] * factor
+
+    return pl.pallas_call(
+        body,
         grid=(width // tile,),
-        in_specs=[pl.BlockSpec(place.shape, lambda i: (0, 0))]
-        + [pl.BlockSpec((b.shape[0], tile), lambda i: (0, i)) for b in blocks],
-        out_specs=pl.BlockSpec((tokens, tile), lambda i: (0, i)),
-        out_shape=jax.ShapeDtypeStruct((tokens, width), BF16),
+        in_specs=[WHOLE] * (len(raws) + len(parts)),
+        out_specs=[pl.BlockSpec((1, rank, tile), lambda i: (0, 0, i))] * len(raws),
+        out_shape=[jax.ShapeDtypeStruct((1, rank, width), F32)] * len(raws),
         compiler_params=kernel_params(),
-    )(place, *in_hbm(blocks[0]), *blocks[1:])
+    )(*in_vmem(*raws, *parts))
 
 
 def corner(rows, first_rows, columns, first_columns):
@@ -302,14 +357,6 @@
     def beside(m):
         return [(i, (i // plane) * plane + ((i % plane) ^ m)) for i in range(ndevices)]
 
-    def add_up(term):
-        around = [beside(m) for m in range(1, plane)]
-        along = [[(i, (i // plane ^ m) * plane + i % plane) for i in range(ndevices)] for m in range(1, 4)]
-        term = jnp.broadcast_to(term, (8, 128))
-        term = term + sum(send(term, pairs) for pairs in around)
-        term = after(term, dx_across[1])
-        return (term + sum(after([send(term, pairs) for pairs in along], grad_acts)))[0, 0]
-
     down, up = pool_down_factors[0], pool_up_factors[0]
     own = jnp.concatenate([pool_down_factors, pool_up_factors])
     pair = send(own, swap)
@@ -349,7 +396,7 @@
     rows3 = jnp.concatenate([r[0, :, :capacity] for r in stage3], axis=1)
     handed = send(rows3, inward)
     across2 = over_x(after(across2, across3[0]))
-    across10 = over_x(after(across10, across2[0]))
+    across10 = over_x(after(across10, across2[1]))
     rows2 = [r[0, :, capacity:2 * capacity] for r in (own_rows, beside_rows)] + [r[0] for r in across2]
     rows2 = jnp.concatenate(rows2, axis=1)
     stage10 = (own_rows, beside_rows) + across10
@@ -372,16 +419,22 @@
         return (a.astype(F32) + b.astype(F32)).astype(BF16)
 
     down2, down1 = add(down2, swapped), add(down1, down3)
-    dx_across = [send(block, beside(2)) for block in dx_across]
+    dx_across[0] = send(dx_across[0], beside(2))
+    dx_across[1] = send(after(dx_across[1], dx_across[0]), beside(2))
     up2_in, up3 = after((up2_in, up3), down2, down1, dx_across[0])
     down2, down1 = send(down2, cross), send(down1, swap)
     up2, up1 = send(add(up2, up2_in), cross), send(add(up1, up3), swap)
 
     back = [dx_own, send(dx_beside, beside(1)), dx_across[0], send(dx_across[1], beside(1))]
-    grad_acts = unpack(place_back.T, back, tokens)
-    raw_up = up0 + up2.astype(F32) + up1.astype(F32)
-    raw_down = down0 + down2.astype(F32) + down1.astype(F32)
-    return (grad_acts,) + clipped(raw_down, raw_up, ndevices, add_up)
+    half_acts = unpack(place_back.T, back, tokens, 0)
+    grad_acts = unpack(place_back.T, back, tokens, 1, half_acts)
+    raw_down, down_squares = final_sum(down0, down2, down1)
+    raw_up, up_squares = final_sum(up0, up2, up1)
+    part = down_squares + up_squares
+    part = part + sum(after([send(part, beside(m)) for m in range(1, plane)], half_acts))
+    along = [[(i, (i // plane ^ m) * plane + i % plane) for i in range(ndevices)] for m in range(1, 4)]
+    parts = after([send(part, pairs) for pairs in along], grad_acts)
+    return (grad_acts, *scaled((raw_down, raw_up), (part, *parts), ndevices))
 
 
 def solution(mesh):

time: 227 us -> 224 us (0.987)
  other arithmetic: 11.4 us -> 6.17 us
  Pallas kernels: 31.4 us -> 36.2 us
    pallas_call x1 -> x5, Pallas kernels: 5.23 us -> 9.83 us  [the longest x2 4.79 us: unpack(): pl.pallas_call(body, grid=(width // 2 // tile,), in_specs=[pl.BlockSpec(p...]
    broadcast_in_dim x1 -> x0, other arithmetic: 2.8 us -> none  [clipped(): return ((raw_down * factor)[None], (raw_up * factor)[None])]
    reduce_sum x2 -> x0, other arithmetic: 2.32 us -> none  [clipped(): local_sq = jnp.sum(raw_down * raw_down) + jnp.sum(raw_up * raw_up)]
    unnamed x43 -> x17, local copies, waits for them, and re-layouts: 5.46 us -> 4.5 us
  transfers between devices with their start and end apart: 30 -> 30, of which waited for: 13 -> 12; matrix products, arithmetic and copies ran while one was open for 5% -> 5% of each run, Pallas kernels for 14% -> 14%
where the time goes in v14:
time: 224 us
  waiting for transfers between devices  113 us (50%)
  starting transfers between devices  57.6 us (26%)
  Pallas kernels  36.2 us (16%)
  local copies, waits for them, and re-layouts  9.53 us (4%)
  other arithmetic  6.17 us (3%)
    ppermute x30, waiting for transfers between devices, send(): return lax.ppermute(array, 'dp', pairs)  113 us
    ppermute x30, starting transfers between devices, send(): return lax.ppermute(array, 'dp', pairs)  57.6 us
    pallas_call x2, Pallas kernels, far_group(): pl.pallas_call(body, grid=(tiles,), in_specs=[pl.BlockSpec(memory_space=p...  13 us
    pallas_call x1, Pallas kernels, near_groups(): pl.pallas_call(body, grid=(tiles,), in_specs=[pl.BlockSpec(memory_space=p...  7.09 us
    pallas_call x1, Pallas kernels, pack(): pl.pallas_call(body, grid=(tiles,), in_specs=[pl.BlockSpec(place.shape, l...  6.36 us
    pallas_call x2, Pallas kernels, unpack(): pl.pallas_call(body, grid=(width // 2 // tile,), in_specs=[pl.BlockSpec(p...  4.79 us
    unnamed x17, local copies, waits for them, and re-layouts  4.5 us
  transfers between devices with their start and end apart: 30, of which 12 were waited for; matrix products, arithmetic and copies ran while one was open for 5% of the time, Pallas kernels for 14%

profile of v14, /device:TPU:0, one launch (start us, length us, event | category | flops | bytes accessed | tf_op | source)
XLA Modules:
  0.0 224.0 jit_solution(7438701627341075992)
XLA Ops:
  6.0 4.6 %collective-permute-start.6 = (bf16[2,64,8192]{2,1,0:T(8,128)(2,1)}, bf16[2,64,8192]{2,1,0:T(8,128)(2,1)}, u32[]{:S(2)}, u32[]{:S(2)}) collective-permute-start(bf16[2,64,8192]{2,1,0:T(8,128)(2,1)} %constant_dynamic-update-slice_fusion), channel_id=1, source_target_pairs={{0,4},{1,5},{2,6},{3,7},{4,0},{5,1},{6,2},{7,3},{8,12},{9,13},{10,... | collective-permute-start | bytes 6291464 | tf_op jit(solution)/shard_map/ppermute | solution.py:352
  11.3 6.4 %shard_map.85 = (bf16[1,2,64,8192]{3,2,1,0:T(8,128)(2,1)S(1)}, bf16[1,2,64,8192]{3,2,1,0:T(8,128)(2,1)S(1)}, bf16[2,2,16,8192]{3,2,1,0:T(8,128)(2,1)S(1)}, bf16[...) custom-call(bf16[256,128]{1,0:T(8,128)(2,1)S(1)} %fusion.1.place_ref, bf16[128,8192]{1,0:T(8,128)(2,1)} %x_in.1, ...), custom_call_target="tpu_custom_call" | custom-call | tf_op jit(solution)/shard_map/pallas_call | solution.py:107
  20.1 22.0 %collective-permute-done.1 = bf16[2,2,16,8192]{3,2,1,0:T(8,128)(2,1)S(1)} collective-permute-done((bf16[2,2,16,8192]{3,2,1,0:T(8,128)(2,1)S(1)}, bf16[2,2,16,8192]{3,2,1,0:T(8,128)(2,1)S(1)}, u32[]{:S(2)}, u32[]{:S(2)}) %collective-permute-start.1) | collective-permute-done | bytes 1048608 | tf_op jit(solution)/shard_map/ppermute | solution.py:352
  47.5 3.6 %collective-permute-start.11 = (bf16[2,64,8192]{2,1,0:T(8,128)(2,1)}, bf16[2,64,8192]{2,1,0:T(8,128)(2,1)}, u32[]{:S(2)}, u32[]{:S(2)}) collective-permute-start(bf16[2,64,8192]{2,1,0:T(8,128)(2,1)} %pad_maximum_fusion.refs_0_), channel_id=1, source_target_pairs={{0,4},{1,5},{2,6},{3,7},{12,8},{13,9},{14,10},{15,11},{16,20},{17,... | collective-permute-start | bytes 6291464 | tf_op jit(solution)/shard_map/ppermute | solution.py:352
  52.4 4.6 %collective-permute-done.6.refs_4_ = bf16[2,64,8192]{2,1,0:T(8,128)(2,1)} collective-permute-done((bf16[2,64,8192]{2,1,0:T(8,128)(2,1)}, bf16[2,64,8192]{2,1,0:T(8,128)(2,1)}, u32[]{:S(2)}, u32[]{:S(2)}) %collective-permute-start.6) | collective-permute-done | bytes 2097184 | tf_op jit(solution)/shard_map/ppermute | solution.py:352
  59.1 6.5 %collective-permute-done.2 = bf16[2,2,16,8192]{3,2,1,0:T(8,128)(2,1)S(1)} collective-permute-done((bf16[2,2,16,8192]{3,2,1,0:T(8,128)(2,1)S(1)}, bf16[2,2,16,8192]{3,2,1,0:T(8,128)(2,1)S(1)}, u32[]{:S(2)}, u32[]{:S(2)}) %collective-permute-start.2) | collective-permute-done | bytes 1048608 | tf_op jit(solution)/shard_map/ppermute | solution.py:352
  70.7 3.0 %pad_maximum_fusion.1.refs_0_.refs_1_ = bf16[2,64,8192]{2,1,0:T(8,128)(2,1)} fusion(bf16[2,16,8192]{2,1,0:T(8,128)(2,1)} %bitcast.20, bf16[2,16,8192]{2,1,0:T(8,128)(2,1)} %get-tuple-element.92, bf16[2,16,8192]{2,1,0:T(8,128)(2,1)} %get-tuple-element.90, bf16[2,16,8192]{2,1,0:T(8,128)(2,1)} %get-tuple-element.88), kind=kLoop, calls=%fused_computation.1 | loop fusion | flops 8388608 | bytes 4194304 | tf_op jit(solution)/shard_map/concatenate | solution.py:401
  73.7 5.2 %shard_map.86 = (bf16[64,8192]{1,0:T(8,128)(2,1)S(1)}, bf16[64,8192]{1,0:T(8,128)(2,1)S(1)}, bf16[64,8192]{1,0:T(8,128)(2,1)S(1)}) custom-call(s32[1]{0:T(128)} %bitcast.1.end_ref, bf16[2,64,8192]{2,1,0:T(8,128)(2,1)} %pad_maximum_fusion.1.refs_0_.refs_1_, bf16[2,64,8192]{2,1,0:T(8,128)(2,1)} %collective-permute-done.8.refs_1_), custom_call_target="tpu_custom_call" | custom-call | tf_op jit(solution)/shard_map/pallas_call | solution.py:254
  78.9 21.6 %collective-permute-done.11.refs_4_ = bf16[2,64,8192]{2,1,0:T(8,128)(2,1)} collective-permute-done((bf16[2,64,8192]{2,1,0:T(8,128)(2,1)}, bf16[2,64,8192]{2,1,0:T(8,128)(2,1)}, u32[]{:S(2)}, u32[]{:S(2)}) %collective-permute-start.11) | collective-permute-done | bytes 2097184 | tf_op jit(solution)/shard_map/ppermute | solution.py:352
  100.5 2.5 %collective-permute-done.10.refs_3_ = bf16[2,64,8192]{2,1,0:T(8,128)(2,1)} collective-permute-done((bf16[2,64,8192]{2,1,0:T(8,128)(2,1)}, bf16[2,64,8192]{2,1,0:T(8,128)(2,1)}, u32[]{:S(2)}, u32[]{:S(2)}) %collective-permute-start.10) | collective-permute-done | bytes 2097184 | tf_op jit(solution)/shard_map/ppermute | solution.py:352
  103.0 7.8 %shard_map.87 = (bf16[64,8192]{1,0:T(8,128)(2,1)S(1)}, bf16[64,8192]{1,0:T(8,128)(2,1)S(1)}, bf16[64,8192]{1,0:T(8,128)(2,1)S(1)}, bf16[64,8192]{1,0:T(8,128)(2,1)S(1)}) custom-call(s32[1]{0:T(128)} %bitcast.1.end_ref, bf16[2,64,8192]{2,1,0:T(8,128)(2,1)} %pad_maximum_fusion.refs_0_, bf16[2,64,8192]{2,1,0:T(8,128)(2,1)} %pad_maximum_fusion.1.refs_0_.refs_1_, ...), custom_call_target="tpu_custom_call" | custom-call | tf_op jit(solution)/shard_map/pallas_call | solution.py:254
  110.8 5.1 %collective-permute-start.12 = (bf16[64,8192]{1,0:T(8,128)(2,1)S(1)}, bf16[64,8192]{1,0:T(8,128)(2,1)S(1)}, u32[]{:S(2)}, u32[]{:S(2)}) collective-permute-start(bf16[64,8192]{1,0:T(8,128)(2,1)S(1)} %get-tuple-element.55), channel_id=1, source_target_pairs={{0,4},{1,5},{2,6},{3,7},{4,0},{5,1},{6,2},{7,3},{8,12},{9,13},{10,... | collective-permute-start | bytes 3145736 | tf_op jit(solution)/shard_map/ppermute | solution.py:352
  116.6 4.8 %collective-permute-start.20 = (bf16[64,8192]{1,0:T(8,128)(2,1)S(1)}, bf16[64,8192]{1,0:T(8,128)(2,1)S(1)}, u32[]{:S(2)}, u32[]{:S(2)}) collective-permute-start(bf16[64,8192]{1,0:T(8,128)(2,1)S(1)} %get-tuple-element.70), channel_id=1, source_target_pairs={{0,4},{1,5},{2,6},{3,7},{12,8},{13,9},{14,10},{15,11},{16,20},{17,... | collective-permute-start | bytes 3145736 | tf_op jit(solution)/shard_map/ppermute | solution.py:352
  123.5 16.0 %collective-permute-done.12.refs_9_ = bf16[64,8192]{1,0:T(8,128)(2,1)S(1)} collective-permute-done((bf16[64,8192]{1,0:T(8,128)(2,1)S(1)}, bf16[64,8192]{1,0:T(8,128)(2,1)S(1)}, u32[]{:S(2)}, u32[]{:S(2)}) %collective-permute-start.12) | collective-permute-done | bytes 1048608 | tf_op jit(solution)/shard_map/ppermute | solution.py:352
  140.5 7.1 %shard_map.88 = (bf16[64,8192]{1,0:T(8,128)(2,1)S(1)}, bf16[64,8192]{1,0:T(8,128)(2,1)S(1)}, bf16[64,8192]{1,0:T(8,128)(2,1)S(1)}, bf16[64,8192]{1,0:T(8,128)(2,...) custom-call(s32[1]{0:T(128)} %bitcast.1.end_ref, ...), custom_call_target="tpu_custom_call" | custom-call | tf_op jit(solution)/shard_map/pallas_call | solution.py:319
  149.4 7.2 %collective-permute-start.19 = (bf16[64,8192]{1,0:T(8,128)(2,1)S(1)}, bf16[64,8192]{1,0:T(8,128)(2,1)S(1)}, u32[]{:S(2)}, u32[]{:S(2)}) collective-permute-start(bf16[64,8192]{1,0:T(8,128)(2,1)S(1)} %add_convert_fusion.2), channel_id=1, source_target_pairs={{0,4},{1,5},{2,6},{3,7},{4,0},{5,1},{6,2},{7,3},{8,12},{9,13},{10,... | collective-permute-start | bytes 3145736 | tf_op jit(solution)/shard_map/ppermute | solution.py:352
  156.6 14.4 %collective-permute-done.15.refs_2_ = bf16[64,8192]{1,0:T(8,128)(2,1)S(1)} collective-permute-done((bf16[64,8192]{1,0:T(8,128)(2,1)S(1)}, bf16[64,8192]{1,0:T(8,128)(2,1)S(1)}, u32[]{:S(2)}, u32[]{:S(2)}) %collective-permute-start.15) | collective-permute-done | bytes 1048608 | tf_op jit(solution)/shard_map/ppermute | solution.py:352
  172.7 7.2 %collective-permute-start.23 = (bf16[64,8192]{1,0:T(8,128)(2,1)S(1)}, bf16[64,8192]{1,0:T(8,128)(2,1)S(1)}, u32[]{:S(2)}, u32[]{:S(2)}) collective-permute-start(bf16[64,8192]{1,0:T(8,128)(2,1)S(1)} %add_convert_fusion), channel_id=1, source_target_pairs={{0,4},{1,5},{2,6},{3,7},{4,0},{5,1},{6,2},{7,3},{8,12},{9,13},{10,... | collective-permute-start | bytes 3145736 | tf_op jit(solution)/shard_map/ppermute | solution.py:352
  181.2 8.9 %collective-permute-done.16 = bf16[64,8192]{1,0:T(8,128)(2,1)S(1)} collective-permute-done((bf16[64,8192]{1,0:T(8,128)(2,1)S(1)}, bf16[64,8192]{1,0:T(8,128)(2,1)S(1)}, u32[]{:S(2)}, u32[]{:S(2)}) %collective-permute-start.16) | collective-permute-done | bytes 1048608 | tf_op jit(solution)/shard_map/ppermute | solution.py:352
  190.6 13.2 %collective-permute-done.23.refs_1_ = bf16[64,8192]{1,0:T(8,128)(2,1)S(1)} collective-permute-done((bf16[64,8192]{1,0:T(8,128)(2,1)S(1)}, bf16[64,8192]{1,0:T(8,128)(2,1)S(1)}, u32[]{:S(2)}, u32[]{:S(2)}) %collective-permute-start.23) | collective-permute-done | bytes 1048608 | tf_op jit(solution)/shard_map/ppermute | solution.py:352
  206.3 2.4 %shard_map.89.refs_4_ = bf16[128,8192]{1,0:T(8,128)(2,1)} custom-call(bf16[128,256]{1,0:T(8,128)(2,1)S(1)} %fusion.place_ref, bf16[64,8192]{1,0:T(8,128)(2,1)} %copy-done.4, bf16[64,8192]{1,0:T(8,128)(2,1)S(1)} %collective-permute-done.14.refs_1_, bf16[64,8192]{1,0:T(8,128)(2,1)S(1)} %collective-permute-done.15.refs_2_, ...), custom_call_target="tpu_custom_call" | custom-call | tf_op jit(solution)/shard_map/pallas_call | solution.py:128
  209.0 4.4 %collective-permute-start.27 = (f32[8,128]{1,0:T(8,128)S(1)}, f32[8,128]{1,0:T(8,128)S(1)}, u32[]{:S(2)}, u32[]{:S(2)}) collective-permute-start(f32[8,128]{1,0:T(8,128)S(1)} %add_add_fusion.refs_2_), channel_id=1, source_target_pairs={{0,4},{1,5},{2,6},{3,7},{4,0},{5,1},{6,2},{7,3},{8,12},{9,13},{10,... | collective-permute-start | bytes 12296 | tf_op jit(solution)/shard_map/ppermute | solution.py:352
  216.0 2.4 %shard_map.90 = bf16[128,8192]{1,0:T(8,128)(2,1)} custom-call(bf16[128,256]{1,0:T(8,128)(2,1)S(1)} %fusion.place_ref, bf16[64,8192]{1,0:T(8,128)(2,1)} %copy-done.4, bf16[64,8192]{1,0:T(8,128)(2,1)S(1)} %collective-permute-done.14.refs_1_, bf16[64,8192]{1,0:T(8,128)(2,1)S(1)} %collective-permute-done.15.refs_2_, ...), custom_call_target="tpu_custom_call", output_to_operand_aliasing={{}: (5, {})} | custom-call | tf_op jit(solution)/shard_map/pallas_call | solution.py:128
  220.0 4.0 %shard_map.93 = (f32[1,64,8192]{2,1,0:T(8,128)}, f32[1,64,8192]{2,1,0:T(8,128)}) custom-call(f32[64,8192]{1,0:T(8,128)S(1)} %get-tuple-element.67.refs_0_, f32[64,8192]{1,0:T(8,128)S(1)} %get-tuple-element.74.refs_1_, f32[8,128]{1,0:T(8,128)S(1)} %add_add_fusion.refs_2_, f32[8,128]{1,0:T(8,128)S(1)} %collective-permute-done.27.refs_3_, ...), custom_call_target="tpu_custom_call" | custom-call | tf_op jit(solution)/shard_map/pallas_call | solution.py:182
  (84 shorter events, 38.3 us)
Async XLA Ops:
  4.1 47.1 %collective-permute-start.8 = (bf16[2,64,8192]{2,1,0:T(8,128)(2,1)}, bf16[2,64,8192]{2,1,0:T(8,128)(2,1)}, u32[]{:S(2)}, u32[]{:S(2)}) collective-permute-start(bf16[2,64,8192]{2,1,0:T(8,128)(2,1)} %constant_dynamic-update-slice_fusion), channel_id=1, source_target_pairs={{4,8},{5,9},{6,10},{7,11},{8,4},{9,5},{10,6},{11,7},{20,24},{21,25... | collective-permute-start | bytes 6291464 | tf_op jit(solution)/shard_map/ppermute | solution.py:352
  6.0 51.0 %collective-permute-start.6 = (bf16[2,64,8192]{2,1,0:T(8,128)(2,1)}, bf16[2,64,8192]{2,1,0:T(8,128)(2,1)}, u32[]{:S(2)}, u32[]{:S(2)}) collective-permute-start(bf16[2,64,8192]{2,1,0:T(8,128)(2,1)} %constant_dynamic-update-slice_fusion), channel_id=1, source_target_pairs={{0,4},{1,5},{2,6},{3,7},{4,0},{5,1},{6,2},{7,3},{8,12},{9,13},{10,... | collective-permute-start | bytes 6291464 | tf_op jit(solution)/shard_map/ppermute | solution.py:352
  17.7 24.4 %collective-permute-start.1 = (bf16[2,2,16,8192]{3,2,1,0:T(8,128)(2,1)S(1)}, bf16[2,2,16,8192]{3,2,1,0:T(8,128)(2,1)S(1)}, u32[]{:S(2)}, u32[]{:S(2)}) collective-permute-start(bf16[2,2,16,8192]{3,2,1,0:T(8,128)(2,1)S(1)} %get-tuple-element.48), channel_id=1, source_target_pairs={{0,2},{1,3},{2,0},{3,1},{4,6},{5,7},{6,4},{7,5},{8,10},{9,11},{10,... | collective-permute-start | bytes 3145736 | tf_op jit(solution)/shard_map/ppermute | solution.py:352
  19.2 24.5 %collective-permute-start = (bf16[1,2,64,8192]{3,2,1,0:T(8,128)(2,1)S(1)}, bf16[1,2,64,8192]{3,2,1,0:T(8,128)(2,1)S(1)}, u32[]{:S(2)}, u32[]{:S(2)}) collective-permute-start(bf16[1,2,64,8192]{3,2,1,0:T(8,128)(2,1)S(1)} %get-tuple-element.45), channel_id=1, source_target_pairs={{0,1},{1,0},{2,3},{3,2},{4,5},{5,4},{6,7},{7,6},{8,9},{9,8},{10,11... | collective-permute-start | bytes 6291464 | tf_op jit(solution)/shard_map/ppermute | solution.py:352
  42.1 23.5 %collective-permute-start.2 = (bf16[2,2,16,8192]{3,2,1,0:T(8,128)(2,1)S(1)}, bf16[2,2,16,8192]{3,2,1,0:T(8,128)(2,1)S(1)}, u32[]{:S(2)}, u32[]{:S(2)}) collective-permute-start(bf16[2,2,16,8192]{3,2,1,0:T(8,128)(2,1)S(1)} %get-tuple-element.49), channel_id=1, source_target_pairs={{0,2},{1,3},{2,0},{3,1},{4,6},{5,7},{6,4},{7,5},{8,10},{9,11},{10,... | collective-permute-start | bytes 3145736 | tf_op jit(solution)/shard_map/ppermute | solution.py:352
  47.5 53.0 %collective-permute-start.11 = (bf16[2,64,8192]{2,1,0:T(8,128)(2,1)}, bf16[2,64,8192]{2,1,0:T(8,128)(2,1)}, u32[]{:S(2)}, u32[]{:S(2)}) collective-permute-start(bf16[2,64,8192]{2,1,0:T(8,128)(2,1)} %pad_maximum_fusion.refs_0_), channel_id=1, source_target_pairs={{0,4},{1,5},{2,6},{3,7},{12,8},{13,9},{14,10},{15,11},{16,20},{17,... | collective-permute-start | bytes 6291464 | tf_op jit(solution)/shard_map/ppermute | solution.py:352
  51.1 51.9 %collective-permute-start.10 = (bf16[2,64,8192]{2,1,0:T(8,128)(2,1)}, bf16[2,64,8192]{2,1,0:T(8,128)(2,1)}, u32[]{:S(2)}, u32[]{:S(2)}) collective-permute-start(bf16[2,64,8192]{2,1,0:T(8,128)(2,1)} %collective-permute-done.8.refs_1_), channel_id=1, source_target_pairs={{4,0},{5,1},{6,2},{7,3},{8,12},{9,13},{10,14},{11,15},{20,16},{21,... | collective-permute-start | bytes 6291464 | tf_op jit(solution)/shard_map/ppermute | solution.py:352
  57.0 46.0 %collective-permute-start.9 = (bf16[2,64,8192]{2,1,0:T(8,128)(2,1)}, bf16[2,64,8192]{2,1,0:T(8,128)(2,1)}, u32[]{:S(2)}, u32[]{:S(2)}) collective-permute-start(bf16[2,64,8192]{2,1,0:T(8,128)(2,1)} %collective-permute-done.6.refs_4_), channel_id=1, source_target_pairs={{4,8},{5,9},{6,10},{7,11},{8,4},{9,5},{10,6},{11,7},{20,24},{21,25... | collective-permute-start | bytes 6291464 | tf_op jit(solution)/shard_map/ppermute | solution.py:352
  69.2 52.9 %collective-permute-start.4 = (bf16[2,2,32,8192]{3,2,1,0:T(8,128)(2,1)}, bf16[2,2,32,8192]{3,2,1,0:T(8,128)(2,1)}, u32[]{:S(2)}, u32[]{:S(2)}) collective-permute-start(bf16[2,2,32,8192]{3,2,1,0:T(8,128)(2,1)} %get-tuple-element.50), channel_id=1, source_target_pairs={{0,2},{1,3},{2,0},{3,1},{4,6},{5,7},{6,4},{7,5},{8,10},{9,11},{10,... | collective-permute-start | bytes 6291464 | tf_op jit(solution)/shard_map/ppermute | solution.py:352
  110.8 28.7 %collective-permute-start.12 = (bf16[64,8192]{1,0:T(8,128)(2,1)S(1)}, bf16[64,8192]{1,0:T(8,128)(2,1)S(1)}, u32[]{:S(2)}, u32[]{:S(2)}) collective-permute-start(bf16[64,8192]{1,0:T(8,128)(2,1)S(1)} %get-tuple-element.55), channel_id=1, source_target_pairs={{0,4},{1,5},{2,6},{3,7},{4,0},{5,1},{6,2},{7,3},{8,12},{9,13},{10,... | collective-permute-start | bytes 3145736 | tf_op jit(solution)/shard_map/ppermute | solution.py:352
  115.9 23.6 %collective-permute-start.13 = (bf16[64,8192]{1,0:T(8,128)(2,1)S(1)}, bf16[64,8192]{1,0:T(8,128)(2,1)S(1)}, u32[]{:S(2)}, u32[]{:S(2)}) collective-permute-start(bf16[64,8192]{1,0:T(8,128)(2,1)S(1)} %get-tuple-element.56), channel_id=1, source_target_pairs={{4,8},{5,9},{6,10},{7,11},{8,4},{9,5},{10,6},{11,7},{20,24},{21,25... | collective-permute-start | bytes 3145736 | tf_op jit(solution)/shard_map/ppermute | solution.py:352
  116.6 55.9 %collective-permute-start.20 = (bf16[64,8192]{1,0:T(8,128)(2,1)S(1)}, bf16[64,8192]{1,0:T(8,128)(2,1)S(1)}, u32[]{:S(2)}, u32[]{:S(2)}) collective-permute-start(bf16[64,8192]{1,0:T(8,128)(2,1)S(1)} %get-tuple-element.70), channel_id=1, source_target_pairs={{0,4},{1,5},{2,6},{3,7},{12,8},{13,9},{14,10},{15,11},{16,20},{17,... | collective-permute-start | bytes 3145736 | tf_op jit(solution)/shard_map/ppermute | solution.py:352
  121.4 51.1 %collective-permute-start.21 = (bf16[64,8192]{1,0:T(8,128)(2,1)S(1)}, bf16[64,8192]{1,0:T(8,128)(2,1)S(1)}, u32[]{:S(2)}, u32[]{:S(2)}) collective-permute-start(bf16[64,8192]{1,0:T(8,128)(2,1)S(1)} %get-tuple-element.70), channel_id=1, source_target_pairs={{4,8},{5,9},{6,10},{7,11},{8,4},{9,5},{10,6},{11,7},{20,24},{21,25... | collective-permute-start | bytes 3145736 | tf_op jit(solution)/shard_map/ppermute | solution.py:352
  123.4 17.0 %collective-permute-start.5 = (bf16[1,2,32,8192]{3,2,1,0:T(8,128)(2,1)S(1)}, bf16[1,2,32,8192]{3,2,1,0:T(8,128)(2,1)S(1)}, u32[]{:S(2)}, u32[]{:S(2)}) collective-permute-start(bf16[1,2,32,8192]{3,2,1,0:T(8,128)(2,1)S(1)} %slice.37), channel_id=1, source_target_pairs={{0,1},{1,0},{2,3},{3,2},{4,5},{5,4},{6,7},{7,6},{8,9},{9,8},{10,11... | collective-permute-start | bytes 3145736 | tf_op jit(solution)/shard_map/ppermute | solution.py:352
  139.8 41.3 %collective-permute-start.18 = (bf16[64,8192]{1,0:T(8,128)(2,1)S(1)}, bf16[64,8192]{1,0:T(8,128)(2,1)S(1)}, u32[]{:S(2)}, u32[]{:S(2)}) collective-permute-start(bf16[64,8192]{1,0:T(8,128)(2,1)S(1)} %add_convert_fusion.3), channel_id=1, source_target_pairs={{4,8},{5,9},{6,10},{7,11},{8,4},{9,5},{10,6},{11,7},{20,24},{21,25... | collective-permute-start | bytes 3145736 | tf_op jit(solution)/shard_map/ppermute | solution.py:352
  147.6 23.4 %collective-permute-start.15 = (bf16[64,8192]{1,0:T(8,128)(2,1)S(1)}, bf16[64,8192]{1,0:T(8,128)(2,1)S(1)}, u32[]{:S(2)}, u32[]{:S(2)}) collective-permute-start(bf16[64,8192]{1,0:T(8,128)(2,1)S(1)} %get-tuple-element.60), channel_id=1, source_target_pairs={{0,2},{1,3},{2,0},{3,1},{4,6},{5,7},{6,4},{7,5},{8,10},{9,11},{10,... | collective-permute-start | bytes 3145736 | tf_op jit(solution)/shard_map/ppermute | solution.py:352
  149.4 40.7 %collective-permute-start.19 = (bf16[64,8192]{1,0:T(8,128)(2,1)S(1)}, bf16[64,8192]{1,0:T(8,128)(2,1)S(1)}, u32[]{:S(2)}, u32[]{:S(2)}) collective-permute-start(bf16[64,8192]{1,0:T(8,128)(2,1)S(1)} %add_convert_fusion.2), channel_id=1, source_target_pairs={{0,4},{1,5},{2,6},{3,7},{4,0},{5,1},{6,2},{7,3},{8,12},{9,13},{10,... | collective-permute-start | bytes 3145736 | tf_op jit(solution)/shard_map/ppermute | solution.py:352
  171.0 19.0 %collective-permute-start.16 = (bf16[64,8192]{1,0:T(8,128)(2,1)S(1)}, bf16[64,8192]{1,0:T(8,128)(2,1)S(1)}, u32[]{:S(2)}, u32[]{:S(2)}) collective-permute-start(bf16[64,8192]{1,0:T(8,128)(2,1)S(1)} %get-tuple-element.62), channel_id=1, source_target_pairs={{0,2},{1,3},{2,0},{3,1},{4,6},{5,7},{6,4},{7,5},{8,10},{9,11},{10,... | collective-permute-start | bytes 3145736 | tf_op jit(solution)/shard_map/ppermute | solution.py:352
  172.7 31.0 %collective-permute-start.23 = (bf16[64,8192]{1,0:T(8,128)(2,1)S(1)}, bf16[64,8192]{1,0:T(8,128)(2,1)S(1)}, u32[]{:S(2)}, u32[]{:S(2)}) collective-permute-start(bf16[64,8192]{1,0:T(8,128)(2,1)S(1)} %add_convert_fusion), channel_id=1, source_target_pairs={{0,4},{1,5},{2,6},{3,7},{4,0},{5,1},{6,2},{7,3},{8,12},{9,13},{10,... | collective-permute-start | bytes 3145736 | tf_op jit(solution)/shard_map/ppermute | solution.py:352
  180.2 23.6 %collective-permute-start.22 = (bf16[64,8192]{1,0:T(8,128)(2,1)S(1)}, bf16[64,8192]{1,0:T(8,128)(2,1)S(1)}, u32[]{:S(2)}, u32[]{:S(2)}) collective-permute-start(bf16[64,8192]{1,0:T(8,128)(2,1)S(1)} %add_convert_fusion.1), channel_id=1, source_target_pairs={{4,8},{5,9},{6,10},{7,11},{8,4},{9,5},{10,6},{11,7},{20,24},{21,25... | collective-permute-start | bytes 3145736 | tf_op jit(solution)/shard_map/ppermute | solution.py:352
  181.1 25.2 %collective-permute-start.14 = (bf16[64,8192]{1,0:T(8,128)(2,1)S(1)}, bf16[64,8192]{1,0:T(8,128)(2,1)S(1)}, u32[]{:S(2)}, u32[]{:S(2)}) collective-permute-start(bf16[64,8192]{1,0:T(8,128)(2,1)S(1)} %get-tuple-element.59), channel_id=1, source_target_pairs={{0,1},{1,0},{2,3},{3,2},{4,5},{5,4},{6,7},{7,6},{8,9},{9,8},{10,11... | collective-permute-start | bytes 3145736 | tf_op jit(solution)/shard_map/ppermute | solution.py:352
  190.0 16.3 %collective-permute-start.17 = (bf16[64,8192]{1,0:T(8,128)(2,1)S(1)}, bf16[64,8192]{1,0:T(8,128)(2,1)S(1)}, u32[]{:S(2)}, u32[]{:S(2)}) collective-permute-start(bf16[64,8192]{1,0:T(8,128)(2,1)S(1)} %collective-permute-done.16), channel_id=1, source_target_pairs={{0,1},{1,0},{2,3},{3,2},{4,5},{5,4},{6,7},{7,6},{8,9},{9,8},{10,11... | collective-permute-start | bytes 3145736 | tf_op jit(solution)/shard_map/ppermute | solution.py:352
  209.0 9.4 %collective-permute-start.27 = (f32[8,128]{1,0:T(8,128)S(1)}, f32[8,128]{1,0:T(8,128)S(1)}, u32[]{:S(2)}, u32[]{:S(2)}) collective-permute-start(f32[8,128]{1,0:T(8,128)S(1)} %add_add_fusion.refs_2_), channel_id=1, source_target_pairs={{0,4},{1,5},{2,6},{3,7},{4,0},{5,1},{6,2},{7,3},{8,12},{9,13},{10,... | collective-permute-start | bytes 12296 | tf_op jit(solution)/shard_map/ppermute | solution.py:352
  214.6 5.4 %collective-permute-start.29 = (f32[8,128]{1,0:T(8,128)S(1)}, f32[8,128]{1,0:T(8,128)S(1)}, u32[]{:S(2)}, u32[]{:S(2)}) collective-permute-start(f32[8,128]{1,0:T(8,128)S(1)} %add_add_fusion.refs_2_), channel_id=1, source_target_pairs={{0,12},{1,13},{2,14},{3,15},{4,8},{5,9},{6,10},{7,11},{8,4},{9,5},... | collective-permute-start | bytes 12296 | tf_op jit(solution)/shard_map/ppermute | solution.py:352
  (14 other events, 81.5 us)

commit v15 on v14

--- a/solution.py
+++ b/solution.py
@@ -11,7 +11,7 @@
 INNER = (((1,), (0,)), ((), ()))
 HBM = pl.BlockSpec(memory_space=pltpu.HBM)
 WHOLE = pl.BlockSpec(memory_space=pltpu.VMEM)
-VMEM_BYTES = 20 * 2**20
+VMEM_BYTES = 16 * 2**20
 
 
 def dot32(a, b, dims=INNER):
@@ -157,13 +157,7 @@
                     squares += total[r:r + 8, c:c + 128]
         square_ref[...] = squares
 
-    return pl.pallas_call(
-        body,
-        in_specs=[WHOLE] * (1 + len(others)),
-        out_specs=[WHOLE] * 2,
-        out_shape=[pltpu.VMEM((rank, width), F32), pltpu.VMEM((8, 128), F32)],
-        compiler_params=pltpu.CompilerParams(vmem_limit_bytes=VMEM_BYTES),
-    )(*in_vmem(first, *others))
+    return in_place(body, [((rank, width), F32), ((8, 128), F32)], first, *others)
 
 
 def scaled(raws, parts, ndevices):
@@ -172,20 +166,30 @@
     limit = float(2 * rank * width * ndevices) ** 0.5
 
     def body(*refs):
-        raw_refs, part_refs, out_refs = refs[:len(raws)], refs[len(raws):-len(raws)], refs[-len(raws):]
+        raw_refs, part_refs = refs[:len(raws)], refs[len(raws):len(raws) + len(parts)]
+        outs, (held, sems) = refs[len(raws) + len(parts):-2], refs[-2:]
         total = jnp.sum(sum(ref[...] for ref in part_refs), axis=(0, 1), keepdims=True)
         factor = jnp.minimum(jnp.float32(1.0), jnp.float32(limit) / jnp.sqrt(total + 1e-06))
-        cut = pl.ds(pl.multiple_of(pl.program_id(0) * tile, tile), tile)
-        for raw_ref, out_ref in zip(raw_refs, out_refs):
-            out_ref[0] = raw_ref[:, cut] * factor
+        copies = []
+        for i in range(width // tile):
+            cut = pl.ds(i * tile, tile)
+            for n, (raw_ref, out) in enumerate(zip(raw_refs, outs)):
+                held[n, :, cut] = raw_ref[:, cut] * factor
+                copies.append(pltpu.make_async_copy(held.at[n, :, cut], out.at[0, :, cut], sems.at[n, i]))
+                copies[-1].start()
+        for c in copies:
+            c.wait()
 
     return pl.pallas_call(
         body,
-        grid=(width // tile,),
         in_specs=[WHOLE] * (len(raws) + len(parts)),
-        out_specs=[pl.BlockSpec((1, rank, tile), lambda i: (0, 0, i))] * len(raws),
-        out_shape=[jax.ShapeDtypeStruct((1, rank, width), F32)] * len(raws),
-        compiler_params=kernel_params(),
+        out_specs=[HBM] * len(raws),
+        out_shape=[pltpu.HBM((1, rank, width), F32)] * len(raws),
+        scratch_shapes=[
+            pltpu.VMEM((len(raws), rank, width), F32),
+            pltpu.SemaphoreType.DMA((len(raws), width // tile)),
+        ],
+        compiler_params=pltpu.CompilerParams(vmem_limit_bytes=VMEM_BYTES),
     )(*in_vmem(*raws, *parts))
 
 
@@ -194,93 +198,81 @@
     return upper == (lax.broadcasted_iota(jnp.int32, (rows, columns), 1) < first_columns)
 
 
-def far_group(is_end, rows, factors, handed=None):
-    _, block, width = rows[0].shape
-    rank = factors[0].shape[1]
+def far_sums(tokens, factor, up_ref, down_ref, dx_refs):
+    rank, width = up_ref.shape
     tile = min(width, 2048)
-    tiles = width // tile
-    total = block if handed is None else 2 * block
-
-    def body(end_ref, *refs):
-        rows_in, refs = refs[:len(rows)], refs[len(rows):]
-        factors_in, refs = refs[:len(factors)], refs[len(factors):]
-        handed_in, refs = (None, refs) if handed is None else (refs[0], refs[1:])
-        (up_ref, down_ref, dx_ref), (held, left, sems) = refs[:3], refs[-3:]
-        step = pl.program_id(0)
-        at_end = end_ref[0] == 1
-
-        def copy(source, i):
-            cut = pl.ds(i * tile, tile)
-            return pltpu.make_async_copy(source.at[:, :, cut], held.at[:, :, cut], sems.at[i])
-
-        def tokens(k, cut):
-            own = held[k, :, cut]
-            return own if handed is None else jnp.concatenate([own, handed_in[k, :, cut]], axis=0)
-
-        def factor(k, cut):
-            first = factors_in[0][k, :, cut]
-            return first if len(factors) == 1 else jnp.where(at_end, factors_in[1][k, :, cut], first)
-
-        @pl.when(step == 0)
-        def _():
-            for n, source in enumerate(rows_in):
-                chosen = at_end == (n == 1) if len(rows) == 2 else step == 0
-
-                @pl.when(chosen)
-                def _(source=source):
-                    for i in range(tiles):
-                        copy(source, i).start()
-
-            sums = [jnp.zeros((rank, total), F32)] * 2
-            for i in range(tiles):
-                copy(rows_in[0], i).wait()
-                cut = pl.ds(i * tile, tile)
-                for k in range(2):
-                    sums[k] += dot32(factor(k, cut), tokens(k, cut), ROWS_OF)
-            for k in range(2):
-                left[k] = sums[k].astype(BF16)
-
-        cut = pl.ds(pl.multiple_of(step * tile, tile), tile)
-        up_ref[...] = dot32(left[0], tokens(1, cut)).astype(BF16)
-        down = dot32(left[1], tokens(0, cut)).astype(BF16)
-        down_ref[...] = down
-        dx = dot32(left[1], factor(0, cut), OUTER).astype(BF16)
-        dx_ref[...] = dx[:block]
-        if handed is not None:
-            refs[3][...] = jnp.where(at_end, down, dx[block:])
-
-    outs = 3 if handed is None else 4
-    more = () if handed is None else (handed,)
+    cuts = [pl.ds(i * tile, tile) for i in range(width // tile)]
+    hidden, inner = (sum(dot32(tokens(k, cut), factor(k, cut), ROWS_OF) for cut in cuts) for k in range(2))
+    hidden_t, inner_t, inner = hidden.T.astype(BF16), inner.T.astype(BF16), inner.astype(BF16)
+    for cut in cuts:
+        up_ref[:, cut] = dot32(hidden_t, tokens(1, cut)).astype(BF16)
+        down_ref[:, cut] = dot32(inner_t, tokens(0, cut)).astype(BF16)
+        dx = dot32(inner, factor(0, cut)).astype(BF16)
+        for n, ref in enumerate(dx_refs):
+            rows = ref.shape[0]
+            ref[:, cut] = dx[n * rows:(n + 1) * rows]
+
+
+def in_place(body, out_shapes, *arrays, flags=None):
+    first = [] if flags is None else [flags]
     return pl.pallas_call(
         body,
-        grid=(tiles,),
-        in_specs=[pl.BlockSpec(memory_space=pltpu.SMEM)] + [HBM] * len(rows) + [WHOLE] * (len(factors) + len(more)),
-        out_specs=[pl.BlockSpec((rank, tile), lambda i: (0, i))] * outs,
-        out_shape=[jax.ShapeDtypeStruct((rank, width), BF16)] * outs,
-        scratch_shapes=[
-            pltpu.VMEM((2, block, width), BF16),
-            pltpu.VMEM((2, rank, total), BF16),
-            pltpu.SemaphoreType.DMA((tiles,)),
-        ],
-        compiler_params=kernel_params(),
-    )(is_end, *in_hbm(*rows), *in_vmem(*factors, *more))
-
-
-def near_groups(is_end, stage, pair, down, up, dx_late, dx_early, swapped, capacity, first1):
+        in_specs=[pl.BlockSpec(memory_space=pltpu.SMEM)] * len(first) + [WHOLE] * len(arrays),
+        out_specs=[WHOLE] * len(out_shapes),
+        out_shape=[pltpu.VMEM(*shape) for shape in out_shapes],
+        compiler_params=pltpu.CompilerParams(vmem_limit_bytes=VMEM_BYTES),
+    )(*first, *in_vmem(*arrays))
+
+
+def early_group(flags, rows3, rows2, crossed):
+    _, block, width = rows2.shape
+    rank = crossed.shape[1]
+
+    def body(flags_ref, rows3_ref, rows2_ref, crossed_ref, up_ref, down_ref, dx_ref, late_ref):
+        far_sums(
+            lambda k, cut: rows2_ref[k, :, cut], lambda k, cut: crossed_ref[k, :, cut], up_ref, down_ref, (dx_ref,)
+        )
+        late_ref[...] = jnp.where(flags_ref[0] == 1, rows2_ref[...], rows3_ref[...])
+
+    shapes = [((rank, width), BF16)] * 2 + [((block, width), BF16), ((2, block, width), BF16)]
+    return in_place(body, shapes, rows3, rows2, crossed, flags=flags)
+
+
+def late_group(flags, rows, handed, far, outer):
+    _, block, width = rows.shape
+    rank = far.shape[1]
+
+    def body(flags_ref, rows_ref, handed_ref, outer_ref, far_ref, up_ref, down_ref, dx_ref, swap_ref):
+        at_end = flags_ref[0] == 1
+        far_sums(
+            lambda k, cut: jnp.concatenate([rows_ref[k, :, cut], handed_ref[k, :, cut]], axis=0),
+            lambda k, cut: jnp.where(at_end, outer_ref[k, :, cut], far_ref[k, :, cut]),
+            up_ref,
+            down_ref,
+            (dx_ref, swap_ref),
+        )
+
+        @pl.when(at_end)
+        def _():
+            swap_ref[...] = down_ref[...]
+
+    shapes = [((rank, width), BF16)] * 2 + [((block, width), BF16)] * 2
+    return in_place(body, shapes, rows, handed, outer, far, flags=flags)
+
+
+def near_groups(flags, stage, pair, down, up, dx_late, dx_early, swapped, capacity, first1):
     plane = len(stage)
     rank, width = down.shape
     block = plane * capacity
     tile = min(width, 2048)
-    tiles = width // tile
-
-    def body(end_ref, *refs):
+    cuts = [pl.ds(i * tile, tile) for i in range(width // tile)]
+
+    def body(flags_ref, *refs):
         stage_in, refs = refs[:plane], refs[plane:]
         pair_in, down_in, up_in, late_ref, early_ref, swapped_ref = refs[:6]
-        dx_refs, sum_refs = refs[6:10], refs[10:14]
-        (left,) = refs[14:]
-        step = pl.program_id(0)
+        dx_refs, sum_refs = refs[6:6 + plane], refs[6 + plane:]
         own_in = (down_in, up_in)
-        is_mine = corner(2 * block, block, 2 * rank, rank)
+        at_end = flags_ref[0] == 1
 
         def rows(k, cut):
             return jnp.concatenate(
@@ -292,43 +284,27 @@
                 axis=0,
             )
 
-        @pl.when(step == 0)
-        def _():
-            sums = [jnp.zeros((2 * block, 2 * rank), F32)] * 2
-            for i in range(tiles):
-                cut = pl.ds(i * tile, tile)
-                for k in range(2):
-                    both = jnp.concatenate([pair_in[k, :, cut], own_in[k][:, cut]], axis=0)
-                    sums[k] += dot32(rows(k, cut), both, ROWS_OF)
+        def factors(k, cut):
+            return jnp.concatenate([pair_in[k, :, cut], own_in[k][:, cut]], axis=0)
+
+        is_mine = corner(2 * block, block, 2 * rank, rank)
+        sums = [sum(dot32(rows(k, cut), factors(k, cut), ROWS_OF) for cut in cuts) for k in range(2)]
+        sums = [jnp.where(is_mine, total, 0.0) for total in sums]
+        left, inner = [total.T.astype(BF16) for total in sums], sums[1].astype(BF16)
+        for cut in cuts:
             for k in range(2):
-                left[k] = jnp.where(is_mine, sums[k], 0.0).astype(BF16)
-
-        cut = pl.ds(pl.multiple_of(step * tile, tile), tile)
-        for k in range(2):
-            both = dot32(left[k], rows(1 - k, cut), OUTER)
-            sum_refs[k][...] = both[:rank]
-            sum_refs[2 + k][...] = both[rank:]
-        downs = jnp.concatenate([pair_in[0, :, cut], down_in[:, cut]], axis=0)
-        dx = dot32(left[1], downs).astype(BF16)
-        at_end, late = end_ref[0] == 1, late_ref[...]
-        moved = [jnp.where(at_end, swapped_ref[...], late), jnp.where(at_end, late, early_ref[...]), dx[:block], dx[block:]]
-        for n, dx in enumerate(moved):
-            for m in range(plane):
-                dx_refs[m][n * capacity:(n + 1) * capacity] = dx[m * capacity:(m + 1) * capacity]
-
-    return pl.pallas_call(
-        body,
-        grid=(tiles,),
-        in_specs=[pl.BlockSpec(memory_space=pltpu.SMEM)]
-        + [WHOLE] * (plane + 3)
-        + [pl.BlockSpec((block, tile), lambda i: (0, i))] * 3,
-        out_specs=[pl.BlockSpec((4 * capacity, tile), lambda i: (0, i))] * plane
-        + [pl.BlockSpec((rank, tile), lambda i: (0, i))] * 4,
-        out_shape=[jax.ShapeDtypeStruct((4 * capacity, width), BF16)] * plane
-        + [jax.ShapeDtypeStruct((rank, width), F32)] * 4,
-        scratch_shapes=[pltpu.VMEM((2, 2 * block, 2 * rank), BF16)],
-        compiler_params=kernel_params(),
-    )(is_end, *in_vmem(*stage, pair, down, up), dx_late, dx_early, swapped)
+                both = dot32(left[k], rows(1 - k, cut))
+                sum_refs[k][:, cut] = both[:rank]
+                sum_refs[2 + k][:, cut] = both[rank:]
+            dx = dot32(inner, factors(0, cut)).astype(BF16)
+            late = late_ref[:, cut]
+            moved = [jnp.where(at_end, swapped_ref[:, cut], late), jnp.where(at_end, late, early_ref[:, cut])]
+            for n, dx in enumerate(moved + [dx[:block], dx[block:]]):
+                for m in range(plane):
+                    dx_refs[m][n * capacity:(n + 1) * capacity, cut] = dx[m * capacity:(m + 1) * capacity]
+
+    shapes = [((4 * capacity, width), BF16)] * plane + [((rank, width), F32)] * 4
+    return in_place(body, shapes, *stage, pair, down, up, dx_late, dx_early, swapped, flags=flags)
 
 
 def move_adapters(plane, acts, cotan, token_task_index, task_slot_lookup, pool_down_factors, pool_up_factors):
@@ -403,9 +379,8 @@
     outer = send(crossed, outward)
     far = send(pair, cross)
 
-    up2, down2, dx_early = far_group(end_flag, (rows2,), (crossed,))
-    rows3, rows2 = after((rows3, rows2), dx_early)
-    up3, down3, dx_late, swapped = far_group(end_flag, (rows3, rows2), (far, outer), handed)
+    up2, down2, dx_early, late_rows = early_group(end_flag, rows3, rows2, crossed)
+    up3, down3, dx_late, swapped = late_group(end_flag, late_rows, handed, far, outer)
     up2_in = send(up3, inward)
     down3, swapped, up3 = send(down3, cross), send(swapped, swap), send(up3, cross)
 

time: 224 us -> 220 us (0.982)
  Pallas kernels: 36.2 us -> 29 us
  waiting for transfers between devices: 113 us -> 120 us
  other arithmetic: 6.17 us -> 3.37 us
    pallas_call x6, Pallas kernels: 25.1 us -> 17.8 us  [the longest x5 15.6 us: in_place(): pl.pallas_call(body, in_specs=[pl.BlockSpec(memory_space=pltpu.SMEM)] * l...]
    ppermute x30, waiting for transfers between devices: 113 us -> 120 us  [send(): return lax.ppermute(array, 'dp', pairs)]
    unnamed x17 -> x21, local copies, waits for them, and re-layouts: 4.5 us -> 4.15 us
  transfers between devices with their start and end apart: 30 -> 30, of which waited for: 12 -> 13; matrix products, arithmetic and copies ran while one was open for 5% -> 3% of each run, Pallas kernels for 14% -> 12%
where the time goes in v15:
time: 220 us
  waiting for transfers between devices  120 us (55%)
  starting transfers between devices  57.5 us (26%)
  Pallas kernels  29 us (13%)
  local copies, waits for them, and re-layouts  9.41 us (4%)
  other arithmetic  3.37 us (2%)
    ppermute x30, waiting for transfers between devices, send(): return lax.ppermute(array, 'dp', pairs)  120 us
    ppermute x30, starting transfers between devices, send(): return lax.ppermute(array, 'dp', pairs)  57.5 us
    pallas_call x5, Pallas kernels, in_place(): pl.pallas_call(body, in_specs=[pl.BlockSpec(memory_space=pltpu.SMEM)] * l...  15.6 us
    pallas_call x1, Pallas kernels, pack(): pl.pallas_call(body, grid=(tiles,), in_specs=[pl.BlockSpec(place.shape, l...  6.37 us
    pallas_call x2, Pallas kernels, unpack(): pl.pallas_call(body, grid=(width // 2 // tile,), in_specs=[pl.BlockSpec(p...  4.78 us
  transfers between devices with their start and end apart: 30, of which 13 were waited for; matrix products, arithmetic and copies ran while one was open for 3% of the time, Pallas kernels for 12%

profile of v15, /device:TPU:0, one launch (start us, length us, event | category | flops | bytes accessed | tf_op | source)
XLA Modules:
  0.0 220.1 jit_solution(10401092365047547728)
XLA Ops:
  0.7 2.3 %constant_dynamic-update-slice_fusion.1 = bf16[2,64,8192]{2,1,0:T(8,128)(2,1)} fusion(bf16[1,64,8192]{2,1,0:T(8,128)(2,1)} %param.10), kind=kLoop, calls=%fused_computation.22 | loop fusion | bytes 2097152
  6.0 4.6 %collective-permute-start.6 = (bf16[2,64,8192]{2,1,0:T(8,128)(2,1)}, bf16[2,64,8192]{2,1,0:T(8,128)(2,1)}, u32[]{:S(2)}, u32[]{:S(2)}) collective-permute-start(bf16[2,64,8192]{2,1,0:T(8,128)(2,1)} %constant_dynamic-update-slice_fusion), channel_id=1, source_target_pairs={{0,4},{1,5},{2,6},{3,7},{4,0},{5,1},{6,2},{7,3},{8,12},{9,13},{10,... | collective-permute-start | bytes 6291464 | tf_op jit(solution)/shard_map/ppermute | solution.py:328
  11.3 6.4 %shard_map.85 = (bf16[1,2,64,8192]{3,2,1,0:T(8,128)(2,1)S(1)}, bf16[1,2,64,8192]{3,2,1,0:T(8,128)(2,1)S(1)}, bf16[2,2,16,8192]{3,2,1,0:T(8,128)(2,1)S(1)}, bf16[...) custom-call(bf16[256,128]{1,0:T(8,128)(2,1)S(1)} %fusion.1.place_ref, bf16[128,8192]{1,0:T(8,128)(2,1)} %x_in.1, ...), custom_call_target="tpu_custom_call" | custom-call | tf_op jit(solution)/shard_map/pallas_call | solution.py:107
  20.1 22.0 %collective-permute-done.1 = bf16[2,2,16,8192]{3,2,1,0:T(8,128)(2,1)S(1)} collective-permute-done((bf16[2,2,16,8192]{3,2,1,0:T(8,128)(2,1)S(1)}, bf16[2,2,16,8192]{3,2,1,0:T(8,128)(2,1)S(1)}, u32[]{:S(2)}, u32[]{:S(2)}) %collective-permute-start.1) | collective-permute-done | bytes 1048608 | tf_op jit(solution)/shard_map/ppermute | solution.py:328
  45.8 3.6 %collective-permute-start.9 = (bf16[2,64,8192]{2,1,0:T(8,128)(2,1)S(1)}, bf16[2,64,8192]{2,1,0:T(8,128)(2,1)}, u32[]{:S(2)}, u32[]{:S(2)}) collective-permute-start(bf16[2,64,8192]{2,1,0:T(8,128)(2,1)S(1)} %pad_maximum_fusion.rows3_ref), channel_id=1, source_target_pairs={{0,4},{1,5},{2,6},{3,7},{12,8},{13,9},{14,10},{15,11},{16,20},{17,... | collective-permute-start | bytes 6291464 | tf_op jit(solution)/shard_map/ppermute | solution.py:328
  50.7 6.3 %collective-permute-done.6.refs_4_ = bf16[2,64,8192]{2,1,0:T(8,128)(2,1)} collective-permute-done((bf16[2,64,8192]{2,1,0:T(8,128)(2,1)}, bf16[2,64,8192]{2,1,0:T(8,128)(2,1)}, u32[]{:S(2)}, u32[]{:S(2)}) %collective-permute-start.6) | collective-permute-done | bytes 2097184 | tf_op jit(solution)/shard_map/ppermute | solution.py:328
  59.0 6.6 %collective-permute-done.2 = bf16[2,2,16,8192]{3,2,1,0:T(8,128)(2,1)S(1)} collective-permute-done((bf16[2,2,16,8192]{3,2,1,0:T(8,128)(2,1)S(1)}, bf16[2,2,16,8192]{3,2,1,0:T(8,128)(2,1)S(1)}, u32[]{:S(2)}, u32[]{:S(2)}) %collective-permute-start.2) | collective-permute-done | bytes 1048608 | tf_op jit(solution)/shard_map/ppermute | solution.py:328
  72.3 3.6 %shard_map.86 = (bf16[64,8192]{1,0:T(8,128)(2,1)S(1)}, bf16[64,8192]{1,0:T(8,128)(2,1)S(1)}, bf16[64,8192]{1,0:T(8,128)(2,1)S(1)}, bf16[2,64,8192]{2,1,0:T(8,128)(2,1)S(1)}) custom-call(s32[1]{0:T(128)} %bitcast.1.flags_ref, bf16[2,64,8192]{2,1,0:T(8,128)(2,1)S(1)} %pad_maximum_fusion.rows3_ref, bf16[2,64,8192]{2,1,0:T(8,128)(2,1)S(1)} %pad_maximum_fusion.1.rows2_ref, ...), custom_call_target="tpu_custom_call" | custom-call | tf_op jit(solution)/shard_map/pallas_call | solution.py:218
  75.9 24.5 %collective-permute-done.9.handed_ref = bf16[2,64,8192]{2,1,0:T(8,128)(2,1)} collective-permute-done((bf16[2,64,8192]{2,1,0:T(8,128)(2,1)S(1)}, bf16[2,64,8192]{2,1,0:T(8,128)(2,1)}, u32[]{:S(2)}, u32[]{:S(2)}) %collective-permute-start.9) | collective-permute-done | bytes 2097184 | tf_op jit(solution)/shard_map/ppermute | solution.py:328
  100.4 2.6 %collective-permute-done.10.outer_ref = bf16[2,64,8192]{2,1,0:T(8,128)(2,1)} collective-permute-done((bf16[2,64,8192]{2,1,0:T(8,128)(2,1)}, bf16[2,64,8192]{2,1,0:T(8,128)(2,1)}, u32[]{:S(2)}, u32[]{:S(2)}) %collective-permute-start.10) | collective-permute-done | bytes 2097184 | tf_op jit(solution)/shard_map/ppermute | solution.py:328
  103.0 5.4 %shard_map.87 = (bf16[64,8192]{1,0:T(8,128)(2,1)S(1)}, bf16[64,8192]{1,0:T(8,128)(2,1)S(1)}, bf16[64,8192]{1,0:T(8,128)(2,1)S(1)}, bf16[64,8192]{1,0:T(8,128)(2,1)S(1)}) custom-call(s32[1]{0:T(128)} %bitcast.1.flags_ref, bf16[2,64,8192]{2,1,0:T(8,128)(2,1)S(1)} %get-tuple-element.50.rows_ref, bf16[2,64,8192]{2,1,0:T(8,128)(2,1)} %collective-permute-done.9.handed_ref, ...), custom_call_target="tpu_custom_call" | custom-call | tf_op jit(solution)/shard_map/pallas_call | solution.py:218
  108.4 5.1 %collective-permute-start.12 = (bf16[64,8192]{1,0:T(8,128)(2,1)S(1)}, bf16[64,8192]{1,0:T(8,128)(2,1)S(1)}, u32[]{:S(2)}, u32[]{:S(2)}) collective-permute-start(bf16[64,8192]{1,0:T(8,128)(2,1)S(1)} %get-tuple-element.53), channel_id=1, source_target_pairs={{0,4},{1,5},{2,6},{3,7},{4,0},{5,1},{6,2},{7,3},{8,12},{9,13},{10,... | collective-permute-start | bytes 3145736 | tf_op jit(solution)/shard_map/ppermute | solution.py:328
  114.2 4.8 %collective-permute-start.20 = (bf16[64,8192]{1,0:T(8,128)(2,1)S(1)}, bf16[64,8192]{1,0:T(8,128)(2,1)S(1)}, u32[]{:S(2)}, u32[]{:S(2)}) collective-permute-start(bf16[64,8192]{1,0:T(8,128)(2,1)S(1)} %get-tuple-element.68), channel_id=1, source_target_pairs={{0,4},{1,5},{2,6},{3,7},{12,8},{13,9},{14,10},{15,11},{16,20},{17,... | collective-permute-start | bytes 3145736 | tf_op jit(solution)/shard_map/ppermute | solution.py:328
  121.3 15.8 %collective-permute-done.12.refs_9_ = bf16[64,8192]{1,0:T(8,128)(2,1)S(1)} collective-permute-done((bf16[64,8192]{1,0:T(8,128)(2,1)S(1)}, bf16[64,8192]{1,0:T(8,128)(2,1)S(1)}, u32[]{:S(2)}, u32[]{:S(2)}) %collective-permute-start.12) | collective-permute-done | bytes 1048608 | tf_op jit(solution)/shard_map/ppermute | solution.py:328
  138.1 5.5 %shard_map.88 = (bf16[64,8192]{1,0:T(8,128)(2,1)S(1)}, bf16[64,8192]{1,0:T(8,128)(2,1)S(1)}, bf16[64,8192]{1,0:T(8,128)(2,1)S(1)}, bf16[64,8192]{1,0:T(8,128)(2,...) custom-call(s32[1]{0:T(128)} %bitcast.1.flags_ref, ...), custom_call_target="tpu_custom_call" | custom-call | tf_op jit(solution)/shard_map/pallas_call | solution.py:218
  146.3 7.2 %collective-permute-start.19 = (bf16[64,8192]{1,0:T(8,128)(2,1)S(1)}, bf16[64,8192]{1,0:T(8,128)(2,1)S(1)}, u32[]{:S(2)}, u32[]{:S(2)}) collective-permute-start(bf16[64,8192]{1,0:T(8,128)(2,1)S(1)} %add_convert_fusion.2), channel_id=1, source_target_pairs={{0,4},{1,5},{2,6},{3,7},{4,0},{5,1},{6,2},{7,3},{8,12},{9,13},{10,... | collective-permute-start | bytes 3145736 | tf_op jit(solution)/shard_map/ppermute | solution.py:328
  153.5 14.5 %collective-permute-done.15.refs_2_ = bf16[64,8192]{1,0:T(8,128)(2,1)S(1)} collective-permute-done((bf16[64,8192]{1,0:T(8,128)(2,1)S(1)}, bf16[64,8192]{1,0:T(8,128)(2,1)S(1)}, u32[]{:S(2)}, u32[]{:S(2)}) %collective-permute-start.15) | collective-permute-done | bytes 1048608 | tf_op jit(solution)/shard_map/ppermute | solution.py:328
  169.6 7.2 %collective-permute-start.23 = (bf16[64,8192]{1,0:T(8,128)(2,1)S(1)}, bf16[64,8192]{1,0:T(8,128)(2,1)S(1)}, u32[]{:S(2)}, u32[]{:S(2)}) collective-permute-start(bf16[64,8192]{1,0:T(8,128)(2,1)S(1)} %add_convert_fusion), channel_id=1, source_target_pairs={{0,4},{1,5},{2,6},{3,7},{4,0},{5,1},{6,2},{7,3},{8,12},{9,13},{10,... | collective-permute-start | bytes 3145736 | tf_op jit(solution)/shard_map/ppermute | solution.py:328
  178.0 8.9 %collective-permute-done.16 = bf16[64,8192]{1,0:T(8,128)(2,1)S(1)} collective-permute-done((bf16[64,8192]{1,0:T(8,128)(2,1)S(1)}, bf16[64,8192]{1,0:T(8,128)(2,1)S(1)}, u32[]{:S(2)}, u32[]{:S(2)}) %collective-permute-start.16) | collective-permute-done | bytes 1048608 | tf_op jit(solution)/shard_map/ppermute | solution.py:328
  187.5 13.8 %collective-permute-done.23.refs_1_ = bf16[64,8192]{1,0:T(8,128)(2,1)S(1)} collective-permute-done((bf16[64,8192]{1,0:T(8,128)(2,1)S(1)}, bf16[64,8192]{1,0:T(8,128)(2,1)S(1)}, u32[]{:S(2)}, u32[]{:S(2)}) %collective-permute-start.23) | collective-permute-done | bytes 1048608 | tf_op jit(solution)/shard_map/ppermute | solution.py:328
  204.0 2.4 %shard_map.89.refs_4_ = bf16[128,8192]{1,0:T(8,128)(2,1)} custom-call(bf16[128,256]{1,0:T(8,128)(2,1)S(1)} %fusion.place_ref, bf16[64,8192]{1,0:T(8,128)(2,1)} %copy-done.6, bf16[64,8192]{1,0:T(8,128)(2,1)S(1)} %collective-permute-done.14.refs_1_, bf16[64,8192]{1,0:T(8,128)(2,1)S(1)} %collective-permute-done.15.refs_2_, ...), custom_call_target="tpu_custom_call" | custom-call | tf_op jit(solution)/shard_map/pallas_call | solution.py:128
  206.6 4.4 %collective-permute-start.27 = (f32[8,128]{1,0:T(8,128)S(1)}, f32[8,128]{1,0:T(8,128)S(1)}, u32[]{:S(2)}, u32[]{:S(2)}) collective-permute-start(f32[8,128]{1,0:T(8,128)S(1)} %add_add_fusion.refs_2_), channel_id=1, source_target_pairs={{0,4},{1,5},{2,6},{3,7},{4,0},{5,1},{6,2},{7,3},{8,12},{9,13},{10,... | collective-permute-start | bytes 12296 | tf_op jit(solution)/shard_map/ppermute | solution.py:328
  213.6 2.4 %shard_map.90 = bf16[128,8192]{1,0:T(8,128)(2,1)} custom-call(bf16[128,256]{1,0:T(8,128)(2,1)S(1)} %fusion.place_ref, bf16[64,8192]{1,0:T(8,128)(2,1)} %copy-done.6, bf16[64,8192]{1,0:T(8,128)(2,1)S(1)} %collective-permute-done.14.refs_1_, bf16[64,8192]{1,0:T(8,128)(2,1)S(1)} %collective-permute-done.15.refs_2_, ...), custom_call_target="tpu_custom_call", output_to_operand_aliasing={{}: (5, {})} | custom-call | tf_op jit(solution)/shard_map/pallas_call | solution.py:128
  217.6 2.3 %shard_map.93 = (f32[1,64,8192]{2,1,0:T(8,128)}, f32[1,64,8192]{2,1,0:T(8,128)}) custom-call(f32[64,8192]{1,0:T(8,128)S(1)} %get-tuple-element.65.refs_0_, f32[64,8192]{1,0:T(8,128)S(1)} %get-tuple-element.72.refs_1_, f32[8,128]{1,0:T(8,128)S(1)} %add_add_fusion.refs_2_, f32[8,128]{1,0:T(8,128)S(1)} %collective-permute-done.27.refs_3_, ...), custom_call_target="tpu_custom_call" | custom-call | tf_op jit(solution)/shard_map/pallas_call | solution.py:183
  (88 shorter events, 36.9 us)
Async XLA Ops:
  4.1 45.4 %collective-permute-start.8 = (bf16[2,64,8192]{2,1,0:T(8,128)(2,1)}, bf16[2,64,8192]{2,1,0:T(8,128)(2,1)}, u32[]{:S(2)}, u32[]{:S(2)}) collective-permute-start(bf16[2,64,8192]{2,1,0:T(8,128)(2,1)} %constant_dynamic-update-slice_fusion), channel_id=1, source_target_pairs={{4,8},{5,9},{6,10},{7,11},{8,4},{9,5},{10,6},{11,7},{20,24},{21,25... | collective-permute-start | bytes 6291464 | tf_op jit(solution)/shard_map/ppermute | solution.py:328
  6.0 51.0 %collective-permute-start.6 = (bf16[2,64,8192]{2,1,0:T(8,128)(2,1)}, bf16[2,64,8192]{2,1,0:T(8,128)(2,1)}, u32[]{:S(2)}, u32[]{:S(2)}) collective-permute-start(bf16[2,64,8192]{2,1,0:T(8,128)(2,1)} %constant_dynamic-update-slice_fusion), channel_id=1, source_target_pairs={{0,4},{1,5},{2,6},{3,7},{4,0},{5,1},{6,2},{7,3},{8,12},{9,13},{10,... | collective-permute-start | bytes 6291464 | tf_op jit(solution)/shard_map/ppermute | solution.py:328
  17.7 24.4 %collective-permute-start.1 = (bf16[2,2,16,8192]{3,2,1,0:T(8,128)(2,1)S(1)}, bf16[2,2,16,8192]{3,2,1,0:T(8,128)(2,1)S(1)}, u32[]{:S(2)}, u32[]{:S(2)}) collective-permute-start(bf16[2,2,16,8192]{3,2,1,0:T(8,128)(2,1)S(1)} %get-tuple-element.47), channel_id=1, source_target_pairs={{0,2},{1,3},{2,0},{3,1},{4,6},{5,7},{6,4},{7,5},{8,10},{9,11},{10,... | collective-permute-start | bytes 3145736 | tf_op jit(solution)/shard_map/ppermute | solution.py:328
  19.3 24.5 %collective-permute-start = (bf16[1,2,64,8192]{3,2,1,0:T(8,128)(2,1)S(1)}, bf16[1,2,64,8192]{3,2,1,0:T(8,128)(2,1)S(1)}, u32[]{:S(2)}, u32[]{:S(2)}) collective-permute-start(bf16[1,2,64,8192]{3,2,1,0:T(8,128)(2,1)S(1)} %get-tuple-element.44), channel_id=1, source_target_pairs={{0,1},{1,0},{2,3},{3,2},{4,5},{5,4},{6,7},{7,6},{8,9},{9,8},{10,11... | collective-permute-start | bytes 6291464 | tf_op jit(solution)/shard_map/ppermute | solution.py:328
  42.1 23.5 %collective-permute-start.2 = (bf16[2,2,16,8192]{3,2,1,0:T(8,128)(2,1)S(1)}, bf16[2,2,16,8192]{3,2,1,0:T(8,128)(2,1)S(1)}, u32[]{:S(2)}, u32[]{:S(2)}) collective-permute-start(bf16[2,2,16,8192]{3,2,1,0:T(8,128)(2,1)S(1)} %get-tuple-element.48), channel_id=1, source_target_pairs={{0,2},{1,3},{2,0},{3,1},{4,6},{5,7},{6,4},{7,5},{8,10},{9,11},{10,... | collective-permute-start | bytes 3145736 | tf_op jit(solution)/shard_map/ppermute | solution.py:328
  45.8 54.6 %collective-permute-start.9 = (bf16[2,64,8192]{2,1,0:T(8,128)(2,1)S(1)}, bf16[2,64,8192]{2,1,0:T(8,128)(2,1)}, u32[]{:S(2)}, u32[]{:S(2)}) collective-permute-start(bf16[2,64,8192]{2,1,0:T(8,128)(2,1)S(1)} %pad_maximum_fusion.rows3_ref), channel_id=1, source_target_pairs={{0,4},{1,5},{2,6},{3,7},{12,8},{13,9},{14,10},{15,11},{16,20},{17,... | collective-permute-start | bytes 6291464 | tf_op jit(solution)/shard_map/ppermute | solution.py:328
  49.4 53.5 %collective-permute-start.10 = (bf16[2,64,8192]{2,1,0:T(8,128)(2,1)}, bf16[2,64,8192]{2,1,0:T(8,128)(2,1)}, u32[]{:S(2)}, u32[]{:S(2)}) collective-permute-start(bf16[2,64,8192]{2,1,0:T(8,128)(2,1)} %collective-permute-done.8.crossed_ref), channel_id=1, source_target_pairs={{4,0},{5,1},{6,2},{7,3},{8,12},{9,13},{10,14},{11,15},{20,16},{21,... | collective-permute-start | bytes 6291464 | tf_op jit(solution)/shard_map/ppermute | solution.py:328
  57.0 46.0 %collective-permute-start.11 = (bf16[2,64,8192]{2,1,0:T(8,128)(2,1)}, bf16[2,64,8192]{2,1,0:T(8,128)(2,1)}, u32[]{:S(2)}, u32[]{:S(2)}) collective-permute-start(bf16[2,64,8192]{2,1,0:T(8,128)(2,1)} %collective-permute-done.6.refs_4_), channel_id=1, source_target_pairs={{4,8},{5,9},{6,10},{7,11},{8,4},{9,5},{10,6},{11,7},{20,24},{21,25... | collective-permute-start | bytes 6291464 | tf_op jit(solution)/shard_map/ppermute | solution.py:328
  69.2 50.5 %collective-permute-start.4 = (bf16[2,2,32,8192]{3,2,1,0:T(8,128)(2,1)}, bf16[2,2,32,8192]{3,2,1,0:T(8,128)(2,1)}, u32[]{:S(2)}, u32[]{:S(2)}) collective-permute-start(bf16[2,2,32,8192]{3,2,1,0:T(8,128)(2,1)} %get-tuple-element.49), channel_id=1, source_target_pairs={{0,2},{1,3},{2,0},{3,1},{4,6},{5,7},{6,4},{7,5},{8,10},{9,11},{10,... | collective-permute-start | bytes 6291464 | tf_op jit(solution)/shard_map/ppermute | solution.py:328
  108.4 28.7 %collective-permute-start.12 = (bf16[64,8192]{1,0:T(8,128)(2,1)S(1)}, bf16[64,8192]{1,0:T(8,128)(2,1)S(1)}, u32[]{:S(2)}, u32[]{:S(2)}) collective-permute-start(bf16[64,8192]{1,0:T(8,128)(2,1)S(1)} %get-tuple-element.53), channel_id=1, source_target_pairs={{0,4},{1,5},{2,6},{3,7},{4,0},{5,1},{6,2},{7,3},{8,12},{9,13},{10,... | collective-permute-start | bytes 3145736 | tf_op jit(solution)/shard_map/ppermute | solution.py:328
  113.5 23.6 %collective-permute-start.13 = (bf16[64,8192]{1,0:T(8,128)(2,1)S(1)}, bf16[64,8192]{1,0:T(8,128)(2,1)S(1)}, u32[]{:S(2)}, u32[]{:S(2)}) collective-permute-start(bf16[64,8192]{1,0:T(8,128)(2,1)S(1)} %get-tuple-element.54), channel_id=1, source_target_pairs={{4,8},{5,9},{6,10},{7,11},{8,4},{9,5},{10,6},{11,7},{20,24},{21,25... | collective-permute-start | bytes 3145736 | tf_op jit(solution)/shard_map/ppermute | solution.py:328
  114.2 55.2 %collective-permute-start.20 = (bf16[64,8192]{1,0:T(8,128)(2,1)S(1)}, bf16[64,8192]{1,0:T(8,128)(2,1)S(1)}, u32[]{:S(2)}, u32[]{:S(2)}) collective-permute-start(bf16[64,8192]{1,0:T(8,128)(2,1)S(1)} %get-tuple-element.68), channel_id=1, source_target_pairs={{0,4},{1,5},{2,6},{3,7},{12,8},{13,9},{14,10},{15,11},{16,20},{17,... | collective-permute-start | bytes 3145736 | tf_op jit(solution)/shard_map/ppermute | solution.py:328
  119.0 50.4 %collective-permute-start.21 = (bf16[64,8192]{1,0:T(8,128)(2,1)S(1)}, bf16[64,8192]{1,0:T(8,128)(2,1)S(1)}, u32[]{:S(2)}, u32[]{:S(2)}) collective-permute-start(bf16[64,8192]{1,0:T(8,128)(2,1)S(1)} %get-tuple-element.68), channel_id=1, source_target_pairs={{4,8},{5,9},{6,10},{7,11},{8,4},{9,5},{10,6},{11,7},{20,24},{21,25... | collective-permute-start | bytes 3145736 | tf_op jit(solution)/shard_map/ppermute | solution.py:328
  121.2 16.9 %collective-permute-start.5 = (bf16[1,2,32,8192]{3,2,1,0:T(8,128)(2,1)S(1)}, bf16[1,2,32,8192]{3,2,1,0:T(8,128)(2,1)S(1)}, u32[]{:S(2)}, u32[]{:S(2)}) collective-permute-start(bf16[1,2,32,8192]{3,2,1,0:T(8,128)(2,1)S(1)} %slice.37), channel_id=1, source_target_pairs={{0,1},{1,0},{2,3},{3,2},{4,5},{5,4},{6,7},{7,6},{8,9},{9,8},{10,11... | collective-permute-start | bytes 3145736 | tf_op jit(solution)/shard_map/ppermute | solution.py:328
  137.4 40.6 %collective-permute-start.18 = (bf16[64,8192]{1,0:T(8,128)(2,1)S(1)}, bf16[64,8192]{1,0:T(8,128)(2,1)S(1)}, u32[]{:S(2)}, u32[]{:S(2)}) collective-permute-start(bf16[64,8192]{1,0:T(8,128)(2,1)S(1)} %add_convert_fusion.3), channel_id=1, source_target_pairs={{4,8},{5,9},{6,10},{7,11},{8,4},{9,5},{10,6},{11,7},{20,24},{21,25... | collective-permute-start | bytes 3145736 | tf_op jit(solution)/shard_map/ppermute | solution.py:328
  144.6 23.3 %collective-permute-start.15 = (bf16[64,8192]{1,0:T(8,128)(2,1)S(1)}, bf16[64,8192]{1,0:T(8,128)(2,1)S(1)}, u32[]{:S(2)}, u32[]{:S(2)}) collective-permute-start(bf16[64,8192]{1,0:T(8,128)(2,1)S(1)} %get-tuple-element.58), channel_id=1, source_target_pairs={{0,2},{1,3},{2,0},{3,1},{4,6},{5,7},{6,4},{7,5},{8,10},{9,11},{10,... | collective-permute-start | bytes 3145736 | tf_op jit(solution)/shard_map/ppermute | solution.py:328
  146.3 40.7 %collective-permute-start.19 = (bf16[64,8192]{1,0:T(8,128)(2,1)S(1)}, bf16[64,8192]{1,0:T(8,128)(2,1)S(1)}, u32[]{:S(2)}, u32[]{:S(2)}) collective-permute-start(bf16[64,8192]{1,0:T(8,128)(2,1)S(1)} %add_convert_fusion.2), channel_id=1, source_target_pairs={{0,4},{1,5},{2,6},{3,7},{4,0},{5,1},{6,2},{7,3},{8,12},{9,13},{10,... | collective-permute-start | bytes 3145736 | tf_op jit(solution)/shard_map/ppermute | solution.py:328
  167.9 19.0 %collective-permute-start.16 = (bf16[64,8192]{1,0:T(8,128)(2,1)S(1)}, bf16[64,8192]{1,0:T(8,128)(2,1)S(1)}, u32[]{:S(2)}, u32[]{:S(2)}) collective-permute-start(bf16[64,8192]{1,0:T(8,128)(2,1)S(1)} %get-tuple-element.60), channel_id=1, source_target_pairs={{0,2},{1,3},{2,0},{3,1},{4,6},{5,7},{6,4},{7,5},{8,10},{9,11},{10,... | collective-permute-start | bytes 3145736 | tf_op jit(solution)/shard_map/ppermute | solution.py:328
  169.6 31.8 %collective-permute-start.23 = (bf16[64,8192]{1,0:T(8,128)(2,1)S(1)}, bf16[64,8192]{1,0:T(8,128)(2,1)S(1)}, u32[]{:S(2)}, u32[]{:S(2)}) collective-permute-start(bf16[64,8192]{1,0:T(8,128)(2,1)S(1)} %add_convert_fusion), channel_id=1, source_target_pairs={{0,4},{1,5},{2,6},{3,7},{4,0},{5,1},{6,2},{7,3},{8,12},{9,13},{10,... | collective-permute-start | bytes 3145736 | tf_op jit(solution)/shard_map/ppermute | solution.py:328
  177.0 24.3 %collective-permute-start.22 = (bf16[64,8192]{1,0:T(8,128)(2,1)S(1)}, bf16[64,8192]{1,0:T(8,128)(2,1)S(1)}, u32[]{:S(2)}, u32[]{:S(2)}) collective-permute-start(bf16[64,8192]{1,0:T(8,128)(2,1)S(1)} %add_convert_fusion.1), channel_id=1, source_target_pairs={{4,8},{5,9},{6,10},{7,11},{8,4},{9,5},{10,6},{11,7},{20,24},{21,25... | collective-permute-start | bytes 3145736 | tf_op jit(solution)/shard_map/ppermute | solution.py:328
  178.0 26.0 %collective-permute-start.14 = (bf16[64,8192]{1,0:T(8,128)(2,1)S(1)}, bf16[64,8192]{1,0:T(8,128)(2,1)S(1)}, u32[]{:S(2)}, u32[]{:S(2)}) collective-permute-start(bf16[64,8192]{1,0:T(8,128)(2,1)S(1)} %get-tuple-element.57), channel_id=1, source_target_pairs={{0,1},{1,0},{2,3},{3,2},{4,5},{5,4},{6,7},{7,6},{8,9},{9,8},{10,11... | collective-permute-start | bytes 3145736 | tf_op jit(solution)/shard_map/ppermute | solution.py:328
  187.0 17.0 %collective-permute-start.17 = (bf16[64,8192]{1,0:T(8,128)(2,1)S(1)}, bf16[64,8192]{1,0:T(8,128)(2,1)S(1)}, u32[]{:S(2)}, u32[]{:S(2)}) collective-permute-start(bf16[64,8192]{1,0:T(8,128)(2,1)S(1)} %collective-permute-done.16), channel_id=1, source_target_pairs={{0,1},{1,0},{2,3},{3,2},{4,5},{5,4},{6,7},{7,6},{8,9},{9,8},{10,11... | collective-permute-start | bytes 3145736 | tf_op jit(solution)/shard_map/ppermute | solution.py:328
  206.6 9.4 %collective-permute-start.27 = (f32[8,128]{1,0:T(8,128)S(1)}, f32[8,128]{1,0:T(8,128)S(1)}, u32[]{:S(2)}, u32[]{:S(2)}) collective-permute-start(f32[8,128]{1,0:T(8,128)S(1)} %add_add_fusion.refs_2_), channel_id=1, source_target_pairs={{0,4},{1,5},{2,6},{3,7},{4,0},{5,1},{6,2},{7,3},{8,12},{9,13},{10,... | collective-permute-start | bytes 12296 | tf_op jit(solution)/shard_map/ppermute | solution.py:328
  212.2 5.4 %collective-permute-start.29 = (f32[8,128]{1,0:T(8,128)S(1)}, f32[8,128]{1,0:T(8,128)S(1)}, u32[]{:S(2)}, u32[]{:S(2)}) collective-permute-start(f32[8,128]{1,0:T(8,128)S(1)} %add_add_fusion.refs_2_), channel_id=1, source_target_pairs={{0,12},{1,13},{2,14},{3,15},{4,8},{5,9},{6,10},{7,11},{8,4},{9,5},... | collective-permute-start | bytes 12296 | tf_op jit(solution)/shard_map/ppermute | solution.py:328
  (16 other events, 125.0 us)

commit v16 on v15

--- a/solution.py
+++ b/solution.py
@@ -222,6 +222,14 @@
         out_shape=[pltpu.VMEM(*shape) for shape in out_shapes],
         compiler_params=pltpu.CompilerParams(vmem_limit_bytes=VMEM_BYTES),
     )(*first, *in_vmem(*arrays))
+
+
+def stack(down, up):
+    def body(down_ref, up_ref, out_ref):
+        out_ref[0] = down_ref[...]
+        out_ref[1] = up_ref[...]
+
+    return in_place(body, [((2, *down.shape), BF16)], down, up)[0]
 
 
 def early_group(flags, rows3, rows2, crossed):
@@ -334,7 +342,7 @@
         return [(i, (i // plane) * plane + ((i % plane) ^ m)) for i in range(ndevices)]
 
     down, up = pool_down_factors[0], pool_up_factors[0]
-    own = jnp.concatenate([pool_down_factors, pool_up_factors])
+    own = stack(down, up)
     pair = send(own, swap)
     crossed = send(own, cross)
 

time: 220 us -> 221 us (level)
  local copies, waits for them, and re-layouts: 9.41 us -> 5.85 us
  waiting for transfers between devices: 120 us -> 123 us
    ppermute x30, waiting for transfers between devices: 120 us -> 123 us  [send(): return lax.ppermute(array, 'dp', pairs)]
    pallas_call x5 -> x6, Pallas kernels: 15.6 us -> 17 us  [in_place(): pl.pallas_call(body, in_specs=[pl.BlockSpec(memory_space=pltpu.SMEM)] * l...]
where the time goes in v16:
time: 221 us
  waiting for transfers between devices  123 us (56%)
  starting transfers between devices  57.5 us (26%)
  Pallas kernels  30.5 us (14%)
  local copies, waits for them, and re-layouts  5.85 us (3%)
  other arithmetic  3.1 us (1%)
    ppermute x30, waiting for transfers between devices, send(): return lax.ppermute(array, 'dp', pairs)  123 us
    ppermute x30, starting transfers between devices, send(): return lax.ppermute(array, 'dp', pairs)  57.5 us
    pallas_call x6, Pallas kernels, in_place(): pl.pallas_call(body, in_specs=[pl.BlockSpec(memory_space=pltpu.SMEM)] * l...  17 us
    pallas_call x1, Pallas kernels, pack(): pl.pallas_call(body, grid=(tiles,), in_specs=[pl.BlockSpec(place.shape, l...  6.36 us
    pallas_call x2, Pallas kernels, unpack(): pl.pallas_call(body, grid=(width // 2 // tile,), in_specs=[pl.BlockSpec(p...  4.79 us
  transfers between devices with their start and end apart: 30, of which 13 were waited for; matrix products, arithmetic and copies ran while one was open for 3% of the time, Pallas kernels for 12%

profile of v16, /device:TPU:0, one launch (start us, length us, event | category | flops | bytes accessed | tf_op | source)
XLA Modules:
  0.0 220.6 jit_solution(17057317347614924365)
XLA Ops:
  4.6 2.0 collective-permute-start.8
  6.5 4.6 %collective-permute-start.6 = (bf16[2,64,8192]{2,1,0:T(8,128)(2,1)}, bf16[2,64,8192]{2,1,0:T(8,128)(2,1)}, u32[]{:S(2)}, u32[]{:S(2)}) collective-permute-start(bf16[2,64,8192]{2,1,0:T(8,128)(2,1)} %shard_map.86), channel_id=1, source_target_pairs={{0,4},{1,5},{2,6},{3,7},{4,0},{5,1},{6,2},{7,3},{8,12},{9,13},{10,... | collective-permute-start | bytes 6291464 | tf_op jit(solution)/shard_map/ppermute | solution.py:336
  11.8 6.4 %shard_map.85 = (bf16[1,2,64,8192]{3,2,1,0:T(8,128)(2,1)S(1)}, bf16[1,2,64,8192]{3,2,1,0:T(8,128)(2,1)S(1)}, bf16[2,2,16,8192]{3,2,1,0:T(8,128)(2,1)S(1)}, bf16[...) custom-call(bf16[256,128]{1,0:T(8,128)(2,1)S(1)} %fusion.1.place_ref, bf16[128,8192]{1,0:T(8,128)(2,1)} %x_in.1, ...), custom_call_target="tpu_custom_call" | custom-call | tf_op jit(solution)/shard_map/pallas_call | solution.py:107
  19.8 22.8 %collective-permute-done.1 = bf16[2,2,16,8192]{3,2,1,0:T(8,128)(2,1)S(1)} collective-permute-done((bf16[2,2,16,8192]{3,2,1,0:T(8,128)(2,1)S(1)}, bf16[2,2,16,8192]{3,2,1,0:T(8,128)(2,1)S(1)}, u32[]{:S(2)}, u32[]{:S(2)}) %collective-permute-start.1) | collective-permute-done | bytes 1048608 | tf_op jit(solution)/shard_map/ppermute | solution.py:336
  46.3 3.6 %collective-permute-start.9 = (bf16[2,64,8192]{2,1,0:T(8,128)(2,1)S(1)}, bf16[2,64,8192]{2,1,0:T(8,128)(2,1)}, u32[]{:S(2)}, u32[]{:S(2)}) collective-permute-start(bf16[2,64,8192]{2,1,0:T(8,128)(2,1)S(1)} %pad_maximum_fusion.rows3_ref), channel_id=1, source_target_pairs={{0,4},{1,5},{2,6},{3,7},{12,8},{13,9},{14,10},{15,11},{16,20},{17,... | collective-permute-start | bytes 6291464 | tf_op jit(solution)/shard_map/ppermute | solution.py:336
  51.2 6.3 %collective-permute-done.6.refs_4_ = bf16[2,64,8192]{2,1,0:T(8,128)(2,1)} collective-permute-done((bf16[2,64,8192]{2,1,0:T(8,128)(2,1)}, bf16[2,64,8192]{2,1,0:T(8,128)(2,1)}, u32[]{:S(2)}, u32[]{:S(2)}) %collective-permute-start.6) | collective-permute-done | bytes 2097184 | tf_op jit(solution)/shard_map/ppermute | solution.py:336
  59.5 6.6 %collective-permute-done.2 = bf16[2,2,16,8192]{3,2,1,0:T(8,128)(2,1)S(1)} collective-permute-done((bf16[2,2,16,8192]{3,2,1,0:T(8,128)(2,1)S(1)}, bf16[2,2,16,8192]{3,2,1,0:T(8,128)(2,1)S(1)}, u32[]{:S(2)}, u32[]{:S(2)}) %collective-permute-start.2) | collective-permute-done | bytes 1048608 | tf_op jit(solution)/shard_map/ppermute | solution.py:336
  72.6 3.5 %shard_map.87 = (bf16[64,8192]{1,0:T(8,128)(2,1)S(1)}, bf16[64,8192]{1,0:T(8,128)(2,1)S(1)}, bf16[64,8192]{1,0:T(8,128)(2,1)S(1)}, bf16[2,64,8192]{2,1,0:T(8,128)(2,1)S(1)}) custom-call(s32[1]{0:T(128)} %bitcast.1.flags_ref, bf16[2,64,8192]{2,1,0:T(8,128)(2,1)S(1)} %pad_maximum_fusion.rows3_ref, bf16[2,64,8192]{2,1,0:T(8,128)(2,1)S(1)} %pad_maximum_fusion.1.rows2_ref, ...), custom_call_target="tpu_custom_call" | custom-call | tf_op jit(solution)/shard_map/pallas_call | solution.py:218
  76.1 24.8 %collective-permute-done.9.handed_ref = bf16[2,64,8192]{2,1,0:T(8,128)(2,1)} collective-permute-done((bf16[2,64,8192]{2,1,0:T(8,128)(2,1)S(1)}, bf16[2,64,8192]{2,1,0:T(8,128)(2,1)}, u32[]{:S(2)}, u32[]{:S(2)}) %collective-permute-start.9) | collective-permute-done | bytes 2097184 | tf_op jit(solution)/shard_map/ppermute | solution.py:336
  100.9 2.6 %collective-permute-done.10.outer_ref = bf16[2,64,8192]{2,1,0:T(8,128)(2,1)} collective-permute-done((bf16[2,64,8192]{2,1,0:T(8,128)(2,1)}, bf16[2,64,8192]{2,1,0:T(8,128)(2,1)}, u32[]{:S(2)}, u32[]{:S(2)}) %collective-permute-start.10) | collective-permute-done | bytes 2097184 | tf_op jit(solution)/shard_map/ppermute | solution.py:336
  103.5 5.5 %shard_map.88 = (bf16[64,8192]{1,0:T(8,128)(2,1)S(1)}, bf16[64,8192]{1,0:T(8,128)(2,1)S(1)}, bf16[64,8192]{1,0:T(8,128)(2,1)S(1)}, bf16[64,8192]{1,0:T(8,128)(2,1)S(1)}) custom-call(s32[1]{0:T(128)} %bitcast.1.flags_ref, bf16[2,64,8192]{2,1,0:T(8,128)(2,1)S(1)} %get-tuple-element.50.rows_ref, bf16[2,64,8192]{2,1,0:T(8,128)(2,1)} %collective-permute-done.9.handed_ref, ...), custom_call_target="tpu_custom_call" | custom-call | tf_op jit(solution)/shard_map/pallas_call | solution.py:218
  109.0 5.0 %collective-permute-start.12 = (bf16[64,8192]{1,0:T(8,128)(2,1)S(1)}, bf16[64,8192]{1,0:T(8,128)(2,1)S(1)}, u32[]{:S(2)}, u32[]{:S(2)}) collective-permute-start(bf16[64,8192]{1,0:T(8,128)(2,1)S(1)} %get-tuple-element.53), channel_id=1, source_target_pairs={{0,4},{1,5},{2,6},{3,7},{4,0},{5,1},{6,2},{7,3},{8,12},{9,13},{10,... | collective-permute-start | bytes 3145736 | tf_op jit(solution)/shard_map/ppermute | solution.py:336
  114.8 4.8 %collective-permute-start.20 = (bf16[64,8192]{1,0:T(8,128)(2,1)S(1)}, bf16[64,8192]{1,0:T(8,128)(2,1)S(1)}, u32[]{:S(2)}, u32[]{:S(2)}) collective-permute-start(bf16[64,8192]{1,0:T(8,128)(2,1)S(1)} %get-tuple-element.68), channel_id=1, source_target_pairs={{0,4},{1,5},{2,6},{3,7},{12,8},{13,9},{14,10},{15,11},{16,20},{17,... | collective-permute-start | bytes 3145736 | tf_op jit(solution)/shard_map/ppermute | solution.py:336
  121.9 15.8 %collective-permute-done.12.refs_9_ = bf16[64,8192]{1,0:T(8,128)(2,1)S(1)} collective-permute-done((bf16[64,8192]{1,0:T(8,128)(2,1)S(1)}, bf16[64,8192]{1,0:T(8,128)(2,1)S(1)}, u32[]{:S(2)}, u32[]{:S(2)}) %collective-permute-start.12) | collective-permute-done | bytes 1048608 | tf_op jit(solution)/shard_map/ppermute | solution.py:336
  138.7 5.5 %shard_map.89 = (bf16[64,8192]{1,0:T(8,128)(2,1)S(1)}, bf16[64,8192]{1,0:T(8,128)(2,1)S(1)}, bf16[64,8192]{1,0:T(8,128)(2,1)S(1)}, bf16[64,8192]{1,0:T(8,128)(2,...) custom-call(s32[1]{0:T(128)} %bitcast.1.flags_ref, ...), custom_call_target="tpu_custom_call" | custom-call | tf_op jit(solution)/shard_map/pallas_call | solution.py:218
  146.0 7.2 %collective-permute-start.19 = (bf16[64,8192]{1,0:T(8,128)(2,1)S(1)}, bf16[64,8192]{1,0:T(8,128)(2,1)S(1)}, u32[]{:S(2)}, u32[]{:S(2)}) collective-permute-start(bf16[64,8192]{1,0:T(8,128)(2,1)S(1)} %add_convert_fusion.2), channel_id=1, source_target_pairs={{0,4},{1,5},{2,6},{3,7},{4,0},{5,1},{6,2},{7,3},{8,12},{9,13},{10,... | collective-permute-start | bytes 3145736 | tf_op jit(solution)/shard_map/ppermute | solution.py:336
  153.2 14.4 %collective-permute-done.15.refs_2_ = bf16[64,8192]{1,0:T(8,128)(2,1)S(1)} collective-permute-done((bf16[64,8192]{1,0:T(8,128)(2,1)S(1)}, bf16[64,8192]{1,0:T(8,128)(2,1)S(1)}, u32[]{:S(2)}, u32[]{:S(2)}) %collective-permute-start.15) | collective-permute-done | bytes 1048608 | tf_op jit(solution)/shard_map/ppermute | solution.py:336
  169.3 7.2 %collective-permute-start.23 = (bf16[64,8192]{1,0:T(8,128)(2,1)S(1)}, bf16[64,8192]{1,0:T(8,128)(2,1)S(1)}, u32[]{:S(2)}, u32[]{:S(2)}) collective-permute-start(bf16[64,8192]{1,0:T(8,128)(2,1)S(1)} %add_convert_fusion), channel_id=1, source_target_pairs={{0,4},{1,5},{2,6},{3,7},{4,0},{5,1},{6,2},{7,3},{8,12},{9,13},{10,... | collective-permute-start | bytes 3145736 | tf_op jit(solution)/shard_map/ppermute | solution.py:336
  177.7 8.9 %collective-permute-done.16 = bf16[64,8192]{1,0:T(8,128)(2,1)S(1)} collective-permute-done((bf16[64,8192]{1,0:T(8,128)(2,1)S(1)}, bf16[64,8192]{1,0:T(8,128)(2,1)S(1)}, u32[]{:S(2)}, u32[]{:S(2)}) %collective-permute-start.16) | collective-permute-done | bytes 1048608 | tf_op jit(solution)/shard_map/ppermute | solution.py:336
  187.2 14.7 %collective-permute-done.23.refs_1_ = bf16[64,8192]{1,0:T(8,128)(2,1)S(1)} collective-permute-done((bf16[64,8192]{1,0:T(8,128)(2,1)S(1)}, bf16[64,8192]{1,0:T(8,128)(2,1)S(1)}, u32[]{:S(2)}, u32[]{:S(2)}) %collective-permute-start.23) | collective-permute-done | bytes 1048608 | tf_op jit(solution)/shard_map/ppermute | solution.py:336
  204.5 2.4 %shard_map.90.refs_4_ = bf16[128,8192]{1,0:T(8,128)(2,1)} custom-call(bf16[128,256]{1,0:T(8,128)(2,1)S(1)} %fusion.place_ref, bf16[64,8192]{1,0:T(8,128)(2,1)} %copy-done.8, bf16[64,8192]{1,0:T(8,128)(2,1)S(1)} %collective-permute-done.14.refs_1_, bf16[64,8192]{1,0:T(8,128)(2,1)S(1)} %collective-permute-done.15.refs_2_, ...), custom_call_target="tpu_custom_call" | custom-call | tf_op jit(solution)/shard_map/pallas_call | solution.py:128
  207.2 4.4 %collective-permute-start.27 = (f32[8,128]{1,0:T(8,128)S(1)}, f32[8,128]{1,0:T(8,128)S(1)}, u32[]{:S(2)}, u32[]{:S(2)}) collective-permute-start(f32[8,128]{1,0:T(8,128)S(1)} %add_add_fusion.refs_2_), channel_id=1, source_target_pairs={{0,4},{1,5},{2,6},{3,7},{4,0},{5,1},{6,2},{7,3},{8,12},{9,13},{10,... | collective-permute-start | bytes 12296 | tf_op jit(solution)/shard_map/ppermute | solution.py:336
  214.2 2.4 %shard_map.91 = bf16[128,8192]{1,0:T(8,128)(2,1)} custom-call(bf16[128,256]{1,0:T(8,128)(2,1)S(1)} %fusion.place_ref, bf16[64,8192]{1,0:T(8,128)(2,1)} %copy-done.8, bf16[64,8192]{1,0:T(8,128)(2,1)S(1)} %collective-permute-done.14.refs_1_, bf16[64,8192]{1,0:T(8,128)(2,1)S(1)} %collective-permute-done.15.refs_2_, ...), custom_call_target="tpu_custom_call", output_to_operand_aliasing={{}: (5, {})} | custom-call | tf_op jit(solution)/shard_map/pallas_call | solution.py:128
  218.2 2.3 %shard_map.94 = (f32[1,64,8192]{2,1,0:T(8,128)}, f32[1,64,8192]{2,1,0:T(8,128)}) custom-call(f32[64,8192]{1,0:T(8,128)S(1)} %get-tuple-element.65.refs_0_, f32[64,8192]{1,0:T(8,128)S(1)} %get-tuple-element.72.refs_1_, f32[8,128]{1,0:T(8,128)S(1)} %add_add_fusion.refs_2_, f32[8,128]{1,0:T(8,128)S(1)} %collective-permute-done.27.refs_3_, ...), custom_call_target="tpu_custom_call" | custom-call | tf_op jit(solution)/shard_map/pallas_call | solution.py:183
  (91 shorter events, 35.8 us)
Async XLA Ops:
  4.6 45.4 %collective-permute-start.8 = (bf16[2,64,8192]{2,1,0:T(8,128)(2,1)}, bf16[2,64,8192]{2,1,0:T(8,128)(2,1)}, u32[]{:S(2)}, u32[]{:S(2)}) collective-permute-start(bf16[2,64,8192]{2,1,0:T(8,128)(2,1)} %shard_map.86), channel_id=1, source_target_pairs={{4,8},{5,9},{6,10},{7,11},{8,4},{9,5},{10,6},{11,7},{20,24},{21,25... | collective-permute-start | bytes 6291464 | tf_op jit(solution)/shard_map/ppermute | solution.py:336
  6.5 51.0 %collective-permute-start.6 = (bf16[2,64,8192]{2,1,0:T(8,128)(2,1)}, bf16[2,64,8192]{2,1,0:T(8,128)(2,1)}, u32[]{:S(2)}, u32[]{:S(2)}) collective-permute-start(bf16[2,64,8192]{2,1,0:T(8,128)(2,1)} %shard_map.86), channel_id=1, source_target_pairs={{0,4},{1,5},{2,6},{3,7},{4,0},{5,1},{6,2},{7,3},{8,12},{9,13},{10,... | collective-permute-start | bytes 6291464 | tf_op jit(solution)/shard_map/ppermute | solution.py:336
  18.2 24.4 %collective-permute-start.1 = (bf16[2,2,16,8192]{3,2,1,0:T(8,128)(2,1)S(1)}, bf16[2,2,16,8192]{3,2,1,0:T(8,128)(2,1)S(1)}, u32[]{:S(2)}, u32[]{:S(2)}) collective-permute-start(bf16[2,2,16,8192]{3,2,1,0:T(8,128)(2,1)S(1)} %get-tuple-element.47), channel_id=1, source_target_pairs={{0,2},{1,3},{2,0},{3,1},{4,6},{5,7},{6,4},{7,5},{8,10},{9,11},{10,... | collective-permute-start | bytes 3145736 | tf_op jit(solution)/shard_map/ppermute | solution.py:336
  19.8 24.5 %collective-permute-start = (bf16[1,2,64,8192]{3,2,1,0:T(8,128)(2,1)S(1)}, bf16[1,2,64,8192]{3,2,1,0:T(8,128)(2,1)S(1)}, u32[]{:S(2)}, u32[]{:S(2)}) collective-permute-start(bf16[1,2,64,8192]{3,2,1,0:T(8,128)(2,1)S(1)} %get-tuple-element.44), channel_id=1, source_target_pairs={{0,1},{1,0},{2,3},{3,2},{4,5},{5,4},{6,7},{7,6},{8,9},{9,8},{10,11... | collective-permute-start | bytes 6291464 | tf_op jit(solution)/shard_map/ppermute | solution.py:336
  42.6 23.5 %collective-permute-start.2 = (bf16[2,2,16,8192]{3,2,1,0:T(8,128)(2,1)S(1)}, bf16[2,2,16,8192]{3,2,1,0:T(8,128)(2,1)S(1)}, u32[]{:S(2)}, u32[]{:S(2)}) collective-permute-start(bf16[2,2,16,8192]{3,2,1,0:T(8,128)(2,1)S(1)} %get-tuple-element.48), channel_id=1, source_target_pairs={{0,2},{1,3},{2,0},{3,1},{4,6},{5,7},{6,4},{7,5},{8,10},{9,11},{10,... | collective-permute-start | bytes 3145736 | tf_op jit(solution)/shard_map/ppermute | solution.py:336
  46.3 54.6 %collective-permute-start.9 = (bf16[2,64,8192]{2,1,0:T(8,128)(2,1)S(1)}, bf16[2,64,8192]{2,1,0:T(8,128)(2,1)}, u32[]{:S(2)}, u32[]{:S(2)}) collective-permute-start(bf16[2,64,8192]{2,1,0:T(8,128)(2,1)S(1)} %pad_maximum_fusion.rows3_ref), channel_id=1, source_target_pairs={{0,4},{1,5},{2,6},{3,7},{12,8},{13,9},{14,10},{15,11},{16,20},{17,... | collective-permute-start | bytes 6291464 | tf_op jit(solution)/shard_map/ppermute | solution.py:336
  49.9 53.6 %collective-permute-start.10 = (bf16[2,64,8192]{2,1,0:T(8,128)(2,1)}, bf16[2,64,8192]{2,1,0:T(8,128)(2,1)}, u32[]{:S(2)}, u32[]{:S(2)}) collective-permute-start(bf16[2,64,8192]{2,1,0:T(8,128)(2,1)} %collective-permute-done.8.crossed_ref), channel_id=1, source_target_pairs={{4,0},{5,1},{6,2},{7,3},{8,12},{9,13},{10,14},{11,15},{20,16},{21,... | collective-permute-start | bytes 6291464 | tf_op jit(solution)/shard_map/ppermute | solution.py:336
  57.5 46.0 %collective-permute-start.11 = (bf16[2,64,8192]{2,1,0:T(8,128)(2,1)}, bf16[2,64,8192]{2,1,0:T(8,128)(2,1)}, u32[]{:S(2)}, u32[]{:S(2)}) collective-permute-start(bf16[2,64,8192]{2,1,0:T(8,128)(2,1)} %collective-permute-done.6.refs_4_), channel_id=1, source_target_pairs={{4,8},{5,9},{6,10},{7,11},{8,4},{9,5},{10,6},{11,7},{20,24},{21,25... | collective-permute-start | bytes 6291464 | tf_op jit(solution)/shard_map/ppermute | solution.py:336
  69.8 50.5 %collective-permute-start.4 = (bf16[2,2,32,8192]{3,2,1,0:T(8,128)(2,1)}, bf16[2,2,32,8192]{3,2,1,0:T(8,128)(2,1)}, u32[]{:S(2)}, u32[]{:S(2)}) collective-permute-start(bf16[2,2,32,8192]{3,2,1,0:T(8,128)(2,1)} %get-tuple-element.49), channel_id=1, source_target_pairs={{0,2},{1,3},{2,0},{3,1},{4,6},{5,7},{6,4},{7,5},{8,10},{9,11},{10,... | collective-permute-start | bytes 6291464 | tf_op jit(solution)/shard_map/ppermute | solution.py:336
  109.0 28.7 %collective-permute-start.12 = (bf16[64,8192]{1,0:T(8,128)(2,1)S(1)}, bf16[64,8192]{1,0:T(8,128)(2,1)S(1)}, u32[]{:S(2)}, u32[]{:S(2)}) collective-permute-start(bf16[64,8192]{1,0:T(8,128)(2,1)S(1)} %get-tuple-element.53), channel_id=1, source_target_pairs={{0,4},{1,5},{2,6},{3,7},{4,0},{5,1},{6,2},{7,3},{8,12},{9,13},{10,... | collective-permute-start | bytes 3145736 | tf_op jit(solution)/shard_map/ppermute | solution.py:336
  114.1 23.6 %collective-permute-start.13 = (bf16[64,8192]{1,0:T(8,128)(2,1)S(1)}, bf16[64,8192]{1,0:T(8,128)(2,1)S(1)}, u32[]{:S(2)}, u32[]{:S(2)}) collective-permute-start(bf16[64,8192]{1,0:T(8,128)(2,1)S(1)} %get-tuple-element.54), channel_id=1, source_target_pairs={{4,8},{5,9},{6,10},{7,11},{8,4},{9,5},{10,6},{11,7},{20,24},{21,25... | collective-permute-start | bytes 3145736 | tf_op jit(solution)/shard_map/ppermute | solution.py:336
  114.8 54.3 %collective-permute-start.20 = (bf16[64,8192]{1,0:T(8,128)(2,1)S(1)}, bf16[64,8192]{1,0:T(8,128)(2,1)S(1)}, u32[]{:S(2)}, u32[]{:S(2)}) collective-permute-start(bf16[64,8192]{1,0:T(8,128)(2,1)S(1)} %get-tuple-element.68), channel_id=1, source_target_pairs={{0,4},{1,5},{2,6},{3,7},{12,8},{13,9},{14,10},{15,11},{16,20},{17,... | collective-permute-start | bytes 3145736 | tf_op jit(solution)/shard_map/ppermute | solution.py:336
  119.5 49.6 %collective-permute-start.21 = (bf16[64,8192]{1,0:T(8,128)(2,1)S(1)}, bf16[64,8192]{1,0:T(8,128)(2,1)S(1)}, u32[]{:S(2)}, u32[]{:S(2)}) collective-permute-start(bf16[64,8192]{1,0:T(8,128)(2,1)S(1)} %get-tuple-element.68), channel_id=1, source_target_pairs={{4,8},{5,9},{6,10},{7,11},{8,4},{9,5},{10,6},{11,7},{20,24},{21,25... | collective-permute-start | bytes 3145736 | tf_op jit(solution)/shard_map/ppermute | solution.py:336
  121.8 16.9 %collective-permute-start.5 = (bf16[1,2,32,8192]{3,2,1,0:T(8,128)(2,1)S(1)}, bf16[1,2,32,8192]{3,2,1,0:T(8,128)(2,1)S(1)}, u32[]{:S(2)}, u32[]{:S(2)}) collective-permute-start(bf16[1,2,32,8192]{3,2,1,0:T(8,128)(2,1)S(1)} %slice.37), channel_id=1, source_target_pairs={{0,1},{1,0},{2,3},{3,2},{4,5},{5,4},{6,7},{7,6},{8,9},{9,8},{10,11... | collective-permute-start | bytes 3145736 | tf_op jit(solution)/shard_map/ppermute | solution.py:336
  137.9 39.7 %collective-permute-start.18 = (bf16[64,8192]{1,0:T(8,128)(2,1)S(1)}, bf16[64,8192]{1,0:T(8,128)(2,1)S(1)}, u32[]{:S(2)}, u32[]{:S(2)}) collective-permute-start(bf16[64,8192]{1,0:T(8,128)(2,1)S(1)} %add_convert_fusion.3), channel_id=1, source_target_pairs={{4,8},{5,9},{6,10},{7,11},{8,4},{9,5},{10,6},{11,7},{20,24},{21,25... | collective-permute-start | bytes 3145736 | tf_op jit(solution)/shard_map/ppermute | solution.py:336
  144.2 23.4 %collective-permute-start.15 = (bf16[64,8192]{1,0:T(8,128)(2,1)S(1)}, bf16[64,8192]{1,0:T(8,128)(2,1)S(1)}, u32[]{:S(2)}, u32[]{:S(2)}) collective-permute-start(bf16[64,8192]{1,0:T(8,128)(2,1)S(1)} %get-tuple-element.58), channel_id=1, source_target_pairs={{0,2},{1,3},{2,0},{3,1},{4,6},{5,7},{6,4},{7,5},{8,10},{9,11},{10,... | collective-permute-start | bytes 3145736 | tf_op jit(solution)/shard_map/ppermute | solution.py:336
  146.0 40.7 %collective-permute-start.19 = (bf16[64,8192]{1,0:T(8,128)(2,1)S(1)}, bf16[64,8192]{1,0:T(8,128)(2,1)S(1)}, u32[]{:S(2)}, u32[]{:S(2)}) collective-permute-start(bf16[64,8192]{1,0:T(8,128)(2,1)S(1)} %add_convert_fusion.2), channel_id=1, source_target_pairs={{0,4},{1,5},{2,6},{3,7},{4,0},{5,1},{6,2},{7,3},{8,12},{9,13},{10,... | collective-permute-start | bytes 3145736 | tf_op jit(solution)/shard_map/ppermute | solution.py:336
  167.6 19.0 %collective-permute-start.16 = (bf16[64,8192]{1,0:T(8,128)(2,1)S(1)}, bf16[64,8192]{1,0:T(8,128)(2,1)S(1)}, u32[]{:S(2)}, u32[]{:S(2)}) collective-permute-start(bf16[64,8192]{1,0:T(8,128)(2,1)S(1)} %get-tuple-element.60), channel_id=1, source_target_pairs={{0,2},{1,3},{2,0},{3,1},{4,6},{5,7},{6,4},{7,5},{8,10},{9,11},{10,... | collective-permute-start | bytes 3145736 | tf_op jit(solution)/shard_map/ppermute | solution.py:336
  169.3 32.7 %collective-permute-start.23 = (bf16[64,8192]{1,0:T(8,128)(2,1)S(1)}, bf16[64,8192]{1,0:T(8,128)(2,1)S(1)}, u32[]{:S(2)}, u32[]{:S(2)}) collective-permute-start(bf16[64,8192]{1,0:T(8,128)(2,1)S(1)} %add_convert_fusion), channel_id=1, source_target_pairs={{0,4},{1,5},{2,6},{3,7},{4,0},{5,1},{6,2},{7,3},{8,12},{9,13},{10,... | collective-permute-start | bytes 3145736 | tf_op jit(solution)/shard_map/ppermute | solution.py:336
  176.7 25.2 %collective-permute-start.22 = (bf16[64,8192]{1,0:T(8,128)(2,1)S(1)}, bf16[64,8192]{1,0:T(8,128)(2,1)S(1)}, u32[]{:S(2)}, u32[]{:S(2)}) collective-permute-start(bf16[64,8192]{1,0:T(8,128)(2,1)S(1)} %add_convert_fusion.1), channel_id=1, source_target_pairs={{4,8},{5,9},{6,10},{7,11},{8,4},{9,5},{10,6},{11,7},{20,24},{21,25... | collective-permute-start | bytes 3145736 | tf_op jit(solution)/shard_map/ppermute | solution.py:336
  177.7 26.9 %collective-permute-start.14 = (bf16[64,8192]{1,0:T(8,128)(2,1)S(1)}, bf16[64,8192]{1,0:T(8,128)(2,1)S(1)}, u32[]{:S(2)}, u32[]{:S(2)}) collective-permute-start(bf16[64,8192]{1,0:T(8,128)(2,1)S(1)} %get-tuple-element.57), channel_id=1, source_target_pairs={{0,1},{1,0},{2,3},{3,2},{4,5},{5,4},{6,7},{7,6},{8,9},{9,8},{10,11... | collective-permute-start | bytes 3145736 | tf_op jit(solution)/shard_map/ppermute | solution.py:336
  186.6 17.9 %collective-permute-start.17 = (bf16[64,8192]{1,0:T(8,128)(2,1)S(1)}, bf16[64,8192]{1,0:T(8,128)(2,1)S(1)}, u32[]{:S(2)}, u32[]{:S(2)}) collective-permute-start(bf16[64,8192]{1,0:T(8,128)(2,1)S(1)} %collective-permute-done.16), channel_id=1, source_target_pairs={{0,1},{1,0},{2,3},{3,2},{4,5},{5,4},{6,7},{7,6},{8,9},{9,8},{10,11... | collective-permute-start | bytes 3145736 | tf_op jit(solution)/shard_map/ppermute | solution.py:336
  207.2 9.4 %collective-permute-start.27 = (f32[8,128]{1,0:T(8,128)S(1)}, f32[8,128]{1,0:T(8,128)S(1)}, u32[]{:S(2)}, u32[]{:S(2)}) collective-permute-start(f32[8,128]{1,0:T(8,128)S(1)} %add_add_fusion.refs_2_), channel_id=1, source_target_pairs={{0,4},{1,5},{2,6},{3,7},{4,0},{5,1},{6,2},{7,3},{8,12},{9,13},{10,... | collective-permute-start | bytes 12296 | tf_op jit(solution)/shard_map/ppermute | solution.py:336
  212.8 5.4 %collective-permute-start.29 = (f32[8,128]{1,0:T(8,128)S(1)}, f32[8,128]{1,0:T(8,128)S(1)}, u32[]{:S(2)}, u32[]{:S(2)}) collective-permute-start(f32[8,128]{1,0:T(8,128)S(1)} %add_add_fusion.refs_2_), channel_id=1, source_target_pairs={{0,12},{1,13},{2,14},{3,15},{4,8},{5,9},{6,10},{7,11},{8,4},{9,5},... | collective-permute-start | bytes 12296 | tf_op jit(solution)/shard_map/ppermute | solution.py:336
  (18 other events, 157.2 us)

commit v17 on v15

--- a/solution.py
+++ b/solution.py
@@ -11,7 +11,7 @@
 INNER = (((1,), (0,)), ((), ()))
 HBM = pl.BlockSpec(memory_space=pltpu.HBM)
 WHOLE = pl.BlockSpec(memory_space=pltpu.VMEM)
-VMEM_BYTES = 16 * 2**20
+VMEM_BYTES = 12 * 2**20
 
 
 def dot32(a, b, dims=INNER):
@@ -198,19 +198,19 @@
     return upper == (lax.broadcasted_iota(jnp.int32, (rows, columns), 1) < first_columns)
 
 
-def far_sums(tokens, factor, up_ref, down_ref, dx_refs):
+def far_sums(tokens, factor, up_ref, down_ref, dx_ref, inner_ref=None):
     rank, width = up_ref.shape
     tile = min(width, 2048)
     cuts = [pl.ds(i * tile, tile) for i in range(width // tile)]
     hidden, inner = (sum(dot32(tokens(k, cut), factor(k, cut), ROWS_OF) for cut in cuts) for k in range(2))
     hidden_t, inner_t, inner = hidden.T.astype(BF16), inner.T.astype(BF16), inner.astype(BF16)
+    rows = inner.shape[0] - dx_ref.shape[0]
+    if inner_ref is not None:
+        inner_ref[...] = inner[:rows]
     for cut in cuts:
         up_ref[:, cut] = dot32(hidden_t, tokens(1, cut)).astype(BF16)
         down_ref[:, cut] = dot32(inner_t, tokens(0, cut)).astype(BF16)
-        dx = dot32(inner, factor(0, cut)).astype(BF16)
-        for n, ref in enumerate(dx_refs):
-            rows = ref.shape[0]
-            ref[:, cut] = dx[n * rows:(n + 1) * rows]
+        dx_ref[:, cut] = dot32(inner[rows:], factor(0, cut)).astype(BF16)
 
 
 def in_place(body, out_shapes, *arrays, flags=None):
@@ -230,7 +230,7 @@
 
     def body(flags_ref, rows3_ref, rows2_ref, crossed_ref, up_ref, down_ref, dx_ref, late_ref):
         far_sums(
-            lambda k, cut: rows2_ref[k, :, cut], lambda k, cut: crossed_ref[k, :, cut], up_ref, down_ref, (dx_ref,)
+            lambda k, cut: rows2_ref[k, :, cut], lambda k, cut: crossed_ref[k, :, cut], up_ref, down_ref, dx_ref
         )
         late_ref[...] = jnp.where(flags_ref[0] == 1, rows2_ref[...], rows3_ref[...])
 
@@ -242,25 +242,26 @@
     _, block, width = rows.shape
     rank = far.shape[1]
 
-    def body(flags_ref, rows_ref, handed_ref, outer_ref, far_ref, up_ref, down_ref, dx_ref, swap_ref):
+    def body(flags_ref, rows_ref, handed_ref, outer_ref, far_ref, up_ref, down_ref, inner_ref, swap_ref):
         at_end = flags_ref[0] == 1
         far_sums(
             lambda k, cut: jnp.concatenate([rows_ref[k, :, cut], handed_ref[k, :, cut]], axis=0),
             lambda k, cut: jnp.where(at_end, outer_ref[k, :, cut], far_ref[k, :, cut]),
             up_ref,
             down_ref,
-            (dx_ref, swap_ref),
+            swap_ref,
+            inner_ref,
         )
 
         @pl.when(at_end)
         def _():
             swap_ref[...] = down_ref[...]
 
-    shapes = [((rank, width), BF16)] * 2 + [((block, width), BF16)] * 2
+    shapes = [((rank, width), BF16)] * 2 + [((block, rank), BF16), ((block, width), BF16)]
     return in_place(body, shapes, rows, handed, outer, far, flags=flags)
 
 
-def near_groups(flags, stage, pair, down, up, dx_late, dx_early, swapped, capacity, first1):
+def near_groups(flags, stage, pair, down, up, outer, far, inner_late, dx_early, swapped, capacity, first1):
     plane = len(stage)
     rank, width = down.shape
     block = plane * capacity
@@ -269,8 +270,8 @@
 
     def body(flags_ref, *refs):
         stage_in, refs = refs[:plane], refs[plane:]
-        pair_in, down_in, up_in, late_ref, early_ref, swapped_ref = refs[:6]
-        dx_refs, sum_refs = refs[6:6 + plane], refs[6 + plane:]
+        pair_in, down_in, up_in, outer_in, far_in, late_ref, early_ref, swapped_ref = refs[:8]
+        dx_refs, sum_refs = refs[8:8 + plane], refs[8 + plane:]
         own_in = (down_in, up_in)
         at_end = flags_ref[0] == 1
 
@@ -297,14 +298,14 @@
                 sum_refs[k][:, cut] = both[:rank]
                 sum_refs[2 + k][:, cut] = both[rank:]
             dx = dot32(inner, factors(0, cut)).astype(BF16)
-            late = late_ref[:, cut]
+            late = dot32(late_ref[...], jnp.where(at_end, outer_in[0, :, cut], far_in[0, :, cut])).astype(BF16)
             moved = [jnp.where(at_end, swapped_ref[:, cut], late), jnp.where(at_end, late, early_ref[:, cut])]
             for n, dx in enumerate(moved + [dx[:block], dx[block:]]):
                 for m in range(plane):
                     dx_refs[m][n * capacity:(n + 1) * capacity, cut] = dx[m * capacity:(m + 1) * capacity]
 
     shapes = [((4 * capacity, width), BF16)] * plane + [((rank, width), F32)] * 4
-    return in_place(body, shapes, *stage, pair, down, up, dx_late, dx_early, swapped, flags=flags)
+    return in_place(body, shapes, *stage, pair, down, up, outer, far, inner_late, dx_early, swapped, flags=flags)
 
 
 def move_adapters(plane, acts, cotan, token_task_index, task_slot_lookup, pool_down_factors, pool_up_factors):
@@ -380,13 +381,13 @@
     far = send(pair, cross)
 
     up2, down2, dx_early, late_rows = early_group(end_flag, rows3, rows2, crossed)
-    up3, down3, dx_late, swapped = late_group(end_flag, late_rows, handed, far, outer)
+    up3, down3, inner_late, swapped = late_group(end_flag, late_rows, handed, far, outer)
     up2_in = send(up3, inward)
     down3, swapped, up3 = send(down3, cross), send(swapped, swap), send(up3, cross)
 
     swapped, down3 = lax.optimization_barrier((swapped, down3))
     dx_own, dx_beside, *dx_across, up1, down1, up0, down0 = near_groups(
-        end_flag, stage10, pair, down, up, dx_late, dx_early, swapped, capacity,
+        end_flag, stage10, pair, down, up, outer, far, inner_late, dx_early, swapped, capacity,
         (2 * capacity, 2 * capacity, 0, 0),
     )
 

time: 220 us -> 220 us (level)
  transfers between devices with their start and end apart: 30 -> 30, of which waited for: 13 -> 13; matrix products, arithmetic and copies ran while one was open for 3% -> 3% of each run, Pallas kernels for 12% -> 13%
where the time goes in v17:
time: 220 us
  waiting for transfers between devices  118 us (54%)
  starting transfers between devices  57.5 us (26%)
  Pallas kernels  30 us (14%)
  local copies, waits for them, and re-layouts  9.52 us (4%)
  other arithmetic  3.42 us (2%)
    ppermute x30, waiting for transfers between devices, send(): return lax.ppermute(array, 'dp', pairs)  118 us
    ppermute x30, starting transfers between devices, send(): return lax.ppermute(array, 'dp', pairs)  57.5 us
    pallas_call x5, Pallas kernels, in_place(): pl.pallas_call(body, in_specs=[pl.BlockSpec(memory_space=pltpu.SMEM)] * l...  16.6 us
    pallas_call x1, Pallas kernels, pack(): pl.pallas_call(body, grid=(tiles,), in_specs=[pl.BlockSpec(place.shape, l...  6.36 us
    pallas_call x2, Pallas kernels, unpack(): pl.pallas_call(body, grid=(width // 2 // tile,), in_specs=[pl.BlockSpec(p...  4.79 us
  transfers between devices with their start and end apart: 30, of which 13 were waited for; matrix products, arithmetic and copies ran while one was open for 3% of the time, Pallas kernels for 13%

profile of v17, /device:TPU:0, one launch (start us, length us, event | category | flops | bytes accessed | tf_op | source)
XLA Modules:
  0.0 219.9 jit_solution(16020547246537840089)
XLA Ops:
  0.7 2.4 %constant_dynamic-update-slice_fusion.1 = bf16[2,64,8192]{2,1,0:T(8,128)(2,1)} fusion(bf16[1,64,8192]{2,1,0:T(8,128)(2,1)} %param.10), kind=kLoop, calls=%fused_computation.22 | loop fusion | bytes 2097152
  6.1 4.6 %collective-permute-start.6 = (bf16[2,64,8192]{2,1,0:T(8,128)(2,1)}, bf16[2,64,8192]{2,1,0:T(8,128)(2,1)}, u32[]{:S(2)}, u32[]{:S(2)}) collective-permute-start(bf16[2,64,8192]{2,1,0:T(8,128)(2,1)} %constant_dynamic-update-slice_fusion), channel_id=1, source_target_pairs={{0,4},{1,5},{2,6},{3,7},{4,0},{5,1},{6,2},{7,3},{8,12},{9,13},{10,... | collective-permute-start | bytes 6291464 | tf_op jit(solution)/shard_map/ppermute | solution.py:329
  11.4 6.4 %shard_map.85 = (bf16[1,2,64,8192]{3,2,1,0:T(8,128)(2,1)S(1)}, bf16[1,2,64,8192]{3,2,1,0:T(8,128)(2,1)S(1)}, bf16[2,2,16,8192]{3,2,1,0:T(8,128)(2,1)S(1)}, bf16[...) custom-call(bf16[256,128]{1,0:T(8,128)(2,1)S(1)} %fusion.1.place_ref, bf16[128,8192]{1,0:T(8,128)(2,1)} %x_in.1, ...), custom_call_target="tpu_custom_call" | custom-call | tf_op jit(solution)/shard_map/pallas_call | solution.py:107
  20.2 22.0 %collective-permute-done.1 = bf16[2,2,16,8192]{3,2,1,0:T(8,128)(2,1)S(1)} collective-permute-done((bf16[2,2,16,8192]{3,2,1,0:T(8,128)(2,1)S(1)}, bf16[2,2,16,8192]{3,2,1,0:T(8,128)(2,1)S(1)}, u32[]{:S(2)}, u32[]{:S(2)}) %collective-permute-start.1) | collective-permute-done | bytes 1048608 | tf_op jit(solution)/shard_map/ppermute | solution.py:329
  45.9 3.6 %collective-permute-start.11 = (bf16[2,64,8192]{2,1,0:T(8,128)(2,1)S(1)}, bf16[2,64,8192]{2,1,0:T(8,128)(2,1)}, u32[]{:S(2)}, u32[]{:S(2)}) collective-permute-start(bf16[2,64,8192]{2,1,0:T(8,128)(2,1)S(1)} %pad_maximum_fusion.rows3_ref), channel_id=1, source_target_pairs={{0,4},{1,5},{2,6},{3,7},{12,8},{13,9},{14,10},{15,11},{16,20},{17,... | collective-permute-start | bytes 6291464 | tf_op jit(solution)/shard_map/ppermute | solution.py:329
  50.8 6.3 %collective-permute-done.6.refs_4_ = bf16[2,64,8192]{2,1,0:T(8,128)(2,1)} collective-permute-done((bf16[2,64,8192]{2,1,0:T(8,128)(2,1)}, bf16[2,64,8192]{2,1,0:T(8,128)(2,1)}, u32[]{:S(2)}, u32[]{:S(2)}) %collective-permute-start.6) | collective-permute-done | bytes 2097184 | tf_op jit(solution)/shard_map/ppermute | solution.py:329
  59.2 6.6 %collective-permute-done.2 = bf16[2,2,16,8192]{3,2,1,0:T(8,128)(2,1)S(1)} collective-permute-done((bf16[2,2,16,8192]{3,2,1,0:T(8,128)(2,1)S(1)}, bf16[2,2,16,8192]{3,2,1,0:T(8,128)(2,1)S(1)}, u32[]{:S(2)}, u32[]{:S(2)}) %collective-permute-start.2) | collective-permute-done | bytes 1048608 | tf_op jit(solution)/shard_map/ppermute | solution.py:329
  72.5 3.5 %shard_map.86 = (bf16[64,8192]{1,0:T(8,128)(2,1)S(1)}, bf16[64,8192]{1,0:T(8,128)(2,1)S(1)}, bf16[64,8192]{1,0:T(8,128)(2,1)S(1)}, bf16[2,64,8192]{2,1,0:T(8,128)(2,1)S(1)}) custom-call(s32[1]{0:T(128)} %bitcast.1.flags_ref, bf16[2,64,8192]{2,1,0:T(8,128)(2,1)S(1)} %pad_maximum_fusion.rows3_ref, bf16[2,64,8192]{2,1,0:T(8,128)(2,1)S(1)} %pad_maximum_fusion.1.rows2_ref, ...), custom_call_target="tpu_custom_call" | custom-call | tf_op jit(solution)/shard_map/pallas_call | solution.py:218
  76.0 24.5 %collective-permute-done.11.handed_ref = bf16[2,64,8192]{2,1,0:T(8,128)(2,1)} collective-permute-done((bf16[2,64,8192]{2,1,0:T(8,128)(2,1)S(1)}, bf16[2,64,8192]{2,1,0:T(8,128)(2,1)}, u32[]{:S(2)}, u32[]{:S(2)}) %collective-permute-start.11) | collective-permute-done | bytes 2097184 | tf_op jit(solution)/shard_map/ppermute | solution.py:329
  100.5 2.6 %collective-permute-done.8.outer_ref.refs_7_ = bf16[2,64,8192]{2,1,0:T(8,128)(2,1)} collective-permute-done((bf16[2,64,8192]{2,1,0:T(8,128)(2,1)}, bf16[2,64,8192]{2,1,0:T(8,128)(2,1)}, u32[]{:S(2)}, u32[]{:S(2)}) %collective-permute-start.8) | collective-permute-done | bytes 2097184 | tf_op jit(solution)/shard_map/ppermute | solution.py:329
  103.1 5.2 %shard_map.87 = (bf16[64,8192]{1,0:T(8,128)(2,1)S(1)}, bf16[64,8192]{1,0:T(8,128)(2,1)S(1)}, bf16[64,64]{1,0:T(8,128)(2,1)S(1)}, bf16[64,8192]{1,0:T(8,128)(2,1)S(1)}) custom-call(s32[1]{0:T(128)} %bitcast.1.flags_ref, bf16[2,64,8192]{2,1,0:T(8,128)(2,1)S(1)} %get-tuple-element.50.rows_ref, bf16[2,64,8192]{2,1,0:T(8,128)(2,1)} %collective-permute-done.11.handed_ref, ...), custom_call_target="tpu_custom_call" | custom-call | tf_op jit(solution)/shard_map/pallas_call | solution.py:218
  108.3 5.0 %collective-permute-start.12 = (bf16[64,8192]{1,0:T(8,128)(2,1)S(1)}, bf16[64,8192]{1,0:T(8,128)(2,1)S(1)}, u32[]{:S(2)}, u32[]{:S(2)}) collective-permute-start(bf16[64,8192]{1,0:T(8,128)(2,1)S(1)} %get-tuple-element.53), channel_id=1, source_target_pairs={{0,4},{1,5},{2,6},{3,7},{4,0},{5,1},{6,2},{7,3},{8,12},{9,13},{10,... | collective-permute-start | bytes 3145736 | tf_op jit(solution)/shard_map/ppermute | solution.py:329
  114.0 4.8 %collective-permute-start.20 = (bf16[64,8192]{1,0:T(8,128)(2,1)S(1)}, bf16[64,8192]{1,0:T(8,128)(2,1)S(1)}, u32[]{:S(2)}, u32[]{:S(2)}) collective-permute-start(bf16[64,8192]{1,0:T(8,128)(2,1)S(1)} %get-tuple-element.68), channel_id=1, source_target_pairs={{0,4},{1,5},{2,6},{3,7},{12,8},{13,9},{14,10},{15,11},{16,20},{17,... | collective-permute-start | bytes 3145736 | tf_op jit(solution)/shard_map/ppermute | solution.py:329
  121.1 15.8 %collective-permute-done.12.refs_11_ = bf16[64,8192]{1,0:T(8,128)(2,1)S(1)} collective-permute-done((bf16[64,8192]{1,0:T(8,128)(2,1)S(1)}, bf16[64,8192]{1,0:T(8,128)(2,1)S(1)}, u32[]{:S(2)}, u32[]{:S(2)}) %collective-permute-start.12) | collective-permute-done | bytes 1048608 | tf_op jit(solution)/shard_map/ppermute | solution.py:329
  137.9 6.8 %shard_map.88 = (bf16[64,8192]{1,0:T(8,128)(2,1)S(1)}, bf16[64,8192]{1,0:T(8,128)(2,1)S(1)}, bf16[64,8192]{1,0:T(8,128)(2,1)S(1)}, bf16[64,8192]{1,0:T(8,128)(2,...) custom-call(s32[1]{0:T(128)} %bitcast.1.flags_ref, ...), custom_call_target="tpu_custom_call" | custom-call | tf_op jit(solution)/shard_map/pallas_call | solution.py:218
  147.4 7.2 %collective-permute-start.19 = (bf16[64,8192]{1,0:T(8,128)(2,1)S(1)}, bf16[64,8192]{1,0:T(8,128)(2,1)S(1)}, u32[]{:S(2)}, u32[]{:S(2)}) collective-permute-start(bf16[64,8192]{1,0:T(8,128)(2,1)S(1)} %add_convert_fusion.2), channel_id=1, source_target_pairs={{0,4},{1,5},{2,6},{3,7},{4,0},{5,1},{6,2},{7,3},{8,12},{9,13},{10,... | collective-permute-start | bytes 3145736 | tf_op jit(solution)/shard_map/ppermute | solution.py:329
  154.6 14.4 %collective-permute-done.15.refs_2_ = bf16[64,8192]{1,0:T(8,128)(2,1)S(1)} collective-permute-done((bf16[64,8192]{1,0:T(8,128)(2,1)S(1)}, bf16[64,8192]{1,0:T(8,128)(2,1)S(1)}, u32[]{:S(2)}, u32[]{:S(2)}) %collective-permute-start.15) | collective-permute-done | bytes 1048608 | tf_op jit(solution)/shard_map/ppermute | solution.py:329
  170.8 7.2 %collective-permute-start.23 = (bf16[64,8192]{1,0:T(8,128)(2,1)S(1)}, bf16[64,8192]{1,0:T(8,128)(2,1)S(1)}, u32[]{:S(2)}, u32[]{:S(2)}) collective-permute-start(bf16[64,8192]{1,0:T(8,128)(2,1)S(1)} %add_convert_fusion), channel_id=1, source_target_pairs={{0,4},{1,5},{2,6},{3,7},{4,0},{5,1},{6,2},{7,3},{8,12},{9,13},{10,... | collective-permute-start | bytes 3145736 | tf_op jit(solution)/shard_map/ppermute | solution.py:329
  179.2 8.9 %collective-permute-done.16 = bf16[64,8192]{1,0:T(8,128)(2,1)S(1)} collective-permute-done((bf16[64,8192]{1,0:T(8,128)(2,1)S(1)}, bf16[64,8192]{1,0:T(8,128)(2,1)S(1)}, u32[]{:S(2)}, u32[]{:S(2)}) %collective-permute-start.16) | collective-permute-done | bytes 1048608 | tf_op jit(solution)/shard_map/ppermute | solution.py:329
  188.7 12.5 %collective-permute-done.23.refs_1_ = bf16[64,8192]{1,0:T(8,128)(2,1)S(1)} collective-permute-done((bf16[64,8192]{1,0:T(8,128)(2,1)S(1)}, bf16[64,8192]{1,0:T(8,128)(2,1)S(1)}, u32[]{:S(2)}, u32[]{:S(2)}) %collective-permute-start.23) | collective-permute-done | bytes 1048608 | tf_op jit(solution)/shard_map/ppermute | solution.py:329
  203.8 2.4 %shard_map.89.refs_4_ = bf16[128,8192]{1,0:T(8,128)(2,1)} custom-call(bf16[128,256]{1,0:T(8,128)(2,1)S(1)} %fusion.place_ref, bf16[64,8192]{1,0:T(8,128)(2,1)} %copy-done.6, bf16[64,8192]{1,0:T(8,128)(2,1)S(1)} %collective-permute-done.14.refs_1_, bf16[64,8192]{1,0:T(8,128)(2,1)S(1)} %collective-permute-done.15.refs_2_, ...), custom_call_target="tpu_custom_call" | custom-call | tf_op jit(solution)/shard_map/pallas_call | solution.py:128
  206.4 4.4 %collective-permute-start.27 = (f32[8,128]{1,0:T(8,128)S(1)}, f32[8,128]{1,0:T(8,128)S(1)}, u32[]{:S(2)}, u32[]{:S(2)}) collective-permute-start(f32[8,128]{1,0:T(8,128)S(1)} %add_add_fusion.refs_2_), channel_id=1, source_target_pairs={{0,4},{1,5},{2,6},{3,7},{4,0},{5,1},{6,2},{7,3},{8,12},{9,13},{10,... | collective-permute-start | bytes 12296 | tf_op jit(solution)/shard_map/ppermute | solution.py:329
  213.4 2.4 %shard_map.90 = bf16[128,8192]{1,0:T(8,128)(2,1)} custom-call(bf16[128,256]{1,0:T(8,128)(2,1)S(1)} %fusion.place_ref, bf16[64,8192]{1,0:T(8,128)(2,1)} %copy-done.6, bf16[64,8192]{1,0:T(8,128)(2,1)S(1)} %collective-permute-done.14.refs_1_, bf16[64,8192]{1,0:T(8,128)(2,1)S(1)} %collective-permute-done.15.refs_2_, ...), custom_call_target="tpu_custom_call", output_to_operand_aliasing={{}: (5, {})} | custom-call | tf_op jit(solution)/shard_map/pallas_call | solution.py:128
  217.5 2.3 %shard_map.93 = (f32[1,64,8192]{2,1,0:T(8,128)}, f32[1,64,8192]{2,1,0:T(8,128)}) custom-call(f32[64,8192]{1,0:T(8,128)S(1)} %get-tuple-element.65.refs_0_, f32[64,8192]{1,0:T(8,128)S(1)} %get-tuple-element.72.refs_1_, f32[8,128]{1,0:T(8,128)S(1)} %add_add_fusion.refs_2_, f32[8,128]{1,0:T(8,128)S(1)} %collective-permute-done.27.refs_3_, ...), custom_call_target="tpu_custom_call" | custom-call | tf_op jit(solution)/shard_map/pallas_call | solution.py:183
  (88 shorter events, 37.1 us)
Async XLA Ops:
  4.2 45.4 %collective-permute-start.7 = (bf16[2,64,8192]{2,1,0:T(8,128)(2,1)}, bf16[2,64,8192]{2,1,0:T(8,128)(2,1)}, u32[]{:S(2)}, u32[]{:S(2)}) collective-permute-start(bf16[2,64,8192]{2,1,0:T(8,128)(2,1)} %constant_dynamic-update-slice_fusion), channel_id=1, source_target_pairs={{4,8},{5,9},{6,10},{7,11},{8,4},{9,5},{10,6},{11,7},{20,24},{21,25... | collective-permute-start | bytes 6291464 | tf_op jit(solution)/shard_map/ppermute | solution.py:329
  6.1 51.0 %collective-permute-start.6 = (bf16[2,64,8192]{2,1,0:T(8,128)(2,1)}, bf16[2,64,8192]{2,1,0:T(8,128)(2,1)}, u32[]{:S(2)}, u32[]{:S(2)}) collective-permute-start(bf16[2,64,8192]{2,1,0:T(8,128)(2,1)} %constant_dynamic-update-slice_fusion), channel_id=1, source_target_pairs={{0,4},{1,5},{2,6},{3,7},{4,0},{5,1},{6,2},{7,3},{8,12},{9,13},{10,... | collective-permute-start | bytes 6291464 | tf_op jit(solution)/shard_map/ppermute | solution.py:329
  17.8 24.4 %collective-permute-start.1 = (bf16[2,2,16,8192]{3,2,1,0:T(8,128)(2,1)S(1)}, bf16[2,2,16,8192]{3,2,1,0:T(8,128)(2,1)S(1)}, u32[]{:S(2)}, u32[]{:S(2)}) collective-permute-start(bf16[2,2,16,8192]{3,2,1,0:T(8,128)(2,1)S(1)} %get-tuple-element.47), channel_id=1, source_target_pairs={{0,2},{1,3},{2,0},{3,1},{4,6},{5,7},{6,4},{7,5},{8,10},{9,11},{10,... | collective-permute-start | bytes 3145736 | tf_op jit(solution)/shard_map/ppermute | solution.py:329
  19.4 24.5 %collective-permute-start = (bf16[1,2,64,8192]{3,2,1,0:T(8,128)(2,1)S(1)}, bf16[1,2,64,8192]{3,2,1,0:T(8,128)(2,1)S(1)}, u32[]{:S(2)}, u32[]{:S(2)}) collective-permute-start(bf16[1,2,64,8192]{3,2,1,0:T(8,128)(2,1)S(1)} %get-tuple-element.44), channel_id=1, source_target_pairs={{0,1},{1,0},{2,3},{3,2},{4,5},{5,4},{6,7},{7,6},{8,9},{9,8},{10,11... | collective-permute-start | bytes 6291464 | tf_op jit(solution)/shard_map/ppermute | solution.py:329
  42.2 23.5 %collective-permute-start.2 = (bf16[2,2,16,8192]{3,2,1,0:T(8,128)(2,1)S(1)}, bf16[2,2,16,8192]{3,2,1,0:T(8,128)(2,1)S(1)}, u32[]{:S(2)}, u32[]{:S(2)}) collective-permute-start(bf16[2,2,16,8192]{3,2,1,0:T(8,128)(2,1)S(1)} %get-tuple-element.48), channel_id=1, source_target_pairs={{0,2},{1,3},{2,0},{3,1},{4,6},{5,7},{6,4},{7,5},{8,10},{9,11},{10,... | collective-permute-start | bytes 3145736 | tf_op jit(solution)/shard_map/ppermute | solution.py:329
  45.9 54.6 %collective-permute-start.11 = (bf16[2,64,8192]{2,1,0:T(8,128)(2,1)S(1)}, bf16[2,64,8192]{2,1,0:T(8,128)(2,1)}, u32[]{:S(2)}, u32[]{:S(2)}) collective-permute-start(bf16[2,64,8192]{2,1,0:T(8,128)(2,1)S(1)} %pad_maximum_fusion.rows3_ref), channel_id=1, source_target_pairs={{0,4},{1,5},{2,6},{3,7},{12,8},{13,9},{14,10},{15,11},{16,20},{17,... | collective-permute-start | bytes 6291464 | tf_op jit(solution)/shard_map/ppermute | solution.py:329
  49.5 53.6 %collective-permute-start.8 = (bf16[2,64,8192]{2,1,0:T(8,128)(2,1)}, bf16[2,64,8192]{2,1,0:T(8,128)(2,1)}, u32[]{:S(2)}, u32[]{:S(2)}) collective-permute-start(bf16[2,64,8192]{2,1,0:T(8,128)(2,1)} %collective-permute-done.7.crossed_ref), channel_id=1, source_target_pairs={{4,0},{5,1},{6,2},{7,3},{8,12},{9,13},{10,14},{11,15},{20,16},{21,... | collective-permute-start | bytes 6291464 | tf_op jit(solution)/shard_map/ppermute | solution.py:329
  57.1 46.0 %collective-permute-start.9 = (bf16[2,64,8192]{2,1,0:T(8,128)(2,1)}, bf16[2,64,8192]{2,1,0:T(8,128)(2,1)}, u32[]{:S(2)}, u32[]{:S(2)}) collective-permute-start(bf16[2,64,8192]{2,1,0:T(8,128)(2,1)} %collective-permute-done.6.refs_4_), channel_id=1, source_target_pairs={{4,8},{5,9},{6,10},{7,11},{8,4},{9,5},{10,6},{11,7},{20,24},{21,25... | collective-permute-start | bytes 6291464 | tf_op jit(solution)/shard_map/ppermute | solution.py:329
  69.3 50.2 %collective-permute-start.4 = (bf16[2,2,32,8192]{3,2,1,0:T(8,128)(2,1)}, bf16[2,2,32,8192]{3,2,1,0:T(8,128)(2,1)}, u32[]{:S(2)}, u32[]{:S(2)}) collective-permute-start(bf16[2,2,32,8192]{3,2,1,0:T(8,128)(2,1)} %get-tuple-element.49), channel_id=1, source_target_pairs={{0,2},{1,3},{2,0},{3,1},{4,6},{5,7},{6,4},{7,5},{8,10},{9,11},{10,... | collective-permute-start | bytes 6291464 | tf_op jit(solution)/shard_map/ppermute | solution.py:329
  108.3 28.7 %collective-permute-start.12 = (bf16[64,8192]{1,0:T(8,128)(2,1)S(1)}, bf16[64,8192]{1,0:T(8,128)(2,1)S(1)}, u32[]{:S(2)}, u32[]{:S(2)}) collective-permute-start(bf16[64,8192]{1,0:T(8,128)(2,1)S(1)} %get-tuple-element.53), channel_id=1, source_target_pairs={{0,4},{1,5},{2,6},{3,7},{4,0},{5,1},{6,2},{7,3},{8,12},{9,13},{10,... | collective-permute-start | bytes 3145736 | tf_op jit(solution)/shard_map/ppermute | solution.py:329
  113.3 23.6 %collective-permute-start.13 = (bf16[64,8192]{1,0:T(8,128)(2,1)S(1)}, bf16[64,8192]{1,0:T(8,128)(2,1)S(1)}, u32[]{:S(2)}, u32[]{:S(2)}) collective-permute-start(bf16[64,8192]{1,0:T(8,128)(2,1)S(1)} %get-tuple-element.54), channel_id=1, source_target_pairs={{4,8},{5,9},{6,10},{7,11},{8,4},{9,5},{10,6},{11,7},{20,24},{21,25... | collective-permute-start | bytes 3145736 | tf_op jit(solution)/shard_map/ppermute | solution.py:329
  114.0 56.6 %collective-permute-start.20 = (bf16[64,8192]{1,0:T(8,128)(2,1)S(1)}, bf16[64,8192]{1,0:T(8,128)(2,1)S(1)}, u32[]{:S(2)}, u32[]{:S(2)}) collective-permute-start(bf16[64,8192]{1,0:T(8,128)(2,1)S(1)} %get-tuple-element.68), channel_id=1, source_target_pairs={{0,4},{1,5},{2,6},{3,7},{12,8},{13,9},{14,10},{15,11},{16,20},{17,... | collective-permute-start | bytes 3145736 | tf_op jit(solution)/shard_map/ppermute | solution.py:329
  118.8 51.8 %collective-permute-start.21 = (bf16[64,8192]{1,0:T(8,128)(2,1)S(1)}, bf16[64,8192]{1,0:T(8,128)(2,1)S(1)}, u32[]{:S(2)}, u32[]{:S(2)}) collective-permute-start(bf16[64,8192]{1,0:T(8,128)(2,1)S(1)} %get-tuple-element.68), channel_id=1, source_target_pairs={{4,8},{5,9},{6,10},{7,11},{8,4},{9,5},{10,6},{11,7},{20,24},{21,25... | collective-permute-start | bytes 3145736 | tf_op jit(solution)/shard_map/ppermute | solution.py:329
  121.0 16.9 %collective-permute-start.5 = (bf16[1,2,32,8192]{3,2,1,0:T(8,128)(2,1)S(1)}, bf16[1,2,32,8192]{3,2,1,0:T(8,128)(2,1)S(1)}, u32[]{:S(2)}, u32[]{:S(2)}) collective-permute-start(bf16[1,2,32,8192]{3,2,1,0:T(8,128)(2,1)S(1)} %slice.37), channel_id=1, source_target_pairs={{0,1},{1,0},{2,3},{3,2},{4,5},{5,4},{6,7},{7,6},{8,9},{9,8},{10,11... | collective-permute-start | bytes 3145736 | tf_op jit(solution)/shard_map/ppermute | solution.py:329
  137.2 42.0 %collective-permute-start.18 = (bf16[64,8192]{1,0:T(8,128)(2,1)S(1)}, bf16[64,8192]{1,0:T(8,128)(2,1)S(1)}, u32[]{:S(2)}, u32[]{:S(2)}) collective-permute-start(bf16[64,8192]{1,0:T(8,128)(2,1)S(1)} %add_convert_fusion.3), channel_id=1, source_target_pairs={{4,8},{5,9},{6,10},{7,11},{8,4},{9,5},{10,6},{11,7},{20,24},{21,25... | collective-permute-start | bytes 3145736 | tf_op jit(solution)/shard_map/ppermute | solution.py:329
  145.8 23.3 %collective-permute-start.15 = (bf16[64,8192]{1,0:T(8,128)(2,1)S(1)}, bf16[64,8192]{1,0:T(8,128)(2,1)S(1)}, u32[]{:S(2)}, u32[]{:S(2)}) collective-permute-start(bf16[64,8192]{1,0:T(8,128)(2,1)S(1)} %get-tuple-element.58), channel_id=1, source_target_pairs={{0,2},{1,3},{2,0},{3,1},{4,6},{5,7},{6,4},{7,5},{8,10},{9,11},{10,... | collective-permute-start | bytes 3145736 | tf_op jit(solution)/shard_map/ppermute | solution.py:329
  147.4 40.7 %collective-permute-start.19 = (bf16[64,8192]{1,0:T(8,128)(2,1)S(1)}, bf16[64,8192]{1,0:T(8,128)(2,1)S(1)}, u32[]{:S(2)}, u32[]{:S(2)}) collective-permute-start(bf16[64,8192]{1,0:T(8,128)(2,1)S(1)} %add_convert_fusion.2), channel_id=1, source_target_pairs={{0,4},{1,5},{2,6},{3,7},{4,0},{5,1},{6,2},{7,3},{8,12},{9,13},{10,... | collective-permute-start | bytes 3145736 | tf_op jit(solution)/shard_map/ppermute | solution.py:329
  169.1 19.0 %collective-permute-start.16 = (bf16[64,8192]{1,0:T(8,128)(2,1)S(1)}, bf16[64,8192]{1,0:T(8,128)(2,1)S(1)}, u32[]{:S(2)}, u32[]{:S(2)}) collective-permute-start(bf16[64,8192]{1,0:T(8,128)(2,1)S(1)} %get-tuple-element.60), channel_id=1, source_target_pairs={{0,2},{1,3},{2,0},{3,1},{4,6},{5,7},{6,4},{7,5},{8,10},{9,11},{10,... | collective-permute-start | bytes 3145736 | tf_op jit(solution)/shard_map/ppermute | solution.py:329
  170.8 30.4 %collective-permute-start.23 = (bf16[64,8192]{1,0:T(8,128)(2,1)S(1)}, bf16[64,8192]{1,0:T(8,128)(2,1)S(1)}, u32[]{:S(2)}, u32[]{:S(2)}) collective-permute-start(bf16[64,8192]{1,0:T(8,128)(2,1)S(1)} %add_convert_fusion), channel_id=1, source_target_pairs={{0,4},{1,5},{2,6},{3,7},{4,0},{5,1},{6,2},{7,3},{8,12},{9,13},{10,... | collective-permute-start | bytes 3145736 | tf_op jit(solution)/shard_map/ppermute | solution.py:329
  178.2 22.9 %collective-permute-start.22 = (bf16[64,8192]{1,0:T(8,128)(2,1)S(1)}, bf16[64,8192]{1,0:T(8,128)(2,1)S(1)}, u32[]{:S(2)}, u32[]{:S(2)}) collective-permute-start(bf16[64,8192]{1,0:T(8,128)(2,1)S(1)} %add_convert_fusion.1), channel_id=1, source_target_pairs={{4,8},{5,9},{6,10},{7,11},{8,4},{9,5},{10,6},{11,7},{20,24},{21,25... | collective-permute-start | bytes 3145736 | tf_op jit(solution)/shard_map/ppermute | solution.py:329
  179.2 24.6 %collective-permute-start.14 = (bf16[64,8192]{1,0:T(8,128)(2,1)S(1)}, bf16[64,8192]{1,0:T(8,128)(2,1)S(1)}, u32[]{:S(2)}, u32[]{:S(2)}) collective-permute-start(bf16[64,8192]{1,0:T(8,128)(2,1)S(1)} %get-tuple-element.57), channel_id=1, source_target_pairs={{0,1},{1,0},{2,3},{3,2},{4,5},{5,4},{6,7},{7,6},{8,9},{9,8},{10,11... | collective-permute-start | bytes 3145736 | tf_op jit(solution)/shard_map/ppermute | solution.py:329
  188.1 15.7 %collective-permute-start.17 = (bf16[64,8192]{1,0:T(8,128)(2,1)S(1)}, bf16[64,8192]{1,0:T(8,128)(2,1)S(1)}, u32[]{:S(2)}, u32[]{:S(2)}) collective-permute-start(bf16[64,8192]{1,0:T(8,128)(2,1)S(1)} %collective-permute-done.16), channel_id=1, source_target_pairs={{0,1},{1,0},{2,3},{3,2},{4,5},{5,4},{6,7},{7,6},{8,9},{9,8},{10,11... | collective-permute-start | bytes 3145736 | tf_op jit(solution)/shard_map/ppermute | solution.py:329
  206.4 9.4 %collective-permute-start.27 = (f32[8,128]{1,0:T(8,128)S(1)}, f32[8,128]{1,0:T(8,128)S(1)}, u32[]{:S(2)}, u32[]{:S(2)}) collective-permute-start(f32[8,128]{1,0:T(8,128)S(1)} %add_add_fusion.refs_2_), channel_id=1, source_target_pairs={{0,4},{1,5},{2,6},{3,7},{4,0},{5,1},{6,2},{7,3},{8,12},{9,13},{10,... | collective-permute-start | bytes 12296 | tf_op jit(solution)/shard_map/ppermute | solution.py:329
  212.0 5.4 %collective-permute-start.29 = (f32[8,128]{1,0:T(8,128)S(1)}, f32[8,128]{1,0:T(8,128)S(1)}, u32[]{:S(2)}, u32[]{:S(2)}) collective-permute-start(f32[8,128]{1,0:T(8,128)S(1)} %add_add_fusion.refs_2_), channel_id=1, source_target_pairs={{0,12},{1,13},{2,14},{3,15},{4,8},{5,9},{6,10},{7,11},{8,4},{9,5},... | collective-permute-start | bytes 12296 | tf_op jit(solution)/shard_map/ppermute | solution.py:329
  (16 other events, 125.2 us)

commit v18 on v17

--- a/solution.py
+++ b/solution.py
@@ -335,7 +335,11 @@
         return [(i, (i // plane) * plane + ((i % plane) ^ m)) for i in range(ndevices)]
 
     down, up = pool_down_factors[0], pool_up_factors[0]
-    own = jnp.concatenate([pool_down_factors, pool_up_factors])
+    lowest, none = jnp.array(-jnp.inf, BF16), (0, 0, 0)
+    own = jnp.maximum(
+        lax.pad(pool_down_factors, lowest, ((0, 1, 0), none, none)),
+        lax.pad(pool_up_factors, lowest, ((1, 0, 0), none, none)),
+    )
     pair = send(own, swap)
     crossed = send(own, cross)
 

time: 220 us -> 220 us (level)
  local copies, waits for them, and re-layouts: 9.52 us -> 4.35 us
  other arithmetic: 3.42 us -> 6.21 us
    max x0 -> x1, other arithmetic: none -> 3.15 us  [move_adapters(): jnp.maximum(lax.pad(pool_down_factors, lowest, ((0, 1, 0), none, none)),...]
    unnamed x21 -> x20, local copies, waits for them, and re-layouts: 4.16 us -> 1.82 us
where the time goes in v18:
time: 220 us
  waiting for transfers between devices  120 us (55%)
  starting transfers between devices  57.5 us (26%)
  Pallas kernels  30.2 us (14%)
  other arithmetic  6.21 us (3%)
  local copies, waits for them, and re-layouts  4.35 us (2%)
    ppermute x30, waiting for transfers between devices, send(): return lax.ppermute(array, 'dp', pairs)  120 us
    ppermute x30, starting transfers between devices, send(): return lax.ppermute(array, 'dp', pairs)  57.5 us
    pallas_call x5, Pallas kernels, in_place(): pl.pallas_call(body, in_specs=[pl.BlockSpec(memory_space=pltpu.SMEM)] * l...  16.7 us
    pallas_call x1, Pallas kernels, pack(): pl.pallas_call(body, grid=(tiles,), in_specs=[pl.BlockSpec(place.shape, l...  6.36 us
    pallas_call x2, Pallas kernels, unpack(): pl.pallas_call(body, grid=(width // 2 // tile,), in_specs=[pl.BlockSpec(p...  4.79 us
  transfers between devices with their start and end apart: 30, of which 13 were waited for; matrix products, arithmetic and copies ran while one was open for 3% of the time, Pallas kernels for 13%

profile of v18, /device:TPU:0, one launch (start us, length us, event | category | flops | bytes accessed | tf_op | source)
XLA Modules:
  0.0 219.6 jit_solution(8184145074862039757)
XLA Ops:
  0.7 3.1 %pad_maximum_fusion.2 = bf16[2,64,8192]{2,1,0:T(8,128)(2,1)} fusion(bf16[1,64,8192]{2,1,0:T(8,128)(2,1)} %param.11, bf16[1,64,8192]{2,1,0:T(8,128)(2,1)} %param.10), kind=kLoop, calls=%fused_computation.6 | loop fusion | flops 1048576 | bytes 4194304 | tf_op jit(solution)/shard_map/max | solution.py:339
  5.8 4.6 %collective-permute-start.6 = (bf16[2,64,8192]{2,1,0:T(8,128)(2,1)}, bf16[2,64,8192]{2,1,0:T(8,128)(2,1)}, u32[]{:S(2)}, u32[]{:S(2)}) collective-permute-start(bf16[2,64,8192]{2,1,0:T(8,128)(2,1)} %pad_maximum_fusion.2), channel_id=1, source_target_pairs={{0,4},{1,5},{2,6},{3,7},{4,0},{5,1},{6,2},{7,3},{8,12},{9,13},{10,... | collective-permute-start | bytes 6291464 | tf_op jit(solution)/shard_map/ppermute | solution.py:329
  11.1 6.4 %shard_map.85 = (bf16[1,2,64,8192]{3,2,1,0:T(8,128)(2,1)S(1)}, bf16[1,2,64,8192]{3,2,1,0:T(8,128)(2,1)S(1)}, bf16[2,2,16,8192]{3,2,1,0:T(8,128)(2,1)S(1)}, bf16[...) custom-call(bf16[256,128]{1,0:T(8,128)(2,1)S(1)} %fusion.1.place_ref, bf16[128,8192]{1,0:T(8,128)(2,1)} %x_in.1, ...), custom_call_target="tpu_custom_call" | custom-call | tf_op jit(solution)/shard_map/pallas_call | solution.py:107
  19.1 22.8 %collective-permute-done.1 = bf16[2,2,16,8192]{3,2,1,0:T(8,128)(2,1)S(1)} collective-permute-done((bf16[2,2,16,8192]{3,2,1,0:T(8,128)(2,1)S(1)}, bf16[2,2,16,8192]{3,2,1,0:T(8,128)(2,1)S(1)}, u32[]{:S(2)}, u32[]{:S(2)}) %collective-permute-start.1) | collective-permute-done | bytes 1048608 | tf_op jit(solution)/shard_map/ppermute | solution.py:329
  45.6 3.6 %collective-permute-start.11 = (bf16[2,64,8192]{2,1,0:T(8,128)(2,1)S(1)}, bf16[2,64,8192]{2,1,0:T(8,128)(2,1)}, u32[]{:S(2)}, u32[]{:S(2)}) collective-permute-start(bf16[2,64,8192]{2,1,0:T(8,128)(2,1)S(1)} %pad_maximum_fusion.rows3_ref), channel_id=1, source_target_pairs={{0,4},{1,5},{2,6},{3,7},{12,8},{13,9},{14,10},{15,11},{16,20},{17,... | collective-permute-start | bytes 6291464 | tf_op jit(solution)/shard_map/ppermute | solution.py:329
  50.4 6.3 %collective-permute-done.6.refs_4_ = bf16[2,64,8192]{2,1,0:T(8,128)(2,1)} collective-permute-done((bf16[2,64,8192]{2,1,0:T(8,128)(2,1)}, bf16[2,64,8192]{2,1,0:T(8,128)(2,1)}, u32[]{:S(2)}, u32[]{:S(2)}) %collective-permute-start.6) | collective-permute-done | bytes 2097184 | tf_op jit(solution)/shard_map/ppermute | solution.py:329
  58.8 6.6 %collective-permute-done.2 = bf16[2,2,16,8192]{3,2,1,0:T(8,128)(2,1)S(1)} collective-permute-done((bf16[2,2,16,8192]{3,2,1,0:T(8,128)(2,1)S(1)}, bf16[2,2,16,8192]{3,2,1,0:T(8,128)(2,1)S(1)}, u32[]{:S(2)}, u32[]{:S(2)}) %collective-permute-start.2) | collective-permute-done | bytes 1048608 | tf_op jit(solution)/shard_map/ppermute | solution.py:329
  71.8 3.6 %shard_map.86 = (bf16[64,8192]{1,0:T(8,128)(2,1)S(1)}, bf16[64,8192]{1,0:T(8,128)(2,1)S(1)}, bf16[64,8192]{1,0:T(8,128)(2,1)S(1)}, bf16[2,64,8192]{2,1,0:T(8,128)(2,1)S(1)}) custom-call(s32[1]{0:T(128)} %bitcast.1.flags_ref, bf16[2,64,8192]{2,1,0:T(8,128)(2,1)S(1)} %pad_maximum_fusion.rows3_ref, bf16[2,64,8192]{2,1,0:T(8,128)(2,1)S(1)} %pad_maximum_fusion.1.rows2_ref, ...), custom_call_target="tpu_custom_call" | custom-call | tf_op jit(solution)/shard_map/pallas_call | solution.py:218
  75.4 24.7 %collective-permute-done.11.handed_ref = bf16[2,64,8192]{2,1,0:T(8,128)(2,1)} collective-permute-done((bf16[2,64,8192]{2,1,0:T(8,128)(2,1)S(1)}, bf16[2,64,8192]{2,1,0:T(8,128)(2,1)}, u32[]{:S(2)}, u32[]{:S(2)}) %collective-permute-start.11) | collective-permute-done | bytes 2097184 | tf_op jit(solution)/shard_map/ppermute | solution.py:329
  100.1 2.6 %collective-permute-done.8.outer_ref.refs_7_ = bf16[2,64,8192]{2,1,0:T(8,128)(2,1)} collective-permute-done((bf16[2,64,8192]{2,1,0:T(8,128)(2,1)}, bf16[2,64,8192]{2,1,0:T(8,128)(2,1)}, u32[]{:S(2)}, u32[]{:S(2)}) %collective-permute-start.8) | collective-permute-done | bytes 2097184 | tf_op jit(solution)/shard_map/ppermute | solution.py:329
  102.7 5.2 %shard_map.87 = (bf16[64,8192]{1,0:T(8,128)(2,1)S(1)}, bf16[64,8192]{1,0:T(8,128)(2,1)S(1)}, bf16[64,64]{1,0:T(8,128)(2,1)S(1)}, bf16[64,8192]{1,0:T(8,128)(2,1)S(1)}) custom-call(s32[1]{0:T(128)} %bitcast.1.flags_ref, bf16[2,64,8192]{2,1,0:T(8,128)(2,1)S(1)} %get-tuple-element.50.rows_ref, bf16[2,64,8192]{2,1,0:T(8,128)(2,1)} %collective-permute-done.11.handed_ref, ...), custom_call_target="tpu_custom_call" | custom-call | tf_op jit(solution)/shard_map/pallas_call | solution.py:218
  108.0 5.0 %collective-permute-start.12 = (bf16[64,8192]{1,0:T(8,128)(2,1)S(1)}, bf16[64,8192]{1,0:T(8,128)(2,1)S(1)}, u32[]{:S(2)}, u32[]{:S(2)}) collective-permute-start(bf16[64,8192]{1,0:T(8,128)(2,1)S(1)} %get-tuple-element.53), channel_id=1, source_target_pairs={{0,4},{1,5},{2,6},{3,7},{4,0},{5,1},{6,2},{7,3},{8,12},{9,13},{10,... | collective-permute-start | bytes 3145736 | tf_op jit(solution)/shard_map/ppermute | solution.py:329
  113.8 4.8 %collective-permute-start.20 = (bf16[64,8192]{1,0:T(8,128)(2,1)S(1)}, bf16[64,8192]{1,0:T(8,128)(2,1)S(1)}, u32[]{:S(2)}, u32[]{:S(2)}) collective-permute-start(bf16[64,8192]{1,0:T(8,128)(2,1)S(1)} %get-tuple-element.68), channel_id=1, source_target_pairs={{0,4},{1,5},{2,6},{3,7},{12,8},{13,9},{14,10},{15,11},{16,20},{17,... | collective-permute-start | bytes 3145736 | tf_op jit(solution)/shard_map/ppermute | solution.py:329
  120.8 15.8 %collective-permute-done.12.refs_11_ = bf16[64,8192]{1,0:T(8,128)(2,1)S(1)} collective-permute-done((bf16[64,8192]{1,0:T(8,128)(2,1)S(1)}, bf16[64,8192]{1,0:T(8,128)(2,1)S(1)}, u32[]{:S(2)}, u32[]{:S(2)}) %collective-permute-start.12) | collective-permute-done | bytes 1048608 | tf_op jit(solution)/shard_map/ppermute | solution.py:329
  137.7 6.8 %shard_map.88 = (bf16[64,8192]{1,0:T(8,128)(2,1)S(1)}, bf16[64,8192]{1,0:T(8,128)(2,1)S(1)}, bf16[64,8192]{1,0:T(8,128)(2,1)S(1)}, bf16[64,8192]{1,0:T(8,128)(2,...) custom-call(s32[1]{0:T(128)} %bitcast.1.flags_ref, ...), custom_call_target="tpu_custom_call" | custom-call | tf_op jit(solution)/shard_map/pallas_call | solution.py:218
  147.2 7.2 %collective-permute-start.19 = (bf16[64,8192]{1,0:T(8,128)(2,1)S(1)}, bf16[64,8192]{1,0:T(8,128)(2,1)S(1)}, u32[]{:S(2)}, u32[]{:S(2)}) collective-permute-start(bf16[64,8192]{1,0:T(8,128)(2,1)S(1)} %add_convert_fusion.2), channel_id=1, source_target_pairs={{0,4},{1,5},{2,6},{3,7},{4,0},{5,1},{6,2},{7,3},{8,12},{9,13},{10,... | collective-permute-start | bytes 3145736 | tf_op jit(solution)/shard_map/ppermute | solution.py:329
  154.4 14.4 %collective-permute-done.15.refs_2_ = bf16[64,8192]{1,0:T(8,128)(2,1)S(1)} collective-permute-done((bf16[64,8192]{1,0:T(8,128)(2,1)S(1)}, bf16[64,8192]{1,0:T(8,128)(2,1)S(1)}, u32[]{:S(2)}, u32[]{:S(2)}) %collective-permute-start.15) | collective-permute-done | bytes 1048608 | tf_op jit(solution)/shard_map/ppermute | solution.py:329
  170.5 7.2 %collective-permute-start.23 = (bf16[64,8192]{1,0:T(8,128)(2,1)S(1)}, bf16[64,8192]{1,0:T(8,128)(2,1)S(1)}, u32[]{:S(2)}, u32[]{:S(2)}) collective-permute-start(bf16[64,8192]{1,0:T(8,128)(2,1)S(1)} %add_convert_fusion), channel_id=1, source_target_pairs={{0,4},{1,5},{2,6},{3,7},{4,0},{5,1},{6,2},{7,3},{8,12},{9,13},{10,... | collective-permute-start | bytes 3145736 | tf_op jit(solution)/shard_map/ppermute | solution.py:329
  179.0 8.9 %collective-permute-done.16 = bf16[64,8192]{1,0:T(8,128)(2,1)S(1)} collective-permute-done((bf16[64,8192]{1,0:T(8,128)(2,1)S(1)}, bf16[64,8192]{1,0:T(8,128)(2,1)S(1)}, u32[]{:S(2)}, u32[]{:S(2)}) %collective-permute-start.16) | collective-permute-done | bytes 1048608 | tf_op jit(solution)/shard_map/ppermute | solution.py:329
  188.4 12.5 %collective-permute-done.23.refs_1_ = bf16[64,8192]{1,0:T(8,128)(2,1)S(1)} collective-permute-done((bf16[64,8192]{1,0:T(8,128)(2,1)S(1)}, bf16[64,8192]{1,0:T(8,128)(2,1)S(1)}, u32[]{:S(2)}, u32[]{:S(2)}) %collective-permute-start.23) | collective-permute-done | bytes 1048608 | tf_op jit(solution)/shard_map/ppermute | solution.py:329
  203.5 2.4 %shard_map.89.refs_4_ = bf16[128,8192]{1,0:T(8,128)(2,1)} custom-call(bf16[128,256]{1,0:T(8,128)(2,1)S(1)} %fusion.place_ref, bf16[64,8192]{1,0:T(8,128)(2,1)} %copy-done.6, bf16[64,8192]{1,0:T(8,128)(2,1)S(1)} %collective-permute-done.14.refs_1_, bf16[64,8192]{1,0:T(8,128)(2,1)S(1)} %collective-permute-done.15.refs_2_, ...), custom_call_target="tpu_custom_call" | custom-call | tf_op jit(solution)/shard_map/pallas_call | solution.py:128
  206.1 4.4 %collective-permute-start.27 = (f32[8,128]{1,0:T(8,128)S(1)}, f32[8,128]{1,0:T(8,128)S(1)}, u32[]{:S(2)}, u32[]{:S(2)}) collective-permute-start(f32[8,128]{1,0:T(8,128)S(1)} %add_add_fusion.refs_2_), channel_id=1, source_target_pairs={{0,4},{1,5},{2,6},{3,7},{4,0},{5,1},{6,2},{7,3},{8,12},{9,13},{10,... | collective-permute-start | bytes 12296 | tf_op jit(solution)/shard_map/ppermute | solution.py:329
  213.2 2.4 %shard_map.90 = bf16[128,8192]{1,0:T(8,128)(2,1)} custom-call(bf16[128,256]{1,0:T(8,128)(2,1)S(1)} %fusion.place_ref, bf16[64,8192]{1,0:T(8,128)(2,1)} %copy-done.6, bf16[64,8192]{1,0:T(8,128)(2,1)S(1)} %collective-permute-done.14.refs_1_, bf16[64,8192]{1,0:T(8,128)(2,1)S(1)} %collective-permute-done.15.refs_2_, ...), custom_call_target="tpu_custom_call", output_to_operand_aliasing={{}: (5, {})} | custom-call | tf_op jit(solution)/shard_map/pallas_call | solution.py:128
  217.2 2.3 %shard_map.93 = (f32[1,64,8192]{2,1,0:T(8,128)}, f32[1,64,8192]{2,1,0:T(8,128)}) custom-call(f32[64,8192]{1,0:T(8,128)S(1)} %get-tuple-element.65.refs_0_, f32[64,8192]{1,0:T(8,128)S(1)} %get-tuple-element.72.refs_1_, f32[8,128]{1,0:T(8,128)S(1)} %add_add_fusion.refs_2_, f32[8,128]{1,0:T(8,128)S(1)} %collective-permute-done.27.refs_3_, ...), custom_call_target="tpu_custom_call" | custom-call | tf_op jit(solution)/shard_map/pallas_call | solution.py:183
  (87 shorter events, 34.8 us)
Async XLA Ops:
  3.8 45.4 %collective-permute-start.7 = (bf16[2,64,8192]{2,1,0:T(8,128)(2,1)}, bf16[2,64,8192]{2,1,0:T(8,128)(2,1)}, u32[]{:S(2)}, u32[]{:S(2)}) collective-permute-start(bf16[2,64,8192]{2,1,0:T(8,128)(2,1)} %pad_maximum_fusion.2), channel_id=1, source_target_pairs={{4,8},{5,9},{6,10},{7,11},{8,4},{9,5},{10,6},{11,7},{20,24},{21,25... | collective-permute-start | bytes 6291464 | tf_op jit(solution)/shard_map/ppermute | solution.py:329
  5.8 51.0 %collective-permute-start.6 = (bf16[2,64,8192]{2,1,0:T(8,128)(2,1)}, bf16[2,64,8192]{2,1,0:T(8,128)(2,1)}, u32[]{:S(2)}, u32[]{:S(2)}) collective-permute-start(bf16[2,64,8192]{2,1,0:T(8,128)(2,1)} %pad_maximum_fusion.2), channel_id=1, source_target_pairs={{0,4},{1,5},{2,6},{3,7},{4,0},{5,1},{6,2},{7,3},{8,12},{9,13},{10,... | collective-permute-start | bytes 6291464 | tf_op jit(solution)/shard_map/ppermute | solution.py:329
  17.4 24.4 %collective-permute-start.1 = (bf16[2,2,16,8192]{3,2,1,0:T(8,128)(2,1)S(1)}, bf16[2,2,16,8192]{3,2,1,0:T(8,128)(2,1)S(1)}, u32[]{:S(2)}, u32[]{:S(2)}) collective-permute-start(bf16[2,2,16,8192]{3,2,1,0:T(8,128)(2,1)S(1)} %get-tuple-element.47), channel_id=1, source_target_pairs={{0,2},{1,3},{2,0},{3,1},{4,6},{5,7},{6,4},{7,5},{8,10},{9,11},{10,... | collective-permute-start | bytes 3145736 | tf_op jit(solution)/shard_map/ppermute | solution.py:329
  19.0 24.5 %collective-permute-start = (bf16[1,2,64,8192]{3,2,1,0:T(8,128)(2,1)S(1)}, bf16[1,2,64,8192]{3,2,1,0:T(8,128)(2,1)S(1)}, u32[]{:S(2)}, u32[]{:S(2)}) collective-permute-start(bf16[1,2,64,8192]{3,2,1,0:T(8,128)(2,1)S(1)} %get-tuple-element.44), channel_id=1, source_target_pairs={{0,1},{1,0},{2,3},{3,2},{4,5},{5,4},{6,7},{7,6},{8,9},{9,8},{10,11... | collective-permute-start | bytes 6291464 | tf_op jit(solution)/shard_map/ppermute | solution.py:329
  41.9 23.5 %collective-permute-start.2 = (bf16[2,2,16,8192]{3,2,1,0:T(8,128)(2,1)S(1)}, bf16[2,2,16,8192]{3,2,1,0:T(8,128)(2,1)S(1)}, u32[]{:S(2)}, u32[]{:S(2)}) collective-permute-start(bf16[2,2,16,8192]{3,2,1,0:T(8,128)(2,1)S(1)} %get-tuple-element.48), channel_id=1, source_target_pairs={{0,2},{1,3},{2,0},{3,1},{4,6},{5,7},{6,4},{7,5},{8,10},{9,11},{10,... | collective-permute-start | bytes 3145736 | tf_op jit(solution)/shard_map/ppermute | solution.py:329
  45.6 54.6 %collective-permute-start.11 = (bf16[2,64,8192]{2,1,0:T(8,128)(2,1)S(1)}, bf16[2,64,8192]{2,1,0:T(8,128)(2,1)}, u32[]{:S(2)}, u32[]{:S(2)}) collective-permute-start(bf16[2,64,8192]{2,1,0:T(8,128)(2,1)S(1)} %pad_maximum_fusion.rows3_ref), channel_id=1, source_target_pairs={{0,4},{1,5},{2,6},{3,7},{12,8},{13,9},{14,10},{15,11},{16,20},{17,... | collective-permute-start | bytes 6291464 | tf_op jit(solution)/shard_map/ppermute | solution.py:329
  49.2 53.6 %collective-permute-start.8 = (bf16[2,64,8192]{2,1,0:T(8,128)(2,1)}, bf16[2,64,8192]{2,1,0:T(8,128)(2,1)}, u32[]{:S(2)}, u32[]{:S(2)}) collective-permute-start(bf16[2,64,8192]{2,1,0:T(8,128)(2,1)} %collective-permute-done.7.crossed_ref), channel_id=1, source_target_pairs={{4,0},{5,1},{6,2},{7,3},{8,12},{9,13},{10,14},{11,15},{20,16},{21,... | collective-permute-start | bytes 6291464 | tf_op jit(solution)/shard_map/ppermute | solution.py:329
  56.8 46.0 %collective-permute-start.9 = (bf16[2,64,8192]{2,1,0:T(8,128)(2,1)}, bf16[2,64,8192]{2,1,0:T(8,128)(2,1)}, u32[]{:S(2)}, u32[]{:S(2)}) collective-permute-start(bf16[2,64,8192]{2,1,0:T(8,128)(2,1)} %collective-permute-done.6.refs_4_), channel_id=1, source_target_pairs={{4,8},{5,9},{6,10},{7,11},{8,4},{9,5},{10,6},{11,7},{20,24},{21,25... | collective-permute-start | bytes 6291464 | tf_op jit(solution)/shard_map/ppermute | solution.py:329
  69.0 50.3 %collective-permute-start.4 = (bf16[2,2,32,8192]{3,2,1,0:T(8,128)(2,1)}, bf16[2,2,32,8192]{3,2,1,0:T(8,128)(2,1)}, u32[]{:S(2)}, u32[]{:S(2)}) collective-permute-start(bf16[2,2,32,8192]{3,2,1,0:T(8,128)(2,1)} %get-tuple-element.49), channel_id=1, source_target_pairs={{0,2},{1,3},{2,0},{3,1},{4,6},{5,7},{6,4},{7,5},{8,10},{9,11},{10,... | collective-permute-start | bytes 6291464 | tf_op jit(solution)/shard_map/ppermute | solution.py:329
  108.0 28.7 %collective-permute-start.12 = (bf16[64,8192]{1,0:T(8,128)(2,1)S(1)}, bf16[64,8192]{1,0:T(8,128)(2,1)S(1)}, u32[]{:S(2)}, u32[]{:S(2)}) collective-permute-start(bf16[64,8192]{1,0:T(8,128)(2,1)S(1)} %get-tuple-element.53), channel_id=1, source_target_pairs={{0,4},{1,5},{2,6},{3,7},{4,0},{5,1},{6,2},{7,3},{8,12},{9,13},{10,... | collective-permute-start | bytes 3145736 | tf_op jit(solution)/shard_map/ppermute | solution.py:329
  113.0 23.6 %collective-permute-start.13 = (bf16[64,8192]{1,0:T(8,128)(2,1)S(1)}, bf16[64,8192]{1,0:T(8,128)(2,1)S(1)}, u32[]{:S(2)}, u32[]{:S(2)}) collective-permute-start(bf16[64,8192]{1,0:T(8,128)(2,1)S(1)} %get-tuple-element.54), channel_id=1, source_target_pairs={{4,8},{5,9},{6,10},{7,11},{8,4},{9,5},{10,6},{11,7},{20,24},{21,25... | collective-permute-start | bytes 3145736 | tf_op jit(solution)/shard_map/ppermute | solution.py:329
  113.8 56.6 %collective-permute-start.20 = (bf16[64,8192]{1,0:T(8,128)(2,1)S(1)}, bf16[64,8192]{1,0:T(8,128)(2,1)S(1)}, u32[]{:S(2)}, u32[]{:S(2)}) collective-permute-start(bf16[64,8192]{1,0:T(8,128)(2,1)S(1)} %get-tuple-element.68), channel_id=1, source_target_pairs={{0,4},{1,5},{2,6},{3,7},{12,8},{13,9},{14,10},{15,11},{16,20},{17,... | collective-permute-start | bytes 3145736 | tf_op jit(solution)/shard_map/ppermute | solution.py:329
  118.5 51.8 %collective-permute-start.21 = (bf16[64,8192]{1,0:T(8,128)(2,1)S(1)}, bf16[64,8192]{1,0:T(8,128)(2,1)S(1)}, u32[]{:S(2)}, u32[]{:S(2)}) collective-permute-start(bf16[64,8192]{1,0:T(8,128)(2,1)S(1)} %get-tuple-element.68), channel_id=1, source_target_pairs={{4,8},{5,9},{6,10},{7,11},{8,4},{9,5},{10,6},{11,7},{20,24},{21,25... | collective-permute-start | bytes 3145736 | tf_op jit(solution)/shard_map/ppermute | solution.py:329
  120.7 16.9 %collective-permute-start.5 = (bf16[1,2,32,8192]{3,2,1,0:T(8,128)(2,1)S(1)}, bf16[1,2,32,8192]{3,2,1,0:T(8,128)(2,1)S(1)}, u32[]{:S(2)}, u32[]{:S(2)}) collective-permute-start(bf16[1,2,32,8192]{3,2,1,0:T(8,128)(2,1)S(1)} %slice.37), channel_id=1, source_target_pairs={{0,1},{1,0},{2,3},{3,2},{4,5},{5,4},{6,7},{7,6},{8,9},{9,8},{10,11... | collective-permute-start | bytes 3145736 | tf_op jit(solution)/shard_map/ppermute | solution.py:329
  136.9 42.0 %collective-permute-start.18 = (bf16[64,8192]{1,0:T(8,128)(2,1)S(1)}, bf16[64,8192]{1,0:T(8,128)(2,1)S(1)}, u32[]{:S(2)}, u32[]{:S(2)}) collective-permute-start(bf16[64,8192]{1,0:T(8,128)(2,1)S(1)} %add_convert_fusion.3), channel_id=1, source_target_pairs={{4,8},{5,9},{6,10},{7,11},{8,4},{9,5},{10,6},{11,7},{20,24},{21,25... | collective-permute-start | bytes 3145736 | tf_op jit(solution)/shard_map/ppermute | solution.py:329
  145.5 23.3 %collective-permute-start.15 = (bf16[64,8192]{1,0:T(8,128)(2,1)S(1)}, bf16[64,8192]{1,0:T(8,128)(2,1)S(1)}, u32[]{:S(2)}, u32[]{:S(2)}) collective-permute-start(bf16[64,8192]{1,0:T(8,128)(2,1)S(1)} %get-tuple-element.58), channel_id=1, source_target_pairs={{0,2},{1,3},{2,0},{3,1},{4,6},{5,7},{6,4},{7,5},{8,10},{9,11},{10,... | collective-permute-start | bytes 3145736 | tf_op jit(solution)/shard_map/ppermute | solution.py:329
  147.2 40.7 %collective-permute-start.19 = (bf16[64,8192]{1,0:T(8,128)(2,1)S(1)}, bf16[64,8192]{1,0:T(8,128)(2,1)S(1)}, u32[]{:S(2)}, u32[]{:S(2)}) collective-permute-start(bf16[64,8192]{1,0:T(8,128)(2,1)S(1)} %add_convert_fusion.2), channel_id=1, source_target_pairs={{0,4},{1,5},{2,6},{3,7},{4,0},{5,1},{6,2},{7,3},{8,12},{9,13},{10,... | collective-permute-start | bytes 3145736 | tf_op jit(solution)/shard_map/ppermute | solution.py:329
  168.8 19.0 %collective-permute-start.16 = (bf16[64,8192]{1,0:T(8,128)(2,1)S(1)}, bf16[64,8192]{1,0:T(8,128)(2,1)S(1)}, u32[]{:S(2)}, u32[]{:S(2)}) collective-permute-start(bf16[64,8192]{1,0:T(8,128)(2,1)S(1)} %get-tuple-element.60), channel_id=1, source_target_pairs={{0,2},{1,3},{2,0},{3,1},{4,6},{5,7},{6,4},{7,5},{8,10},{9,11},{10,... | collective-permute-start | bytes 3145736 | tf_op jit(solution)/shard_map/ppermute | solution.py:329
  170.5 30.4 %collective-permute-start.23 = (bf16[64,8192]{1,0:T(8,128)(2,1)S(1)}, bf16[64,8192]{1,0:T(8,128)(2,1)S(1)}, u32[]{:S(2)}, u32[]{:S(2)}) collective-permute-start(bf16[64,8192]{1,0:T(8,128)(2,1)S(1)} %add_convert_fusion), channel_id=1, source_target_pairs={{0,4},{1,5},{2,6},{3,7},{4,0},{5,1},{6,2},{7,3},{8,12},{9,13},{10,... | collective-permute-start | bytes 3145736 | tf_op jit(solution)/shard_map/ppermute | solution.py:329
  178.0 22.9 %collective-permute-start.22 = (bf16[64,8192]{1,0:T(8,128)(2,1)S(1)}, bf16[64,8192]{1,0:T(8,128)(2,1)S(1)}, u32[]{:S(2)}, u32[]{:S(2)}) collective-permute-start(bf16[64,8192]{1,0:T(8,128)(2,1)S(1)} %add_convert_fusion.1), channel_id=1, source_target_pairs={{4,8},{5,9},{6,10},{7,11},{8,4},{9,5},{10,6},{11,7},{20,24},{21,25... | collective-permute-start | bytes 3145736 | tf_op jit(solution)/shard_map/ppermute | solution.py:329
  178.9 24.6 %collective-permute-start.14 = (bf16[64,8192]{1,0:T(8,128)(2,1)S(1)}, bf16[64,8192]{1,0:T(8,128)(2,1)S(1)}, u32[]{:S(2)}, u32[]{:S(2)}) collective-permute-start(bf16[64,8192]{1,0:T(8,128)(2,1)S(1)} %get-tuple-element.57), channel_id=1, source_target_pairs={{0,1},{1,0},{2,3},{3,2},{4,5},{5,4},{6,7},{7,6},{8,9},{9,8},{10,11... | collective-permute-start | bytes 3145736 | tf_op jit(solution)/shard_map/ppermute | solution.py:329
  187.9 15.6 %collective-permute-start.17 = (bf16[64,8192]{1,0:T(8,128)(2,1)S(1)}, bf16[64,8192]{1,0:T(8,128)(2,1)S(1)}, u32[]{:S(2)}, u32[]{:S(2)}) collective-permute-start(bf16[64,8192]{1,0:T(8,128)(2,1)S(1)} %collective-permute-done.16), channel_id=1, source_target_pairs={{0,1},{1,0},{2,3},{3,2},{4,5},{5,4},{6,7},{7,6},{8,9},{9,8},{10,11... | collective-permute-start | bytes 3145736 | tf_op jit(solution)/shard_map/ppermute | solution.py:329
  206.1 9.4 %collective-permute-start.27 = (f32[8,128]{1,0:T(8,128)S(1)}, f32[8,128]{1,0:T(8,128)S(1)}, u32[]{:S(2)}, u32[]{:S(2)}) collective-permute-start(f32[8,128]{1,0:T(8,128)S(1)} %add_add_fusion.refs_2_), channel_id=1, source_target_pairs={{0,4},{1,5},{2,6},{3,7},{4,0},{5,1},{6,2},{7,3},{8,12},{9,13},{10,... | collective-permute-start | bytes 12296 | tf_op jit(solution)/shard_map/ppermute | solution.py:329
  211.8 5.4 %collective-permute-start.29 = (f32[8,128]{1,0:T(8,128)S(1)}, f32[8,128]{1,0:T(8,128)S(1)}, u32[]{:S(2)}, u32[]{:S(2)}) collective-permute-start(f32[8,128]{1,0:T(8,128)S(1)} %add_add_fusion.refs_2_), channel_id=1, source_target_pairs={{0,12},{1,13},{2,14},{3,15},{4,8},{5,9},{6,10},{7,11},{8,4},{9,5},... | collective-permute-start | bytes 12296 | tf_op jit(solution)/shard_map/ppermute | solution.py:329
  (16 other events, 157.1 us)

commit v19 on v18

--- a/solution.py
+++ b/solution.py
@@ -261,18 +261,17 @@
     return in_place(body, shapes, rows, handed, outer, far, flags=flags)
 
 
-def near_groups(flags, stage, pair, down, up, outer, far, inner_late, dx_early, swapped, capacity, first1):
+def near_groups(flags, stage, pair, own, outer, far, inner_late, dx_early, swapped, capacity, first1):
     plane = len(stage)
-    rank, width = down.shape
+    _, rank, width = own.shape
     block = plane * capacity
     tile = min(width, 2048)
     cuts = [pl.ds(i * tile, tile) for i in range(width // tile)]
 
     def body(flags_ref, *refs):
         stage_in, refs = refs[:plane], refs[plane:]
-        pair_in, down_in, up_in, outer_in, far_in, late_ref, early_ref, swapped_ref = refs[:8]
-        dx_refs, sum_refs = refs[8:8 + plane], refs[8 + plane:]
-        own_in = (down_in, up_in)
+        pair_in, own_in, outer_in, far_in, late_ref, early_ref, swapped_ref = refs[:7]
+        dx_refs, sum_refs = refs[7:7 + plane], refs[7 + plane:]
         at_end = flags_ref[0] == 1
 
         def rows(k, cut):
@@ -286,7 +285,7 @@
             )
 
         def factors(k, cut):
-            return jnp.concatenate([pair_in[k, :, cut], own_in[k][:, cut]], axis=0)
+            return jnp.concatenate([pair_in[k, :, cut], own_in[k, :, cut]], axis=0)
 
         is_mine = corner(2 * block, block, 2 * rank, rank)
         sums = [sum(dot32(rows(k, cut), factors(k, cut), ROWS_OF) for cut in cuts) for k in range(2)]
@@ -305,7 +304,7 @@
                     dx_refs[m][n * capacity:(n + 1) * capacity, cut] = dx[m * capacity:(m + 1) * capacity]
 
     shapes = [((4 * capacity, width), BF16)] * plane + [((rank, width), F32)] * 4
-    return in_place(body, shapes, *stage, pair, down, up, outer, far, inner_late, dx_early, swapped, flags=flags)
+    return in_place(body, shapes, *stage, pair, own, outer, far, inner_late, dx_early, swapped, flags=flags)
 
 
 def move_adapters(plane, acts, cotan, token_task_index, task_slot_lookup, pool_down_factors, pool_up_factors):
@@ -334,7 +333,6 @@
     def beside(m):
         return [(i, (i // plane) * plane + ((i % plane) ^ m)) for i in range(ndevices)]
 
-    down, up = pool_down_factors[0], pool_up_factors[0]
     lowest, none = jnp.array(-jnp.inf, BF16), (0, 0, 0)
     own = jnp.maximum(
         lax.pad(pool_down_factors, lowest, ((0, 1, 0), none, none)),
@@ -391,7 +389,7 @@
 
     swapped, down3 = lax.optimization_barrier((swapped, down3))
     dx_own, dx_beside, *dx_across, up1, down1, up0, down0 = near_groups(
-        end_flag, stage10, pair, down, up, outer, far, inner_late, dx_early, swapped, capacity,
+        end_flag, stage10, pair, own, outer, far, inner_late, dx_early, swapped, capacity,
         (2 * capacity, 2 * capacity, 0, 0),
     )
 

time: 220 us -> 218 us (level)
  waiting for transfers between devices: 120 us -> 117 us
    ppermute x30, waiting for transfers between devices: 120 us -> 117 us  [send(): return lax.ppermute(array, 'dp', pairs)]
where the time goes in v19:
time: 218 us
  waiting for transfers between devices  117 us (54%)
  starting transfers between devices  57.5 us (26%)
  Pallas kernels  30.6 us (14%)
  other arithmetic  6.23 us (3%)
  local copies, waits for them, and re-layouts  5.63 us (3%)
    ppermute x30, waiting for transfers between devices, send(): return lax.ppermute(array, 'dp', pairs)  117 us
    ppermute x30, starting transfers between devices, send(): return lax.ppermute(array, 'dp', pairs)  57.5 us
    pallas_call x5, Pallas kernels, in_place(): pl.pallas_call(body, in_specs=[pl.BlockSpec(memory_space=pltpu.SMEM)] * l...  17.2 us
    pallas_call x1, Pallas kernels, pack(): pl.pallas_call(body, grid=(tiles,), in_specs=[pl.BlockSpec(place.shape, l...  6.36 us
    pallas_call x2, Pallas kernels, unpack(): pl.pallas_call(body, grid=(width // 2 // tile,), in_specs=[pl.BlockSpec(p...  4.79 us
  transfers between devices with their start and end apart: 30, of which 13 were waited for; matrix products, arithmetic and copies ran while one was open for 3% of the time, Pallas kernels for 13%

profile of v19, /device:TPU:0, one launch (start us, length us, event | category | flops | bytes accessed | tf_op | source)
XLA Modules:
  0.0 217.9 jit_solution(11653419557385566640)
XLA Ops:
  4.4 4.6 %collective-permute-start.6 = (bf16[2,64,8192]{2,1,0:T(8,128)(2,1)S(1)}, bf16[2,64,8192]{2,1,0:T(8,128)(2,1)}, u32[]{:S(2)}, u32[]{:S(2)}) collective-permute-start(bf16[2,64,8192]{2,1,0:T(8,128)(2,1)S(1)} %pad_maximum_fusion.2.refs_5_), channel_id=1, source_target_pairs={{0,4},{1,5},{2,6},{3,7},{4,0},{5,1},{6,2},{7,3},{8,12},{9,13},{10,... | collective-permute-start | bytes 6291464 | tf_op jit(solution)/shard_map/ppermute | solution.py:328
  9.7 6.4 %shard_map.85 = (bf16[1,2,64,8192]{3,2,1,0:T(8,128)(2,1)S(1)}, bf16[1,2,64,8192]{3,2,1,0:T(8,128)(2,1)S(1)}, bf16[2,2,16,8192]{3,2,1,0:T(8,128)(2,1)S(1)}, bf16[...) custom-call(bf16[256,128]{1,0:T(8,128)(2,1)S(1)} %fusion.1.place_ref, bf16[128,8192]{1,0:T(8,128)(2,1)} %x_in.1, ...), custom_call_target="tpu_custom_call" | custom-call | tf_op jit(solution)/shard_map/pallas_call | solution.py:107
  17.7 22.8 %collective-permute-done.1 = bf16[2,2,16,8192]{3,2,1,0:T(8,128)(2,1)S(1)} collective-permute-done((bf16[2,2,16,8192]{3,2,1,0:T(8,128)(2,1)S(1)}, bf16[2,2,16,8192]{3,2,1,0:T(8,128)(2,1)S(1)}, u32[]{:S(2)}, u32[]{:S(2)}) %collective-permute-start.1) | collective-permute-done | bytes 1048608 | tf_op jit(solution)/shard_map/ppermute | solution.py:328
  45.5 3.6 %collective-permute-start.11 = (bf16[2,64,8192]{2,1,0:T(8,128)(2,1)}, bf16[2,64,8192]{2,1,0:T(8,128)(2,1)}, u32[]{:S(2)}, u32[]{:S(2)}) collective-permute-start(bf16[2,64,8192]{2,1,0:T(8,128)(2,1)} %pad_maximum_fusion.rows3_ref), channel_id=1, source_target_pairs={{0,4},{1,5},{2,6},{3,7},{12,8},{13,9},{14,10},{15,11},{16,20},{17,... | collective-permute-start | bytes 6291464 | tf_op jit(solution)/shard_map/ppermute | solution.py:328
  50.4 4.6 %collective-permute-done.6.refs_4_ = bf16[2,64,8192]{2,1,0:T(8,128)(2,1)} collective-permute-done((bf16[2,64,8192]{2,1,0:T(8,128)(2,1)S(1)}, bf16[2,64,8192]{2,1,0:T(8,128)(2,1)}, u32[]{:S(2)}, u32[]{:S(2)}) %collective-permute-start.6) | collective-permute-done | bytes 2097184 | tf_op jit(solution)/shard_map/ppermute | solution.py:328
  55.1 2.1 collective-permute-start.9
  57.1 6.9 %collective-permute-done.2 = bf16[2,2,16,8192]{3,2,1,0:T(8,128)(2,1)S(1)} collective-permute-done((bf16[2,2,16,8192]{3,2,1,0:T(8,128)(2,1)S(1)}, bf16[2,2,16,8192]{3,2,1,0:T(8,128)(2,1)S(1)}, u32[]{:S(2)}, u32[]{:S(2)}) %collective-permute-start.2) | collective-permute-done | bytes 1048608 | tf_op jit(solution)/shard_map/ppermute | solution.py:328
  70.4 4.1 %shard_map.86 = (bf16[64,8192]{1,0:T(8,128)(2,1)S(1)}, bf16[64,8192]{1,0:T(8,128)(2,1)S(1)}, bf16[64,8192]{1,0:T(8,128)(2,1)S(1)}, bf16[2,64,8192]{2,1,0:T(8,128)(2,1)S(1)}) custom-call(s32[1]{0:T(128)} %bitcast.1.flags_ref, bf16[2,64,8192]{2,1,0:T(8,128)(2,1)} %pad_maximum_fusion.rows3_ref, bf16[2,64,8192]{2,1,0:T(8,128)(2,1)S(1)} %pad_maximum_fusion.1.rows2_ref, ...), custom_call_target="tpu_custom_call" | custom-call | tf_op jit(solution)/shard_map/pallas_call | solution.py:218
  74.6 24.1 %collective-permute-done.11.handed_ref = bf16[2,64,8192]{2,1,0:T(8,128)(2,1)} collective-permute-done((bf16[2,64,8192]{2,1,0:T(8,128)(2,1)}, bf16[2,64,8192]{2,1,0:T(8,128)(2,1)}, u32[]{:S(2)}, u32[]{:S(2)}) %collective-permute-start.11) | collective-permute-done | bytes 2097184 | tf_op jit(solution)/shard_map/ppermute | solution.py:328
  98.6 2.5 %collective-permute-done.8.outer_ref.refs_6_ = bf16[2,64,8192]{2,1,0:T(8,128)(2,1)} collective-permute-done((bf16[2,64,8192]{2,1,0:T(8,128)(2,1)}, bf16[2,64,8192]{2,1,0:T(8,128)(2,1)}, u32[]{:S(2)}, u32[]{:S(2)}) %collective-permute-start.8) | collective-permute-done | bytes 2097184 | tf_op jit(solution)/shard_map/ppermute | solution.py:328
  101.1 5.2 %shard_map.87 = (bf16[64,8192]{1,0:T(8,128)(2,1)S(1)}, bf16[64,8192]{1,0:T(8,128)(2,1)S(1)}, bf16[64,64]{1,0:T(8,128)(2,1)S(1)}, bf16[64,8192]{1,0:T(8,128)(2,1)S(1)}) custom-call(s32[1]{0:T(128)} %bitcast.1.flags_ref, bf16[2,64,8192]{2,1,0:T(8,128)(2,1)S(1)} %get-tuple-element.50.rows_ref, bf16[2,64,8192]{2,1,0:T(8,128)(2,1)} %collective-permute-done.11.handed_ref, ...), custom_call_target="tpu_custom_call" | custom-call | tf_op jit(solution)/shard_map/pallas_call | solution.py:218
  106.3 5.0 %collective-permute-start.12 = (bf16[64,8192]{1,0:T(8,128)(2,1)S(1)}, bf16[64,8192]{1,0:T(8,128)(2,1)S(1)}, u32[]{:S(2)}, u32[]{:S(2)}) collective-permute-start(bf16[64,8192]{1,0:T(8,128)(2,1)S(1)} %get-tuple-element.53), channel_id=1, source_target_pairs={{0,4},{1,5},{2,6},{3,7},{4,0},{5,1},{6,2},{7,3},{8,12},{9,13},{10,... | collective-permute-start | bytes 3145736 | tf_op jit(solution)/shard_map/ppermute | solution.py:328
  112.1 4.8 %collective-permute-start.20 = (bf16[64,8192]{1,0:T(8,128)(2,1)S(1)}, bf16[64,8192]{1,0:T(8,128)(2,1)S(1)}, u32[]{:S(2)}, u32[]{:S(2)}) collective-permute-start(bf16[64,8192]{1,0:T(8,128)(2,1)S(1)} %get-tuple-element.68), channel_id=1, source_target_pairs={{0,4},{1,5},{2,6},{3,7},{12,8},{13,9},{14,10},{15,11},{16,20},{17,... | collective-permute-start | bytes 3145736 | tf_op jit(solution)/shard_map/ppermute | solution.py:328
  119.1 15.8 %collective-permute-done.12.refs_10_ = bf16[64,8192]{1,0:T(8,128)(2,1)S(1)} collective-permute-done((bf16[64,8192]{1,0:T(8,128)(2,1)S(1)}, bf16[64,8192]{1,0:T(8,128)(2,1)S(1)}, u32[]{:S(2)}, u32[]{:S(2)}) %collective-permute-start.12) | collective-permute-done | bytes 1048608 | tf_op jit(solution)/shard_map/ppermute | solution.py:328
  136.0 6.8 %shard_map.88 = (bf16[64,8192]{1,0:T(8,128)(2,1)S(1)}, bf16[64,8192]{1,0:T(8,128)(2,1)S(1)}, bf16[64,8192]{1,0:T(8,128)(2,1)S(1)}, bf16[64,8192]{1,0:T(8,128)(2,...) custom-call(s32[1]{0:T(128)} %bitcast.1.flags_ref, ...), custom_call_target="tpu_custom_call" | custom-call | tf_op jit(solution)/shard_map/pallas_call | solution.py:218
  145.5 7.2 %collective-permute-start.19 = (bf16[64,8192]{1,0:T(8,128)(2,1)S(1)}, bf16[64,8192]{1,0:T(8,128)(2,1)S(1)}, u32[]{:S(2)}, u32[]{:S(2)}) collective-permute-start(bf16[64,8192]{1,0:T(8,128)(2,1)S(1)} %add_convert_fusion.2), channel_id=1, source_target_pairs={{0,4},{1,5},{2,6},{3,7},{4,0},{5,1},{6,2},{7,3},{8,12},{9,13},{10,... | collective-permute-start | bytes 3145736 | tf_op jit(solution)/shard_map/ppermute | solution.py:328
  152.7 14.5 %collective-permute-done.15.refs_2_ = bf16[64,8192]{1,0:T(8,128)(2,1)S(1)} collective-permute-done((bf16[64,8192]{1,0:T(8,128)(2,1)S(1)}, bf16[64,8192]{1,0:T(8,128)(2,1)S(1)}, u32[]{:S(2)}, u32[]{:S(2)}) %collective-permute-start.15) | collective-permute-done | bytes 1048608 | tf_op jit(solution)/shard_map/ppermute | solution.py:328
  168.8 7.2 %collective-permute-start.23 = (bf16[64,8192]{1,0:T(8,128)(2,1)S(1)}, bf16[64,8192]{1,0:T(8,128)(2,1)S(1)}, u32[]{:S(2)}, u32[]{:S(2)}) collective-permute-start(bf16[64,8192]{1,0:T(8,128)(2,1)S(1)} %add_convert_fusion), channel_id=1, source_target_pairs={{0,4},{1,5},{2,6},{3,7},{4,0},{5,1},{6,2},{7,3},{8,12},{9,13},{10,... | collective-permute-start | bytes 3145736 | tf_op jit(solution)/shard_map/ppermute | solution.py:328
  177.3 8.9 %collective-permute-done.16 = bf16[64,8192]{1,0:T(8,128)(2,1)S(1)} collective-permute-done((bf16[64,8192]{1,0:T(8,128)(2,1)S(1)}, bf16[64,8192]{1,0:T(8,128)(2,1)S(1)}, u32[]{:S(2)}, u32[]{:S(2)}) %collective-permute-start.16) | collective-permute-done | bytes 1048608 | tf_op jit(solution)/shard_map/ppermute | solution.py:328
  186.7 12.5 %collective-permute-done.23.refs_1_ = bf16[64,8192]{1,0:T(8,128)(2,1)S(1)} collective-permute-done((bf16[64,8192]{1,0:T(8,128)(2,1)S(1)}, bf16[64,8192]{1,0:T(8,128)(2,1)S(1)}, u32[]{:S(2)}, u32[]{:S(2)}) %collective-permute-start.23) | collective-permute-done | bytes 1048608 | tf_op jit(solution)/shard_map/ppermute | solution.py:328
  201.8 2.4 %shard_map.89.refs_4_ = bf16[128,8192]{1,0:T(8,128)(2,1)} custom-call(bf16[128,256]{1,0:T(8,128)(2,1)S(1)} %fusion.place_ref, bf16[64,8192]{1,0:T(8,128)(2,1)} %copy-done.4, bf16[64,8192]{1,0:T(8,128)(2,1)S(1)} %collective-permute-done.14.refs_1_, bf16[64,8192]{1,0:T(8,128)(2,1)S(1)} %collective-permute-done.15.refs_2_, ...), custom_call_target="tpu_custom_call" | custom-call | tf_op jit(solution)/shard_map/pallas_call | solution.py:128
  204.4 4.4 %collective-permute-start.27 = (f32[8,128]{1,0:T(8,128)S(1)}, f32[8,128]{1,0:T(8,128)S(1)}, u32[]{:S(2)}, u32[]{:S(2)}) collective-permute-start(f32[8,128]{1,0:T(8,128)S(1)} %add_add_fusion.refs_2_), channel_id=1, source_target_pairs={{0,4},{1,5},{2,6},{3,7},{4,0},{5,1},{6,2},{7,3},{8,12},{9,13},{10,... | collective-permute-start | bytes 12296 | tf_op jit(solution)/shard_map/ppermute | solution.py:328
  211.5 2.4 %shard_map.90 = bf16[128,8192]{1,0:T(8,128)(2,1)} custom-call(bf16[128,256]{1,0:T(8,128)(2,1)S(1)} %fusion.place_ref, bf16[64,8192]{1,0:T(8,128)(2,1)} %copy-done.4, bf16[64,8192]{1,0:T(8,128)(2,1)S(1)} %collective-permute-done.14.refs_1_, bf16[64,8192]{1,0:T(8,128)(2,1)S(1)} %collective-permute-done.15.refs_2_, ...), custom_call_target="tpu_custom_call", output_to_operand_aliasing={{}: (5, {})} | custom-call | tf_op jit(solution)/shard_map/pallas_call | solution.py:128
  215.5 2.3 %shard_map.93 = (f32[1,64,8192]{2,1,0:T(8,128)}, f32[1,64,8192]{2,1,0:T(8,128)}) custom-call(f32[64,8192]{1,0:T(8,128)S(1)} %get-tuple-element.65.refs_0_, f32[64,8192]{1,0:T(8,128)S(1)} %get-tuple-element.72.refs_1_, f32[8,128]{1,0:T(8,128)S(1)} %add_add_fusion.refs_2_, f32[8,128]{1,0:T(8,128)S(1)} %collective-permute-done.27.refs_3_, ...), custom_call_target="tpu_custom_call" | custom-call | tf_op jit(solution)/shard_map/pallas_call | solution.py:183
  (83 shorter events, 35.9 us)
Async XLA Ops:
  2.4 46.7 %collective-permute-start.7 = (bf16[2,64,8192]{2,1,0:T(8,128)(2,1)S(1)}, bf16[2,64,8192]{2,1,0:T(8,128)(2,1)}, u32[]{:S(2)}, u32[]{:S(2)}) collective-permute-start(bf16[2,64,8192]{2,1,0:T(8,128)(2,1)S(1)} %pad_maximum_fusion.2.refs_5_), channel_id=1, source_target_pairs={{4,8},{5,9},{6,10},{7,11},{8,4},{9,5},{10,6},{11,7},{20,24},{21,25... | collective-permute-start | bytes 6291464 | tf_op jit(solution)/shard_map/ppermute | solution.py:328
  4.4 50.7 %collective-permute-start.6 = (bf16[2,64,8192]{2,1,0:T(8,128)(2,1)S(1)}, bf16[2,64,8192]{2,1,0:T(8,128)(2,1)}, u32[]{:S(2)}, u32[]{:S(2)}) collective-permute-start(bf16[2,64,8192]{2,1,0:T(8,128)(2,1)S(1)} %pad_maximum_fusion.2.refs_5_), channel_id=1, source_target_pairs={{0,4},{1,5},{2,6},{3,7},{4,0},{5,1},{6,2},{7,3},{8,12},{9,13},{10,... | collective-permute-start | bytes 6291464 | tf_op jit(solution)/shard_map/ppermute | solution.py:328
  16.1 24.4 %collective-permute-start.1 = (bf16[2,2,16,8192]{3,2,1,0:T(8,128)(2,1)S(1)}, bf16[2,2,16,8192]{3,2,1,0:T(8,128)(2,1)S(1)}, u32[]{:S(2)}, u32[]{:S(2)}) collective-permute-start(bf16[2,2,16,8192]{3,2,1,0:T(8,128)(2,1)S(1)} %get-tuple-element.47), channel_id=1, source_target_pairs={{0,2},{1,3},{2,0},{3,1},{4,6},{5,7},{6,4},{7,5},{8,10},{9,11},{10,... | collective-permute-start | bytes 3145736 | tf_op jit(solution)/shard_map/ppermute | solution.py:328
  17.6 24.5 %collective-permute-start = (bf16[1,2,64,8192]{3,2,1,0:T(8,128)(2,1)S(1)}, bf16[1,2,64,8192]{3,2,1,0:T(8,128)(2,1)S(1)}, u32[]{:S(2)}, u32[]{:S(2)}) collective-permute-start(bf16[1,2,64,8192]{3,2,1,0:T(8,128)(2,1)S(1)} %get-tuple-element.44), channel_id=1, source_target_pairs={{0,1},{1,0},{2,3},{3,2},{4,5},{5,4},{6,7},{7,6},{8,9},{9,8},{10,11... | collective-permute-start | bytes 6291464 | tf_op jit(solution)/shard_map/ppermute | solution.py:328
  40.5 23.5 %collective-permute-start.2 = (bf16[2,2,16,8192]{3,2,1,0:T(8,128)(2,1)S(1)}, bf16[2,2,16,8192]{3,2,1,0:T(8,128)(2,1)S(1)}, u32[]{:S(2)}, u32[]{:S(2)}) collective-permute-start(bf16[2,2,16,8192]{3,2,1,0:T(8,128)(2,1)S(1)} %get-tuple-element.48), channel_id=1, source_target_pairs={{0,2},{1,3},{2,0},{3,1},{4,6},{5,7},{6,4},{7,5},{8,10},{9,11},{10,... | collective-permute-start | bytes 3145736 | tf_op jit(solution)/shard_map/ppermute | solution.py:328
  45.5 53.1 %collective-permute-start.11 = (bf16[2,64,8192]{2,1,0:T(8,128)(2,1)}, bf16[2,64,8192]{2,1,0:T(8,128)(2,1)}, u32[]{:S(2)}, u32[]{:S(2)}) collective-permute-start(bf16[2,64,8192]{2,1,0:T(8,128)(2,1)} %pad_maximum_fusion.rows3_ref), channel_id=1, source_target_pairs={{0,4},{1,5},{2,6},{3,7},{12,8},{13,9},{14,10},{15,11},{16,20},{17,... | collective-permute-start | bytes 6291464 | tf_op jit(solution)/shard_map/ppermute | solution.py:328
  49.1 52.0 %collective-permute-start.8 = (bf16[2,64,8192]{2,1,0:T(8,128)(2,1)}, bf16[2,64,8192]{2,1,0:T(8,128)(2,1)}, u32[]{:S(2)}, u32[]{:S(2)}) collective-permute-start(bf16[2,64,8192]{2,1,0:T(8,128)(2,1)} %collective-permute-done.7.crossed_ref), channel_id=1, source_target_pairs={{4,0},{5,1},{6,2},{7,3},{8,12},{9,13},{10,14},{11,15},{20,16},{21,... | collective-permute-start | bytes 6291464 | tf_op jit(solution)/shard_map/ppermute | solution.py:328
  55.1 46.1 %collective-permute-start.9 = (bf16[2,64,8192]{2,1,0:T(8,128)(2,1)}, bf16[2,64,8192]{2,1,0:T(8,128)(2,1)}, u32[]{:S(2)}, u32[]{:S(2)}) collective-permute-start(bf16[2,64,8192]{2,1,0:T(8,128)(2,1)} %collective-permute-done.6.refs_4_), channel_id=1, source_target_pairs={{4,8},{5,9},{6,10},{7,11},{8,4},{9,5},{10,6},{11,7},{20,24},{21,25... | collective-permute-start | bytes 6291464 | tf_op jit(solution)/shard_map/ppermute | solution.py:328
  67.6 50.0 %collective-permute-start.4 = (bf16[2,2,32,8192]{3,2,1,0:T(8,128)(2,1)}, bf16[2,2,32,8192]{3,2,1,0:T(8,128)(2,1)}, u32[]{:S(2)}, u32[]{:S(2)}) collective-permute-start(bf16[2,2,32,8192]{3,2,1,0:T(8,128)(2,1)} %get-tuple-element.49), channel_id=1, source_target_pairs={{0,2},{1,3},{2,0},{3,1},{4,6},{5,7},{6,4},{7,5},{8,10},{9,11},{10,... | collective-permute-start | bytes 6291464 | tf_op jit(solution)/shard_map/ppermute | solution.py:328
  106.3 28.7 %collective-permute-start.12 = (bf16[64,8192]{1,0:T(8,128)(2,1)S(1)}, bf16[64,8192]{1,0:T(8,128)(2,1)S(1)}, u32[]{:S(2)}, u32[]{:S(2)}) collective-permute-start(bf16[64,8192]{1,0:T(8,128)(2,1)S(1)} %get-tuple-element.53), channel_id=1, source_target_pairs={{0,4},{1,5},{2,6},{3,7},{4,0},{5,1},{6,2},{7,3},{8,12},{9,13},{10,... | collective-permute-start | bytes 3145736 | tf_op jit(solution)/shard_map/ppermute | solution.py:328
  111.3 23.6 %collective-permute-start.13 = (bf16[64,8192]{1,0:T(8,128)(2,1)S(1)}, bf16[64,8192]{1,0:T(8,128)(2,1)S(1)}, u32[]{:S(2)}, u32[]{:S(2)}) collective-permute-start(bf16[64,8192]{1,0:T(8,128)(2,1)S(1)} %get-tuple-element.54), channel_id=1, source_target_pairs={{4,8},{5,9},{6,10},{7,11},{8,4},{9,5},{10,6},{11,7},{20,24},{21,25... | collective-permute-start | bytes 3145736 | tf_op jit(solution)/shard_map/ppermute | solution.py:328
  112.1 56.6 %collective-permute-start.20 = (bf16[64,8192]{1,0:T(8,128)(2,1)S(1)}, bf16[64,8192]{1,0:T(8,128)(2,1)S(1)}, u32[]{:S(2)}, u32[]{:S(2)}) collective-permute-start(bf16[64,8192]{1,0:T(8,128)(2,1)S(1)} %get-tuple-element.68), channel_id=1, source_target_pairs={{0,4},{1,5},{2,6},{3,7},{12,8},{13,9},{14,10},{15,11},{16,20},{17,... | collective-permute-start | bytes 3145736 | tf_op jit(solution)/shard_map/ppermute | solution.py:328
  116.8 51.8 %collective-permute-start.21 = (bf16[64,8192]{1,0:T(8,128)(2,1)S(1)}, bf16[64,8192]{1,0:T(8,128)(2,1)S(1)}, u32[]{:S(2)}, u32[]{:S(2)}) collective-permute-start(bf16[64,8192]{1,0:T(8,128)(2,1)S(1)} %get-tuple-element.68), channel_id=1, source_target_pairs={{4,8},{5,9},{6,10},{7,11},{8,4},{9,5},{10,6},{11,7},{20,24},{21,25... | collective-permute-start | bytes 3145736 | tf_op jit(solution)/shard_map/ppermute | solution.py:328
  119.0 16.9 %collective-permute-start.5 = (bf16[1,2,32,8192]{3,2,1,0:T(8,128)(2,1)S(1)}, bf16[1,2,32,8192]{3,2,1,0:T(8,128)(2,1)S(1)}, u32[]{:S(2)}, u32[]{:S(2)}) collective-permute-start(bf16[1,2,32,8192]{3,2,1,0:T(8,128)(2,1)S(1)} %slice.37), channel_id=1, source_target_pairs={{0,1},{1,0},{2,3},{3,2},{4,5},{5,4},{6,7},{7,6},{8,9},{9,8},{10,11... | collective-permute-start | bytes 3145736 | tf_op jit(solution)/shard_map/ppermute | solution.py:328
  135.2 42.0 %collective-permute-start.18 = (bf16[64,8192]{1,0:T(8,128)(2,1)S(1)}, bf16[64,8192]{1,0:T(8,128)(2,1)S(1)}, u32[]{:S(2)}, u32[]{:S(2)}) collective-permute-start(bf16[64,8192]{1,0:T(8,128)(2,1)S(1)} %add_convert_fusion.3), channel_id=1, source_target_pairs={{4,8},{5,9},{6,10},{7,11},{8,4},{9,5},{10,6},{11,7},{20,24},{21,25... | collective-permute-start | bytes 3145736 | tf_op jit(solution)/shard_map/ppermute | solution.py:328
  143.8 23.3 %collective-permute-start.15 = (bf16[64,8192]{1,0:T(8,128)(2,1)S(1)}, bf16[64,8192]{1,0:T(8,128)(2,1)S(1)}, u32[]{:S(2)}, u32[]{:S(2)}) collective-permute-start(bf16[64,8192]{1,0:T(8,128)(2,1)S(1)} %get-tuple-element.58), channel_id=1, source_target_pairs={{0,2},{1,3},{2,0},{3,1},{4,6},{5,7},{6,4},{7,5},{8,10},{9,11},{10,... | collective-permute-start | bytes 3145736 | tf_op jit(solution)/shard_map/ppermute | solution.py:328
  145.5 40.7 %collective-permute-start.19 = (bf16[64,8192]{1,0:T(8,128)(2,1)S(1)}, bf16[64,8192]{1,0:T(8,128)(2,1)S(1)}, u32[]{:S(2)}, u32[]{:S(2)}) collective-permute-start(bf16[64,8192]{1,0:T(8,128)(2,1)S(1)} %add_convert_fusion.2), channel_id=1, source_target_pairs={{0,4},{1,5},{2,6},{3,7},{4,0},{5,1},{6,2},{7,3},{8,12},{9,13},{10,... | collective-permute-start | bytes 3145736 | tf_op jit(solution)/shard_map/ppermute | solution.py:328
  167.1 19.0 %collective-permute-start.16 = (bf16[64,8192]{1,0:T(8,128)(2,1)S(1)}, bf16[64,8192]{1,0:T(8,128)(2,1)S(1)}, u32[]{:S(2)}, u32[]{:S(2)}) collective-permute-start(bf16[64,8192]{1,0:T(8,128)(2,1)S(1)} %get-tuple-element.60), channel_id=1, source_target_pairs={{0,2},{1,3},{2,0},{3,1},{4,6},{5,7},{6,4},{7,5},{8,10},{9,11},{10,... | collective-permute-start | bytes 3145736 | tf_op jit(solution)/shard_map/ppermute | solution.py:328
  168.8 30.4 %collective-permute-start.23 = (bf16[64,8192]{1,0:T(8,128)(2,1)S(1)}, bf16[64,8192]{1,0:T(8,128)(2,1)S(1)}, u32[]{:S(2)}, u32[]{:S(2)}) collective-permute-start(bf16[64,8192]{1,0:T(8,128)(2,1)S(1)} %add_convert_fusion), channel_id=1, source_target_pairs={{0,4},{1,5},{2,6},{3,7},{4,0},{5,1},{6,2},{7,3},{8,12},{9,13},{10,... | collective-permute-start | bytes 3145736 | tf_op jit(solution)/shard_map/ppermute | solution.py:328
  176.3 22.9 %collective-permute-start.22 = (bf16[64,8192]{1,0:T(8,128)(2,1)S(1)}, bf16[64,8192]{1,0:T(8,128)(2,1)S(1)}, u32[]{:S(2)}, u32[]{:S(2)}) collective-permute-start(bf16[64,8192]{1,0:T(8,128)(2,1)S(1)} %add_convert_fusion.1), channel_id=1, source_target_pairs={{4,8},{5,9},{6,10},{7,11},{8,4},{9,5},{10,6},{11,7},{20,24},{21,25... | collective-permute-start | bytes 3145736 | tf_op jit(solution)/shard_map/ppermute | solution.py:328
  177.2 24.6 %collective-permute-start.14 = (bf16[64,8192]{1,0:T(8,128)(2,1)S(1)}, bf16[64,8192]{1,0:T(8,128)(2,1)S(1)}, u32[]{:S(2)}, u32[]{:S(2)}) collective-permute-start(bf16[64,8192]{1,0:T(8,128)(2,1)S(1)} %get-tuple-element.57), channel_id=1, source_target_pairs={{0,1},{1,0},{2,3},{3,2},{4,5},{5,4},{6,7},{7,6},{8,9},{9,8},{10,11... | collective-permute-start | bytes 3145736 | tf_op jit(solution)/shard_map/ppermute | solution.py:328
  186.1 15.7 %collective-permute-start.17 = (bf16[64,8192]{1,0:T(8,128)(2,1)S(1)}, bf16[64,8192]{1,0:T(8,128)(2,1)S(1)}, u32[]{:S(2)}, u32[]{:S(2)}) collective-permute-start(bf16[64,8192]{1,0:T(8,128)(2,1)S(1)} %collective-permute-done.16), channel_id=1, source_target_pairs={{0,1},{1,0},{2,3},{3,2},{4,5},{5,4},{6,7},{7,6},{8,9},{9,8},{10,11... | collective-permute-start | bytes 3145736 | tf_op jit(solution)/shard_map/ppermute | solution.py:328
  204.4 9.4 %collective-permute-start.27 = (f32[8,128]{1,0:T(8,128)S(1)}, f32[8,128]{1,0:T(8,128)S(1)}, u32[]{:S(2)}, u32[]{:S(2)}) collective-permute-start(f32[8,128]{1,0:T(8,128)S(1)} %add_add_fusion.refs_2_), channel_id=1, source_target_pairs={{0,4},{1,5},{2,6},{3,7},{4,0},{5,1},{6,2},{7,3},{8,12},{9,13},{10,... | collective-permute-start | bytes 12296 | tf_op jit(solution)/shard_map/ppermute | solution.py:328
  210.1 5.4 %collective-permute-start.29 = (f32[8,128]{1,0:T(8,128)S(1)}, f32[8,128]{1,0:T(8,128)S(1)}, u32[]{:S(2)}, u32[]{:S(2)}) collective-permute-start(f32[8,128]{1,0:T(8,128)S(1)} %add_add_fusion.refs_2_), channel_id=1, source_target_pairs={{0,12},{1,13},{2,14},{3,15},{4,8},{5,9},{6,10},{7,11},{8,4},{9,5},... | collective-permute-start | bytes 12296 | tf_op jit(solution)/shard_map/ppermute | solution.py:328
  (14 other events, 101.9 us)

commit v20 on v19

--- a/solution.py
+++ b/solution.py
@@ -333,15 +333,17 @@
     def beside(m):
         return [(i, (i // plane) * plane + ((i % plane) ^ m)) for i in range(ndevices)]
 
-    lowest, none = jnp.array(-jnp.inf, BF16), (0, 0, 0)
-    own = jnp.maximum(
-        lax.pad(pool_down_factors, lowest, ((0, 1, 0), none, none)),
-        lax.pad(pool_up_factors, lowest, ((1, 0, 0), none, none)),
-    )
+    def stacked(first, second):
+        lowest, none = jnp.array(-jnp.inf, BF16), (0, 0, 0)
+        padded = lax.pad(first, lowest, ((0, 1, 0), none, none)), lax.pad(second, lowest, ((1, 0, 0), none, none))
+        return jnp.maximum(*padded)
+
+    own = stacked(pool_down_factors, pool_up_factors)
     pair = send(own, swap)
+    own = after(own, own[0, 0, 0] * 2)
     crossed = send(own, cross)
 
-    owner, position = route(token_task_index, task_slot_lookup, ndevices)
+    owner, position = route(after(token_task_index, own), task_slot_lookup, ndevices)
     owner_z, turn = owner // plane, (owner % plane) ^ column
     other_mid = jnp.where(z < 2, 2, 1)
     kind = jnp.where(owner_z == z, 0, jnp.where(owner_z == (z ^ 1), 1, jnp.where(owner_z == other_mid, 2, 3)))

time: 218 us -> 219 us (level)
  transfers between devices with their start and end apart: 30 -> 30, of which waited for: 13 -> 12; matrix products, arithmetic and copies ran while one was open for 3% -> 3% of each run, Pallas kernels for 13% -> 13%
where the time goes in v20:
time: 219 us
  waiting for transfers between devices  117 us (53%)
  starting transfers between devices  57.8 us (26%)
  Pallas kernels  30.6 us (14%)
  other arithmetic  6.23 us (3%)
  local copies, waits for them, and re-layouts  5.63 us (3%)
    ppermute x30, waiting for transfers between devices, send(): return lax.ppermute(array, 'dp', pairs)  117 us
    ppermute x30, starting transfers between devices, send(): return lax.ppermute(array, 'dp', pairs)  57.8 us
    pallas_call x5, Pallas kernels, in_place(): pl.pallas_call(body, in_specs=[pl.BlockSpec(memory_space=pltpu.SMEM)] * l...  17.2 us
    pallas_call x1, Pallas kernels, pack(): pl.pallas_call(body, grid=(tiles,), in_specs=[pl.BlockSpec(place.shape, l...  6.36 us
    pallas_call x2, Pallas kernels, unpack(): pl.pallas_call(body, grid=(width // 2 // tile,), in_specs=[pl.BlockSpec(p...  4.79 us
  transfers between devices with their start and end apart: 30, of which 12 were waited for; matrix products, arithmetic and copies ran while one was open for 3% of the time, Pallas kernels for 13%

profile of v20, /device:TPU:0, one launch (start us, length us, event | category | flops | bytes accessed | tf_op | source)
XLA Modules:
  0.0 218.6 jit_solution(4520003373090994256)
XLA Ops:
  2.4 3.1 %collective-permute-start.6 = (bf16[2,64,8192]{2,1,0:T(8,128)(2,1)S(1)}, bf16[2,64,8192]{2,1,0:T(8,128)(2,1)}, u32[]{:S(2)}, u32[]{:S(2)}) collective-permute-start(bf16[2,64,8192]{2,1,0:T(8,128)(2,1)S(1)} %pad_maximum_fusion.2.refs_5_), channel_id=1, source_target_pairs={{0,4},{1,5},{2,6},{3,7},{4,0},{5,1},{6,2},{7,3},{8,12},{9,13},{10,... | collective-permute-start | bytes 6291464 | tf_op jit(solution)/shard_map/ppermute | solution.py:328
  5.5 2.0 collective-permute-start.7
  8.2 6.4 %shard_map.85 = (bf16[1,2,64,8192]{3,2,1,0:T(8,128)(2,1)S(1)}, bf16[1,2,64,8192]{3,2,1,0:T(8,128)(2,1)S(1)}, bf16[2,2,16,8192]{3,2,1,0:T(8,128)(2,1)S(1)}, bf16[...) custom-call(bf16[256,128]{1,0:T(8,128)(2,1)S(1)} %fusion.1.place_ref, bf16[128,8192]{1,0:T(8,128)(2,1)} %x_in.1, ...), custom_call_target="tpu_custom_call" | custom-call | tf_op jit(solution)/shard_map/pallas_call | solution.py:107
  16.2 23.1 %collective-permute-done.1 = bf16[2,2,16,8192]{3,2,1,0:T(8,128)(2,1)S(1)} collective-permute-done((bf16[2,2,16,8192]{3,2,1,0:T(8,128)(2,1)S(1)}, bf16[2,2,16,8192]{3,2,1,0:T(8,128)(2,1)S(1)}, u32[]{:S(2)}, u32[]{:S(2)}) %collective-permute-start.1) | collective-permute-done | bytes 1048608 | tf_op jit(solution)/shard_map/ppermute | solution.py:328
  44.3 6.1 %collective-permute-start.11 = (bf16[2,64,8192]{2,1,0:T(8,128)(2,1)}, bf16[2,64,8192]{2,1,0:T(8,128)(2,1)}, u32[]{:S(2)}, u32[]{:S(2)}) collective-permute-start(bf16[2,64,8192]{2,1,0:T(8,128)(2,1)} %pad_maximum_fusion.rows3_ref), channel_id=1, source_target_pairs={{0,4},{1,5},{2,6},{3,7},{12,8},{13,9},{14,10},{15,11},{16,20},{17,... | collective-permute-start | bytes 6291464 | tf_op jit(solution)/shard_map/ppermute | solution.py:328
  51.7 2.1 collective-permute-start.9
  53.8 9.3 %collective-permute-done.2 = bf16[2,2,16,8192]{3,2,1,0:T(8,128)(2,1)S(1)} collective-permute-done((bf16[2,2,16,8192]{3,2,1,0:T(8,128)(2,1)S(1)}, bf16[2,2,16,8192]{3,2,1,0:T(8,128)(2,1)S(1)}, u32[]{:S(2)}, u32[]{:S(2)}) %collective-permute-start.2) | collective-permute-done | bytes 1048608 | tf_op jit(solution)/shard_map/ppermute | solution.py:328
  69.5 4.1 %shard_map.86 = (bf16[64,8192]{1,0:T(8,128)(2,1)S(1)}, bf16[64,8192]{1,0:T(8,128)(2,1)S(1)}, bf16[64,8192]{1,0:T(8,128)(2,1)S(1)}, bf16[2,64,8192]{2,1,0:T(8,128)(2,1)S(1)}) custom-call(s32[1]{0:T(128)} %bitcast.1.flags_ref, bf16[2,64,8192]{2,1,0:T(8,128)(2,1)} %pad_maximum_fusion.rows3_ref, bf16[2,64,8192]{2,1,0:T(8,128)(2,1)S(1)} %pad_maximum_fusion.1.rows2_ref, ...), custom_call_target="tpu_custom_call" | custom-call | tf_op jit(solution)/shard_map/pallas_call | solution.py:218
  73.6 21.8 %collective-permute-done.11.handed_ref = bf16[2,64,8192]{2,1,0:T(8,128)(2,1)} collective-permute-done((bf16[2,64,8192]{2,1,0:T(8,128)(2,1)}, bf16[2,64,8192]{2,1,0:T(8,128)(2,1)}, u32[]{:S(2)}, u32[]{:S(2)}) %collective-permute-start.11) | collective-permute-done | bytes 2097184 | tf_op jit(solution)/shard_map/ppermute | solution.py:328
  95.4 6.9 %collective-permute-done.8.outer_ref.refs_6_ = bf16[2,64,8192]{2,1,0:T(8,128)(2,1)} collective-permute-done((bf16[2,64,8192]{2,1,0:T(8,128)(2,1)}, bf16[2,64,8192]{2,1,0:T(8,128)(2,1)}, u32[]{:S(2)}, u32[]{:S(2)}) %collective-permute-start.8) | collective-permute-done | bytes 2097184 | tf_op jit(solution)/shard_map/ppermute | solution.py:328
  102.3 5.2 %shard_map.87 = (bf16[64,8192]{1,0:T(8,128)(2,1)S(1)}, bf16[64,8192]{1,0:T(8,128)(2,1)S(1)}, bf16[64,64]{1,0:T(8,128)(2,1)S(1)}, bf16[64,8192]{1,0:T(8,128)(2,1)S(1)}) custom-call(s32[1]{0:T(128)} %bitcast.1.flags_ref, bf16[2,64,8192]{2,1,0:T(8,128)(2,1)S(1)} %get-tuple-element.52.rows_ref, bf16[2,64,8192]{2,1,0:T(8,128)(2,1)} %collective-permute-done.11.handed_ref, ...), custom_call_target="tpu_custom_call" | custom-call | tf_op jit(solution)/shard_map/pallas_call | solution.py:218
  107.5 5.0 %collective-permute-start.12 = (bf16[64,8192]{1,0:T(8,128)(2,1)S(1)}, bf16[64,8192]{1,0:T(8,128)(2,1)S(1)}, u32[]{:S(2)}, u32[]{:S(2)}) collective-permute-start(bf16[64,8192]{1,0:T(8,128)(2,1)S(1)} %get-tuple-element.55), channel_id=1, source_target_pairs={{0,4},{1,5},{2,6},{3,7},{4,0},{5,1},{6,2},{7,3},{8,12},{9,13},{10,... | collective-permute-start | bytes 3145736 | tf_op jit(solution)/shard_map/ppermute | solution.py:328
  113.3 4.6 %collective-permute-start.20 = (bf16[64,8192]{1,0:T(8,128)(2,1)S(1)}, bf16[64,8192]{1,0:T(8,128)(2,1)S(1)}, u32[]{:S(2)}, u32[]{:S(2)}) collective-permute-start(bf16[64,8192]{1,0:T(8,128)(2,1)S(1)} %get-tuple-element.70), channel_id=1, source_target_pairs={{0,4},{1,5},{2,6},{3,7},{12,8},{13,9},{14,10},{15,11},{16,20},{17,... | collective-permute-start | bytes 3145736 | tf_op jit(solution)/shard_map/ppermute | solution.py:328
  120.1 16.0 %collective-permute-done.12.refs_10_ = bf16[64,8192]{1,0:T(8,128)(2,1)S(1)} collective-permute-done((bf16[64,8192]{1,0:T(8,128)(2,1)S(1)}, bf16[64,8192]{1,0:T(8,128)(2,1)S(1)}, u32[]{:S(2)}, u32[]{:S(2)}) %collective-permute-start.12) | collective-permute-done | bytes 1048608 | tf_op jit(solution)/shard_map/ppermute | solution.py:328
  137.2 6.8 %shard_map.88 = (bf16[64,8192]{1,0:T(8,128)(2,1)S(1)}, bf16[64,8192]{1,0:T(8,128)(2,1)S(1)}, bf16[64,8192]{1,0:T(8,128)(2,1)S(1)}, bf16[64,8192]{1,0:T(8,128)(2,...) custom-call(s32[1]{0:T(128)} %bitcast.1.flags_ref, ...), custom_call_target="tpu_custom_call" | custom-call | tf_op jit(solution)/shard_map/pallas_call | solution.py:218
  146.7 7.0 %collective-permute-start.19 = (bf16[64,8192]{1,0:T(8,128)(2,1)S(1)}, bf16[64,8192]{1,0:T(8,128)(2,1)S(1)}, u32[]{:S(2)}, u32[]{:S(2)}) collective-permute-start(bf16[64,8192]{1,0:T(8,128)(2,1)S(1)} %add_convert_fusion.2), channel_id=1, source_target_pairs={{0,4},{1,5},{2,6},{3,7},{4,0},{5,1},{6,2},{7,3},{8,12},{9,13},{10,... | collective-permute-start | bytes 3145736 | tf_op jit(solution)/shard_map/ppermute | solution.py:328
  153.7 14.6 %collective-permute-done.15.refs_2_ = bf16[64,8192]{1,0:T(8,128)(2,1)S(1)} collective-permute-done((bf16[64,8192]{1,0:T(8,128)(2,1)S(1)}, bf16[64,8192]{1,0:T(8,128)(2,1)S(1)}, u32[]{:S(2)}, u32[]{:S(2)}) %collective-permute-start.15) | collective-permute-done | bytes 1048608 | tf_op jit(solution)/shard_map/ppermute | solution.py:328
  170.0 7.0 %collective-permute-start.23 = (bf16[64,8192]{1,0:T(8,128)(2,1)S(1)}, bf16[64,8192]{1,0:T(8,128)(2,1)S(1)}, u32[]{:S(2)}, u32[]{:S(2)}) collective-permute-start(bf16[64,8192]{1,0:T(8,128)(2,1)S(1)} %add_convert_fusion), channel_id=1, source_target_pairs={{0,4},{1,5},{2,6},{3,7},{4,0},{5,1},{6,2},{7,3},{8,12},{9,13},{10,... | collective-permute-start | bytes 3145736 | tf_op jit(solution)/shard_map/ppermute | solution.py:328
  178.3 9.4 %collective-permute-done.16 = bf16[64,8192]{1,0:T(8,128)(2,1)S(1)} collective-permute-done((bf16[64,8192]{1,0:T(8,128)(2,1)S(1)}, bf16[64,8192]{1,0:T(8,128)(2,1)S(1)}, u32[]{:S(2)}, u32[]{:S(2)}) %collective-permute-start.16) | collective-permute-done | bytes 1048608 | tf_op jit(solution)/shard_map/ppermute | solution.py:328
  188.2 12.3 %collective-permute-done.23.refs_1_ = bf16[64,8192]{1,0:T(8,128)(2,1)S(1)} collective-permute-done((bf16[64,8192]{1,0:T(8,128)(2,1)S(1)}, bf16[64,8192]{1,0:T(8,128)(2,1)S(1)}, u32[]{:S(2)}, u32[]{:S(2)}) %collective-permute-start.23) | collective-permute-done | bytes 1048608 | tf_op jit(solution)/shard_map/ppermute | solution.py:328
  203.2 2.4 %shard_map.89.refs_4_ = bf16[128,8192]{1,0:T(8,128)(2,1)} custom-call(bf16[128,256]{1,0:T(8,128)(2,1)S(1)} %fusion.place_ref, bf16[64,8192]{1,0:T(8,128)(2,1)} %copy-done.4, bf16[64,8192]{1,0:T(8,128)(2,1)S(1)} %collective-permute-done.14.refs_1_, bf16[64,8192]{1,0:T(8,128)(2,1)S(1)} %collective-permute-done.15.refs_2_, ...), custom_call_target="tpu_custom_call" | custom-call | tf_op jit(solution)/shard_map/pallas_call | solution.py:128
  205.8 4.4 %collective-permute-start.27 = (f32[8,128]{1,0:T(8,128)S(1)}, f32[8,128]{1,0:T(8,128)S(1)}, u32[]{:S(2)}, u32[]{:S(2)}) collective-permute-start(f32[8,128]{1,0:T(8,128)S(1)} %add_add_fusion.refs_2_), channel_id=1, source_target_pairs={{0,4},{1,5},{2,6},{3,7},{4,0},{5,1},{6,2},{7,3},{8,12},{9,13},{10,... | collective-permute-start | bytes 12296 | tf_op jit(solution)/shard_map/ppermute | solution.py:328
  212.6 2.4 %shard_map.90 = bf16[128,8192]{1,0:T(8,128)(2,1)} custom-call(bf16[128,256]{1,0:T(8,128)(2,1)S(1)} %fusion.place_ref, bf16[64,8192]{1,0:T(8,128)(2,1)} %copy-done.4, bf16[64,8192]{1,0:T(8,128)(2,1)S(1)} %collective-permute-done.14.refs_1_, bf16[64,8192]{1,0:T(8,128)(2,1)S(1)} %collective-permute-done.15.refs_2_, ...), custom_call_target="tpu_custom_call", output_to_operand_aliasing={{}: (5, {})} | custom-call | tf_op jit(solution)/shard_map/pallas_call | solution.py:128
  216.2 2.3 %shard_map.93 = (f32[1,64,8192]{2,1,0:T(8,128)}, f32[1,64,8192]{2,1,0:T(8,128)}) custom-call(f32[64,8192]{1,0:T(8,128)S(1)} %get-tuple-element.67.refs_0_, f32[64,8192]{1,0:T(8,128)S(1)} %get-tuple-element.74.refs_1_, f32[8,128]{1,0:T(8,128)S(1)} %add_add_fusion.refs_2_, f32[8,128]{1,0:T(8,128)S(1)} %collective-permute-done.27.refs_3_, ...), custom_call_target="tpu_custom_call" | custom-call | tf_op jit(solution)/shard_map/pallas_call | solution.py:183
  (83 shorter events, 33.2 us)
Async XLA Ops:
  2.4 49.3 %collective-permute-start.6 = (bf16[2,64,8192]{2,1,0:T(8,128)(2,1)S(1)}, bf16[2,64,8192]{2,1,0:T(8,128)(2,1)}, u32[]{:S(2)}, u32[]{:S(2)}) collective-permute-start(bf16[2,64,8192]{2,1,0:T(8,128)(2,1)S(1)} %pad_maximum_fusion.2.refs_5_), channel_id=1, source_target_pairs={{0,4},{1,5},{2,6},{3,7},{4,0},{5,1},{6,2},{7,3},{8,12},{9,13},{10,... | collective-permute-start | bytes 6291464 | tf_op jit(solution)/shard_map/ppermute | solution.py:328
  5.5 44.9 %collective-permute-start.7 = (bf16[2,64,8192]{2,1,0:T(8,128)(2,1)S(1)}, bf16[2,64,8192]{2,1,0:T(8,128)(2,1)}, u32[]{:S(2)}, u32[]{:S(2)}) collective-permute-start(bf16[2,64,8192]{2,1,0:T(8,128)(2,1)S(1)} %pad_maximum_fusion.2.refs_5_), channel_id=1, source_target_pairs={{4,8},{5,9},{6,10},{7,11},{8,4},{9,5},{10,6},{11,7},{20,24},{21,25... | collective-permute-start | bytes 6291464 | tf_op jit(solution)/shard_map/ppermute | solution.py:328
  14.6 24.7 %collective-permute-start.1 = (bf16[2,2,16,8192]{3,2,1,0:T(8,128)(2,1)S(1)}, bf16[2,2,16,8192]{3,2,1,0:T(8,128)(2,1)S(1)}, u32[]{:S(2)}, u32[]{:S(2)}) collective-permute-start(bf16[2,2,16,8192]{3,2,1,0:T(8,128)(2,1)S(1)} %get-tuple-element.49), channel_id=1, source_target_pairs={{0,2},{1,3},{2,0},{3,1},{4,6},{5,7},{6,4},{7,5},{8,10},{9,11},{10,... | collective-permute-start | bytes 3145736 | tf_op jit(solution)/shard_map/ppermute | solution.py:328
  16.1 24.8 %collective-permute-start = (bf16[1,2,64,8192]{3,2,1,0:T(8,128)(2,1)S(1)}, bf16[1,2,64,8192]{3,2,1,0:T(8,128)(2,1)S(1)}, u32[]{:S(2)}, u32[]{:S(2)}) collective-permute-start(bf16[1,2,64,8192]{3,2,1,0:T(8,128)(2,1)S(1)} %get-tuple-element.46), channel_id=1, source_target_pairs={{0,1},{1,0},{2,3},{3,2},{4,5},{5,4},{6,7},{7,6},{8,9},{9,8},{10,11... | collective-permute-start | bytes 6291464 | tf_op jit(solution)/shard_map/ppermute | solution.py:328
  39.2 23.8 %collective-permute-start.2 = (bf16[2,2,16,8192]{3,2,1,0:T(8,128)(2,1)S(1)}, bf16[2,2,16,8192]{3,2,1,0:T(8,128)(2,1)S(1)}, u32[]{:S(2)}, u32[]{:S(2)}) collective-permute-start(bf16[2,2,16,8192]{3,2,1,0:T(8,128)(2,1)S(1)} %get-tuple-element.50), channel_id=1, source_target_pairs={{0,2},{1,3},{2,0},{3,1},{4,6},{5,7},{6,4},{7,5},{8,10},{9,11},{10,... | collective-permute-start | bytes 3145736 | tf_op jit(solution)/shard_map/ppermute | solution.py:328
  44.3 51.1 %collective-permute-start.11 = (bf16[2,64,8192]{2,1,0:T(8,128)(2,1)}, bf16[2,64,8192]{2,1,0:T(8,128)(2,1)}, u32[]{:S(2)}, u32[]{:S(2)}) collective-permute-start(bf16[2,64,8192]{2,1,0:T(8,128)(2,1)} %pad_maximum_fusion.rows3_ref), channel_id=1, source_target_pairs={{0,4},{1,5},{2,6},{3,7},{12,8},{13,9},{14,10},{15,11},{16,20},{17,... | collective-permute-start | bytes 6291464 | tf_op jit(solution)/shard_map/ppermute | solution.py:328
  50.4 51.9 %collective-permute-start.8 = (bf16[2,64,8192]{2,1,0:T(8,128)(2,1)}, bf16[2,64,8192]{2,1,0:T(8,128)(2,1)}, u32[]{:S(2)}, u32[]{:S(2)}) collective-permute-start(bf16[2,64,8192]{2,1,0:T(8,128)(2,1)} %collective-permute-done.7.crossed_ref), channel_id=1, source_target_pairs={{4,0},{5,1},{6,2},{7,3},{8,12},{9,13},{10,14},{11,15},{20,16},{21,... | collective-permute-start | bytes 6291464 | tf_op jit(solution)/shard_map/ppermute | solution.py:328
  51.7 50.6 %collective-permute-start.9 = (bf16[2,64,8192]{2,1,0:T(8,128)(2,1)}, bf16[2,64,8192]{2,1,0:T(8,128)(2,1)}, u32[]{:S(2)}, u32[]{:S(2)}) collective-permute-start(bf16[2,64,8192]{2,1,0:T(8,128)(2,1)} %collective-permute-done.6.refs_4_), channel_id=1, source_target_pairs={{4,8},{5,9},{6,10},{7,11},{8,4},{9,5},{10,6},{11,7},{20,24},{21,25... | collective-permute-start | bytes 6291464 | tf_op jit(solution)/shard_map/ppermute | solution.py:328
  66.7 51.9 %collective-permute-start.4 = (bf16[2,2,32,8192]{3,2,1,0:T(8,128)(2,1)}, bf16[2,2,32,8192]{3,2,1,0:T(8,128)(2,1)}, u32[]{:S(2)}, u32[]{:S(2)}) collective-permute-start(bf16[2,2,32,8192]{3,2,1,0:T(8,128)(2,1)} %get-tuple-element.51), channel_id=1, source_target_pairs={{0,2},{1,3},{2,0},{3,1},{4,6},{5,7},{6,4},{7,5},{8,10},{9,11},{10,... | collective-permute-start | bytes 6291464 | tf_op jit(solution)/shard_map/ppermute | solution.py:328
  107.5 28.7 %collective-permute-start.12 = (bf16[64,8192]{1,0:T(8,128)(2,1)S(1)}, bf16[64,8192]{1,0:T(8,128)(2,1)S(1)}, u32[]{:S(2)}, u32[]{:S(2)}) collective-permute-start(bf16[64,8192]{1,0:T(8,128)(2,1)S(1)} %get-tuple-element.55), channel_id=1, source_target_pairs={{0,4},{1,5},{2,6},{3,7},{4,0},{5,1},{6,2},{7,3},{8,12},{9,13},{10,... | collective-permute-start | bytes 3145736 | tf_op jit(solution)/shard_map/ppermute | solution.py:328
  112.5 23.6 %collective-permute-start.13 = (bf16[64,8192]{1,0:T(8,128)(2,1)S(1)}, bf16[64,8192]{1,0:T(8,128)(2,1)S(1)}, u32[]{:S(2)}, u32[]{:S(2)}) collective-permute-start(bf16[64,8192]{1,0:T(8,128)(2,1)S(1)} %get-tuple-element.56), channel_id=1, source_target_pairs={{4,8},{5,9},{6,10},{7,11},{8,4},{9,5},{10,6},{11,7},{20,24},{21,25... | collective-permute-start | bytes 3145736 | tf_op jit(solution)/shard_map/ppermute | solution.py:328
  113.3 56.6 %collective-permute-start.20 = (bf16[64,8192]{1,0:T(8,128)(2,1)S(1)}, bf16[64,8192]{1,0:T(8,128)(2,1)S(1)}, u32[]{:S(2)}, u32[]{:S(2)}) collective-permute-start(bf16[64,8192]{1,0:T(8,128)(2,1)S(1)} %get-tuple-element.70), channel_id=1, source_target_pairs={{0,4},{1,5},{2,6},{3,7},{12,8},{13,9},{14,10},{15,11},{16,20},{17,... | collective-permute-start | bytes 3145736 | tf_op jit(solution)/shard_map/ppermute | solution.py:328
  117.8 52.0 %collective-permute-start.21 = (bf16[64,8192]{1,0:T(8,128)(2,1)S(1)}, bf16[64,8192]{1,0:T(8,128)(2,1)S(1)}, u32[]{:S(2)}, u32[]{:S(2)}) collective-permute-start(bf16[64,8192]{1,0:T(8,128)(2,1)S(1)} %get-tuple-element.70), channel_id=1, source_target_pairs={{4,8},{5,9},{6,10},{7,11},{8,4},{9,5},{10,6},{11,7},{20,24},{21,25... | collective-permute-start | bytes 3145736 | tf_op jit(solution)/shard_map/ppermute | solution.py:328
  120.1 17.1 %collective-permute-start.5 = (bf16[1,2,32,8192]{3,2,1,0:T(8,128)(2,1)S(1)}, bf16[1,2,32,8192]{3,2,1,0:T(8,128)(2,1)S(1)}, u32[]{:S(2)}, u32[]{:S(2)}) collective-permute-start(bf16[1,2,32,8192]{3,2,1,0:T(8,128)(2,1)S(1)} %slice.38), channel_id=1, source_target_pairs={{0,1},{1,0},{2,3},{3,2},{4,5},{5,4},{6,7},{7,6},{8,9},{9,8},{10,11... | collective-permute-start | bytes 3145736 | tf_op jit(solution)/shard_map/ppermute | solution.py:328
  136.4 41.8 %collective-permute-start.18 = (bf16[64,8192]{1,0:T(8,128)(2,1)S(1)}, bf16[64,8192]{1,0:T(8,128)(2,1)S(1)}, u32[]{:S(2)}, u32[]{:S(2)}) collective-permute-start(bf16[64,8192]{1,0:T(8,128)(2,1)S(1)} %add_convert_fusion.3), channel_id=1, source_target_pairs={{4,8},{5,9},{6,10},{7,11},{8,4},{9,5},{10,6},{11,7},{20,24},{21,25... | collective-permute-start | bytes 3145736 | tf_op jit(solution)/shard_map/ppermute | solution.py:328
  145.0 23.3 %collective-permute-start.15 = (bf16[64,8192]{1,0:T(8,128)(2,1)S(1)}, bf16[64,8192]{1,0:T(8,128)(2,1)S(1)}, u32[]{:S(2)}, u32[]{:S(2)}) collective-permute-start(bf16[64,8192]{1,0:T(8,128)(2,1)S(1)} %get-tuple-element.60), channel_id=1, source_target_pairs={{0,2},{1,3},{2,0},{3,1},{4,6},{5,7},{6,4},{7,5},{8,10},{9,11},{10,... | collective-permute-start | bytes 3145736 | tf_op jit(solution)/shard_map/ppermute | solution.py:328
  146.7 41.0 %collective-permute-start.19 = (bf16[64,8192]{1,0:T(8,128)(2,1)S(1)}, bf16[64,8192]{1,0:T(8,128)(2,1)S(1)}, u32[]{:S(2)}, u32[]{:S(2)}) collective-permute-start(bf16[64,8192]{1,0:T(8,128)(2,1)S(1)} %add_convert_fusion.2), channel_id=1, source_target_pairs={{0,4},{1,5},{2,6},{3,7},{4,0},{5,1},{6,2},{7,3},{8,12},{9,13},{10,... | collective-permute-start | bytes 3145736 | tf_op jit(solution)/shard_map/ppermute | solution.py:328
  168.3 19.3 %collective-permute-start.16 = (bf16[64,8192]{1,0:T(8,128)(2,1)S(1)}, bf16[64,8192]{1,0:T(8,128)(2,1)S(1)}, u32[]{:S(2)}, u32[]{:S(2)}) collective-permute-start(bf16[64,8192]{1,0:T(8,128)(2,1)S(1)} %get-tuple-element.62), channel_id=1, source_target_pairs={{0,2},{1,3},{2,0},{3,1},{4,6},{5,7},{6,4},{7,5},{8,10},{9,11},{10,... | collective-permute-start | bytes 3145736 | tf_op jit(solution)/shard_map/ppermute | solution.py:328
  170.0 30.6 %collective-permute-start.23 = (bf16[64,8192]{1,0:T(8,128)(2,1)S(1)}, bf16[64,8192]{1,0:T(8,128)(2,1)S(1)}, u32[]{:S(2)}, u32[]{:S(2)}) collective-permute-start(bf16[64,8192]{1,0:T(8,128)(2,1)S(1)} %add_convert_fusion), channel_id=1, source_target_pairs={{0,4},{1,5},{2,6},{3,7},{4,0},{5,1},{6,2},{7,3},{8,12},{9,13},{10,... | collective-permute-start | bytes 3145736 | tf_op jit(solution)/shard_map/ppermute | solution.py:328
  177.3 23.3 %collective-permute-start.22 = (bf16[64,8192]{1,0:T(8,128)(2,1)S(1)}, bf16[64,8192]{1,0:T(8,128)(2,1)S(1)}, u32[]{:S(2)}, u32[]{:S(2)}) collective-permute-start(bf16[64,8192]{1,0:T(8,128)(2,1)S(1)} %add_convert_fusion.1), channel_id=1, source_target_pairs={{4,8},{5,9},{6,10},{7,11},{8,4},{9,5},{10,6},{11,7},{20,24},{21,25... | collective-permute-start | bytes 3145736 | tf_op jit(solution)/shard_map/ppermute | solution.py:328
  178.2 24.9 %collective-permute-start.14 = (bf16[64,8192]{1,0:T(8,128)(2,1)S(1)}, bf16[64,8192]{1,0:T(8,128)(2,1)S(1)}, u32[]{:S(2)}, u32[]{:S(2)}) collective-permute-start(bf16[64,8192]{1,0:T(8,128)(2,1)S(1)} %get-tuple-element.59), channel_id=1, source_target_pairs={{0,1},{1,0},{2,3},{3,2},{4,5},{5,4},{6,7},{7,6},{8,9},{9,8},{10,11... | collective-permute-start | bytes 3145736 | tf_op jit(solution)/shard_map/ppermute | solution.py:328
  187.7 15.5 %collective-permute-start.17 = (bf16[64,8192]{1,0:T(8,128)(2,1)S(1)}, bf16[64,8192]{1,0:T(8,128)(2,1)S(1)}, u32[]{:S(2)}, u32[]{:S(2)}) collective-permute-start(bf16[64,8192]{1,0:T(8,128)(2,1)S(1)} %collective-permute-done.16), channel_id=1, source_target_pairs={{0,1},{1,0},{2,3},{3,2},{4,5},{5,4},{6,7},{7,6},{8,9},{9,8},{10,11... | collective-permute-start | bytes 3145736 | tf_op jit(solution)/shard_map/ppermute | solution.py:328
  205.8 9.2 %collective-permute-start.27 = (f32[8,128]{1,0:T(8,128)S(1)}, f32[8,128]{1,0:T(8,128)S(1)}, u32[]{:S(2)}, u32[]{:S(2)}) collective-permute-start(f32[8,128]{1,0:T(8,128)S(1)} %add_add_fusion.refs_2_), channel_id=1, source_target_pairs={{0,4},{1,5},{2,6},{3,7},{4,0},{5,1},{6,2},{7,3},{8,12},{9,13},{10,... | collective-permute-start | bytes 12296 | tf_op jit(solution)/shard_map/ppermute | solution.py:328
  210.8 5.4 %collective-permute-start.29 = (f32[8,128]{1,0:T(8,128)S(1)}, f32[8,128]{1,0:T(8,128)S(1)}, u32[]{:S(2)}, u32[]{:S(2)}) collective-permute-start(f32[8,128]{1,0:T(8,128)S(1)} %add_add_fusion.refs_2_), channel_id=1, source_target_pairs={{0,12},{1,13},{2,14},{3,15},{4,8},{5,9},{6,10},{7,11},{8,4},{9,5},... | collective-permute-start | bytes 12296 | tf_op jit(solution)/shard_map/ppermute | solution.py:328
  (14 other events, 99.3 us)

commit v21 on v19

--- a/solution.py
+++ b/solution.py
@@ -200,7 +200,7 @@
 
 def far_sums(tokens, factor, up_ref, down_ref, dx_ref, inner_ref=None):
     rank, width = up_ref.shape
-    tile = min(width, 2048)
+    tile = min(width, 4096)
     cuts = [pl.ds(i * tile, tile) for i in range(width // tile)]
     hidden, inner = (sum(dot32(tokens(k, cut), factor(k, cut), ROWS_OF) for cut in cuts) for k in range(2))
     hidden_t, inner_t, inner = hidden.T.astype(BF16), inner.T.astype(BF16), inner.astype(BF16)
@@ -410,7 +410,7 @@
     raw_up, up_squares = final_sum(up0, up2, up1)
     part = down_squares + up_squares
     part = part + sum(after([send(part, beside(m)) for m in range(1, plane)], half_acts))
-    along = [[(i, (i // plane ^ m) * plane + i % plane) for i in range(ndevices)] for m in range(1, 4)]
+    along = [[(i, (i // plane ^ m) * plane + i % plane) for i in range(ndevices)] for m in (3, 2, 1)]
     parts = after([send(part, pairs) for pairs in along], grad_acts)
     return (grad_acts, *scaled((raw_down, raw_up), (part, *parts), ndevices))
 

time: 218 us -> 217 us (level)
  no operation moved by 1% of the time
where the time goes in v21:
time: 217 us; the launch traced here: 216 us
  waiting for transfers between devices  116 us (53%)
  starting transfers between devices  56.6 us (26%)
  Pallas kernels  30.6 us (14%)
  other arithmetic  6.23 us (3%)
  local copies, waits for them, and re-layouts  5.63 us (3%)
    ppermute x30, waiting for transfers between devices, send(): return lax.ppermute(array, 'dp', pairs)  116 us
    ppermute x30, starting transfers between devices, send(): return lax.ppermute(array, 'dp', pairs)  56.6 us
    pallas_call x5, Pallas kernels, in_place(): pl.pallas_call(body, in_specs=[pl.BlockSpec(memory_space=pltpu.SMEM)] * l...  17.2 us
    pallas_call x1, Pallas kernels, pack(): pl.pallas_call(body, grid=(tiles,), in_specs=[pl.BlockSpec(place.shape, l...  6.36 us
    pallas_call x2, Pallas kernels, unpack(): pl.pallas_call(body, grid=(width // 2 // tile,), in_specs=[pl.BlockSpec(p...  4.79 us
  transfers between devices with their start and end apart: 30, of which 13 were waited for; matrix products, arithmetic and copies ran while one was open for 3% of the time, Pallas kernels for 13%

profile of v21, /device:TPU:0, one launch (start us, length us, event | category | flops | bytes accessed | tf_op | source)
XLA Modules:
  0.0 216.4 jit_solution(16982115732407268510)
XLA Ops:
  4.4 4.6 %collective-permute-start.6 = (bf16[2,64,8192]{2,1,0:T(8,128)(2,1)S(1)}, bf16[2,64,8192]{2,1,0:T(8,128)(2,1)}, u32[]{:S(2)}, u32[]{:S(2)}) collective-permute-start(bf16[2,64,8192]{2,1,0:T(8,128)(2,1)S(1)} %pad_maximum_fusion.2.refs_5_), channel_id=1, source_target_pairs={{0,4},{1,5},{2,6},{3,7},{4,0},{5,1},{6,2},{7,3},{8,12},{9,13},{10,... | collective-permute-start | bytes 6291464 | tf_op jit(solution)/shard_map/ppermute | solution.py:328
  9.7 6.4 %shard_map.85 = (bf16[1,2,64,8192]{3,2,1,0:T(8,128)(2,1)S(1)}, bf16[1,2,64,8192]{3,2,1,0:T(8,128)(2,1)S(1)}, bf16[2,2,16,8192]{3,2,1,0:T(8,128)(2,1)S(1)}, bf16[...) custom-call(bf16[256,128]{1,0:T(8,128)(2,1)S(1)} %fusion.1.place_ref, bf16[128,8192]{1,0:T(8,128)(2,1)} %x_in.1, ...), custom_call_target="tpu_custom_call" | custom-call | tf_op jit(solution)/shard_map/pallas_call | solution.py:107
  17.7 22.8 %collective-permute-done.1 = bf16[2,2,16,8192]{3,2,1,0:T(8,128)(2,1)S(1)} collective-permute-done((bf16[2,2,16,8192]{3,2,1,0:T(8,128)(2,1)S(1)}, bf16[2,2,16,8192]{3,2,1,0:T(8,128)(2,1)S(1)}, u32[]{:S(2)}, u32[]{:S(2)}) %collective-permute-start.1) | collective-permute-done | bytes 1048608 | tf_op jit(solution)/shard_map/ppermute | solution.py:328
  45.5 3.6 %collective-permute-start.11 = (bf16[2,64,8192]{2,1,0:T(8,128)(2,1)}, bf16[2,64,8192]{2,1,0:T(8,128)(2,1)}, u32[]{:S(2)}, u32[]{:S(2)}) collective-permute-start(bf16[2,64,8192]{2,1,0:T(8,128)(2,1)} %pad_maximum_fusion.rows3_ref), channel_id=1, source_target_pairs={{0,4},{1,5},{2,6},{3,7},{12,8},{13,9},{14,10},{15,11},{16,20},{17,... | collective-permute-start | bytes 6291464 | tf_op jit(solution)/shard_map/ppermute | solution.py:328
  50.4 4.6 %collective-permute-done.6.refs_4_ = bf16[2,64,8192]{2,1,0:T(8,128)(2,1)} collective-permute-done((bf16[2,64,8192]{2,1,0:T(8,128)(2,1)S(1)}, bf16[2,64,8192]{2,1,0:T(8,128)(2,1)}, u32[]{:S(2)}, u32[]{:S(2)}) %collective-permute-start.6) | collective-permute-done | bytes 2097184 | tf_op jit(solution)/shard_map/ppermute | solution.py:328
  57.1 6.9 %collective-permute-done.2 = bf16[2,2,16,8192]{3,2,1,0:T(8,128)(2,1)S(1)} collective-permute-done((bf16[2,2,16,8192]{3,2,1,0:T(8,128)(2,1)S(1)}, bf16[2,2,16,8192]{3,2,1,0:T(8,128)(2,1)S(1)}, u32[]{:S(2)}, u32[]{:S(2)}) %collective-permute-start.2) | collective-permute-done | bytes 1048608 | tf_op jit(solution)/shard_map/ppermute | solution.py:328
  70.4 4.1 %shard_map.86 = (bf16[64,8192]{1,0:T(8,128)(2,1)S(1)}, bf16[64,8192]{1,0:T(8,128)(2,1)S(1)}, bf16[64,8192]{1,0:T(8,128)(2,1)S(1)}, bf16[2,64,8192]{2,1,0:T(8,128)(2,1)S(1)}) custom-call(s32[1]{0:T(128)} %bitcast.1.flags_ref, bf16[2,64,8192]{2,1,0:T(8,128)(2,1)} %pad_maximum_fusion.rows3_ref, bf16[2,64,8192]{2,1,0:T(8,128)(2,1)S(1)} %pad_maximum_fusion.1.rows2_ref, ...), custom_call_target="tpu_custom_call" | custom-call | tf_op jit(solution)/shard_map/pallas_call | solution.py:218
  74.6 24.1 %collective-permute-done.11.handed_ref = bf16[2,64,8192]{2,1,0:T(8,128)(2,1)} collective-permute-done((bf16[2,64,8192]{2,1,0:T(8,128)(2,1)}, bf16[2,64,8192]{2,1,0:T(8,128)(2,1)}, u32[]{:S(2)}, u32[]{:S(2)}) %collective-permute-start.11) | collective-permute-done | bytes 2097184 | tf_op jit(solution)/shard_map/ppermute | solution.py:328
  98.6 2.5 %collective-permute-done.8.outer_ref.refs_6_ = bf16[2,64,8192]{2,1,0:T(8,128)(2,1)} collective-permute-done((bf16[2,64,8192]{2,1,0:T(8,128)(2,1)}, bf16[2,64,8192]{2,1,0:T(8,128)(2,1)}, u32[]{:S(2)}, u32[]{:S(2)}) %collective-permute-start.8) | collective-permute-done | bytes 2097184 | tf_op jit(solution)/shard_map/ppermute | solution.py:328
  101.1 5.2 %shard_map.87 = (bf16[64,8192]{1,0:T(8,128)(2,1)S(1)}, bf16[64,8192]{1,0:T(8,128)(2,1)S(1)}, bf16[64,64]{1,0:T(8,128)(2,1)S(1)}, bf16[64,8192]{1,0:T(8,128)(2,1)S(1)}) custom-call(s32[1]{0:T(128)} %bitcast.1.flags_ref, bf16[2,64,8192]{2,1,0:T(8,128)(2,1)S(1)} %get-tuple-element.50.rows_ref, bf16[2,64,8192]{2,1,0:T(8,128)(2,1)} %collective-permute-done.11.handed_ref, ...), custom_call_target="tpu_custom_call" | custom-call | tf_op jit(solution)/shard_map/pallas_call | solution.py:218
  106.3 5.0 %collective-permute-start.12 = (bf16[64,8192]{1,0:T(8,128)(2,1)S(1)}, bf16[64,8192]{1,0:T(8,128)(2,1)S(1)}, u32[]{:S(2)}, u32[]{:S(2)}) collective-permute-start(bf16[64,8192]{1,0:T(8,128)(2,1)S(1)} %get-tuple-element.53), channel_id=1, source_target_pairs={{0,4},{1,5},{2,6},{3,7},{4,0},{5,1},{6,2},{7,3},{8,12},{9,13},{10,... | collective-permute-start | bytes 3145736 | tf_op jit(solution)/shard_map/ppermute | solution.py:328
  112.1 4.8 %collective-permute-start.20 = (bf16[64,8192]{1,0:T(8,128)(2,1)S(1)}, bf16[64,8192]{1,0:T(8,128)(2,1)S(1)}, u32[]{:S(2)}, u32[]{:S(2)}) collective-permute-start(bf16[64,8192]{1,0:T(8,128)(2,1)S(1)} %get-tuple-element.68), channel_id=1, source_target_pairs={{0,4},{1,5},{2,6},{3,7},{12,8},{13,9},{14,10},{15,11},{16,20},{17,... | collective-permute-start | bytes 3145736 | tf_op jit(solution)/shard_map/ppermute | solution.py:328
  119.1 15.8 %collective-permute-done.12.refs_10_ = bf16[64,8192]{1,0:T(8,128)(2,1)S(1)} collective-permute-done((bf16[64,8192]{1,0:T(8,128)(2,1)S(1)}, bf16[64,8192]{1,0:T(8,128)(2,1)S(1)}, u32[]{:S(2)}, u32[]{:S(2)}) %collective-permute-start.12) | collective-permute-done | bytes 1048608 | tf_op jit(solution)/shard_map/ppermute | solution.py:328
  136.0 6.8 %shard_map.88 = (bf16[64,8192]{1,0:T(8,128)(2,1)S(1)}, bf16[64,8192]{1,0:T(8,128)(2,1)S(1)}, bf16[64,8192]{1,0:T(8,128)(2,1)S(1)}, bf16[64,8192]{1,0:T(8,128)(2,...) custom-call(s32[1]{0:T(128)} %bitcast.1.flags_ref, ...), custom_call_target="tpu_custom_call" | custom-call | tf_op jit(solution)/shard_map/pallas_call | solution.py:218
  145.5 7.2 %collective-permute-start.19 = (bf16[64,8192]{1,0:T(8,128)(2,1)S(1)}, bf16[64,8192]{1,0:T(8,128)(2,1)S(1)}, u32[]{:S(2)}, u32[]{:S(2)}) collective-permute-start(bf16[64,8192]{1,0:T(8,128)(2,1)S(1)} %add_convert_fusion.2), channel_id=1, source_target_pairs={{0,4},{1,5},{2,6},{3,7},{4,0},{5,1},{6,2},{7,3},{8,12},{9,13},{10,... | collective-permute-start | bytes 3145736 | tf_op jit(solution)/shard_map/ppermute | solution.py:328
  152.7 14.5 %collective-permute-done.15.refs_2_ = bf16[64,8192]{1,0:T(8,128)(2,1)S(1)} collective-permute-done((bf16[64,8192]{1,0:T(8,128)(2,1)S(1)}, bf16[64,8192]{1,0:T(8,128)(2,1)S(1)}, u32[]{:S(2)}, u32[]{:S(2)}) %collective-permute-start.15) | collective-permute-done | bytes 1048608 | tf_op jit(solution)/shard_map/ppermute | solution.py:328
  168.8 7.2 %collective-permute-start.23 = (bf16[64,8192]{1,0:T(8,128)(2,1)S(1)}, bf16[64,8192]{1,0:T(8,128)(2,1)S(1)}, u32[]{:S(2)}, u32[]{:S(2)}) collective-permute-start(bf16[64,8192]{1,0:T(8,128)(2,1)S(1)} %add_convert_fusion), channel_id=1, source_target_pairs={{0,4},{1,5},{2,6},{3,7},{4,0},{5,1},{6,2},{7,3},{8,12},{9,13},{10,... | collective-permute-start | bytes 3145736 | tf_op jit(solution)/shard_map/ppermute | solution.py:328
  177.3 8.9 %collective-permute-done.16 = bf16[64,8192]{1,0:T(8,128)(2,1)S(1)} collective-permute-done((bf16[64,8192]{1,0:T(8,128)(2,1)S(1)}, bf16[64,8192]{1,0:T(8,128)(2,1)S(1)}, u32[]{:S(2)}, u32[]{:S(2)}) %collective-permute-start.16) | collective-permute-done | bytes 1048608 | tf_op jit(solution)/shard_map/ppermute | solution.py:328
  186.7 12.5 %collective-permute-done.23.refs_1_ = bf16[64,8192]{1,0:T(8,128)(2,1)S(1)} collective-permute-done((bf16[64,8192]{1,0:T(8,128)(2,1)S(1)}, bf16[64,8192]{1,0:T(8,128)(2,1)S(1)}, u32[]{:S(2)}, u32[]{:S(2)}) %collective-permute-start.23) | collective-permute-done | bytes 1048608 | tf_op jit(solution)/shard_map/ppermute | solution.py:328
  201.8 2.4 %shard_map.89.refs_4_ = bf16[128,8192]{1,0:T(8,128)(2,1)} custom-call(bf16[128,256]{1,0:T(8,128)(2,1)S(1)} %fusion.place_ref, bf16[64,8192]{1,0:T(8,128)(2,1)} %copy-done.4, bf16[64,8192]{1,0:T(8,128)(2,1)S(1)} %collective-permute-done.14.refs_1_, bf16[64,8192]{1,0:T(8,128)(2,1)S(1)} %collective-permute-done.15.refs_2_, ...), custom_call_target="tpu_custom_call" | custom-call | tf_op jit(solution)/shard_map/pallas_call | solution.py:128
  204.4 2.7 %collective-permute-start.27 = (f32[8,128]{1,0:T(8,128)S(1)}, f32[8,128]{1,0:T(8,128)S(1)}, u32[]{:S(2)}, u32[]{:S(2)}) collective-permute-start(f32[8,128]{1,0:T(8,128)S(1)} %add_add_fusion.refs_2_), channel_id=1, source_target_pairs={{0,12},{1,13},{2,14},{3,15},{4,8},{5,9},{6,10},{7,11},{8,4},{9,5},... | collective-permute-start | bytes 12296 | tf_op jit(solution)/shard_map/ppermute | solution.py:328
  207.1 3.2 %collective-permute-start.28 = (f32[8,128]{1,0:T(8,128)S(1)}, f32[8,128]{1,0:T(8,128)S(1)}, u32[]{:S(2)}, u32[]{:S(2)}) collective-permute-start(f32[8,128]{1,0:T(8,128)S(1)} %add_add_fusion.refs_2_), channel_id=1, source_target_pairs={{0,8},{1,9},{2,10},{3,11},{4,12},{5,13},{6,14},{7,15},{8,0},{9,1},... | collective-permute-start | bytes 12296 | tf_op jit(solution)/shard_map/ppermute | solution.py:328
  210.6 2.4 %shard_map.90 = bf16[128,8192]{1,0:T(8,128)(2,1)} custom-call(bf16[128,256]{1,0:T(8,128)(2,1)S(1)} %fusion.place_ref, bf16[64,8192]{1,0:T(8,128)(2,1)} %copy-done.4, bf16[64,8192]{1,0:T(8,128)(2,1)S(1)} %collective-permute-done.14.refs_1_, bf16[64,8192]{1,0:T(8,128)(2,1)S(1)} %collective-permute-done.15.refs_2_, ...), custom_call_target="tpu_custom_call", output_to_operand_aliasing={{}: (5, {})} | custom-call | tf_op jit(solution)/shard_map/pallas_call | solution.py:128
  213.9 2.3 %shard_map.93 = (f32[1,64,8192]{2,1,0:T(8,128)}, f32[1,64,8192]{2,1,0:T(8,128)}) custom-call(f32[64,8192]{1,0:T(8,128)S(1)} %get-tuple-element.65.refs_0_, f32[64,8192]{1,0:T(8,128)S(1)} %get-tuple-element.72.refs_1_, f32[8,128]{1,0:T(8,128)S(1)} %add_add_fusion.refs_2_, f32[8,128]{1,0:T(8,128)S(1)} %collective-permute-done.27.refs_3_, ...), custom_call_target="tpu_custom_call" | custom-call | tf_op jit(solution)/shard_map/pallas_call | solution.py:183
  (83 shorter events, 34.9 us)
Async XLA Ops:
  2.4 46.7 %collective-permute-start.7 = (bf16[2,64,8192]{2,1,0:T(8,128)(2,1)S(1)}, bf16[2,64,8192]{2,1,0:T(8,128)(2,1)}, u32[]{:S(2)}, u32[]{:S(2)}) collective-permute-start(bf16[2,64,8192]{2,1,0:T(8,128)(2,1)S(1)} %pad_maximum_fusion.2.refs_5_), channel_id=1, source_target_pairs={{4,8},{5,9},{6,10},{7,11},{8,4},{9,5},{10,6},{11,7},{20,24},{21,25... | collective-permute-start | bytes 6291464 | tf_op jit(solution)/shard_map/ppermute | solution.py:328
  4.4 50.7 %collective-permute-start.6 = (bf16[2,64,8192]{2,1,0:T(8,128)(2,1)S(1)}, bf16[2,64,8192]{2,1,0:T(8,128)(2,1)}, u32[]{:S(2)}, u32[]{:S(2)}) collective-permute-start(bf16[2,64,8192]{2,1,0:T(8,128)(2,1)S(1)} %pad_maximum_fusion.2.refs_5_), channel_id=1, source_target_pairs={{0,4},{1,5},{2,6},{3,7},{4,0},{5,1},{6,2},{7,3},{8,12},{9,13},{10,... | collective-permute-start | bytes 6291464 | tf_op jit(solution)/shard_map/ppermute | solution.py:328
  16.1 24.4 %collective-permute-start.1 = (bf16[2,2,16,8192]{3,2,1,0:T(8,128)(2,1)S(1)}, bf16[2,2,16,8192]{3,2,1,0:T(8,128)(2,1)S(1)}, u32[]{:S(2)}, u32[]{:S(2)}) collective-permute-start(bf16[2,2,16,8192]{3,2,1,0:T(8,128)(2,1)S(1)} %get-tuple-element.47), channel_id=1, source_target_pairs={{0,2},{1,3},{2,0},{3,1},{4,6},{5,7},{6,4},{7,5},{8,10},{9,11},{10,... | collective-permute-start | bytes 3145736 | tf_op jit(solution)/shard_map/ppermute | solution.py:328
  17.6 24.5 %collective-permute-start = (bf16[1,2,64,8192]{3,2,1,0:T(8,128)(2,1)S(1)}, bf16[1,2,64,8192]{3,2,1,0:T(8,128)(2,1)S(1)}, u32[]{:S(2)}, u32[]{:S(2)}) collective-permute-start(bf16[1,2,64,8192]{3,2,1,0:T(8,128)(2,1)S(1)} %get-tuple-element.44), channel_id=1, source_target_pairs={{0,1},{1,0},{2,3},{3,2},{4,5},{5,4},{6,7},{7,6},{8,9},{9,8},{10,11... | collective-permute-start | bytes 6291464 | tf_op jit(solution)/shard_map/ppermute | solution.py:328
  40.5 23.5 %collective-permute-start.2 = (bf16[2,2,16,8192]{3,2,1,0:T(8,128)(2,1)S(1)}, bf16[2,2,16,8192]{3,2,1,0:T(8,128)(2,1)S(1)}, u32[]{:S(2)}, u32[]{:S(2)}) collective-permute-start(bf16[2,2,16,8192]{3,2,1,0:T(8,128)(2,1)S(1)} %get-tuple-element.48), channel_id=1, source_target_pairs={{0,2},{1,3},{2,0},{3,1},{4,6},{5,7},{6,4},{7,5},{8,10},{9,11},{10,... | collective-permute-start | bytes 3145736 | tf_op jit(solution)/shard_map/ppermute | solution.py:328
  45.5 53.1 %collective-permute-start.11 = (bf16[2,64,8192]{2,1,0:T(8,128)(2,1)}, bf16[2,64,8192]{2,1,0:T(8,128)(2,1)}, u32[]{:S(2)}, u32[]{:S(2)}) collective-permute-start(bf16[2,64,8192]{2,1,0:T(8,128)(2,1)} %pad_maximum_fusion.rows3_ref), channel_id=1, source_target_pairs={{0,4},{1,5},{2,6},{3,7},{12,8},{13,9},{14,10},{15,11},{16,20},{17,... | collective-permute-start | bytes 6291464 | tf_op jit(solution)/shard_map/ppermute | solution.py:328
  49.1 52.0 %collective-permute-start.8 = (bf16[2,64,8192]{2,1,0:T(8,128)(2,1)}, bf16[2,64,8192]{2,1,0:T(8,128)(2,1)}, u32[]{:S(2)}, u32[]{:S(2)}) collective-permute-start(bf16[2,64,8192]{2,1,0:T(8,128)(2,1)} %collective-permute-done.7.crossed_ref), channel_id=1, source_target_pairs={{4,0},{5,1},{6,2},{7,3},{8,12},{9,13},{10,14},{11,15},{20,16},{21,... | collective-permute-start | bytes 6291464 | tf_op jit(solution)/shard_map/ppermute | solution.py:328
  55.1 46.1 %collective-permute-start.9 = (bf16[2,64,8192]{2,1,0:T(8,128)(2,1)}, bf16[2,64,8192]{2,1,0:T(8,128)(2,1)}, u32[]{:S(2)}, u32[]{:S(2)}) collective-permute-start(bf16[2,64,8192]{2,1,0:T(8,128)(2,1)} %collective-permute-done.6.refs_4_), channel_id=1, source_target_pairs={{4,8},{5,9},{6,10},{7,11},{8,4},{9,5},{10,6},{11,7},{20,24},{21,25... | collective-permute-start | bytes 6291464 | tf_op jit(solution)/shard_map/ppermute | solution.py:328
  67.6 50.0 %collective-permute-start.4 = (bf16[2,2,32,8192]{3,2,1,0:T(8,128)(2,1)}, bf16[2,2,32,8192]{3,2,1,0:T(8,128)(2,1)}, u32[]{:S(2)}, u32[]{:S(2)}) collective-permute-start(bf16[2,2,32,8192]{3,2,1,0:T(8,128)(2,1)} %get-tuple-element.49), channel_id=1, source_target_pairs={{0,2},{1,3},{2,0},{3,1},{4,6},{5,7},{6,4},{7,5},{8,10},{9,11},{10,... | collective-permute-start | bytes 6291464 | tf_op jit(solution)/shard_map/ppermute | solution.py:328
  106.3 28.7 %collective-permute-start.12 = (bf16[64,8192]{1,0:T(8,128)(2,1)S(1)}, bf16[64,8192]{1,0:T(8,128)(2,1)S(1)}, u32[]{:S(2)}, u32[]{:S(2)}) collective-permute-start(bf16[64,8192]{1,0:T(8,128)(2,1)S(1)} %get-tuple-element.53), channel_id=1, source_target_pairs={{0,4},{1,5},{2,6},{3,7},{4,0},{5,1},{6,2},{7,3},{8,12},{9,13},{10,... | collective-permute-start | bytes 3145736 | tf_op jit(solution)/shard_map/ppermute | solution.py:328
  111.3 23.6 %collective-permute-start.13 = (bf16[64,8192]{1,0:T(8,128)(2,1)S(1)}, bf16[64,8192]{1,0:T(8,128)(2,1)S(1)}, u32[]{:S(2)}, u32[]{:S(2)}) collective-permute-start(bf16[64,8192]{1,0:T(8,128)(2,1)S(1)} %get-tuple-element.54), channel_id=1, source_target_pairs={{4,8},{5,9},{6,10},{7,11},{8,4},{9,5},{10,6},{11,7},{20,24},{21,25... | collective-permute-start | bytes 3145736 | tf_op jit(solution)/shard_map/ppermute | solution.py:328
  112.1 56.6 %collective-permute-start.20 = (bf16[64,8192]{1,0:T(8,128)(2,1)S(1)}, bf16[64,8192]{1,0:T(8,128)(2,1)S(1)}, u32[]{:S(2)}, u32[]{:S(2)}) collective-permute-start(bf16[64,8192]{1,0:T(8,128)(2,1)S(1)} %get-tuple-element.68), channel_id=1, source_target_pairs={{0,4},{1,5},{2,6},{3,7},{12,8},{13,9},{14,10},{15,11},{16,20},{17,... | collective-permute-start | bytes 3145736 | tf_op jit(solution)/shard_map/ppermute | solution.py:328
  116.8 51.8 %collective-permute-start.21 = (bf16[64,8192]{1,0:T(8,128)(2,1)S(1)}, bf16[64,8192]{1,0:T(8,128)(2,1)S(1)}, u32[]{:S(2)}, u32[]{:S(2)}) collective-permute-start(bf16[64,8192]{1,0:T(8,128)(2,1)S(1)} %get-tuple-element.68), channel_id=1, source_target_pairs={{4,8},{5,9},{6,10},{7,11},{8,4},{9,5},{10,6},{11,7},{20,24},{21,25... | collective-permute-start | bytes 3145736 | tf_op jit(solution)/shard_map/ppermute | solution.py:328
  119.0 16.9 %collective-permute-start.5 = (bf16[1,2,32,8192]{3,2,1,0:T(8,128)(2,1)S(1)}, bf16[1,2,32,8192]{3,2,1,0:T(8,128)(2,1)S(1)}, u32[]{:S(2)}, u32[]{:S(2)}) collective-permute-start(bf16[1,2,32,8192]{3,2,1,0:T(8,128)(2,1)S(1)} %slice.37), channel_id=1, source_target_pairs={{0,1},{1,0},{2,3},{3,2},{4,5},{5,4},{6,7},{7,6},{8,9},{9,8},{10,11... | collective-permute-start | bytes 3145736 | tf_op jit(solution)/shard_map/ppermute | solution.py:328
  135.2 42.0 %collective-permute-start.18 = (bf16[64,8192]{1,0:T(8,128)(2,1)S(1)}, bf16[64,8192]{1,0:T(8,128)(2,1)S(1)}, u32[]{:S(2)}, u32[]{:S(2)}) collective-permute-start(bf16[64,8192]{1,0:T(8,128)(2,1)S(1)} %add_convert_fusion.3), channel_id=1, source_target_pairs={{4,8},{5,9},{6,10},{7,11},{8,4},{9,5},{10,6},{11,7},{20,24},{21,25... | collective-permute-start | bytes 3145736 | tf_op jit(solution)/shard_map/ppermute | solution.py:328
  143.8 23.3 %collective-permute-start.15 = (bf16[64,8192]{1,0:T(8,128)(2,1)S(1)}, bf16[64,8192]{1,0:T(8,128)(2,1)S(1)}, u32[]{:S(2)}, u32[]{:S(2)}) collective-permute-start(bf16[64,8192]{1,0:T(8,128)(2,1)S(1)} %get-tuple-element.58), channel_id=1, source_target_pairs={{0,2},{1,3},{2,0},{3,1},{4,6},{5,7},{6,4},{7,5},{8,10},{9,11},{10,... | collective-permute-start | bytes 3145736 | tf_op jit(solution)/shard_map/ppermute | solution.py:328
  145.5 40.7 %collective-permute-start.19 = (bf16[64,8192]{1,0:T(8,128)(2,1)S(1)}, bf16[64,8192]{1,0:T(8,128)(2,1)S(1)}, u32[]{:S(2)}, u32[]{:S(2)}) collective-permute-start(bf16[64,8192]{1,0:T(8,128)(2,1)S(1)} %add_convert_fusion.2), channel_id=1, source_target_pairs={{0,4},{1,5},{2,6},{3,7},{4,0},{5,1},{6,2},{7,3},{8,12},{9,13},{10,... | collective-permute-start | bytes 3145736 | tf_op jit(solution)/shard_map/ppermute | solution.py:328
  167.1 19.0 %collective-permute-start.16 = (bf16[64,8192]{1,0:T(8,128)(2,1)S(1)}, bf16[64,8192]{1,0:T(8,128)(2,1)S(1)}, u32[]{:S(2)}, u32[]{:S(2)}) collective-permute-start(bf16[64,8192]{1,0:T(8,128)(2,1)S(1)} %get-tuple-element.60), channel_id=1, source_target_pairs={{0,2},{1,3},{2,0},{3,1},{4,6},{5,7},{6,4},{7,5},{8,10},{9,11},{10,... | collective-permute-start | bytes 3145736 | tf_op jit(solution)/shard_map/ppermute | solution.py:328
  168.8 30.4 %collective-permute-start.23 = (bf16[64,8192]{1,0:T(8,128)(2,1)S(1)}, bf16[64,8192]{1,0:T(8,128)(2,1)S(1)}, u32[]{:S(2)}, u32[]{:S(2)}) collective-permute-start(bf16[64,8192]{1,0:T(8,128)(2,1)S(1)} %add_convert_fusion), channel_id=1, source_target_pairs={{0,4},{1,5},{2,6},{3,7},{4,0},{5,1},{6,2},{7,3},{8,12},{9,13},{10,... | collective-permute-start | bytes 3145736 | tf_op jit(solution)/shard_map/ppermute | solution.py:328
  176.3 22.9 %collective-permute-start.22 = (bf16[64,8192]{1,0:T(8,128)(2,1)S(1)}, bf16[64,8192]{1,0:T(8,128)(2,1)S(1)}, u32[]{:S(2)}, u32[]{:S(2)}) collective-permute-start(bf16[64,8192]{1,0:T(8,128)(2,1)S(1)} %add_convert_fusion.1), channel_id=1, source_target_pairs={{4,8},{5,9},{6,10},{7,11},{8,4},{9,5},{10,6},{11,7},{20,24},{21,25... | collective-permute-start | bytes 3145736 | tf_op jit(solution)/shard_map/ppermute | solution.py:328
  177.2 24.6 %collective-permute-start.14 = (bf16[64,8192]{1,0:T(8,128)(2,1)S(1)}, bf16[64,8192]{1,0:T(8,128)(2,1)S(1)}, u32[]{:S(2)}, u32[]{:S(2)}) collective-permute-start(bf16[64,8192]{1,0:T(8,128)(2,1)S(1)} %get-tuple-element.57), channel_id=1, source_target_pairs={{0,1},{1,0},{2,3},{3,2},{4,5},{5,4},{6,7},{7,6},{8,9},{9,8},{10,11... | collective-permute-start | bytes 3145736 | tf_op jit(solution)/shard_map/ppermute | solution.py:328
  186.1 15.7 %collective-permute-start.17 = (bf16[64,8192]{1,0:T(8,128)(2,1)S(1)}, bf16[64,8192]{1,0:T(8,128)(2,1)S(1)}, u32[]{:S(2)}, u32[]{:S(2)}) collective-permute-start(bf16[64,8192]{1,0:T(8,128)(2,1)S(1)} %collective-permute-done.16), channel_id=1, source_target_pairs={{0,1},{1,0},{2,3},{3,2},{4,5},{5,4},{6,7},{7,6},{8,9},{9,8},{10,11... | collective-permute-start | bytes 3145736 | tf_op jit(solution)/shard_map/ppermute | solution.py:328
  204.4 8.5 %collective-permute-start.27 = (f32[8,128]{1,0:T(8,128)S(1)}, f32[8,128]{1,0:T(8,128)S(1)}, u32[]{:S(2)}, u32[]{:S(2)}) collective-permute-start(f32[8,128]{1,0:T(8,128)S(1)} %add_add_fusion.refs_2_), channel_id=1, source_target_pairs={{0,12},{1,13},{2,14},{3,15},{4,8},{5,9},{6,10},{7,11},{8,4},{9,5},... | collective-permute-start | bytes 12296 | tf_op jit(solution)/shard_map/ppermute | solution.py:328
  207.1 5.9 %collective-permute-start.28 = (f32[8,128]{1,0:T(8,128)S(1)}, f32[8,128]{1,0:T(8,128)S(1)}, u32[]{:S(2)}, u32[]{:S(2)}) collective-permute-start(f32[8,128]{1,0:T(8,128)S(1)} %add_add_fusion.refs_2_), channel_id=1, source_target_pairs={{0,8},{1,9},{2,10},{3,11},{4,12},{5,13},{6,14},{7,15},{8,0},{9,1},... | collective-permute-start | bytes 12296 | tf_op jit(solution)/shard_map/ppermute | solution.py:328
  (14 other events, 100.5 us)

commit v22 on v21

--- a/solution.py
+++ b/solution.py
@@ -162,7 +162,7 @@
 
 def scaled(raws, parts, ndevices):
     rank, width = raws[0].shape
-    tile = min(width, 1024)
+    tile = min(width, 512)
     limit = float(2 * rank * width * ndevices) ** 0.5
 
     def body(*refs):
@@ -409,7 +409,7 @@
     raw_down, down_squares = final_sum(down0, down2, down1)
     raw_up, up_squares = final_sum(up0, up2, up1)
     part = down_squares + up_squares
-    part = part + sum(after([send(part, beside(m)) for m in range(1, plane)], half_acts))
+    part = part + sum(after([send(part, beside(m)) for m in range(plane - 1, 0, -1)], half_acts))
     along = [[(i, (i // plane ^ m) * plane + i % plane) for i in range(ndevices)] for m in (3, 2, 1)]
     parts = after([send(part, pairs) for pairs in along], grad_acts)
     return (grad_acts, *scaled((raw_down, raw_up), (part, *parts), ndevices))

time: 217 us -> 217 us (level)
  transfers between devices with their start and end apart: 30 -> 30, of which waited for: 13 -> 12; matrix products, arithmetic and copies ran while one was open for 3% -> 3% of each run, Pallas kernels for 13% -> 13%
where the time goes in v22:
time: 217 us; the launch traced here: 216 us
  waiting for transfers between devices  116 us (53%)
  starting transfers between devices  56.7 us (26%)
  Pallas kernels  30.8 us (14%)
  other arithmetic  6.23 us (3%)
  local copies, waits for them, and re-layouts  5.63 us (3%)
    ppermute x30, waiting for transfers between devices, send(): return lax.ppermute(array, 'dp', pairs)  116 us
    ppermute x30, starting transfers between devices, send(): return lax.ppermute(array, 'dp', pairs)  56.7 us
    pallas_call x5, Pallas kernels, in_place(): pl.pallas_call(body, in_specs=[pl.BlockSpec(memory_space=pltpu.SMEM)] * l...  17.2 us
    pallas_call x1, Pallas kernels, pack(): pl.pallas_call(body, grid=(tiles,), in_specs=[pl.BlockSpec(place.shape, l...  6.36 us
    pallas_call x2, Pallas kernels, unpack(): pl.pallas_call(body, grid=(width // 2 // tile,), in_specs=[pl.BlockSpec(p...  4.79 us
  transfers between devices with their start and end apart: 30, of which 12 were waited for; matrix products, arithmetic and copies ran while one was open for 3% of the time, Pallas kernels for 13%

profile of v22, /device:TPU:0, one launch (start us, length us, event | category | flops | bytes accessed | tf_op | source)
XLA Modules:
  0.0 216.3 jit_solution(9094958232345301589)
XLA Ops:
  4.4 4.6 %collective-permute-start.6 = (bf16[2,64,8192]{2,1,0:T(8,128)(2,1)S(1)}, bf16[2,64,8192]{2,1,0:T(8,128)(2,1)}, u32[]{:S(2)}, u32[]{:S(2)}) collective-permute-start(bf16[2,64,8192]{2,1,0:T(8,128)(2,1)S(1)} %pad_maximum_fusion.2.refs_5_), channel_id=1, source_target_pairs={{0,4},{1,5},{2,6},{3,7},{4,0},{5,1},{6,2},{7,3},{8,12},{9,13},{10,... | collective-permute-start | bytes 6291464 | tf_op jit(solution)/shard_map/ppermute | solution.py:328
  9.7 6.4 %shard_map.85 = (bf16[1,2,64,8192]{3,2,1,0:T(8,128)(2,1)S(1)}, bf16[1,2,64,8192]{3,2,1,0:T(8,128)(2,1)S(1)}, bf16[2,2,16,8192]{3,2,1,0:T(8,128)(2,1)S(1)}, bf16[...) custom-call(bf16[256,128]{1,0:T(8,128)(2,1)S(1)} %fusion.1.place_ref, bf16[128,8192]{1,0:T(8,128)(2,1)} %x_in.1, ...), custom_call_target="tpu_custom_call" | custom-call | tf_op jit(solution)/shard_map/pallas_call | solution.py:107
  17.7 22.8 %collective-permute-done.1 = bf16[2,2,16,8192]{3,2,1,0:T(8,128)(2,1)S(1)} collective-permute-done((bf16[2,2,16,8192]{3,2,1,0:T(8,128)(2,1)S(1)}, bf16[2,2,16,8192]{3,2,1,0:T(8,128)(2,1)S(1)}, u32[]{:S(2)}, u32[]{:S(2)}) %collective-permute-start.1) | collective-permute-done | bytes 1048608 | tf_op jit(solution)/shard_map/ppermute | solution.py:328
  45.5 3.6 %collective-permute-start.11 = (bf16[2,64,8192]{2,1,0:T(8,128)(2,1)}, bf16[2,64,8192]{2,1,0:T(8,128)(2,1)}, u32[]{:S(2)}, u32[]{:S(2)}) collective-permute-start(bf16[2,64,8192]{2,1,0:T(8,128)(2,1)} %pad_maximum_fusion.rows3_ref), channel_id=1, source_target_pairs={{0,4},{1,5},{2,6},{3,7},{12,8},{13,9},{14,10},{15,11},{16,20},{17,... | collective-permute-start | bytes 6291464 | tf_op jit(solution)/shard_map/ppermute | solution.py:328
  50.4 4.6 %collective-permute-done.6.refs_4_ = bf16[2,64,8192]{2,1,0:T(8,128)(2,1)} collective-permute-done((bf16[2,64,8192]{2,1,0:T(8,128)(2,1)S(1)}, bf16[2,64,8192]{2,1,0:T(8,128)(2,1)}, u32[]{:S(2)}, u32[]{:S(2)}) %collective-permute-start.6) | collective-permute-done | bytes 2097184 | tf_op jit(solution)/shard_map/ppermute | solution.py:328
  57.1 6.9 %collective-permute-done.2 = bf16[2,2,16,8192]{3,2,1,0:T(8,128)(2,1)S(1)} collective-permute-done((bf16[2,2,16,8192]{3,2,1,0:T(8,128)(2,1)S(1)}, bf16[2,2,16,8192]{3,2,1,0:T(8,128)(2,1)S(1)}, u32[]{:S(2)}, u32[]{:S(2)}) %collective-permute-start.2) | collective-permute-done | bytes 1048608 | tf_op jit(solution)/shard_map/ppermute | solution.py:328
  70.4 4.1 %shard_map.86 = (bf16[64,8192]{1,0:T(8,128)(2,1)S(1)}, bf16[64,8192]{1,0:T(8,128)(2,1)S(1)}, bf16[64,8192]{1,0:T(8,128)(2,1)S(1)}, bf16[2,64,8192]{2,1,0:T(8,128)(2,1)S(1)}) custom-call(s32[1]{0:T(128)} %bitcast.1.flags_ref, bf16[2,64,8192]{2,1,0:T(8,128)(2,1)} %pad_maximum_fusion.rows3_ref, bf16[2,64,8192]{2,1,0:T(8,128)(2,1)S(1)} %pad_maximum_fusion.1.rows2_ref, ...), custom_call_target="tpu_custom_call" | custom-call | tf_op jit(solution)/shard_map/pallas_call | solution.py:218
  74.6 24.1 %collective-permute-done.11.handed_ref = bf16[2,64,8192]{2,1,0:T(8,128)(2,1)} collective-permute-done((bf16[2,64,8192]{2,1,0:T(8,128)(2,1)}, bf16[2,64,8192]{2,1,0:T(8,128)(2,1)}, u32[]{:S(2)}, u32[]{:S(2)}) %collective-permute-start.11) | collective-permute-done | bytes 2097184 | tf_op jit(solution)/shard_map/ppermute | solution.py:328
  98.6 2.5 %collective-permute-done.8.outer_ref.refs_6_ = bf16[2,64,8192]{2,1,0:T(8,128)(2,1)} collective-permute-done((bf16[2,64,8192]{2,1,0:T(8,128)(2,1)}, bf16[2,64,8192]{2,1,0:T(8,128)(2,1)}, u32[]{:S(2)}, u32[]{:S(2)}) %collective-permute-start.8) | collective-permute-done | bytes 2097184 | tf_op jit(solution)/shard_map/ppermute | solution.py:328
  101.1 5.2 %shard_map.87 = (bf16[64,8192]{1,0:T(8,128)(2,1)S(1)}, bf16[64,8192]{1,0:T(8,128)(2,1)S(1)}, bf16[64,64]{1,0:T(8,128)(2,1)S(1)}, bf16[64,8192]{1,0:T(8,128)(2,1)S(1)}) custom-call(s32[1]{0:T(128)} %bitcast.1.flags_ref, bf16[2,64,8192]{2,1,0:T(8,128)(2,1)S(1)} %get-tuple-element.50.rows_ref, bf16[2,64,8192]{2,1,0:T(8,128)(2,1)} %collective-permute-done.11.handed_ref, ...), custom_call_target="tpu_custom_call" | custom-call | tf_op jit(solution)/shard_map/pallas_call | solution.py:218
  106.3 5.0 %collective-permute-start.12 = (bf16[64,8192]{1,0:T(8,128)(2,1)S(1)}, bf16[64,8192]{1,0:T(8,128)(2,1)S(1)}, u32[]{:S(2)}, u32[]{:S(2)}) collective-permute-start(bf16[64,8192]{1,0:T(8,128)(2,1)S(1)} %get-tuple-element.53), channel_id=1, source_target_pairs={{0,4},{1,5},{2,6},{3,7},{4,0},{5,1},{6,2},{7,3},{8,12},{9,13},{10,... | collective-permute-start | bytes 3145736 | tf_op jit(solution)/shard_map/ppermute | solution.py:328
  112.1 4.8 %collective-permute-start.20 = (bf16[64,8192]{1,0:T(8,128)(2,1)S(1)}, bf16[64,8192]{1,0:T(8,128)(2,1)S(1)}, u32[]{:S(2)}, u32[]{:S(2)}) collective-permute-start(bf16[64,8192]{1,0:T(8,128)(2,1)S(1)} %get-tuple-element.68), channel_id=1, source_target_pairs={{0,4},{1,5},{2,6},{3,7},{12,8},{13,9},{14,10},{15,11},{16,20},{17,... | collective-permute-start | bytes 3145736 | tf_op jit(solution)/shard_map/ppermute | solution.py:328
  119.1 15.8 %collective-permute-done.12.refs_10_ = bf16[64,8192]{1,0:T(8,128)(2,1)S(1)} collective-permute-done((bf16[64,8192]{1,0:T(8,128)(2,1)S(1)}, bf16[64,8192]{1,0:T(8,128)(2,1)S(1)}, u32[]{:S(2)}, u32[]{:S(2)}) %collective-permute-start.12) | collective-permute-done | bytes 1048608 | tf_op jit(solution)/shard_map/ppermute | solution.py:328
  136.0 6.8 %shard_map.88 = (bf16[64,8192]{1,0:T(8,128)(2,1)S(1)}, bf16[64,8192]{1,0:T(8,128)(2,1)S(1)}, bf16[64,8192]{1,0:T(8,128)(2,1)S(1)}, bf16[64,8192]{1,0:T(8,128)(2,...) custom-call(s32[1]{0:T(128)} %bitcast.1.flags_ref, ...), custom_call_target="tpu_custom_call" | custom-call | tf_op jit(solution)/shard_map/pallas_call | solution.py:218
  145.5 7.2 %collective-permute-start.19 = (bf16[64,8192]{1,0:T(8,128)(2,1)S(1)}, bf16[64,8192]{1,0:T(8,128)(2,1)S(1)}, u32[]{:S(2)}, u32[]{:S(2)}) collective-permute-start(bf16[64,8192]{1,0:T(8,128)(2,1)S(1)} %add_convert_fusion.2), channel_id=1, source_target_pairs={{0,4},{1,5},{2,6},{3,7},{4,0},{5,1},{6,2},{7,3},{8,12},{9,13},{10,... | collective-permute-start | bytes 3145736 | tf_op jit(solution)/shard_map/ppermute | solution.py:328
  152.7 14.5 %collective-permute-done.15.refs_2_ = bf16[64,8192]{1,0:T(8,128)(2,1)S(1)} collective-permute-done((bf16[64,8192]{1,0:T(8,128)(2,1)S(1)}, bf16[64,8192]{1,0:T(8,128)(2,1)S(1)}, u32[]{:S(2)}, u32[]{:S(2)}) %collective-permute-start.15) | collective-permute-done | bytes 1048608 | tf_op jit(solution)/shard_map/ppermute | solution.py:328
  168.8 7.2 %collective-permute-start.23 = (bf16[64,8192]{1,0:T(8,128)(2,1)S(1)}, bf16[64,8192]{1,0:T(8,128)(2,1)S(1)}, u32[]{:S(2)}, u32[]{:S(2)}) collective-permute-start(bf16[64,8192]{1,0:T(8,128)(2,1)S(1)} %add_convert_fusion), channel_id=1, source_target_pairs={{0,4},{1,5},{2,6},{3,7},{4,0},{5,1},{6,2},{7,3},{8,12},{9,13},{10,... | collective-permute-start | bytes 3145736 | tf_op jit(solution)/shard_map/ppermute | solution.py:328
  177.3 8.9 %collective-permute-done.16 = bf16[64,8192]{1,0:T(8,128)(2,1)S(1)} collective-permute-done((bf16[64,8192]{1,0:T(8,128)(2,1)S(1)}, bf16[64,8192]{1,0:T(8,128)(2,1)S(1)}, u32[]{:S(2)}, u32[]{:S(2)}) %collective-permute-start.16) | collective-permute-done | bytes 1048608 | tf_op jit(solution)/shard_map/ppermute | solution.py:328
  186.7 12.5 %collective-permute-done.23.refs_1_ = bf16[64,8192]{1,0:T(8,128)(2,1)S(1)} collective-permute-done((bf16[64,8192]{1,0:T(8,128)(2,1)S(1)}, bf16[64,8192]{1,0:T(8,128)(2,1)S(1)}, u32[]{:S(2)}, u32[]{:S(2)}) %collective-permute-start.23) | collective-permute-done | bytes 1048608 | tf_op jit(solution)/shard_map/ppermute | solution.py:328
  201.8 2.4 %shard_map.89.refs_4_ = bf16[128,8192]{1,0:T(8,128)(2,1)} custom-call(bf16[128,256]{1,0:T(8,128)(2,1)S(1)} %fusion.place_ref, bf16[64,8192]{1,0:T(8,128)(2,1)} %copy-done.4, bf16[64,8192]{1,0:T(8,128)(2,1)S(1)} %collective-permute-done.14.refs_1_, bf16[64,8192]{1,0:T(8,128)(2,1)S(1)} %collective-permute-done.15.refs_2_, ...), custom_call_target="tpu_custom_call" | custom-call | tf_op jit(solution)/shard_map/pallas_call | solution.py:128
  204.2 2.7 %collective-permute-start.27 = (f32[8,128]{1,0:T(8,128)S(1)}, f32[8,128]{1,0:T(8,128)S(1)}, u32[]{:S(2)}, u32[]{:S(2)}) collective-permute-start(f32[8,128]{1,0:T(8,128)S(1)} %add_add_fusion.refs_2_), channel_id=1, source_target_pairs={{0,12},{1,13},{2,14},{3,15},{4,8},{5,9},{6,10},{7,11},{8,4},{9,5},... | collective-permute-start | bytes 12296 | tf_op jit(solution)/shard_map/ppermute | solution.py:328
  206.9 3.2 %collective-permute-start.28 = (f32[8,128]{1,0:T(8,128)S(1)}, f32[8,128]{1,0:T(8,128)S(1)}, u32[]{:S(2)}, u32[]{:S(2)}) collective-permute-start(f32[8,128]{1,0:T(8,128)S(1)} %add_add_fusion.refs_2_), channel_id=1, source_target_pairs={{0,8},{1,9},{2,10},{3,11},{4,12},{5,13},{6,14},{7,15},{8,0},{9,1},... | collective-permute-start | bytes 12296 | tf_op jit(solution)/shard_map/ppermute | solution.py:328
  210.4 2.4 %shard_map.90 = bf16[128,8192]{1,0:T(8,128)(2,1)} custom-call(bf16[128,256]{1,0:T(8,128)(2,1)S(1)} %fusion.place_ref, bf16[64,8192]{1,0:T(8,128)(2,1)} %copy-done.4, bf16[64,8192]{1,0:T(8,128)(2,1)S(1)} %collective-permute-done.14.refs_1_, bf16[64,8192]{1,0:T(8,128)(2,1)S(1)} %collective-permute-done.15.refs_2_, ...), custom_call_target="tpu_custom_call", output_to_operand_aliasing={{}: (5, {})} | custom-call | tf_op jit(solution)/shard_map/pallas_call | solution.py:128
  213.8 2.4 %shard_map.93 = (f32[1,64,8192]{2,1,0:T(8,128)}, f32[1,64,8192]{2,1,0:T(8,128)}) custom-call(f32[64,8192]{1,0:T(8,128)S(1)} %get-tuple-element.65.refs_0_, f32[64,8192]{1,0:T(8,128)S(1)} %get-tuple-element.72.refs_1_, f32[8,128]{1,0:T(8,128)S(1)} %add_add_fusion.refs_2_, f32[8,128]{1,0:T(8,128)S(1)} %collective-permute-done.27.refs_3_, ...), custom_call_target="tpu_custom_call" | custom-call | tf_op jit(solution)/shard_map/pallas_call | solution.py:183
  (83 shorter events, 34.7 us)
Async XLA Ops:
  2.4 46.7 %collective-permute-start.7 = (bf16[2,64,8192]{2,1,0:T(8,128)(2,1)S(1)}, bf16[2,64,8192]{2,1,0:T(8,128)(2,1)}, u32[]{:S(2)}, u32[]{:S(2)}) collective-permute-start(bf16[2,64,8192]{2,1,0:T(8,128)(2,1)S(1)} %pad_maximum_fusion.2.refs_5_), channel_id=1, source_target_pairs={{4,8},{5,9},{6,10},{7,11},{8,4},{9,5},{10,6},{11,7},{20,24},{21,25... | collective-permute-start | bytes 6291464 | tf_op jit(solution)/shard_map/ppermute | solution.py:328
  4.4 50.7 %collective-permute-start.6 = (bf16[2,64,8192]{2,1,0:T(8,128)(2,1)S(1)}, bf16[2,64,8192]{2,1,0:T(8,128)(2,1)}, u32[]{:S(2)}, u32[]{:S(2)}) collective-permute-start(bf16[2,64,8192]{2,1,0:T(8,128)(2,1)S(1)} %pad_maximum_fusion.2.refs_5_), channel_id=1, source_target_pairs={{0,4},{1,5},{2,6},{3,7},{4,0},{5,1},{6,2},{7,3},{8,12},{9,13},{10,... | collective-permute-start | bytes 6291464 | tf_op jit(solution)/shard_map/ppermute | solution.py:328
  16.1 24.4 %collective-permute-start.1 = (bf16[2,2,16,8192]{3,2,1,0:T(8,128)(2,1)S(1)}, bf16[2,2,16,8192]{3,2,1,0:T(8,128)(2,1)S(1)}, u32[]{:S(2)}, u32[]{:S(2)}) collective-permute-start(bf16[2,2,16,8192]{3,2,1,0:T(8,128)(2,1)S(1)} %get-tuple-element.47), channel_id=1, source_target_pairs={{0,2},{1,3},{2,0},{3,1},{4,6},{5,7},{6,4},{7,5},{8,10},{9,11},{10,... | collective-permute-start | bytes 3145736 | tf_op jit(solution)/shard_map/ppermute | solution.py:328
  17.6 24.5 %collective-permute-start = (bf16[1,2,64,8192]{3,2,1,0:T(8,128)(2,1)S(1)}, bf16[1,2,64,8192]{3,2,1,0:T(8,128)(2,1)S(1)}, u32[]{:S(2)}, u32[]{:S(2)}) collective-permute-start(bf16[1,2,64,8192]{3,2,1,0:T(8,128)(2,1)S(1)} %get-tuple-element.44), channel_id=1, source_target_pairs={{0,1},{1,0},{2,3},{3,2},{4,5},{5,4},{6,7},{7,6},{8,9},{9,8},{10,11... | collective-permute-start | bytes 6291464 | tf_op jit(solution)/shard_map/ppermute | solution.py:328
  40.5 23.5 %collective-permute-start.2 = (bf16[2,2,16,8192]{3,2,1,0:T(8,128)(2,1)S(1)}, bf16[2,2,16,8192]{3,2,1,0:T(8,128)(2,1)S(1)}, u32[]{:S(2)}, u32[]{:S(2)}) collective-permute-start(bf16[2,2,16,8192]{3,2,1,0:T(8,128)(2,1)S(1)} %get-tuple-element.48), channel_id=1, source_target_pairs={{0,2},{1,3},{2,0},{3,1},{4,6},{5,7},{6,4},{7,5},{8,10},{9,11},{10,... | collective-permute-start | bytes 3145736 | tf_op jit(solution)/shard_map/ppermute | solution.py:328
  45.5 53.1 %collective-permute-start.11 = (bf16[2,64,8192]{2,1,0:T(8,128)(2,1)}, bf16[2,64,8192]{2,1,0:T(8,128)(2,1)}, u32[]{:S(2)}, u32[]{:S(2)}) collective-permute-start(bf16[2,64,8192]{2,1,0:T(8,128)(2,1)} %pad_maximum_fusion.rows3_ref), channel_id=1, source_target_pairs={{0,4},{1,5},{2,6},{3,7},{12,8},{13,9},{14,10},{15,11},{16,20},{17,... | collective-permute-start | bytes 6291464 | tf_op jit(solution)/shard_map/ppermute | solution.py:328
  49.1 52.0 %collective-permute-start.8 = (bf16[2,64,8192]{2,1,0:T(8,128)(2,1)}, bf16[2,64,8192]{2,1,0:T(8,128)(2,1)}, u32[]{:S(2)}, u32[]{:S(2)}) collective-permute-start(bf16[2,64,8192]{2,1,0:T(8,128)(2,1)} %collective-permute-done.7.crossed_ref), channel_id=1, source_target_pairs={{4,0},{5,1},{6,2},{7,3},{8,12},{9,13},{10,14},{11,15},{20,16},{21,... | collective-permute-start | bytes 6291464 | tf_op jit(solution)/shard_map/ppermute | solution.py:328
  55.1 46.1 %collective-permute-start.9 = (bf16[2,64,8192]{2,1,0:T(8,128)(2,1)}, bf16[2,64,8192]{2,1,0:T(8,128)(2,1)}, u32[]{:S(2)}, u32[]{:S(2)}) collective-permute-start(bf16[2,64,8192]{2,1,0:T(8,128)(2,1)} %collective-permute-done.6.refs_4_), channel_id=1, source_target_pairs={{4,8},{5,9},{6,10},{7,11},{8,4},{9,5},{10,6},{11,7},{20,24},{21,25... | collective-permute-start | bytes 6291464 | tf_op jit(solution)/shard_map/ppermute | solution.py:328
  67.6 50.0 %collective-permute-start.4 = (bf16[2,2,32,8192]{3,2,1,0:T(8,128)(2,1)}, bf16[2,2,32,8192]{3,2,1,0:T(8,128)(2,1)}, u32[]{:S(2)}, u32[]{:S(2)}) collective-permute-start(bf16[2,2,32,8192]{3,2,1,0:T(8,128)(2,1)} %get-tuple-element.49), channel_id=1, source_target_pairs={{0,2},{1,3},{2,0},{3,1},{4,6},{5,7},{6,4},{7,5},{8,10},{9,11},{10,... | collective-permute-start | bytes 6291464 | tf_op jit(solution)/shard_map/ppermute | solution.py:328
  106.3 28.7 %collective-permute-start.12 = (bf16[64,8192]{1,0:T(8,128)(2,1)S(1)}, bf16[64,8192]{1,0:T(8,128)(2,1)S(1)}, u32[]{:S(2)}, u32[]{:S(2)}) collective-permute-start(bf16[64,8192]{1,0:T(8,128)(2,1)S(1)} %get-tuple-element.53), channel_id=1, source_target_pairs={{0,4},{1,5},{2,6},{3,7},{4,0},{5,1},{6,2},{7,3},{8,12},{9,13},{10,... | collective-permute-start | bytes 3145736 | tf_op jit(solution)/shard_map/ppermute | solution.py:328
  111.3 23.6 %collective-permute-start.13 = (bf16[64,8192]{1,0:T(8,128)(2,1)S(1)}, bf16[64,8192]{1,0:T(8,128)(2,1)S(1)}, u32[]{:S(2)}, u32[]{:S(2)}) collective-permute-start(bf16[64,8192]{1,0:T(8,128)(2,1)S(1)} %get-tuple-element.54), channel_id=1, source_target_pairs={{4,8},{5,9},{6,10},{7,11},{8,4},{9,5},{10,6},{11,7},{20,24},{21,25... | collective-permute-start | bytes 3145736 | tf_op jit(solution)/shard_map/ppermute | solution.py:328
  112.1 56.6 %collective-permute-start.20 = (bf16[64,8192]{1,0:T(8,128)(2,1)S(1)}, bf16[64,8192]{1,0:T(8,128)(2,1)S(1)}, u32[]{:S(2)}, u32[]{:S(2)}) collective-permute-start(bf16[64,8192]{1,0:T(8,128)(2,1)S(1)} %get-tuple-element.68), channel_id=1, source_target_pairs={{0,4},{1,5},{2,6},{3,7},{12,8},{13,9},{14,10},{15,11},{16,20},{17,... | collective-permute-start | bytes 3145736 | tf_op jit(solution)/shard_map/ppermute | solution.py:328
  116.8 51.8 %collective-permute-start.21 = (bf16[64,8192]{1,0:T(8,128)(2,1)S(1)}, bf16[64,8192]{1,0:T(8,128)(2,1)S(1)}, u32[]{:S(2)}, u32[]{:S(2)}) collective-permute-start(bf16[64,8192]{1,0:T(8,128)(2,1)S(1)} %get-tuple-element.68), channel_id=1, source_target_pairs={{4,8},{5,9},{6,10},{7,11},{8,4},{9,5},{10,6},{11,7},{20,24},{21,25... | collective-permute-start | bytes 3145736 | tf_op jit(solution)/shard_map/ppermute | solution.py:328
  119.0 16.9 %collective-permute-start.5 = (bf16[1,2,32,8192]{3,2,1,0:T(8,128)(2,1)S(1)}, bf16[1,2,32,8192]{3,2,1,0:T(8,128)(2,1)S(1)}, u32[]{:S(2)}, u32[]{:S(2)}) collective-permute-start(bf16[1,2,32,8192]{3,2,1,0:T(8,128)(2,1)S(1)} %slice.37), channel_id=1, source_target_pairs={{0,1},{1,0},{2,3},{3,2},{4,5},{5,4},{6,7},{7,6},{8,9},{9,8},{10,11... | collective-permute-start | bytes 3145736 | tf_op jit(solution)/shard_map/ppermute | solution.py:328
  135.2 42.0 %collective-permute-start.18 = (bf16[64,8192]{1,0:T(8,128)(2,1)S(1)}, bf16[64,8192]{1,0:T(8,128)(2,1)S(1)}, u32[]{:S(2)}, u32[]{:S(2)}) collective-permute-start(bf16[64,8192]{1,0:T(8,128)(2,1)S(1)} %add_convert_fusion.3), channel_id=1, source_target_pairs={{4,8},{5,9},{6,10},{7,11},{8,4},{9,5},{10,6},{11,7},{20,24},{21,25... | collective-permute-start | bytes 3145736 | tf_op jit(solution)/shard_map/ppermute | solution.py:328
  143.8 23.3 %collective-permute-start.15 = (bf16[64,8192]{1,0:T(8,128)(2,1)S(1)}, bf16[64,8192]{1,0:T(8,128)(2,1)S(1)}, u32[]{:S(2)}, u32[]{:S(2)}) collective-permute-start(bf16[64,8192]{1,0:T(8,128)(2,1)S(1)} %get-tuple-element.58), channel_id=1, source_target_pairs={{0,2},{1,3},{2,0},{3,1},{4,6},{5,7},{6,4},{7,5},{8,10},{9,11},{10,... | collective-permute-start | bytes 3145736 | tf_op jit(solution)/shard_map/ppermute | solution.py:328
  145.5 40.7 %collective-permute-start.19 = (bf16[64,8192]{1,0:T(8,128)(2,1)S(1)}, bf16[64,8192]{1,0:T(8,128)(2,1)S(1)}, u32[]{:S(2)}, u32[]{:S(2)}) collective-permute-start(bf16[64,8192]{1,0:T(8,128)(2,1)S(1)} %add_convert_fusion.2), channel_id=1, source_target_pairs={{0,4},{1,5},{2,6},{3,7},{4,0},{5,1},{6,2},{7,3},{8,12},{9,13},{10,... | collective-permute-start | bytes 3145736 | tf_op jit(solution)/shard_map/ppermute | solution.py:328
  167.1 19.0 %collective-permute-start.16 = (bf16[64,8192]{1,0:T(8,128)(2,1)S(1)}, bf16[64,8192]{1,0:T(8,128)(2,1)S(1)}, u32[]{:S(2)}, u32[]{:S(2)}) collective-permute-start(bf16[64,8192]{1,0:T(8,128)(2,1)S(1)} %get-tuple-element.60), channel_id=1, source_target_pairs={{0,2},{1,3},{2,0},{3,1},{4,6},{5,7},{6,4},{7,5},{8,10},{9,11},{10,... | collective-permute-start | bytes 3145736 | tf_op jit(solution)/shard_map/ppermute | solution.py:328
  168.8 30.4 %collective-permute-start.23 = (bf16[64,8192]{1,0:T(8,128)(2,1)S(1)}, bf16[64,8192]{1,0:T(8,128)(2,1)S(1)}, u32[]{:S(2)}, u32[]{:S(2)}) collective-permute-start(bf16[64,8192]{1,0:T(8,128)(2,1)S(1)} %add_convert_fusion), channel_id=1, source_target_pairs={{0,4},{1,5},{2,6},{3,7},{4,0},{5,1},{6,2},{7,3},{8,12},{9,13},{10,... | collective-permute-start | bytes 3145736 | tf_op jit(solution)/shard_map/ppermute | solution.py:328
  176.3 22.9 %collective-permute-start.22 = (bf16[64,8192]{1,0:T(8,128)(2,1)S(1)}, bf16[64,8192]{1,0:T(8,128)(2,1)S(1)}, u32[]{:S(2)}, u32[]{:S(2)}) collective-permute-start(bf16[64,8192]{1,0:T(8,128)(2,1)S(1)} %add_convert_fusion.1), channel_id=1, source_target_pairs={{4,8},{5,9},{6,10},{7,11},{8,4},{9,5},{10,6},{11,7},{20,24},{21,25... | collective-permute-start | bytes 3145736 | tf_op jit(solution)/shard_map/ppermute | solution.py:328
  177.2 24.6 %collective-permute-start.14 = (bf16[64,8192]{1,0:T(8,128)(2,1)S(1)}, bf16[64,8192]{1,0:T(8,128)(2,1)S(1)}, u32[]{:S(2)}, u32[]{:S(2)}) collective-permute-start(bf16[64,8192]{1,0:T(8,128)(2,1)S(1)} %get-tuple-element.57), channel_id=1, source_target_pairs={{0,1},{1,0},{2,3},{3,2},{4,5},{5,4},{6,7},{7,6},{8,9},{9,8},{10,11... | collective-permute-start | bytes 3145736 | tf_op jit(solution)/shard_map/ppermute | solution.py:328
  186.1 15.7 %collective-permute-start.17 = (bf16[64,8192]{1,0:T(8,128)(2,1)S(1)}, bf16[64,8192]{1,0:T(8,128)(2,1)S(1)}, u32[]{:S(2)}, u32[]{:S(2)}) collective-permute-start(bf16[64,8192]{1,0:T(8,128)(2,1)S(1)} %collective-permute-done.16), channel_id=1, source_target_pairs={{0,1},{1,0},{2,3},{3,2},{4,5},{5,4},{6,7},{7,6},{8,9},{9,8},{10,11... | collective-permute-start | bytes 3145736 | tf_op jit(solution)/shard_map/ppermute | solution.py:328
  204.2 8.6 %collective-permute-start.27 = (f32[8,128]{1,0:T(8,128)S(1)}, f32[8,128]{1,0:T(8,128)S(1)}, u32[]{:S(2)}, u32[]{:S(2)}) collective-permute-start(f32[8,128]{1,0:T(8,128)S(1)} %add_add_fusion.refs_2_), channel_id=1, source_target_pairs={{0,12},{1,13},{2,14},{3,15},{4,8},{5,9},{6,10},{7,11},{8,4},{9,5},... | collective-permute-start | bytes 12296 | tf_op jit(solution)/shard_map/ppermute | solution.py:328
  206.9 5.9 %collective-permute-start.28 = (f32[8,128]{1,0:T(8,128)S(1)}, f32[8,128]{1,0:T(8,128)S(1)}, u32[]{:S(2)}, u32[]{:S(2)}) collective-permute-start(f32[8,128]{1,0:T(8,128)S(1)} %add_add_fusion.refs_2_), channel_id=1, source_target_pairs={{0,8},{1,9},{2,10},{3,11},{4,12},{5,13},{6,14},{7,15},{8,0},{9,1},... | collective-permute-start | bytes 12296 | tf_op jit(solution)/shard_map/ppermute | solution.py:328
  (14 other events, 100.2 us)
